TPU v7x, 32 devices: a whole 2x2x4 slice. The times are simulated.
32 devices in a mesh: dp: 8 (over z, x), row: 2 (over y), col: 2 (over core).
Axes of the slice: x: 2, y: 2, z: 4, core: 2. Of those that a mesh axis runs over, the one named last changes fastest.
Arguments:
- tokens_in: bfloat16 [8192, 1536], P(('dp', 'row'), 'col'), may hold values from -6 to 6
- norm_gain_attn: float32 [1536], P('col'), may hold values from 0.5 to 1.5
- w_query: bfloat16 [1536, 1536], P('col', 'row'), may hold values from -0.15625 to 0.15625
- w_key: bfloat16 [1536, 512], P('col', 'row'), may hold values from -0.15625 to 0.15625
- w_value: bfloat16 [1536, 512], P('col', 'row'), may hold values from -0.15625 to 0.15625
- w_out: bfloat16 [1536, 1536], P('row', 'col'), may hold values from -2.5 to 2.5
- norm_gain_ffn: float32 [1536], P('col'), may hold values from 0.5 to 1.5
- w_gate: bfloat16 [16, 1536, 512], P(None, 'col', 'row'), may hold values from -0.15625 to 0.15625
- w_up: bfloat16 [16, 1536, 512], P(None, 'col', 'row'), may hold values from -0.15625 to 0.15625
- w_down: bfloat16 [16, 512, 1536], P(None, 'row', 'col'), may hold values from -1 to 1
- w_shared_gate: bfloat16 [1536, 1024], P('col', 'row'), may hold values from -0.15625 to 0.15625
- w_shared_up: bfloat16 [1536, 1024], P('col', 'row'), may hold values from -0.15625 to 0.15625
- w_shared_down: bfloat16 [1024, 1536], P('row', 'col'), may hold values from -0.375 to 0.375
- routes: int32 [8192, 6], P('dp'), may hold values from 0 to 15, all different within a row; in each aligned block of 1024 rows (0 to 1023, 1024 to 2047, ...) at most 512 rows name the same one
- gate_weights: float32 [8192, 6], P('dp'), may hold values from 0.08 to 0.32
- seq_lengths: int32 [8], P('dp'), may hold values from 256 to 1024, as said below
- out_grad: bfloat16 [8192, 1536], P(('dp', 'row'), 'col'), may hold values from -6 to 6
Outputs:
- block_out: bfloat16 [8192, 1536], P(('dp', 'row'), 'col')
- tokens_grad: bfloat16 [8192, 1536], P(('dp', 'row'), 'col')
- gain_attn_grad: float32 [1536], P('col')
- query_grad: float32 [1536, 1536], P('col', 'row')
- key_grad: float32 [1536, 512], P('col', 'row')
- value_grad: float32 [1536, 512], P('col', 'row')
- out_proj_grad: float32 [1536, 1536], P('row', 'col')
- gain_ffn_grad: float32 [1536], P('col')
- gate_grad: float32 [16, 1536, 512], P(None, 'col', 'row')
- up_grad: float32 [16, 1536, 512], P(None, 'col', 'row')
- down_grad: float32 [16, 512, 1536], P(None, 'row', 'col')
- shared_gate_grad: float32 [1536, 1024], P('col', 'row')
- shared_up_grad: float32 [1536, 1024], P('col', 'row')
- shared_down_grad: float32 [1024, 1536], P('row', 'col')
Inputs may be any that keep to these rules, and one draw needn't show every extreme that they name: `routes`: each row names 6 different experts; within each data shard's 1024 rows no expert is named by more than 512 rows, and that bound is reached. `seq_lengths`: keys at or past a sequence's length are masked; some sequence has the full 1024 and some has 256.
All inputs are finite; a program needn't handle non-finite values.
Results may differ from a plain program's by a relative error of at most 0.023.
Values may be sent and summed in bfloat16 or wider, within the bound.
No kernel may reach another device: no remote copies, remote signals or barrier semaphores. Data moves between devices by JAX's collectives and lax.ppermute only.
A program may use at most 384 MiB of HBM per device.

v0:
```python
import jax
import jax.numpy as jnp
from jax import lax
from jax.sharding import PartitionSpec as P

D = 1536
HQ = 12
HK = 4
DH = 128
CAP = 512


EPSILON = 1e-05


def product(left, right):
    return jnp.dot(left, right, preferred_element_type=jnp.float32)


def product_back(left, right):
    return lax.dot_general(
        left, right, (((1,), (1,)), ((), ())), preferred_element_type=jnp.float32
    )


def product_rows(left, right):
    return lax.dot_general(
        left, right, (((0,), (0,)), ((), ())), preferred_element_type=jnp.float32
    )


def across_rows(values):
    return lax.all_gather(values, "row", axis=0, tiled=True)


def feature_total(values):
    return lax.psum(values, "col")


def row_total(function, row_count):
    return lax.psum_scatter(
        function(jnp.int32(0), lax.axis_size("row") * row_count),
        "row",
        scatter_dimension=0,
        tiled=True,
    )


def sum_ffn_grads(grad_gate, grad_up, grad_down, grad_sgate, grad_sup, grad_sdown):
    shares = (
        lax.psum_scatter(
            grad_gate.astype(jnp.bfloat16), "dp", scatter_dimension=1, tiled=True
        ).astype(jnp.float32),
        lax.psum_scatter(
            grad_up.astype(jnp.bfloat16), "dp", scatter_dimension=1, tiled=True
        ).astype(jnp.float32),
        lax.psum_scatter(
            grad_down.astype(jnp.bfloat16), "dp", scatter_dimension=2, tiled=True
        ).astype(jnp.float32),
        lax.psum_scatter(
            grad_sgate.astype(jnp.bfloat16), "dp", scatter_dimension=0, tiled=True
        ).astype(jnp.float32),
        lax.psum_scatter(
            grad_sup.astype(jnp.bfloat16), "dp", scatter_dimension=0, tiled=True
        ).astype(jnp.float32),
        lax.psum_scatter(
            grad_sdown.astype(jnp.bfloat16), "dp", scatter_dimension=1, tiled=True
        ).astype(jnp.float32),
    )
    return (
        lax.all_gather(shares[0].astype(jnp.bfloat16), "dp", axis=1, tiled=True).astype(
            jnp.float32
        ),
        lax.all_gather(shares[1].astype(jnp.bfloat16), "dp", axis=1, tiled=True).astype(
            jnp.float32
        ),
        lax.all_gather(shares[2].astype(jnp.bfloat16), "dp", axis=2, tiled=True).astype(
            jnp.float32
        ),
        lax.all_gather(shares[3].astype(jnp.bfloat16), "dp", axis=0, tiled=True).astype(
            jnp.float32
        ),
        lax.all_gather(shares[4].astype(jnp.bfloat16), "dp", axis=0, tiled=True).astype(
            jnp.float32
        ),
        lax.all_gather(shares[5].astype(jnp.bfloat16), "dp", axis=1, tiled=True).astype(
            jnp.float32
        ),
    )


def sum_attn_grads(grad_query, grad_key, grad_value, grad_out):
    shares = (
        lax.psum_scatter(
            grad_query.astype(jnp.bfloat16), "dp", scatter_dimension=0, tiled=True
        ).astype(jnp.float32),
        lax.psum_scatter(
            grad_key.astype(jnp.bfloat16), "dp", scatter_dimension=0, tiled=True
        ).astype(jnp.float32),
        lax.psum_scatter(
            grad_value.astype(jnp.bfloat16), "dp", scatter_dimension=0, tiled=True
        ).astype(jnp.float32),
        lax.psum_scatter(
            grad_out.astype(jnp.bfloat16), "dp", scatter_dimension=1, tiled=True
        ).astype(jnp.float32),
    )
    return (
        lax.all_gather(shares[0].astype(jnp.bfloat16), "dp", axis=0, tiled=True).astype(
            jnp.float32
        ),
        lax.all_gather(shares[1].astype(jnp.bfloat16), "dp", axis=0, tiled=True).astype(
            jnp.float32
        ),
        lax.all_gather(shares[2].astype(jnp.bfloat16), "dp", axis=0, tiled=True).astype(
            jnp.float32
        ),
        lax.all_gather(shares[3].astype(jnp.bfloat16), "dp", axis=1, tiled=True).astype(
            jnp.float32
        ),
    )


def slot_table(routes, experts, capacity):
    group_rows = routes.shape[0]
    choices_count = routes.shape[1]
    pair_experts = routes.reshape(-1)
    onehot = (pair_experts[:, None] == jnp.arange(experts, dtype=jnp.int32)[None, :]).astype(
        jnp.int32
    )
    pair_ranks = jnp.sum((jnp.cumsum(onehot, axis=0) - 1) * onehot, axis=1)
    pair_slots = pair_ranks * experts + pair_experts
    owners = jnp.arange(pair_experts.shape[0], dtype=jnp.int32) // choices_count
    holder = jnp.full((capacity * experts,), group_rows, jnp.int32).at[pair_slots].set(owners)
    return (pair_slots.reshape(group_rows, choices_count), holder)


def masked_scores(grouped, key_heads, length):
    seq_tokens = grouped.shape[0]
    scores = jnp.einsum(
        "qgrd,kgd->grqk", grouped, key_heads, preferred_element_type=jnp.float32
    ) * DH ** (-0.5)
    position = jnp.arange(seq_tokens, dtype=jnp.int32)
    allowed = (position[None, :] <= position[:, None]) & (position[None, :] < length)
    return jnp.where(allowed, scores, -1e30)


def attend(parts):
    queries, key_rows, value_rows, length = parts
    seq_tokens = queries.shape[0]
    key_groups = key_rows.shape[1] // DH
    grouped = queries.reshape(seq_tokens, key_groups, HQ // HK, DH)
    key_heads = key_rows.reshape(seq_tokens, key_groups, DH)
    value_heads = value_rows.reshape(seq_tokens, key_groups, DH)
    scores = masked_scores(grouped, key_heads, length)
    highest = jnp.max(scores, axis=-1, keepdims=True)
    weights = jnp.exp(scores - highest)
    totals = jnp.sum(weights, axis=-1, keepdims=True)
    key_probs = weights / totals
    attended = jnp.einsum(
        "grqk,kgd->qgrd",
        key_probs.astype(jnp.bfloat16),
        value_heads,
        preferred_element_type=jnp.float32,
    )
    return (
        attended.reshape(seq_tokens, -1).astype(jnp.bfloat16),
        highest[..., 0] + jnp.log(totals[..., 0]),
    )


def attend_back(parts):
    queries, key_rows, value_rows, logsum, attended_grad, length = parts
    seq_tokens = queries.shape[0]
    key_groups = key_rows.shape[1] // DH
    grouped = queries.reshape(seq_tokens, key_groups, HQ // HK, DH)
    key_heads = key_rows.reshape(seq_tokens, key_groups, DH)
    value_heads = value_rows.reshape(seq_tokens, key_groups, DH)
    key_probs = jnp.exp(masked_scores(grouped, key_heads, length) - logsum[..., None])
    grad_heads = attended_grad.reshape(seq_tokens, key_groups, HQ // HK, DH)
    probs_grad = jnp.einsum(
        "qgrd,kgd->grqk", grad_heads, value_heads, preferred_element_type=jnp.float32
    )
    carried = jnp.sum(key_probs * probs_grad, axis=-1, keepdims=True)
    score_grad = (key_probs * (probs_grad - carried)).astype(jnp.bfloat16)
    score_scale = DH ** (-0.5)
    query_back = (
        jnp.einsum("grqk,kgd->qgrd", score_grad, key_heads, preferred_element_type=jnp.float32)
        * score_scale
    ).astype(jnp.bfloat16)
    key_back = (
        jnp.einsum("grqk,qgrd->kgd", score_grad, grouped, preferred_element_type=jnp.float32)
        * score_scale
    ).astype(jnp.bfloat16)
    value_back = jnp.einsum(
        "grqk,qgrd->kgd",
        key_probs.astype(jnp.bfloat16),
        grad_heads,
        preferred_element_type=jnp.float32,
    ).astype(jnp.bfloat16)
    return (
        query_back.reshape(seq_tokens, -1),
        key_back.reshape(seq_tokens, -1),
        value_back.reshape(seq_tokens, -1),
    )


def silu_back(pre_gate, pre_up, inner_grad):
    sigmoid = jax.nn.sigmoid(pre_gate)
    gate_part = inner_grad * pre_up * (sigmoid * (1.0 + pre_gate * (1.0 - sigmoid)))
    up_part = inner_grad * (pre_gate * sigmoid)
    return jnp.concatenate([gate_part, up_part], axis=-1).astype(jnp.bfloat16)


def body(
    tokens_in,
    norm_gain_attn,
    w_query,
    w_key,
    w_value,
    w_out,
    norm_gain_ffn,
    w_gate,
    w_up,
    w_down,
    w_shared_gate,
    w_shared_up,
    w_shared_down,
    routes,
    gate_weights,
    seq_lengths,
    out_grad,
):
    local_rows = tokens_in.shape[0]
    group_rows = routes.shape[0]
    experts = w_gate.shape[0]
    hidden_width = w_gate.shape[2]
    shared_width = w_shared_gate.shape[1]
    query_width = w_query.shape[1]
    key_width = w_key.shape[1]
    sequences = seq_lengths.shape[0]
    seq_tokens = group_rows // sequences
    tokens = tokens_in.astype(jnp.float32)
    scale_attn = lax.rsqrt(feature_total(jnp.sum(tokens * tokens, axis=1)) / D + EPSILON)[:, None]
    normed_attn = across_rows((tokens * scale_attn * norm_gain_attn).astype(jnp.bfloat16))
    w_project = jnp.concatenate([w_query, w_key, w_value], axis=1)
    projected = lax.psum(product(normed_attn, w_project), "col").astype(jnp.bfloat16)
    queries = projected[:, :query_width]
    key_rows = projected[:, query_width : query_width + key_width]
    value_rows = projected[:, query_width + key_width :]
    attended, logsum = lax.map(
        attend,
        (
            queries.reshape(sequences, seq_tokens, -1),
            key_rows.reshape(sequences, seq_tokens, -1),
            value_rows.reshape(sequences, seq_tokens, -1),
            seq_lengths,
        ),
    )
    attended = attended.reshape(group_rows, query_width)

    def attn_rows(first_row, row_count):
        return product(attended, w_out)

    hidden = tokens + row_total(attn_rows, local_rows)
    scale_ffn = lax.rsqrt(feature_total(jnp.sum(hidden * hidden, axis=1)) / D + EPSILON)[:, None]
    normed_ffn = across_rows((hidden * scale_ffn * norm_gain_ffn).astype(jnp.bfloat16))
    grad_all = across_rows(out_grad)
    pair_slots, holder = slot_table(routes, experts, CAP)
    padded = jnp.concatenate(
        [normed_ffn, jnp.zeros((1, normed_ffn.shape[1]), jnp.bfloat16)], axis=0
    )
    dispatched = padded[holder].reshape(CAP, experts, -1)
    w_gate_up = jnp.concatenate([w_gate, w_up], axis=2)
    w_shared_pair = jnp.concatenate([w_shared_gate, w_shared_up], axis=1)
    pair_terms = jnp.einsum(
        "ced,edh->ceh", dispatched, w_gate_up, preferred_element_type=jnp.float32
    )
    shared_terms = product(normed_ffn, w_shared_pair)
    pair_sums, shared_sums = (
        lax.psum_scatter(
            pair_terms.astype(jnp.bfloat16), "col", scatter_dimension=0, tiled=True
        ).astype(jnp.float32),
        lax.psum_scatter(
            shared_terms.astype(jnp.bfloat16), "col", scatter_dimension=0, tiled=True
        ).astype(jnp.float32),
    )
    pre_gate = pair_sums[..., :hidden_width]
    pre_up = pair_sums[..., hidden_width:]
    shared_gate = shared_sums[:, :shared_width]
    shared_up = shared_sums[:, shared_width:]
    inner = (jax.nn.silu(pre_gate) * pre_up).astype(jnp.bfloat16)
    shared_inner = (jax.nn.silu(shared_gate) * shared_up).astype(jnp.bfloat16)
    inner_all, shared_all = (
        lax.all_gather(inner, "col", axis=0, tiled=True),
        lax.all_gather(shared_inner, "col", axis=0, tiled=True),
    )
    expert_out = jnp.einsum(
        "ceh,ehd->ced", inner_all, w_down, preferred_element_type=jnp.float32
    ).reshape(CAP * experts, -1)

    def ffn_rows(first_row, row_count):
        routed = jnp.sum(gate_weights[:, :, None] * expert_out[pair_slots], axis=1)
        return routed + product(shared_all, w_shared_down)

    block_out = (hidden + row_total(ffn_rows, local_rows)).astype(jnp.bfloat16)
    grad_padded = jnp.concatenate(
        [grad_all, jnp.zeros((1, grad_all.shape[1]), jnp.bfloat16)], axis=0
    )
    slot_gates = (
        jnp.zeros((CAP * experts,), jnp.float32)
        .at[pair_slots.reshape(-1)]
        .set(gate_weights.reshape(-1))
    )
    expert_grad = (slot_gates[:, None] * grad_padded[holder].astype(jnp.float32)).astype(
        jnp.bfloat16
    )
    expert_grad = expert_grad.reshape(CAP, experts, -1)
    down_grad = jnp.einsum(
        "ceh,ced->ehd", inner_all, expert_grad, preferred_element_type=jnp.float32
    )
    shared_down_grad = product_rows(shared_all, grad_all)
    inner_part = jnp.einsum("ced,ehd->ceh", expert_grad, w_down, preferred_element_type=jnp.float32)
    shared_part = product_back(grad_all, w_shared_down)
    inner_grad, shared_grad = (
        lax.psum_scatter(
            inner_part.astype(jnp.bfloat16), "col", scatter_dimension=0, tiled=True
        ).astype(jnp.float32),
        lax.psum_scatter(
            shared_part.astype(jnp.bfloat16), "col", scatter_dimension=0, tiled=True
        ).astype(jnp.float32),
    )
    pair_grad = silu_back(pre_gate, pre_up, inner_grad)
    shared_pair_grad = silu_back(shared_gate, shared_up, shared_grad)
    pair_all, shared_pair_all = (
        lax.all_gather(pair_grad, "col", axis=0, tiled=True),
        lax.all_gather(shared_pair_grad, "col", axis=0, tiled=True),
    )
    gate_up_grad = jnp.einsum(
        "ced,ceh->edh", dispatched, pair_all, preferred_element_type=jnp.float32
    )
    gate_grad = gate_up_grad[..., :hidden_width]
    up_grad = gate_up_grad[..., hidden_width:]
    shared_pair_wgrad = product_rows(normed_ffn, shared_pair_all)
    shared_gate_grad = shared_pair_wgrad[:, :shared_width]
    shared_up_grad = shared_pair_wgrad[:, shared_width:]
    dispatched_grad = jnp.einsum(
        "ceh,edh->ced", pair_all, w_gate_up, preferred_element_type=jnp.float32
    ).reshape(CAP * experts, -1)

    def normed_rows(first_row, row_count):
        routed_back = jnp.sum(dispatched_grad[pair_slots], axis=1)
        return routed_back + product_back(shared_pair_all, w_shared_pair)

    normed_ffn_grad = row_total(normed_rows, local_rows)
    scaled_ffn = normed_ffn_grad * norm_gain_ffn
    gain_ffn_part = jnp.sum(normed_ffn_grad * hidden * scale_ffn, axis=0)
    ffn_mean = feature_total(jnp.sum(scaled_ffn * hidden, axis=1)) / D
    hidden_grad = (
        out_grad.astype(jnp.float32)
        + scale_ffn * scaled_ffn
        - hidden * scale_ffn**3 * ffn_mean[:, None]
    )
    attn_grad = across_rows(hidden_grad.astype(jnp.bfloat16))
    out_proj_grad = product_rows(attended, attn_grad)
    attended_grad = lax.psum(product_back(attn_grad, w_out).astype(jnp.bfloat16), "col")
    query_back, key_back, value_back = lax.map(
        attend_back,
        (
            queries.reshape(sequences, seq_tokens, -1),
            key_rows.reshape(sequences, seq_tokens, -1),
            value_rows.reshape(sequences, seq_tokens, -1),
            logsum,
            attended_grad.reshape(sequences, seq_tokens, -1),
            seq_lengths,
        ),
    )
    project_grad = jnp.concatenate(
        [
            query_back.reshape(group_rows, -1),
            key_back.reshape(group_rows, -1),
            value_back.reshape(group_rows, -1),
        ],
        axis=1,
    )
    project_wgrad = product_rows(normed_attn, project_grad)
    query_grad = project_wgrad[:, :query_width]
    key_grad = project_wgrad[:, query_width : query_width + key_width]
    value_grad = project_wgrad[:, query_width + key_width :]

    def attn_in_rows(first_row, row_count):
        return product_back(project_grad, w_project)

    normed_attn_grad = row_total(attn_in_rows, local_rows)
    scaled_attn = normed_attn_grad * norm_gain_attn
    gain_attn_part = jnp.sum(normed_attn_grad * tokens * scale_attn, axis=0)
    attn_mean = feature_total(jnp.sum(scaled_attn * tokens, axis=1)) / D
    tokens_grad = (
        hidden_grad + scale_attn * scaled_attn - tokens * scale_attn**3 * attn_mean[:, None]
    ).astype(jnp.bfloat16)
    gain_attn_grad, gain_ffn_grad = lax.psum((gain_attn_part, gain_ffn_part), ("dp", "row"))
    ffn_grads = sum_ffn_grads(
        gate_grad, up_grad, down_grad, shared_gate_grad, shared_up_grad, shared_down_grad
    )
    attn_grads = sum_attn_grads(query_grad, key_grad, value_grad, out_proj_grad)
    return (
        block_out,
        tokens_grad,
        gain_attn_grad,
        attn_grads[0],
        attn_grads[1],
        attn_grads[2],
        attn_grads[3],
        gain_ffn_grad,
        ffn_grads[0],
        ffn_grads[1],
        ffn_grads[2],
        ffn_grads[3],
        ffn_grads[4],
        ffn_grads[5],
    )


def solution(mesh):
    in_specs = (
        P(("dp", "row"), "col"),
        P("col"),
        P("col", "row"),
        P("col", "row"),
        P("col", "row"),
        P("row", "col"),
        P("col"),
        P(None, "col", "row"),
        P(None, "col", "row"),
        P(None, "row", "col"),
        P("col", "row"),
        P("col", "row"),
        P("row", "col"),
        P("dp", None),
        P("dp", None),
        P("dp"),
        P(("dp", "row"), "col"),
    )
    out_specs = (
        P(("dp", "row"), "col"),
        P(("dp", "row"), "col"),
        P("col"),
        P("col", "row"),
        P("col", "row"),
        P("col", "row"),
        P("row", "col"),
        P("col"),
        P(None, "col", "row"),
        P(None, "col", "row"),
        P(None, "row", "col"),
        P("col", "row"),
        P("col", "row"),
        P("row", "col"),
    )
    return jax.shard_map(body, mesh=mesh, in_specs=in_specs, out_specs=out_specs, check_vma=False)
```

profile of v0, /device:TPU:0, one launch (start us, length us, event | category | flops | bytes accessed | tf_op | source)
XLA Modules:
  0.0 2072.2 jit_solution(17255310987503622570)
XLA Ops:
  19.8 25.0 %all-gather.14.cloned.1.call-done = bf16[1024,768]{1,0:T(8,128)(2,1)} async-done(((bf16[512,768]{1,0:T(8,128)(2,1)}), bf16[1024,768]{1,0:T(8,128)(2,1)}) %all-gather.14.cloned.1.call-update) | async-done | bytes 1572880 | tf_op jit(solution)/shard_map/all_gather | solution.py:33
  51.4 17.7 all-reduce.7
  78.5 11.9 fusion.64
  90.4 10.2 fusion.3
  100.6 10.9 fusion.18
  116.0 43.5 %reduce-scatter.19.cloned.1.call-done = f32[512,768]{1,0:T(8,128)} async-done(((f32[1024,768]{1,0:T(8,128)}), f32[512,768]{1,0:T(8,128)}) %reduce-scatter.19.cloned.1.call-update) | async-done | bytes 1572880 | tf_op jit(solution)/shard_map/reduce_scatter | solution.py:41
  169.1 9.8 reduce-window.6
  182.6 23.0 %scatter_custom_fusion = s32[8192]{0:T(1024)S(1)} fusion(s32[6144]{0:T(1024)S(1)} %bitcast.131, s32[6144]{0:T(1024)S(1)} %add_select_fusion, s32[]{:T(128)} %constant.90.clone.1), kind=kCustom, calls=%fused_computation.116 | custom fusion | bytes 32772 | tf_op jit(solution)/shard_map/scatter | solution.py:133
  205.6 8.7 copy.65
  214.3 8.7 copy.66
  224.5 34.4 %gather_fusion = bf16[8192,768]{1,0:T(8,128)(2,1)} fusion(bf16[1025,768]{1,0:T(8,128)(2,1)S(1)} %concatenate.28, s32[8192]{0:T(1024)S(1)} %fusion.47), kind=kCustom, calls=%fused_computation | custom fusion | bytes 25198592 | tf_op jit(solution)/shard_map/gather | solution.py:272
  258.9 17.4 copy.89
  276.3 13.7 convert_bitcast_fusion
  291.4 23.0 %scatter_custom_fusion.1 = f32[8192]{0:T(1024)S(1)} fusion(s32[6144]{0:T(1024)S(1)} %bitcast.132, f32[6144]{0:T(1024)S(1)} %reshape.254, f32[]{:T(128)} %constant.53.clone.1), kind=kCustom, calls=%fused_computation.114 | custom fusion | bytes 32772 | tf_op jit(solution)/shard_map/scatter | solution.py:312
  316.1 34.4 %gather_fusion.2 = bf16[8192,768]{1,0:T(8,128)(2,1)} fusion(bf16[1025,768]{1,0:T(8,128)(2,1)S(1)} %concatenate.30, s32[8192]{0:T(1024)S(1)} %fusion.47), kind=kCustom, calls=%fused_computation.2 | custom fusion | bytes 25198592 | tf_op jit(solution)/shard_map/gather | solution.py:314
  350.6 20.0 copy.76
  370.6 13.9 convert_bitcast_fusion.1
  384.5 12.4 reduce-scatter.23.cloned.1.call-start
  429.8 16.3 all-gather.24.cloned.1.call-done
  446.1 18.9 convolution_bitcast_fusion
  464.9 25.8 %copy.81 = f32[512,16,768]{2,1,0:T(8,128)} copy(f32[512,16,768]{2,0,1:T(8,128)} %convolution_bitcast_fusion) | data formatting | bytes 50331648 | tf_op jit(solution)/shard_map/ceh,edh->ced/transpose | solution.py:346
  490.7 38.0 %gather_fusion.3 = f32[6144,768]{1,0:T(8,128)} fusion(f32[8192,768]{1,0:T(8,128)} %bitcast.113, s32[6144]{0:T(1024)S(1)} %broadcast_clamp_fusion), kind=kCustom, calls=%fused_computation.3 | custom fusion | bytes 37773312 | tf_op jit(solution)/shard_map/gather | solution.py:351
  528.8 21.7 %reshape.239 = f32[1024,6,768]{2,1,0:T(8,128)} reshape(f32[6144,768]{1,0:T(8,128)} %gather_fusion.3) | data formatting | bytes 37748736 | tf_op jit(solution)/shard_map/gather | solution.py:351
  550.4 20.3 reduce_sum.106
  577.2 16.0 convolution_bitcast_fusion.1
  593.2 25.0 %copy.72 = f32[512,16,768]{2,1,0:T(8,128)} copy(f32[512,16,768]{2,0,1:T(8,128)} %convolution_bitcast_fusion.1) | data formatting | bytes 50331648 | tf_op jit(solution)/shard_map/ceh,ehd->ced/transpose | solution.py:297
  618.2 38.2 %gather_fusion.1 = f32[6144,768]{1,0:T(8,128)} fusion(f32[8192,768]{1,0:T(8,128)} %bitcast.112, s32[6144]{0:T(1024)S(1)} %broadcast_clamp_fusion), kind=kCustom, calls=%fused_computation.1 | custom fusion | bytes 37773312 | tf_op jit(solution)/shard_map/gather | solution.py:302
  656.4 21.8 %reshape.219 = f32[1024,6,768]{2,1,0:T(8,128)} reshape(f32[6144,768]{1,0:T(8,128)} %gather_fusion.1) | data formatting | bytes 37748736 | tf_op jit(solution)/shard_map/gather | solution.py:302
  678.2 14.2 multiply_reduce_fusion
  704.3 37.9 %reduce-scatter.25.cloned.1.call-done = f32[512,768]{1,0:T(8,128)} async-done(((f32[1024,768]{1,0:T(8,128)}), f32[512,768]{1,0:T(8,128)}) %reduce-scatter.25.cloned.1.call-update) | async-done | bytes 1572880 | tf_op jit(solution)/shard_map/reduce_scatter | solution.py:41
  746.5 27.1 %all-gather.28.cloned.1.call-done = bf16[1024,768]{1,0:T(8,128)(2,1)} async-done(((bf16[512,768]{1,0:T(8,128)(2,1)}), bf16[1024,768]{1,0:T(8,128)(2,1)}) %all-gather.28.cloned.1.call-update) | async-done | bytes 1572880 | tf_op jit(solution)/shard_map/all_gather | solution.py:33
  782.7 16.0 all-reduce.6.cloned.1.call-done
  798.6 16.0 fusion
  814.6 21.7 %fusion.2 = bf16[2,3,1024,1024]{2,3,1,0:T(8,128)(2,1)} fusion(f32[2,1024,1024,3]{2,1,3,0:T(8,128)} %get-tuple-element.125, f32[2,3,1024,1024]{2,3,1,0:T(8,128)} %get-tuple-element.123, f32[2,3,1024]{2,1,0:T(4,128)S(1)} %get-tuple-element.124, f32[2,3,1024]{2,1,0:T(4,128)S(1)} %log_add_fusion), kind=kLoop, calls=%fused_computation.10 | loop fusion | flops 25165824 | bytes 62963712 | tf_op jit(solution)/shard_map/while/body/eval_jaxpr/convert_element_type | solution.py:184
  836.3 9.7 fusion.32
  846.0 7.7 multiply_convert_fusion.6
  853.8 11.6 fusion.33
  871.0 14.1 fusion.17
  885.2 13.7 convolution_convert_fusion
  898.9 10.6 fusion.60
  922.1 14.7 reduce-scatter.35.cloned.1.call-done
  943.4 113.8 %reduce-scatter.47.cloned.1.call-done = bf16[16,256,96]{1,2,0:T(8,128)(2,1)} async-done(((bf16[16,256,768]{1,2,0:T(8,128)(2,1)}), bf16[16,256,96]{1,2,0:T(8,128)(2,1)}) %reduce-scatter.47.cloned.1.call-update) | async-done | bytes 786448 | tf_op jit(solution)/shard_map/reduce_scatter | solution.py:57
  1057.3 121.1 %reduce-scatter.43.cloned.1.call-done = bf16[16,96,256]{2,1,0:T(8,128)(2,1)} async-done(((bf16[16,768,256]{2,1,0:T(8,128)(2,1)}), bf16[16,96,256]{2,1,0:T(8,128)(2,1)}) %reduce-scatter.43.cloned.1.call-update) | async-done | bytes 786448 | tf_op jit(solution)/shard_map/reduce_scatter | solution.py:51
  1178.4 121.2 %reduce-scatter.45.cloned.1.call-done = bf16[16,96,256]{2,1,0:T(8,128)(2,1)} async-done(((bf16[16,768,256]{2,1,0:T(8,128)(2,1)}), bf16[16,96,256]{2,1,0:T(8,128)(2,1)}) %reduce-scatter.45.cloned.1.call-update) | async-done | bytes 786448 | tf_op jit(solution)/shard_map/reduce_scatter | solution.py:54
  1299.7 65.5 %reduce-scatter.53.cloned.1.call-done = bf16[512,96]{0,1:T(8,128)(2,1)} async-done(((bf16[512,768]{0,1:T(8,128)(2,1)}), bf16[512,96]{0,1:T(8,128)(2,1)}) %reduce-scatter.53.cloned.1.call-update) | async-done | bytes 98320 | tf_op jit(solution)/shard_map/reduce_scatter | solution.py:66
  1365.1 33.7 %all_gather.71 = bf16[512,768]{0,1:T(8,128)(2,1)S(1)} all-gather(bf16[512,96]{0,1:T(8,128)(2,1)} %reduce-scatter.53.cloned.1.call-done), channel_id=1, replica_groups=mesh['dp'=8,'row'=2,'col'=2] {'dp'}, dimensions={1}, use_global_device_ids=true | all-gather | bytes 884736 | tf_op jit(solution)/shard_map/all_gather | solution.py:86
  1400.2 30.5 %reduce-scatter.51.cloned.1.call-done = bf16[96,512]{1,0:T(8,128)(2,1)} async-done(((bf16[768,512]{1,0:T(8,128)(2,1)}), bf16[96,512]{1,0:T(8,128)(2,1)}) %reduce-scatter.51.cloned.1.call-update) | async-done | bytes 98320 | tf_op jit(solution)/shard_map/reduce_scatter | solution.py:63
  1430.7 33.2 %all_gather.70 = bf16[768,512]{1,0:T(8,128)(2,1)S(1)} all-gather(bf16[96,512]{1,0:T(8,128)(2,1)} %reduce-scatter.51.cloned.1.call-done), channel_id=1, replica_groups=mesh['dp'=8,'row'=2,'col'=2] {'dp'}, dimensions={0}, use_global_device_ids=true | all-gather | bytes 884736 | tf_op jit(solution)/shard_map/all_gather | solution.py:83
  1465.3 31.1 %reduce-scatter.49.cloned.1.call-done = bf16[96,512]{1,0:T(8,128)(2,1)} async-done(((bf16[768,512]{1,0:T(8,128)(2,1)}), bf16[96,512]{1,0:T(8,128)(2,1)}) %reduce-scatter.49.cloned.1.call-update) | async-done | bytes 98320 | tf_op jit(solution)/shard_map/reduce_scatter | solution.py:60
  1496.3 32.6 %all_gather.69 = bf16[768,512]{1,0:T(8,128)(2,1)S(1)} all-gather(bf16[96,512]{1,0:T(8,128)(2,1)} %reduce-scatter.49.cloned.1.call-done), channel_id=1, replica_groups=mesh['dp'=8,'row'=2,'col'=2] {'dp'}, dimensions={0}, use_global_device_ids=true | all-gather | bytes 884736 | tf_op jit(solution)/shard_map/all_gather | solution.py:80
  1530.3 30.1 %reduce-scatter.39.cloned.1.call-done = bf16[96,256]{1,0:T(8,128)(2,1)} async-done(((bf16[768,256]{1,0:T(8,128)(2,1)}), bf16[96,256]{1,0:T(8,128)(2,1)}) %reduce-scatter.39.cloned.1.call-update) | async-done | bytes 49168 | tf_op jit(solution)/shard_map/reduce_scatter | solution.py:100
  1560.4 31.6 %all_gather.64 = bf16[768,256]{1,0:T(8,128)(2,1)S(1)} all-gather(bf16[96,256]{1,0:T(8,128)(2,1)} %reduce-scatter.39.cloned.1.call-done), channel_id=1, replica_groups=mesh['dp'=8,'row'=2,'col'=2] {'dp'}, dimensions={0}, use_global_device_ids=true | all-gather | bytes 442368 | tf_op jit(solution)/shard_map/all_gather | solution.py:114
  1593.0 31.4 %reduce-scatter.37.cloned.1.call-done = bf16[96,256]{1,0:T(8,128)(2,1)} async-done(((bf16[768,256]{1,0:T(8,128)(2,1)}), bf16[96,256]{1,0:T(8,128)(2,1)}) %reduce-scatter.37.cloned.1.call-update) | async-done | bytes 49168 | tf_op jit(solution)/shard_map/reduce_scatter | solution.py:97
  1624.3 31.6 %all_gather.63 = bf16[768,256]{1,0:T(8,128)(2,1)S(1)} all-gather(bf16[96,256]{1,0:T(8,128)(2,1)} %reduce-scatter.37.cloned.1.call-done), channel_id=1, replica_groups=mesh['dp'=8,'row'=2,'col'=2] {'dp'}, dimensions={0}, use_global_device_ids=true | all-gather | bytes 442368 | tf_op jit(solution)/shard_map/all_gather | solution.py:111
  1656.9 10.8 all-gather.32.cloned.1.call-done
  1670.4 39.7 %all-gather.30.cloned.1.call-done = bf16[768,768]{1,0:T(8,128)(2,1)} async-done(((bf16[96,768]{1,0:T(8,128)(2,1)}), bf16[768,768]{1,0:T(8,128)(2,1)}) %all-gather.30.cloned.1.call-update) | async-done | bytes 1179664 | tf_op jit(solution)/shard_map/all_gather | solution.py:108
  1713.0 42.2 %reduce-scatter.33.cloned.1.call-done = f32[512,768]{1,0:T(8,128)} async-done(((f32[1024,768]{1,0:T(8,128)}), f32[512,768]{1,0:T(8,128)}) %reduce-scatter.33.cloned.1.call-update) | async-done | bytes 1572880 | tf_op jit(solution)/shard_map/reduce_scatter | solution.py:41
  1761.0 43.0 %all-reduce.2 = (f32[768]{0:T(1024)}, f32[768]{0:T(1024)}) all-reduce(f32[768]{0:T(1024)S(1)} %get-tuple-element.95, f32[768]{0:T(1024)S(1)} %get-tuple-element.93), channel_id=1, replica_groups=mesh['dp'=8,'row'=2,'col'=2] {'dp','row'}, use_global_device_ids=true, to_apply=%region_29.30 | all-reduce | flops 1536 | bytes 12288 | tf_op jit(solution)/shard_map/psum | solution.py:400
  1807.5 50.0 %all-gather.38.cloned.1.call-done = bf16[16,256,768]{1,2,0:T(8,128)(2,1)} async-done(((bf16[16,256,96]{1,2,0:T(8,128)(2,1)}), bf16[16,256,768]{1,2,0:T(8,128)(2,1)}) %all-gather.38.cloned.1.call-update) | async-done | bytes 6291472 | tf_op jit(solution)/shard_map/all_gather | solution.py:77
  1857.4 9.5 copy.93
  1866.9 89.9 %all-gather.34.cloned.1.call-done = bf16[16,768,256]{2,1,0:T(8,128)(2,1)} async-done(((bf16[16,96,256]{2,1,0:T(8,128)(2,1)}), bf16[16,768,256]{2,1,0:T(8,128)(2,1)}) %all-gather.34.cloned.1.call-update) | async-done | bytes 6291472 | tf_op jit(solution)/shard_map/all_gather | solution.py:71
  1956.9 8.9 convert_element_type.232
  1965.8 90.5 %all-gather.36.cloned.1.call-done = bf16[16,768,256]{2,1,0:T(8,128)(2,1)} async-done(((bf16[16,96,256]{2,1,0:T(8,128)(2,1)}), bf16[16,768,256]{2,1,0:T(8,128)(2,1)}) %all-gather.36.cloned.1.call-update) | async-done | bytes 6291472 | tf_op jit(solution)/shard_map/all_gather | solution.py:74
  2056.3 8.9 convert_element_type.233
  (243 shorter events, 160.0 us)
Async XLA Ops:
  7.2 105.6 %copy-start = (bf16[768,768]{1,0:T(8,128)(2,1)S(1)}, bf16[768,768]{1,0:T(8,128)(2,1)}, u32[]{:S(2)}) copy-start(bf16[768,768]{1,0:T(8,128)(2,1)} %param.22) | copy-start | bytes 3538948
  7.2 8.3 copy-start.20
  7.2 9.5 copy-start.26
  7.2 10.4 copy-start.27
  7.2 37.6 %all-gather.14.cloned.1.call-start = ((), (), s32[]{:S(2)}) async-start(), calls=%async_computation.18 | async-start | bytes 2359296 | tf_op jit(solution)/shard_map/all_gather | solution.py:33
  14.8 144.6 %reduce-scatter.19.cloned.1.call-start = ((), (), s32[]{:S(2)}) async-start(), calls=%async_computation.19 | async-start | bytes 4718592 | tf_op jit(solution)/shard_map/reduce_scatter | solution.py:41
  69.0 2.4 slice-start
  73.0 5.5 copy-start.8
  74.3 26.3 %copy-start.14 = (bf16[1024,2,128]{2,1,0:T(2,128)(2,1)}, bf16[1024,2,128]{2,1,0:T(2,128)(2,1)S(1)}, u32[]{:S(2)}) copy-start(bf16[1024,2,128]{2,1,0:T(2,128)(2,1)S(1)} %reshape.196) | copy-start | bytes 1572868
  90.4 10.3 copy-start.30
  100.6 10.9 copy-start.32
  115.9 43.6 %copy-start.3 = (bf16[512,768]{1,0:T(8,128)(2,1)S(1)}, bf16[512,768]{1,0:T(8,128)(2,1)}, u32[]{:S(2)}) copy-start(bf16[512,768]{1,0:T(8,128)(2,1)} %param.17) | copy-start | bytes 2359300
  115.9 48.6 %copy-start.34 = (f32[768]{0:T(1024)S(1)}, f32[768]{0:T(1024)}, u32[]{:S(2)}) copy-start(f32[768]{0:T(1024)} %param.23) | copy-start | bytes 9220
  115.9 107.0 %all-gather.16.cloned.1.call-start = ((), (), s32[]{:S(2)}) async-start(), calls=%async_computation.20 | async-start | bytes 2359296 | tf_op jit(solution)/shard_map/all_gather | solution.py:33
  161.2 7.9 copy-start.1
  165.6 149.0 %all-gather.22.cloned.1.call-start = ((), (), s32[]{:S(2)}) async-start(), calls=%async_computation.26 | async-start | bytes 2359296 | tf_op jit(solution)/shard_map/all_gather | solution.py:33
  166.2 239.9 %reduce-scatter.21.cloned.1.call-start = ((), (), s32[]{:S(2)}) async-start(), calls=%async_computation.21 | async-start | bytes 12582912 | tf_op jit(solution)/shard_map/reduce_scatter | solution.py:280
  167.2 47.0 %copy-start.5 = (s32[1024,6]{1,0:T(8,128)}, s32[1024,6]{1,0:T(8,128)S(1)}, u32[]{:S(2)}) copy-start(s32[1024,6]{1,0:T(8,128)S(1)} %copy.67) | copy-start | bytes 73732
  290.0 122.6 %reduce-scatter.27.cloned.1.call-start = ((), (), s32[]{:S(2)}) async-start(), calls=%async_computation.27 | async-start | bytes 6291456 | tf_op jit(solution)/shard_map/reduce_scatter | solution.py:325
  291.0 23.6 %copy-start.11 = (f32[1024,6]{1,0:T(8,128)}, f32[1024,6]{1,0:T(8,128)S(1)}, u32[]{:S(2)}) copy-start(f32[1024,6]{1,0:T(8,128)S(1)} %copy.64) | copy-start | bytes 73732
  314.6 56.0 %copy-start.17 = (f32[512,16]{0,1:T(8,128)}, f32[512,16]{0,1:T(8,128)S(1)}, u32[]{:S(2)}) copy-start(f32[512,16]{0,1:T(8,128)S(1)} %copy.75) | copy-start | bytes 98308
  384.5 12.4 copy-start.21
  384.5 15.0 copy-start.19
  384.5 37.0 %reduce-scatter.23.cloned.1.call-start = ((), (), s32[]{:S(2)}) async-start(), calls=%async_computation.23 | async-start | bytes 3145728 | tf_op jit(solution)/shard_map/reduce_scatter | solution.py:283
  399.4 3.2 copy-start.22
  402.6 21.8 %reduce-scatter.29.cloned.1.call-start = ((), (), s32[]{:S(2)}) async-start(), calls=%async_computation.29 | async-start | bytes 1572864 | tf_op jit(solution)/shard_map/reduce_scatter | solution.py:328
  406.1 40.0 %all-gather.24.cloned.1.call-start = ((), (), s32[]{:S(2)}) async-start(), calls=%async_computation.28 | async-start | bytes 12582912 | tf_op jit(solution)/shard_map/all_gather | solution.py:335
  421.5 149.2 %all-gather.26.cloned.1.call-start = ((), (), s32[]{:S(2)}) async-start(), calls=%async_computation.30 | async-start | bytes 3145728 | tf_op jit(solution)/shard_map/all_gather | solution.py:336
  426.9 1.9 copy-start.29
  426.9 2.4 copy-start.6
  428.0 149.2 %all-gather.18.cloned.1.call-start = ((), (), s32[]{:S(2)}) async-start(), calls=%async_computation.22 | async-start | bytes 6291456 | tf_op jit(solution)/shard_map/all_gather | solution.py:294
  428.8 263.7 %all-gather.20.cloned.1.call-start = ((), (), s32[]{:S(2)}) async-start(), calls=%async_computation.24 | async-start | bytes 1572864 | tf_op jit(solution)/shard_map/all_gather | solution.py:295
  429.8 267.6 %reduce-scatter.31.cloned.1.call-start = ((), (), s32[]{:S(2)}) async-start(), calls=%async_computation.31 | async-start | bytes 4718592 | tf_op jit(solution)/shard_map/reduce_scatter | solution.py:41
  550.4 20.3 copy-start.25
  576.7 165.4 %reduce-scatter.25.cloned.1.call-start = ((), (), s32[]{:S(2)}) async-start(), calls=%async_computation.25 | async-start | bytes 4718592 | tf_op jit(solution)/shard_map/reduce_scatter | solution.py:41
  656.4 21.8 %copy-start.12 = (f32[1024,6]{1,0:T(8,128)S(1)}, f32[1024,6]{1,0:T(8,128)}, u32[]{:S(2)}) copy-start(f32[1024,6]{1,0:T(8,128)} %copy-done.11) | copy-start | bytes 73732
  678.2 14.2 copy-start.23
  697.3 44.9 %copy-start.13 = (bf16[512,768]{1,0:T(8,128)(2,1)S(1)}, bf16[512,768]{1,0:T(8,128)(2,1)}, u32[]{:S(2)}) copy-start(bf16[512,768]{1,0:T(8,128)(2,1)} %param.33) | copy-start | bytes 2359300
  697.3 76.3 %all-gather.28.cloned.1.call-start = ((), (), s32[]{:S(2)}) async-start(), calls=%async_computation.32 | async-start | bytes 2359296 | tf_op jit(solution)/shard_map/all_gather | solution.py:33
  746.3 52.3 %all-reduce.6.cloned.1.call-start = ((), (), s32[]{:S(2)}) async-start(), calls=%async_computation.33 | async-start | bytes 3145728 | tf_op jit(solution)/shard_map/psum | solution.py:365
  778.1 143.4 %reduce-scatter.41.cloned.1.call-start = ((), (), s32[]{:S(2)}) async-start(), calls=%async_computation.39 | async-start | bytes 1327104 | tf_op jit(solution)/shard_map/reduce_scatter | solution.py:103
  778.2 20.5 copy-start.15
  782.6 154.1 %reduce-scatter.35.cloned.1.call-start = ((), (), s32[]{:S(2)}) async-start(), calls=%async_computation.35 | async-start | bytes 1327104 | tf_op jit(solution)/shard_map/reduce_scatter | solution.py:94
  814.6 21.7 %copy-start.9 = (bf16[1024,768]{0,1:T(8,128)(2,1)S(1)}, bf16[1024,768]{0,1:T(8,128)(2,1)}, u32[]{:S(2)}) copy-start(bf16[1024,768]{0,1:T(8,128)(2,1)} %copy.59) | copy-start | bytes 4718596
  836.3 9.7 copy-start.16
  846.0 7.7 copy-start.7
  870.9 186.3 %reduce-scatter.47.cloned.1.call-start = ((), (), s32[]{:S(2)}) async-start(), calls=%async_computation.45 | async-start | bytes 7077888 | tf_op jit(solution)/shard_map/reduce_scatter | solution.py:57
  885.2 293.2 %reduce-scatter.43.cloned.1.call-start = ((), (), s32[]{:S(2)}) async-start(), calls=%async_computation.41 | async-start | bytes 7077888 | tf_op jit(solution)/shard_map/reduce_scatter | solution.py:51
  909.5 390.1 %reduce-scatter.45.cloned.1.call-start = ((), (), s32[]{:S(2)}) async-start(), calls=%async_computation.43 | async-start | bytes 7077888 | tf_op jit(solution)/shard_map/reduce_scatter | solution.py:54
  910.3 454.9 %reduce-scatter.53.cloned.1.call-start = ((), (), s32[]{:S(2)}) async-start(), calls=%async_computation.49 | async-start | bytes 884736 | tf_op jit(solution)/shard_map/reduce_scatter | solution.py:66
  914.0 516.7 %reduce-scatter.51.cloned.1.call-start = ((), (), s32[]{:S(2)}) async-start(), calls=%async_computation.48 | async-start | bytes 884736 | tf_op jit(solution)/shard_map/reduce_scatter | solution.py:63
  919.2 577.1 %reduce-scatter.49.cloned.1.call-start = ((), (), s32[]{:S(2)}) async-start(), calls=%async_computation.47 | async-start | bytes 884736 | tf_op jit(solution)/shard_map/reduce_scatter | solution.py:60
  919.8 640.6 %reduce-scatter.39.cloned.1.call-start = ((), (), s32[]{:S(2)}) async-start(), calls=%async_computation.38 | async-start | bytes 442368 | tf_op jit(solution)/shard_map/reduce_scatter | solution.py:100
  920.8 703.5 %reduce-scatter.37.cloned.1.call-start = ((), (), s32[]{:S(2)}) async-start(), calls=%async_computation.37 | async-start | bytes 442368 | tf_op jit(solution)/shard_map/reduce_scatter | solution.py:97
  921.4 746.3 %all-gather.32.cloned.1.call-start = ((), (), s32[]{:S(2)}) async-start(), calls=%async_computation.40 | async-start | bytes 1327104 | tf_op jit(solution)/shard_map/all_gather | solution.py:117
  922.0 788.1 %all-gather.30.cloned.1.call-start = ((), (), s32[]{:S(2)}) async-start(), calls=%async_computation.36 | async-start | bytes 1327104 | tf_op jit(solution)/shard_map/all_gather | solution.py:108
  936.7 818.4 %reduce-scatter.33.cloned.1.call-start = ((), (), s32[]{:S(2)}) async-start(), calls=%async_computation.34 | async-start | bytes 4718592 | tf_op jit(solution)/shard_map/reduce_scatter | solution.py:41
  943.3 914.1 %all-gather.38.cloned.1.call-start = ((), (), s32[]{:S(2)}) async-start(), calls=%async_computation.46 | async-start | bytes 7077888 | tf_op jit(solution)/shard_map/all_gather | solution.py:77
  1057.3 899.6 %all-gather.34.cloned.1.call-start = ((), (), s32[]{:S(2)}) async-start(), calls=%async_computation.42 | async-start | bytes 7077888 | tf_op jit(solution)/shard_map/all_gather | solution.py:71
  1178.4 877.9 %all-gather.36.cloned.1.call-start = ((), (), s32[]{:S(2)}) async-start(), calls=%async_computation.44 | async-start | bytes 7077888 | tf_op jit(solution)/shard_map/all_gather | solution.py:74
  1656.8 98.3 %copy-start.4 = (bf16[512,768]{1,0:T(8,128)(2,1)S(1)}, bf16[512,768]{1,0:T(8,128)(2,1)}, u32[]{:S(2)}) copy-start(bf16[512,768]{1,0:T(8,128)(2,1)} %param.17) | copy-start | bytes 2359300
  1656.8 98.3 %copy-start.36 = (f32[768]{0:T(1024)S(1)}, f32[768]{0:T(1024)}, u32[]{:S(2)}) copy-start(f32[768]{0:T(1024)} %param.18) | copy-start | bytes 9220
  1656.9 98.3 %copy-start.38 = (f32[512]{0:T(512)S(1)}, f32[512]{0:T(512)}, u32[]{:S(2)}) copy-start(f32[512]{0:T(512)} %copy-done.37) | copy-start | bytes 6148
  1755.2 49.6 %copy-start.10 = (f32[512,768]{1,0:T(8,128)S(1)}, f32[512,768]{1,0:T(8,128)}, u32[]{:S(2)}) copy-start(f32[512,768]{1,0:T(8,128)} %reduce-scatter.33.cloned.1.call-done) | copy-start | bytes 4718596
  (12 other events, 14.8 us)
Sparse Core Ops, SparseCore 0:
  15.0 29.7 all-gather.13
  116.1 43.3 reduce-scatter.18
  165.7 27.2 all-gather.15
  194.4 27.1 all-gather.21
  290.2 16.7 reduce-scatter.20
  384.6 12.0 reduce-scatter.26
  402.7 9.6 reduce-scatter.22
  414.7 9.6 reduce-scatter.28
  426.6 19.4 all-gather.23
  448.1 11.7 all-gather.25
  462.1 14.1 all-gather.17
  478.3 10.2 all-gather.19
  576.9 44.5 reduce-scatter.30
  697.5 44.6 reduce-scatter.24
  746.4 27.1 all-gather.27
  778.2 20.3 all-reduce.5
  802.5 65.0 reduce-scatter.40
  871.4 65.2 reduce-scatter.34
  940.3 116.8 reduce-scatter.46
  1061.2 117.0 reduce-scatter.42
  1182.5 117.0 reduce-scatter.44
  1303.5 61.5 reduce-scatter.52
  1369.4 61.2 reduce-scatter.50
  1434.4 61.8 reduce-scatter.48
  1499.9 60.4 reduce-scatter.38
  1563.9 60.3 reduce-scatter.36
  1626.6 41.0 all-gather.31
  1670.1 39.9 all-gather.29
  1713.0 42.0 reduce-scatter.32
  1757.2 100.1 all-gather.37
  1859.6 97.1 all-gather.33
  1959.1 97.1 all-gather.35
where the time goes:
time: 2090 us; the launch traced here: 2070 us
  waiting for transfers between devices  1050 us (50%)
  local copies, waits for them, and re-layouts  397 us (19%)
  blocking collectives  235 us (11%)
  matrix products  211 us (10%)
  other arithmetic  146 us (7%)
    reduce_scatter x4, waiting for transfers between devices, row_total(): lax.psum_scatter(function(jnp.int32(0), lax.axis_size('row') * row_count)...  124 us
    reduce_scatter x1, waiting for transfers between devices, sum_ffn_grads(): lax.psum_scatter(grad_up.astype(jnp.bfloat16), 'dp', scatter_dimension=1,...  121 us
    reduce_scatter x1, waiting for transfers between devices, sum_ffn_grads(): lax.psum_scatter(grad_gate.astype(jnp.bfloat16), 'dp', scatter_dimension=...  121 us
    reduce_scatter x1, waiting for transfers between devices, sum_ffn_grads(): lax.psum_scatter(grad_down.astype(jnp.bfloat16), 'dp', scatter_dimension=...  114 us
    all_gather x1, waiting for transfers between devices, sum_ffn_grads(): lax.all_gather(shares[1].astype(jnp.bfloat16), 'dp', axis=1, tiled=True)  90.5 us
    all_gather x1, waiting for transfers between devices, sum_ffn_grads(): lax.all_gather(shares[0].astype(jnp.bfloat16), 'dp', axis=1, tiled=True)  89.9 us
    reduce_scatter x1, waiting for transfers between devices, sum_ffn_grads(): lax.psum_scatter(grad_sdown.astype(jnp.bfloat16), 'dp', scatter_dimension...  65.5 us
    gather x2, local copies, waits for them, and re-layouts, ffn_rows(): routed = jnp.sum(gate_weights[:, :, None] * expert_out[pair_slots], axis=1)  60 us
  transfers between devices with their start and end apart: 32, of which 22 were waited for; matrix products, arithmetic and copies ran while one was open for 32% of the time, Pallas kernels for 0%

commit v1 on v0

v1 whole, which is shorter than its diff:
```python
import functools

import jax
import jax.numpy as jnp
from jax import lax
from jax.experimental import pallas as pl
from jax.experimental.pallas import tpu as pltpu
from jax.sharding import PartitionSpec as P

D = 1536
HQ = 12
HK = 4
DH = 128
GROUP_HEADS = HQ // HK
LANES = 128

EPSILON = 1e-05
F32 = jnp.float32
BF16 = jnp.bfloat16
VMEM_LIMIT = 56 * 1024 * 1024


def params(*semantics):
    return pltpu.CompilerParams(
        dimension_semantics=semantics or None, vmem_limit_bytes=VMEM_LIMIT
    )


def dot(left, right):
    return jnp.dot(left, right, preferred_element_type=F32)


def dot_nt(left, right):
    return lax.dot_general(left, right, (((1,), (1,)), ((), ())), preferred_element_type=F32)


def dot_tn(left, right):
    return lax.dot_general(left, right, (((0,), (0,)), ((), ())), preferred_element_type=F32)


def swap(values, axis):
    return lax.ppermute(values, axis, [(0, 1), (1, 0)])


def halves(values, axis, mine):
    size = values.shape[axis] // 2
    low = lax.slice_in_dim(values, 0, size, axis=axis)
    high = lax.slice_in_dim(values, size, 2 * size, axis=axis)
    return jnp.where(mine == 0, low, high), jnp.where(mine == 0, high, low)


def in_order(own, other, mine, axis):
    return jnp.concatenate(
        [jnp.where(mine == 0, own, other), jnp.where(mine == 0, other, own)], axis=axis
    )


def attend_kernel(place_ref, own_ref, other_ref, out_ref, all_ref):
    row = place_ref[0]
    length = place_ref[1]
    rows = own_ref.shape[0]
    all_ref[pl.ds(pl.multiple_of(row * rows, rows), rows), :] = own_ref[...]
    all_ref[pl.ds(pl.multiple_of((1 - row) * rows, rows), rows), :] = other_ref[...]
    block = 256
    width = GROUP_HEADS * DH
    for at in range(2 * rows // block):
        first, keys = at * block, (at + 1) * block
        query = jnp.concatenate(
            [
                all_ref[first : first + block, h * DH : (h + 1) * DH]
                for h in range(GROUP_HEADS)
            ],
            axis=0,
        )
        key = all_ref[0:keys, width : width + DH]
        value = all_ref[0:keys, width + DH : width + 2 * DH]
        scores = dot_nt(query, key) * DH ** (-0.5)
        shape = (block, keys)
        query_at = lax.broadcasted_iota(jnp.int32, shape, 0) + first
        key_at = lax.broadcasted_iota(jnp.int32, shape, 1)
        allowed = (key_at <= query_at) & (key_at < length)
        allowed = jnp.concatenate([allowed] * GROUP_HEADS, axis=0)
        scores = jnp.where(allowed, scores, -1e30)
        weights = jnp.exp(scores - jnp.max(scores, axis=1, keepdims=True))
        probs = weights * (1.0 / jnp.sum(weights, axis=1, keepdims=True))
        result = dot(probs.astype(BF16), value).astype(BF16)
        for h in range(GROUP_HEADS):
            out_ref[first : first + block, h * DH : (h + 1) * DH] = result[
                h * block : (h + 1) * block
            ]


def attend(place, own, other):
    rows, width = own.shape
    spec = pl.BlockSpec(memory_space=pltpu.VMEM)
    return pl.pallas_call(
        attend_kernel,
        out_shape=jax.ShapeDtypeStruct((2 * rows, GROUP_HEADS * DH), BF16),
        in_specs=[pl.BlockSpec(memory_space=pltpu.SMEM), spec, spec],
        out_specs=spec,
        scratch_shapes=[pltpu.VMEM((2 * rows, width), BF16)],
        compiler_params=params(),
        cost_estimate=pl.CostEstimate(
            flops=4 * 2 * rows * rows * width, bytes_accessed=8 * rows * width, transcendentals=0
        ),
        name="attend",
    )(place, own, other)


def attend_back(qkv, attended_grad, length):
    seq = qkv.shape[0]
    width = GROUP_HEADS * DH
    queries = qkv[:, :width].reshape(seq, GROUP_HEADS, DH)
    key, value = qkv[:, width : width + DH], qkv[:, width + DH :]
    grads = attended_grad.reshape(seq, GROUP_HEADS, DH)
    scale = DH ** (-0.5)
    scores = jnp.einsum("qrd,kd->rqk", queries, key, preferred_element_type=F32) * scale
    position = jnp.arange(seq, dtype=jnp.int32)
    allowed = (position[None, :] <= position[:, None]) & (position[None, :] < length)
    scores = jnp.where(allowed, scores, -1e30)
    weights = jnp.exp(scores - jnp.max(scores, axis=-1, keepdims=True))
    probs = weights / jnp.sum(weights, axis=-1, keepdims=True)
    probs_grad = jnp.einsum("qrd,kd->rqk", grads, value, preferred_element_type=F32)
    carried = jnp.sum(probs * probs_grad, axis=-1, keepdims=True)
    score_grad = (probs * (probs_grad - carried)).astype(BF16)
    query_back = jnp.einsum("rqk,kd->qrd", score_grad, key, preferred_element_type=F32) * scale
    key_back = jnp.einsum("rqk,qrd->kd", score_grad, queries, preferred_element_type=F32) * scale
    value_back = jnp.einsum(
        "rqk,qrd->kd", probs.astype(BF16), grads, preferred_element_type=F32
    )
    return jnp.concatenate(
        [query_back.reshape(seq, width), key_back, value_back], axis=1
    ).astype(BF16)


def hidden_kernel(tokens_ref, a0, a1, a2, a3, w0, w1, w2, w3, hidden_ref, square_ref):
    hidden = tokens_ref[...].astype(F32)
    for a, w in ((a0, w0), (a1, w1), (a2, w2), (a3, w3)):
        hidden = hidden + dot(a[...], w[...])
    hidden_ref[...] = hidden
    square_ref[...] = jnp.sum(hidden * hidden, axis=1, keepdims=True)


def hidden_rows(tokens, attended, weights):
    rows, features = tokens.shape
    heads = attended[0].shape[1]
    tile = 256

    def rowwise(width):
        return pl.BlockSpec((tile, width), lambda i: (i, 0))

    def whole(width):
        return pl.BlockSpec((width, features), lambda i: (0, 0))

    return pl.pallas_call(
        hidden_kernel,
        grid=(rows // tile,),
        out_shape=(
            jax.ShapeDtypeStruct((rows, features), F32),
            jax.ShapeDtypeStruct((rows, 1), F32),
        ),
        in_specs=[rowwise(features)] + [rowwise(heads)] * 4 + [whole(heads)] * 4,
        out_specs=(rowwise(features), rowwise(1)),
        compiler_params=params("arbitrary"),
        cost_estimate=pl.CostEstimate(
            flops=8 * rows * features * heads,
            bytes_accessed=10 * rows * features,
            transcendentals=0,
        ),
        name="hidden_rows",
    )(tokens, *attended, *weights)


def expert_kernel(routed, order_ref, *refs):
    (x_own, x_other, x_turned, o_own, o_other, routes, gates) = refs[:7]
    weights = refs[7:15]
    grads = refs[15:17]
    pair_refs = refs[17:19]
    inner_refs = refs[19:21]
    step = pl.program_id(0)
    rows = x_own.shape[0]
    features = x_own.shape[1]
    tile = 256
    up_own = jnp.concatenate([weights[0][0], weights[4][0]], axis=1)
    up_other = jnp.concatenate([weights[1][0], weights[5][0]], axis=1)
    down_own = jnp.concatenate([weights[2][0], weights[6][0]], axis=0)
    down_other = jnp.concatenate([weights[3][0], weights[7][0]], axis=0)

    def token_tile(t, carry):
        at = pl.ds(pl.multiple_of(t * tile, tile), tile)
        pre = dot(x_own[at, :], up_own) + dot(x_other[at, :], up_other)
        back = dot_nt(o_own[at, :], down_own) + dot_nt(o_other[at, :], down_other)
        for k in range(2):
            expert = order_ref[2 * step + k]
            chosen = jnp.where(routes[at, :] == expert, gates[at, :], 0.0)
            gate = jnp.sum(chosen, axis=1, keepdims=True)
            gate = jnp.where(expert >= routed, 1.0, gate)
            pre_gate = pre[:, 2 * k * LANES : (2 * k + 1) * LANES]
            pre_up = pre[:, (2 * k + 1) * LANES : (2 * k + 2) * LANES]
            inner_grad = gate * back[:, k * LANES : (k + 1) * LANES]
            sigmoid = 1.0 / (1.0 + jnp.exp(-pre_gate))
            silu = pre_gate * sigmoid
            inner_refs[k][0, at, :] = (gate * (silu * pre_up)).astype(BF16)
            gate_grad = inner_grad * pre_up * (sigmoid * (1.0 + pre_gate * (1.0 - sigmoid)))
            pair_refs[k][0, at, 0:LANES] = gate_grad.astype(BF16)
            pair_refs[k][0, at, LANES : 2 * LANES] = (inner_grad * silu).astype(BF16)
        return carry

    lax.fori_loop(0, rows // tile, token_tile, 0)
    for k in range(2):
        pairs = pair_refs[k][0]

        def feature_tile(t, carry, k=k, pairs=pairs):
            at = pl.ds(pl.multiple_of(t * tile, tile), tile)
            grads[k][0, at, 0 : 2 * LANES] = dot(x_turned[at, :], pairs).astype(BF16)
            return carry

        lax.fori_loop(0, 2 * features // tile, feature_tile, 0)
    inner = jnp.concatenate([inner_refs[0][0], inner_refs[1][0]], axis=1)
    turned = inner.T
    for h, o in enumerate((o_own, o_other)):
        for j in range(features // tile):
            down = dot(turned, o[:, j * tile : (j + 1) * tile]).astype(BF16)
            for k in range(2):
                for b in range(tile // LANES):
                    at = h * features + j * tile + b * LANES
                    grads[k][0, at : at + LANES, 2 * LANES :] = down[
                        k * LANES : (k + 1) * LANES, b * LANES : (b + 1) * LANES
                    ]


def expert_grads(routed, order, x_own, x_other, x_turned, o_own, o_other, routes, gates, weights):
    steps = order.shape[0] // 2
    rows, features = x_own.shape
    choices = routes.shape[1]
    hidden = weights[2].shape[1]

    def fixed(*shape):
        return pl.BlockSpec(shape, lambda i, o: (0,) * len(shape))

    def picked(k, *shape):
        return pl.BlockSpec((1, *shape), lambda i, o: (o[2 * i + k], 0, 0))

    def stepped(*shape):
        return pl.BlockSpec((1, *shape), lambda i, o: (i, 0, 0))

    weight_specs = []
    for k in range(2):
        weight_specs += [
            picked(k, features, 2 * hidden),
            picked(k, features, 2 * hidden),
            picked(k, hidden, features),
            picked(k, hidden, features),
        ]
    return pl.pallas_call(
        functools.partial(expert_kernel, routed),
        grid_spec=pltpu.PrefetchScalarGridSpec(
            num_scalar_prefetch=1,
            grid=(steps,),
            in_specs=[
                fixed(rows, features),
                fixed(rows, features),
                fixed(2 * features, rows),
                fixed(rows, features),
                fixed(rows, features),
                fixed(rows, choices),
                fixed(rows, choices),
            ]
            + weight_specs,
            out_specs=[stepped(2 * features, 3 * hidden)] * 2
            + [stepped(rows, 2 * hidden)] * 2
            + [stepped(rows, hidden)] * 2,
        ),
        out_shape=[jax.ShapeDtypeStruct((steps, 2 * features, 3 * hidden), BF16)] * 2
        + [jax.ShapeDtypeStruct((steps, rows, 2 * hidden), BF16)] * 2
        + [jax.ShapeDtypeStruct((steps, rows, hidden), BF16)] * 2,
        compiler_params=params("arbitrary"),
        cost_estimate=pl.CostEstimate(
            flops=steps * 24 * rows * features * hidden * 2,
            bytes_accessed=12 * rows * features + steps * 12 * features * hidden * 2,
            transcendentals=0,
        ),
        name="expert_grads",
    )(order, x_own, x_other, x_turned, o_own, o_other, routes, gates, *weights, *weights)


def combine_kernel(order_ref, *refs):
    pairs = refs[0:2]
    inners = refs[2:4]
    weights = refs[4:12]
    out_own, out_other, back_own, back_other = refs[12:16]
    step = pl.program_id(0)
    rows, features = out_own.shape
    tile = 256
    up = [
        jnp.concatenate([weights[h][0], weights[4 + h][0]], axis=1) for h in range(2)
    ]
    down = [
        jnp.concatenate([weights[2 + h][0], weights[6 + h][0]], axis=0) for h in range(2)
    ]

    def token_tile(t, carry):
        at = pl.ds(pl.multiple_of(t * tile, tile), tile)
        pair = jnp.concatenate([pairs[0][0, at, :], pairs[1][0, at, :]], axis=1)
        inner = jnp.concatenate([inners[0][0, at, :], inners[1][0, at, :]], axis=1)
        for h, (out, back) in enumerate(((out_own, back_own), (out_other, back_other))):
            out_term = dot(inner, down[h])
            back_term = dot_nt(pair, up[h])

            @pl.when(step == 0)
            def _():
                out[at, :] = out_term
                back[at, :] = back_term

            @pl.when(step > 0)
            def _():
                out[at, :] += out_term
                back[at, :] += back_term

        return carry

    lax.fori_loop(0, rows // tile, token_tile, 0)


def combine(order, pairs, inners, weights):
    steps, rows, double = pairs[0].shape
    hidden = double // 2
    features = weights[0].shape[1]

    def picked(k, *shape):
        return pl.BlockSpec((1, *shape), lambda i, o: (o[2 * i + k], 0, 0))

    def stepped(*shape):
        return pl.BlockSpec((1, *shape), lambda i, o: (i, 0, 0))

    weight_specs = []
    for k in range(2):
        weight_specs += [
            picked(k, features, 2 * hidden),
            picked(k, features, 2 * hidden),
            picked(k, hidden, features),
            picked(k, hidden, features),
        ]
    return pl.pallas_call(
        combine_kernel,
        grid_spec=pltpu.PrefetchScalarGridSpec(
            num_scalar_prefetch=1,
            grid=(steps,),
            in_specs=[stepped(rows, 2 * hidden)] * 2
            + [stepped(rows, hidden)] * 2
            + weight_specs,
            out_specs=[pl.BlockSpec((rows, features), lambda i, o: (0, 0))] * 4,
        ),
        out_shape=[jax.ShapeDtypeStruct((rows, features), F32)] * 4,
        compiler_params=params("arbitrary"),
        cost_estimate=pl.CostEstimate(
            flops=steps * 24 * rows * features * hidden,
            bytes_accessed=16 * rows * features,
            transcendentals=0,
        ),
        name="combine",
    )(order, *pairs, *inners, *weights, *weights)


def ring_of(size):
    return list(range(0, size, 2)) + list(range(1, size, 2))[::-1]


def unpack_kernel(aliased, index_ref, *refs):
    right_ref, left_ref = refs[0:2]
    gate_ref, up_ref, down_ref = refs[2 + aliased : 5 + aliased]
    blocks = right_ref.shape[1] // LANES

    def write(chunk_ref):
        for c in range(2):
            base = 3 * LANES * c
            to = slice(c * LANES, (c + 1) * LANES)
            gate_ref[0, :, to] = chunk_ref[0, :, base : base + LANES].astype(F32)
            up_ref[0, :, to] = chunk_ref[0, :, base + LANES : base + 2 * LANES].astype(F32)
            for b in range(blocks):
                down_ref[0, to, b * LANES : (b + 1) * LANES] = chunk_ref[
                    0, b * LANES : (b + 1) * LANES, base + 2 * LANES : base + 3 * LANES
                ].astype(F32)

    pl.when(pl.program_id(1) == 0)(lambda: write(right_ref))
    pl.when(pl.program_id(1) == 1)(lambda: write(left_ref))


def unpack(index, right, left, shapes, outs):
    count, rows, width = right.shape
    chunk = pl.BlockSpec((1, rows, width), lambda i, d, n: (i, 0, 0))

    def placed(shape):
        return pl.BlockSpec((1, *shape[1:]), lambda i, d, n: (n[2 * i + d], 0, 0))

    aliased = len(outs)
    return pl.pallas_call(
        functools.partial(unpack_kernel, aliased),
        grid_spec=pltpu.PrefetchScalarGridSpec(
            num_scalar_prefetch=1,
            grid=(count, 2),
            in_specs=[chunk, chunk] + [pl.BlockSpec(memory_space=pl.ANY)] * aliased,
            out_specs=[placed(shape) for shape in shapes],
        ),
        out_shape=[jax.ShapeDtypeStruct(shape, F32) for shape in shapes],
        input_output_aliases={3 + k: k for k in range(aliased)},
        compiler_params=params("arbitrary", "arbitrary"),
        cost_estimate=pl.CostEstimate(
            flops=0, bytes_accessed=count * rows * width * 12, transcendentals=0
        ),
        name="unpack",
    )(index, right, left, *outs)


def add_rounded(left, right):
    return (left.astype(F32) + right.astype(F32)).astype(BF16)


def body(
    tokens_in,
    norm_gain_attn,
    w_query,
    w_key,
    w_value,
    w_out,
    norm_gain_ffn,
    w_gate,
    w_up,
    w_down,
    w_shared_gate,
    w_shared_up,
    w_shared_down,
    routes,
    gate_weights,
    seq_lengths,
    out_grad,
):
    row = lax.axis_index("row")
    col = lax.axis_index("col")
    dp = lax.axis_index("dp")
    dp_size = lax.axis_size("dp")
    local_rows, local_features = tokens_in.shape
    experts = w_gate.shape[0]
    hidden_part = w_gate.shape[2] // 2
    group_width = GROUP_HEADS * DH

    ring_size = min(8, dp_size)
    ring = ring_of(ring_size)
    starts = range(0, dp_size, ring_size)
    to_right = [
        (g + ring[k], g + ring[(k + 1) % ring_size]) for g in starts for k in range(ring_size)
    ]
    to_left = [(b, a) for a, b in to_right]
    place_of = [ring.index(k) for k in range(ring_size)]
    place = jnp.asarray(place_of, jnp.int32)[dp % ring_size]
    peers = [[g + k for g in starts] for k in range(ring_size)]

    def across_rings(values):
        if len(starts) == 1:
            return values
        return lax.psum(values, "dp", axis_index_groups=peers)

    def send(values, left):
        if ring_size == 1:
            return values
        return lax.ppermute(values, "dp", to_left if left else to_right)

    tokens_y = swap(tokens_in, "row")
    tokens_c = swap(tokens_in, "col")
    gains = jnp.stack([norm_gain_attn, norm_gain_ffn])
    gains_c = swap(gains, "col")

    query_own, query_send = halves(w_query, 1, col)
    key_own, key_send = halves(w_key, 1, col)
    value_own, value_send = halves(w_value, 1, col)
    project_own = jnp.concatenate([query_own, key_own, value_own], axis=1)
    project_other = swap(jnp.concatenate([query_send, key_send, value_send], axis=1), "col")

    def project(own, other):
        own, other = own.astype(F32), other.astype(F32)
        total = jnp.sum(own * own, axis=1) + jnp.sum(other * other, axis=1)
        scale = lax.rsqrt(total / D + EPSILON)[:, None]
        own = (own * scale * gains[0]).astype(BF16)
        other = (other * scale * gains_c[0]).astype(BF16)
        qkv = (dot(own, project_own) + dot(other, project_other)).astype(BF16)
        return own, other, qkv, scale

    tokens_yc = swap(tokens_y, "col")
    near = project(tokens_in, tokens_c)
    far = project(tokens_y, tokens_yc)
    grad_y = swap(out_grad, "row")
    grad_own = in_order(out_grad, grad_y, row, 0)
    grad_other = swap(grad_own, "col")

    gate_own, gate_send = halves(w_gate, 2, col)
    up_own, up_send = halves(w_up, 2, col)
    down_own, down_send = halves(w_down, 1, col)
    sgate_own, sgate_send = halves(w_shared_gate, 1, col)
    sup_own, sup_send = halves(w_shared_up, 1, col)
    sdown_own, sdown_send = halves(w_shared_down, 0, col)
    shared_blocks = sgate_own.shape[1] // hidden_part

    def blocks(values):
        return values.reshape(local_features, shared_blocks, hidden_part).transpose(1, 0, 2)

    def down_blocks(values):
        return values.reshape(shared_blocks, hidden_part, local_features)

    def widen(gate, up, shared_gate, shared_up):
        return jnp.concatenate(
            [
                jnp.concatenate([gate, up], axis=2),
                jnp.concatenate([blocks(shared_gate), blocks(shared_up)], axis=2),
            ],
            axis=0,
        )

    up_mine = widen(gate_own, up_own, sgate_own, sup_own)
    up_theirs = swap(widen(gate_send, up_send, sgate_send, sup_send), "col")
    down_mine = jnp.concatenate([down_own, down_blocks(sdown_own)], axis=0)
    down_theirs = swap(jnp.concatenate([down_send, down_blocks(sdown_send)], axis=0), "col")
    expert_weights = [up_mine, up_theirs, down_mine, down_theirs]

    where = jnp.stack([row, seq_lengths[0]])
    attended = attend(where, near[2], far[2])
    attended_y = swap(attended, "row")
    attended_c = swap(attended, "col")
    attended_yc = swap(attended_y, "col")
    out_own, out_other = halves(w_out, 0, col)
    out_y_own, out_y_other = halves(swap(w_out, "row"), 0, col)
    tokens = in_order(tokens_in, tokens_y, row, 0)
    hidden, squares = hidden_rows(
        tokens,
        [attended, attended_c, attended_y, attended_yc],
        [out_own, out_other, out_y_own, out_y_other],
    )
    squares = squares + swap(squares, "col")
    scale_ffn = lax.rsqrt(squares / D + EPSILON)
    x_own = (hidden * scale_ffn * norm_gain_ffn).astype(BF16)
    x_other = swap(x_own, "col")
    x_turned = jnp.concatenate([x_own.T, x_other.T], axis=0)

    each = experts // (2 * ring_size)
    orders = []
    for s in range(ring_size):
        right = (place - s) % ring_size
        left = (place + s) % ring_size
        for k in range(each):
            orders.append(2 * each * right + k)
            orders.append(2 * each * left + each + k)
    for k in range(shared_blocks):
        orders.append(jnp.int32(experts + k))
    order = jnp.stack(orders).astype(jnp.int32)

    def run(first, last):
        return expert_grads(
            experts,
            order[2 * first : 2 * last],
            x_own,
            x_other,
            x_turned,
            grad_own,
            grad_other,
            routes,
            gate_weights,
            expert_weights,
        )

    pairs_total = (experts + shared_blocks) // 2
    cuts = [0] + list(range(each, pairs_total, 2 * each)) + [pairs_total]
    runs = [run(a, b) for a, b in zip(cuts[:-1], cuts[1:], strict=True)]

    def part(which, first, count):
        for a, b, result in zip(cuts[:-1], cuts[1:], runs, strict=True):
            if a <= first and first + count <= b:
                return result[which][first - a : first - a + count]
        raise ValueError

    sums = []
    for left in range(2):
        total = part(left, 0, each)
        for s in range(1, ring_size):
            total = add_rounded(send(total, left), part(left, s * each, each))
        total = across_rings(total)
        mine = total[:, :local_features]
        theirs = swap(total[:, local_features:], "col")
        sums.append(in_order(mine, theirs, col, 2))

    expert_shapes = [w_gate.shape, w_up.shape, w_down.shape]
    expert_outs = ()
    right, left = sums
    for s in range(ring_size):
        at_right = (place + 1 - s) % ring_size
        at_left = (place - 1 + s) % ring_size
        index = []
        for k in range(each):
            index.append(2 * each * at_right + k)
            index.append(2 * each * at_left + each + k)
        expert_outs = unpack(
            jnp.stack(index).astype(jnp.int32), right, left, expert_shapes, expert_outs
        )
        if s + 1 < ring_size:
            right, left = send(right, 0), send(left, 1)
    gate_grad, up_grad, down_grad = expert_outs

    joined = [jnp.concatenate([result[k] for result in runs], axis=0) for k in range(2, 6)]
    sum_own, sum_other, back_own, back_other = combine(
        order, joined[0:2], joined[2:4], expert_weights
    )
    start = row * local_rows

    def my_rows(values):
        return lax.dynamic_slice_in_dim(values, start, local_rows, axis=0)

    def their_rows(values):
        return lax.dynamic_slice_in_dim(values, local_rows - start, local_rows, axis=0)

    ffn_sum = sum_own + swap(sum_other.astype(BF16), "col").astype(F32)
    ffn_rows = my_rows(ffn_sum) + swap(their_rows(ffn_sum).astype(BF16), "row").astype(F32)
    block_out = (my_rows(hidden) + ffn_rows).astype(BF16)

    normed_grad = back_own + swap(back_other.astype(BF16), "col").astype(F32)
    normed_grad = normed_grad + swap(normed_grad.astype(BF16), "row").astype(F32)
    gain_ffn_part = jnp.sum(my_rows(normed_grad * hidden * scale_ffn), axis=0)
    scaled = normed_grad * norm_gain_ffn
    products = jnp.sum(scaled * hidden, axis=1, keepdims=True)
    mean = (products + swap(products, "col")) / D
    hidden_grad = grad_own.astype(F32) + scale_ffn * scaled - hidden * scale_ffn**3 * mean
    attn_grad = hidden_grad.astype(BF16)
    attn_grad_c = swap(attn_grad, "col")

    out_back = swap(out_other, "col")
    attended_grad = (dot_nt(attn_grad, out_own) + dot_nt(attn_grad_c, out_back)).astype(BF16)
    out_grads = [dot_tn(attended, attn_grad), dot_tn(attended, attn_grad_c)]
    qkv = in_order(near[2], far[2], row, 0)
    qkv_grad = attend_back(qkv, attended_grad, seq_lengths[0])
    normed_own = in_order(near[0], far[0], row, 0)
    normed_other = in_order(near[1], far[1], row, 0)
    project_grads = [dot_tn(normed_own, qkv_grad), dot_tn(normed_other, qkv_grad)]
    tokens_back = dot_nt(qkv_grad, project_own)
    tokens_back = tokens_back + swap(
        dot_nt(qkv_grad, project_other).astype(BF16), "col"
    ).astype(F32)
    tokens_back = my_rows(tokens_back) + swap(
        their_rows(tokens_back).astype(BF16), "row"
    ).astype(F32)
    scale_attn = near[3]
    tokens_f32 = tokens_in.astype(F32)
    gain_attn_part = jnp.sum(tokens_back * tokens_f32 * scale_attn, axis=0)
    scaled = tokens_back * norm_gain_attn
    products = jnp.sum(scaled * tokens_f32, axis=1, keepdims=True)
    mean = (products + swap(products, "col")) / D
    tokens_grad = (
        my_rows(hidden_grad) + scale_attn * scaled - tokens_f32 * scale_attn**3 * mean
    ).astype(BF16)
    gain_attn_grad, gain_ffn_grad = lax.psum((gain_attn_part, gain_ffn_part), ("dp", "row"))

    share = local_features // ring_size
    shared_grads = jnp.concatenate([runs[-1][k][-1:] for k in range(2)], axis=0)
    shared_pack = shared_grads.reshape(shared_blocks, 2, ring_size, share, 3 * hidden_part)
    shared_pack = shared_pack.transpose(2, 1, 3, 0, 4).reshape(ring_size, 2, share, -1)
    project_pack = jnp.stack([g.astype(BF16) for g in project_grads])
    project_pack = project_pack.reshape(2, ring_size, share, -1).transpose(1, 0, 2, 3)
    out_pack = jnp.stack([g.astype(BF16) for g in out_grads])
    out_share = group_width // ring_size
    out_pack = out_pack.reshape(2, ring_size, out_share, 2, local_features // 2)
    out_pack = out_pack.transpose(1, 0, 3, 2, 4).reshape(ring_size, 2, share, -1)
    pack = jnp.concatenate([shared_pack, project_pack, out_pack], axis=3)
    middle = pack.shape[3] // 2
    finals = []
    for left in range(2):
        lanes = pack[..., middle:] if left else pack[..., :middle]

        def chunk(s, left=left, lanes=lanes):
            at = (place + s if left else place - s) % ring_size
            return lax.dynamic_index_in_dim(lanes, at, axis=0, keepdims=False)

        total = chunk(0)
        for s in range(1, ring_size):
            total = add_rounded(send(total, left), chunk(s))
        total = across_rings(total)
        current = jnp.stack([total[0], swap(total[1], "col")])
        final = jnp.zeros((ring_size, *current.shape), BF16)
        for s in range(ring_size):
            at = (place - 1 + s if left else place + 1 - s) % ring_size
            final = lax.dynamic_update_index_in_dim(final, current, at, 0)
            if s + 1 < ring_size:
                current = send(current, left)
        finals.append(final)
    final = jnp.concatenate(finals, axis=3)
    final = in_order(final[:, 0:1], final[:, 1:2], col, 1).astype(F32)
    lanes_shared = shared_blocks * 3 * hidden_part
    lanes_project = project_grads[0].shape[1]
    shared_final = final[..., :lanes_shared].reshape(
        ring_size, 2, share, shared_blocks, 3, hidden_part
    )

    def shared_up(which):
        picked = shared_final[:, :, :, :, which]
        return picked.transpose(0, 2, 1, 3, 4).reshape(local_features, -1)

    shared_gate_grad = shared_up(0)
    shared_up_grad = shared_up(1)
    down_final = shared_final[:, :, :, :, 2].transpose(1, 3, 0, 2, 4)
    down_final = down_final.reshape(
        2, shared_blocks, local_features // LANES, hidden_part, LANES
    )
    shared_down_grad = down_final.transpose(0, 1, 3, 2, 4).reshape(-1, local_features)
    project_final = final[..., lanes_shared : lanes_shared + lanes_project]
    project_final = project_final.transpose(0, 2, 1, 3).reshape(local_features, 2, -1)
    query_grad = project_final[:, :, :group_width].reshape(local_features, -1)
    key_grad = project_final[:, :, group_width : group_width + DH].reshape(local_features, -1)
    value_grad = project_final[:, :, group_width + DH :].reshape(local_features, -1)
    out_final = final[..., lanes_shared + lanes_project :]
    out_final = out_final.reshape(ring_size, 2, 2, out_share, local_features // 2)
    out_proj_grad = out_final.transpose(1, 0, 3, 2, 4).reshape(-1, local_features)

    return (
        block_out,
        tokens_grad,
        gain_attn_grad,
        query_grad,
        key_grad,
        value_grad,
        out_proj_grad,
        gain_ffn_grad,
        gate_grad,
        up_grad,
        down_grad,
        shared_gate_grad,
        shared_up_grad,
        shared_down_grad,
    )


def solution(mesh):
    in_specs = (
        P(("dp", "row"), "col"),
        P("col"),
        P("col", "row"),
        P("col", "row"),
        P("col", "row"),
        P("row", "col"),
        P("col"),
        P(None, "col", "row"),
        P(None, "col", "row"),
        P(None, "row", "col"),
        P("col", "row"),
        P("col", "row"),
        P("row", "col"),
        P("dp", None),
        P("dp", None),
        P("dp"),
        P(("dp", "row"), "col"),
    )
    out_specs = (
        P(("dp", "row"), "col"),
        P(("dp", "row"), "col"),
        P("col"),
        P("col", "row"),
        P("col", "row"),
        P("col", "row"),
        P("row", "col"),
        P("col"),
        P(None, "col", "row"),
        P(None, "col", "row"),
        P(None, "row", "col"),
        P("col", "row"),
        P("col", "row"),
        P("row", "col"),
    )
    return jax.shard_map(body, mesh=mesh, in_specs=in_specs, out_specs=out_specs, check_vma=False)
```

time: 2090 us -> 993 us (0.48)
  waiting for transfers between devices: 1050 us -> 306 us
  local copies, waits for them, and re-layouts: 397 us -> 121 us
  Pallas kernels: 0 us -> 226 us
  blocking collectives: 235 us -> 63.5 us
  matrix products: 211 us -> 55.2 us
  starting transfers between devices: 14.5 us -> 77.7 us
  other arithmetic: 146 us -> 123 us
    reduce_scatter x18 -> x0, waiting for transfers between devices: 684 us -> none  [the longest x4 124 us: row_total(): lax.psum_scatter(function(jnp.int32(0), lax.axis_size('row') * row_count)...]
    all_gather x13 -> x0, waiting for transfers between devices: 349 us -> none  [the longest x1 90.5 us: sum_ffn_grads(): lax.all_gather(shares[1].astype(jnp.bfloat16), 'dp', axis=1, tiled=True)]
    ppermute x0 -> x85, waiting for transfers between devices: none -> 306 us  [the longest x56 288 us: send(): return lax.ppermute(values, 'dp', to_left if left else to_right)]
    pallas_call x0 -> x16, Pallas kernels: none -> 226 us  [the longest x5 112 us: expert_grads(): pl.pallas_call(functools.partial(expert_kernel, routed), grid_spec=pltpu....]
    gather x6 -> x0, local copies, waits for them, and re-layouts: 189 us -> none  [the longest x2 60 us: ffn_rows(): routed = jnp.sum(gate_weights[:, :, None] * expert_out[pair_slots], axis=1)]
    dot_general x24 -> x16, matrix products: 211 us -> 44 us  [the longest x4 8.81 us: dot_nt(): lax.dot_general(left, right, (((1,), (1,)), ((), ())), preferred_element_...]
    all_gather x5 -> x0, blocking collectives: 163 us -> none  [the longest x1 33.7 us: sum_ffn_grads(): lax.all_gather(shares[5].astype(jnp.bfloat16), 'dp', axis=1, tiled=True)]
    ppermute x0 -> x85, starting transfers between devices: none -> 77.7 us  [the longest x56 62 us: send(): return lax.ppermute(values, 'dp', to_left if left else to_right)]
  transfers between devices with their start and end apart: 32 -> 85, of which waited for: 22 -> 31; matrix products, arithmetic and copies ran while one was open for 32% -> 27% of each run, Pallas kernels for 0% -> 5%
where the time goes in v1:
time: 993 us; the launch traced here: 987 us
  waiting for transfers between devices  306 us (31%)
  Pallas kernels  226 us (23%)
  other arithmetic  123 us (12%)
  local copies, waits for them, and re-layouts  121 us (12%)
  starting transfers between devices  77.7 us (8%)
  blocking collectives  63.5 us (6%)
  matrix products  55.2 us (6%)
  between operations  14.9 us (2%)
    ppermute x56, waiting for transfers between devices, send(): return lax.ppermute(values, 'dp', to_left if left else to_right)  288 us
    pallas_call x5, Pallas kernels, expert_grads(): pl.pallas_call(functools.partial(expert_kernel, routed), grid_spec=pltpu....  112 us
    psum x1, blocking collectives, body(): lax.psum((gain_attn_part, gain_ffn_part), ('dp', 'row'))  63.5 us
    ppermute x56, starting transfers between devices, send(): return lax.ppermute(values, 'dp', to_left if left else to_right)  62 us
    pallas_call x1, Pallas kernels, combine(): pl.pallas_call(combine_kernel, grid_spec=pltpu.PrefetchScalarGridSpec(num...  61.8 us
    unnamed x264, local copies, waits for them, and re-layouts  44.5 us
    pallas_call x8, Pallas kernels, unpack(): pl.pallas_call(functools.partial(unpack_kernel, aliased), grid_spec=pltpu...  37.8 us
    select_n x8, other arithmetic, halves(): return (jnp.where(mine == 0, low, high), jnp.where(mine == 0, high, low))  23.1 us
  transfers between devices with their start and end apart: 85, of which 31 were waited for; matrix products, arithmetic and copies ran while one was open for 27% of the time, Pallas kernels for 5%

profile of v1, /device:TPU:0, one launch (start us, length us, event | category | flops | bytes accessed | tf_op | source)
XLA Modules:
  0.0 987.4 jit_solution(2975312654935423463)
XLA Ops:
  13.5 4.3 broadcast_select_fusion
  17.8 7.8 broadcast_select_fusion.2
  25.6 3.7 maximum_maximum_fusion.1
  59.8 4.8 collective-permute-done.4
  69.3 3.9 broadcast_select_fusion.17
  73.2 7.1 attend.1.a0
  88.9 11.4 %collective-permute-done.6.a2 = bf16[1024,384]{1,0:T(8,128)(2,1)S(1)} collective-permute-done((bf16[1024,384]{1,0:T(8,128)(2,1)}, bf16[1024,384]{1,0:T(8,128)(2,1)S(1)}, u32[]{:S(2)}, u32[]{:S(2)}) %collective-permute-start.6) | collective-permute-done | bytes 786464 | tf_op jit(solution)/shard_map/ppermute | solution.py:42
  102.9 4.2 broadcast_select_fusion.11
  109.7 7.8 hidden_rows.1
  125.7 3.5 maximum_maximum_fusion.refs_7_.refs_11_.refs_4_.refs_8_
  132.5 4.6 copy.200.refs_2_
  138.9 15.2 %expert_grads.5 = (bf16[1,1536,384]{2,1,0:T(8,128)(2,1)}, bf16[1,1536,384]{2,1,0:T(8,128)(2,1)}, bf16[1,1024,256]{2,1,0:T(8,128)(2,1)}, bf16[1,1024,256]{2,1,0:T...) custom-call(s32[2]{0:T(128)} %pad_add_fusion.1.order_ref.index_ref, ...), custom_call_target="tpu_custom_call" | custom-call | flops 4831838208 | bytes 11796480 | tf_op jit(solution)/shard_map/expert_grads/pallas_call | solution.py:255
  158.8 24.0 %expert_grads.6 = (bf16[2,1536,384]{2,1,0:T(8,128)(2,1)}, bf16[2,1536,384]{2,1,0:T(8,128)(2,1)}, bf16[2,1024,256]{2,1,0:T(8,128)(2,1)}, bf16[2,1024,256]{2,1,0:T...) custom-call(s32[4]{0:T(128)} %get-tuple-element.252.order_ref, bf16[1024,768]{1,0:T(8,128)(2,1)} %copy-done.5, ...), custom_call_target="tpu_custom_call" | custom-call | flops 9663676416 | bytes 14155776 | tf_op jit(solution)/shard_map/expert_grads/pallas_call | solution.py:255
  185.1 24.0 %expert_grads.7 = (bf16[2,1536,384]{2,1,0:T(8,128)(2,1)}, bf16[2,1536,384]{2,1,0:T(8,128)(2,1)}, bf16[2,1024,256]{2,1,0:T(8,128)(2,1)}, bf16[2,1024,256]{2,1,0:T...) custom-call(s32[4]{0:T(128)} %get-tuple-element.253.order_ref, bf16[1024,768]{1,0:T(8,128)(2,1)} %copy-done.5, ...), custom_call_target="tpu_custom_call" | custom-call | flops 9663676416 | bytes 14155776 | tf_op jit(solution)/shard_map/expert_grads/pallas_call | solution.py:255
  211.4 24.0 %expert_grads.8 = (bf16[2,1536,384]{2,1,0:T(8,128)(2,1)}, bf16[2,1536,384]{2,1,0:T(8,128)(2,1)}, bf16[2,1024,256]{2,1,0:T(8,128)(2,1)}, bf16[2,1024,256]{2,1,0:T...) custom-call(s32[4]{0:T(128)} %get-tuple-element.254.order_ref, bf16[1024,768]{1,0:T(8,128)(2,1)} %copy-done.5, ...), custom_call_target="tpu_custom_call" | custom-call | flops 9663676416 | bytes 14155776 | tf_op jit(solution)/shard_map/expert_grads/pallas_call | solution.py:255
  237.7 24.4 %expert_grads.9 = (bf16[2,1536,384]{2,1,0:T(8,128)(2,1)}, bf16[2,1536,384]{2,1,0:T(8,128)(2,1)}, bf16[2,1024,256]{2,1,0:T(8,128)(2,1)}, bf16[2,1024,256]{2,1,0:T...) custom-call(s32[4]{0:T(128)} %get-tuple-element.255.order_ref, bf16[1024,768]{1,0:T(8,128)(2,1)} %copy-done.5, ...), custom_call_target="tpu_custom_call" | custom-call | flops 9663676416 | bytes 14155776 | tf_op jit(solution)/shard_map/expert_grads/pallas_call | solution.py:255
  271.9 61.8 %combine.1 = (f32[1024,768]{1,0:T(8,128)}, f32[1024,768]{1,0:T(8,128)}, f32[1024,768]{1,0:T(8,128)}, f32[1024,768]{1,0:T(8,128)}) custom-call(s32[18]{0:T(128)} %stack.170.order_ref, bf16[9,1024,256]{2,1,0:T(8,128)(2,1)} %constant_dynamic-update-slice_fusion.refs_0_, bf16[9,1024,256]{2,1,0:T(8,128)(2,1)} %copy-done.102, bf16[9,1024,128]{2,1,0:T(8,128)(2,1)} %copy-done.107, ...), custom_call_target="tpu_custom_call" | custom-call | flops 21743271936 | bytes 12582912 | tf_op jit(solution)/shard_map/combine/pallas_call | solution.py:344
  333.7 3.2 convert_element_type.418
  354.7 13.5 %collective-permute-done.55 = bf16[1,1536,384]{2,1,0:T(8,128)(2,1)} collective-permute-done((bf16[1,1536,384]{2,1,0:T(8,128)(2,1)}, bf16[1,1536,384]{2,1,0:T(8,128)(2,1)}, u32[]{:S(2)}, u32[]{:S(2)}) %collective-permute-start.55) | collective-permute-done | bytes 1179680 | tf_op jit(solution)/shard_map/ppermute | solution.py:466
  372.7 11.2 %fusion.117 = (f32[3,1024]{1,0:T(4,128)S(1)}, f32[3,1024,1024]{1,2,0:T(8,128)}) fusion(pred[1024,1024]{0,1:T(8,128)(4,1)} %fusion.10, bf16[1024,128,1]{1,0,2:T(8,128)(2,1)S(1)} %maximum_bitcast_fusion.2, bf16[1024,3,128]{0,2,1:T(8,128)(2,1)} %bitcast.307), kind=kOutput, calls=%fused_computation.328 | convolution fusion | flops 817890304 | bytes 14692352 | tf_op jit(solution)/shard_map/sub | solution.py:121
  393.0 4.4 multiply_reduce_fusion
  398.7 3.2 add_convert_fusion.12
  404.9 3.5 fusion.110
  413.9 6.5 collective-permute-done.71
  423.9 3.2 convolution_convert_fusion.2
  439.2 7.7 fusion.55
  448.8 3.9 fusion.3
  452.7 4.7 fusion.58
  459.9 3.8 multiply_convert_fusion.1
  474.1 5.2 collective-permute-done.25
  482.9 4.6 collective-permute-done.26
  492.6 6.0 collective-permute-done.27
  503.2 25.1 %collective-permute-done.28 = bf16[2,96,896]{2,1,0:T(8,128)(2,1)S(1)} collective-permute-done((bf16[2,96,896]{2,1,0:T(8,128)(2,1)S(1)}, bf16[2,96,896]{2,1,0:T(8,128)(2,1)S(1)}, u32[]{:S(2)}, u32[]{:S(2)}) %collective-permute-start.28) | collective-permute-done | bytes 344096 | tf_op jit(solution)/shard_map/ppermute | solution.py:466
  532.2 7.3 collective-permute-done.29
  544.8 24.1 %collective-permute-done.30 = bf16[2,96,896]{2,1,0:T(8,128)(2,1)S(1)} collective-permute-done((bf16[2,96,896]{2,1,0:T(8,128)(2,1)S(1)}, bf16[2,96,896]{2,1,0:T(8,128)(2,1)S(1)}, u32[]{:S(2)}, u32[]{:S(2)}) %collective-permute-start.30) | collective-permute-done | bytes 344096 | tf_op jit(solution)/shard_map/ppermute | solution.py:466
  571.5 7.2 collective-permute-done.40
  583.4 8.6 collective-permute-done.41
  594.1 22.1 %collective-permute-done.42 = bf16[2,96,896]{2,1,0:T(8,128)(2,1)S(1)} collective-permute-done((bf16[2,96,896]{2,1,0:T(8,128)(2,1)S(1)}, bf16[2,96,896]{2,1,0:T(8,128)(2,1)S(1)}, u32[]{:S(2)}, u32[]{:S(2)}) %collective-permute-start.42) | collective-permute-done | bytes 344096 | tf_op jit(solution)/shard_map/ppermute | solution.py:466
  618.4 8.6 collective-permute-done.43
  633.7 4.4 collective-permute-done.44
  642.1 22.4 %collective-permute-done.33 = bf16[2,96,896]{2,1,0:T(8,128)(2,1)} collective-permute-done((bf16[2,96,896]{2,1,0:T(8,128)(2,1)S(1)}, bf16[2,96,896]{2,1,0:T(8,128)(2,1)}, u32[]{:S(2)}, u32[]{:S(2)}) %collective-permute-start.33) | collective-permute-done | bytes 344096 | tf_op jit(solution)/shard_map/ppermute | solution.py:466
  666.3 4.1 collective-permute-done.45
  674.4 63.5 %all-reduce = (f32[768]{0:T(1024)}, f32[768]{0:T(1024)}) all-reduce(f32[768]{0:T(1024)S(1)} %get-tuple-element.176, f32[768]{0:T(1024)S(1)} %get-tuple-element.201), channel_id=1, replica_groups=mesh['dp'=8,'row'=2,'col'=2] {'dp','row'}, use_global_device_ids=true, to_apply=%region_10.11 | all-reduce | flops 1536 | bytes 12288 | tf_op jit(solution)/shard_map/psum | solution.py:656
  748.6 29.8 %collective-permute-done.36 = bf16[2,96,896]{2,1,0:T(8,128)(2,1)S(1)} collective-permute-done((bf16[2,96,896]{2,1,0:T(8,128)(2,1)S(1)}, bf16[2,96,896]{2,1,0:T(8,128)(2,1)S(1)}, u32[]{:S(2)}, u32[]{:S(2)}) %collective-permute-start.36) | collective-permute-done | bytes 344096 | tf_op jit(solution)/shard_map/ppermute | solution.py:466
  781.6 6.5 collective-permute-done.37
  788.2 4.7 unpack.8
  799.3 4.6 collective-permute-done.50
  806.3 28.1 %collective-permute-done.51 = bf16[2,96,896]{2,1,0:T(8,128)(2,1)} collective-permute-done((bf16[2,96,896]{2,1,0:T(8,128)(2,1)S(1)}, bf16[2,96,896]{2,1,0:T(8,128)(2,1)}, u32[]{:S(2)}, u32[]{:S(2)}) %collective-permute-start.51) | collective-permute-done | bytes 344096 | tf_op jit(solution)/shard_map/ppermute | solution.py:466
  836.3 4.9 unpack.9
  848.3 5.6 collective-permute-done.53
  856.3 4.7 unpack.10
  861.1 21.7 %collective-permute-done.54 = bf16[2,96,896]{2,1,0:T(8,128)(2,1)S(1)} collective-permute-done((bf16[2,96,896]{2,1,0:T(8,128)(2,1)S(1)}, bf16[2,96,896]{2,1,0:T(8,128)(2,1)S(1)}, u32[]{:S(2)}, u32[]{:S(2)}) %collective-permute-start.54) | collective-permute-done | bytes 344096 | tf_op jit(solution)/shard_map/ppermute | solution.py:466
  884.9 3.4 broadcast_select_fusion.7
  890.1 18.6 %collective-permute-done.68.refs_0_ = bf16[1,768,768]{2,1,0:T(8,128)(2,1)} collective-permute-done((bf16[1,768,768]{2,1,0:T(8,128)(2,1)S(1)}, bf16[1,768,768]{2,1,0:T(8,128)(2,1)}, u32[]{:S(2)}, u32[]{:S(2)}) %collective-permute-start.68) | collective-permute-done | bytes 1179680 | tf_op jit(solution)/shard_map/ppermute | solution.py:466
  913.8 3.3 copy.244
  933.5 8.1 reshape.188
  941.7 9.4 fusion.111
  952.7 3.3 reshape.189
  957.7 3.3 reshape.190
  963.7 4.7 unpack.11
  968.4 4.7 unpack.12
  973.1 4.7 unpack.13
  977.8 4.7 unpack.14
  982.5 4.7 unpack.15
  (567 shorter events, 270.5 us)
Async XLA Ops:
  0.7 54.3 %collective-permute-start.1 = (bf16[512,768]{1,0:T(8,128)(2,1)}, bf16[512,768]{1,0:T(8,128)(2,1)}, u32[]{:S(2)}, u32[]{:S(2)}) collective-permute-start(bf16[512,768]{1,0:T(8,128)(2,1)} %param.18), channel_id=1, source_target_pairs={{0,1},{1,0},{2,3},{3,2},{4,5},{5,4},{6,7},{7,6},{8,9},{9,8},{10,11... | collective-permute-start | bytes 2359304 | tf_op jit(solution)/shard_map/ppermute | solution.py:42
  1.2 51.9 %collective-permute-start = (bf16[512,768]{1,0:T(8,128)(2,1)}, bf16[512,768]{1,0:T(8,128)(2,1)}, u32[]{:S(2)}, u32[]{:S(2)}) collective-permute-start(bf16[512,768]{1,0:T(8,128)(2,1)} %param.18), channel_id=1, source_target_pairs={{0,2},{2,0},{1,3},{3,1},{4,6},{6,4},{5,7},{7,5},{8,10},{10,8},{9,1... | collective-permute-start | bytes 2359304 | tf_op jit(solution)/shard_map/ppermute | solution.py:42
  5.2 47.1 %collective-permute-start.2 = (f32[2,768]{1,0:T(2,128)S(1)}, f32[2,768]{1,0:T(2,128)}, u32[]{:S(2)}, u32[]{:S(2)}) collective-permute-start(f32[2,768]{1,0:T(2,128)S(1)} %pad_maximum_fusion.15), channel_id=1, source_target_pairs={{0,1},{1,0},{2,3},{3,2},{4,5},{5,4},{6,7},{7,6},{8,9},{9,8},{10,11... | collective-permute-start | bytes 18440 | tf_op jit(solution)/shard_map/ppermute | solution.py:42
  9.5 55.8 %collective-permute-start.3 = (bf16[768,640]{1,0:T(8,128)(2,1)}, bf16[768,640]{1,0:T(8,128)(2,1)}, u32[]{:S(2)}, u32[]{:S(2)}) collective-permute-start(bf16[768,640]{1,0:T(8,128)(2,1)} %pad_maximum_fusion.11), channel_id=1, source_target_pairs={{0,1},{1,0},{2,3},{3,2},{4,5},{5,4},{6,7},{7,6},{8,9},{9,8},{10,11... | collective-permute-start | bytes 2949128 | tf_op jit(solution)/shard_map/ppermute | solution.py:42
  9.8 79.1 %collective-permute-start.8 = (bf16[768,768]{1,0:T(8,128)(2,1)}, bf16[768,768]{1,0:T(8,128)(2,1)}, u32[]{:S(2)}, u32[]{:S(2)}) collective-permute-start(bf16[768,768]{1,0:T(8,128)(2,1)} %param.23), channel_id=1, source_target_pairs={{0,2},{2,0},{1,3},{3,1},{4,6},{6,4},{5,7},{7,5},{8,10},{10,8},{9,1... | collective-permute-start | bytes 3538952 | tf_op jit(solution)/shard_map/ppermute | solution.py:42
  52.3 84.9 %collective-permute-start.13 = (bf16[18,768,256]{2,1,0:T(8,128)(2,1)}, bf16[18,768,256]{2,1,0:T(8,128)(2,1)}, u32[]{:S(2)}, u32[]{:S(2)}) collective-permute-start(bf16[18,768,256]{2,1,0:T(8,128)(2,1)} %maximum_maximum_fusion.1), channel_id=1, source_target_pairs={{0,1},{1,0},{2,3},{3,2},{4,5},{5,4},{6,7},{7,6},{8,9},{9,8},{10,11... | collective-permute-start | bytes 21233672 | tf_op jit(solution)/shard_map/ppermute | solution.py:42
  53.1 11.5 %collective-permute-start.4 = (bf16[512,768]{1,0:T(8,128)(2,1)}, bf16[512,768]{1,0:T(8,128)(2,1)S(1)}, u32[]{:S(2)}, u32[]{:S(2)}) collective-permute-start(bf16[512,768]{1,0:T(8,128)(2,1)} %collective-permute-done), channel_id=1, source_target_pairs={{0,1},{1,0},{2,3},{3,2},{4,5},{5,4},{6,7},{7,6},{8,9},{9,8},{10,11... | collective-permute-start | bytes 2359304 | tf_op jit(solution)/shard_map/ppermute | solution.py:42
  55.0 62.9 %collective-permute-start.11 = (bf16[512,768]{1,0:T(8,128)(2,1)}, bf16[512,768]{1,0:T(8,128)(2,1)}, u32[]{:S(2)}, u32[]{:S(2)}) collective-permute-start(bf16[512,768]{1,0:T(8,128)(2,1)} %param.34), channel_id=1, source_target_pairs={{0,2},{2,0},{1,3},{3,1},{4,6},{6,4},{5,7},{7,5},{8,10},{10,8},{9,1... | collective-permute-start | bytes 2359304 | tf_op jit(solution)/shard_map/ppermute | solution.py:42
  64.6 72.5 %collective-permute-start.14 = (bf16[18,128,768]{2,1,0:T(8,128)(2,1)}, bf16[18,128,768]{2,1,0:T(8,128)(2,1)S(1)}, u32[]{:S(2)}, u32[]{:S(2)}) collective-permute-start(bf16[18,128,768]{2,1,0:T(8,128)(2,1)} %pad_maximum_fusion.1), channel_id=1, source_target_pairs={{0,1},{1,0},{2,3},{3,2},{4,5},{5,4},{6,7},{7,6},{8,9},{9,8},{10,11... | collective-permute-start | bytes 10616840 | tf_op jit(solution)/shard_map/ppermute | solution.py:42
  80.3 19.9 %collective-permute-start.6 = (bf16[1024,384]{1,0:T(8,128)(2,1)}, bf16[1024,384]{1,0:T(8,128)(2,1)S(1)}, u32[]{:S(2)}, u32[]{:S(2)}) collective-permute-start(bf16[1024,384]{1,0:T(8,128)(2,1)} %attend.1.a0), channel_id=1, source_target_pairs={{0,2},{2,0},{1,3},{3,1},{4,6},{6,4},{5,7},{7,5},{8,10},{10,8},{9,1... | collective-permute-start | bytes 2359304 | tf_op jit(solution)/shard_map/ppermute | solution.py:42
  88.9 19.7 %collective-permute-start.5 = (bf16[1024,384]{1,0:T(8,128)(2,1)S(1)}, bf16[1024,384]{1,0:T(8,128)(2,1)S(1)}, u32[]{:S(2)}, u32[]{:S(2)}) collective-permute-start(bf16[1024,384]{1,0:T(8,128)(2,1)S(1)} %copy-done.36), channel_id=1, source_target_pairs={{0,1},{1,0},{2,3},{3,2},{4,5},{5,4},{6,7},{7,6},{8,9},{9,8},{10,11... | collective-permute-start | bytes 2359304 | tf_op jit(solution)/shard_map/ppermute | solution.py:42
  123.5 13.6 %collective-permute-start.12 = (bf16[1024,768]{1,0:T(8,128)(2,1)}, bf16[1024,768]{1,0:T(8,128)(2,1)}, u32[]{:S(2)}, u32[]{:S(2)}) collective-permute-start(bf16[1024,768]{1,0:T(8,128)(2,1)} %pad_maximum_fusion.6.refs_3_), channel_id=1, source_target_pairs={{0,1},{1,0},{2,3},{3,2},{4,5},{5,4},{6,7},{7,6},{8,9},{9,8},{10,11... | collective-permute-start | bytes 4718600 | tf_op jit(solution)/shard_map/ppermute | solution.py:42
  336.9 13.1 %collective-permute-start.17 = (bf16[1024,768]{1,0:T(8,128)(2,1)}, bf16[1024,768]{1,0:T(8,128)(2,1)}, u32[]{:S(2)}, u32[]{:S(2)}) collective-permute-start(bf16[1024,768]{1,0:T(8,128)(2,1)} %convert_element_type.418), channel_id=1, source_target_pairs={{0,1},{1,0},{2,3},{3,2},{4,5},{5,4},{6,7},{7,6},{8,9},{9,8},{10,11... | collective-permute-start | bytes 4718600 | tf_op jit(solution)/shard_map/ppermute | solution.py:42
  337.2 97.2 %collective-permute-start.21 = (bf16[384,768]{1,0:T(8,128)(2,1)}, bf16[384,768]{1,0:T(8,128)(2,1)}, u32[]{:S(2)}, u32[]{:S(2)}) collective-permute-start(bf16[384,768]{1,0:T(8,128)(2,1)} %get-tuple-element.223.w1), channel_id=1, source_target_pairs={{0,1},{1,0},{2,3},{3,2},{4,5},{5,4},{6,7},{7,6},{8,9},{9,8},{10,11... | collective-permute-start | bytes 1769480 | tf_op jit(solution)/shard_map/ppermute | solution.py:42
  339.8 28.5 %collective-permute-start.55 = (bf16[1,1536,384]{2,1,0:T(8,128)(2,1)}, bf16[1,1536,384]{2,1,0:T(8,128)(2,1)}, u32[]{:S(2)}, u32[]{:S(2)}) collective-permute-start(bf16[1,1536,384]{2,1,0:T(8,128)(2,1)} %get-tuple-element.102), channel_id=1, source_target_pairs={{0,8},{8,16},{16,24},{24,28},{28,20},{20,12},{12,4},{4,0},{1,9},{9... | collective-permute-start | bytes 3538952 | tf_op jit(solution)/shard_map/ppermute | solution.py:466
  349.5 40.3 %collective-permute-start.70 = (bf16[1,1536,384]{2,1,0:T(8,128)(2,1)}, bf16[1,1536,384]{2,1,0:T(8,128)(2,1)}, u32[]{:S(2)}, u32[]{:S(2)}) collective-permute-start(bf16[1,1536,384]{2,1,0:T(8,128)(2,1)} %get-tuple-element.106), channel_id=1, source_target_pairs={{8,0},{16,8},{24,16},{28,24},{20,28},{12,20},{4,12},{0,4},{9,1},{1... | collective-permute-start | bytes 3538952 | tf_op jit(solution)/shard_map/ppermute | solution.py:466
  353.0 40.0 %collective-permute-start.18 = (bf16[1024,768]{1,0:T(8,128)(2,1)}, bf16[1024,768]{1,0:T(8,128)(2,1)}, u32[]{:S(2)}, u32[]{:S(2)}) collective-permute-start(bf16[1024,768]{1,0:T(8,128)(2,1)} %fusion.12), channel_id=1, source_target_pairs={{0,2},{2,0},{1,3},{3,1},{4,6},{6,4},{5,7},{7,5},{8,10},{10,8},{9,1... | collective-permute-start | bytes 4718600 | tf_op jit(solution)/shard_map/ppermute | solution.py:42
  370.9 27.8 %collective-permute-start.56 = (bf16[1,1536,384]{2,1,0:T(8,128)(2,1)}, bf16[1,1536,384]{2,1,0:T(8,128)(2,1)}, u32[]{:S(2)}, u32[]{:S(2)}) collective-permute-start(bf16[1,1536,384]{2,1,0:T(8,128)(2,1)} %add_convert_fusion.13), channel_id=1, source_target_pairs={{0,8},{8,16},{16,24},{24,28},{28,20},{20,12},{12,4},{4,0},{1,9},{9... | collective-permute-start | bytes 3538952 | tf_op jit(solution)/shard_map/ppermute | solution.py:466
  385.2 95.9 %collective-permute-start.15 = (bf16[1024,768]{1,0:T(8,128)(2,1)}, bf16[1024,768]{1,0:T(8,128)(2,1)}, u32[]{:S(2)}, u32[]{:S(2)}) collective-permute-start(bf16[1024,768]{1,0:T(8,128)(2,1)} %convert_element_type.412), channel_id=1, source_target_pairs={{0,1},{1,0},{2,3},{3,2},{4,5},{5,4},{6,7},{7,6},{8,9},{9,8},{10,11... | collective-permute-start | bytes 4718600 | tf_op jit(solution)/shard_map/ppermute | solution.py:42
  392.6 27.8 %collective-permute-start.71 = (bf16[1,1536,384]{2,1,0:T(8,128)(2,1)}, bf16[1,1536,384]{2,1,0:T(8,128)(2,1)}, u32[]{:S(2)}, u32[]{:S(2)}) collective-permute-start(bf16[1,1536,384]{2,1,0:T(8,128)(2,1)} %add_convert_fusion.6), channel_id=1, source_target_pairs={{8,0},{16,8},{24,16},{28,24},{20,28},{12,20},{4,12},{0,4},{9,1},{1... | collective-permute-start | bytes 3538952 | tf_op jit(solution)/shard_map/ppermute | solution.py:466
  401.9 28.2 %collective-permute-start.57 = (bf16[1,1536,384]{2,1,0:T(8,128)(2,1)}, bf16[1,1536,384]{2,1,0:T(8,128)(2,1)}, u32[]{:S(2)}, u32[]{:S(2)}) collective-permute-start(bf16[1,1536,384]{2,1,0:T(8,128)(2,1)} %add_convert_fusion.12), channel_id=1, source_target_pairs={{0,8},{8,16},{16,24},{24,28},{28,20},{20,12},{12,4},{4,0},{1,9},{9... | collective-permute-start | bytes 3538952 | tf_op jit(solution)/shard_map/ppermute | solution.py:466
  408.4 26.0 %collective-permute-start.20 = (bf16[1024,768]{1,0:T(8,128)(2,1)}, bf16[1024,768]{1,0:T(8,128)(2,1)}, u32[]{:S(2)}, u32[]{:S(2)}) collective-permute-start(bf16[1024,768]{1,0:T(8,128)(2,1)} %get-tuple-element.184), channel_id=1, source_target_pairs={{0,1},{1,0},{2,3},{3,2},{4,5},{5,4},{6,7},{7,6},{8,9},{9,8},{10,11... | collective-permute-start | bytes 4718600 | tf_op jit(solution)/shard_map/ppermute | solution.py:42
  423.4 48.6 %collective-permute-start.72 = (bf16[1,1536,384]{2,1,0:T(8,128)(2,1)}, bf16[1,1536,384]{2,1,0:T(8,128)(2,1)}, u32[]{:S(2)}, u32[]{:S(2)}) collective-permute-start(bf16[1,1536,384]{2,1,0:T(8,128)(2,1)} %add_convert_fusion.5), channel_id=1, source_target_pairs={{8,0},{16,8},{24,16},{28,24},{20,28},{12,20},{4,12},{0,4},{9,1},{1... | collective-permute-start | bytes 3538952 | tf_op jit(solution)/shard_map/ppermute | solution.py:466
  432.7 56.5 %collective-permute-start.58 = (bf16[1,1536,384]{2,1,0:T(8,128)(2,1)}, bf16[1,1536,384]{2,1,0:T(8,128)(2,1)}, u32[]{:S(2)}, u32[]{:S(2)}) collective-permute-start(bf16[1,1536,384]{2,1,0:T(8,128)(2,1)} %add_convert_fusion.11), channel_id=1, source_target_pairs={{0,8},{8,16},{16,24},{24,28},{28,20},{20,12},{12,4},{4,0},{1,9},{9... | collective-permute-start | bytes 3538952 | tf_op jit(solution)/shard_map/ppermute | solution.py:466
  473.6 26.8 %collective-permute-start.73 = (bf16[1,1536,384]{2,1,0:T(8,128)(2,1)S(1)}, bf16[1,1536,384]{2,1,0:T(8,128)(2,1)S(1)}, u32[]{:S(2)}, u32[]{:S(2)}) collective-permute-start(bf16[1,1536,384]{2,1,0:T(8,128)(2,1)S(1)} %add_convert_fusion.4), channel_id=1, source_target_pairs={{8,0},{16,8},{24,16},{28,24},{20,28},{12,20},{4,12},{0,4},{9,1},{1... | collective-permute-start | bytes 3538952 | tf_op jit(solution)/shard_map/ppermute | solution.py:466
  490.9 39.3 %collective-permute-start.59 = (bf16[1,1536,384]{2,1,0:T(8,128)(2,1)S(1)}, bf16[1,1536,384]{2,1,0:T(8,128)(2,1)S(1)}, u32[]{:S(2)}, u32[]{:S(2)}) collective-permute-start(bf16[1,1536,384]{2,1,0:T(8,128)(2,1)S(1)} %add_convert_fusion.10), channel_id=1, source_target_pairs={{0,8},{8,16},{16,24},{24,28},{28,20},{20,12},{12,4},{4,0},{1,9},{9... | collective-permute-start | bytes 3538952 | tf_op jit(solution)/shard_map/ppermute | solution.py:466
  498.7 29.6 %collective-permute-start.28 = (bf16[2,96,896]{2,1,0:T(8,128)(2,1)S(1)}, bf16[2,96,896]{2,1,0:T(8,128)(2,1)S(1)}, u32[]{:S(2)}, u32[]{:S(2)}) collective-permute-start(bf16[2,96,896]{2,1,0:T(8,128)(2,1)S(1)} %fusion.71), channel_id=1, source_target_pairs={{0,8},{8,16},{16,24},{24,28},{28,20},{20,12},{12,4},{4,0},{1,9},{9... | collective-permute-start | bytes 1032200 | tf_op jit(solution)/shard_map/ppermute | solution.py:466
  500.8 40.5 %collective-permute-start.74 = (bf16[1,1536,384]{2,1,0:T(8,128)(2,1)S(1)}, bf16[1,1536,384]{2,1,0:T(8,128)(2,1)S(1)}, u32[]{:S(2)}, u32[]{:S(2)}) collective-permute-start(bf16[1,1536,384]{2,1,0:T(8,128)(2,1)S(1)} %add_convert_fusion.3), channel_id=1, source_target_pairs={{8,0},{16,8},{24,16},{28,24},{20,28},{12,20},{4,12},{0,4},{9,1},{1... | collective-permute-start | bytes 3538952 | tf_op jit(solution)/shard_map/ppermute | solution.py:466
  501.4 138.5 %collective-permute-start.16 = (bf16[512,768]{1,0:T(8,128)(2,1)S(1)}, bf16[512,768]{1,0:T(8,128)(2,1)S(1)}, u32[]{:S(2)}, u32[]{:S(2)}) collective-permute-start(bf16[512,768]{1,0:T(8,128)(2,1)S(1)} %dynamic-slice_convert_fusion.1), channel_id=1, source_target_pairs={{0,2},{2,0},{1,3},{3,1},{4,6},{6,4},{5,7},{7,5},{8,10},{10,8},{9,1... | collective-permute-start | bytes 2359304 | tf_op jit(solution)/shard_map/ppermute | solution.py:42
  530.5 38.5 %collective-permute-start.60 = (bf16[1,1536,384]{2,1,0:T(8,128)(2,1)S(1)}, bf16[1,1536,384]{2,1,0:T(8,128)(2,1)S(1)}, u32[]{:S(2)}, u32[]{:S(2)}) collective-permute-start(bf16[1,1536,384]{2,1,0:T(8,128)(2,1)S(1)} %add_convert_fusion.9), channel_id=1, source_target_pairs={{0,8},{8,16},{16,24},{24,28},{28,20},{20,12},{12,4},{4,0},{1,9},{9... | collective-permute-start | bytes 3538952 | tf_op jit(solution)/shard_map/ppermute | solution.py:466
  539.6 29.4 %collective-permute-start.30 = (bf16[2,96,896]{2,1,0:T(8,128)(2,1)S(1)}, bf16[2,96,896]{2,1,0:T(8,128)(2,1)S(1)}, u32[]{:S(2)}, u32[]{:S(2)}) collective-permute-start(bf16[2,96,896]{2,1,0:T(8,128)(2,1)S(1)} %fusion.69), channel_id=1, source_target_pairs={{0,8},{8,16},{16,24},{24,28},{28,20},{20,12},{12,4},{4,0},{1,9},{9... | collective-permute-start | bytes 1032200 | tf_op jit(solution)/shard_map/ppermute | solution.py:466
  541.6 39.8 %collective-permute-start.75 = (bf16[1,1536,384]{2,1,0:T(8,128)(2,1)S(1)}, bf16[1,1536,384]{2,1,0:T(8,128)(2,1)S(1)}, u32[]{:S(2)}, u32[]{:S(2)}) collective-permute-start(bf16[1,1536,384]{2,1,0:T(8,128)(2,1)S(1)} %add_convert_fusion.2), channel_id=1, source_target_pairs={{8,0},{16,8},{24,16},{28,24},{20,28},{12,20},{4,12},{0,4},{9,1},{1... | collective-permute-start | bytes 3538952 | tf_op jit(solution)/shard_map/ppermute | solution.py:466
  544.7 86.3 %collective-permute-start.22 = (bf16[1024,768]{1,0:T(8,128)(2,1)S(1)}, bf16[1024,768]{1,0:T(8,128)(2,1)S(1)}, u32[]{:S(2)}, u32[]{:S(2)}) collective-permute-start(bf16[1024,768]{1,0:T(8,128)(2,1)S(1)} %convolution_convert_fusion), channel_id=1, source_target_pairs={{0,1},{1,0},{2,3},{3,2},{4,5},{5,4},{6,7},{7,6},{8,9},{9,8},{10,11... | collective-permute-start | bytes 4718600 | tf_op jit(solution)/shard_map/ppermute | solution.py:42
  569.0 11.7 %collective-permute-start.31 = (bf16[2,96,896]{2,1,0:T(8,128)(2,1)S(1)}, bf16[2,96,896]{2,1,0:T(8,128)(2,1)S(1)}, u32[]{:S(2)}, u32[]{:S(2)}) collective-permute-start(bf16[2,96,896]{2,1,0:T(8,128)(2,1)S(1)} %fusion.68), channel_id=1, source_target_pairs={{0,8},{8,16},{16,24},{24,28},{28,20},{20,12},{12,4},{4,0},{1,9},{9... | collective-permute-start | bytes 1032200 | tf_op jit(solution)/shard_map/ppermute | solution.py:466
  578.6 37.7 %collective-permute-start.61 = (bf16[1,1536,384]{2,1,0:T(8,128)(2,1)S(1)}, bf16[1,1536,384]{2,1,0:T(8,128)(2,1)S(1)}, u32[]{:S(2)}, u32[]{:S(2)}) collective-permute-start(bf16[1,1536,384]{2,1,0:T(8,128)(2,1)S(1)} %add_convert_fusion.8), channel_id=1, source_target_pairs={{0,8},{8,16},{16,24},{24,28},{28,20},{20,12},{12,4},{4,0},{1,9},{9... | collective-permute-start | bytes 3538952 | tf_op jit(solution)/shard_map/ppermute | solution.py:466
  581.8 35.0 %collective-permute-start.76 = (bf16[1,1536,384]{2,1,0:T(8,128)(2,1)S(1)}, bf16[1,1536,384]{2,1,0:T(8,128)(2,1)S(1)}, u32[]{:S(2)}, u32[]{:S(2)}) collective-permute-start(bf16[1,1536,384]{2,1,0:T(8,128)(2,1)S(1)} %add_convert_fusion.1), channel_id=1, source_target_pairs={{8,0},{16,8},{24,16},{28,24},{20,28},{12,20},{4,12},{0,4},{9,1},{1... | collective-permute-start | bytes 3538952 | tf_op jit(solution)/shard_map/ppermute | solution.py:466
  592.1 24.1 %collective-permute-start.42 = (bf16[2,96,896]{2,1,0:T(8,128)(2,1)S(1)}, bf16[2,96,896]{2,1,0:T(8,128)(2,1)S(1)}, u32[]{:S(2)}, u32[]{:S(2)}) collective-permute-start(bf16[2,96,896]{2,1,0:T(8,128)(2,1)S(1)} %fusion.65), channel_id=1, source_target_pairs={{8,0},{16,8},{24,16},{28,24},{20,28},{12,20},{4,12},{0,4},{9,1},{1... | collective-permute-start | bytes 1032200 | tf_op jit(solution)/shard_map/ppermute | solution.py:466
  616.2 15.9 %collective-permute-start.32 = (bf16[96,896]{1,0:T(8,128)(2,1)S(1)}, bf16[96,896]{1,0:T(8,128)(2,1)S(1)}, u32[]{:S(2)}, u32[]{:S(2)}) collective-permute-start(bf16[96,896]{1,0:T(8,128)(2,1)S(1)} %get-tuple-element.242), channel_id=1, source_target_pairs={{0,1},{1,0},{2,3},{3,2},{4,5},{5,4},{6,7},{7,6},{8,9},{9,8},{10,11... | collective-permute-start | bytes 516104 | tf_op jit(solution)/shard_map/ppermute | solution.py:42
  629.0 42.4 %collective-permute-start.63 = (bf16[1,768,768]{2,1,0:T(8,128)(2,1)S(1)}, bf16[1,768,768]{2,1,0:T(8,128)(2,1)}, u32[]{:S(2)}, u32[]{:S(2)}) collective-permute-start(bf16[1,768,768]{2,1,0:T(8,128)(2,1)S(1)} %pad_maximum_fusion.8.refs_0_), channel_id=1, source_target_pairs={{0,8},{8,16},{16,24},{24,28},{28,20},{20,12},{12,4},{4,0},{1,9},{9... | collective-permute-start | bytes 3538952 | tf_op jit(solution)/shard_map/ppermute | solution.py:466
  631.0 42.1 %collective-permute-start.78 = (bf16[1,768,768]{2,1,0:T(8,128)(2,1)S(1)}, bf16[1,768,768]{2,1,0:T(8,128)(2,1)}, u32[]{:S(2)}, u32[]{:S(2)}) collective-permute-start(bf16[1,768,768]{2,1,0:T(8,128)(2,1)S(1)} %pad_maximum_fusion.9.refs_1_), channel_id=1, source_target_pairs={{8,0},{16,8},{24,16},{28,24},{20,28},{12,20},{4,12},{0,4},{9,1},{1... | collective-permute-start | bytes 3538952 | tf_op jit(solution)/shard_map/ppermute | solution.py:466
  632.1 41.3 %collective-permute-start.23 = (bf16[512,768]{1,0:T(8,128)(2,1)S(1)}, bf16[512,768]{1,0:T(8,128)(2,1)S(1)}, u32[]{:S(2)}, u32[]{:S(2)}) collective-permute-start(bf16[512,768]{1,0:T(8,128)(2,1)S(1)} %dynamic-slice_convert_fusion), channel_id=1, source_target_pairs={{0,2},{2,0},{1,3},{3,1},{4,6},{6,4},{5,7},{7,5},{8,10},{10,8},{9,1... | collective-permute-start | bytes 2359304 | tf_op jit(solution)/shard_map/ppermute | solution.py:42
  638.1 26.5 %collective-permute-start.33 = (bf16[2,96,896]{2,1,0:T(8,128)(2,1)S(1)}, bf16[2,96,896]{2,1,0:T(8,128)(2,1)}, u32[]{:S(2)}, u32[]{:S(2)}) collective-permute-start(bf16[2,96,896]{2,1,0:T(8,128)(2,1)S(1)} %pad_maximum_fusion.12), channel_id=1, source_target_pairs={{0,8},{8,16},{16,24},{24,28},{28,20},{20,12},{12,4},{4,0},{1,9},{9... | collective-permute-start | bytes 1032200 | tf_op jit(solution)/shard_map/ppermute | solution.py:466
  639.9 30.4 %collective-permute-start.45 = (bf16[2,96,896]{2,1,0:T(8,128)(2,1)S(1)}, bf16[2,96,896]{2,1,0:T(8,128)(2,1)S(1)}, u32[]{:S(2)}, u32[]{:S(2)}) collective-permute-start(bf16[2,96,896]{2,1,0:T(8,128)(2,1)S(1)} %fusion.62), channel_id=1, source_target_pairs={{8,0},{16,8},{24,16},{28,24},{20,28},{12,20},{4,12},{0,4},{9,1},{1... | collective-permute-start | bytes 1032200 | tf_op jit(solution)/shard_map/ppermute | solution.py:466
  664.5 73.4 %collective-permute-start.34 = (bf16[2,96,896]{2,1,0:T(8,128)(2,1)}, bf16[2,96,896]{2,1,0:T(8,128)(2,1)}, u32[]{:S(2)}, u32[]{:S(2)}) collective-permute-start(bf16[2,96,896]{2,1,0:T(8,128)(2,1)} %collective-permute-done.33), channel_id=1, source_target_pairs={{0,8},{8,16},{16,24},{24,28},{28,20},{20,12},{12,4},{4,0},{1,9},{9... | collective-permute-start | bytes 1032200 | tf_op jit(solution)/shard_map/ppermute | solution.py:466
  671.1 66.9 %collective-permute-start.46 = (bf16[2,96,896]{2,1,0:T(8,128)(2,1)}, bf16[2,96,896]{2,1,0:T(8,128)(2,1)}, u32[]{:S(2)}, u32[]{:S(2)}) collective-permute-start(bf16[2,96,896]{2,1,0:T(8,128)(2,1)} %fusion.61), channel_id=1, source_target_pairs={{8,0},{16,8},{24,16},{28,24},{20,28},{12,20},{4,12},{0,4},{9,1},{1... | collective-permute-start | bytes 1032200 | tf_op jit(solution)/shard_map/ppermute | solution.py:466
  671.4 71.7 %collective-permute-start.64 = (bf16[1,768,768]{2,1,0:T(8,128)(2,1)}, bf16[1,768,768]{2,1,0:T(8,128)(2,1)}, u32[]{:S(2)}, u32[]{:S(2)}) collective-permute-start(bf16[1,768,768]{2,1,0:T(8,128)(2,1)} %collective-permute-done.63.refs_0_), channel_id=1, source_target_pairs={{0,8},{8,16},{16,24},{24,28},{28,20},{20,12},{12,4},{4,0},{1,9},{9... | collective-permute-start | bytes 3538952 | tf_op jit(solution)/shard_map/ppermute | solution.py:466
  673.2 70.0 %collective-permute-start.79 = (bf16[1,768,768]{2,1,0:T(8,128)(2,1)}, bf16[1,768,768]{2,1,0:T(8,128)(2,1)}, u32[]{:S(2)}, u32[]{:S(2)}) collective-permute-start(bf16[1,768,768]{2,1,0:T(8,128)(2,1)} %collective-permute-done.78.refs_1_), channel_id=1, source_target_pairs={{8,0},{16,8},{24,16},{28,24},{20,28},{12,20},{4,12},{0,4},{9,1},{1... | collective-permute-start | bytes 3538952 | tf_op jit(solution)/shard_map/ppermute | solution.py:466
  674.4 63.5 %collective-permute-start.24 = (f32[512,1]{0,1:T(1,128)S(1)}, f32[512,1]{0,1:T(1,128)S(1)}, u32[]{:S(2)}, u32[]{:S(2)}) collective-permute-start(f32[512,1]{0,1:T(1,128)S(1)} %bitcast.317), channel_id=1, source_target_pairs={{0,1},{1,0},{2,3},{3,2},{4,5},{5,4},{6,7},{7,6},{8,9},{9,8},{10,11... | collective-permute-start | bytes 6152 | tf_op jit(solution)/shard_map/ppermute | solution.py:42
  743.1 51.8 %collective-permute-start.65 = (bf16[1,768,768]{2,1,0:T(8,128)(2,1)}, bf16[1,768,768]{2,1,0:T(8,128)(2,1)S(1)}, u32[]{:S(2)}, u32[]{:S(2)}) collective-permute-start(bf16[1,768,768]{2,1,0:T(8,128)(2,1)} %collective-permute-done.64.refs_0_), channel_id=1, source_target_pairs={{0,8},{8,16},{16,24},{24,28},{28,20},{20,12},{12,4},{4,0},{1,9},{9... | collective-permute-start | bytes 3538952 | tf_op jit(solution)/shard_map/ppermute | solution.py:466
  743.2 51.8 %collective-permute-start.80 = (bf16[1,768,768]{2,1,0:T(8,128)(2,1)}, bf16[1,768,768]{2,1,0:T(8,128)(2,1)}, u32[]{:S(2)}, u32[]{:S(2)}) collective-permute-start(bf16[1,768,768]{2,1,0:T(8,128)(2,1)} %collective-permute-done.79.refs_1_), channel_id=1, source_target_pairs={{8,0},{16,8},{24,16},{28,24},{20,28},{12,20},{4,12},{0,4},{9,1},{1... | collective-permute-start | bytes 3538952 | tf_op jit(solution)/shard_map/ppermute | solution.py:466
  745.5 33.0 %collective-permute-start.36 = (bf16[2,96,896]{2,1,0:T(8,128)(2,1)S(1)}, bf16[2,96,896]{2,1,0:T(8,128)(2,1)S(1)}, u32[]{:S(2)}, u32[]{:S(2)}) collective-permute-start(bf16[2,96,896]{2,1,0:T(8,128)(2,1)S(1)} %collective-permute-done.35), channel_id=1, source_target_pairs={{0,8},{8,16},{16,24},{24,28},{28,20},{20,12},{12,4},{4,0},{1,9},{9... | collective-permute-start | bytes 1032200 | tf_op jit(solution)/shard_map/ppermute | solution.py:466
  745.6 34.1 %collective-permute-start.48 = (bf16[2,96,896]{2,1,0:T(8,128)(2,1)S(1)}, bf16[2,96,896]{2,1,0:T(8,128)(2,1)S(1)}, u32[]{:S(2)}, u32[]{:S(2)}) collective-permute-start(bf16[2,96,896]{2,1,0:T(8,128)(2,1)S(1)} %pad_maximum_fusion.13), channel_id=1, source_target_pairs={{8,0},{16,8},{24,16},{28,24},{20,28},{12,20},{4,12},{0,4},{9,1},{1... | collective-permute-start | bytes 1032200 | tf_op jit(solution)/shard_map/ppermute | solution.py:466
  779.7 13.2 %collective-permute-start.49 = (bf16[2,96,896]{2,1,0:T(8,128)(2,1)S(1)}, bf16[2,96,896]{2,1,0:T(8,128)(2,1)S(1)}, u32[]{:S(2)}, u32[]{:S(2)}) collective-permute-start(bf16[2,96,896]{2,1,0:T(8,128)(2,1)S(1)} %collective-permute-done.48), channel_id=1, source_target_pairs={{8,0},{16,8},{24,16},{28,24},{20,28},{12,20},{4,12},{0,4},{9,1},{1... | collective-permute-start | bytes 1032200 | tf_op jit(solution)/shard_map/ppermute | solution.py:466
  795.0 49.1 %collective-permute-start.66 = (bf16[1,768,768]{2,1,0:T(8,128)(2,1)S(1)}, bf16[1,768,768]{2,1,0:T(8,128)(2,1)S(1)}, u32[]{:S(2)}, u32[]{:S(2)}) collective-permute-start(bf16[1,768,768]{2,1,0:T(8,128)(2,1)S(1)} %collective-permute-done.65.refs_0_), channel_id=1, source_target_pairs={{0,8},{8,16},{16,24},{24,28},{28,20},{20,12},{12,4},{4,0},{1,9},{9... | collective-permute-start | bytes 3538952 | tf_op jit(solution)/shard_map/ppermute | solution.py:466
  795.0 49.7 %collective-permute-start.81 = (bf16[1,768,768]{2,1,0:T(8,128)(2,1)}, bf16[1,768,768]{2,1,0:T(8,128)(2,1)}, u32[]{:S(2)}, u32[]{:S(2)}) collective-permute-start(bf16[1,768,768]{2,1,0:T(8,128)(2,1)} %collective-permute-done.80.refs_1_), channel_id=1, source_target_pairs={{8,0},{16,8},{24,16},{28,24},{20,28},{12,20},{4,12},{0,4},{9,1},{1... | collective-permute-start | bytes 3538952 | tf_op jit(solution)/shard_map/ppermute | solution.py:466
  798.0 38.2 %collective-permute-start.39 = (bf16[2,96,896]{2,1,0:T(8,128)(2,1)}, bf16[2,96,896]{2,1,0:T(8,128)(2,1)S(1)}, u32[]{:S(2)}, u32[]{:S(2)}) collective-permute-start(bf16[2,96,896]{2,1,0:T(8,128)(2,1)} %collective-permute-done.38), channel_id=1, source_target_pairs={{0,8},{8,16},{16,24},{24,28},{28,20},{20,12},{12,4},{4,0},{1,9},{9... | collective-permute-start | bytes 1032200 | tf_op jit(solution)/shard_map/ppermute | solution.py:466
  804.0 30.5 %collective-permute-start.51 = (bf16[2,96,896]{2,1,0:T(8,128)(2,1)S(1)}, bf16[2,96,896]{2,1,0:T(8,128)(2,1)}, u32[]{:S(2)}, u32[]{:S(2)}) collective-permute-start(bf16[2,96,896]{2,1,0:T(8,128)(2,1)S(1)} %collective-permute-done.50), channel_id=1, source_target_pairs={{8,0},{16,8},{24,16},{28,24},{20,28},{12,20},{4,12},{0,4},{9,1},{1... | collective-permute-start | bytes 1032200 | tf_op jit(solution)/shard_map/ppermute | solution.py:466
  844.1 38.7 %collective-permute-start.67 = (bf16[1,768,768]{2,1,0:T(8,128)(2,1)S(1)}, bf16[1,768,768]{2,1,0:T(8,128)(2,1)S(1)}, u32[]{:S(2)}, u32[]{:S(2)}) collective-permute-start(bf16[1,768,768]{2,1,0:T(8,128)(2,1)S(1)} %collective-permute-done.66.refs_0_), channel_id=1, source_target_pairs={{0,8},{8,16},{16,24},{24,28},{28,20},{20,12},{12,4},{4,0},{1,9},{9... | collective-permute-start | bytes 3538952 | tf_op jit(solution)/shard_map/ppermute | solution.py:466
  844.7 38.6 %collective-permute-start.82 = (bf16[1,768,768]{2,1,0:T(8,128)(2,1)}, bf16[1,768,768]{2,1,0:T(8,128)(2,1)}, u32[]{:S(2)}, u32[]{:S(2)}) collective-permute-start(bf16[1,768,768]{2,1,0:T(8,128)(2,1)} %collective-permute-done.81.refs_1_), channel_id=1, source_target_pairs={{8,0},{16,8},{24,16},{28,24},{20,28},{12,20},{4,12},{0,4},{9,1},{1... | collective-permute-start | bytes 3538952 | tf_op jit(solution)/shard_map/ppermute | solution.py:466
  853.9 28.8 %collective-permute-start.54 = (bf16[2,96,896]{2,1,0:T(8,128)(2,1)S(1)}, bf16[2,96,896]{2,1,0:T(8,128)(2,1)S(1)}, u32[]{:S(2)}, u32[]{:S(2)}) collective-permute-start(bf16[2,96,896]{2,1,0:T(8,128)(2,1)S(1)} %collective-permute-done.53), channel_id=1, source_target_pairs={{8,0},{16,8},{24,16},{28,24},{20,28},{12,20},{4,12},{0,4},{9,1},{1... | collective-permute-start | bytes 1032200 | tf_op jit(solution)/shard_map/ppermute | solution.py:466
  882.8 26.0 %collective-permute-start.68 = (bf16[1,768,768]{2,1,0:T(8,128)(2,1)S(1)}, bf16[1,768,768]{2,1,0:T(8,128)(2,1)}, u32[]{:S(2)}, u32[]{:S(2)}) collective-permute-start(bf16[1,768,768]{2,1,0:T(8,128)(2,1)S(1)} %collective-permute-done.67.refs_0_), channel_id=1, source_target_pairs={{0,8},{8,16},{16,24},{24,28},{28,20},{20,12},{12,4},{4,0},{1,9},{9... | collective-permute-start | bytes 3538952 | tf_op jit(solution)/shard_map/ppermute | solution.py:466
  883.4 26.1 %collective-permute-start.83 = (bf16[1,768,768]{2,1,0:T(8,128)(2,1)}, bf16[1,768,768]{2,1,0:T(8,128)(2,1)}, u32[]{:S(2)}, u32[]{:S(2)}) collective-permute-start(bf16[1,768,768]{2,1,0:T(8,128)(2,1)} %collective-permute-done.82.refs_1_), channel_id=1, source_target_pairs={{8,0},{16,8},{24,16},{28,24},{20,28},{12,20},{4,12},{0,4},{9,1},{1... | collective-permute-start | bytes 3538952 | tf_op jit(solution)/shard_map/ppermute | solution.py:466
  908.8 73.7 %collective-permute-start.69 = (bf16[1,768,768]{2,1,0:T(8,128)(2,1)}, bf16[1,768,768]{2,1,0:T(8,128)(2,1)}, u32[]{:S(2)}, u32[]{:S(2)}) collective-permute-start(bf16[1,768,768]{2,1,0:T(8,128)(2,1)} %collective-permute-done.68.refs_0_), channel_id=1, source_target_pairs={{0,8},{8,16},{16,24},{24,28},{28,20},{20,12},{12,4},{4,0},{1,9},{9... | collective-permute-start | bytes 3538952 | tf_op jit(solution)/shard_map/ppermute | solution.py:466
  909.5 73.0 %collective-permute-start.84 = (bf16[1,768,768]{2,1,0:T(8,128)(2,1)}, bf16[1,768,768]{2,1,0:T(8,128)(2,1)}, u32[]{:S(2)}, u32[]{:S(2)}) collective-permute-start(bf16[1,768,768]{2,1,0:T(8,128)(2,1)} %collective-permute-done.83.refs_1_), channel_id=1, source_target_pairs={{8,0},{16,8},{24,16},{28,24},{20,28},{12,20},{4,12},{0,4},{9,1},{1... | collective-permute-start | bytes 3538952 | tf_op jit(solution)/shard_map/ppermute | solution.py:466
  (139 other events, 1196.3 us)

commit v2 on v1

v2 whole, which is shorter than its diff:
```python
import functools

import jax
import jax.numpy as jnp
from jax import lax
from jax.experimental import pallas as pl
from jax.experimental.pallas import tpu as pltpu
from jax.sharding import PartitionSpec as P

D = 1536
HQ = 12
HK = 4
DH = 128
GROUP_HEADS = HQ // HK
LANES = 128

EPSILON = 1e-05
F32 = jnp.float32
BF16 = jnp.bfloat16
VMEM_LIMIT = 56 * 1024 * 1024
SMALL = pl.CostEstimate(flops=0, bytes_accessed=0, transcendentals=0)


def params(*semantics):
    return pltpu.CompilerParams(
        dimension_semantics=semantics or None, vmem_limit_bytes=VMEM_LIMIT
    )


def dot(left, right):
    return jnp.dot(left, right, preferred_element_type=F32)


def dot_nt(left, right):
    return lax.dot_general(left, right, (((1,), (1,)), ((), ())), preferred_element_type=F32)


def dot_tn(left, right):
    return lax.dot_general(left, right, (((0,), (0,)), ((), ())), preferred_element_type=F32)


def after(values, *others):
    return lax.optimization_barrier((values, *others))[0]


def swap(values, axis):
    return lax.ppermute(values, axis, [(0, 1), (1, 0)])


def halves(values, axis, mine):
    size = values.shape[axis] // 2
    low = lax.slice_in_dim(values, 0, size, axis=axis)
    high = lax.slice_in_dim(values, size, 2 * size, axis=axis)
    return jnp.where(mine == 0, low, high), jnp.where(mine == 0, high, low)


def in_order(own, other, mine, axis):
    return jnp.concatenate(
        [jnp.where(mine == 0, own, other), jnp.where(mine == 0, other, own)], axis=axis
    )


def attend_kernel(place_ref, own_ref, other_ref, out_ref, all_ref):
    row = place_ref[0]
    length = place_ref[1]
    rows = own_ref.shape[0]
    all_ref[pl.ds(pl.multiple_of(row * rows, rows), rows), :] = own_ref[...]
    all_ref[pl.ds(pl.multiple_of((1 - row) * rows, rows), rows), :] = other_ref[...]
    block = 256
    width = GROUP_HEADS * DH
    for at in range(2 * rows // block):
        first, keys = at * block, (at + 1) * block
        query = jnp.concatenate(
            [
                all_ref[first : first + block, h * DH : (h + 1) * DH]
                for h in range(GROUP_HEADS)
            ],
            axis=0,
        )
        key = all_ref[0:keys, width : width + DH]
        value = all_ref[0:keys, width + DH : width + 2 * DH]
        scores = dot_nt(query, key) * DH ** (-0.5)
        shape = (block, keys)
        query_at = lax.broadcasted_iota(jnp.int32, shape, 0) + first
        key_at = lax.broadcasted_iota(jnp.int32, shape, 1)
        allowed = (key_at <= query_at) & (key_at < length)
        allowed = jnp.concatenate([allowed] * GROUP_HEADS, axis=0)
        scores = jnp.where(allowed, scores, -1e30)
        weights = jnp.exp(scores - jnp.max(scores, axis=1, keepdims=True))
        probs = weights * (1.0 / jnp.sum(weights, axis=1, keepdims=True))
        result = dot(probs.astype(BF16), value).astype(BF16)
        for h in range(GROUP_HEADS):
            out_ref[first : first + block, h * DH : (h + 1) * DH] = result[
                h * block : (h + 1) * block
            ]


def attend(place, own, other):
    rows, width = own.shape
    spec = pl.BlockSpec(memory_space=pltpu.VMEM)
    return pl.pallas_call(
        attend_kernel,
        out_shape=jax.ShapeDtypeStruct((2 * rows, GROUP_HEADS * DH), BF16),
        in_specs=[pl.BlockSpec(memory_space=pltpu.SMEM), spec, spec],
        out_specs=spec,
        scratch_shapes=[pltpu.VMEM((2 * rows, width), BF16)],
        compiler_params=params(),
        cost_estimate=SMALL,
        name="attend",
    )(place, own, other)


def attend_back(qkv, attended_grad, length):
    seq = qkv.shape[0]
    width = GROUP_HEADS * DH
    queries = qkv[:, :width].reshape(seq, GROUP_HEADS, DH)
    key, value = qkv[:, width : width + DH], qkv[:, width + DH :]
    grads = attended_grad.reshape(seq, GROUP_HEADS, DH)
    scale = DH ** (-0.5)
    scores = jnp.einsum("qrd,kd->rqk", queries, key, preferred_element_type=F32) * scale
    position = jnp.arange(seq, dtype=jnp.int32)
    allowed = (position[None, :] <= position[:, None]) & (position[None, :] < length)
    scores = jnp.where(allowed, scores, -1e30)
    weights = jnp.exp(scores - jnp.max(scores, axis=-1, keepdims=True))
    probs = weights / jnp.sum(weights, axis=-1, keepdims=True)
    probs_grad = jnp.einsum("qrd,kd->rqk", grads, value, preferred_element_type=F32)
    carried = jnp.sum(probs * probs_grad, axis=-1, keepdims=True)
    score_grad = (probs * (probs_grad - carried)).astype(BF16)
    query_back = jnp.einsum("rqk,kd->qrd", score_grad, key, preferred_element_type=F32) * scale
    key_back = jnp.einsum("rqk,qrd->kd", score_grad, queries, preferred_element_type=F32) * scale
    value_back = jnp.einsum(
        "rqk,qrd->kd", probs.astype(BF16), grads, preferred_element_type=F32
    )
    return jnp.concatenate(
        [query_back.reshape(seq, width), key_back, value_back], axis=1
    ).astype(BF16)


def project_kernel(col_ref, own_ref, other_ref, gains_ref, gains_c_ref, query_ref, key_ref, value_ref, there_ref, x_own_ref, x_other_ref, qkv_ref, scale_ref):
    own = own_ref[...].astype(F32)
    other = other_ref[...].astype(F32)
    total = jnp.sum(own * own, axis=1, keepdims=True)
    total = total + jnp.sum(other * other, axis=1, keepdims=True)
    scale = lax.rsqrt(total / D + EPSILON)
    own = (own * scale * gains_ref[0:1, :]).astype(BF16)
    other = (other * scale * gains_c_ref[0:1, :]).astype(BF16)
    x_own_ref[...] = own
    x_other_ref[...] = other
    scale_ref[...] = scale
    here = jnp.concatenate([query_ref[...], key_ref[...], value_ref[...]], axis=1)
    qkv_ref[...] = (dot(own, here) + dot(other, there_ref[...])).astype(BF16)


def project(col, own, other, gains, gains_c, w_query, w_key, w_value, there):
    rows, features = own.shape
    width = there.shape[1]
    group = GROUP_HEADS * DH
    tile = rows // 2

    def whole(*shape):
        return pl.BlockSpec(shape, lambda i, c: (0,) * len(shape))

    def mine(width):
        return pl.BlockSpec((features, width), lambda i, c: (0, c[0]))

    def rowwise(width):
        return pl.BlockSpec((tile, width), lambda i, c: (i, 0))

    return pl.pallas_call(
        project_kernel,
        grid_spec=pltpu.PrefetchScalarGridSpec(
            num_scalar_prefetch=1,
            grid=(rows // tile,),
            in_specs=[
                rowwise(features),
                rowwise(features),
                whole(2, features),
                whole(2, features),
                mine(group),
                mine(DH),
                mine(DH),
                whole(features, width),
            ],
            out_specs=[rowwise(features), rowwise(features), rowwise(width), rowwise(1)],
        ),
        out_shape=[
            jax.ShapeDtypeStruct((rows, features), BF16),
            jax.ShapeDtypeStruct((rows, features), BF16),
            jax.ShapeDtypeStruct((rows, width), BF16),
            jax.ShapeDtypeStruct((rows, 1), F32),
        ],
        compiler_params=params("arbitrary"),
        cost_estimate=SMALL,
        name="project",
    )(col, own, other, gains, gains_c, w_query, w_key, w_value, there)


def hidden_kernel(tiles, place_ref, *refs):
    near, near_c, far, far_c = refs[0:4]
    attended = refs[4:8]
    here = refs[8:12]
    there = refs[12:16]
    gains_ref, gains_c_ref = refs[16:18]
    hidden_ref, x_own_ref, x_other_ref, scale_ref = refs[18:22]
    is_near = (pl.program_id(0) >= tiles // 2).astype(jnp.int32) == place_ref[0]
    own = jnp.where(is_near, near[...], far[...]).astype(F32)
    other = jnp.where(is_near, near_c[...], far_c[...]).astype(F32)
    for k in range(4):
        own = own + dot(attended[k][...], here[k][...])
        other = other + dot(attended[k][...], there[k][...])
    total = jnp.sum(own * own, axis=1, keepdims=True)
    total = total + jnp.sum(other * other, axis=1, keepdims=True)
    scale = lax.rsqrt(total / D + EPSILON)
    hidden_ref[...] = own
    scale_ref[...] = scale
    x_own_ref[...] = (own * scale * gains_ref[1:2, :]).astype(BF16)
    x_other_ref[...] = (other * scale * gains_c_ref[1:2, :]).astype(BF16)


def hidden_rows(place, tokens, attended, w_here, w_there, gains, gains_c):
    half, features = tokens[0].shape
    rows, heads = attended[0].shape
    tile = 256
    tiles = rows // tile
    per_half = half // tile

    def rowwise(width):
        return pl.BlockSpec((tile, width), lambda i, p: (i, 0))

    def halfwise(width):
        return pl.BlockSpec((tile, width), lambda i, p: (i % per_half, 0))

    def whole(*shape):
        return pl.BlockSpec(shape, lambda i, p: (0,) * len(shape))

    mine = pl.BlockSpec((heads, features), lambda i, p: (p[1], 0))
    others = pl.BlockSpec((heads, features), lambda i, p: (1 - p[1], 0))
    return pl.pallas_call(
        functools.partial(hidden_kernel, tiles),
        grid_spec=pltpu.PrefetchScalarGridSpec(
            num_scalar_prefetch=1,
            grid=(tiles,),
            in_specs=[halfwise(features)] * 4
            + [rowwise(heads)] * 4
            + [mine, others, mine, others] * 2
            + [whole(2, features)] * 2,
            out_specs=[rowwise(features)] * 3 + [rowwise(1)],
        ),
        out_shape=[
            jax.ShapeDtypeStruct((rows, features), F32),
            jax.ShapeDtypeStruct((rows, features), BF16),
            jax.ShapeDtypeStruct((rows, features), BF16),
            jax.ShapeDtypeStruct((rows, 1), F32),
        ],
        compiler_params=params("arbitrary"),
        cost_estimate=SMALL,
        name="hidden_rows",
    )(
        place,
        *tokens,
        *attended,
        *[w_here[k // 2] for k in range(4)],
        *[w_there[k // 2] for k in range(4)],
        gains,
        gains_c,
    )


def expert_kernel(shared, aliased, first, order_ref, *refs):
    x_own, x_other, o_own, o_other, routes, gates = refs[0:6]
    weights = refs[6:18]
    grads = refs[18 + aliased : 20 + aliased]
    pair_ref, inner_ref = refs[20 + aliased : 22 + aliased]
    step = pl.program_id(0) + first
    rows, features = x_own.shape
    tile = 512
    up_own = jnp.concatenate([weights[k][0] for k in (0, 1, 6, 7)], axis=1)
    up_other = jnp.concatenate([weights[k][0] for k in (2, 3, 8, 9)], axis=1)
    down_own = jnp.concatenate([weights[k][0] for k in (4, 10)], axis=0)
    down_other = jnp.concatenate([weights[k][0] for k in (5, 11)], axis=0)

    def token_tile(t, carry):
        at = pl.ds(pl.multiple_of(t * tile, tile), tile)
        pre = dot(x_own[at, :], up_own) + dot(x_other[at, :], up_other)
        back = dot_nt(o_own[at, :], down_own) + dot_nt(o_other[at, :], down_other)
        for k in range(2):
            pre_gate = pre[:, 2 * k * LANES : (2 * k + 1) * LANES]
            pre_up = pre[:, (2 * k + 1) * LANES : (2 * k + 2) * LANES]
            inner_grad = back[:, k * LANES : (k + 1) * LANES]
            sigmoid = 1.0 / (1.0 + jnp.exp(-pre_gate))
            silu = pre_gate * sigmoid
            inner = silu * pre_up
            if not shared:
                chosen = jnp.where(routes[at, :] == order_ref[2 * step + k], gates[at, :], 0.0)
                gate = jnp.sum(chosen, axis=1, keepdims=True)
                inner = gate * inner
                inner_grad = gate * inner_grad
            gate_grad = inner_grad * pre_up * (sigmoid * (1.0 + pre_gate * (1.0 - sigmoid)))
            inner_ref[0, at, k * LANES : (k + 1) * LANES] = inner.astype(BF16)
            pair_ref[0, at, 2 * k * LANES : (2 * k + 1) * LANES] = gate_grad.astype(BF16)
            pair_ref[0, at, (2 * k + 1) * LANES : (2 * k + 2) * LANES] = (
                inner_grad * silu
            ).astype(BF16)
        return carry

    lax.fori_loop(0, rows // tile, token_tile, 0)
    pairs = pair_ref[0]
    for h, x in enumerate((x_own, x_other)):
        wide = dot_tn(x[...], pairs).astype(BF16)
        for k in range(2):
            grads[k][0, h * features : (h + 1) * features, 0 : 2 * LANES] = wide[
                :, 2 * k * LANES : (2 * k + 2) * LANES
            ]
    inner = inner_ref[0]
    tile = 256
    for h, o in enumerate((o_own, o_other)):
        for j in range(features // tile):
            low = dot_tn(inner, o[:, j * tile : (j + 1) * tile]).astype(BF16)
            for k in range(2):
                for b in range(tile // LANES):
                    at = h * features + j * tile + b * LANES
                    grads[k][0, at : at + LANES, 2 * LANES :] = low[
                        k * LANES : (k + 1) * LANES, b * LANES : (b + 1) * LANES
                    ]


def expert_specs(features, place, wide, low):
    specs = []
    if wide:
        block = pl.BlockSpec((1, features, LANES), lambda i, o: (place(i, o)[0], 0, place(i, o)[1]))
        specs += [block] * 4
    if low:
        block = pl.BlockSpec((1, LANES, features), lambda i, o: (*place(i, o), 0))
        specs += [block] * 2
    return specs


def expert_grads(order, first, last, total, x, o, routes, gates, weights, kept):
    shared = total is None
    steps = last - first
    rows, features = x[0].shape
    choices = routes.shape[1]
    aliased = len(kept)

    def fixed(*shape):
        return pl.BlockSpec(shape, lambda i, o: (0,) * len(shape))

    def stepped(*shape):
        return pl.BlockSpec((1, *shape), lambda i, o: (i, 0, 0))

    def placed(*shape):
        return pl.BlockSpec((1, *shape), lambda i, o: (i + first, 0, 0))

    specs = []
    for k in range(2):
        if shared:

            def picked(i, o, k=k):
                return 0, 2 * o[o.shape[0] - 1] + k

        else:

            def picked(i, o, k=k):
                return o[2 * (i + first) + k], o[o.shape[0] - 1]

        specs += expert_specs(features, picked, True, True)
    total = steps if shared else total
    return pl.pallas_call(
        functools.partial(expert_kernel, shared, aliased, first),
        grid_spec=pltpu.PrefetchScalarGridSpec(
            num_scalar_prefetch=1,
            grid=(steps,),
            in_specs=[fixed(rows, features)] * 4
            + [fixed(rows, choices)] * 2
            + specs
            + [pl.BlockSpec(memory_space=pl.ANY)] * aliased,
            out_specs=[stepped(2 * features, 3 * LANES)] * 2
            + [placed(rows, 4 * LANES), placed(rows, 2 * LANES)],
        ),
        out_shape=[jax.ShapeDtypeStruct((steps, 2 * features, 3 * LANES), BF16)] * 2
        + [
            jax.ShapeDtypeStruct((total, rows, 4 * LANES), BF16),
            jax.ShapeDtypeStruct((total, rows, 2 * LANES), BF16),
        ],
        input_output_aliases={19 + k: 2 + k for k in range(aliased)},
        compiler_params=params("arbitrary"),
        cost_estimate=SMALL,
        name="expert_grads",
    )(order, *x, *o, routes, gates, *weights, *weights, *kept)


def mix_kernel(back, group, order_ref, *refs):
    acts_ref, shared_ref = refs[0:2]
    each = 4 if back else 2
    count = 2 * group
    weights = refs[2 : 2 + each * count]
    shared = refs[2 + each * count : 2 + each * count + 2 * each]
    own_ref, other_ref, total_ref = refs[2 + each * (count + 2) :]
    step = pl.program_id(0)
    rows, features = own_ref.shape
    tile = 512

    def gathered(parts):
        if back:
            own = [p[0] for k in range(len(parts) // 4) for p in parts[4 * k : 4 * k + 2]]
            other = [p[0] for k in range(len(parts) // 4) for p in parts[4 * k + 2 : 4 * k + 4]]
            return [jnp.concatenate(own, axis=1), jnp.concatenate(other, axis=1)]
        own = [parts[2 * k][0] for k in range(len(parts) // 2)]
        other = [parts[2 * k + 1][0] for k in range(len(parts) // 2)]
        return [jnp.concatenate(own, axis=0), jnp.concatenate(other, axis=0)]

    times = dot_nt if back else dot

    @pl.when(step == 0)
    def _():
        both = gathered(shared)
        for t in range(rows // tile):
            at = slice(t * tile, (t + 1) * tile)
            for h in range(2):
                total_ref[h, at, :] = times(shared_ref[0, at, :], both[h])

    both = gathered(weights)
    for t in range(rows // tile):
        at = slice(t * tile, (t + 1) * tile)
        acts = jnp.concatenate([acts_ref[g, at, :] for g in range(group)], axis=1)
        for h in range(2):
            total_ref[h, at, :] += times(acts, both[h])

    @pl.when(step == pl.num_programs(0) - 1)
    def _():
        own_ref[...] = total_ref[0]
        other_ref[...] = total_ref[1].astype(BF16)


def mix(back, order, acts, shared_acts, weights, shared_weights):
    pairs, rows, width = acts.shape
    features = weights[0].shape[1] if back else weights[0].shape[2]
    group = 2 if pairs % 2 == 0 else 1

    specs = []
    for k in range(2 * group):

        def picked(i, o, k=k):
            return o[2 * group * i + k], o[o.shape[0] - 1]

        specs += expert_specs(features, picked, back, not back)
    for k in range(2):

        def picked(i, o, k=k):
            return 0, 2 * o[o.shape[0] - 1] + k

        specs += expert_specs(features, picked, back, not back)
    whole = pl.BlockSpec((rows, features), lambda i, o: (0, 0))
    return pl.pallas_call(
        functools.partial(mix_kernel, back, group),
        grid_spec=pltpu.PrefetchScalarGridSpec(
            num_scalar_prefetch=1,
            grid=(pairs // group,),
            in_specs=[
                pl.BlockSpec((group, rows, width), lambda i, o: (i, 0, 0)),
                pl.BlockSpec((1, rows, width), lambda i, o: (0, 0, 0)),
            ]
            + specs,
            out_specs=[whole, whole],
            scratch_shapes=[pltpu.VMEM((2, rows, features), F32)],
        ),
        out_shape=[
            jax.ShapeDtypeStruct((rows, features), F32),
            jax.ShapeDtypeStruct((rows, features), BF16),
        ],
        compiler_params=params("arbitrary"),
        cost_estimate=SMALL,
        name="mix",
    )(order, acts, shared_acts, *weights * (2 * group), *shared_weights * 2)


def ring_of(size):
    return list(range(0, size, 2)) + list(range(1, size, 2))[::-1]


def unpack_kernel(aliased, index_ref, *refs):
    first_ref, second_ref = refs[0:2]
    gate_ref, up_ref, down_ref = refs[2 + aliased : 5 + aliased]
    blocks = first_ref.shape[1] // LANES

    def write(chunk_ref):
        for c in range(2):
            base = 3 * LANES * c
            to = slice(c * LANES, (c + 1) * LANES)
            gate_ref[0, :, to] = chunk_ref[0, :, base : base + LANES].astype(F32)
            up_ref[0, :, to] = chunk_ref[0, :, base + LANES : base + 2 * LANES].astype(F32)
            for b in range(blocks):
                down_ref[0, to, b * LANES : (b + 1) * LANES] = chunk_ref[
                    0, b * LANES : (b + 1) * LANES, base + 2 * LANES : base + 3 * LANES
                ].astype(F32)

    pl.when(pl.program_id(1) == 0)(lambda: write(first_ref))
    pl.when(pl.program_id(1) == 1)(lambda: write(second_ref))


def unpack(index, first, second, shapes, outs):
    count, rows, width = first.shape
    chunk = pl.BlockSpec((1, rows, width), lambda i, d, n: (i, 0, 0))

    def placed(shape):
        return pl.BlockSpec((1, *shape[1:]), lambda i, d, n: (n[2 * i + d], 0, 0))

    aliased = len(outs)
    return pl.pallas_call(
        functools.partial(unpack_kernel, aliased),
        grid_spec=pltpu.PrefetchScalarGridSpec(
            num_scalar_prefetch=1,
            grid=(count, 2),
            in_specs=[chunk, chunk] + [pl.BlockSpec(memory_space=pl.ANY)] * aliased,
            out_specs=[placed(shape) for shape in shapes],
        ),
        out_shape=[jax.ShapeDtypeStruct(shape, F32) for shape in shapes],
        input_output_aliases={3 + k: k for k in range(aliased)},
        compiler_params=params("arbitrary", "arbitrary"),
        cost_estimate=SMALL,
        name="unpack",
    )(index, first, second, *outs)

def unpack_late_kernel(col_ref, first_ref, second_ref, *outs):
    sgate, sup, sdown, query, key, value, out = outs
    features = first_ref.shape[1]
    flipped = col_ref[0] != 0
    for c in range(2):
        for b in range(14):
            lanes = slice(b % 7 * LANES, (b % 7 + 1) * LANES)
            first, second = first_ref[c, :, lanes], second_ref[c, :, lanes]
            if b >= 7:
                first, second = second, first
            block = jnp.where(flipped, second, first).astype(F32)
            if b < 6:
                at = slice((2 * c + b // 3) * LANES, (2 * c + b // 3 + 1) * LANES)
                if b % 3 < 2:
                    (sgate, sup)[b % 3][:, at] = block
                else:
                    for k in range(features // LANES):
                        here = slice(k * LANES, (k + 1) * LANES)
                        sdown[at, here] = block[here, :]
            elif b < 9:
                at = (GROUP_HEADS * c + b - 6) * LANES
                query[:, at : at + LANES] = block
            elif b < 11:
                (key, value)[b - 9][:, c * LANES : (c + 1) * LANES] = block
            else:
                at = (GROUP_HEADS * c + b - 11) * LANES
                out[at : at + LANES, :] = block.T


def unpack_late(col, first, second, shapes):
    spec = pl.BlockSpec(memory_space=pltpu.VMEM)
    return pl.pallas_call(
        unpack_late_kernel,
        in_specs=[pl.BlockSpec(memory_space=pltpu.SMEM), spec, spec],
        out_specs=[spec] * len(shapes),
        out_shape=[jax.ShapeDtypeStruct(shape, F32) for shape in shapes],
        compiler_params=params(),
        name="unpack_late",
    )(col, first, second)


def add_rounded(left, right):
    return (left.astype(F32) + right.astype(F32)).astype(BF16)


def body(
    tokens_in,
    norm_gain_attn,
    w_query,
    w_key,
    w_value,
    w_out,
    norm_gain_ffn,
    w_gate,
    w_up,
    w_down,
    w_shared_gate,
    w_shared_up,
    w_shared_down,
    routes,
    gate_weights,
    seq_lengths,
    out_grad,
):
    row = lax.axis_index("row")
    col = lax.axis_index("col")
    dp = lax.axis_index("dp")
    dp_size = lax.axis_size("dp")
    local_rows, local_features = tokens_in.shape
    experts = w_gate.shape[0]
    group_width = GROUP_HEADS * DH
    col_ref = col.reshape(1)

    ring_size = min(8, dp_size)
    ring = ring_of(ring_size)
    starts = range(0, dp_size, ring_size)
    rights = [
        (g + ring[k], g + ring[(k + 1) % ring_size]) for g in starts for k in range(ring_size)
    ]
    lefts = [(b, a) for a, b in rights]
    routes_of = [
        [(2 * a, 2 * b) for a, b in ways[0]] + [(2 * a + 1, 2 * b + 1) for a, b in ways[1]]
        for ways in ((rights, lefts), (lefts, rights))
    ]
    place_of = [ring.index(k) for k in range(ring_size)]
    place = jnp.asarray(place_of, jnp.int32)[dp % ring_size]
    signs = [1 - 2 * col, 2 * col - 1]

    def send(values, which):
        if ring_size == 1:
            return values
        return lax.ppermute(values, ("dp", "col"), routes_of[which])

    def chunk_at(step, which):
        return (place - signs[which] * step) % ring_size

    def across_rings(values):
        if len(starts) == 1:
            return values
        peers = [[g + k for g in starts] for k in range(ring_size)]
        return lax.psum(values, "dp", axis_index_groups=peers)

    tokens_y = swap(tokens_in, "row")
    tokens_c = swap(tokens_in, "col")
    gains = jnp.stack([norm_gain_attn, norm_gain_ffn])
    gains_c = swap(gains, "col")
    there = jnp.concatenate(
        [halves(w, 1, col)[1] for w in (w_query, w_key, w_value)], axis=1
    )
    there = swap(there, "col")
    count = min(ring_size, 4)
    share = w_out.shape[0] // count
    member = dp % count
    out_share = swap(lax.dynamic_slice_in_dim(w_out, member * share, share, axis=0), "row")

    def project_half(own, other):
        return project(col_ref, own, other, gains, gains_c, w_query, w_key, w_value, there)

    near = project_half(tokens_in, tokens_c)

    shares = [after(out_share, near[2])]
    for k in range(1, count):
        pairs = [(m, m ^ k) for m in range(dp_size)]
        shares.append(lax.ppermute(shares[0], "dp", pairs))
    tokens_y = after(tokens_y, near[2], out_share)
    tokens_yc = swap(tokens_y, "col")
    grad_cut = local_rows // 8 * 3
    grad_y = [
        swap(after(part, tokens_y), "row") for part in (out_grad[:grad_cut], out_grad[grad_cut:])
    ]
    far = project_half(tokens_y, tokens_yc)

    attended = attend(
        after(jnp.stack([row, seq_lengths[0]]), grad_y[0], *shares), near[2], far[2]
    )
    out_c = swap(after(w_out, attended), "col")
    shares = jnp.stack([after(shares[0], attended)] + shares[1:])
    out_y = jnp.concatenate(
        [lax.dynamic_index_in_dim(shares, member ^ k, keepdims=False) for k in range(count)],
        axis=0,
    )
    attended_y = swap(after(attended, grad_y[1]), "row")
    attended_c = swap(attended, "col")

    w_sgate, w_sup, w_sdown = w_shared_gate[None], w_shared_up[None], w_shared_down[None]
    gate_c = swap(w_gate, "col")
    up_c, down_c, sgate_c, sup_c, sdown_c = (
        swap(after(w, attended), "col") for w in (w_up, w_down, w_sgate, w_sup, w_sdown)
    )

    grad_own = in_order(out_grad, jnp.concatenate(grad_y, axis=0), row, 0)
    grad_other = swap(grad_own, "col")
    out_yc = swap(out_y, "col")
    attended_y = after(attended_y, grad_own, out_yc)
    attended_yc = swap(attended_y, "col")
    hidden, x_own, x_other, scale_ffn = hidden_rows(
        jnp.stack([row, col]),
        [tokens_in, tokens_c, tokens_y, tokens_yc],
        [attended, attended_c, attended_y, attended_yc],
        [w_out, out_y],
        [out_c, out_yc],
        gains,
        gains_c,
    )

    each = experts // (2 * ring_size)
    orders = []
    for s in range(ring_size):
        for k in range(each):
            for which in range(2):
                second = col if which == 0 else 1 - col
                orders.append(2 * each * chunk_at(s, which) + each * second + k)
    order = jnp.stack(orders + [col]).astype(jnp.int32)
    pairs_total = experts // 2
    routed = [w_gate, w_up, gate_c, up_c, w_down, down_c]
    shared = [w_sgate, w_sup, sgate_c, sup_c, w_sdown, sdown_c]

    def run(first, last, order, kept):
        return expert_grads(
            order,
            first,
            last,
            pairs_total,
            [x_own, x_other],
            [grad_own, grad_other],
            routes,
            gate_weights,
            routed,
            kept,
        )

    first = run(0, each, order, ())
    kept = first[2:]
    sums = [first[0], first[1]]
    ready = {s: [first[0], first[1]] for s in (0,)}
    done = each
    runs = {}
    for s in range(1, ring_size):
        got = [send(sums[k], k) for k in range(2)]
        work = []
        last = min(max(done, each * s) + 2 * each, pairs_total)
        if done < last:
            result = run(done, last, after(order, *sums), tuple(kept))
            kept = result[2:]
            for at in range(done, last):
                runs[at] = (result[0], result[1], at - done)
            done = last
            work = list(kept)
        elif "shared" not in runs:
            runs["shared"] = expert_grads(
                after(order, *sums),
                0,
                1,
                None,
                [x_own, x_other],
                [grad_own, grad_other],
                routes,
                gate_weights,
                shared,
                (),
            )
            work = [runs["shared"][2]]
        elif "back" not in runs:
            runs["back"] = mix(
                True,
                after(order, *sums),
                kept[0],
                runs["shared"][2],
                routed[:4],
                shared[:4],
            )
            work = [runs["back"][1]]
        elif "out" not in runs:
            runs["out"] = mix(
                False,
                after(order, *sums),
                kept[1],
                runs["shared"][3],
                routed[4:],
                shared[4:],
            )
            work = [runs["out"][1]]
        for k in range(2):
            got[k] = after(got[k], *(sums[:1] if k else work))
            parts = [runs[at] for at in range(each * s, each * s + each)]
            mine = jnp.concatenate([p[k][p[2] : p[2] + 1] for p in parts], axis=0)
            sums[k] = add_rounded(got[k], mine)
    if "shared" not in runs:
        runs["shared"] = expert_grads(
            order, 0, 1, None, [x_own, x_other], [grad_own, grad_other], routes, gate_weights, shared, ()
        )
    if "back" not in runs:
        runs["back"] = mix(True, order, kept[0], runs["shared"][2], routed[:4], shared[:4])
    if "out" not in runs:
        runs["out"] = mix(False, order, kept[1], runs["shared"][3], routed[4:], shared[4:])

    sums = [across_rings(total) for total in sums]
    crossed = [swap(total[:, local_features:], "col") for total in sums]
    chunks = [
        in_order(sums[k][:, :local_features], crossed[1 - k], col, 2) for k in range(2)
    ]

    start = row * local_rows

    def my_rows(values):
        return lax.dynamic_slice_in_dim(values, start, local_rows, axis=0)

    def their_rows(values):
        return lax.dynamic_slice_in_dim(values, local_rows - start, local_rows, axis=0)

    back_own, back_other = runs["back"]
    normed_grad = back_own + swap(back_other, "col").astype(F32)
    normed_grad = normed_grad + swap(normed_grad.astype(BF16), "row").astype(F32)
    sum_own, sum_other = runs["out"]
    ffn_sum = sum_own + swap(sum_other, "col").astype(F32)
    ffn_rows = my_rows(ffn_sum) + swap(their_rows(ffn_sum).astype(BF16), "row").astype(F32)
    block_out = (my_rows(hidden) + ffn_rows).astype(BF16)

    gain_ffn_part = jnp.sum(my_rows(normed_grad * hidden * scale_ffn), axis=0)
    scaled = normed_grad * norm_gain_ffn
    products = jnp.sum(scaled * hidden, axis=1, keepdims=True)
    mean = (products + swap(products, "col")) / D
    hidden_grad = grad_own.astype(F32) + scale_ffn * scaled - hidden * scale_ffn**3 * mean
    attn_grad = hidden_grad.astype(BF16)
    attn_grad_c = swap(attn_grad, "col")

    out_own = lax.dynamic_slice_in_dim(w_out, col * group_width, group_width, axis=0)
    out_back = lax.dynamic_slice_in_dim(out_c, col * group_width, group_width, axis=0)
    attended_grad = (dot_nt(attn_grad, out_own) + dot_nt(attn_grad_c, out_back)).astype(BF16)
    out_grads = [dot_tn(attn_grad, attended), dot_tn(attn_grad_c, attended)]
    qkv = in_order(near[2], far[2], row, 0)
    qkv_grad = attend_back(qkv, attended_grad, seq_lengths[0])
    normed_own = in_order(near[0], far[0], row, 0)
    normed_other = in_order(near[1], far[1], row, 0)
    project_grads = [dot_tn(normed_own, qkv_grad), dot_tn(normed_other, qkv_grad)]
    here = jnp.concatenate(
        [halves(w, 1, col)[0] for w in (w_query, w_key, w_value)], axis=1
    )
    tokens_back = dot_nt(qkv_grad, here) + swap(
        dot_nt(qkv_grad, there).astype(BF16), "col"
    ).astype(F32)
    tokens_back = my_rows(tokens_back) + swap(
        their_rows(tokens_back).astype(BF16), "row"
    ).astype(F32)
    scale_attn = near[3]
    tokens_f32 = tokens_in.astype(F32)
    gain_attn_part = jnp.sum(tokens_back * tokens_f32 * scale_attn, axis=0)
    scaled = tokens_back * norm_gain_attn
    products = jnp.sum(scaled * tokens_f32, axis=1, keepdims=True)
    mean = (products + swap(products, "col")) / D
    tokens_grad = (
        my_rows(hidden_grad) + scale_attn * scaled - tokens_f32 * scale_attn**3 * mean
    ).astype(BF16)

    shared_grads = runs["shared"]
    pack = jnp.concatenate(
        [shared_grads[0][0], shared_grads[1][0]]
        + [
            jnp.concatenate(grads, axis=0).astype(BF16) for grads in (project_grads, out_grads)
        ],
        axis=1,
    )
    pack = pack.reshape(2, ring_size, local_features // ring_size, -1)
    middle = pack.shape[3] // 2

    def late_chunk(step, which):
        chunk = lax.dynamic_index_in_dim(pack, chunk_at(step, which), axis=1, keepdims=False)
        low, high = chunk[..., :middle], chunk[..., middle:]
        return jnp.where(col == which, low, high)

    def late_place(current, step, which):
        at = chunk_at(ring_size - 1 + step, which)
        return lax.dynamic_update_index_in_dim(late_out[which], current, at, 1)

    late_out = [jnp.zeros((*pack.shape[:3], middle), BF16) for _ in range(2)]
    late = [late_chunk(0, k) for k in range(2)]
    late_steps = 0

    def late_step(late_steps, late):
        late = [send(late[k], k) for k in range(2)]
        step = late_steps + 1
        if step < ring_size:
            late = [add_rounded(late[k], late_chunk(step, k)) for k in range(2)]
        else:
            for k in range(2):
                late_out[k] = late_place(late[k], step - ring_size + 1, k)
        if step == ring_size - 1:
            late = [across_rings(values) for values in late]
            others = [swap(values[1], "col") for values in late]
            late = [in_order(late[k][0:1], others[1 - k][None], col, 0) for k in range(2)]
            for k in range(2):
                late_out[k] = late_place(late[k], 0, k)
        return step, late

    shapes = [w_gate.shape, w_up.shape, w_down.shape]
    placed = ()
    late_slots = 5
    late_total = 2 * (ring_size - 1)
    for s in range(ring_size):
        index = []
        for k in range(each):
            for which in range(2):
                second = col if which == 0 else 1 - col
                at = chunk_at(ring_size - 1 + s, which)
                index.append(2 * each * at + each * second + k)
        index = jnp.stack(index).astype(jnp.int32)
        if s + 1 < ring_size:
            got = [send(chunks[k], k) for k in range(2)]
            placed = unpack(index, chunks[0], chunks[1], shapes, placed)
            slots_left = ring_size - 1 - s
            if slots_left <= late_slots:
                if late_steps == 0:
                    late = list(lax.optimization_barrier((*late, *chunks))[:2])
                until = late_total - late_total * (slots_left - 1) // late_slots
                while late_steps < until:
                    late_steps, late = late_step(late_steps, late)
            held = lax.optimization_barrier((*got, *late, *placed))
            got, late, placed = held[0:2], list(held[2:4]), held[4:]
            chunks = got
        else:
            placed = unpack(index, chunks[0], chunks[1], shapes, placed)
    while late_steps < late_total:
        late_steps, late = late_step(late_steps, late)
    if late_total == 0:
        others = [swap(values[1], "col") for values in late]
        late = [in_order(late[k][0:1], others[1 - k][None], col, 0) for k in range(2)]
        late_out = [late_place(late[k], 0, k) for k in range(2)]
    gate_grad, up_grad, down_grad = placed
    shapes = [w.shape for w in (w_shared_gate, w_shared_up, w_shared_down)]
    shapes += [w.shape for w in (w_query, w_key, w_value, w_out)]
    late_grads = unpack_late(
        col_ref,
        late_out[0].reshape(2, local_features, middle),
        late_out[1].reshape(2, local_features, middle),
        shapes,
    )
    shared_gate_grad, shared_up_grad, shared_down_grad = late_grads[0:3]
    query_grad, key_grad, value_grad, out_proj_grad = late_grads[3:7]

    gain_parts = jnp.stack([gain_attn_part, gain_ffn_part])
    bit = 1
    while bit < ring_size:
        pairs = [(g + k, g + (k ^ bit)) for g in starts for k in range(ring_size)]
        gain_parts = gain_parts + lax.ppermute(gain_parts, "dp", pairs)
        bit *= 2
    gain_parts = across_rings(gain_parts + swap(gain_parts, "row"))

    return (
        block_out,
        tokens_grad,
        gain_parts[0],
        query_grad,
        key_grad,
        value_grad,
        out_proj_grad,
        gain_parts[1],
        gate_grad,
        up_grad,
        down_grad,
        shared_gate_grad,
        shared_up_grad,
        shared_down_grad,
    )


def solution(mesh):
    in_specs = (
        P(("dp", "row"), "col"),
        P("col"),
        P("col", "row"),
        P("col", "row"),
        P("col", "row"),
        P("row", "col"),
        P("col"),
        P(None, "col", "row"),
        P(None, "col", "row"),
        P(None, "row", "col"),
        P("col", "row"),
        P("col", "row"),
        P("row", "col"),
        P("dp", None),
        P("dp", None),
        P("dp"),
        P(("dp", "row"), "col"),
    )
    out_specs = (
        P(("dp", "row"), "col"),
        P(("dp", "row"), "col"),
        P("col"),
        P("col", "row"),
        P("col", "row"),
        P("col", "row"),
        P("row", "col"),
        P("col"),
        P(None, "col", "row"),
        P(None, "col", "row"),
        P(None, "row", "col"),
        P("col", "row"),
        P("col", "row"),
        P("row", "col"),
    )
    return jax.shard_map(body, mesh=mesh, in_specs=in_specs, out_specs=out_specs, check_vma=False)
```

time: 993 us -> 775 us (0.78)
  local copies, waits for them, and re-layouts: 121 us -> 40 us
  blocking collectives: 63.5 us -> 0 us
  other arithmetic: 123 us -> 76.6 us
  Pallas kernels: 226 us -> 205 us
  waiting for transfers between devices: 306 us -> 289 us
    psum x1 -> x0, blocking collectives: 63.5 us -> none  [body(): lax.psum((gain_attn_part, gain_ffn_part), ('dp', 'row'))]
    ppermute x56 -> x62, waiting for transfers between devices: 288 us -> 239 us  [the longest x56 227 us: send(): return lax.ppermute(values, ('dp', 'col'), routes_of[which])]
    ppermute x29 -> x34, waiting for transfers between devices: 17.9 us -> 50.3 us  [swap(): return lax.ppermute(values, axis, [(0, 1), (1, 0)])]
    unnamed x264 -> x217, local copies, waits for them, and re-layouts: 44.5 us -> 18.1 us
    slice x17 -> x4, local copies, waits for them, and re-layouts: 25.9 us -> 2.62 us  [the longest x1 1.91 us: body(): out_grad[:grad_cut]]
    reshape x9 -> x0, local copies, waits for them, and re-layouts: 23 us -> none  [the longest x1 8.15 us: body(): final[..., :lanes_shared]]
    pallas_call x7 -> x12, Pallas kernels: 181 us -> 159 us  [the longest x6 91 us: expert_grads(): pl.pallas_call(functools.partial(expert_kernel, shared, aliased, first),...]
    select_n x8 -> x2, other arithmetic: 23.1 us -> 3.07 us  [halves(): return (jnp.where(mine == 0, low, high), jnp.where(mine == 0, high, low))]
  transfers between devices with their start and end apart: 85 -> 96, of which waited for: 31 -> 36; matrix products, arithmetic and copies ran while one was open for 27% -> 19% of each run, Pallas kernels for 5% -> 25%
where the time goes in v2:
time: 775 us; the launch traced here: 764 us
  waiting for transfers between devices  289 us (37%)
  Pallas kernels  205 us (26%)
  starting transfers between devices  84 us (11%)
  other arithmetic  76.6 us (10%)
  matrix products  47.8 us (6%)
  local copies, waits for them, and re-layouts  40 us (5%)
  between operations  21.6 us (3%)
    ppermute x56, waiting for transfers between devices, send(): return lax.ppermute(values, ('dp', 'col'), routes_of[which])  227 us
    pallas_call x6, Pallas kernels, expert_grads(): pl.pallas_call(functools.partial(expert_kernel, shared, aliased, first),...  91 us
    ppermute x56, starting transfers between devices, send(): return lax.ppermute(values, ('dp', 'col'), routes_of[which])  61.6 us
    ppermute x34, waiting for transfers between devices, swap(): return lax.ppermute(values, axis, [(0, 1), (1, 0)])  50.3 us
    pallas_call x2, Pallas kernels, mix(): pl.pallas_call(functools.partial(mix_kernel, back, group), grid_spec=pltp...  38.7 us
    pallas_call x8, Pallas kernels, unpack(): pl.pallas_call(functools.partial(unpack_kernel, aliased), grid_spec=pltpu...  38.5 us
    convert_element_type x28, other arithmetic, add_rounded(): return (left.astype(F32) + right.astype(F32)).astype(BF16)  35.4 us
    unnamed x217, local copies, waits for them, and re-layouts  18.1 us
  transfers between devices with their start and end apart: 96, of which 36 were waited for; matrix products, arithmetic and copies ran while one was open for 19% of the time, Pallas kernels for 25%

profile of v2, /device:TPU:0, one launch (start us, length us, event | category | flops | bytes accessed | tf_op | source)
XLA Modules:
  0.0 764.1 jit_solution(1658236260232920181)
XLA Ops:
  5.3 3.0 collective-permute-start.1
  11.9 4.5 project.2
  16.4 16.1 %collective-permute-done.4 = bf16[192,768]{1,0:T(8,128)(2,1)} collective-permute-done((bf16[192,768]{1,0:T(8,128)(2,1)S(1)}, bf16[192,768]{1,0:T(8,128)(2,1)}, u32[]{:S(2)}, u32[]{:S(2)}) %collective-permute-start.4) | collective-permute-done | bytes 294944 | tf_op jit(solution)/shard_map/ppermute | solution.py:47
  40.8 3.0 collective-permute-done.6
  47.7 5.0 collective-permute-done.9
  53.7 4.5 project.3
  58.2 7.0 attend.1.refs_4_
  66.2 12.8 %collective-permute-done.11 = bf16[320,768]{1,0:T(8,128)(2,1)S(1)} collective-permute-done((bf16[320,768]{1,0:T(8,128)(2,1)S(1)}, bf16[320,768]{1,0:T(8,128)(2,1)S(1)}, u32[]{:S(2)}, u32[]{:S(2)}) %collective-permute-start.11) | collective-permute-done | bytes 491552 | tf_op jit(solution)/shard_map/ppermute | solution.py:47
  82.2 15.7 %collective-permute-done.12.refs_6_ = bf16[1024,384]{1,0:T(8,128)(2,1)} collective-permute-done((bf16[1024,384]{1,0:T(8,128)(2,1)}, bf16[1024,384]{1,0:T(8,128)(2,1)}, u32[]{:S(2)}, u32[]{:S(2)}) %collective-permute-start.12) | collective-permute-done | bytes 786464 | tf_op jit(solution)/shard_map/ppermute | solution.py:47
  115.8 13.3 %hidden_rows.1 = (f32[1024,768]{1,0:T(8,128)}, bf16[1024,768]{1,0:T(8,128)(2,1)}, bf16[1024,768]{1,0:T(8,128)(2,1)}, f32[1024,1]{1,0:T(8,128)}) custom-call(s32[2]{0:T(128)} %pad_add_fusion.place_ref, bf16[512,768]{1,0:T(8,128)(2,1)} %refs_0_.1, bf16[512,768]{1,0:T(8,128)(2,1)} %copy-done.41, bf16[512,768]{1,0:T(8,128)(2,1)} %copy-done.42, ...), custom_call_target="tpu_custom_call" | custom-call | tf_op jit(solution)/shard_map/hidden_rows/pallas_call | solution.py:238
  130.3 12.3 %expert_grads.6 = (bf16[1,1536,384]{2,1,0:T(8,128)(2,1)}, bf16[1,1536,384]{2,1,0:T(8,128)(2,1)}, bf16[8,1024,512]{2,1,0:T(8,128)(2,1)}, bf16[8,1024,256]{2,1,0:T(8,128)(2,1)}) custom-call(s32[17]{0:T(128)} %stack.194.order_ref, bf16[1024,768]{1,0:T(8,128)(2,1)} %get-tuple-element.180.refs_0_, bf16[1024,768]{1,0:T(8,128)(2,1)} %get-tuple-element.181.refs_1_, ...), custom_call_target="tpu_custom_call" | custom-call | tf_op jit(solution)/shard_map/expert_grads/pallas_call | solution.py:368
  144.6 18.2 %expert_grads.7 = (bf16[2,1536,384]{2,1,0:T(8,128)(2,1)}, bf16[2,1536,384]{2,1,0:T(8,128)(2,1)}, bf16[8,1024,512]{2,1,0:T(8,128)(2,1)}, bf16[8,1024,256]{2,1,0:T(8,128)(2,1)}) custom-call(s32[17]{0:T(128)} %stack.194.order_ref, bf16[1024,768]{1,0:T(8,128)(2,1)} %get-tuple-element.180.refs_0_, ...), custom_call_target="tpu_custom_call", output_to_operand_aliasing={{2}: (19, {}), {3}: (20, {})} | custom-call | tf_op jit(solution)/shard_map/expert_grads/pallas_call | solution.py:368
  162.8 8.2 %collective-permute-done.20 = bf16[1,1536,384]{2,1,0:T(8,128)(2,1)S(1)} collective-permute-done((bf16[1,1536,384]{2,1,0:T(8,128)(2,1)}, bf16[1,1536,384]{2,1,0:T(8,128)(2,1)S(1)}, u32[]{:S(2)}, u32[]{:S(2)}) %collective-permute-start.20) | collective-permute-done | bytes 1179680 | tf_op jit(solution)/shard_map/ppermute | solution.py:615
  176.1 18.3 %expert_grads.8 = (bf16[2,1536,384]{2,1,0:T(8,128)(2,1)}, bf16[2,1536,384]{2,1,0:T(8,128)(2,1)}, bf16[8,1024,512]{2,1,0:T(8,128)(2,1)}, bf16[8,1024,256]{2,1,0:T(8,128)(2,1)}) custom-call(s32[17]{0:T(128)} %stack.194.order_ref, bf16[1024,768]{1,0:T(8,128)(2,1)} %get-tuple-element.180.refs_0_, ...), custom_call_target="tpu_custom_call", output_to_operand_aliasing={{2}: (19, {}), {3}: (20, {})} | custom-call | tf_op jit(solution)/shard_map/expert_grads/pallas_call | solution.py:368
  194.4 6.3 collective-permute-done.21
  204.4 18.5 %expert_grads.9 = (bf16[2,1536,384]{2,1,0:T(8,128)(2,1)}, bf16[2,1536,384]{2,1,0:T(8,128)(2,1)}, bf16[8,1024,512]{2,1,0:T(8,128)(2,1)}, bf16[8,1024,256]{2,1,0:T(8,128)(2,1)}) custom-call(s32[17]{0:T(128)} %stack.194.order_ref, bf16[1024,768]{1,0:T(8,128)(2,1)} %get-tuple-element.180.refs_0_, ...), custom_call_target="tpu_custom_call", output_to_operand_aliasing={{2}: (19, {}), {3}: (20, {})} | custom-call | tf_op jit(solution)/shard_map/expert_grads/pallas_call | solution.py:368
  222.9 6.3 collective-permute-done.23
  233.0 2.6 add_convert_fusion.8
  236.2 11.8 %expert_grads.10 = (bf16[1,1536,384]{2,1,0:T(8,128)(2,1)}, bf16[1,1536,384]{2,1,0:T(8,128)(2,1)}, bf16[8,1024,512]{2,1,0:T(8,128)(2,1)}, bf16[8,1024,256]{2,1,0:T(8,128)(2,1)}) custom-call(s32[17]{0:T(128)} %stack.194.order_ref, bf16[1024,768]{1,0:T(8,128)(2,1)} %get-tuple-element.180.refs_0_, ...), custom_call_target="tpu_custom_call", output_to_operand_aliasing={{2}: (19, {}), {3}: (20, {})} | custom-call | tf_op jit(solution)/shard_map/expert_grads/pallas_call | solution.py:368
  248.0 11.5 %collective-permute-done.25 = bf16[1,1536,384]{2,1,0:T(8,128)(2,1)S(1)} collective-permute-done((bf16[1,1536,384]{2,1,0:T(8,128)(2,1)}, bf16[1,1536,384]{2,1,0:T(8,128)(2,1)S(1)}, u32[]{:S(2)}, u32[]{:S(2)}) %collective-permute-start.25) | collective-permute-done | bytes 1179680 | tf_op jit(solution)/shard_map/ppermute | solution.py:615
  265.0 2.7 add_convert_fusion.6
  269.7 11.9 %expert_grads.11 = (bf16[1,1536,384]{2,1,0:T(8,128)(2,1)}, bf16[1,1536,384]{2,1,0:T(8,128)(2,1)}, bf16[1,1024,512]{2,1,0:T(8,128)(2,1)}, bf16[1,1024,256]{2,1,0:T(8,128)(2,1)}) custom-call(s32[17]{0:T(128)} %stack.194.order_ref, bf16[1024,768]{1,0:T(8,128)(2,1)} %get-tuple-element.180.refs_0_, bf16[1024,768]{1,0:T(8,128)(2,1)} %get-tuple-element.181.refs_1_, ...), custom_call_target="tpu_custom_call" | custom-call | tf_op jit(solution)/shard_map/expert_grads/pallas_call | solution.py:368
  281.5 7.0 collective-permute-done.27
  288.5 2.6 add_convert_fusion.5
  291.1 2.8 collective-permute-start.32
  293.9 2.6 add_convert_fusion.4
  296.5 23.8 %mix.2 = (f32[1024,768]{1,0:T(8,128)}, bf16[1024,768]{1,0:T(8,128)(2,1)}) custom-call(s32[17]{0:T(128)} %stack.194.order_ref, bf16[8,1024,512]{2,1,0:T(8,128)(2,1)} %get-tuple-element.208.refs_0_, bf16[1,1024,512]{2,1,0:T(8,128)(2,1)} %get-tuple-element.216.refs_1_, bf16[16,768,256]{2,1,0:T(8,128)(2,1)} %refs_14_.1, bf16[16,768,256]{2,1,0:T(8,128)(2,1)} %refs_15_.1, ...), custom_call_target="tpu_custom_call" | custom-call | tf_op jit(solution)/shard_map/mix/pallas_call | solution.py:454
  328.4 3.1 add_convert_fusion.3
  335.8 10.6 %fusion.75 = (f32[3,1024]{1,0:T(4,128)S(1)}, f32[3,1024,1024]{1,2,0:T(8,128)}) fusion(pred[1024,1024]{0,1:T(8,128)(4,1)S(1)} %copy-done.77, bf16[1024,128,1]{1,0,2:T(8,128)(2,1)S(1)} %maximum_bitcast_fusion, bf16[1024,3,128]{0,2,1:T(8,128)(2,1)} %bitcast.249), kind=kOutput, calls=%fused_computation.230 | convolution fusion | flops 817890304 | bytes 14692352 | tf_op jit(solution)/shard_map/sub | solution.py:124
  347.6 7.3 collective-permute-done.34
  354.9 2.6 add_convert_fusion.2
  358.3 14.9 %mix.3 = (f32[1024,768]{1,0:T(8,128)}, bf16[1024,768]{1,0:T(8,128)(2,1)}) custom-call(s32[17]{0:T(128)} %stack.194.order_ref, bf16[8,1024,256]{2,1,0:T(8,128)(2,1)} %get-tuple-element.209.refs_0_, bf16[1,1024,256]{2,1,0:T(8,128)(2,1)} %get-tuple-element.226.refs_1_, bf16[16,256,768]{2,1,0:T(8,128)(2,1)} %refs_8_.3, ...), custom_call_target="tpu_custom_call" | custom-call | tf_op jit(solution)/shard_map/mix/pallas_call | solution.py:454
  375.7 2.6 add_convert_fusion.1
  378.5 3.1 fusion.74
  386.8 3.4 convolution_convert_fusion.2
  392.7 4.7 unpack.8
  402.2 7.0 fusion.40
  409.4 5.9 fusion.1
  415.3 6.7 fusion.3
  425.3 2.7 convolution_convert_fusion.1
  434.9 3.8 dynamic-slice_bitcast_fusion.1
  448.5 4.3 convolution_convert_fusion
  456.6 5.1 unpack.9
  461.6 7.0 collective-permute-done.54.refs_0_
  472.1 3.1 fusion.44
  483.4 28.4 %collective-permute-done.59 = bf16[2,96,896]{2,1,0:T(8,128)(2,1)S(1)} collective-permute-done((bf16[2,96,896]{2,1,0:T(8,128)(2,1)S(1)}, bf16[2,96,896]{2,1,0:T(8,128)(2,1)S(1)}, u32[]{:S(2)}, u32[]{:S(2)}) %collective-permute-start.59) | collective-permute-done | bytes 344096 | tf_op jit(solution)/shard_map/ppermute | solution.py:615
  516.6 4.0 collective-permute-done.60
  521.9 5.1 unpack.10
  533.1 2.9 fusion.19
  539.2 4.8 unpack.11
  547.6 24.9 %collective-permute-done.67 = bf16[2,96,896]{2,1,0:T(8,128)(2,1)S(1)} collective-permute-done((bf16[2,96,896]{2,1,0:T(8,128)(2,1)S(1)}, bf16[2,96,896]{2,1,0:T(8,128)(2,1)S(1)}, u32[]{:S(2)}, u32[]{:S(2)}) %collective-permute-start.67) | collective-permute-done | bytes 344096 | tf_op jit(solution)/shard_map/ppermute | solution.py:615
  578.4 7.8 %collective-permute-done.68 = bf16[2,96,896]{2,1,0:T(8,128)(2,1)S(1)} collective-permute-done((bf16[2,96,896]{2,1,0:T(8,128)(2,1)S(1)}, bf16[2,96,896]{2,1,0:T(8,128)(2,1)S(1)}, u32[]{:S(2)}, u32[]{:S(2)}) %collective-permute-start.68) | collective-permute-done | bytes 344096 | tf_op jit(solution)/shard_map/ppermute | solution.py:615
  589.9 3.3 collective-permute-start.46
  598.5 4.8 collective-permute-done.73
  611.6 4.7 unpack.12
  616.8 24.3 %collective-permute-done.80 = bf16[2,96,896]{2,1,0:T(8,128)(2,1)} collective-permute-done((bf16[2,96,896]{2,1,0:T(8,128)(2,1)}, bf16[2,96,896]{2,1,0:T(8,128)(2,1)}, u32[]{:S(2)}, u32[]{:S(2)}) %collective-permute-start.80) | collective-permute-done | bytes 344096 | tf_op jit(solution)/shard_map/ppermute | solution.py:615
  645.3 6.5 collective-permute-done.81
  657.2 4.7 unpack.13
  666.4 29.4 %collective-permute-done.83 = bf16[2,96,896]{2,1,0:T(8,128)(2,1)S(1)} collective-permute-done((bf16[2,96,896]{2,1,0:T(8,128)(2,1)S(1)}, bf16[2,96,896]{2,1,0:T(8,128)(2,1)S(1)}, u32[]{:S(2)}, u32[]{:S(2)}) %collective-permute-start.83) | collective-permute-done | bytes 344096 | tf_op jit(solution)/shard_map/ppermute | solution.py:615
  697.9 7.9 %collective-permute-done.84 = bf16[2,96,896]{2,1,0:T(8,128)(2,1)S(1)} collective-permute-done((bf16[2,96,896]{2,1,0:T(8,128)(2,1)S(1)}, bf16[2,96,896]{2,1,0:T(8,128)(2,1)S(1)}, u32[]{:S(2)}, u32[]{:S(2)}) %collective-permute-start.84) | collective-permute-done | bytes 344096 | tf_op jit(solution)/shard_map/ppermute | solution.py:615
  711.1 4.7 unpack.14
  721.3 27.7 %collective-permute-done.91 = bf16[2,96,896]{2,1,0:T(8,128)(2,1)S(1)} collective-permute-done((bf16[2,96,896]{2,1,0:T(8,128)(2,1)}, bf16[2,96,896]{2,1,0:T(8,128)(2,1)S(1)}, u32[]{:S(2)}, u32[]{:S(2)}) %collective-permute-start.91) | collective-permute-done | bytes 344096 | tf_op jit(solution)/shard_map/ppermute | solution.py:615
  751.5 7.4 unpack_late.1
  758.9 4.7 unpack.15
  (496 shorter events, 184.5 us)
Async XLA Ops:
  5.3 27.1 %collective-permute-start.1 = (bf16[512,768]{1,0:T(8,128)(2,1)S(1)}, bf16[512,768]{1,0:T(8,128)(2,1)S(1)}, u32[]{:S(2)}, u32[]{:S(2)}) collective-permute-start(bf16[512,768]{1,0:T(8,128)(2,1)S(1)} %copy-done.14), channel_id=1, source_target_pairs={{0,2},{2,0},{1,3},{3,1},{4,6},{6,4},{5,7},{7,5},{8,10},{10,8},{9,1... | collective-permute-start | bytes 2359304 | tf_op jit(solution)/shard_map/ppermute | solution.py:47
  9.3 23.1 %collective-permute-start.4 = (bf16[192,768]{1,0:T(8,128)(2,1)S(1)}, bf16[192,768]{1,0:T(8,128)(2,1)}, u32[]{:S(2)}, u32[]{:S(2)}) collective-permute-start(bf16[192,768]{1,0:T(8,128)(2,1)S(1)} %constant_dynamic-slice_fusion), channel_id=1, source_target_pairs={{0,2},{2,0},{1,3},{3,1},{4,6},{6,4},{5,7},{7,5},{8,10},{10,8},{9,1... | collective-permute-start | bytes 884744 | tf_op jit(solution)/shard_map/ppermute | solution.py:47
  32.4 20.3 %collective-permute-start.5 = (bf16[512,768]{1,0:T(8,128)(2,1)S(1)}, bf16[512,768]{1,0:T(8,128)(2,1)S(1)}, u32[]{:S(2)}, u32[]{:S(2)}) collective-permute-start(bf16[512,768]{1,0:T(8,128)(2,1)S(1)} %collective-permute-done.1.own_ref.refs_2_), channel_id=1, source_target_pairs={{0,1},{1,0},{2,3},{3,2},{4,5},{5,4},{6,7},{7,6},{8,9},{9,8},{10,11... | collective-permute-start | bytes 2359304 | tf_op jit(solution)/shard_map/ppermute | solution.py:47
  39.2 13.6 %collective-permute-start.9 = (bf16[192,768]{1,0:T(8,128)(2,1)}, bf16[192,768]{1,0:T(8,128)(2,1)S(1)}, u32[]{:S(2)}, u32[]{:S(2)}) collective-permute-start(bf16[192,768]{1,0:T(8,128)(2,1)} %collective-permute-done.4), channel_id=1, source_target_pairs={{0,12},{4,8},{8,4},{12,0},{16,28},{20,24},{24,20},{28,16},{1,13},{... | collective-permute-start | bytes 884744 | tf_op jit(solution)/shard_map/ppermute | solution.py:647
  43.9 85.3 %collective-permute-start.17 = (bf16[16,768,256]{2,1,0:T(8,128)(2,1)}, bf16[16,768,256]{2,1,0:T(8,128)(2,1)}, u32[]{:S(2)}, u32[]{:S(2)}) collective-permute-start(bf16[16,768,256]{2,1,0:T(8,128)(2,1)} %refs_14_.1), channel_id=1, source_target_pairs={{0,1},{1,0},{2,3},{3,2},{4,5},{5,4},{6,7},{7,6},{8,9},{9,8},{10,11... | collective-permute-start | bytes 18874376 | tf_op jit(solution)/shard_map/ppermute | solution.py:47
  65.2 64.0 %collective-permute-start.18 = (bf16[16,768,256]{2,1,0:T(8,128)(2,1)}, bf16[16,768,256]{2,1,0:T(8,128)(2,1)}, u32[]{:S(2)}, u32[]{:S(2)}) collective-permute-start(bf16[16,768,256]{2,1,0:T(8,128)(2,1)} %refs_15_.1), channel_id=1, source_target_pairs={{0,1},{1,0},{2,3},{3,2},{4,5},{5,4},{6,7},{7,6},{8,9},{9,8},{10,11... | collective-permute-start | bytes 18874376 | tf_op jit(solution)/shard_map/ppermute | solution.py:47
  65.2 64.0 %collective-permute-start.19 = (bf16[16,256,768]{2,1,0:T(8,128)(2,1)}, bf16[16,256,768]{2,1,0:T(8,128)(2,1)}, u32[]{:S(2)}, u32[]{:S(2)}) collective-permute-start(bf16[16,256,768]{2,1,0:T(8,128)(2,1)} %refs_8_.3), channel_id=1, source_target_pairs={{0,1},{1,0},{2,3},{3,2},{4,5},{5,4},{6,7},{7,6},{8,9},{9,8},{10,11... | collective-permute-start | bytes 18874376 | tf_op jit(solution)/shard_map/ppermute | solution.py:47
  65.8 13.2 %collective-permute-start.11 = (bf16[320,768]{1,0:T(8,128)(2,1)S(1)}, bf16[320,768]{1,0:T(8,128)(2,1)S(1)}, u32[]{:S(2)}, u32[]{:S(2)}) collective-permute-start(bf16[320,768]{1,0:T(8,128)(2,1)S(1)} %slice.204), channel_id=1, source_target_pairs={{0,2},{2,0},{1,3},{3,1},{4,6},{6,4},{5,7},{7,5},{8,10},{10,8},{9,1... | collective-permute-start | bytes 1474568 | tf_op jit(solution)/shard_map/ppermute | solution.py:47
  66.2 14.6 %collective-permute-start.10 = (bf16[1024,384]{1,0:T(8,128)(2,1)}, bf16[1024,384]{1,0:T(8,128)(2,1)S(1)}, u32[]{:S(2)}, u32[]{:S(2)}) collective-permute-start(bf16[1024,384]{1,0:T(8,128)(2,1)} %attend.1.refs_4_), channel_id=1, source_target_pairs={{0,1},{1,0},{2,3},{3,2},{4,5},{5,4},{6,7},{7,6},{8,9},{9,8},{10,11... | collective-permute-start | bytes 2359304 | tf_op jit(solution)/shard_map/ppermute | solution.py:47
  79.0 18.9 %collective-permute-start.12 = (bf16[1024,384]{1,0:T(8,128)(2,1)}, bf16[1024,384]{1,0:T(8,128)(2,1)}, u32[]{:S(2)}, u32[]{:S(2)}) collective-permute-start(bf16[1024,384]{1,0:T(8,128)(2,1)} %attend.1.refs_4_), channel_id=1, source_target_pairs={{0,2},{2,0},{1,3},{3,1},{4,6},{6,4},{5,7},{7,5},{8,10},{10,8},{9,1... | collective-permute-start | bytes 2359304 | tf_op jit(solution)/shard_map/ppermute | solution.py:47
  80.8 17.3 %collective-permute-start.13 = (bf16[768,768]{1,0:T(8,128)(2,1)S(1)}, bf16[768,768]{1,0:T(8,128)(2,1)}, u32[]{:S(2)}, u32[]{:S(2)}) collective-permute-start(bf16[768,768]{1,0:T(8,128)(2,1)S(1)} %pad_maximum_fusion.5.refs_10_.refs_11_), channel_id=1, source_target_pairs={{0,1},{1,0},{2,3},{3,2},{4,5},{5,4},{6,7},{7,6},{8,9},{9,8},{10,11... | collective-permute-start | bytes 3538952 | tf_op jit(solution)/shard_map/ppermute | solution.py:47
  98.9 30.3 %collective-permute-start.16 = (bf16[1024,768]{1,0:T(8,128)(2,1)S(1)}, bf16[1024,768]{1,0:T(8,128)(2,1)S(1)}, u32[]{:S(2)}, u32[]{:S(2)}) collective-permute-start(bf16[1024,768]{1,0:T(8,128)(2,1)S(1)} %pad_maximum_fusion.2.refs_2_), channel_id=1, source_target_pairs={{0,1},{1,0},{2,3},{3,2},{4,5},{5,4},{6,7},{7,6},{8,9},{9,8},{10,11... | collective-permute-start | bytes 4718600 | tf_op jit(solution)/shard_map/ppermute | solution.py:47
  101.9 13.9 %collective-permute-start.14 = (bf16[1024,384]{1,0:T(8,128)(2,1)}, bf16[1024,384]{1,0:T(8,128)(2,1)}, u32[]{:S(2)}, u32[]{:S(2)}) collective-permute-start(bf16[1024,384]{1,0:T(8,128)(2,1)} %collective-permute-done.12.refs_6_), channel_id=1, source_target_pairs={{0,1},{1,0},{2,3},{3,2},{4,5},{5,4},{6,7},{7,6},{8,9},{9,8},{10,11... | collective-permute-start | bytes 2359304 | tf_op jit(solution)/shard_map/ppermute | solution.py:47
  142.6 28.4 %collective-permute-start.20 = (bf16[1,1536,384]{2,1,0:T(8,128)(2,1)}, bf16[1,1536,384]{2,1,0:T(8,128)(2,1)S(1)}, u32[]{:S(2)}, u32[]{:S(2)}) collective-permute-start(bf16[1,1536,384]{2,1,0:T(8,128)(2,1)} %get-tuple-element.184), channel_id=1, source_target_pairs={{0,8},{8,16},{16,24},{24,28},{28,20},{20,12},{12,4},{4,0},{9,1},{1... | collective-permute-start | bytes 3538952 | tf_op jit(solution)/shard_map/ppermute | solution.py:615
  144.2 30.3 %collective-permute-start.22 = (bf16[1,1536,384]{2,1,0:T(8,128)(2,1)}, bf16[1,1536,384]{2,1,0:T(8,128)(2,1)S(1)}, u32[]{:S(2)}, u32[]{:S(2)}) collective-permute-start(bf16[1,1536,384]{2,1,0:T(8,128)(2,1)} %get-tuple-element.185), channel_id=1, source_target_pairs={{8,0},{16,8},{24,16},{28,24},{20,28},{12,20},{4,12},{0,4},{1,9},{9... | collective-permute-start | bytes 3538952 | tf_op jit(solution)/shard_map/ppermute | solution.py:615
  172.6 28.0 %collective-permute-start.21 = (bf16[1,1536,384]{2,1,0:T(8,128)(2,1)S(1)}, bf16[1,1536,384]{2,1,0:T(8,128)(2,1)S(1)}, u32[]{:S(2)}, u32[]{:S(2)}) collective-permute-start(bf16[1,1536,384]{2,1,0:T(8,128)(2,1)S(1)} %add_convert_fusion.13), channel_id=1, source_target_pairs={{0,8},{8,16},{16,24},{24,28},{28,20},{20,12},{12,4},{4,0},{9,1},{1... | collective-permute-start | bytes 3538952 | tf_op jit(solution)/shard_map/ppermute | solution.py:615
  175.8 27.2 %collective-permute-start.24 = (bf16[1,1536,384]{2,1,0:T(8,128)(2,1)}, bf16[1,1536,384]{2,1,0:T(8,128)(2,1)S(1)}, u32[]{:S(2)}, u32[]{:S(2)}) collective-permute-start(bf16[1,1536,384]{2,1,0:T(8,128)(2,1)} %add_convert_fusion.12), channel_id=1, source_target_pairs={{8,0},{16,8},{24,16},{28,24},{20,28},{12,20},{4,12},{0,4},{1,9},{9... | collective-permute-start | bytes 3538952 | tf_op jit(solution)/shard_map/ppermute | solution.py:615
  201.0 28.2 %collective-permute-start.23 = (bf16[1,1536,384]{2,1,0:T(8,128)(2,1)S(1)}, bf16[1,1536,384]{2,1,0:T(8,128)(2,1)S(1)}, u32[]{:S(2)}, u32[]{:S(2)}) collective-permute-start(bf16[1,1536,384]{2,1,0:T(8,128)(2,1)S(1)} %add_convert_fusion.11), channel_id=1, source_target_pairs={{0,8},{8,16},{16,24},{24,28},{28,20},{20,12},{12,4},{4,0},{9,1},{1... | collective-permute-start | bytes 3538952 | tf_op jit(solution)/shard_map/ppermute | solution.py:615
  204.4 28.7 %collective-permute-start.26 = (bf16[1,1536,384]{2,1,0:T(8,128)(2,1)}, bf16[1,1536,384]{2,1,0:T(8,128)(2,1)}, u32[]{:S(2)}, u32[]{:S(2)}) collective-permute-start(bf16[1,1536,384]{2,1,0:T(8,128)(2,1)} %add_convert_fusion.10), channel_id=1, source_target_pairs={{8,0},{16,8},{24,16},{28,24},{20,28},{12,20},{4,12},{0,4},{1,9},{9... | collective-permute-start | bytes 3538952 | tf_op jit(solution)/shard_map/ppermute | solution.py:615
  230.5 29.0 %collective-permute-start.25 = (bf16[1,1536,384]{2,1,0:T(8,128)(2,1)}, bf16[1,1536,384]{2,1,0:T(8,128)(2,1)S(1)}, u32[]{:S(2)}, u32[]{:S(2)}) collective-permute-start(bf16[1,1536,384]{2,1,0:T(8,128)(2,1)} %add_convert_fusion.9), channel_id=1, source_target_pairs={{0,8},{8,16},{16,24},{24,28},{28,20},{20,12},{12,4},{4,0},{9,1},{1... | collective-permute-start | bytes 3538952 | tf_op jit(solution)/shard_map/ppermute | solution.py:615
  235.6 29.3 %collective-permute-start.28 = (bf16[1,1536,384]{2,1,0:T(8,128)(2,1)}, bf16[1,1536,384]{2,1,0:T(8,128)(2,1)}, u32[]{:S(2)}, u32[]{:S(2)}) collective-permute-start(bf16[1,1536,384]{2,1,0:T(8,128)(2,1)} %add_convert_fusion.8), channel_id=1, source_target_pairs={{8,0},{16,8},{24,16},{28,24},{20,28},{12,20},{4,12},{0,4},{1,9},{9... | collective-permute-start | bytes 3538952 | tf_op jit(solution)/shard_map/ppermute | solution.py:615
  235.6 32.0 %collective-permute-start.29 = (bf16[1,768,512]{2,1,0:T(8,128)(2,1)S(1)}, bf16[1,768,512]{2,1,0:T(8,128)(2,1)S(1)}, u32[]{:S(2)}, u32[]{:S(2)}) collective-permute-start(bf16[1,768,512]{2,1,0:T(8,128)(2,1)S(1)} %bitcast.226), channel_id=1, source_target_pairs={{0,1},{1,0},{2,3},{3,2},{4,5},{5,4},{6,7},{7,6},{8,9},{9,8},{10,11... | collective-permute-start | bytes 2359304 | tf_op jit(solution)/shard_map/ppermute | solution.py:47
  235.7 32.0 %collective-permute-start.30 = (bf16[1,768,512]{2,1,0:T(8,128)(2,1)S(1)}, bf16[1,768,512]{2,1,0:T(8,128)(2,1)S(1)}, u32[]{:S(2)}, u32[]{:S(2)}) collective-permute-start(bf16[1,768,512]{2,1,0:T(8,128)(2,1)S(1)} %bitcast.231), channel_id=1, source_target_pairs={{0,1},{1,0},{2,3},{3,2},{4,5},{5,4},{6,7},{7,6},{8,9},{9,8},{10,11... | collective-permute-start | bytes 2359304 | tf_op jit(solution)/shard_map/ppermute | solution.py:47
  262.5 26.0 %collective-permute-start.27 = (bf16[1,1536,384]{2,1,0:T(8,128)(2,1)S(1)}, bf16[1,1536,384]{2,1,0:T(8,128)(2,1)}, u32[]{:S(2)}, u32[]{:S(2)}) collective-permute-start(bf16[1,1536,384]{2,1,0:T(8,128)(2,1)S(1)} %add_convert_fusion.7), channel_id=1, source_target_pairs={{0,8},{8,16},{16,24},{24,28},{28,20},{20,12},{12,4},{4,0},{9,1},{1... | collective-permute-start | bytes 3538952 | tf_op jit(solution)/shard_map/ppermute | solution.py:615
  267.7 26.2 %collective-permute-start.33 = (bf16[1,1536,384]{2,1,0:T(8,128)(2,1)}, bf16[1,1536,384]{2,1,0:T(8,128)(2,1)}, u32[]{:S(2)}, u32[]{:S(2)}) collective-permute-start(bf16[1,1536,384]{2,1,0:T(8,128)(2,1)} %add_convert_fusion.6), channel_id=1, source_target_pairs={{8,0},{16,8},{24,16},{28,24},{20,28},{12,20},{4,12},{0,4},{1,9},{9... | collective-permute-start | bytes 3538952 | tf_op jit(solution)/shard_map/ppermute | solution.py:615
  291.1 37.3 %collective-permute-start.32 = (bf16[1,1536,384]{2,1,0:T(8,128)(2,1)}, bf16[1,1536,384]{2,1,0:T(8,128)(2,1)}, u32[]{:S(2)}, u32[]{:S(2)}) collective-permute-start(bf16[1,1536,384]{2,1,0:T(8,128)(2,1)} %add_convert_fusion.5), channel_id=1, source_target_pairs={{0,8},{8,16},{16,24},{24,28},{28,20},{20,12},{12,4},{4,0},{9,1},{1... | collective-permute-start | bytes 3538952 | tf_op jit(solution)/shard_map/ppermute | solution.py:615
  320.3 13.0 %collective-permute-start.37 = (bf16[1024,768]{1,0:T(8,128)(2,1)}, bf16[1024,768]{1,0:T(8,128)(2,1)S(1)}, u32[]{:S(2)}, u32[]{:S(2)}) collective-permute-start(bf16[1024,768]{1,0:T(8,128)(2,1)} %get-tuple-element.222), channel_id=1, source_target_pairs={{0,1},{1,0},{2,3},{3,2},{4,5},{5,4},{6,7},{7,6},{8,9},{9,8},{10,11... | collective-permute-start | bytes 4718600 | tf_op jit(solution)/shard_map/ppermute | solution.py:47
  328.3 26.6 %collective-permute-start.34 = (bf16[1,1536,384]{2,1,0:T(8,128)(2,1)}, bf16[1,1536,384]{2,1,0:T(8,128)(2,1)}, u32[]{:S(2)}, u32[]{:S(2)}) collective-permute-start(bf16[1,1536,384]{2,1,0:T(8,128)(2,1)} %add_convert_fusion.4), channel_id=1, source_target_pairs={{8,0},{16,8},{24,16},{28,24},{20,28},{12,20},{4,12},{0,4},{1,9},{9... | collective-permute-start | bytes 3538952 | tf_op jit(solution)/shard_map/ppermute | solution.py:615
  331.5 41.7 %collective-permute-start.48 = (bf16[1,1536,384]{2,1,0:T(8,128)(2,1)}, bf16[1,1536,384]{2,1,0:T(8,128)(2,1)}, u32[]{:S(2)}, u32[]{:S(2)}) collective-permute-start(bf16[1,1536,384]{2,1,0:T(8,128)(2,1)} %add_convert_fusion.3), channel_id=1, source_target_pairs={{0,8},{8,16},{16,24},{24,28},{28,20},{20,12},{12,4},{4,0},{9,1},{1... | collective-permute-start | bytes 3538952 | tf_op jit(solution)/shard_map/ppermute | solution.py:615
  335.0 38.2 %collective-permute-start.38 = (bf16[1024,768]{1,0:T(8,128)(2,1)}, bf16[1024,768]{1,0:T(8,128)(2,1)}, u32[]{:S(2)}, u32[]{:S(2)}) collective-permute-start(bf16[1024,768]{1,0:T(8,128)(2,1)} %fusion.11), channel_id=1, source_target_pairs={{0,2},{2,0},{1,3},{3,1},{4,6},{6,4},{5,7},{7,5},{8,10},{10,8},{9,1... | collective-permute-start | bytes 4718600 | tf_op jit(solution)/shard_map/ppermute | solution.py:47
  357.5 20.9 %collective-permute-start.49 = (bf16[1,1536,384]{2,1,0:T(8,128)(2,1)}, bf16[1,1536,384]{2,1,0:T(8,128)(2,1)}, u32[]{:S(2)}, u32[]{:S(2)}) collective-permute-start(bf16[1,1536,384]{2,1,0:T(8,128)(2,1)} %add_convert_fusion.2), channel_id=1, source_target_pairs={{8,0},{16,8},{24,16},{28,24},{20,28},{12,20},{4,12},{0,4},{1,9},{9... | collective-permute-start | bytes 3538952 | tf_op jit(solution)/shard_map/ppermute | solution.py:615
  381.7 15.7 %collective-permute-start.40 = (bf16[1024,768]{1,0:T(8,128)(2,1)}, bf16[1024,768]{1,0:T(8,128)(2,1)}, u32[]{:S(2)}, u32[]{:S(2)}) collective-permute-start(bf16[1024,768]{1,0:T(8,128)(2,1)} %get-tuple-element.330), channel_id=1, source_target_pairs={{0,1},{1,0},{2,3},{3,2},{4,5},{5,4},{6,7},{7,6},{8,9},{9,8},{10,11... | collective-permute-start | bytes 4718600 | tf_op jit(solution)/shard_map/ppermute | solution.py:47
  386.4 68.4 %collective-permute-start.35 = (bf16[1024,768]{1,0:T(8,128)(2,1)}, bf16[1024,768]{1,0:T(8,128)(2,1)}, u32[]{:S(2)}, u32[]{:S(2)}) collective-permute-start(bf16[1024,768]{1,0:T(8,128)(2,1)} %get-tuple-element.228), channel_id=1, source_target_pairs={{0,1},{1,0},{2,3},{3,2},{4,5},{5,4},{6,7},{7,6},{8,9},{9,8},{10,11... | collective-permute-start | bytes 4718600 | tf_op jit(solution)/shard_map/ppermute | solution.py:47
  386.5 53.0 %collective-permute-start.53 = (bf16[1,768,768]{2,1,0:T(8,128)(2,1)S(1)}, bf16[1,768,768]{2,1,0:T(8,128)(2,1)}, u32[]{:S(2)}, u32[]{:S(2)}) collective-permute-start(bf16[1,768,768]{2,1,0:T(8,128)(2,1)S(1)} %pad_maximum_fusion.7.refs_1_), channel_id=1, source_target_pairs={{8,0},{16,8},{24,16},{28,24},{20,28},{12,20},{4,12},{0,4},{1,9},{9... | collective-permute-start | bytes 3538952 | tf_op jit(solution)/shard_map/ppermute | solution.py:615
  390.4 49.1 %collective-permute-start.51 = (bf16[1,768,768]{2,1,0:T(8,128)(2,1)S(1)}, bf16[1,768,768]{2,1,0:T(8,128)(2,1)}, u32[]{:S(2)}, u32[]{:S(2)}) collective-permute-start(bf16[1,768,768]{2,1,0:T(8,128)(2,1)S(1)} %pad_maximum_fusion.6.refs_0_), channel_id=1, source_target_pairs={{0,8},{8,16},{16,24},{24,28},{28,20},{20,12},{12,4},{4,0},{9,1},{1... | collective-permute-start | bytes 3538952 | tf_op jit(solution)/shard_map/ppermute | solution.py:615
  439.5 29.1 %collective-permute-start.54 = (bf16[1,768,768]{2,1,0:T(8,128)(2,1)}, bf16[1,768,768]{2,1,0:T(8,128)(2,1)}, u32[]{:S(2)}, u32[]{:S(2)}) collective-permute-start(bf16[1,768,768]{2,1,0:T(8,128)(2,1)} %collective-permute-done.51.refs_0_), channel_id=1, source_target_pairs={{0,8},{8,16},{16,24},{24,28},{28,20},{20,12},{12,4},{4,0},{9,1},{1... | collective-permute-start | bytes 3538952 | tf_op jit(solution)/shard_map/ppermute | solution.py:615
  441.1 27.5 %collective-permute-start.55 = (bf16[1,768,768]{2,1,0:T(8,128)(2,1)}, bf16[1,768,768]{2,1,0:T(8,128)(2,1)}, u32[]{:S(2)}, u32[]{:S(2)}) collective-permute-start(bf16[1,768,768]{2,1,0:T(8,128)(2,1)} %collective-permute-done.53.refs_1_), channel_id=1, source_target_pairs={{8,0},{16,8},{24,16},{28,24},{20,28},{12,20},{4,12},{0,4},{1,9},{9... | collective-permute-start | bytes 3538952 | tf_op jit(solution)/shard_map/ppermute | solution.py:615
  452.9 28.5 %collective-permute-start.41 = (bf16[1024,768]{1,0:T(8,128)(2,1)}, bf16[1024,768]{1,0:T(8,128)(2,1)S(1)}, u32[]{:S(2)}, u32[]{:S(2)}) collective-permute-start(bf16[1024,768]{1,0:T(8,128)(2,1)} %convolution_convert_fusion), channel_id=1, source_target_pairs={{0,1},{1,0},{2,3},{3,2},{4,5},{5,4},{6,7},{7,6},{8,9},{9,8},{10,11... | collective-permute-start | bytes 4718600 | tf_op jit(solution)/shard_map/ppermute | solution.py:47
  471.0 62.2 %collective-permute-start.36 = (bf16[512,768]{1,0:T(8,128)(2,1)}, bf16[512,768]{1,0:T(8,128)(2,1)}, u32[]{:S(2)}, u32[]{:S(2)}) collective-permute-start(bf16[512,768]{1,0:T(8,128)(2,1)} %dynamic-slice_convert_fusion.1), channel_id=1, source_target_pairs={{0,2},{2,0},{1,3},{3,1},{4,6},{6,4},{5,7},{7,5},{8,10},{10,8},{9,1... | collective-permute-start | bytes 2359304 | tf_op jit(solution)/shard_map/ppermute | solution.py:47
  475.3 55.5 %collective-permute-start.56 = (bf16[1,768,768]{2,1,0:T(8,128)(2,1)}, bf16[1,768,768]{2,1,0:T(8,128)(2,1)}, u32[]{:S(2)}, u32[]{:S(2)}) collective-permute-start(bf16[1,768,768]{2,1,0:T(8,128)(2,1)} %collective-permute-done.54.refs_0_), channel_id=1, source_target_pairs={{0,8},{8,16},{16,24},{24,28},{28,20},{20,12},{12,4},{4,0},{9,1},{1... | collective-permute-start | bytes 3538952 | tf_op jit(solution)/shard_map/ppermute | solution.py:615
  478.8 52.0 %collective-permute-start.57 = (bf16[1,768,768]{2,1,0:T(8,128)(2,1)}, bf16[1,768,768]{2,1,0:T(8,128)(2,1)}, u32[]{:S(2)}, u32[]{:S(2)}) collective-permute-start(bf16[1,768,768]{2,1,0:T(8,128)(2,1)} %collective-permute-done.55.refs_1_), channel_id=1, source_target_pairs={{8,0},{16,8},{24,16},{28,24},{20,28},{12,20},{4,12},{0,4},{1,9},{9... | collective-permute-start | bytes 3538952 | tf_op jit(solution)/shard_map/ppermute | solution.py:615
  480.7 31.1 %collective-permute-start.59 = (bf16[2,96,896]{2,1,0:T(8,128)(2,1)S(1)}, bf16[2,96,896]{2,1,0:T(8,128)(2,1)S(1)}, u32[]{:S(2)}, u32[]{:S(2)}) collective-permute-start(bf16[2,96,896]{2,1,0:T(8,128)(2,1)S(1)} %add_convert_fusion.29), channel_id=1, source_target_pairs={{0,8},{8,16},{16,24},{24,28},{28,20},{20,12},{12,4},{4,0},{9,1},{1... | collective-permute-start | bytes 1032200 | tf_op jit(solution)/shard_map/ppermute | solution.py:615
  481.4 33.3 %collective-permute-start.62 = (bf16[2,96,896]{2,1,0:T(8,128)(2,1)S(1)}, bf16[2,96,896]{2,1,0:T(8,128)(2,1)S(1)}, u32[]{:S(2)}, u32[]{:S(2)}) collective-permute-start(bf16[2,96,896]{2,1,0:T(8,128)(2,1)S(1)} %add_convert_fusion.26), channel_id=1, source_target_pairs={{8,0},{16,8},{24,16},{28,24},{20,28},{12,20},{4,12},{0,4},{1,9},{9... | collective-permute-start | bytes 1032200 | tf_op jit(solution)/shard_map/ppermute | solution.py:615
  514.7 21.3 %collective-permute-start.42 = (bf16[512,768]{1,0:T(8,128)(2,1)}, bf16[512,768]{1,0:T(8,128)(2,1)S(1)}, u32[]{:S(2)}, u32[]{:S(2)}) collective-permute-start(bf16[512,768]{1,0:T(8,128)(2,1)} %dynamic-slice_convert_fusion), channel_id=1, source_target_pairs={{0,2},{2,0},{1,3},{3,1},{4,6},{6,4},{5,7},{7,5},{8,10},{10,8},{9,1... | collective-permute-start | bytes 2359304 | tf_op jit(solution)/shard_map/ppermute | solution.py:47
  530.8 13.2 %collective-permute-start.66 = (bf16[2,96,896]{2,1,0:T(8,128)(2,1)}, bf16[2,96,896]{2,1,0:T(8,128)(2,1)}, u32[]{:S(2)}, u32[]{:S(2)}) collective-permute-start(bf16[2,96,896]{2,1,0:T(8,128)(2,1)} %add_convert_fusion.27), channel_id=1, source_target_pairs={{0,8},{8,16},{16,24},{24,28},{28,20},{20,12},{12,4},{4,0},{9,1},{1... | collective-permute-start | bytes 1032200 | tf_op jit(solution)/shard_map/ppermute | solution.py:615
  536.7 56.4 %collective-permute-start.43 = (f32[512,1]{0,1:T(1,128)S(1)}, f32[512,1]{0,1:T(1,128)S(1)}, u32[]{:S(2)}, u32[]{:S(2)}) collective-permute-start(f32[512,1]{0,1:T(1,128)S(1)} %bitcast.258), channel_id=1, source_target_pairs={{0,1},{1,0},{2,3},{3,2},{4,5},{5,4},{6,7},{7,6},{8,9},{9,8},{10,11... | collective-permute-start | bytes 6152 | tf_op jit(solution)/shard_map/ppermute | solution.py:47
  536.8 51.4 %collective-permute-start.64 = (bf16[1,768,768]{2,1,0:T(8,128)(2,1)}, bf16[1,768,768]{2,1,0:T(8,128)(2,1)S(1)}, u32[]{:S(2)}, u32[]{:S(2)}) collective-permute-start(bf16[1,768,768]{2,1,0:T(8,128)(2,1)} %collective-permute-done.56.refs_0_), channel_id=1, source_target_pairs={{0,8},{8,16},{16,24},{24,28},{28,20},{20,12},{12,4},{4,0},{9,1},{1... | collective-permute-start | bytes 3538952 | tf_op jit(solution)/shard_map/ppermute | solution.py:615
  538.9 49.4 %collective-permute-start.65 = (bf16[1,768,768]{2,1,0:T(8,128)(2,1)}, bf16[1,768,768]{2,1,0:T(8,128)(2,1)S(1)}, u32[]{:S(2)}, u32[]{:S(2)}) collective-permute-start(bf16[1,768,768]{2,1,0:T(8,128)(2,1)} %collective-permute-done.57.refs_1_), channel_id=1, source_target_pairs={{8,0},{16,8},{24,16},{28,24},{20,28},{12,20},{4,12},{0,4},{1,9},{9... | collective-permute-start | bytes 3538952 | tf_op jit(solution)/shard_map/ppermute | solution.py:615
  545.3 27.3 %collective-permute-start.67 = (bf16[2,96,896]{2,1,0:T(8,128)(2,1)S(1)}, bf16[2,96,896]{2,1,0:T(8,128)(2,1)S(1)}, u32[]{:S(2)}, u32[]{:S(2)}) collective-permute-start(bf16[2,96,896]{2,1,0:T(8,128)(2,1)S(1)} %add_convert_fusion.23), channel_id=1, source_target_pairs={{0,8},{8,16},{16,24},{24,28},{28,20},{20,12},{12,4},{4,0},{9,1},{1... | collective-permute-start | bytes 1032200 | tf_op jit(solution)/shard_map/ppermute | solution.py:615
  547.2 28.9 %collective-permute-start.70 = (bf16[2,96,896]{2,1,0:T(8,128)(2,1)S(1)}, bf16[2,96,896]{2,1,0:T(8,128)(2,1)S(1)}, u32[]{:S(2)}, u32[]{:S(2)}) collective-permute-start(bf16[2,96,896]{2,1,0:T(8,128)(2,1)S(1)} %add_convert_fusion.20), channel_id=1, source_target_pairs={{8,0},{16,8},{24,16},{28,24},{20,28},{12,20},{4,12},{0,4},{1,9},{9... | collective-permute-start | bytes 1032200 | tf_op jit(solution)/shard_map/ppermute | solution.py:615
  605.0 40.2 %collective-permute-start.77 = (bf16[1,768,768]{2,1,0:T(8,128)(2,1)S(1)}, bf16[1,768,768]{2,1,0:T(8,128)(2,1)}, u32[]{:S(2)}, u32[]{:S(2)}) collective-permute-start(bf16[1,768,768]{2,1,0:T(8,128)(2,1)S(1)} %collective-permute-done.64.refs_0_), channel_id=1, source_target_pairs={{0,8},{8,16},{16,24},{24,28},{28,20},{20,12},{12,4},{4,0},{9,1},{1... | collective-permute-start | bytes 3538952 | tf_op jit(solution)/shard_map/ppermute | solution.py:615
  607.1 38.2 %collective-permute-start.78 = (bf16[1,768,768]{2,1,0:T(8,128)(2,1)S(1)}, bf16[1,768,768]{2,1,0:T(8,128)(2,1)}, u32[]{:S(2)}, u32[]{:S(2)}) collective-permute-start(bf16[1,768,768]{2,1,0:T(8,128)(2,1)S(1)} %collective-permute-done.65.refs_1_), channel_id=1, source_target_pairs={{8,0},{16,8},{24,16},{28,24},{20,28},{12,20},{4,12},{0,4},{1,9},{9... | collective-permute-start | bytes 3538952 | tf_op jit(solution)/shard_map/ppermute | solution.py:615
  608.2 33.0 %collective-permute-start.80 = (bf16[2,96,896]{2,1,0:T(8,128)(2,1)}, bf16[2,96,896]{2,1,0:T(8,128)(2,1)}, u32[]{:S(2)}, u32[]{:S(2)}) collective-permute-start(bf16[2,96,896]{2,1,0:T(8,128)(2,1)} %pad_maximum_fusion.11), channel_id=1, source_target_pairs={{8,0},{16,8},{24,16},{28,24},{20,28},{12,20},{4,12},{0,4},{1,9},{9... | collective-permute-start | bytes 1032200 | tf_op jit(solution)/shard_map/ppermute | solution.py:615
  610.9 32.2 %collective-permute-start.75 = (bf16[2,96,896]{2,1,0:T(8,128)(2,1)}, bf16[2,96,896]{2,1,0:T(8,128)(2,1)}, u32[]{:S(2)}, u32[]{:S(2)}) collective-permute-start(bf16[2,96,896]{2,1,0:T(8,128)(2,1)} %pad_maximum_fusion.10), channel_id=1, source_target_pairs={{0,8},{8,16},{16,24},{24,28},{28,20},{20,12},{12,4},{4,0},{9,1},{1... | collective-permute-start | bytes 1032200 | tf_op jit(solution)/shard_map/ppermute | solution.py:615
  653.8 11.3 %collective-permute-start.87 = (bf16[2,96,896]{2,1,0:T(8,128)(2,1)}, bf16[2,96,896]{2,1,0:T(8,128)(2,1)}, u32[]{:S(2)}, u32[]{:S(2)}) collective-permute-start(bf16[2,96,896]{2,1,0:T(8,128)(2,1)} %collective-permute-done.81), channel_id=1, source_target_pairs={{8,0},{16,8},{24,16},{28,24},{20,28},{12,20},{4,12},{0,4},{1,9},{9... | collective-permute-start | bytes 1032200 | tf_op jit(solution)/shard_map/ppermute | solution.py:615
  655.1 50.8 %collective-permute-start.85 = (bf16[1,768,768]{2,1,0:T(8,128)(2,1)}, bf16[1,768,768]{2,1,0:T(8,128)(2,1)S(1)}, u32[]{:S(2)}, u32[]{:S(2)}) collective-permute-start(bf16[1,768,768]{2,1,0:T(8,128)(2,1)} %collective-permute-done.77.refs_0_), channel_id=1, source_target_pairs={{0,8},{8,16},{16,24},{24,28},{28,20},{20,12},{12,4},{4,0},{9,1},{1... | collective-permute-start | bytes 3538952 | tf_op jit(solution)/shard_map/ppermute | solution.py:615
  656.9 49.0 %collective-permute-start.86 = (bf16[1,768,768]{2,1,0:T(8,128)(2,1)}, bf16[1,768,768]{2,1,0:T(8,128)(2,1)S(1)}, u32[]{:S(2)}, u32[]{:S(2)}) collective-permute-start(bf16[1,768,768]{2,1,0:T(8,128)(2,1)} %collective-permute-done.78.refs_1_), channel_id=1, source_target_pairs={{8,0},{16,8},{24,16},{28,24},{20,28},{12,20},{4,12},{0,4},{1,9},{9... | collective-permute-start | bytes 3538952 | tf_op jit(solution)/shard_map/ppermute | solution.py:615
  663.1 32.6 %collective-permute-start.83 = (bf16[2,96,896]{2,1,0:T(8,128)(2,1)S(1)}, bf16[2,96,896]{2,1,0:T(8,128)(2,1)S(1)}, u32[]{:S(2)}, u32[]{:S(2)}) collective-permute-start(bf16[2,96,896]{2,1,0:T(8,128)(2,1)S(1)} %collective-permute-done.82), channel_id=1, source_target_pairs={{0,8},{8,16},{16,24},{24,28},{28,20},{20,12},{12,4},{4,0},{9,1},{1... | collective-permute-start | bytes 1032200 | tf_op jit(solution)/shard_map/ppermute | solution.py:615
  665.1 31.7 %collective-permute-start.88 = (bf16[2,96,896]{2,1,0:T(8,128)(2,1)}, bf16[2,96,896]{2,1,0:T(8,128)(2,1)S(1)}, u32[]{:S(2)}, u32[]{:S(2)}) collective-permute-start(bf16[2,96,896]{2,1,0:T(8,128)(2,1)} %collective-permute-done.87), channel_id=1, source_target_pairs={{8,0},{16,8},{24,16},{28,24},{20,28},{12,20},{4,12},{0,4},{1,9},{9... | collective-permute-start | bytes 1032200 | tf_op jit(solution)/shard_map/ppermute | solution.py:615
  706.2 11.3 %collective-permute-start.92 = (bf16[2,96,896]{2,1,0:T(8,128)(2,1)}, bf16[2,96,896]{2,1,0:T(8,128)(2,1)}, u32[]{:S(2)}, u32[]{:S(2)}) collective-permute-start(bf16[2,96,896]{2,1,0:T(8,128)(2,1)} %collective-permute-done.89), channel_id=1, source_target_pairs={{8,0},{16,8},{24,16},{28,24},{20,28},{12,20},{4,12},{0,4},{1,9},{9... | collective-permute-start | bytes 1032200 | tf_op jit(solution)/shard_map/ppermute | solution.py:615
  708.0 50.9 %collective-permute-start.94 = (bf16[1,768,768]{2,1,0:T(8,128)(2,1)S(1)}, bf16[1,768,768]{2,1,0:T(8,128)(2,1)}, u32[]{:S(2)}, u32[]{:S(2)}) collective-permute-start(bf16[1,768,768]{2,1,0:T(8,128)(2,1)S(1)} %collective-permute-done.85.refs_0_), channel_id=1, source_target_pairs={{0,8},{8,16},{16,24},{24,28},{28,20},{20,12},{12,4},{4,0},{9,1},{1... | collective-permute-start | bytes 3538952 | tf_op jit(solution)/shard_map/ppermute | solution.py:615
  708.4 50.6 %collective-permute-start.95 = (bf16[1,768,768]{2,1,0:T(8,128)(2,1)S(1)}, bf16[1,768,768]{2,1,0:T(8,128)(2,1)}, u32[]{:S(2)}, u32[]{:S(2)}) collective-permute-start(bf16[1,768,768]{2,1,0:T(8,128)(2,1)S(1)} %collective-permute-done.86.refs_1_), channel_id=1, source_target_pairs={{8,0},{16,8},{24,16},{28,24},{20,28},{12,20},{4,12},{0,4},{1,9},{9... | collective-permute-start | bytes 3538952 | tf_op jit(solution)/shard_map/ppermute | solution.py:615
  716.9 32.1 %collective-permute-start.91 = (bf16[2,96,896]{2,1,0:T(8,128)(2,1)}, bf16[2,96,896]{2,1,0:T(8,128)(2,1)S(1)}, u32[]{:S(2)}, u32[]{:S(2)}) collective-permute-start(bf16[2,96,896]{2,1,0:T(8,128)(2,1)} %collective-permute-done.90), channel_id=1, source_target_pairs={{0,8},{8,16},{16,24},{24,28},{28,20},{20,12},{12,4},{4,0},{9,1},{1... | collective-permute-start | bytes 1032200 | tf_op jit(solution)/shard_map/ppermute | solution.py:615
  717.6 31.5 %collective-permute-start.93 = (bf16[2,96,896]{2,1,0:T(8,128)(2,1)}, bf16[2,96,896]{2,1,0:T(8,128)(2,1)S(1)}, u32[]{:S(2)}, u32[]{:S(2)}) collective-permute-start(bf16[2,96,896]{2,1,0:T(8,128)(2,1)} %collective-permute-done.92), channel_id=1, source_target_pairs={{8,0},{16,8},{24,16},{28,24},{20,28},{12,20},{4,12},{0,4},{1,9},{9... | collective-permute-start | bytes 1032200 | tf_op jit(solution)/shard_map/ppermute | solution.py:615
  (139 other events, 1347.2 us)

commit v3 on v2

v3 whole, which is shorter than its diff:
```python
import functools

import jax
import jax.numpy as jnp
from jax import lax
from jax.experimental import pallas as pl
from jax.experimental.pallas import tpu as pltpu
from jax.sharding import PartitionSpec as P

D = 1536
HQ = 12
HK = 4
DH = 128
GROUP_HEADS = HQ // HK
LANES = 128

EPSILON = 1e-05
F32 = jnp.float32
BF16 = jnp.bfloat16
MIB = 1024 * 1024
SMALL = pl.CostEstimate(flops=0, bytes_accessed=0, transcendentals=0)


def params(mib, *semantics):
    return pltpu.CompilerParams(
        dimension_semantics=semantics or None, vmem_limit_bytes=mib * MIB
    )


def dot(left, right):
    return jnp.dot(left, right, preferred_element_type=F32)


def dot_nt(left, right):
    return lax.dot_general(left, right, (((1,), (1,)), ((), ())), preferred_element_type=F32)


def dot_tn(left, right):
    return lax.dot_general(left, right, (((0,), (0,)), ((), ())), preferred_element_type=F32)


def after(values, *others):
    return lax.optimization_barrier((values, *others))[0]


def swap(values, axis):
    return lax.ppermute(values, axis, [(0, 1), (1, 0)])


def halves(values, axis, mine):
    size = values.shape[axis] // 2
    low = lax.slice_in_dim(values, 0, size, axis=axis)
    high = lax.slice_in_dim(values, size, 2 * size, axis=axis)
    return jnp.where(mine == 0, low, high), jnp.where(mine == 0, high, low)


def in_order(own, other, mine, axis):
    return jnp.concatenate(
        [jnp.where(mine == 0, own, other), jnp.where(mine == 0, other, own)], axis=axis
    )


def gather_rows(place_ref, own_ref, other_ref, all_ref):
    row = place_ref[0]
    rows = own_ref.shape[0]
    all_ref[pl.ds(pl.multiple_of(row * rows, rows), rows), :] = own_ref[...]
    all_ref[pl.ds(pl.multiple_of((1 - row) * rows, rows), rows), :] = other_ref[...]


def head_rows(ref, first, block):
    return jnp.concatenate(
        [ref[first : first + block, h * DH : (h + 1) * DH] for h in range(GROUP_HEADS)], axis=0
    )


def key_probs(query, key, first, length):
    block, keys = query.shape[0] // GROUP_HEADS, key.shape[0]
    scores = dot_nt(query, key) * DH ** (-0.5)
    shape = (block, keys)
    query_at = lax.broadcasted_iota(jnp.int32, shape, 0) + first
    key_at = lax.broadcasted_iota(jnp.int32, shape, 1)
    allowed = (key_at <= query_at) & (key_at < length)
    allowed = jnp.concatenate([allowed] * GROUP_HEADS, axis=0)
    scores = jnp.where(allowed, scores, -1e30)
    weights = jnp.exp(scores - jnp.max(scores, axis=1, keepdims=True))
    return weights * (1.0 / jnp.sum(weights, axis=1, keepdims=True))


def attend_kernel(place_ref, own_ref, other_ref, out_ref, all_ref):
    gather_rows(place_ref, own_ref, other_ref, all_ref)
    rows = own_ref.shape[0]
    block = 256
    width = GROUP_HEADS * DH
    for at in range(2 * rows // block):
        first, keys = at * block, (at + 1) * block
        query = head_rows(all_ref, first, block)
        key = all_ref[0:keys, width : width + DH]
        value = all_ref[0:keys, width + DH : width + 2 * DH]
        probs = key_probs(query, key, first, place_ref[1])
        result = dot(probs.astype(BF16), value).astype(BF16)
        for h in range(GROUP_HEADS):
            out_ref[first : first + block, h * DH : (h + 1) * DH] = result[
                h * block : (h + 1) * block
            ]


def attend(place, own, other):
    rows, width = own.shape
    spec = pl.BlockSpec(memory_space=pltpu.VMEM)
    return pl.pallas_call(
        attend_kernel,
        out_shape=jax.ShapeDtypeStruct((2 * rows, GROUP_HEADS * DH), BF16),
        in_specs=[pl.BlockSpec(memory_space=pltpu.SMEM), spec, spec],
        out_specs=spec,
        scratch_shapes=[pltpu.VMEM((2 * rows, width), BF16)],
        compiler_params=params(32),
        cost_estimate=SMALL,
        name="attend",
    )(place, own, other)


def attend_back_kernel(
    place_ref, own_ref, other_ref, grad_ref, grad_c_ref, out_ref, out_c_ref, result_ref, all_ref, total_ref
):
    gather_rows(place_ref, own_ref, other_ref, all_ref)
    rows = own_ref.shape[0]
    block = 256
    width = GROUP_HEADS * DH
    group = pl.ds(pl.multiple_of(place_ref[2] * width, width), width)
    blocks = 2 * rows // block
    for at in reversed(range(blocks)):
        first, keys = at * block, (at + 1) * block
        query = head_rows(all_ref, first, block)
        key = all_ref[0:keys, width : width + DH]
        value = all_ref[0:keys, width + DH : width + 2 * DH]
        probs = key_probs(query, key, first, place_ref[1])
        grad = dot_nt(grad_ref[first:keys, :], out_ref[group, :])
        grad = (grad + dot_nt(grad_c_ref[first:keys, :], out_c_ref[group, :])).astype(BF16)
        grad = jnp.concatenate(
            [grad[:, h * DH : (h + 1) * DH] for h in range(GROUP_HEADS)], axis=0
        )
        probs_grad = dot_nt(grad, value)
        carried = jnp.sum(probs * probs_grad, axis=1, keepdims=True)
        score_grad = (probs * (probs_grad - carried)).astype(BF16)
        query_back = (dot(score_grad, key) * DH ** (-0.5)).astype(BF16)
        for h in range(GROUP_HEADS):
            result_ref[first:keys, h * DH : (h + 1) * DH] = query_back[
                h * block : (h + 1) * block
            ]
        key_back = dot_tn(score_grad, query)
        value_back = dot_tn(probs.astype(BF16), grad)
        if at == blocks - 1:
            total_ref[:, 0:DH] = key_back
            total_ref[:, DH:] = value_back
        else:
            total_ref[0:keys, 0:DH] += key_back
            total_ref[0:keys, DH:] += value_back
    result_ref[:, width : width + DH] = (total_ref[:, 0:DH] * DH ** (-0.5)).astype(BF16)
    result_ref[:, width + DH :] = total_ref[:, DH:].astype(BF16)


def attend_back(place, own, other, grad, grad_c, w_out, out_c):
    rows, width = own.shape
    spec = pl.BlockSpec(memory_space=pltpu.VMEM)
    return pl.pallas_call(
        attend_back_kernel,
        out_shape=jax.ShapeDtypeStruct((2 * rows, width), BF16),
        in_specs=[pl.BlockSpec(memory_space=pltpu.SMEM)] + [spec] * 6,
        out_specs=spec,
        scratch_shapes=[
            pltpu.VMEM((2 * rows, width), BF16),
            pltpu.VMEM((2 * rows, 2 * DH), F32),
        ],
        compiler_params=params(48),
        cost_estimate=SMALL,
        name="attend_back",
    )(place, own, other, grad, grad_c, w_out, out_c)


def late_kernel(place_ref, *refs):
    near, near_c, far, far_c, qkv_ref, attended_ref, grad_ref, grad_c_ref = refs[0:8]
    shared = refs[8:10]
    outs = refs[10:12]
    rows, features = near.shape
    own_rows = pl.ds(pl.multiple_of(place_ref[0] * rows, rows), rows)
    far_rows = pl.ds(pl.multiple_of((1 - place_ref[0]) * rows, rows), rows)
    split = 7 * LANES

    def store(h, at, values):
        values = values.astype(BF16)
        for part in range(2):
            low, high = max(at, part * split), min(at + values.shape[1], (part + 1) * split)
            if low < high:
                piece = values[:, low - at : high - at]
                to = slice(low - part * split, high - part * split)

                @pl.when(place_ref[2] == 0)
                def _(part=part, to=to, piece=piece):
                    outs[part][h, :, to] = piece

                @pl.when(place_ref[2] != 0)
                def _(part=part, to=to, piece=piece):
                    outs[1 - part][h, :, to] = piece

    for h, (x, y, grad) in enumerate(((near, far, grad_ref), (near_c, far_c, grad_c_ref))):
        for k in range(2):
            store(h, 3 * LANES * k, shared[k][0, h * features : (h + 1) * features, :])
        project = dot_tn(x[...], qkv_ref[own_rows, :]) + dot_tn(y[...], qkv_ref[far_rows, :])
        store(h, 6 * LANES, project)
        store(h, 11 * LANES, dot_tn(grad[...], attended_ref[...]))


def late_grads(place, near, far, qkv_grad, attended, grad, grad_c, shared):
    features = near[0].shape[1]
    spec = pl.BlockSpec(memory_space=pltpu.VMEM)
    return pl.pallas_call(
        late_kernel,
        out_shape=[jax.ShapeDtypeStruct((2, features, 7 * LANES), BF16)] * 2,
        in_specs=[pl.BlockSpec(memory_space=pltpu.SMEM)] + [spec] * 10,
        out_specs=[spec] * 2,
        compiler_params=params(40),
        cost_estimate=SMALL,
        name="late_grads",
    )(place, *near, *far, qkv_grad, attended, grad, grad_c, *shared)


def columns_kernel(
    col_ref, query_ref, key_ref, value_ref, gain_ref, gain_ffn_ref, out_ref, gains_ref
):
    gains_ref[0:1, :] = gain_ref[...]
    gains_ref[1:2, :] = gain_ffn_ref[...]
    width = GROUP_HEADS * DH
    out_ref[:, 0:width] = query_ref[...]
    out_ref[:, width : width + DH] = key_ref[...]
    out_ref[:, width + DH :] = value_ref[...]


def their_columns(col, w_query, w_key, w_value, gain_attn, gain_ffn):
    rows = w_query.shape[0]
    width = GROUP_HEADS * DH + 2 * DH

    def theirs(width):
        return pl.BlockSpec((rows, width), lambda i, c: (0, 1 - c[0]))

    return pl.pallas_call(
        columns_kernel,
        grid_spec=pltpu.PrefetchScalarGridSpec(
            num_scalar_prefetch=1,
            grid=(1,),
            in_specs=[theirs(GROUP_HEADS * DH), theirs(DH), theirs(DH)]
            + [pl.BlockSpec(gain_attn.shape, lambda i, c: (0, 0))] * 2,
            out_specs=[
                pl.BlockSpec((rows, width), lambda i, c: (0, 0)),
                pl.BlockSpec((2, rows), lambda i, c: (0, 0)),
            ],
        ),
        out_shape=[
            jax.ShapeDtypeStruct((rows, width), BF16),
            jax.ShapeDtypeStruct((2, rows), F32),
        ],
        compiler_params=params(16, "arbitrary"),
        cost_estimate=SMALL,
        name="their_columns",
    )(col, w_query, w_key, w_value, gain_attn, gain_ffn)


def project_kernel(col_ref, own_ref, other_ref, gains_ref, gains_c_ref, query_ref, key_ref, value_ref, there_ref, x_own_ref, x_other_ref, qkv_ref, scale_ref):
    own = own_ref[...].astype(F32)
    other = other_ref[...].astype(F32)
    total = jnp.sum(own * own, axis=1, keepdims=True)
    total = total + jnp.sum(other * other, axis=1, keepdims=True)
    scale = lax.rsqrt(total / D + EPSILON)
    own = (own * scale * gains_ref[0:1, :]).astype(BF16)
    other = (other * scale * gains_c_ref[0:1, :]).astype(BF16)
    x_own_ref[...] = own
    x_other_ref[...] = other
    scale_ref[...] = scale
    here = jnp.concatenate([query_ref[...], key_ref[...], value_ref[...]], axis=1)
    qkv_ref[...] = (dot(own, here) + dot(other, there_ref[...])).astype(BF16)


def project(col, own, other, gains, gains_c, w_query, w_key, w_value, there):
    rows, features = own.shape
    width = there.shape[1]
    group = GROUP_HEADS * DH
    tile = rows // 2

    def whole(*shape):
        return pl.BlockSpec(shape, lambda i, c: (0,) * len(shape))

    def mine(width):
        return pl.BlockSpec((features, width), lambda i, c: (0, c[0]))

    def rowwise(width):
        return pl.BlockSpec((tile, width), lambda i, c: (i, 0))

    return pl.pallas_call(
        project_kernel,
        grid_spec=pltpu.PrefetchScalarGridSpec(
            num_scalar_prefetch=1,
            grid=(rows // tile,),
            in_specs=[
                rowwise(features),
                rowwise(features),
                whole(2, features),
                whole(2, features),
                mine(group),
                mine(DH),
                mine(DH),
                whole(features, width),
            ],
            out_specs=[rowwise(features), rowwise(features), rowwise(width), rowwise(1)],
        ),
        out_shape=[
            jax.ShapeDtypeStruct((rows, features), BF16),
            jax.ShapeDtypeStruct((rows, features), BF16),
            jax.ShapeDtypeStruct((rows, width), BF16),
            jax.ShapeDtypeStruct((rows, 1), F32),
        ],
        compiler_params=params(24, "arbitrary"),
        cost_estimate=SMALL,
        name="project",
    )(col, own, other, gains, gains_c, w_query, w_key, w_value, there)


def head_pair(col_ref, own, other):
    first, second = own[...], other[...]
    flipped = col_ref != 0
    return jnp.concatenate(
        [jnp.where(flipped, second, first), jnp.where(flipped, first, second)], axis=1
    )


def before_kernel(tiles, place_ref, *refs):
    near, near_c, far, far_c, attended, attended_c, here, there, own_ref, other_ref = refs
    is_near = (pl.program_id(0) >= tiles // 2).astype(jnp.int32) == place_ref[0]
    heads = head_pair(place_ref[2], attended, attended_c)
    own = jnp.where(is_near, near[...], far[...]).astype(F32)
    other = jnp.where(is_near, near_c[...], far_c[...]).astype(F32)
    own_ref[...] = own + dot(heads, here[...])
    other_ref[...] = other + dot(heads, there[...])


def after_kernel(place_ref, *refs):
    own_ref, other_ref, attended, attended_c, here, there, gains_ref, gains_c_ref = refs[0:8]
    hidden_ref, x_own_ref, x_other_ref, scale_ref = refs[8:12]
    heads = head_pair(place_ref[2], attended, attended_c)
    own = own_ref[...] + dot(heads, here[...])
    other = other_ref[...] + dot(heads, there[...])
    total = jnp.sum(own * own, axis=1, keepdims=True)
    total = total + jnp.sum(other * other, axis=1, keepdims=True)
    scale = lax.rsqrt(total / D + EPSILON)
    hidden_ref[...] = own
    scale_ref[...] = scale
    x_own_ref[...] = (own * scale * gains_ref[1:2, :]).astype(BF16)
    x_other_ref[...] = (other * scale * gains_c_ref[1:2, :]).astype(BF16)


TOKEN_TILE = 256


def rowwise(width):
    return pl.BlockSpec((TOKEN_TILE, width), lambda i, p: (i, 0))


def whole(*shape):
    return pl.BlockSpec(shape, lambda i, p: (0,) * len(shape))


def hidden_before(place, tokens, attended, here, there):
    half, features = tokens[0].shape
    rows, heads = attended[0].shape
    tiles = rows // TOKEN_TILE
    per_half = half // TOKEN_TILE
    halfwise = pl.BlockSpec((TOKEN_TILE, features), lambda i, p: (i % per_half, 0))
    return pl.pallas_call(
        functools.partial(before_kernel, tiles),
        grid_spec=pltpu.PrefetchScalarGridSpec(
            num_scalar_prefetch=1,
            grid=(tiles,),
            in_specs=[halfwise] * 4 + [rowwise(heads)] * 2 + [whole(2 * heads, features)] * 2,
            out_specs=[rowwise(features)] * 2,
        ),
        out_shape=[jax.ShapeDtypeStruct((rows, features), F32)] * 2,
        compiler_params=params(32, "arbitrary"),
        cost_estimate=pl.CostEstimate(
            flops=8 * rows * features * heads,
            bytes_accessed=16 * rows * features,
            transcendentals=0,
        ),
        name="hidden_before",
    )(place, *tokens, *attended, here, there)


def hidden_after(place, before, attended, here, there, gains, gains_c):
    rows, features = before[0].shape
    heads = attended[0].shape[1]
    return pl.pallas_call(
        after_kernel,
        grid_spec=pltpu.PrefetchScalarGridSpec(
            num_scalar_prefetch=1,
            grid=(rows // TOKEN_TILE,),
            in_specs=[rowwise(features)] * 2
            + [rowwise(heads)] * 2
            + [whole(2 * heads, features)] * 2
            + [whole(2, features)] * 2,
            out_specs=[rowwise(features)] * 3 + [rowwise(1)],
        ),
        out_shape=[
            jax.ShapeDtypeStruct((rows, features), F32),
            jax.ShapeDtypeStruct((rows, features), BF16),
            jax.ShapeDtypeStruct((rows, features), BF16),
            jax.ShapeDtypeStruct((rows, 1), F32),
        ],
        compiler_params=params(32, "arbitrary"),
        cost_estimate=SMALL,
        name="hidden_after",
    )(place, *before, *attended, here, there, gains, gains_c)


def expert_kernel(shared, aliased, first, order_ref, *refs):
    x_own, x_other, o_own, o_other, gates_ref = refs[0:5]
    weights = refs[5:17]
    grads = refs[17 + aliased : 19 + aliased]
    pair_ref, inner_ref = refs[19 + aliased : 21 + aliased]
    step = pl.program_id(0) + first
    rows, features = x_own.shape
    tile = 512
    up_own = jnp.concatenate([weights[k][0] for k in (0, 1, 6, 7)], axis=1)
    up_other = jnp.concatenate([weights[k][0] for k in (2, 3, 8, 9)], axis=1)
    down_own = jnp.concatenate([weights[k][0] for k in (4, 10)], axis=0)
    down_other = jnp.concatenate([weights[k][0] for k in (5, 11)], axis=0)

    def token_tile(t, carry):
        at = pl.ds(pl.multiple_of(t * tile, tile), tile)
        pre = dot(x_own[at, :], up_own) + dot(x_other[at, :], up_other)
        back = dot_nt(o_own[at, :], down_own) + dot_nt(o_other[at, :], down_other)
        for k in range(2):
            pre_gate = pre[:, 2 * k * LANES : (2 * k + 1) * LANES]
            pre_up = pre[:, (2 * k + 1) * LANES : (2 * k + 2) * LANES]
            inner_grad = back[:, k * LANES : (k + 1) * LANES]
            sigmoid = 1.0 / (1.0 + jnp.exp(-pre_gate))
            silu = pre_gate * sigmoid
            inner = silu * pre_up
            if not shared:
                shape = (gates_ref.shape[0], LANES)
                expert = lax.broadcasted_iota(jnp.int32, shape, 0) % (gates_ref.shape[0] // 3)
                chosen = (expert == order_ref[2 * step + k]).astype(F32).astype(BF16)
                gate = dot_tn(gates_ref[:, at], chosen)
                inner = gate * inner
                inner_grad = gate * inner_grad
            gate_grad = inner_grad * pre_up * (sigmoid * (1.0 + pre_gate * (1.0 - sigmoid)))
            inner_ref[0, at, k * LANES : (k + 1) * LANES] = inner.astype(BF16)
            pair_ref[0, at, 2 * k * LANES : (2 * k + 1) * LANES] = gate_grad.astype(BF16)
            pair_ref[0, at, (2 * k + 1) * LANES : (2 * k + 2) * LANES] = (
                inner_grad * silu
            ).astype(BF16)
        return carry

    lax.fori_loop(0, rows // tile, token_tile, 0)
    pairs = pair_ref[0]
    for h, x in enumerate((x_own, x_other)):
        wide = dot_tn(x[...], pairs).astype(BF16)
        for k in range(2):
            grads[k][0, h * features : (h + 1) * features, 0 : 2 * LANES] = wide[
                :, 2 * k * LANES : (2 * k + 2) * LANES
            ]
    inner = inner_ref[0]
    tile = 256
    for h, o in enumerate((o_own, o_other)):
        for j in range(features // tile):
            low = dot_tn(inner, o[:, j * tile : (j + 1) * tile]).astype(BF16)
            for k in range(2):
                for b in range(tile // LANES):
                    at = h * features + j * tile + b * LANES
                    grads[k][0, at : at + LANES, 2 * LANES :] = low[
                        k * LANES : (k + 1) * LANES, b * LANES : (b + 1) * LANES
                    ]


def expert_specs(features, place, wide, low):
    specs = []
    if wide:
        block = pl.BlockSpec((1, features, LANES), lambda i, o: (place(i, o)[0], 0, place(i, o)[1]))
        specs += [block] * 4
    if low:
        block = pl.BlockSpec((1, LANES, features), lambda i, o: (*place(i, o), 0))
        specs += [block] * 2
    return specs


def expert_grads(order, first, last, total, x, o, gates, weights, kept):
    shared = total is None
    steps = last - first
    rows, features = x[0].shape
    aliased = len(kept)

    def fixed(*shape):
        return pl.BlockSpec(shape, lambda i, o: (0,) * len(shape))

    def stepped(*shape):
        return pl.BlockSpec((1, *shape), lambda i, o: (i, 0, 0))

    def placed(*shape):
        return pl.BlockSpec((1, *shape), lambda i, o: (i + first, 0, 0))

    specs = []
    for k in range(2):
        if shared:

            def picked(i, o, k=k):
                return 0, 2 * o[o.shape[0] - 1] + k

        else:

            def picked(i, o, k=k):
                return o[2 * (i + first) + k], o[o.shape[0] - 1]

        specs += expert_specs(features, picked, True, True)
    total = steps if shared else total
    return pl.pallas_call(
        functools.partial(expert_kernel, shared, aliased, first),
        grid_spec=pltpu.PrefetchScalarGridSpec(
            num_scalar_prefetch=1,
            grid=(steps,),
            in_specs=[fixed(rows, features)] * 4
            + [fixed(*gates.shape)]
            + specs
            + [pl.BlockSpec(memory_space=pl.ANY)] * aliased,
            out_specs=[stepped(2 * features, 3 * LANES)] * 2
            + [placed(rows, 4 * LANES), placed(rows, 2 * LANES)],
        ),
        out_shape=[jax.ShapeDtypeStruct((steps, 2 * features, 3 * LANES), BF16)] * 2
        + [
            jax.ShapeDtypeStruct((total, rows, 4 * LANES), BF16),
            jax.ShapeDtypeStruct((total, rows, 2 * LANES), BF16),
        ],
        input_output_aliases={18 + k: 2 + k for k in range(aliased)},
        compiler_params=params(40, "arbitrary"),
        cost_estimate=SMALL,
        name="expert_grads",
    )(order, *x, *o, gates, *weights, *weights, *kept)


def mix_kernel(back, group, order_ref, *refs):
    acts_ref, shared_ref = refs[0:2]
    each = 2 if back else 1
    count = 2 * group * each
    weights = refs[2 : 2 + count]
    shared = refs[2 + count : 2 + count + 2 * each]
    out_ref, total_ref = refs[2 + count + 2 * each :]
    step = pl.program_id(0)
    rows = out_ref.shape[0]
    tile = 512
    times = dot_nt if back else dot
    along = 1 if back else 0

    @pl.when(step == 0)
    def _():
        both = jnp.concatenate([w[0] for w in shared], axis=along)
        for t in range(rows // tile):
            at = slice(t * tile, (t + 1) * tile)
            total_ref[at, :] = times(shared_ref[0, at, :], both)

    both = jnp.concatenate([w[0] for w in weights], axis=along)
    for t in range(rows // tile):
        at = slice(t * tile, (t + 1) * tile)
        acts = jnp.concatenate([acts_ref[g, at, :] for g in range(group)], axis=1)
        total_ref[at, :] += times(acts, both)

    @pl.when(step == pl.num_programs(0) - 1)
    def _():
        out_ref[...] = total_ref[...].astype(out_ref.dtype)


def mix(back, dtype, order, acts, shared_acts, weights, shared_weights):
    pairs, rows, width = acts.shape
    features = weights[0].shape[1] if back else weights[0].shape[2]
    group = 4 if pairs % 4 == 0 else 1

    def spec(place):
        if back:
            return pl.BlockSpec((1, features, LANES), lambda i, o: (place(i, o)[0], 0, place(i, o)[1]))
        return pl.BlockSpec((1, LANES, features), lambda i, o: (*place(i, o), 0))

    def routed(k):
        return spec(lambda i, o: (o[2 * group * i + k], o[o.shape[0] - 1]))

    def common(k):
        return spec(lambda i, o: (0, 2 * o[o.shape[0] - 1] + k))

    return pl.pallas_call(
        functools.partial(mix_kernel, back, group),
        grid_spec=pltpu.PrefetchScalarGridSpec(
            num_scalar_prefetch=1,
            grid=(pairs // group,),
            in_specs=[
                pl.BlockSpec((group, rows, width), lambda i, o: (i, 0, 0)),
                pl.BlockSpec((1, rows, width), lambda i, o: (0, 0, 0)),
            ]
            + [routed(k) for k in range(2 * group) for _ in weights]
            + [common(k) for k in range(2) for _ in weights],
            out_specs=pl.BlockSpec((rows, features), lambda i, o: (0, 0)),
            scratch_shapes=[pltpu.VMEM((rows, features), F32)],
        ),
        out_shape=jax.ShapeDtypeStruct((rows, features), dtype),
        compiler_params=params(48, "arbitrary"),
        cost_estimate=SMALL,
        name="mix",
    )(order, acts, shared_acts, *weights * (2 * group), *shared_weights * 2)


def ring_of(size):
    return list(range(0, size, 2)) + list(range(1, size, 2))[::-1]


def unpack_kernel(aliased, index_ref, *refs):
    chunks = refs[0:2]
    gate_ref, up_ref, down_ref = refs[2 + aliased : 5 + aliased]
    blocks = chunks[0].shape[1] // LANES

    def write(chunk_ref):
        gate_ref[0] = chunk_ref[0, :, 0:LANES].astype(F32)
        up_ref[0] = chunk_ref[0, :, LANES : 2 * LANES].astype(F32)
        for b in range(blocks):
            at = slice(b * LANES, (b + 1) * LANES)
            down_ref[0, :, at] = chunk_ref[0, at, 2 * LANES :].astype(F32)

    for k in range(2):
        pl.when(pl.program_id(1) == k)(lambda k=k: write(chunks[k]))


def unpack(index, chunks, shapes, outs):
    count, rows, width = chunks[0].shape
    chunk = pl.BlockSpec((1, rows, width), lambda i, d, n: (i, 0, 0))

    def wide(i, d, n):
        return (n[2 * i + d], 0, n[2 * count])

    def low(i, d, n):
        return (n[2 * i + d], n[2 * count], 0)

    aliased = len(outs)
    return pl.pallas_call(
        functools.partial(unpack_kernel, aliased),
        grid_spec=pltpu.PrefetchScalarGridSpec(
            num_scalar_prefetch=1,
            grid=(count, 2),
            in_specs=[chunk, chunk] + [pl.BlockSpec(memory_space=pl.ANY)] * aliased,
            out_specs=[
                pl.BlockSpec((1, rows, LANES), wide),
                pl.BlockSpec((1, rows, LANES), wide),
                pl.BlockSpec((1, LANES, rows), low),
            ],
        ),
        out_shape=[jax.ShapeDtypeStruct(shape, F32) for shape in shapes],
        input_output_aliases={3 + k: k for k in range(aliased)},
        compiler_params=params(16, "arbitrary", "arbitrary"),
        cost_estimate=SMALL,
        name="unpack",
    )(index, *chunks, *outs)


def unpack_late_kernel(col_ref, first_ref, second_ref, *outs):
    sgate, sup, sdown, query, key, value, out = outs
    features = first_ref.shape[1]
    flipped = col_ref[0] != 0
    for c in range(2):
        for b in range(14):
            lanes = slice(b % 7 * LANES, (b % 7 + 1) * LANES)
            first, second = first_ref[c, :, lanes], second_ref[c, :, lanes]
            if b >= 7:
                first, second = second, first
            block = jnp.where(flipped, second, first).astype(F32)
            if b < 6:
                at = slice((2 * c + b // 3) * LANES, (2 * c + b // 3 + 1) * LANES)
                if b % 3 < 2:
                    (sgate, sup)[b % 3][:, at] = block
                else:
                    for k in range(features // LANES):
                        here = slice(k * LANES, (k + 1) * LANES)
                        sdown[at, here] = block[here, :]
            elif b < 9:
                at = (GROUP_HEADS * c + b - 6) * LANES
                query[:, at : at + LANES] = block
            elif b < 11:
                (key, value)[b - 9][:, c * LANES : (c + 1) * LANES] = block
            else:
                at = (GROUP_HEADS * c + b - 11) * LANES
                out[at : at + LANES, :] = block.T


def unpack_late(col, first, second, shapes):
    spec = pl.BlockSpec(memory_space=pltpu.VMEM)
    return pl.pallas_call(
        unpack_late_kernel,
        in_specs=[pl.BlockSpec(memory_space=pltpu.SMEM), spec, spec],
        out_specs=[spec] * len(shapes),
        out_shape=[jax.ShapeDtypeStruct(shape, F32) for shape in shapes],
        compiler_params=params(48),
        name="unpack_late",
    )(col, first, second)


LATE_ROUND = 3


def add_rounded(left, right):
    return (left.astype(F32) + right.astype(F32)).astype(BF16)


def body(
    tokens_in,
    norm_gain_attn,
    w_query,
    w_key,
    w_value,
    w_out,
    norm_gain_ffn,
    w_gate,
    w_up,
    w_down,
    w_shared_gate,
    w_shared_up,
    w_shared_down,
    routes,
    gate_weights,
    seq_lengths,
    out_grad,
):
    row = lax.axis_index("row")
    col = lax.axis_index("col")
    dp = lax.axis_index("dp")
    dp_size = lax.axis_size("dp")
    local_rows, local_features = tokens_in.shape
    experts = w_gate.shape[0]
    group_width = GROUP_HEADS * DH
    col_ref = col.reshape(1)

    ring_size = min(8, dp_size)
    ring = ring_of(ring_size)
    starts = range(0, dp_size, ring_size)
    rights = [
        (g + ring[k], g + ring[(k + 1) % ring_size]) for g in starts for k in range(ring_size)
    ]
    lefts = [(b, a) for a, b in rights]
    routes_of = [
        [(2 * a, 2 * b) for a, b in ways[0]] + [(2 * a + 1, 2 * b + 1) for a, b in ways[1]]
        for ways in ((rights, lefts), (lefts, rights))
    ]
    place_of = [ring.index(k) for k in range(ring_size)]
    place = jnp.asarray(place_of, jnp.int32)[dp % ring_size]
    signs = [1 - 2 * col, 2 * col - 1]

    def send(values, which):
        if ring_size == 1:
            return values
        return lax.ppermute(values, ("dp", "col"), routes_of[which])

    def chunk_at(step, which):
        return (place - signs[which] * step) % ring_size

    def across_rings(values):
        if len(starts) == 1:
            return values
        peers = [[g + k for g in starts] for k in range(ring_size)]
        return lax.psum(values, "dp", axis_index_groups=peers)

    where = jnp.stack([row, seq_lengths[0], col])
    tokens_y = swap(tokens_in, "row")
    tokens_c = swap(tokens_in, "col")
    there, gains = their_columns(
        col_ref, w_query, w_key, w_value, norm_gain_attn[None], norm_gain_ffn[None]
    )
    there = swap(there, "col")
    gains_c = swap(gains, "col")

    def project_half(own, other):
        return project(col_ref, own, other, gains, gains_c, w_query, w_key, w_value, there)

    near = project_half(tokens_in, tokens_c)
    gate_c = swap(w_gate, "col")
    count = min(ring_size, 4)
    share = w_out.shape[0] // count
    member = dp % count
    out_y = lax.dynamic_slice_in_dim(w_out, member * share, share, axis=0)
    out_y = swap(out_y, "row")
    tokens_y = after(tokens_y, near[2], out_y)
    tokens_yc = swap(tokens_y, "col")
    grad_y = swap(after(out_grad, tokens_y), "row")
    far = project_half(tokens_y, tokens_yc)

    def double(part, bit, *others):
        if bit >= count:
            return part
        pairs = [(m, m ^ bit) for m in range(dp_size)]
        came = after(lax.ppermute(part, "dp", pairs), *others)
        return in_order(part, came, member // bit % 2, 0)

    out_y = double(out_y, 1)
    where = after(where, out_y)

    w_sgate, w_sup, w_sdown = w_shared_gate[None], w_shared_up[None], w_shared_down[None]
    up_c = swap(after(w_up, gate_c, tokens_yc), "col")

    attended = attend(where, near[2], far[2])
    attended_y = swap(attended, "row")
    attended_c = swap(attended, "col")
    out_c = swap(after(w_out, tokens_yc), "col")
    before = hidden_before(
        where,
        [tokens_in, tokens_c, tokens_y, tokens_yc],
        [attended, attended_c],
        w_out,
        out_c,
    )
    down_c = swap(after(w_down, up_c, attended_c, out_c, grad_y), "col")
    grad_own = in_order(out_grad, grad_y, row, 0)
    grad_other = swap(grad_own, "col")
    attended_y = after(attended_y, grad_own, before[0])
    out_y = double(out_y, 2, attended_y)
    out_yc = swap(out_y, "col")
    attended_yc = swap(attended_y, "col")
    hidden, x_own, x_other, scale_ffn = hidden_after(
        where, before, [attended_y, attended_yc], out_y, out_yc, gains, gains_c
    )
    sgate_c, sup_c, sdown_c = (
        swap(after(w, attended_yc), "col") for w in (w_sgate, w_sup, w_sdown)
    )

    choices = jnp.arange(experts, dtype=jnp.int32)[:, None]
    dense = sum(
        jnp.where(routes[:, k][None, :] == choices, gate_weights[:, k][None, :], 0.0)
        for k in range(routes.shape[1])
    )
    gates = []
    for _ in range(3):
        gates.append(lax.reduce_precision(dense, 8, 7))
        dense = dense - gates[-1]
    gates = jnp.concatenate(gates, axis=0).astype(BF16)

    each = experts // (2 * ring_size)
    orders = []
    for s in range(ring_size):
        for k in range(each):
            for which in range(2):
                second = col if which == 0 else 1 - col
                orders.append(2 * each * chunk_at(s, which) + each * second + k)
    order = jnp.stack(orders + [col]).astype(jnp.int32)
    pairs_total = experts // 2
    routed = [w_gate, w_up, gate_c, up_c, w_down, down_c]
    shared = [w_sgate, w_sup, sgate_c, sup_c, w_sdown, sdown_c]

    def run(first, last, order, kept):
        return expert_grads(
            order,
            first,
            last,
            pairs_total,
            [x_own, x_other],
            [grad_own, grad_other],
            gates,
            routed,
            kept,
        )

    first = run(0, each, order, ())
    kept = first[2:]
    sums = [first[0], first[1]]
    runs = {}
    mixed = {}

    def work_experts(first, last):
        def work(order):
            nonlocal kept
            result = run(first, last, order, tuple(kept))
            kept = result[2:]
            for at in range(first, last):
                runs[at] = (result[0], result[1], at - first)
            return kept[0]

        return work

    def work_shared(order):
        runs["shared"] = expert_grads(
            order, 0, 1, None, [x_own, x_other], [grad_own, grad_other], gates, shared, ()
        )
        return runs["shared"][2]

    def work_mix(back, half):
        def work(order):
            pick = slice(2 * half, 2 * half + 2) if back else slice(4 + half, 5 + half)
            mixed[back, half] = mix(
                back,
                BF16 if half else F32,
                order,
                kept[0 if back else 1],
                runs["shared"][2 if back else 3],
                routed[pick],
                shared[pick],
            )
            return mixed[back, half]

        return work

    bounds = list(range(each, pairs_total, 2 * each)) + [pairs_total]
    tasks = [[work_experts(a, b)] for a, b in zip(bounds[:-1], bounds[1:], strict=True)]
    if not tasks:
        tasks.append([])
    tasks[-1].append(work_shared)
    tasks += [[work_mix(True, 1)], [work_mix(True, 0)], [work_mix(False, 1)], [work_mix(False, 0)]]
    for s in range(1, ring_size):
        got = [send(sums[k], k) for k in range(2)]
        last = sums
        if s <= len(tasks):
            for task in tasks[s - 1]:
                last = [task(after(order, *last))]
        for k in range(2):
            got[k] = after(got[k], *last)
            parts = [runs[at] for at in range(each * s, each * s + each)]
            mine = [p[k][p[2] : p[2] + 1] for p in parts]
            mine = mine[0] if each == 1 else jnp.concatenate(mine, axis=0)
            sums[k] = add_rounded(got[k], mine)
            last = [sums[k]]
    for task in [task for step in tasks[ring_size - 1 :] for task in step]:
        task(after(order, *sums))
    sums = [across_rings(total) for total in sums]
    waves = [[total[:, :local_features] for total in sums]]
    crossed = [swap(total[:, local_features:], "col") for total in sums]
    waves.append([crossed[1], crossed[0]])

    start = row * local_rows

    def my_rows(values):
        return lax.dynamic_slice_in_dim(values, start, local_rows, axis=0)

    def their_rows(values):
        return lax.dynamic_slice_in_dim(values, local_rows - start, local_rows, axis=0)

    normed_grad = mixed[True, 0] + swap(mixed[True, 1], "col").astype(F32)
    normed_grad = normed_grad + swap(normed_grad.astype(BF16), "row").astype(F32)
    ffn_sum = mixed[False, 0] + swap(mixed[False, 1], "col").astype(F32)
    ffn_rows = my_rows(ffn_sum) + swap(their_rows(ffn_sum).astype(BF16), "row").astype(F32)
    block_out = (my_rows(hidden) + ffn_rows).astype(BF16)

    gain_ffn_part = jnp.sum(my_rows(normed_grad * hidden * scale_ffn), axis=0)
    scaled = normed_grad * norm_gain_ffn
    products = jnp.sum(scaled * hidden, axis=1, keepdims=True)
    mean = (products + swap(products, "col")) / D
    hidden_grad = grad_own.astype(F32) + scale_ffn * scaled - hidden * scale_ffn**3 * mean
    attn_grad = hidden_grad.astype(BF16)
    attn_grad_c = swap(attn_grad, "col")

    qkv_grad = attend_back(where, near[2], far[2], attn_grad, attn_grad_c, w_out, out_c)
    packs = late_grads(
        where,
        near[0:2],
        far[0:2],
        qkv_grad,
        attended,
        attn_grad,
        attn_grad_c,
        runs["shared"][0:2],
    )
    here = jnp.concatenate(
        [halves(w, 1, col)[0] for w in (w_query, w_key, w_value)], axis=1
    )

    packs = [
        pack.reshape(2, ring_size, local_features // ring_size, pack.shape[2]) for pack in packs
    ]

    def late_chunk(step, which):
        at = chunk_at(step, which)
        return lax.dynamic_index_in_dim(packs[which], at, axis=1, keepdims=False)

    def late_place(current, step, which):
        at = chunk_at(ring_size - 1 + step, which)
        return lax.dynamic_update_index_in_dim(late_out[which], current, at, 1)

    late_out = [jnp.zeros(pack.shape, BF16) for pack in packs]
    late = [late_chunk(0, k) for k in range(2)]
    late_done = 0
    late_total = 2 * (ring_size - 1)

    def late_turn():
        totals = [across_rings(values) for values in late]
        others = [swap(values[1], "col") for values in totals]
        for k in range(2):
            late[k] = in_order(totals[k][0:1], others[1 - k][None], col, 0)
            late_out[k] = late_place(late[k], 0, k)

    def late_finish(got, last):
        nonlocal late_done
        late_done += 1
        for k in range(2):
            values = after(got[k], *last)
            if late_done < ring_size:
                late[k] = add_rounded(values, late_chunk(late_done, k))
            else:
                late[k] = values
                late_out[k] = late_place(values, late_done - ring_size + 1, k)
            last = [late[k]]
        if late_done == ring_size - 1:
            late_turn()

    shapes = [w_gate.shape, w_up.shape, w_down.shape]
    placed = ()

    def place_chunks(wave, step, chunks, placed):
        index = []
        for k in range(each):
            for which in range(2):
                second = col if which == 0 else 1 - col
                at = chunk_at(ring_size - 1 + step, which)
                index.append(2 * each * at + each * second + k)
        index.append(col if wave == 0 else 1 - col)
        return unpack(jnp.stack(index).astype(jnp.int32), chunks, shapes, placed)

    if late_total == 0:
        late_turn()
    rounds = [(wave, step) for wave in range(2) for step in range(ring_size - 1)]
    for number, (wave, step) in enumerate(rounds):
        if step == 0:
            chunks = waves[wave]
        got = [send(chunks[k], k) for k in range(2)]
        steps = 0 if number < LATE_ROUND else 1
        if number >= len(rounds) - LATE_ROUND:
            steps = 2
        steps = min(steps, late_total - late_done)
        if number == LATE_ROUND:
            late = [after(values, *chunks) for values in late]
        late_got = [send(late[k], k) for k in range(2)] if steps else None
        placed = place_chunks(wave, step, chunks, placed)
        for k in range(2):
            got[k] = after(got[k], placed[0])
        for at in range(steps):
            if at:
                late_got = [send(late[k], k) for k in range(2)]
            late_finish(late_got, got)
        chunks = got
        if step == ring_size - 2:
            placed = place_chunks(wave, step + 1, chunks, placed)
    if not rounds:
        for wave in range(2):
            placed = place_chunks(wave, 0, waves[wave], placed)
    while late_done < late_total:
        late_finish([send(late[k], k) for k in range(2)], placed[0:1])
    gate_grad, up_grad, down_grad = placed
    shapes = [w.shape for w in (w_shared_gate, w_shared_up, w_shared_down)]
    shapes += [w.shape for w in (w_query, w_key, w_value, w_out)]
    finals = unpack_late(
        col_ref, *[out.reshape(2, local_features, out.shape[3]) for out in late_out], shapes
    )
    shared_gate_grad, shared_up_grad, shared_down_grad = finals[0:3]
    query_grad, key_grad, value_grad, out_proj_grad = finals[3:7]

    tokens_back = dot_nt(qkv_grad, here) + swap(
        dot_nt(qkv_grad, there).astype(BF16), "col"
    ).astype(F32)
    tokens_back = my_rows(tokens_back) + swap(
        their_rows(tokens_back).astype(BF16), "row"
    ).astype(F32)
    scale_attn = near[3]
    tokens_f32 = tokens_in.astype(F32)
    gain_attn_part = jnp.sum(tokens_back * tokens_f32 * scale_attn, axis=0)
    scaled = tokens_back * norm_gain_attn
    products = jnp.sum(scaled * tokens_f32, axis=1, keepdims=True)
    mean = (products + swap(products, "col")) / D
    tokens_grad = (
        my_rows(hidden_grad) + scale_attn * scaled - tokens_f32 * scale_attn**3 * mean
    ).astype(BF16)

    gain_parts = jnp.stack([gain_attn_part, gain_ffn_part])
    bit = 1
    while bit < ring_size:
        pairs = [(g + k, g + (k ^ bit)) for g in starts for k in range(ring_size)]
        gain_parts = gain_parts + lax.ppermute(gain_parts, "dp", pairs)
        bit *= 2
    gain_parts = across_rings(gain_parts + swap(gain_parts, "row"))

    return (
        block_out,
        tokens_grad,
        gain_parts[0],
        query_grad,
        key_grad,
        value_grad,
        out_proj_grad,
        gain_parts[1],
        gate_grad,
        up_grad,
        down_grad,
        shared_gate_grad,
        shared_up_grad,
        shared_down_grad,
    )


def solution(mesh):
    in_specs = (
        P(("dp", "row"), "col"),
        P("col"),
        P("col", "row"),
        P("col", "row"),
        P("col", "row"),
        P("row", "col"),
        P("col"),
        P(None, "col", "row"),
        P(None, "col", "row"),
        P(None, "row", "col"),
        P("col", "row"),
        P("col", "row"),
        P("row", "col"),
        P("dp", None),
        P("dp", None),
        P("dp"),
        P(("dp", "row"), "col"),
    )
    out_specs = (
        P(("dp", "row"), "col"),
        P(("dp", "row"), "col"),
        P("col"),
        P("col", "row"),
        P("col", "row"),
        P("col", "row"),
        P("row", "col"),
        P("col"),
        P(None, "col", "row"),
        P(None, "col", "row"),
        P(None, "row", "col"),
        P("col", "row"),
        P("col", "row"),
        P("row", "col"),
    )
    return jax.shard_map(body, mesh=mesh, in_specs=in_specs, out_specs=out_specs, check_vma=False)
```

time: 775 us -> 706 us (0.911)
  matrix products: 47.8 us -> 5.45 us
  other arithmetic: 76.6 us -> 43.7 us
  starting transfers between devices: 84 us -> 101 us
  waiting for transfers between devices: 289 us -> 280 us
    dot_general x8 -> x0, matrix products: 25.1 us -> none  [the longest x4 8.98 us: dot_tn(): lax.dot_general(left, right, (((0,), (0,)), ((), ())), preferred_element_...]
    pallas_call x1 -> x5, Pallas kernels: 13.3 us -> 34.7 us  [the longest x1 11.3 us: attend_back(): pl.pallas_call(attend_back_kernel, out_shape=jax.ShapeDtypeStruct((2 * ro...]
    pallas_call x6, Pallas kernels: 91 us -> 72.5 us  [expert_grads(): pl.pallas_call(functools.partial(expert_kernel, shared, aliased, first),...]
    convert_element_type x28, other arithmetic: 35.4 us -> 19.3 us  [add_rounded(): return (left.astype(F32) + right.astype(F32)).astype(BF16)]
    ppermute x34 -> x33, waiting for transfers between devices: 50.3 us -> 36.4 us  [swap(): return lax.ppermute(values, axis, [(0, 1), (1, 0)])]
    ppermute x56 -> x70, starting transfers between devices: 61.6 us -> 74.6 us  [send(): return lax.ppermute(values, ('dp', 'col'), routes_of[which])]
    unnamed x217 -> x230, local copies, waits for them, and re-layouts: 18.1 us -> 31.2 us
    sub x1 -> x0, matrix products: 10.6 us -> none  [attend_back(): weights = jnp.exp(scores - jnp.max(scores, axis=-1, keepdims=True))]
  transfers between devices with their start and end apart: 96 -> 108, of which waited for: 36 -> 51; matrix products, arithmetic and copies ran while one was open for 19% -> 8% of each run, Pallas kernels for 25% -> 27%
where the time goes in v3:
time: 706 us; the launch traced here: 695 us
  waiting for transfers between devices  280 us (40%)
  Pallas kernels  204 us (29%)
  starting transfers between devices  101 us (14%)
  other arithmetic  43.7 us (6%)
  local copies, waits for them, and re-layouts  38.4 us (5%)
  between operations  22.9 us (3%)
    ppermute x70, waiting for transfers between devices, send(): return lax.ppermute(values, ('dp', 'col'), routes_of[which])  236 us
    ppermute x70, starting transfers between devices, send(): return lax.ppermute(values, ('dp', 'col'), routes_of[which])  74.6 us
    pallas_call x6, Pallas kernels, expert_grads(): pl.pallas_call(functools.partial(expert_kernel, shared, aliased, first),...  72.5 us
    pallas_call x4, Pallas kernels, mix(): pl.pallas_call(functools.partial(mix_kernel, back, group), grid_spec=pltp...  40.5 us
    pallas_call x16, Pallas kernels, unpack(): pl.pallas_call(functools.partial(unpack_kernel, aliased), grid_spec=pltpu...  39.1 us
    ppermute x33, waiting for transfers between devices, swap(): return lax.ppermute(values, axis, [(0, 1), (1, 0)])  36.4 us
    unnamed x230, local copies, waits for them, and re-layouts  31.2 us
    ppermute x33, starting transfers between devices, swap(): return lax.ppermute(values, axis, [(0, 1), (1, 0)])  19.7 us
  transfers between devices with their start and end apart: 108, of which 51 were waited for; matrix products, arithmetic and copies ran while one was open for 8% of the time, Pallas kernels for 27%

profile of v3, /device:TPU:0, one launch (start us, length us, event | category | flops | bytes accessed | tf_op | source)
XLA Modules:
  0.0 695.1 jit_solution(1203308845523858909)
XLA Ops:
  7.5 2.5 collective-permute-start.3
  14.9 3.2 project.2
  21.5 13.4 %collective-permute-done = bf16[192,768]{1,0:T(8,128)(2,1)} collective-permute-done((bf16[192,768]{1,0:T(8,128)(2,1)S(1)}, bf16[192,768]{1,0:T(8,128)(2,1)}, u32[]{:S(2)}, u32[]{:S(2)}) %collective-permute-start) | collective-permute-done | bytes 294944 | tf_op jit(solution)/shard_map/ppermute | solution.py:47
  34.9 2.5 collective-permute-done.6.other_ref.refs_3_
  42.9 5.1 collective-permute-done.1
  51.8 3.0 project.3
  56.7 6.2 attend.1.refs_4_.refs_5_
  63.0 6.1 collective-permute-done.10
  78.1 5.9 hidden_before.1
  85.7 5.4 collective-permute-done.9.refs_2_
  109.7 6.2 hidden_after.1
  118.4 9.0 %expert_grads.6 = (bf16[1,1536,384]{2,1,0:T(8,128)(2,1)S(1)}, bf16[1,1536,384]{2,1,0:T(8,128)(2,1)S(1)}, bf16[8,1024,512]{2,1,0:T(8,128)(2,1)}, bf16[8,1024,256]{2,1,0:T(8,128)(2,1)S(1)}) custom-call(s32[17]{0:T(128)S(1)} %stack.215.order_ref, bf16[1024,768]{1,0:T(8,128)(2,1)S(1)} %get-tuple-element.215.refs_0_, ...), custom_call_target="tpu_custom_call" | custom-call | tf_op jit(solution)/shard_map/expert_grads/pallas_call | solution.py:521
  131.5 15.1 %expert_grads.7 = (bf16[2,1536,384]{2,1,0:T(8,128)(2,1)S(1)}, bf16[2,1536,384]{2,1,0:T(8,128)(2,1)S(1)}, bf16[8,1024,512]{2,1,0:T(8,128)(2,1)}, bf16[8,1024,256]{2,1,0:T(8,128)(2,1)}) custom-call(s32[17]{0:T(128)S(1)} %stack.215.order_ref, bf16[1024,768]{1,0:T(8,128)(2,1)S(1)} %get-tuple-element.215.refs_0_, ...), custom_call_target="tpu_custom_call", output_to_operand_aliasing={{2}: (18, {}), {3}: (19, {})} | custom-call | tf_op jit(solution)/shard_map/expert_grads/pallas_call | solution.py:521
  146.6 10.9 %collective-permute-done.18 = bf16[1,1536,384]{2,1,0:T(8,128)(2,1)S(1)} collective-permute-done((bf16[1,1536,384]{2,1,0:T(8,128)(2,1)S(1)}, bf16[1,1536,384]{2,1,0:T(8,128)(2,1)S(1)}, u32[]{:S(2)}, u32[]{:S(2)}) %collective-permute-start.18) | collective-permute-done | bytes 1179680 | tf_op jit(solution)/shard_map/ppermute | solution.py:758
  160.2 15.2 %expert_grads.8 = (bf16[2,1536,384]{2,1,0:T(8,128)(2,1)S(1)}, bf16[2,1536,384]{2,1,0:T(8,128)(2,1)S(1)}, bf16[8,1024,512]{2,1,0:T(8,128)(2,1)}, bf16[8,1024,256]{2,1,0:T(8,128)(2,1)}) custom-call(s32[17]{0:T(128)S(1)} %stack.215.order_ref, bf16[1024,768]{1,0:T(8,128)(2,1)S(1)} %get-tuple-element.215.refs_0_, ...), custom_call_target="tpu_custom_call", output_to_operand_aliasing={{2}: (18, {}), {3}: (19, {})} | custom-call | tf_op jit(solution)/shard_map/expert_grads/pallas_call | solution.py:521
  175.4 10.9 %collective-permute-done.19 = bf16[1,1536,384]{2,1,0:T(8,128)(2,1)S(1)} collective-permute-done((bf16[1,1536,384]{2,1,0:T(8,128)(2,1)S(1)}, bf16[1,1536,384]{2,1,0:T(8,128)(2,1)S(1)}, u32[]{:S(2)}, u32[]{:S(2)}) %collective-permute-start.19) | collective-permute-done | bytes 1179680 | tf_op jit(solution)/shard_map/ppermute | solution.py:758
  190.6 15.5 %expert_grads.9 = (bf16[2,1536,384]{2,1,0:T(8,128)(2,1)S(1)}, bf16[2,1536,384]{2,1,0:T(8,128)(2,1)S(1)}, bf16[8,1024,512]{2,1,0:T(8,128)(2,1)}, bf16[8,1024,256]{2,1,0:T(8,128)(2,1)}) custom-call(s32[17]{0:T(128)S(1)} %stack.215.order_ref, bf16[1024,768]{1,0:T(8,128)(2,1)S(1)} %get-tuple-element.215.refs_0_, ...), custom_call_target="tpu_custom_call", output_to_operand_aliasing={{2}: (18, {}), {3}: (19, {})} | custom-call | tf_op jit(solution)/shard_map/expert_grads/pallas_call | solution.py:521
  206.1 9.1 %collective-permute-done.21 = bf16[1,1536,384]{2,1,0:T(8,128)(2,1)S(1)} collective-permute-done((bf16[1,1536,384]{2,1,0:T(8,128)(2,1)S(1)}, bf16[1,1536,384]{2,1,0:T(8,128)(2,1)S(1)}, u32[]{:S(2)}, u32[]{:S(2)}) %collective-permute-start.21) | collective-permute-done | bytes 1179680 | tf_op jit(solution)/shard_map/ppermute | solution.py:758
  216.3 3.1 add_convert_fusion.9
  220.3 2.6 add_convert_fusion.8
  224.2 8.8 %expert_grads.10 = (bf16[1,1536,384]{2,1,0:T(8,128)(2,1)S(1)}, bf16[1,1536,384]{2,1,0:T(8,128)(2,1)S(1)}, bf16[8,1024,512]{2,1,0:T(8,128)(2,1)}, bf16[8,1024,256]{2,1,0:T(8,128)(2,1)S(1)}) custom-call(s32[17]{0:T(128)S(1)} %stack.215.order_ref, bf16[1024,768]{1,0:T(8,128)(2,1)S(1)} %get-tuple-element.215.refs_0_, ...), custom_call_target="tpu_custom_call", output_to_operand_aliasing={{2}: (18, {}), {3}: (19, {})} | custom-call | tf_op jit(solution)/shard_map/expert_grads/pallas_call | solution.py:521
  235.1 8.8 %expert_grads.11 = (bf16[1,1536,384]{2,1,0:T(8,128)(2,1)S(1)}, bf16[1,1536,384]{2,1,0:T(8,128)(2,1)S(1)}, bf16[1,1024,512]{2,1,0:T(8,128)(2,1)S(1)}, bf16[1,1024,256]{2,1,0:T(8,128)(2,1)S(1)}) custom-call(s32[17]{0:T(128)S(1)} %stack.215.order_ref, bf16[1024,768]{1,0:T(8,128)(2,1)S(1)} %get-tuple-element.215.refs_0_, ...), custom_call_target="tpu_custom_call" | custom-call | tf_op jit(solution)/shard_map/expert_grads/pallas_call | solution.py:521
  252.1 12.6 %mix.4 = bf16[1024,768]{1,0:T(8,128)(2,1)S(1)} custom-call(s32[17]{0:T(128)S(1)} %stack.215.order_ref, bf16[8,1024,512]{2,1,0:T(8,128)(2,1)} %get-tuple-element.243.refs_0_, bf16[1,1024,512]{2,1,0:T(8,128)(2,1)S(1)} %get-tuple-element.248.refs_1_, ...), custom_call_target="tpu_custom_call" | custom-call | tf_op jit(solution)/shard_map/mix/pallas_call | solution.py:592
  264.8 11.0 %collective-permute-done.28 = bf16[1,1536,384]{2,1,0:T(8,128)(2,1)S(1)} collective-permute-done((bf16[1,1536,384]{2,1,0:T(8,128)(2,1)S(1)}, bf16[1,1536,384]{2,1,0:T(8,128)(2,1)S(1)}, u32[]{:S(2)}, u32[]{:S(2)}) %collective-permute-start.28) | collective-permute-done | bytes 1179680 | tf_op jit(solution)/shard_map/ppermute | solution.py:758
  278.8 12.5 %mix.5 = f32[1024,768]{1,0:T(8,128)S(1)} custom-call(s32[17]{0:T(128)S(1)} %stack.215.order_ref, bf16[8,1024,512]{2,1,0:T(8,128)(2,1)} %get-tuple-element.243.refs_0_, bf16[1,1024,512]{2,1,0:T(8,128)(2,1)S(1)} %get-tuple-element.248.refs_1_, bf16[16,768,256]{2,1,0:T(8,128)(2,1)} %refs_16_.1, bf16[16,768,256]{2,1,0:T(8,128)(2,1)} %refs_17_.1, ...), custom_call_target="tpu_custom_call" | custom-call | tf_op jit(solution)/shard_map/mix/pallas_call | solution.py:592
  292.8 2.3 collective-permute-start.38
  299.1 24.7 %collective-permute-done.33 = bf16[1,1536,384]{2,1,0:T(8,128)(2,1)S(1)} collective-permute-done((bf16[1,1536,384]{2,1,0:T(8,128)(2,1)S(1)}, bf16[1,1536,384]{2,1,0:T(8,128)(2,1)S(1)}, u32[]{:S(2)}, u32[]{:S(2)}) %collective-permute-start.33) | collective-permute-done | bytes 1179680 | tf_op jit(solution)/shard_map/ppermute | solution.py:758
  323.8 5.0 collective-permute-done.38
  328.8 3.8 multiply_reduce_fusion
  334.8 8.0 %mix.6 = bf16[1024,768]{1,0:T(8,128)(2,1)S(1)} custom-call(s32[17]{0:T(128)S(1)} %stack.215.order_ref, bf16[8,1024,256]{2,1,0:T(8,128)(2,1)} %copy-done.2, bf16[1,1024,256]{2,1,0:T(8,128)(2,1)S(1)} %get-tuple-element.261.refs_1_, ...), custom_call_target="tpu_custom_call" | custom-call | tf_op jit(solution)/shard_map/mix/pallas_call | solution.py:592
  342.9 3.1 fusion.52
  362.8 3.3 unpack.16
  371.5 3.5 unpack.17
  374.9 6.6 collective-permute-done.49.refs_0_
  384.1 11.3 %attend_back.1.refs_4_ = bf16[1024,640]{1,0:T(8,128)(2,1)S(1)} custom-call(s32[3]{0:T(128)S(1)} %copy-done.75, bf16[512,640]{1,0:T(8,128)(2,1)S(1)} %copy-done.40, bf16[512,640]{1,0:T(8,128)(2,1)S(1)} %copy-done.42, bf16[1024,768]{1,0:T(8,128)(2,1)} %get-tuple-element.398.grad_ref.refs_6_, bf16[1024,768]{1,0:T(8,128)(2,1)} %collective-permute-done.40.grad_c_ref.refs_7_, ...), custom_call_target="tpu_custom_call" | custom-call | tf_op jit(solution)/shard_map/attend_back/pallas_call | solution.py:165
  395.4 2.6 convolution_convert_fusion
  400.8 7.4 %mix.7 = f32[1024,768]{1,0:T(8,128)S(1)} custom-call(s32[17]{0:T(128)S(1)} %stack.215.order_ref, bf16[8,1024,256]{2,1,0:T(8,128)(2,1)} %copy-done.2, bf16[1,1024,256]{2,1,0:T(8,128)(2,1)S(1)} %copy-done.47, bf16[16,256,768]{2,1,0:T(8,128)(2,1)} %refs_9_.13, bf16[16,256,768]{2,1,0:T(8,128)(2,1)} %refs_9_.13, bf16[16,256,768]{2,1,0:T(8,128)(2,1)} %refs_9_.13, ...), custom_call_target="tpu_custom_call" | custom-call | tf_op jit(solution)/shard_map/mix/pallas_call | solution.py:592
  408.4 3.7 unpack.18
  412.1 10.1 %late_grads.1 = (bf16[2,768,896]{2,1,0:T(8,128)(2,1)S(1)}, bf16[2,768,896]{2,1,0:T(8,128)(2,1)}) custom-call(s32[3]{0:T(128)S(1)} %copy-done.75, bf16[512,768]{1,0:T(8,128)(2,1)S(1)} %copy-done.63, bf16[512,768]{1,0:T(8,128)(2,1)S(1)} %copy-done.65, bf16[512,768]{1,0:T(8,128)(2,1)S(1)} %copy-done.67, bf16[512,768]{1,0:T(8,128)(2,1)S(1)} %copy-done.69, ...), custom_call_target="tpu_custom_call" | custom-call | tf_op jit(solution)/shard_map/late_grads/pallas_call | solution.py:216
  428.2 3.3 unpack.19
  431.5 5.8 collective-permute-done.55.refs_0_
  440.0 4.7 collective-permute-done.54
  451.3 3.3 collective-permute-done.58.refs_0_
  456.9 2.9 convert_add_fusion
  469.9 5.3 collective-permute-done.61.refs_0_
  478.5 2.3 unpack.21
  484.4 5.2 collective-permute-done.79
  494.6 15.1 %collective-permute-done.64.refs_0_ = bf16[1,768,384]{2,1,0:T(8,128)(2,1)S(1)} collective-permute-done((bf16[1,768,384]{2,1,0:T(8,128)(2,1)S(1)}, bf16[1,768,384]{2,1,0:T(8,128)(2,1)S(1)}, u32[]{:S(2)}, u32[]{:S(2)}) %collective-permute-start.64) | collective-permute-done | bytes 589856 | tf_op jit(solution)/shard_map/ppermute | solution.py:758
  511.0 3.5 collective-permute-done.65.refs_1_
  514.5 2.6 collective-permute-done.63
  518.5 2.3 collective-permute-done.44
  532.9 14.0 %collective-permute-done.81 = bf16[2,96,896]{2,1,0:T(8,128)(2,1)S(1)} collective-permute-done((bf16[2,96,896]{2,1,0:T(8,128)(2,1)S(1)}, bf16[2,96,896]{2,1,0:T(8,128)(2,1)S(1)}, u32[]{:S(2)}, u32[]{:S(2)}) %collective-permute-start.81) | collective-permute-done | bytes 344096 | tf_op jit(solution)/shard_map/ppermute | solution.py:758
  556.8 2.9 collective-permute-done.82
  561.0 5.2 collective-permute-done.75.refs_0_
  566.2 5.7 collective-permute-done.76.refs_1_
  584.6 8.6 %collective-permute-done.86.refs_0_ = bf16[1,768,384]{2,1,0:T(8,128)(2,1)S(1)} collective-permute-done((bf16[1,768,384]{2,1,0:T(8,128)(2,1)S(1)}, bf16[1,768,384]{2,1,0:T(8,128)(2,1)S(1)}, u32[]{:S(2)}, u32[]{:S(2)}) %collective-permute-start.86) | collective-permute-done | bytes 589856 | tf_op jit(solution)/shard_map/ppermute | solution.py:758
  603.0 10.2 %collective-permute-done.89.refs_0_ = bf16[1,768,384]{2,1,0:T(8,128)(2,1)S(1)} collective-permute-done((bf16[1,768,384]{2,1,0:T(8,128)(2,1)S(1)}, bf16[1,768,384]{2,1,0:T(8,128)(2,1)S(1)}, u32[]{:S(2)}, u32[]{:S(2)}) %collective-permute-start.89) | collective-permute-done | bytes 589856 | tf_op jit(solution)/shard_map/ppermute | solution.py:758
  617.2 3.4 collective-permute-done.88
  625.1 15.4 %collective-permute-done.91 = bf16[2,96,896]{2,1,0:T(8,128)(2,1)S(1)} collective-permute-done((bf16[2,96,896]{2,1,0:T(8,128)(2,1)S(1)}, bf16[2,96,896]{2,1,0:T(8,128)(2,1)S(1)}, u32[]{:S(2)}, u32[]{:S(2)}) %collective-permute-start.91) | collective-permute-done | bytes 344096 | tf_op jit(solution)/shard_map/ppermute | solution.py:758
  646.9 4.6 collective-permute-done.92
  653.7 17.0 %collective-permute-done.95 = bf16[2,96,896]{2,1,0:T(8,128)(2,1)S(1)} collective-permute-done((bf16[2,96,896]{2,1,0:T(8,128)(2,1)S(1)}, bf16[2,96,896]{2,1,0:T(8,128)(2,1)S(1)}, u32[]{:S(2)}, u32[]{:S(2)}) %collective-permute-start.95) | collective-permute-done | bytes 344096 | tf_op jit(solution)/shard_map/ppermute | solution.py:758
  674.9 5.0 collective-permute-done.96
  683.5 4.8 collective-permute-done.99
  689.9 4.8 unpack_late.1
  (522 shorter events, 214.0 us)
Async XLA Ops:
  0.6 37.6 %collective-permute-start.15 = (bf16[16,768,256]{2,1,0:T(8,128)(2,1)}, bf16[16,768,256]{2,1,0:T(8,128)(2,1)}, u32[]{:S(2)}, u32[]{:S(2)}) collective-permute-start(bf16[16,768,256]{2,1,0:T(8,128)(2,1)} %refs_16_.1), channel_id=1, source_target_pairs={{0,1},{1,0},{2,3},{3,2},{4,5},{5,4},{6,7},{7,6},{8,9},{9,8},{10,11... | collective-permute-start | bytes 18874376 | tf_op jit(solution)/shard_map/ppermute | solution.py:47
  7.5 27.4 %collective-permute-start.3 = (bf16[512,768]{1,0:T(8,128)(2,1)}, bf16[512,768]{1,0:T(8,128)(2,1)}, u32[]{:S(2)}, u32[]{:S(2)}) collective-permute-start(bf16[512,768]{1,0:T(8,128)(2,1)} %refs_0_.1), channel_id=1, source_target_pairs={{0,2},{2,0},{1,3},{3,1},{4,6},{6,4},{5,7},{7,5},{8,10},{10,8},{9,1... | collective-permute-start | bytes 2359304 | tf_op jit(solution)/shard_map/ppermute | solution.py:47
  13.2 21.7 %collective-permute-start = (bf16[192,768]{1,0:T(8,128)(2,1)S(1)}, bf16[192,768]{1,0:T(8,128)(2,1)}, u32[]{:S(2)}, u32[]{:S(2)}) collective-permute-start(bf16[192,768]{1,0:T(8,128)(2,1)S(1)} %constant_dynamic-slice_fusion), channel_id=1, source_target_pairs={{0,2},{2,0},{1,3},{3,1},{4,6},{6,4},{5,7},{7,5},{8,10},{10,8},{9,1... | collective-permute-start | bytes 884744 | tf_op jit(solution)/shard_map/ppermute | solution.py:47
  38.3 32.6 %collective-permute-start.16 = (bf16[16,768,256]{2,1,0:T(8,128)(2,1)}, bf16[16,768,256]{2,1,0:T(8,128)(2,1)}, u32[]{:S(2)}, u32[]{:S(2)}) collective-permute-start(bf16[16,768,256]{2,1,0:T(8,128)(2,1)} %refs_17_.1), channel_id=1, source_target_pairs={{0,1},{1,0},{2,3},{3,2},{4,5},{5,4},{6,7},{7,6},{8,9},{9,8},{10,11... | collective-permute-start | bytes 18874376 | tf_op jit(solution)/shard_map/ppermute | solution.py:47
  42.7 28.2 %collective-permute-start.8 = (bf16[768,768]{1,0:T(8,128)(2,1)}, bf16[768,768]{1,0:T(8,128)(2,1)}, u32[]{:S(2)}, u32[]{:S(2)}) collective-permute-start(bf16[768,768]{1,0:T(8,128)(2,1)} %out_ref.1), channel_id=1, source_target_pairs={{0,1},{1,0},{2,3},{3,2},{4,5},{5,4},{6,7},{7,6},{8,9},{9,8},{10,11... | collective-permute-start | bytes 3538952 | tf_op jit(solution)/shard_map/ppermute | solution.py:47
  50.1 19.0 %collective-permute-start.10 = (bf16[512,768]{1,0:T(8,128)(2,1)S(1)}, bf16[512,768]{1,0:T(8,128)(2,1)S(1)}, u32[]{:S(2)}, u32[]{:S(2)}) collective-permute-start(bf16[512,768]{1,0:T(8,128)(2,1)S(1)} %copy-done.101), channel_id=1, source_target_pairs={{0,2},{2,0},{1,3},{3,1},{4,6},{6,4},{5,7},{7,5},{8,10},{10,8},{9,1... | collective-permute-start | bytes 2359304 | tf_op jit(solution)/shard_map/ppermute | solution.py:47
  70.9 47.5 %collective-permute-start.17 = (bf16[16,256,768]{2,1,0:T(8,128)(2,1)}, bf16[16,256,768]{2,1,0:T(8,128)(2,1)}, u32[]{:S(2)}, u32[]{:S(2)}) collective-permute-start(bf16[16,256,768]{2,1,0:T(8,128)(2,1)} %refs_9_.13), channel_id=1, source_target_pairs={{0,1},{1,0},{2,3},{3,2},{4,5},{5,4},{6,7},{7,6},{8,9},{9,8},{10,11... | collective-permute-start | bytes 18874376 | tf_op jit(solution)/shard_map/ppermute | solution.py:47
  70.9 20.3 %collective-permute-start.9 = (bf16[1024,384]{1,0:T(8,128)(2,1)}, bf16[1024,384]{1,0:T(8,128)(2,1)}, u32[]{:S(2)}, u32[]{:S(2)}) collective-permute-start(bf16[1024,384]{1,0:T(8,128)(2,1)} %attend.1.refs_4_.refs_5_), channel_id=1, source_target_pairs={{0,2},{2,0},{1,3},{3,1},{4,6},{6,4},{5,7},{7,5},{8,10},{10,8},{9,1... | collective-permute-start | bytes 2359304 | tf_op jit(solution)/shard_map/ppermute | solution.py:47
  72.7 18.5 %collective-permute-start.12 = (bf16[384,768]{1,0:T(8,128)(2,1)}, bf16[384,768]{1,0:T(8,128)(2,1)S(1)}, u32[]{:S(2)}, u32[]{:S(2)}) collective-permute-start(bf16[384,768]{1,0:T(8,128)(2,1)} %pad_maximum_fusion.2), channel_id=1, source_target_pairs={{0,8},{4,12},{8,0},{12,4},{16,24},{20,28},{24,16},{28,20},{1,9},{5... | collective-permute-start | bytes 1769480 | tf_op jit(solution)/shard_map/ppermute | solution.py:797
  77.1 41.3 %collective-permute-start.14 = (bf16[1024,768]{1,0:T(8,128)(2,1)S(1)}, bf16[1024,768]{1,0:T(8,128)(2,1)S(1)}, u32[]{:S(2)}, u32[]{:S(2)}) collective-permute-start(bf16[1024,768]{1,0:T(8,128)(2,1)S(1)} %pad_maximum_fusion.refs_2_), channel_id=1, source_target_pairs={{0,1},{1,0},{2,3},{3,2},{4,5},{5,4},{6,7},{7,6},{8,9},{9,8},{10,11... | collective-permute-start | bytes 4718600 | tf_op jit(solution)/shard_map/ppermute | solution.py:47
  129.4 28.0 %collective-permute-start.18 = (bf16[1,1536,384]{2,1,0:T(8,128)(2,1)S(1)}, bf16[1,1536,384]{2,1,0:T(8,128)(2,1)S(1)}, u32[]{:S(2)}, u32[]{:S(2)}) collective-permute-start(bf16[1,1536,384]{2,1,0:T(8,128)(2,1)S(1)} %get-tuple-element.219), channel_id=1, source_target_pairs={{0,8},{8,16},{16,24},{24,28},{28,20},{20,12},{12,4},{4,0},{9,1},{1... | collective-permute-start | bytes 3538952 | tf_op jit(solution)/shard_map/ppermute | solution.py:758
  131.3 28.6 %collective-permute-start.20 = (bf16[1,1536,384]{2,1,0:T(8,128)(2,1)S(1)}, bf16[1,1536,384]{2,1,0:T(8,128)(2,1)S(1)}, u32[]{:S(2)}, u32[]{:S(2)}) collective-permute-start(bf16[1,1536,384]{2,1,0:T(8,128)(2,1)S(1)} %get-tuple-element.220), channel_id=1, source_target_pairs={{8,0},{16,8},{24,16},{28,24},{20,28},{12,20},{4,12},{0,4},{1,9},{9... | collective-permute-start | bytes 3538952 | tf_op jit(solution)/shard_map/ppermute | solution.py:758
  157.7 28.6 %collective-permute-start.19 = (bf16[1,1536,384]{2,1,0:T(8,128)(2,1)S(1)}, bf16[1,1536,384]{2,1,0:T(8,128)(2,1)S(1)}, u32[]{:S(2)}, u32[]{:S(2)}) collective-permute-start(bf16[1,1536,384]{2,1,0:T(8,128)(2,1)S(1)} %add_convert_fusion.13), channel_id=1, source_target_pairs={{0,8},{8,16},{16,24},{24,28},{28,20},{20,12},{12,4},{4,0},{9,1},{1... | collective-permute-start | bytes 3538952 | tf_op jit(solution)/shard_map/ppermute | solution.py:758
  160.2 27.5 %collective-permute-start.22 = (bf16[1,1536,384]{2,1,0:T(8,128)(2,1)S(1)}, bf16[1,1536,384]{2,1,0:T(8,128)(2,1)S(1)}, u32[]{:S(2)}, u32[]{:S(2)}) collective-permute-start(bf16[1,1536,384]{2,1,0:T(8,128)(2,1)S(1)} %add_convert_fusion.12), channel_id=1, source_target_pairs={{8,0},{16,8},{24,16},{28,24},{20,28},{12,20},{4,12},{0,4},{1,9},{9... | collective-permute-start | bytes 3538952 | tf_op jit(solution)/shard_map/ppermute | solution.py:758
  186.7 28.6 %collective-permute-start.21 = (bf16[1,1536,384]{2,1,0:T(8,128)(2,1)S(1)}, bf16[1,1536,384]{2,1,0:T(8,128)(2,1)S(1)}, u32[]{:S(2)}, u32[]{:S(2)}) collective-permute-start(bf16[1,1536,384]{2,1,0:T(8,128)(2,1)S(1)} %add_convert_fusion.11), channel_id=1, source_target_pairs={{0,8},{8,16},{16,24},{24,28},{28,20},{20,12},{12,4},{4,0},{9,1},{1... | collective-permute-start | bytes 3538952 | tf_op jit(solution)/shard_map/ppermute | solution.py:758
  189.0 31.3 %collective-permute-start.24 = (bf16[1,1536,384]{2,1,0:T(8,128)(2,1)}, bf16[1,1536,384]{2,1,0:T(8,128)(2,1)}, u32[]{:S(2)}, u32[]{:S(2)}) collective-permute-start(bf16[1,1536,384]{2,1,0:T(8,128)(2,1)} %add_convert_fusion.10), channel_id=1, source_target_pairs={{8,0},{16,8},{24,16},{28,24},{20,28},{12,20},{4,12},{0,4},{1,9},{9... | collective-permute-start | bytes 3538952 | tf_op jit(solution)/shard_map/ppermute | solution.py:758
  190.1 45.0 %collective-permute-start.25 = (bf16[1,768,512]{2,1,0:T(8,128)(2,1)S(1)}, bf16[1,768,512]{2,1,0:T(8,128)(2,1)S(1)}, u32[]{:S(2)}, u32[]{:S(2)}) collective-permute-start(bf16[1,768,512]{2,1,0:T(8,128)(2,1)S(1)} %bitcast.206), channel_id=1, source_target_pairs={{0,1},{1,0},{2,3},{3,2},{4,5},{5,4},{6,7},{7,6},{8,9},{9,8},{10,11... | collective-permute-start | bytes 2359304 | tf_op jit(solution)/shard_map/ppermute | solution.py:47
  190.1 45.0 %collective-permute-start.26 = (bf16[1,768,512]{2,1,0:T(8,128)(2,1)S(1)}, bf16[1,768,512]{2,1,0:T(8,128)(2,1)S(1)}, u32[]{:S(2)}, u32[]{:S(2)}) collective-permute-start(bf16[1,768,512]{2,1,0:T(8,128)(2,1)S(1)} %bitcast.211), channel_id=1, source_target_pairs={{0,1},{1,0},{2,3},{3,2},{4,5},{5,4},{6,7},{7,6},{8,9},{9,8},{10,11... | collective-permute-start | bytes 2359304 | tf_op jit(solution)/shard_map/ppermute | solution.py:47
  219.4 26.4 %collective-permute-start.23 = (bf16[1,1536,384]{2,1,0:T(8,128)(2,1)}, bf16[1,1536,384]{2,1,0:T(8,128)(2,1)}, u32[]{:S(2)}, u32[]{:S(2)}) collective-permute-start(bf16[1,1536,384]{2,1,0:T(8,128)(2,1)} %add_convert_fusion.9), channel_id=1, source_target_pairs={{0,8},{8,16},{16,24},{24,28},{28,20},{20,12},{12,4},{4,0},{9,1},{1... | collective-permute-start | bytes 3538952 | tf_op jit(solution)/shard_map/ppermute | solution.py:758
  222.9 25.5 %collective-permute-start.29 = (bf16[1,1536,384]{2,1,0:T(8,128)(2,1)}, bf16[1,1536,384]{2,1,0:T(8,128)(2,1)}, u32[]{:S(2)}, u32[]{:S(2)}) collective-permute-start(bf16[1,1536,384]{2,1,0:T(8,128)(2,1)} %add_convert_fusion.8), channel_id=1, source_target_pairs={{8,0},{16,8},{24,16},{28,24},{20,28},{12,20},{4,12},{0,4},{1,9},{9... | collective-permute-start | bytes 3538952 | tf_op jit(solution)/shard_map/ppermute | solution.py:758
  247.8 28.0 %collective-permute-start.28 = (bf16[1,1536,384]{2,1,0:T(8,128)(2,1)S(1)}, bf16[1,1536,384]{2,1,0:T(8,128)(2,1)S(1)}, u32[]{:S(2)}, u32[]{:S(2)}) collective-permute-start(bf16[1,1536,384]{2,1,0:T(8,128)(2,1)S(1)} %add_convert_fusion.7), channel_id=1, source_target_pairs={{0,8},{8,16},{16,24},{24,28},{28,20},{20,12},{12,4},{4,0},{9,1},{1... | collective-permute-start | bytes 3538952 | tf_op jit(solution)/shard_map/ppermute | solution.py:758
  250.0 27.0 %collective-permute-start.31 = (bf16[1,1536,384]{2,1,0:T(8,128)(2,1)S(1)}, bf16[1,1536,384]{2,1,0:T(8,128)(2,1)S(1)}, u32[]{:S(2)}, u32[]{:S(2)}) collective-permute-start(bf16[1,1536,384]{2,1,0:T(8,128)(2,1)S(1)} %add_convert_fusion.6), channel_id=1, source_target_pairs={{8,0},{16,8},{24,16},{28,24},{20,28},{12,20},{4,12},{0,4},{1,9},{9... | collective-permute-start | bytes 3538952 | tf_op jit(solution)/shard_map/ppermute | solution.py:758
  264.7 26.6 %collective-permute-start.37 = (bf16[1024,768]{1,0:T(8,128)(2,1)S(1)}, bf16[1024,768]{1,0:T(8,128)(2,1)S(1)}, u32[]{:S(2)}, u32[]{:S(2)}) collective-permute-start(bf16[1024,768]{1,0:T(8,128)(2,1)S(1)} %mix.4), channel_id=1, source_target_pairs={{0,1},{1,0},{2,3},{3,2},{4,5},{5,4},{6,7},{7,6},{8,9},{9,8},{10,11... | collective-permute-start | bytes 4718600 | tf_op jit(solution)/shard_map/ppermute | solution.py:47
  277.1 20.0 %collective-permute-start.30 = (bf16[1,1536,384]{2,1,0:T(8,128)(2,1)}, bf16[1,1536,384]{2,1,0:T(8,128)(2,1)}, u32[]{:S(2)}, u32[]{:S(2)}) collective-permute-start(bf16[1,1536,384]{2,1,0:T(8,128)(2,1)} %add_convert_fusion.5), channel_id=1, source_target_pairs={{0,8},{8,16},{16,24},{24,28},{28,20},{20,12},{12,4},{4,0},{9,1},{1... | collective-permute-start | bytes 3538952 | tf_op jit(solution)/shard_map/ppermute | solution.py:758
  292.8 36.0 %collective-permute-start.38 = (bf16[1024,768]{1,0:T(8,128)(2,1)S(1)}, bf16[1024,768]{1,0:T(8,128)(2,1)S(1)}, u32[]{:S(2)}, u32[]{:S(2)}) collective-permute-start(bf16[1024,768]{1,0:T(8,128)(2,1)S(1)} %fusion), channel_id=1, source_target_pairs={{0,2},{2,0},{1,3},{3,1},{4,6},{6,4},{5,7},{7,5},{8,10},{10,8},{9,1... | collective-permute-start | bytes 4718600 | tf_op jit(solution)/shard_map/ppermute | solution.py:47
  295.1 28.7 %collective-permute-start.33 = (bf16[1,1536,384]{2,1,0:T(8,128)(2,1)S(1)}, bf16[1,1536,384]{2,1,0:T(8,128)(2,1)S(1)}, u32[]{:S(2)}, u32[]{:S(2)}) collective-permute-start(bf16[1,1536,384]{2,1,0:T(8,128)(2,1)S(1)} %copy-done.99), channel_id=1, source_target_pairs={{8,0},{16,8},{24,16},{28,24},{20,28},{12,20},{4,12},{0,4},{1,9},{9... | collective-permute-start | bytes 3538952 | tf_op jit(solution)/shard_map/ppermute | solution.py:758
  298.7 47.4 %collective-permute-start.32 = (bf16[1,1536,384]{2,1,0:T(8,128)(2,1)S(1)}, bf16[1,1536,384]{2,1,0:T(8,128)(2,1)}, u32[]{:S(2)}, u32[]{:S(2)}) collective-permute-start(bf16[1,1536,384]{2,1,0:T(8,128)(2,1)S(1)} %add_convert_fusion.3), channel_id=1, source_target_pairs={{0,8},{8,16},{16,24},{24,28},{28,20},{20,12},{12,4},{4,0},{9,1},{1... | collective-permute-start | bytes 3538952 | tf_op jit(solution)/shard_map/ppermute | solution.py:758
  346.0 38.0 %collective-permute-start.40 = (bf16[1024,768]{1,0:T(8,128)(2,1)}, bf16[1024,768]{1,0:T(8,128)(2,1)}, u32[]{:S(2)}, u32[]{:S(2)}) collective-permute-start(bf16[1024,768]{1,0:T(8,128)(2,1)} %get-tuple-element.398.grad_ref.refs_6_), channel_id=1, source_target_pairs={{0,1},{1,0},{2,3},{3,2},{4,5},{5,4},{6,7},{7,6},{8,9},{9,8},{10,11... | collective-permute-start | bytes 4718600 | tf_op jit(solution)/shard_map/ppermute | solution.py:47
  358.3 66.3 %collective-permute-start.35 = (bf16[1024,768]{1,0:T(8,128)(2,1)}, bf16[1024,768]{1,0:T(8,128)(2,1)}, u32[]{:S(2)}, u32[]{:S(2)}) collective-permute-start(bf16[1024,768]{1,0:T(8,128)(2,1)} %copy-done.50), channel_id=1, source_target_pairs={{0,1},{1,0},{2,3},{3,2},{4,5},{5,4},{6,7},{7,6},{8,9},{9,8},{10,11... | collective-permute-start | bytes 4718600 | tf_op jit(solution)/shard_map/ppermute | solution.py:47
  381.5 40.7 %collective-permute-start.51 = (bf16[1,768,384]{2,1,0:T(8,128)(2,1)}, bf16[1,768,384]{2,1,0:T(8,128)(2,1)}, u32[]{:S(2)}, u32[]{:S(2)}) collective-permute-start(bf16[1,768,384]{2,1,0:T(8,128)(2,1)} %collective-permute-done.49.refs_0_), channel_id=1, source_target_pairs={{0,8},{8,16},{16,24},{24,28},{28,20},{20,12},{12,4},{4,0},{9,1},{1... | collective-permute-start | bytes 1769480 | tf_op jit(solution)/shard_map/ppermute | solution.py:758
  382.2 40.3 %collective-permute-start.53 = (bf16[1,768,384]{2,1,0:T(8,128)(2,1)}, bf16[1,768,384]{2,1,0:T(8,128)(2,1)}, u32[]{:S(2)}, u32[]{:S(2)}) collective-permute-start(bf16[1,768,384]{2,1,0:T(8,128)(2,1)} %collective-permute-done.52.refs_1_), channel_id=1, source_target_pairs={{8,0},{16,8},{24,16},{28,24},{20,28},{12,20},{4,12},{0,4},{1,9},{9... | collective-permute-start | bytes 1769480 | tf_op jit(solution)/shard_map/ppermute | solution.py:758
  398.0 52.4 %collective-permute-start.41 = (bf16[1024,768]{1,0:T(8,128)(2,1)}, bf16[1024,768]{1,0:T(8,128)(2,1)}, u32[]{:S(2)}, u32[]{:S(2)}) collective-permute-start(bf16[1024,768]{1,0:T(8,128)(2,1)} %convolution_convert_fusion), channel_id=1, source_target_pairs={{0,1},{1,0},{2,3},{3,2},{4,5},{5,4},{6,7},{7,6},{8,9},{9,8},{10,11... | collective-permute-start | bytes 4718600 | tf_op jit(solution)/shard_map/ppermute | solution.py:47
  424.4 20.4 %collective-permute-start.54 = (bf16[2,96,896]{2,1,0:T(8,128)(2,1)S(1)}, bf16[2,96,896]{2,1,0:T(8,128)(2,1)S(1)}, u32[]{:S(2)}, u32[]{:S(2)}) collective-permute-start(bf16[2,96,896]{2,1,0:T(8,128)(2,1)S(1)} %dynamic-slice_bitcast_fusion.1), channel_id=1, source_target_pairs={{0,8},{8,16},{16,24},{24,28},{28,20},{20,12},{12,4},{4,0},{9,1},{1... | collective-permute-start | bytes 1032200 | tf_op jit(solution)/shard_map/ppermute | solution.py:758
  426.4 20.6 %collective-permute-start.77 = (bf16[2,96,896]{2,1,0:T(8,128)(2,1)S(1)}, bf16[2,96,896]{2,1,0:T(8,128)(2,1)S(1)}, u32[]{:S(2)}, u32[]{:S(2)}) collective-permute-start(bf16[2,96,896]{2,1,0:T(8,128)(2,1)S(1)} %dynamic-slice_bitcast_fusion), channel_id=1, source_target_pairs={{8,0},{16,8},{24,16},{28,24},{20,28},{12,20},{4,12},{0,4},{1,9},{9... | collective-permute-start | bytes 1032200 | tf_op jit(solution)/shard_map/ppermute | solution.py:758
  438.9 29.0 %collective-permute-start.67 = (bf16[1,768,384]{2,1,0:T(8,128)(2,1)S(1)}, bf16[1,768,384]{2,1,0:T(8,128)(2,1)S(1)}, u32[]{:S(2)}, u32[]{:S(2)}) collective-permute-start(bf16[1,768,384]{2,1,0:T(8,128)(2,1)S(1)} %copy-done.104), channel_id=1, source_target_pairs={{0,1},{1,0},{2,3},{3,2},{4,5},{5,4},{6,7},{7,6},{8,9},{9,8},{10,11... | collective-permute-start | bytes 1769480 | tf_op jit(solution)/shard_map/ppermute | solution.py:47
  444.7 24.5 %collective-permute-start.36 = (bf16[512,768]{1,0:T(8,128)(2,1)S(1)}, bf16[512,768]{1,0:T(8,128)(2,1)S(1)}, u32[]{:S(2)}, u32[]{:S(2)}) collective-permute-start(bf16[512,768]{1,0:T(8,128)(2,1)S(1)} %dynamic-slice_convert_fusion.1), channel_id=1, source_target_pairs={{0,2},{2,0},{1,3},{3,1},{4,6},{6,4},{5,7},{7,5},{8,10},{10,8},{9,1... | collective-permute-start | bytes 2359304 | tf_op jit(solution)/shard_map/ppermute | solution.py:47
  462.4 18.4 %collective-permute-start.69 = (bf16[1,768,384]{2,1,0:T(8,128)(2,1)S(1)}, bf16[1,768,384]{2,1,0:T(8,128)(2,1)S(1)}, u32[]{:S(2)}, u32[]{:S(2)}) collective-permute-start(bf16[1,768,384]{2,1,0:T(8,128)(2,1)S(1)} %copy-done.103), channel_id=1, source_target_pairs={{0,1},{1,0},{2,3},{3,2},{4,5},{5,4},{6,7},{7,6},{8,9},{9,8},{10,11... | collective-permute-start | bytes 1769480 | tf_op jit(solution)/shard_map/ppermute | solution.py:47
  468.0 25.7 %collective-permute-start.42 = (bf16[512,768]{1,0:T(8,128)(2,1)S(1)}, bf16[512,768]{1,0:T(8,128)(2,1)S(1)}, u32[]{:S(2)}, u32[]{:S(2)}) collective-permute-start(bf16[512,768]{1,0:T(8,128)(2,1)S(1)} %dynamic-slice_convert_fusion), channel_id=1, source_target_pairs={{0,2},{2,0},{1,3},{3,1},{4,6},{6,4},{5,7},{7,5},{8,10},{10,8},{9,1... | collective-permute-start | bytes 2359304 | tf_op jit(solution)/shard_map/ppermute | solution.py:47
  480.8 45.3 %collective-permute-start.68 = (bf16[1,768,384]{2,1,0:T(8,128)(2,1)S(1)}, bf16[1,768,384]{2,1,0:T(8,128)(2,1)S(1)}, u32[]{:S(2)}, u32[]{:S(2)}) collective-permute-start(bf16[1,768,384]{2,1,0:T(8,128)(2,1)S(1)} %collective-permute-done.67.refs_0_), channel_id=1, source_target_pairs={{0,8},{8,16},{16,24},{24,28},{28,20},{20,12},{12,4},{4,0},{9,1},{1... | collective-permute-start | bytes 1769480 | tf_op jit(solution)/shard_map/ppermute | solution.py:758
  482.2 44.2 %collective-permute-start.70 = (bf16[1,768,384]{2,1,0:T(8,128)(2,1)S(1)}, bf16[1,768,384]{2,1,0:T(8,128)(2,1)S(1)}, u32[]{:S(2)}, u32[]{:S(2)}) collective-permute-start(bf16[1,768,384]{2,1,0:T(8,128)(2,1)S(1)} %collective-permute-done.69.refs_1_), channel_id=1, source_target_pairs={{8,0},{16,8},{24,16},{28,24},{20,28},{12,20},{4,12},{0,4},{1,9},{9... | collective-permute-start | bytes 1769480 | tf_op jit(solution)/shard_map/ppermute | solution.py:758
  484.1 25.6 %collective-permute-start.64 = (bf16[1,768,384]{2,1,0:T(8,128)(2,1)S(1)}, bf16[1,768,384]{2,1,0:T(8,128)(2,1)S(1)}, u32[]{:S(2)}, u32[]{:S(2)}) collective-permute-start(bf16[1,768,384]{2,1,0:T(8,128)(2,1)S(1)} %collective-permute-done.61.refs_0_), channel_id=1, source_target_pairs={{0,8},{8,16},{16,24},{24,28},{28,20},{20,12},{12,4},{4,0},{9,1},{1... | collective-permute-start | bytes 1769480 | tf_op jit(solution)/shard_map/ppermute | solution.py:758
  489.6 24.9 %collective-permute-start.65 = (bf16[1,768,384]{2,1,0:T(8,128)(2,1)S(1)}, bf16[1,768,384]{2,1,0:T(8,128)(2,1)S(1)}, u32[]{:S(2)}, u32[]{:S(2)}) collective-permute-start(bf16[1,768,384]{2,1,0:T(8,128)(2,1)S(1)} %collective-permute-done.62.refs_1_), channel_id=1, source_target_pairs={{8,0},{16,8},{24,16},{28,24},{20,28},{12,20},{4,12},{0,4},{1,9},{9... | collective-permute-start | bytes 1769480 | tf_op jit(solution)/shard_map/ppermute | solution.py:758
  493.7 23.4 %collective-permute-start.63 = (bf16[2,96,896]{2,1,0:T(8,128)(2,1)S(1)}, bf16[2,96,896]{2,1,0:T(8,128)(2,1)S(1)}, u32[]{:S(2)}, u32[]{:S(2)}) collective-permute-start(bf16[2,96,896]{2,1,0:T(8,128)(2,1)S(1)} %fusion.25), channel_id=1, source_target_pairs={{0,8},{8,16},{16,24},{24,28},{28,20},{20,12},{12,4},{4,0},{9,1},{1... | collective-permute-start | bytes 1032200 | tf_op jit(solution)/shard_map/ppermute | solution.py:758
  509.7 18.5 %collective-permute-start.80 = (bf16[2,96,896]{2,1,0:T(8,128)(2,1)S(1)}, bf16[2,96,896]{2,1,0:T(8,128)(2,1)S(1)}, u32[]{:S(2)}, u32[]{:S(2)}) collective-permute-start(bf16[2,96,896]{2,1,0:T(8,128)(2,1)S(1)} %fusion.18), channel_id=1, source_target_pairs={{8,0},{16,8},{24,16},{28,24},{20,28},{12,20},{4,12},{0,4},{1,9},{9... | collective-permute-start | bytes 1032200 | tf_op jit(solution)/shard_map/ppermute | solution.py:758
  514.5 37.5 %collective-permute-start.43 = (f32[512,1]{0,1:T(1,128)S(1)}, f32[512,1]{0,1:T(1,128)S(1)}, u32[]{:S(2)}, u32[]{:S(2)}) collective-permute-start(f32[512,1]{0,1:T(1,128)S(1)} %bitcast.255), channel_id=1, source_target_pairs={{0,1},{1,0},{2,3},{3,2},{4,5},{5,4},{6,7},{7,6},{8,9},{9,8},{10,11... | collective-permute-start | bytes 6152 | tf_op jit(solution)/shard_map/ppermute | solution.py:47
  526.4 22.3 %collective-permute-start.72 = (bf16[1,768,384]{2,1,0:T(8,128)(2,1)S(1)}, bf16[1,768,384]{2,1,0:T(8,128)(2,1)S(1)}, u32[]{:S(2)}, u32[]{:S(2)}) collective-permute-start(bf16[1,768,384]{2,1,0:T(8,128)(2,1)S(1)} %collective-permute-done.68.refs_0_), channel_id=1, source_target_pairs={{0,8},{8,16},{16,24},{24,28},{28,20},{20,12},{12,4},{4,0},{9,1},{1... | collective-permute-start | bytes 1769480 | tf_op jit(solution)/shard_map/ppermute | solution.py:758
  528.2 21.7 %collective-permute-start.73 = (bf16[1,768,384]{2,1,0:T(8,128)(2,1)S(1)}, bf16[1,768,384]{2,1,0:T(8,128)(2,1)S(1)}, u32[]{:S(2)}, u32[]{:S(2)}) collective-permute-start(bf16[1,768,384]{2,1,0:T(8,128)(2,1)S(1)} %collective-permute-done.70.refs_1_), channel_id=1, source_target_pairs={{8,0},{16,8},{24,16},{28,24},{20,28},{12,20},{4,12},{0,4},{1,9},{9... | collective-permute-start | bytes 1769480 | tf_op jit(solution)/shard_map/ppermute | solution.py:758
  530.5 20.3 %collective-permute-start.71 = (bf16[2,96,896]{2,1,0:T(8,128)(2,1)S(1)}, bf16[2,96,896]{2,1,0:T(8,128)(2,1)S(1)}, u32[]{:S(2)}, u32[]{:S(2)}) collective-permute-start(bf16[2,96,896]{2,1,0:T(8,128)(2,1)S(1)} %fusion.23), channel_id=1, source_target_pairs={{0,8},{8,16},{16,24},{24,28},{28,20},{20,12},{12,4},{4,0},{9,1},{1... | collective-permute-start | bytes 1032200 | tf_op jit(solution)/shard_map/ppermute | solution.py:758
  550.9 21.0 %collective-permute-start.76 = (bf16[1,768,384]{2,1,0:T(8,128)(2,1)S(1)}, bf16[1,768,384]{2,1,0:T(8,128)(2,1)S(1)}, u32[]{:S(2)}, u32[]{:S(2)}) collective-permute-start(bf16[1,768,384]{2,1,0:T(8,128)(2,1)S(1)} %collective-permute-done.73.refs_1_), channel_id=1, source_target_pairs={{8,0},{16,8},{24,16},{28,24},{20,28},{12,20},{4,12},{0,4},{1,9},{9... | collective-permute-start | bytes 1769480 | tf_op jit(solution)/shard_map/ppermute | solution.py:758
  552.0 21.5 %collective-permute-start.74 = (bf16[2,96,896]{2,1,0:T(8,128)(2,1)S(1)}, bf16[2,96,896]{2,1,0:T(8,128)(2,1)S(1)}, u32[]{:S(2)}, u32[]{:S(2)}) collective-permute-start(bf16[2,96,896]{2,1,0:T(8,128)(2,1)S(1)} %fusion.22), channel_id=1, source_target_pairs={{0,8},{8,16},{16,24},{24,28},{28,20},{20,12},{12,4},{4,0},{9,1},{1... | collective-permute-start | bytes 1032200 | tf_op jit(solution)/shard_map/ppermute | solution.py:758
  553.1 24.1 %collective-permute-start.47 = (f32[2,768]{1,0:T(2,128)S(1)}, f32[2,768]{1,0:T(2,128)S(1)}, u32[]{:S(2)}, u32[]{:S(2)}) collective-permute-start(f32[2,768]{1,0:T(2,128)S(1)} %add.587), channel_id=1, source_target_pairs={{0,2},{2,0},{1,3},{3,1},{4,6},{6,4},{5,7},{7,5},{8,10},{10,8},{9,1... | collective-permute-start | bytes 18440 | tf_op jit(solution)/shard_map/ppermute | solution.py:47
  579.4 23.1 %collective-permute-start.101 = (bf16[2,96,896]{2,1,0:T(8,128)(2,1)S(1)}, bf16[2,96,896]{2,1,0:T(8,128)(2,1)S(1)}, u32[]{:S(2)}, u32[]{:S(2)}) collective-permute-start(bf16[2,96,896]{2,1,0:T(8,128)(2,1)S(1)} %pad_maximum_fusion.4), channel_id=1, source_target_pairs={{8,0},{16,8},{24,16},{28,24},{20,28},{12,20},{4,12},{0,4},{1,9},{9... | collective-permute-start | bytes 1032200 | tf_op jit(solution)/shard_map/ppermute | solution.py:758
  580.8 19.7 %collective-permute-start.85 = (bf16[2,96,896]{2,1,0:T(8,128)(2,1)S(1)}, bf16[2,96,896]{2,1,0:T(8,128)(2,1)S(1)}, u32[]{:S(2)}, u32[]{:S(2)}) collective-permute-start(bf16[2,96,896]{2,1,0:T(8,128)(2,1)S(1)} %pad_maximum_fusion.3), channel_id=1, source_target_pairs={{0,8},{8,16},{16,24},{24,28},{28,20},{20,12},{12,4},{4,0},{9,1},{1... | collective-permute-start | bytes 1032200 | tf_op jit(solution)/shard_map/ppermute | solution.py:758
  595.6 19.5 %collective-permute-start.90 = (bf16[1,768,384]{2,1,0:T(8,128)(2,1)S(1)}, bf16[1,768,384]{2,1,0:T(8,128)(2,1)S(1)}, u32[]{:S(2)}, u32[]{:S(2)}) collective-permute-start(bf16[1,768,384]{2,1,0:T(8,128)(2,1)S(1)} %collective-permute-done.87.refs_1_), channel_id=1, source_target_pairs={{8,0},{16,8},{24,16},{28,24},{20,28},{12,20},{4,12},{0,4},{1,9},{9... | collective-permute-start | bytes 1769480 | tf_op jit(solution)/shard_map/ppermute | solution.py:758
  600.5 20.0 %collective-permute-start.88 = (bf16[2,96,896]{2,1,0:T(8,128)(2,1)S(1)}, bf16[2,96,896]{2,1,0:T(8,128)(2,1)S(1)}, u32[]{:S(2)}, u32[]{:S(2)}) collective-permute-start(bf16[2,96,896]{2,1,0:T(8,128)(2,1)S(1)} %collective-permute-done.85), channel_id=1, source_target_pairs={{0,8},{8,16},{16,24},{24,28},{28,20},{20,12},{12,4},{4,0},{9,1},{1... | collective-permute-start | bytes 1032200 | tf_op jit(solution)/shard_map/ppermute | solution.py:758
  602.5 20.0 %collective-permute-start.102 = (bf16[2,96,896]{2,1,0:T(8,128)(2,1)S(1)}, bf16[2,96,896]{2,1,0:T(8,128)(2,1)S(1)}, u32[]{:S(2)}, u32[]{:S(2)}) collective-permute-start(bf16[2,96,896]{2,1,0:T(8,128)(2,1)S(1)} %collective-permute-done.101), channel_id=1, source_target_pairs={{8,0},{16,8},{24,16},{28,24},{20,28},{12,20},{4,12},{0,4},{1,9},{9... | collective-permute-start | bytes 1032200 | tf_op jit(solution)/shard_map/ppermute | solution.py:758
  615.1 27.6 %collective-permute-start.93 = (bf16[1,768,384]{2,1,0:T(8,128)(2,1)S(1)}, bf16[1,768,384]{2,1,0:T(8,128)(2,1)S(1)}, u32[]{:S(2)}, u32[]{:S(2)}) collective-permute-start(bf16[1,768,384]{2,1,0:T(8,128)(2,1)S(1)} %collective-permute-done.89.refs_0_), channel_id=1, source_target_pairs={{0,8},{8,16},{16,24},{24,28},{28,20},{20,12},{12,4},{4,0},{9,1},{1... | collective-permute-start | bytes 1769480 | tf_op jit(solution)/shard_map/ppermute | solution.py:758
  615.6 27.1 %collective-permute-start.94 = (bf16[1,768,384]{2,1,0:T(8,128)(2,1)S(1)}, bf16[1,768,384]{2,1,0:T(8,128)(2,1)S(1)}, u32[]{:S(2)}, u32[]{:S(2)}) collective-permute-start(bf16[1,768,384]{2,1,0:T(8,128)(2,1)S(1)} %collective-permute-done.90.refs_1_), channel_id=1, source_target_pairs={{8,0},{16,8},{24,16},{28,24},{20,28},{12,20},{4,12},{0,4},{1,9},{9... | collective-permute-start | bytes 1769480 | tf_op jit(solution)/shard_map/ppermute | solution.py:758
  620.6 20.0 %collective-permute-start.91 = (bf16[2,96,896]{2,1,0:T(8,128)(2,1)S(1)}, bf16[2,96,896]{2,1,0:T(8,128)(2,1)S(1)}, u32[]{:S(2)}, u32[]{:S(2)}) collective-permute-start(bf16[2,96,896]{2,1,0:T(8,128)(2,1)S(1)} %collective-permute-done.88), channel_id=1, source_target_pairs={{0,8},{8,16},{16,24},{24,28},{28,20},{20,12},{12,4},{4,0},{9,1},{1... | collective-permute-start | bytes 1032200 | tf_op jit(solution)/shard_map/ppermute | solution.py:758
  622.5 19.6 %collective-permute-start.103 = (bf16[2,96,896]{2,1,0:T(8,128)(2,1)S(1)}, bf16[2,96,896]{2,1,0:T(8,128)(2,1)S(1)}, u32[]{:S(2)}, u32[]{:S(2)}) collective-permute-start(bf16[2,96,896]{2,1,0:T(8,128)(2,1)S(1)} %collective-permute-done.102), channel_id=1, source_target_pairs={{8,0},{16,8},{24,16},{28,24},{20,28},{12,20},{4,12},{0,4},{1,9},{9... | collective-permute-start | bytes 1032200 | tf_op jit(solution)/shard_map/ppermute | solution.py:758
  642.7 30.1 %collective-permute-start.97 = (bf16[1,768,384]{2,1,0:T(8,128)(2,1)S(1)}, bf16[1,768,384]{2,1,0:T(8,128)(2,1)S(1)}, u32[]{:S(2)}, u32[]{:S(2)}) collective-permute-start(bf16[1,768,384]{2,1,0:T(8,128)(2,1)S(1)} %collective-permute-done.93.refs_0_), channel_id=1, source_target_pairs={{0,8},{8,16},{16,24},{24,28},{28,20},{20,12},{12,4},{4,0},{9,1},{1... | collective-permute-start | bytes 1769480 | tf_op jit(solution)/shard_map/ppermute | solution.py:758
  644.3 28.5 %collective-permute-start.98 = (bf16[1,768,384]{2,1,0:T(8,128)(2,1)S(1)}, bf16[1,768,384]{2,1,0:T(8,128)(2,1)S(1)}, u32[]{:S(2)}, u32[]{:S(2)}) collective-permute-start(bf16[1,768,384]{2,1,0:T(8,128)(2,1)S(1)} %collective-permute-done.94.refs_1_), channel_id=1, source_target_pairs={{8,0},{16,8},{24,16},{28,24},{20,28},{12,20},{4,12},{0,4},{1,9},{9... | collective-permute-start | bytes 1769480 | tf_op jit(solution)/shard_map/ppermute | solution.py:758
  651.5 19.2 %collective-permute-start.95 = (bf16[2,96,896]{2,1,0:T(8,128)(2,1)S(1)}, bf16[2,96,896]{2,1,0:T(8,128)(2,1)S(1)}, u32[]{:S(2)}, u32[]{:S(2)}) collective-permute-start(bf16[2,96,896]{2,1,0:T(8,128)(2,1)S(1)} %collective-permute-done.92), channel_id=1, source_target_pairs={{0,8},{8,16},{16,24},{24,28},{28,20},{20,12},{12,4},{4,0},{9,1},{1... | collective-permute-start | bytes 1032200 | tf_op jit(solution)/shard_map/ppermute | solution.py:758
  653.2 18.8 %collective-permute-start.105 = (bf16[2,96,896]{2,1,0:T(8,128)(2,1)S(1)}, bf16[2,96,896]{2,1,0:T(8,128)(2,1)S(1)}, u32[]{:S(2)}, u32[]{:S(2)}) collective-permute-start(bf16[2,96,896]{2,1,0:T(8,128)(2,1)S(1)} %collective-permute-done.104), channel_id=1, source_target_pairs={{8,0},{16,8},{24,16},{28,24},{20,28},{12,20},{4,12},{0,4},{1,9},{9... | collective-permute-start | bytes 1032200 | tf_op jit(solution)/shard_map/ppermute | solution.py:758
  (159 other events, 1629.6 us)

commit v4 on v3

--- a/solution.py
+++ b/solution.py
@@ -225,8 +225,9 @@
 
 
 def columns_kernel(
-    col_ref, query_ref, key_ref, value_ref, gain_ref, gain_ffn_ref, out_ref, gains_ref
+    place_ref, query_ref, key_ref, value_ref, gain_ref, gain_ffn_ref, w_out_ref, out_ref, gains_ref, share_ref
 ):
+    share_ref[...] = w_out_ref[...]
     gains_ref[0:1, :] = gain_ref[...]
     gains_ref[1:2, :] = gain_ffn_ref[...]
     width = GROUP_HEADS * DH
@@ -235,7 +236,7 @@
     out_ref[:, width + DH :] = value_ref[...]
 
 
-def their_columns(col, w_query, w_key, w_value, gain_attn, gain_ffn):
+def their_columns(place, w_query, w_key, w_value, gain_attn, gain_ffn, w_out, shares):
     rows = w_query.shape[0]
     width = GROUP_HEADS * DH + 2 * DH
 
@@ -248,20 +249,43 @@
             num_scalar_prefetch=1,
             grid=(1,),
             in_specs=[theirs(GROUP_HEADS * DH), theirs(DH), theirs(DH)]
-            + [pl.BlockSpec(gain_attn.shape, lambda i, c: (0, 0))] * 2,
+            + [pl.BlockSpec(gain_attn.shape, lambda i, c: (0, 0))] * 2
+            + [pl.BlockSpec((rows // shares, rows), lambda i, c: (c[1], 0))],
             out_specs=[
                 pl.BlockSpec((rows, width), lambda i, c: (0, 0)),
                 pl.BlockSpec((2, rows), lambda i, c: (0, 0)),
+                pl.BlockSpec((rows // shares, rows), lambda i, c: (0, 0)),
             ],
         ),
         out_shape=[
             jax.ShapeDtypeStruct((rows, width), BF16),
             jax.ShapeDtypeStruct((2, rows), F32),
+            jax.ShapeDtypeStruct((rows // shares, rows), BF16),
         ],
         compiler_params=params(16, "arbitrary"),
         cost_estimate=SMALL,
         name="their_columns",
-    )(col, w_query, w_key, w_value, gain_attn, gain_ffn)
+    )(place, w_query, w_key, w_value, gain_attn, gain_ffn, w_out)
+
+
+def join_kernel(mine_ref, own_ref, other_ref, out_ref):
+    rows = own_ref.shape[0]
+    out_ref[pl.ds(pl.multiple_of(mine_ref[0] * rows, rows), rows), :] = own_ref[...]
+    out_ref[pl.ds(pl.multiple_of((1 - mine_ref[0]) * rows, rows), rows), :] = other_ref[...]
+
+
+def join(mine, own, other):
+    rows, width = own.shape
+    spec = pl.BlockSpec(memory_space=pltpu.VMEM)
+    return pl.pallas_call(
+        join_kernel,
+        out_shape=jax.ShapeDtypeStruct((2 * rows, width), own.dtype),
+        in_specs=[pl.BlockSpec(memory_space=pltpu.SMEM), spec, spec],
+        out_specs=spec,
+        compiler_params=params(16),
+        cost_estimate=SMALL,
+        name="join",
+    )(mine.reshape(1), own, other)
 
 
 def project_kernel(col_ref, own_ref, other_ref, gains_ref, gains_c_ref, query_ref, key_ref, value_ref, there_ref, x_own_ref, x_other_ref, qkv_ref, scale_ref):
@@ -382,7 +406,7 @@
             out_specs=[rowwise(features)] * 2,
         ),
         out_shape=[jax.ShapeDtypeStruct((rows, features), F32)] * 2,
-        compiler_params=params(32, "arbitrary"),
+        compiler_params=params(56, "arbitrary"),
         cost_estimate=pl.CostEstimate(
             flops=8 * rows * features * heads,
             bytes_accessed=16 * rows * features,
@@ -412,7 +436,7 @@
             jax.ShapeDtypeStruct((rows, features), BF16),
             jax.ShapeDtypeStruct((rows, 1), F32),
         ],
-        compiler_params=params(32, "arbitrary"),
+        compiler_params=params(56, "arbitrary"),
         cost_estimate=SMALL,
         name="hidden_after",
     )(place, *before, *attended, here, there, gains, gains_c)
@@ -769,8 +793,17 @@
     where = jnp.stack([row, seq_lengths[0], col])
     tokens_y = swap(tokens_in, "row")
     tokens_c = swap(tokens_in, "col")
-    there, gains = their_columns(
-        col_ref, w_query, w_key, w_value, norm_gain_attn[None], norm_gain_ffn[None]
+    count = min(ring_size, 4)
+    member = dp % count
+    there, gains, out_y = their_columns(
+        jnp.stack([col, member]),
+        w_query,
+        w_key,
+        w_value,
+        norm_gain_attn[None],
+        norm_gain_ffn[None],
+        w_out,
+        count,
     )
     there = swap(there, "col")
     gains_c = swap(gains, "col")
@@ -780,14 +813,11 @@
 
     near = project_half(tokens_in, tokens_c)
     gate_c = swap(w_gate, "col")
-    count = min(ring_size, 4)
-    share = w_out.shape[0] // count
-    member = dp % count
-    out_y = lax.dynamic_slice_in_dim(w_out, member * share, share, axis=0)
     out_y = swap(out_y, "row")
     tokens_y = after(tokens_y, near[2], out_y)
     tokens_yc = swap(tokens_y, "col")
-    grad_y = swap(after(out_grad, tokens_y), "row")
+    grad_cut = local_rows // 8 * 5
+    grad_y = swap(after(out_grad[:grad_cut], tokens_y), "row")
     far = project_half(tokens_y, tokens_yc)
 
     def double(part, bit, *others):
@@ -795,10 +825,10 @@
             return part
         pairs = [(m, m ^ bit) for m in range(dp_size)]
         came = after(lax.ppermute(part, "dp", pairs), *others)
-        return in_order(part, came, member // bit % 2, 0)
+        return join(member // bit % 2, part, came)
 
     out_y = double(out_y, 1)
-    where = after(where, out_y)
+    where = after(where, out_y, grad_y)
 
     w_sgate, w_sup, w_sdown = w_shared_gate[None], w_shared_up[None], w_shared_down[None]
     up_c = swap(after(w_up, gate_c, tokens_yc), "col")
@@ -814,13 +844,14 @@
         w_out,
         out_c,
     )
-    down_c = swap(after(w_down, up_c, attended_c, out_c, grad_y), "col")
-    grad_own = in_order(out_grad, grad_y, row, 0)
-    grad_other = swap(grad_own, "col")
-    attended_y = after(attended_y, grad_own, before[0])
+    down_c = swap(after(w_down, up_c, attended_c), "col")
+    rest_y = swap(after(out_grad[grad_cut:], attended_c), "row")
+    attended_y = after(attended_y, before[0])
     out_y = double(out_y, 2, attended_y)
     out_yc = swap(out_y, "col")
     attended_yc = swap(attended_y, "col")
+    grad_own = join(row, out_grad, jnp.concatenate([grad_y, rest_y], axis=0))
+    grad_other = swap(grad_own, "col")
     hidden, x_own, x_other, scale_ffn = hidden_after(
         where, before, [attended_y, attended_yc], out_y, out_yc, gains, gains_c
     )
@@ -903,27 +934,28 @@
 
         return work
 
-    bounds = list(range(each, pairs_total, 2 * each)) + [pairs_total]
-    tasks = [[work_experts(a, b)] for a, b in zip(bounds[:-1], bounds[1:], strict=True)]
-    if not tasks:
-        tasks.append([])
-    tasks[-1].append(work_shared)
-    tasks += [[work_mix(True, 1)], [work_mix(True, 0)], [work_mix(False, 1)], [work_mix(False, 0)]]
+    tasks = [work_experts(at, at + each) for at in range(each, pairs_total, each)]
+    tasks += [work_shared, work_mix(True, 1), work_mix(True, 0)]
+    later = [work_mix(False, 1), work_mix(False, 0)]
+    got = [None, None]
+    if ring_size > 1:
+        got[0] = send(sums[0], 0)
+        tasks.pop(0)(after(order, *sums))
+        got[1] = send(after(sums[1], kept[0]), 1)
     for s in range(1, ring_size):
-        got = [send(sums[k], k) for k in range(2)]
-        last = sums
-        if s <= len(tasks):
-            for task in tasks[s - 1]:
-                last = [task(after(order, *last))]
         for k in range(2):
+            last = sums
+            if tasks:
+                last = [tasks.pop(0)(after(order, *last))]
             got[k] = after(got[k], *last)
             parts = [runs[at] for at in range(each * s, each * s + each)]
             mine = [p[k][p[2] : p[2] + 1] for p in parts]
             mine = mine[0] if each == 1 else jnp.concatenate(mine, axis=0)
             sums[k] = add_rounded(got[k], mine)
-            last = [sums[k]]
-    for task in [task for step in tasks[ring_size - 1 :] for task in step]:
-        task(after(order, *sums))
+            if s + 1 < ring_size:
+                got[k] = send(sums[k], k)
+    while tasks:
+        tasks.pop(0)(after(order, *sums))
     sums = [across_rings(total) for total in sums]
     waves = [[total[:, :local_features] for total in sums]]
     crossed = [swap(total[:, local_features:], "col") for total in sums]
@@ -939,10 +971,6 @@
 
     normed_grad = mixed[True, 0] + swap(mixed[True, 1], "col").astype(F32)
     normed_grad = normed_grad + swap(normed_grad.astype(BF16), "row").astype(F32)
-    ffn_sum = mixed[False, 0] + swap(mixed[False, 1], "col").astype(F32)
-    ffn_rows = my_rows(ffn_sum) + swap(their_rows(ffn_sum).astype(BF16), "row").astype(F32)
-    block_out = (my_rows(hidden) + ffn_rows).astype(BF16)
-
     gain_ffn_part = jnp.sum(my_rows(normed_grad * hidden * scale_ffn), axis=0)
     scaled = normed_grad * norm_gain_ffn
     products = jnp.sum(scaled * hidden, axis=1, keepdims=True)
@@ -961,9 +989,6 @@
         attn_grad,
         attn_grad_c,
         runs["shared"][0:2],
-    )
-    here = jnp.concatenate(
-        [halves(w, 1, col)[0] for w in (w_query, w_key, w_value)], axis=1
     )
 
     packs = [
@@ -1023,17 +1048,22 @@
     for number, (wave, step) in enumerate(rounds):
         if step == 0:
             chunks = waves[wave]
-        got = [send(chunks[k], k) for k in range(2)]
-        steps = 0 if number < LATE_ROUND else 1
+        if number == LATE_ROUND:
+            late = [after(values, *chunks) for values in late]
+        steps = 1 if number >= LATE_ROUND else 0
         if number >= len(rounds) - LATE_ROUND:
             steps = 2
         steps = min(steps, late_total - late_done)
-        if number == LATE_ROUND:
-            late = [after(values, *chunks) for values in late]
+        got = [send(chunks[k], k) for k in range(2)]
         late_got = [send(late[k], k) for k in range(2)] if steps else None
         placed = place_chunks(wave, step, chunks, placed)
+        last = placed[0:1]
+        if number in (LATE_ROUND + 1, LATE_ROUND + 2):
+            last = [later.pop(0)(after(order, *last))]
+        if number == LATE_ROUND + 5:
+            qkv_grad = after(qkv_grad, *last)
         for k in range(2):
-            got[k] = after(got[k], placed[0])
+            got[k] = after(got[k], *last)
         for at in range(steps):
             if at:
                 late_got = [send(late[k], k) for k in range(2)]
@@ -1041,6 +1071,8 @@
         chunks = got
         if step == ring_size - 2:
             placed = place_chunks(wave, step + 1, chunks, placed)
+    while later:
+        later.pop(0)(order)
     if not rounds:
         for wave in range(2):
             placed = place_chunks(wave, 0, waves[wave], placed)
@@ -1055,6 +1087,13 @@
     shared_gate_grad, shared_up_grad, shared_down_grad = finals[0:3]
     query_grad, key_grad, value_grad, out_proj_grad = finals[3:7]
 
+    ffn_sum = mixed[False, 0] + swap(mixed[False, 1], "col").astype(F32)
+    ffn_rows = my_rows(ffn_sum) + swap(their_rows(ffn_sum).astype(BF16), "row").astype(F32)
+    block_out = (my_rows(hidden) + ffn_rows).astype(BF16)
+
+    here = jnp.concatenate(
+        [halves(w, 1, col)[0] for w in (w_query, w_key, w_value)], axis=1
+    )
     tokens_back = dot_nt(qkv_grad, here) + swap(
         dot_nt(qkv_grad, there).astype(BF16), "col"
     ).astype(F32)

time: 706 us -> 687 us (0.973)
  waiting for transfers between devices: 280 us -> 264 us
  Pallas kernels: 204 us -> 219 us
  other arithmetic: 43.7 us -> 34.8 us
    ppermute x70, waiting for transfers between devices: 236 us -> 174 us  [send(): return lax.ppermute(values, ('dp', 'col'), routes_of[which])]
    ppermute x33 -> x34, waiting for transfers between devices: 36.4 us -> 61.8 us  [swap(): return lax.ppermute(values, axis, [(0, 1), (1, 0)])]
    ppermute x3, waiting for transfers between devices: 2.27 us -> 21.4 us  [body(): gain_parts = gain_parts + lax.ppermute(gain_parts, 'dp', pairs)]
    pallas_call x6 -> x9, Pallas kernels: 72.5 us -> 79.2 us  [expert_grads(): pl.pallas_call(functools.partial(expert_kernel, shared, aliased, first),...]
    unnamed x230 -> x182, local copies, waits for them, and re-layouts: 31.2 us -> 24.8 us
    ppermute x33 -> x34, starting transfers between devices: 19.7 us -> 17.6 us  [swap(): return lax.ppermute(values, axis, [(0, 1), (1, 0)])]
  transfers between devices with their start and end apart: 108 -> 109, of which waited for: 51 -> 50; matrix products, arithmetic and copies ran while one was open for 8% -> 6% of each run, Pallas kernels for 27% -> 30%
where the time goes in v4:
time: 687 us; the launch traced here: 676 us
  waiting for transfers between devices  264 us (38%)
  Pallas kernels  219 us (32%)
  starting transfers between devices  99.8 us (15%)
  other arithmetic  34.8 us (5%)
  local copies, waits for them, and re-layouts  32.1 us (5%)
  between operations  23.6 us (3%)
    ppermute x70, waiting for transfers between devices, send(): return lax.ppermute(values, ('dp', 'col'), routes_of[which])  174 us
    pallas_call x9, Pallas kernels, expert_grads(): pl.pallas_call(functools.partial(expert_kernel, shared, aliased, first),...  79.2 us
    ppermute x70, starting transfers between devices, send(): return lax.ppermute(values, ('dp', 'col'), routes_of[which])  76.9 us
    ppermute x34, waiting for transfers between devices, swap(): return lax.ppermute(values, axis, [(0, 1), (1, 0)])  61.8 us
    pallas_call x16, Pallas kernels, unpack(): pl.pallas_call(functools.partial(unpack_kernel, aliased), grid_spec=pltpu...  39.9 us
    pallas_call x4, Pallas kernels, mix(): pl.pallas_call(functools.partial(mix_kernel, back, group), grid_spec=pltp...  39.6 us
    unnamed x182, local copies, waits for them, and re-layouts  24.8 us
    convert_element_type x28, other arithmetic, add_rounded(): return (left.astype(F32) + right.astype(F32)).astype(BF16)  23 us
  transfers between devices with their start and end apart: 109, of which 50 were waited for; matrix products, arithmetic and copies ran while one was open for 6% of the time, Pallas kernels for 30%

profile of v4, /device:TPU:0, one launch (start us, length us, event | category | flops | bytes accessed | tf_op | source)
XLA Modules:
  0.0 676.4 jit_solution(13429083454899585445)
XLA Ops:
  8.4 2.6 collective-permute-start.2
  13.5 2.9 collective-permute-start
  21.1 14.4 %collective-permute-done.own_ref = bf16[192,768]{1,0:T(8,128)(2,1)S(1)} collective-permute-done((bf16[192,768]{1,0:T(8,128)(2,1)S(1)}, bf16[192,768]{1,0:T(8,128)(2,1)S(1)}, u32[]{:S(2)}, u32[]{:S(2)}) %collective-permute-start) | collective-permute-done | bytes 294944 | tf_op jit(solution)/shard_map/ppermute | solution.py:47
  43.6 6.8 %collective-permute-done.1.other_ref = bf16[192,768]{1,0:T(8,128)(2,1)S(1)} collective-permute-done((bf16[192,768]{1,0:T(8,128)(2,1)S(1)}, bf16[192,768]{1,0:T(8,128)(2,1)S(1)}, u32[]{:S(2)}, u32[]{:S(2)}) %collective-permute-start.1) | collective-permute-done | bytes 294944 | tf_op jit(solution)/shard_map/ppermute | solution.py:827
  59.7 6.2 attend.1.refs_4_.refs_5_
  66.0 2.5 collective-permute-done.8.refs_5_
  73.4 6.0 collective-permute-done.14
  80.7 8.9 %hidden_before.1 = (f32[1024,768]{1,0:T(8,128)}, f32[1024,768]{1,0:T(8,128)}) custom-call(s32[3]{0:T(128)} %copy-done.72, bf16[512,768]{1,0:T(8,128)(2,1)} %refs_0_.1, bf16[512,768]{1,0:T(8,128)(2,1)} %copy-done.55, bf16[512,768]{1,0:T(8,128)(2,1)} %copy-done.56, bf16[512,768]{1,0:T(8,128)(2,1)} %copy-done.58, bf16[1024,384]{1,0:T(8,128)(2,1)} %attend.1.refs_4_.refs_5_, ...), custom_call_target="tpu_custom_call" | custom-call | flops 2415919104 | bytes 12582912 | tf_op jit(solution)/shard_map/hidden_before/pallas_call | solution.py:400
  89.7 6.1 collective-permute-done.10.refs_2_
  113.6 9.4 %hidden_after.1 = (f32[1024,768]{1,0:T(8,128)}, bf16[1024,768]{1,0:T(8,128)(2,1)}, bf16[1024,768]{1,0:T(8,128)(2,1)}, f32[1024,1]{1,0:T(8,128)}) custom-call(s32[3]{0:T(128)} %copy-done.72, f32[1024,768]{1,0:T(8,128)} %get-tuple-element.229.refs_0_, f32[1024,768]{1,0:T(8,128)} %get-tuple-element.230.refs_1_, ...), custom_call_target="tpu_custom_call" | custom-call | tf_op jit(solution)/shard_map/hidden_after/pallas_call | solution.py:422
  126.4 9.0 %expert_grads.9 = (bf16[1,1536,384]{2,1,0:T(8,128)(2,1)S(1)}, bf16[1,1536,384]{2,1,0:T(8,128)(2,1)S(1)}, bf16[8,1024,512]{2,1,0:T(8,128)(2,1)}, bf16[8,1024,256]{2,1,0:T(8,128)(2,1)S(1)}) custom-call(s32[17]{0:T(128)S(1)} %stack.224.order_ref, bf16[1024,768]{1,0:T(8,128)(2,1)S(1)} %copy-done.2, bf16[1024,768]{1,0:T(8,128)(2,1)S(1)} %copy-done.3, ...), custom_call_target="tpu_custom_call" | custom-call | tf_op jit(solution)/shard_map/expert_grads/pallas_call | solution.py:545
  137.3 8.8 %expert_grads.10 = (bf16[1,1536,384]{2,1,0:T(8,128)(2,1)S(1)}, bf16[1,1536,384]{2,1,0:T(8,128)(2,1)S(1)}, bf16[8,1024,512]{2,1,0:T(8,128)(2,1)}, bf16[8,1024,256]{2,1,0:T(8,128)(2,1)S(1)}) custom-call(s32[17]{0:T(128)S(1)} %stack.224.order_ref, bf16[1024,768]{1,0:T(8,128)(2,1)S(1)} %copy-done.2, ...), custom_call_target="tpu_custom_call", output_to_operand_aliasing={{2}: (18, {}), {3}: (19, {})} | custom-call | tf_op jit(solution)/shard_map/expert_grads/pallas_call | solution.py:545
  146.3 8.8 %expert_grads.11 = (bf16[1,1536,384]{2,1,0:T(8,128)(2,1)S(1)}, bf16[1,1536,384]{2,1,0:T(8,128)(2,1)S(1)}, bf16[8,1024,512]{2,1,0:T(8,128)(2,1)}, bf16[8,1024,256]{2,1,0:T(8,128)(2,1)S(1)}) custom-call(s32[17]{0:T(128)S(1)} %stack.224.order_ref, bf16[1024,768]{1,0:T(8,128)(2,1)S(1)} %copy-done.2, ...), custom_call_target="tpu_custom_call", output_to_operand_aliasing={{2}: (18, {}), {3}: (19, {})} | custom-call | tf_op jit(solution)/shard_map/expert_grads/pallas_call | solution.py:545
  155.6 2.5 collective-permute-start.20
  158.2 9.2 %expert_grads.12 = (bf16[1,1536,384]{2,1,0:T(8,128)(2,1)S(1)}, bf16[1,1536,384]{2,1,0:T(8,128)(2,1)S(1)}, bf16[8,1024,512]{2,1,0:T(8,128)(2,1)}, bf16[8,1024,256]{2,1,0:T(8,128)(2,1)S(1)}) custom-call(s32[17]{0:T(128)S(1)} %stack.224.order_ref, bf16[1024,768]{1,0:T(8,128)(2,1)S(1)} %copy-done.2, ...), custom_call_target="tpu_custom_call", output_to_operand_aliasing={{2}: (18, {}), {3}: (19, {})} | custom-call | tf_op jit(solution)/shard_map/expert_grads/pallas_call | solution.py:545
  172.4 8.8 %expert_grads.13 = (bf16[1,1536,384]{2,1,0:T(8,128)(2,1)S(1)}, bf16[1,1536,384]{2,1,0:T(8,128)(2,1)S(1)}, bf16[8,1024,512]{2,1,0:T(8,128)(2,1)}, bf16[8,1024,256]{2,1,0:T(8,128)(2,1)S(1)}) custom-call(s32[17]{0:T(128)S(1)} %stack.224.order_ref, bf16[1024,768]{1,0:T(8,128)(2,1)S(1)} %copy-done.2, ...), custom_call_target="tpu_custom_call", output_to_operand_aliasing={{2}: (18, {}), {3}: (19, {})} | custom-call | tf_op jit(solution)/shard_map/expert_grads/pallas_call | solution.py:545
  183.1 8.8 %expert_grads.14 = (bf16[1,1536,384]{2,1,0:T(8,128)(2,1)S(1)}, bf16[1,1536,384]{2,1,0:T(8,128)(2,1)S(1)}, bf16[8,1024,512]{2,1,0:T(8,128)(2,1)}, bf16[8,1024,256]{2,1,0:T(8,128)(2,1)S(1)}) custom-call(s32[17]{0:T(128)S(1)} %stack.224.order_ref, bf16[1024,768]{1,0:T(8,128)(2,1)S(1)} %copy-done.2, ...), custom_call_target="tpu_custom_call", output_to_operand_aliasing={{2}: (18, {}), {3}: (19, {})} | custom-call | tf_op jit(solution)/shard_map/expert_grads/pallas_call | solution.py:545
  192.0 2.8 collective-permute-done.23
  194.8 2.6 add_convert_fusion.10
  200.2 9.0 %expert_grads.15 = (bf16[1,1536,384]{2,1,0:T(8,128)(2,1)S(1)}, bf16[1,1536,384]{2,1,0:T(8,128)(2,1)S(1)}, bf16[8,1024,512]{2,1,0:T(8,128)(2,1)}, bf16[8,1024,256]{2,1,0:T(8,128)(2,1)S(1)}) custom-call(s32[17]{0:T(128)S(1)} %stack.224.order_ref, bf16[1024,768]{1,0:T(8,128)(2,1)S(1)} %copy-done.2, ...), custom_call_target="tpu_custom_call", output_to_operand_aliasing={{2}: (18, {}), {3}: (19, {})} | custom-call | tf_op jit(solution)/shard_map/expert_grads/pallas_call | solution.py:545
  209.2 2.4 add_convert_fusion.9
  212.3 8.9 %expert_grads.16 = (bf16[1,1536,384]{2,1,0:T(8,128)(2,1)S(1)}, bf16[1,1536,384]{2,1,0:T(8,128)(2,1)S(1)}, bf16[8,1024,512]{2,1,0:T(8,128)(2,1)}, bf16[8,1024,256]{2,1,0:T(8,128)(2,1)S(1)}) custom-call(s32[17]{0:T(128)S(1)} %stack.224.order_ref, bf16[1024,768]{1,0:T(8,128)(2,1)S(1)} %copy-done.2, ...), custom_call_target="tpu_custom_call", output_to_operand_aliasing={{2}: (18, {}), {3}: (19, {})} | custom-call | tf_op jit(solution)/shard_map/expert_grads/pallas_call | solution.py:545
  224.2 3.1 add_convert_fusion.8
  228.8 7.7 %expert_grads.17 = (bf16[1,1536,384]{2,1,0:T(8,128)(2,1)S(1)}, bf16[1,1536,384]{2,1,0:T(8,128)(2,1)S(1)}, bf16[1,1024,512]{2,1,0:T(8,128)(2,1)S(1)}, bf16[1,1024,256]{2,1,0:T(8,128)(2,1)S(1)}) custom-call(s32[17]{0:T(128)S(1)} %stack.224.order_ref, bf16[1024,768]{1,0:T(8,128)(2,1)S(1)} %copy-done.2, bf16[1024,768]{1,0:T(8,128)(2,1)S(1)} %copy-done.4, ...), custom_call_target="tpu_custom_call" | custom-call | tf_op jit(solution)/shard_map/expert_grads/pallas_call | solution.py:545
  236.5 3.5 add_convert_fusion.7
  240.7 12.6 %mix.4 = bf16[1024,768]{1,0:T(8,128)(2,1)S(1)} custom-call(s32[17]{0:T(128)S(1)} %stack.224.order_ref, bf16[8,1024,512]{2,1,0:T(8,128)(2,1)} %get-tuple-element.272.refs_0_, bf16[1,1024,512]{2,1,0:T(8,128)(2,1)S(1)} %get-tuple-element.279.refs_1_, ...), custom_call_target="tpu_custom_call" | custom-call | tf_op jit(solution)/shard_map/mix/pallas_call | solution.py:616
  256.1 12.5 %mix.5 = f32[1024,768]{1,0:T(8,128)S(1)} custom-call(s32[17]{0:T(128)S(1)} %stack.224.order_ref, bf16[8,1024,512]{2,1,0:T(8,128)(2,1)} %get-tuple-element.272.refs_0_, bf16[1,1024,512]{2,1,0:T(8,128)(2,1)S(1)} %get-tuple-element.279.refs_1_, bf16[16,768,256]{2,1,0:T(8,128)(2,1)} %refs_16_.1, bf16[16,768,256]{2,1,0:T(8,128)(2,1)} %refs_17_.1, ...), custom_call_target="tpu_custom_call" | custom-call | tf_op jit(solution)/shard_map/mix/pallas_call | solution.py:616
  274.7 23.5 %collective-permute-done.31 = bf16[1,1536,384]{2,1,0:T(8,128)(2,1)S(1)} collective-permute-done((bf16[1,1536,384]{2,1,0:T(8,128)(2,1)S(1)}, bf16[1,1536,384]{2,1,0:T(8,128)(2,1)S(1)}, u32[]{:S(2)}, u32[]{:S(2)}) %collective-permute-start.31) | collective-permute-done | bytes 1179680 | tf_op jit(solution)/shard_map/ppermute | solution.py:782
  301.0 8.5 %collective-permute-done.49 = bf16[1024,768]{1,0:T(8,128)(2,1)S(1)} collective-permute-done((bf16[1024,768]{1,0:T(8,128)(2,1)S(1)}, bf16[1024,768]{1,0:T(8,128)(2,1)S(1)}, u32[]{:S(2)}, u32[]{:S(2)}) %collective-permute-start.49) | collective-permute-done | bytes 1572896 | tf_op jit(solution)/shard_map/ppermute | solution.py:47
  311.6 15.6 %collective-permute-done.33 = bf16[1,1536,384]{2,1,0:T(8,128)(2,1)S(1)} collective-permute-done((bf16[1,1536,384]{2,1,0:T(8,128)(2,1)S(1)}, bf16[1,1536,384]{2,1,0:T(8,128)(2,1)S(1)}, u32[]{:S(2)}, u32[]{:S(2)}) %collective-permute-start.33) | collective-permute-done | bytes 1179680 | tf_op jit(solution)/shard_map/ppermute | solution.py:782
  331.4 2.6 fusion.52
  335.4 3.3 unpack.16
  338.7 7.0 %collective-permute-done.35.refs_0_ = bf16[1,768,384]{2,1,0:T(8,128)(2,1)} collective-permute-done((bf16[1,768,384]{2,1,0:T(8,128)(2,1)}, bf16[1,768,384]{2,1,0:T(8,128)(2,1)}, u32[]{:S(2)}, u32[]{:S(2)}) %collective-permute-start.35) | collective-permute-done | bytes 589856 | tf_op jit(solution)/shard_map/ppermute | solution.py:782
  347.7 3.3 unpack.17
  351.1 10.1 %collective-permute-done.37.refs_0_ = bf16[1,768,384]{2,1,0:T(8,128)(2,1)} collective-permute-done((bf16[1,768,384]{2,1,0:T(8,128)(2,1)}, bf16[1,768,384]{2,1,0:T(8,128)(2,1)}, u32[]{:S(2)}, u32[]{:S(2)}) %collective-permute-start.37) | collective-permute-done | bytes 589856 | tf_op jit(solution)/shard_map/ppermute | solution.py:782
  371.4 3.3 unpack.18
  379.3 12.2 %attend_back.1.refs_4_ = bf16[1024,640]{1,0:T(8,128)(2,1)S(1)} custom-call(s32[3]{0:T(128)S(1)} %copy-done.73, bf16[512,640]{1,0:T(8,128)(2,1)S(1)} %copy-done.32, bf16[512,640]{1,0:T(8,128)(2,1)S(1)} %copy-done.34, bf16[1024,768]{1,0:T(8,128)(2,1)} %copy-done.8, bf16[1024,768]{1,0:T(8,128)(2,1)} %copy-done.18, bf16[768,768]{1,0:T(8,128)(2,1)} %out_ref.1, ...), custom_call_target="tpu_custom_call" | custom-call | tf_op jit(solution)/shard_map/attend_back/pallas_call | solution.py:165
  395.3 9.4 %late_grads.1 = (bf16[2,768,896]{2,1,0:T(8,128)(2,1)S(1)}, bf16[2,768,896]{2,1,0:T(8,128)(2,1)}) custom-call(s32[3]{0:T(128)S(1)} %copy-done.73, bf16[512,768]{1,0:T(8,128)(2,1)S(1)} %copy-done.61, bf16[512,768]{1,0:T(8,128)(2,1)S(1)} %copy-done.63, bf16[512,768]{1,0:T(8,128)(2,1)S(1)} %copy-done.65, bf16[512,768]{1,0:T(8,128)(2,1)S(1)} %copy-done.67, ...), custom_call_target="tpu_custom_call" | custom-call | tf_op jit(solution)/shard_map/late_grads/pallas_call | solution.py:216
  408.8 3.3 unpack.19
  414.1 2.6 collective-permute-done.67
  417.9 3.6 unpack.20
  423.5 7.2 %mix.6 = bf16[1024,768]{1,0:T(8,128)(2,1)S(1)} custom-call(s32[17]{0:T(128)S(1)} %stack.224.order_ref, bf16[8,1024,256]{2,1,0:T(8,128)(2,1)} %copy-done, bf16[1,1024,256]{2,1,0:T(8,128)(2,1)S(1)} %copy-done.36, bf16[16,256,768]{2,1,0:T(8,128)(2,1)} %collective-permute-done.18.refs_10_.refs_16_.refs_2_.refs_3_.refs_4_.refs_5_.refs_6_.refs_7_.refs_8_.refs_9_, ...), custom_call_target="tpu_custom_call" | custom-call | tf_op jit(solution)/shard_map/mix/pallas_call | solution.py:616
  433.2 3.6 collective-permute-done.68
  441.4 7.3 %mix.7 = f32[1024,768]{1,0:T(8,128)S(1)} custom-call(s32[17]{0:T(128)S(1)} %stack.224.order_ref, bf16[8,1024,256]{2,1,0:T(8,128)(2,1)} %copy-done, bf16[1,1024,256]{2,1,0:T(8,128)(2,1)S(1)} %copy-done.36, bf16[16,256,768]{2,1,0:T(8,128)(2,1)} %refs_9_.19, bf16[16,256,768]{2,1,0:T(8,128)(2,1)} %refs_9_.19, bf16[16,256,768]{2,1,0:T(8,128)(2,1)} %refs_9_.19, ...), custom_call_target="tpu_custom_call" | custom-call | tf_op jit(solution)/shard_map/mix/pallas_call | solution.py:616
  457.0 6.9 %collective-permute-done.80 = bf16[2,96,896]{2,1,0:T(8,128)(2,1)S(1)} collective-permute-done((bf16[2,96,896]{2,1,0:T(8,128)(2,1)S(1)}, bf16[2,96,896]{2,1,0:T(8,128)(2,1)S(1)}, u32[]{:S(2)}, u32[]{:S(2)}) %collective-permute-start.80) | collective-permute-done | bytes 344096 | tf_op jit(solution)/shard_map/ppermute | solution.py:782
  468.7 5.3 collective-permute-done.58.refs_1_
  480.7 7.0 %collective-permute-done.53.refs_0_ = bf16[1,768,384]{2,1,0:T(8,128)(2,1)S(1)} collective-permute-done((bf16[1,768,384]{2,1,0:T(8,128)(2,1)S(1)}, bf16[1,768,384]{2,1,0:T(8,128)(2,1)S(1)}, u32[]{:S(2)}, u32[]{:S(2)}) %collective-permute-start.53) | collective-permute-done | bytes 589856 | tf_op jit(solution)/shard_map/ppermute | solution.py:782
  489.8 4.3 collective-permute-done.81
  498.8 15.1 %collective-permute-done.82 = bf16[2,96,896]{2,1,0:T(8,128)(2,1)S(1)} collective-permute-done((bf16[2,96,896]{2,1,0:T(8,128)(2,1)S(1)}, bf16[2,96,896]{2,1,0:T(8,128)(2,1)S(1)}, u32[]{:S(2)}, u32[]{:S(2)}) %collective-permute-start.82) | collective-permute-done | bytes 344096 | tf_op jit(solution)/shard_map/ppermute | solution.py:782
  521.9 2.8 collective-permute-done.83
  525.8 5.6 collective-permute-done.76.refs_0_
  531.4 6.0 collective-permute-done.77.refs_1_
  539.0 2.4 collective-permute-done.84
  549.1 12.6 %collective-permute-done.47 = bf16[512,768]{1,0:T(8,128)(2,1)S(1)} collective-permute-done((bf16[512,768]{1,0:T(8,128)(2,1)S(1)}, bf16[512,768]{1,0:T(8,128)(2,1)S(1)}, u32[]{:S(2)}, u32[]{:S(2)}) %collective-permute-start.47) | collective-permute-done | bytes 786464 | tf_op jit(solution)/shard_map/ppermute | solution.py:47
  573.1 9.6 %collective-permute-done.90.refs_0_ = bf16[1,768,384]{2,1,0:T(8,128)(2,1)S(1)} collective-permute-done((bf16[1,768,384]{2,1,0:T(8,128)(2,1)S(1)}, bf16[1,768,384]{2,1,0:T(8,128)(2,1)S(1)}, u32[]{:S(2)}, u32[]{:S(2)}) %collective-permute-start.90) | collective-permute-done | bytes 589856 | tf_op jit(solution)/shard_map/ppermute | solution.py:782
  585.2 4.9 collective-permute-done.89
  594.8 15.4 %collective-permute-done.63 = f32[2,768]{1,0:T(2,128)S(1)} collective-permute-done((f32[2,768]{1,0:T(2,128)S(1)}, f32[2,768]{1,0:T(2,128)S(1)}, u32[]{:S(2)}, u32[]{:S(2)}) %collective-permute-start.63) | collective-permute-done | bytes 6176 | tf_op jit(solution)/shard_map/ppermute | solution.py:1117
  615.1 4.6 collective-permute-done.65
  630.5 4.5 collective-permute-done.93
  637.1 14.8 %collective-permute-done.96 = bf16[2,96,896]{2,1,0:T(8,128)(2,1)S(1)} collective-permute-done((bf16[2,96,896]{2,1,0:T(8,128)(2,1)S(1)}, bf16[2,96,896]{2,1,0:T(8,128)(2,1)S(1)}, u32[]{:S(2)}, u32[]{:S(2)}) %collective-permute-start.96) | collective-permute-done | bytes 344096 | tf_op jit(solution)/shard_map/ppermute | solution.py:782
  656.1 3.2 collective-permute-done.97
  659.3 2.5 collective-permute-start.100
  666.6 4.4 collective-permute-done.108
  671.1 4.8 unpack_late.1
  (477 shorter events, 202.5 us)
Async XLA Ops:
  0.6 38.0 %collective-permute-start.16 = (bf16[16,768,256]{2,1,0:T(8,128)(2,1)}, bf16[16,768,256]{2,1,0:T(8,128)(2,1)}, u32[]{:S(2)}, u32[]{:S(2)}) collective-permute-start(bf16[16,768,256]{2,1,0:T(8,128)(2,1)} %refs_16_.1), channel_id=1, source_target_pairs={{0,1},{1,0},{2,3},{3,2},{4,5},{5,4},{6,7},{7,6},{8,9},{9,8},{10,11... | collective-permute-start | bytes 18874376 | tf_op jit(solution)/shard_map/ppermute | solution.py:47
  8.4 27.1 %collective-permute-start.2 = (bf16[512,768]{1,0:T(8,128)(2,1)S(1)}, bf16[512,768]{1,0:T(8,128)(2,1)S(1)}, u32[]{:S(2)}, u32[]{:S(2)}) collective-permute-start(bf16[512,768]{1,0:T(8,128)(2,1)S(1)} %copy-done.16), channel_id=1, source_target_pairs={{0,2},{2,0},{1,3},{3,1},{4,6},{6,4},{5,7},{7,5},{8,10},{10,8},{9,1... | collective-permute-start | bytes 2359304 | tf_op jit(solution)/shard_map/ppermute | solution.py:47
  13.5 22.0 %collective-permute-start = (bf16[192,768]{1,0:T(8,128)(2,1)S(1)}, bf16[192,768]{1,0:T(8,128)(2,1)S(1)}, u32[]{:S(2)}, u32[]{:S(2)}) collective-permute-start(bf16[192,768]{1,0:T(8,128)(2,1)S(1)} %get-tuple-element.220), channel_id=1, source_target_pairs={{0,2},{2,0},{1,3},{3,1},{4,6},{6,4},{5,7},{7,5},{8,10},{10,8},{9,1... | collective-permute-start | bytes 884744 | tf_op jit(solution)/shard_map/ppermute | solution.py:47
  38.6 29.8 %collective-permute-start.17 = (bf16[16,768,256]{2,1,0:T(8,128)(2,1)}, bf16[16,768,256]{2,1,0:T(8,128)(2,1)}, u32[]{:S(2)}, u32[]{:S(2)}) collective-permute-start(bf16[16,768,256]{2,1,0:T(8,128)(2,1)} %refs_17_.1), channel_id=1, source_target_pairs={{0,1},{1,0},{2,3},{3,2},{4,5},{5,4},{6,7},{7,6},{8,9},{9,8},{10,11... | collective-permute-start | bytes 18874376 | tf_op jit(solution)/shard_map/ppermute | solution.py:47
  68.5 54.6 %collective-permute-start.18 = (bf16[16,256,768]{2,1,0:T(8,128)(2,1)}, bf16[16,256,768]{2,1,0:T(8,128)(2,1)}, u32[]{:S(2)}, u32[]{:S(2)}) collective-permute-start(bf16[16,256,768]{2,1,0:T(8,128)(2,1)} %refs_9_.19), channel_id=1, source_target_pairs={{0,1},{1,0},{2,3},{3,2},{4,5},{5,4},{6,7},{7,6},{8,9},{9,8},{10,11... | collective-permute-start | bytes 18874376 | tf_op jit(solution)/shard_map/ppermute | solution.py:47
  71.3 24.5 %collective-permute-start.10 = (bf16[1024,384]{1,0:T(8,128)(2,1)}, bf16[1024,384]{1,0:T(8,128)(2,1)}, u32[]{:S(2)}, u32[]{:S(2)}) collective-permute-start(bf16[1024,384]{1,0:T(8,128)(2,1)} %attend.1.refs_4_.refs_5_), channel_id=1, source_target_pairs={{0,2},{2,0},{1,3},{3,1},{4,6},{6,4},{5,7},{7,5},{8,10},{10,8},{9,1... | collective-permute-start | bytes 2359304 | tf_op jit(solution)/shard_map/ppermute | solution.py:47
  71.6 24.2 %collective-permute-start.12 = (bf16[384,768]{1,0:T(8,128)(2,1)}, bf16[384,768]{1,0:T(8,128)(2,1)}, u32[]{:S(2)}, u32[]{:S(2)}) collective-permute-start(bf16[384,768]{1,0:T(8,128)(2,1)} %join.3.own_ref), channel_id=1, source_target_pairs={{0,8},{4,12},{8,0},{12,4},{16,24},{20,28},{24,16},{28,20},{1,9},{5... | collective-permute-start | bytes 1769480 | tf_op jit(solution)/shard_map/ppermute | solution.py:827
  80.6 42.4 %collective-permute-start.15 = (bf16[1024,768]{1,0:T(8,128)(2,1)S(1)}, bf16[1024,768]{1,0:T(8,128)(2,1)S(1)}, u32[]{:S(2)}, u32[]{:S(2)}) collective-permute-start(bf16[1024,768]{1,0:T(8,128)(2,1)S(1)} %join.5.refs_2_), channel_id=1, source_target_pairs={{0,1},{1,0},{2,3},{3,2},{4,5},{5,4},{6,7},{7,6},{8,9},{9,8},{10,11... | collective-permute-start | bytes 4718600 | tf_op jit(solution)/shard_map/ppermute | solution.py:47
  135.5 19.9 %collective-permute-start.19 = (bf16[1,1536,384]{2,1,0:T(8,128)(2,1)S(1)}, bf16[1,1536,384]{2,1,0:T(8,128)(2,1)S(1)}, u32[]{:S(2)}, u32[]{:S(2)}) collective-permute-start(bf16[1,1536,384]{2,1,0:T(8,128)(2,1)S(1)} %get-tuple-element.239), channel_id=1, source_target_pairs={{0,8},{8,16},{16,24},{24,28},{28,20},{20,12},{12,4},{4,0},{9,1},{1... | collective-permute-start | bytes 3538952 | tf_op jit(solution)/shard_map/ppermute | solution.py:782
  146.1 23.4 %collective-permute-start.21 = (bf16[1,1536,384]{2,1,0:T(8,128)(2,1)S(1)}, bf16[1,1536,384]{2,1,0:T(8,128)(2,1)S(1)}, u32[]{:S(2)}, u32[]{:S(2)}) collective-permute-start(bf16[1,1536,384]{2,1,0:T(8,128)(2,1)S(1)} %get-tuple-element.249), channel_id=1, source_target_pairs={{8,0},{16,8},{24,16},{28,24},{20,28},{12,20},{4,12},{0,4},{1,9},{9... | collective-permute-start | bytes 3538952 | tf_op jit(solution)/shard_map/ppermute | solution.py:782
  155.6 25.7 %collective-permute-start.20 = (bf16[1,1536,384]{2,1,0:T(8,128)(2,1)S(1)}, bf16[1,1536,384]{2,1,0:T(8,128)(2,1)S(1)}, u32[]{:S(2)}, u32[]{:S(2)}) collective-permute-start(bf16[1,1536,384]{2,1,0:T(8,128)(2,1)S(1)} %add_convert_fusion.13), channel_id=1, source_target_pairs={{0,8},{8,16},{16,24},{24,28},{28,20},{20,12},{12,4},{4,0},{9,1},{1... | collective-permute-start | bytes 3538952 | tf_op jit(solution)/shard_map/ppermute | solution.py:782
  170.8 24.0 %collective-permute-start.23 = (bf16[1,1536,384]{2,1,0:T(8,128)(2,1)}, bf16[1,1536,384]{2,1,0:T(8,128)(2,1)}, u32[]{:S(2)}, u32[]{:S(2)}) collective-permute-start(bf16[1,1536,384]{2,1,0:T(8,128)(2,1)} %add_convert_fusion.12), channel_id=1, source_target_pairs={{8,0},{16,8},{24,16},{28,24},{20,28},{12,20},{4,12},{0,4},{1,9},{9... | collective-permute-start | bytes 3538952 | tf_op jit(solution)/shard_map/ppermute | solution.py:782
  181.6 27.6 %collective-permute-start.22 = (bf16[1,1536,384]{2,1,0:T(8,128)(2,1)S(1)}, bf16[1,1536,384]{2,1,0:T(8,128)(2,1)}, u32[]{:S(2)}, u32[]{:S(2)}) collective-permute-start(bf16[1,1536,384]{2,1,0:T(8,128)(2,1)S(1)} %add_convert_fusion.11), channel_id=1, source_target_pairs={{0,8},{8,16},{16,24},{24,28},{28,20},{20,12},{12,4},{4,0},{9,1},{1... | collective-permute-start | bytes 3538952 | tf_op jit(solution)/shard_map/ppermute | solution.py:782
  197.3 26.9 %collective-permute-start.25 = (bf16[1,1536,384]{2,1,0:T(8,128)(2,1)}, bf16[1,1536,384]{2,1,0:T(8,128)(2,1)}, u32[]{:S(2)}, u32[]{:S(2)}) collective-permute-start(bf16[1,1536,384]{2,1,0:T(8,128)(2,1)} %add_convert_fusion.10), channel_id=1, source_target_pairs={{8,0},{16,8},{24,16},{28,24},{20,28},{12,20},{4,12},{0,4},{1,9},{9... | collective-permute-start | bytes 3538952 | tf_op jit(solution)/shard_map/ppermute | solution.py:782
  199.6 29.1 %collective-permute-start.26 = (bf16[1,768,512]{2,1,0:T(8,128)(2,1)S(1)}, bf16[1,768,512]{2,1,0:T(8,128)(2,1)S(1)}, u32[]{:S(2)}, u32[]{:S(2)}) collective-permute-start(bf16[1,768,512]{2,1,0:T(8,128)(2,1)S(1)} %bitcast.209), channel_id=1, source_target_pairs={{0,1},{1,0},{2,3},{3,2},{4,5},{5,4},{6,7},{7,6},{8,9},{9,8},{10,11... | collective-permute-start | bytes 2359304 | tf_op jit(solution)/shard_map/ppermute | solution.py:47
  199.6 29.1 %collective-permute-start.27 = (bf16[1,768,512]{2,1,0:T(8,128)(2,1)S(1)}, bf16[1,768,512]{2,1,0:T(8,128)(2,1)S(1)}, u32[]{:S(2)}, u32[]{:S(2)}) collective-permute-start(bf16[1,768,512]{2,1,0:T(8,128)(2,1)S(1)} %bitcast.214), channel_id=1, source_target_pairs={{0,1},{1,0},{2,3},{3,2},{4,5},{5,4},{6,7},{7,6},{8,9},{9,8},{10,11... | collective-permute-start | bytes 2359304 | tf_op jit(solution)/shard_map/ppermute | solution.py:47
  200.1 28.6 %collective-permute-start.28 = (bf16[1,512,768]{2,1,0:T(8,128)(2,1)S(1)}, bf16[1,512,768]{2,1,0:T(8,128)(2,1)S(1)}, u32[]{:S(2)}, u32[]{:S(2)}) collective-permute-start(bf16[1,512,768]{2,1,0:T(8,128)(2,1)S(1)} %bitcast.219), channel_id=1, source_target_pairs={{0,1},{1,0},{2,3},{3,2},{4,5},{5,4},{6,7},{7,6},{8,9},{9,8},{10,11... | collective-permute-start | bytes 2359304 | tf_op jit(solution)/shard_map/ppermute | solution.py:47
  211.6 24.9 %collective-permute-start.24 = (bf16[1,1536,384]{2,1,0:T(8,128)(2,1)S(1)}, bf16[1,1536,384]{2,1,0:T(8,128)(2,1)}, u32[]{:S(2)}, u32[]{:S(2)}) collective-permute-start(bf16[1,1536,384]{2,1,0:T(8,128)(2,1)S(1)} %add_convert_fusion.9), channel_id=1, source_target_pairs={{0,8},{8,16},{16,24},{24,28},{28,20},{20,12},{12,4},{4,0},{9,1},{1... | collective-permute-start | bytes 3538952 | tf_op jit(solution)/shard_map/ppermute | solution.py:782
  227.3 26.0 %collective-permute-start.30 = (bf16[1,1536,384]{2,1,0:T(8,128)(2,1)}, bf16[1,1536,384]{2,1,0:T(8,128)(2,1)S(1)}, u32[]{:S(2)}, u32[]{:S(2)}) collective-permute-start(bf16[1,1536,384]{2,1,0:T(8,128)(2,1)} %add_convert_fusion.8), channel_id=1, source_target_pairs={{8,0},{16,8},{24,16},{28,24},{20,28},{12,20},{4,12},{0,4},{1,9},{9... | collective-permute-start | bytes 3538952 | tf_op jit(solution)/shard_map/ppermute | solution.py:782
  240.0 28.6 %collective-permute-start.29 = (bf16[1,1536,384]{2,1,0:T(8,128)(2,1)}, bf16[1,1536,384]{2,1,0:T(8,128)(2,1)}, u32[]{:S(2)}, u32[]{:S(2)}) collective-permute-start(bf16[1,1536,384]{2,1,0:T(8,128)(2,1)} %add_convert_fusion.7), channel_id=1, source_target_pairs={{0,8},{8,16},{16,24},{24,28},{28,20},{20,12},{12,4},{4,0},{9,1},{1... | collective-permute-start | bytes 3538952 | tf_op jit(solution)/shard_map/ppermute | solution.py:782
  270.3 27.8 %collective-permute-start.31 = (bf16[1,1536,384]{2,1,0:T(8,128)(2,1)S(1)}, bf16[1,1536,384]{2,1,0:T(8,128)(2,1)S(1)}, u32[]{:S(2)}, u32[]{:S(2)}) collective-permute-start(bf16[1,1536,384]{2,1,0:T(8,128)(2,1)S(1)} %add_convert_fusion.5), channel_id=1, source_target_pairs={{0,8},{8,16},{16,24},{24,28},{28,20},{20,12},{12,4},{4,0},{9,1},{1... | collective-permute-start | bytes 3538952 | tf_op jit(solution)/shard_map/ppermute | solution.py:782
  271.5 27.7 %collective-permute-start.34 = (bf16[1,1536,384]{2,1,0:T(8,128)(2,1)S(1)}, bf16[1,1536,384]{2,1,0:T(8,128)(2,1)S(1)}, u32[]{:S(2)}, u32[]{:S(2)}) collective-permute-start(bf16[1,1536,384]{2,1,0:T(8,128)(2,1)S(1)} %add_convert_fusion.4), channel_id=1, source_target_pairs={{8,0},{16,8},{24,16},{28,24},{20,28},{12,20},{4,12},{0,4},{1,9},{9... | collective-permute-start | bytes 3538952 | tf_op jit(solution)/shard_map/ppermute | solution.py:782
  273.3 36.2 %collective-permute-start.49 = (bf16[1024,768]{1,0:T(8,128)(2,1)S(1)}, bf16[1024,768]{1,0:T(8,128)(2,1)S(1)}, u32[]{:S(2)}, u32[]{:S(2)}) collective-permute-start(bf16[1024,768]{1,0:T(8,128)(2,1)S(1)} %fusion), channel_id=1, source_target_pairs={{0,2},{2,0},{1,3},{3,1},{4,6},{6,4},{5,7},{7,5},{8,10},{10,8},{9,1... | collective-permute-start | bytes 4718600 | tf_op jit(solution)/shard_map/ppermute | solution.py:47
  298.5 28.7 %collective-permute-start.33 = (bf16[1,1536,384]{2,1,0:T(8,128)(2,1)S(1)}, bf16[1,1536,384]{2,1,0:T(8,128)(2,1)S(1)}, u32[]{:S(2)}, u32[]{:S(2)}) collective-permute-start(bf16[1,1536,384]{2,1,0:T(8,128)(2,1)S(1)} %add_convert_fusion.3), channel_id=1, source_target_pairs={{0,8},{8,16},{16,24},{24,28},{28,20},{20,12},{12,4},{4,0},{9,1},{1... | collective-permute-start | bytes 3538952 | tf_op jit(solution)/shard_map/ppermute | solution.py:782
  299.5 28.1 %collective-permute-start.36 = (bf16[1,1536,384]{2,1,0:T(8,128)(2,1)S(1)}, bf16[1,1536,384]{2,1,0:T(8,128)(2,1)S(1)}, u32[]{:S(2)}, u32[]{:S(2)}) collective-permute-start(bf16[1,1536,384]{2,1,0:T(8,128)(2,1)S(1)} %add_convert_fusion.2), channel_id=1, source_target_pairs={{8,0},{16,8},{24,16},{28,24},{20,28},{12,20},{4,12},{0,4},{1,9},{9... | collective-permute-start | bytes 3538952 | tf_op jit(solution)/shard_map/ppermute | solution.py:782
  334.0 44.1 %collective-permute-start.51 = (bf16[1024,768]{1,0:T(8,128)(2,1)S(1)}, bf16[1024,768]{1,0:T(8,128)(2,1)S(1)}, u32[]{:S(2)}, u32[]{:S(2)}) collective-permute-start(bf16[1024,768]{1,0:T(8,128)(2,1)S(1)} %get-tuple-element.434.grad_ref.refs_6_), channel_id=1, source_target_pairs={{0,1},{1,0},{2,3},{3,2},{4,5},{5,4},{6,7},{7,6},{8,9},{9,8},{10,11... | collective-permute-start | bytes 4718600 | tf_op jit(solution)/shard_map/ppermute | solution.py:47
  376.0 36.1 %collective-permute-start.41 = (bf16[1,768,384]{2,1,0:T(8,128)(2,1)}, bf16[1,768,384]{2,1,0:T(8,128)(2,1)}, u32[]{:S(2)}, u32[]{:S(2)}) collective-permute-start(bf16[1,768,384]{2,1,0:T(8,128)(2,1)} %collective-permute-done.39.refs_0_), channel_id=1, source_target_pairs={{0,8},{8,16},{16,24},{24,28},{28,20},{20,12},{12,4},{4,0},{9,1},{1... | collective-permute-start | bytes 1769480 | tf_op jit(solution)/shard_map/ppermute | solution.py:782
  376.9 36.1 %collective-permute-start.44 = (bf16[1,768,384]{2,1,0:T(8,128)(2,1)}, bf16[1,768,384]{2,1,0:T(8,128)(2,1)}, u32[]{:S(2)}, u32[]{:S(2)}) collective-permute-start(bf16[1,768,384]{2,1,0:T(8,128)(2,1)} %collective-permute-done.42.refs_1_), channel_id=1, source_target_pairs={{8,0},{16,8},{24,16},{28,24},{20,28},{12,20},{4,12},{0,4},{1,9},{9... | collective-permute-start | bytes 1769480 | tf_op jit(solution)/shard_map/ppermute | solution.py:782
  412.1 18.7 %collective-permute-start.43 = (bf16[1,768,384]{2,1,0:T(8,128)(2,1)}, bf16[1,768,384]{2,1,0:T(8,128)(2,1)S(1)}, u32[]{:S(2)}, u32[]{:S(2)}) collective-permute-start(bf16[1,768,384]{2,1,0:T(8,128)(2,1)} %collective-permute-done.41.refs_0_), channel_id=1, source_target_pairs={{0,8},{8,16},{16,24},{24,28},{28,20},{20,12},{12,4},{4,0},{9,1},{1... | collective-permute-start | bytes 1769480 | tf_op jit(solution)/shard_map/ppermute | solution.py:782
  413.0 18.2 %collective-permute-start.45 = (bf16[1,768,384]{2,1,0:T(8,128)(2,1)}, bf16[1,768,384]{2,1,0:T(8,128)(2,1)S(1)}, u32[]{:S(2)}, u32[]{:S(2)}) collective-permute-start(bf16[1,768,384]{2,1,0:T(8,128)(2,1)} %collective-permute-done.44.refs_1_), channel_id=1, source_target_pairs={{8,0},{16,8},{24,16},{28,24},{20,28},{12,20},{4,12},{0,4},{1,9},{9... | collective-permute-start | bytes 1769480 | tf_op jit(solution)/shard_map/ppermute | solution.py:782
  416.9 19.9 %collective-permute-start.68 = (bf16[2,96,896]{2,1,0:T(8,128)(2,1)S(1)}, bf16[2,96,896]{2,1,0:T(8,128)(2,1)S(1)}, u32[]{:S(2)}, u32[]{:S(2)}) collective-permute-start(bf16[2,96,896]{2,1,0:T(8,128)(2,1)S(1)} %fusion.27), channel_id=1, source_target_pairs={{0,8},{8,16},{16,24},{24,28},{28,20},{20,12},{12,4},{4,0},{9,1},{1... | collective-permute-start | bytes 1032200 | tf_op jit(solution)/shard_map/ppermute | solution.py:782
  422.4 26.4 %collective-permute-start.79 = (bf16[2,96,896]{2,1,0:T(8,128)(2,1)}, bf16[2,96,896]{2,1,0:T(8,128)(2,1)}, u32[]{:S(2)}, u32[]{:S(2)}) collective-permute-start(bf16[2,96,896]{2,1,0:T(8,128)(2,1)} %fusion.20), channel_id=1, source_target_pairs={{8,0},{16,8},{24,16},{28,24},{20,28},{12,20},{4,12},{0,4},{1,9},{9... | collective-permute-start | bytes 1032200 | tf_op jit(solution)/shard_map/ppermute | solution.py:782
  431.2 18.1 %collective-permute-start.55 = (bf16[1,768,384]{2,1,0:T(8,128)(2,1)S(1)}, bf16[1,768,384]{2,1,0:T(8,128)(2,1)S(1)}, u32[]{:S(2)}, u32[]{:S(2)}) collective-permute-start(bf16[1,768,384]{2,1,0:T(8,128)(2,1)S(1)} %collective-permute-done.43.refs_0_), channel_id=1, source_target_pairs={{0,8},{8,16},{16,24},{24,28},{28,20},{20,12},{12,4},{4,0},{9,1},{1... | collective-permute-start | bytes 1769480 | tf_op jit(solution)/shard_map/ppermute | solution.py:782
  431.7 21.1 %collective-permute-start.57 = (bf16[1,768,384]{2,1,0:T(8,128)(2,1)S(1)}, bf16[1,768,384]{2,1,0:T(8,128)(2,1)S(1)}, u32[]{:S(2)}, u32[]{:S(2)}) collective-permute-start(bf16[1,768,384]{2,1,0:T(8,128)(2,1)S(1)} %collective-permute-done.45.refs_1_), channel_id=1, source_target_pairs={{8,0},{16,8},{24,16},{28,24},{20,28},{12,20},{4,12},{0,4},{1,9},{9... | collective-permute-start | bytes 1769480 | tf_op jit(solution)/shard_map/ppermute | solution.py:782
  448.7 17.8 %collective-permute-start.54 = (bf16[1,768,384]{2,1,0:T(8,128)(2,1)S(1)}, bf16[1,768,384]{2,1,0:T(8,128)(2,1)S(1)}, u32[]{:S(2)}, u32[]{:S(2)}) collective-permute-start(bf16[1,768,384]{2,1,0:T(8,128)(2,1)S(1)} %copy-done.81), channel_id=1, source_target_pairs={{0,1},{1,0},{2,3},{3,2},{4,5},{5,4},{6,7},{7,6},{8,9},{9,8},{10,11... | collective-permute-start | bytes 1769480 | tf_op jit(solution)/shard_map/ppermute | solution.py:47
  449.3 47.1 %collective-permute-start.46 = (bf16[1024,768]{1,0:T(8,128)(2,1)S(1)}, bf16[1024,768]{1,0:T(8,128)(2,1)S(1)}, u32[]{:S(2)}, u32[]{:S(2)}) collective-permute-start(bf16[1024,768]{1,0:T(8,128)(2,1)S(1)} %mix.6), channel_id=1, source_target_pairs={{0,1},{1,0},{2,3},{3,2},{4,5},{5,4},{6,7},{7,6},{8,9},{9,8},{10,11... | collective-permute-start | bytes 4718600 | tf_op jit(solution)/shard_map/ppermute | solution.py:47
  454.2 19.9 %collective-permute-start.58 = (bf16[1,768,384]{2,1,0:T(8,128)(2,1)S(1)}, bf16[1,768,384]{2,1,0:T(8,128)(2,1)S(1)}, u32[]{:S(2)}, u32[]{:S(2)}) collective-permute-start(bf16[1,768,384]{2,1,0:T(8,128)(2,1)S(1)} %collective-permute-done.57.refs_1_), channel_id=1, source_target_pairs={{8,0},{16,8},{24,16},{28,24},{20,28},{12,20},{4,12},{0,4},{1,9},{9... | collective-permute-start | bytes 1769480 | tf_op jit(solution)/shard_map/ppermute | solution.py:782
  466.6 21.2 %collective-permute-start.53 = (bf16[1,768,384]{2,1,0:T(8,128)(2,1)S(1)}, bf16[1,768,384]{2,1,0:T(8,128)(2,1)S(1)}, u32[]{:S(2)}, u32[]{:S(2)}) collective-permute-start(bf16[1,768,384]{2,1,0:T(8,128)(2,1)S(1)} %collective-permute-done.52.refs_0_), channel_id=1, source_target_pairs={{0,8},{8,16},{16,24},{24,28},{28,20},{20,12},{12,4},{4,0},{9,1},{1... | collective-permute-start | bytes 1769480 | tf_op jit(solution)/shard_map/ppermute | solution.py:782
  466.7 21.0 %collective-permute-start.59 = (bf16[1,768,384]{2,1,0:T(8,128)(2,1)S(1)}, bf16[1,768,384]{2,1,0:T(8,128)(2,1)S(1)}, u32[]{:S(2)}, u32[]{:S(2)}) collective-permute-start(bf16[1,768,384]{2,1,0:T(8,128)(2,1)S(1)} %collective-permute-done.54.refs_1_), channel_id=1, source_target_pairs={{8,0},{16,8},{24,16},{28,24},{20,28},{12,20},{4,12},{0,4},{1,9},{9... | collective-permute-start | bytes 1769480 | tf_op jit(solution)/shard_map/ppermute | solution.py:782
  474.1 20.0 %collective-permute-start.81 = (bf16[2,96,896]{2,1,0:T(8,128)(2,1)S(1)}, bf16[2,96,896]{2,1,0:T(8,128)(2,1)S(1)}, u32[]{:S(2)}, u32[]{:S(2)}) collective-permute-start(bf16[2,96,896]{2,1,0:T(8,128)(2,1)S(1)} %fusion.18), channel_id=1, source_target_pairs={{8,0},{16,8},{24,16},{28,24},{20,28},{12,20},{4,12},{0,4},{1,9},{9... | collective-permute-start | bytes 1032200 | tf_op jit(solution)/shard_map/ppermute | solution.py:782
  475.5 20.1 %collective-permute-start.71 = (bf16[2,96,896]{2,1,0:T(8,128)(2,1)S(1)}, bf16[2,96,896]{2,1,0:T(8,128)(2,1)S(1)}, u32[]{:S(2)}, u32[]{:S(2)}) collective-permute-start(bf16[2,96,896]{2,1,0:T(8,128)(2,1)S(1)} %fusion.24), channel_id=1, source_target_pairs={{0,8},{8,16},{16,24},{24,28},{28,20},{20,12},{12,4},{4,0},{9,1},{1... | collective-permute-start | bytes 1032200 | tf_op jit(solution)/shard_map/ppermute | solution.py:782
  487.7 27.4 %collective-permute-start.73 = (bf16[1,768,384]{2,1,0:T(8,128)(2,1)S(1)}, bf16[1,768,384]{2,1,0:T(8,128)(2,1)S(1)}, u32[]{:S(2)}, u32[]{:S(2)}) collective-permute-start(bf16[1,768,384]{2,1,0:T(8,128)(2,1)S(1)} %collective-permute-done.53.refs_0_), channel_id=1, source_target_pairs={{0,8},{8,16},{16,24},{24,28},{28,20},{20,12},{12,4},{4,0},{9,1},{1... | collective-permute-start | bytes 1769480 | tf_op jit(solution)/shard_map/ppermute | solution.py:782
  488.1 27.1 %collective-permute-start.74 = (bf16[1,768,384]{2,1,0:T(8,128)(2,1)S(1)}, bf16[1,768,384]{2,1,0:T(8,128)(2,1)S(1)}, u32[]{:S(2)}, u32[]{:S(2)}) collective-permute-start(bf16[1,768,384]{2,1,0:T(8,128)(2,1)S(1)} %collective-permute-done.59.refs_1_), channel_id=1, source_target_pairs={{8,0},{16,8},{24,16},{28,24},{20,28},{12,20},{4,12},{0,4},{1,9},{9... | collective-permute-start | bytes 1769480 | tf_op jit(solution)/shard_map/ppermute | solution.py:782
  494.2 19.8 %collective-permute-start.82 = (bf16[2,96,896]{2,1,0:T(8,128)(2,1)S(1)}, bf16[2,96,896]{2,1,0:T(8,128)(2,1)S(1)}, u32[]{:S(2)}, u32[]{:S(2)}) collective-permute-start(bf16[2,96,896]{2,1,0:T(8,128)(2,1)S(1)} %fusion.17), channel_id=1, source_target_pairs={{8,0},{16,8},{24,16},{28,24},{20,28},{12,20},{4,12},{0,4},{1,9},{9... | collective-permute-start | bytes 1032200 | tf_op jit(solution)/shard_map/ppermute | solution.py:782
  495.7 21.5 %collective-permute-start.72 = (bf16[2,96,896]{2,1,0:T(8,128)(2,1)S(1)}, bf16[2,96,896]{2,1,0:T(8,128)(2,1)S(1)}, u32[]{:S(2)}, u32[]{:S(2)}) collective-permute-start(bf16[2,96,896]{2,1,0:T(8,128)(2,1)S(1)} %fusion.23), channel_id=1, source_target_pairs={{0,8},{8,16},{16,24},{24,28},{28,20},{20,12},{12,4},{4,0},{9,1},{1... | collective-permute-start | bytes 1032200 | tf_op jit(solution)/shard_map/ppermute | solution.py:782
  516.1 21.3 %collective-permute-start.77 = (bf16[1,768,384]{2,1,0:T(8,128)(2,1)S(1)}, bf16[1,768,384]{2,1,0:T(8,128)(2,1)S(1)}, u32[]{:S(2)}, u32[]{:S(2)}) collective-permute-start(bf16[1,768,384]{2,1,0:T(8,128)(2,1)S(1)} %collective-permute-done.74.refs_1_), channel_id=1, source_target_pairs={{8,0},{16,8},{24,16},{28,24},{20,28},{12,20},{4,12},{0,4},{1,9},{9... | collective-permute-start | bytes 1769480 | tf_op jit(solution)/shard_map/ppermute | solution.py:782
  517.3 21.5 %collective-permute-start.75 = (bf16[2,96,896]{2,1,0:T(8,128)(2,1)S(1)}, bf16[2,96,896]{2,1,0:T(8,128)(2,1)S(1)}, u32[]{:S(2)}, u32[]{:S(2)}) collective-permute-start(bf16[2,96,896]{2,1,0:T(8,128)(2,1)S(1)} %fusion.22), channel_id=1, source_target_pairs={{0,8},{8,16},{16,24},{24,28},{28,20},{20,12},{12,4},{4,0},{9,1},{1... | collective-permute-start | bytes 1032200 | tf_op jit(solution)/shard_map/ppermute | solution.py:782
  519.7 27.3 %collective-permute-start.60 = (bf16[1024,768]{1,0:T(8,128)(2,1)S(1)}, bf16[1024,768]{1,0:T(8,128)(2,1)S(1)}, u32[]{:S(2)}, u32[]{:S(2)}) collective-permute-start(bf16[1024,768]{1,0:T(8,128)(2,1)S(1)} %convolution_convert_fusion), channel_id=1, source_target_pairs={{0,1},{1,0},{2,3},{3,2},{4,5},{5,4},{6,7},{7,6},{8,9},{9,8},{10,11... | collective-permute-start | bytes 4718600 | tf_op jit(solution)/shard_map/ppermute | solution.py:47
  541.7 20.0 %collective-permute-start.47 = (bf16[512,768]{1,0:T(8,128)(2,1)S(1)}, bf16[512,768]{1,0:T(8,128)(2,1)S(1)}, u32[]{:S(2)}, u32[]{:S(2)}) collective-permute-start(bf16[512,768]{1,0:T(8,128)(2,1)S(1)} %dynamic-slice_convert_fusion.1), channel_id=1, source_target_pairs={{0,2},{2,0},{1,3},{3,1},{4,6},{6,4},{5,7},{7,5},{8,10},{10,8},{9,1... | collective-permute-start | bytes 2359304 | tf_op jit(solution)/shard_map/ppermute | solution.py:47
  543.3 23.2 %collective-permute-start.87 = (bf16[1,768,384]{2,1,0:T(8,128)(2,1)S(1)}, bf16[1,768,384]{2,1,0:T(8,128)(2,1)S(1)}, u32[]{:S(2)}, u32[]{:S(2)}) collective-permute-start(bf16[1,768,384]{2,1,0:T(8,128)(2,1)S(1)} %collective-permute-done.76.refs_0_), channel_id=1, source_target_pairs={{0,8},{8,16},{16,24},{24,28},{28,20},{20,12},{12,4},{4,0},{9,1},{1... | collective-permute-start | bytes 1769480 | tf_op jit(solution)/shard_map/ppermute | solution.py:782
  543.8 22.7 %collective-permute-start.88 = (bf16[1,768,384]{2,1,0:T(8,128)(2,1)S(1)}, bf16[1,768,384]{2,1,0:T(8,128)(2,1)S(1)}, u32[]{:S(2)}, u32[]{:S(2)}) collective-permute-start(bf16[1,768,384]{2,1,0:T(8,128)(2,1)S(1)} %collective-permute-done.77.refs_1_), channel_id=1, source_target_pairs={{8,0},{16,8},{24,16},{28,24},{20,28},{12,20},{4,12},{0,4},{1,9},{9... | collective-permute-start | bytes 1769480 | tf_op jit(solution)/shard_map/ppermute | solution.py:782
  545.4 26.0 %collective-permute-start.102 = (bf16[2,96,896]{2,1,0:T(8,128)(2,1)S(1)}, bf16[2,96,896]{2,1,0:T(8,128)(2,1)S(1)}, u32[]{:S(2)}, u32[]{:S(2)}) collective-permute-start(bf16[2,96,896]{2,1,0:T(8,128)(2,1)S(1)} %pad_maximum_fusion.2), channel_id=1, source_target_pairs={{8,0},{16,8},{24,16},{28,24},{20,28},{12,20},{4,12},{0,4},{1,9},{9... | collective-permute-start | bytes 1032200 | tf_op jit(solution)/shard_map/ppermute | solution.py:782
  547.0 23.9 %collective-permute-start.86 = (bf16[2,96,896]{2,1,0:T(8,128)(2,1)S(1)}, bf16[2,96,896]{2,1,0:T(8,128)(2,1)S(1)}, u32[]{:S(2)}, u32[]{:S(2)}) collective-permute-start(bf16[2,96,896]{2,1,0:T(8,128)(2,1)S(1)} %pad_maximum_fusion.1), channel_id=1, source_target_pairs={{0,8},{8,16},{16,24},{24,28},{28,20},{20,12},{12,4},{4,0},{9,1},{1... | collective-permute-start | bytes 1032200 | tf_op jit(solution)/shard_map/ppermute | solution.py:782
  561.7 30.5 %collective-permute-start.61 = (bf16[512,768]{1,0:T(8,128)(2,1)S(1)}, bf16[512,768]{1,0:T(8,128)(2,1)S(1)}, u32[]{:S(2)}, u32[]{:S(2)}) collective-permute-start(bf16[512,768]{1,0:T(8,128)(2,1)S(1)} %dynamic-slice_convert_fusion), channel_id=1, source_target_pairs={{0,2},{2,0},{1,3},{3,1},{4,6},{6,4},{5,7},{7,5},{8,10},{10,8},{9,1... | collective-permute-start | bytes 2359304 | tf_op jit(solution)/shard_map/ppermute | solution.py:47
  571.0 19.2 %collective-permute-start.89 = (bf16[2,96,896]{2,1,0:T(8,128)(2,1)S(1)}, bf16[2,96,896]{2,1,0:T(8,128)(2,1)S(1)}, u32[]{:S(2)}, u32[]{:S(2)}) collective-permute-start(bf16[2,96,896]{2,1,0:T(8,128)(2,1)S(1)} %collective-permute-done.86), channel_id=1, source_target_pairs={{0,8},{8,16},{16,24},{24,28},{28,20},{20,12},{12,4},{4,0},{9,1},{1... | collective-permute-start | bytes 1032200 | tf_op jit(solution)/shard_map/ppermute | solution.py:782
  571.3 19.2 %collective-permute-start.103 = (bf16[2,96,896]{2,1,0:T(8,128)(2,1)S(1)}, bf16[2,96,896]{2,1,0:T(8,128)(2,1)S(1)}, u32[]{:S(2)}, u32[]{:S(2)}) collective-permute-start(bf16[2,96,896]{2,1,0:T(8,128)(2,1)S(1)} %collective-permute-done.102), channel_id=1, source_target_pairs={{8,0},{16,8},{24,16},{28,24},{20,28},{12,20},{4,12},{0,4},{1,9},{9... | collective-permute-start | bytes 1032200 | tf_op jit(solution)/shard_map/ppermute | solution.py:782
  583.2 42.9 %collective-permute-start.94 = (bf16[1,768,384]{2,1,0:T(8,128)(2,1)S(1)}, bf16[1,768,384]{2,1,0:T(8,128)(2,1)S(1)}, u32[]{:S(2)}, u32[]{:S(2)}) collective-permute-start(bf16[1,768,384]{2,1,0:T(8,128)(2,1)S(1)} %collective-permute-done.90.refs_0_), channel_id=1, source_target_pairs={{0,8},{8,16},{16,24},{24,28},{28,20},{20,12},{12,4},{4,0},{9,1},{1... | collective-permute-start | bytes 1769480 | tf_op jit(solution)/shard_map/ppermute | solution.py:782
  583.5 42.6 %collective-permute-start.95 = (bf16[1,768,384]{2,1,0:T(8,128)(2,1)S(1)}, bf16[1,768,384]{2,1,0:T(8,128)(2,1)S(1)}, u32[]{:S(2)}, u32[]{:S(2)}) collective-permute-start(bf16[1,768,384]{2,1,0:T(8,128)(2,1)S(1)} %collective-permute-done.91.refs_1_), channel_id=1, source_target_pairs={{8,0},{16,8},{24,16},{28,24},{20,28},{12,20},{4,12},{0,4},{1,9},{9... | collective-permute-start | bytes 1769480 | tf_op jit(solution)/shard_map/ppermute | solution.py:782
  590.1 33.8 %collective-permute-start.92 = (bf16[2,96,896]{2,1,0:T(8,128)(2,1)S(1)}, bf16[2,96,896]{2,1,0:T(8,128)(2,1)S(1)}, u32[]{:S(2)}, u32[]{:S(2)}) collective-permute-start(bf16[2,96,896]{2,1,0:T(8,128)(2,1)S(1)} %collective-permute-done.89), channel_id=1, source_target_pairs={{0,8},{8,16},{16,24},{24,28},{28,20},{20,12},{12,4},{4,0},{9,1},{1... | collective-permute-start | bytes 1032200 | tf_op jit(solution)/shard_map/ppermute | solution.py:782
  590.6 33.9 %collective-permute-start.104 = (bf16[2,96,896]{2,1,0:T(8,128)(2,1)S(1)}, bf16[2,96,896]{2,1,0:T(8,128)(2,1)S(1)}, u32[]{:S(2)}, u32[]{:S(2)}) collective-permute-start(bf16[2,96,896]{2,1,0:T(8,128)(2,1)S(1)} %collective-permute-done.103), channel_id=1, source_target_pairs={{8,0},{16,8},{24,16},{28,24},{20,28},{12,20},{4,12},{0,4},{1,9},{9... | collective-permute-start | bytes 1032200 | tf_op jit(solution)/shard_map/ppermute | solution.py:782
  592.9 17.3 %collective-permute-start.63 = (f32[2,768]{1,0:T(2,128)S(1)}, f32[2,768]{1,0:T(2,128)S(1)}, u32[]{:S(2)}, u32[]{:S(2)}) collective-permute-start(f32[2,768]{1,0:T(2,128)S(1)} %pad_maximum_fusion.4), channel_id=1, source_target_pairs={{0,4},{4,0},{8,12},{12,8},{16,20},{20,16},{24,28},{28,24},{1,5},{5... | collective-permute-start | bytes 18440 | tf_op jit(solution)/shard_map/ppermute | solution.py:1117
  626.1 27.9 %collective-permute-start.98 = (bf16[1,768,384]{2,1,0:T(8,128)(2,1)S(1)}, bf16[1,768,384]{2,1,0:T(8,128)(2,1)S(1)}, u32[]{:S(2)}, u32[]{:S(2)}) collective-permute-start(bf16[1,768,384]{2,1,0:T(8,128)(2,1)S(1)} %collective-permute-done.94.refs_0_), channel_id=1, source_target_pairs={{0,8},{8,16},{16,24},{24,28},{28,20},{20,12},{12,4},{4,0},{9,1},{1... | collective-permute-start | bytes 1769480 | tf_op jit(solution)/shard_map/ppermute | solution.py:782
  626.6 27.4 %collective-permute-start.99 = (bf16[1,768,384]{2,1,0:T(8,128)(2,1)S(1)}, bf16[1,768,384]{2,1,0:T(8,128)(2,1)S(1)}, u32[]{:S(2)}, u32[]{:S(2)}) collective-permute-start(bf16[1,768,384]{2,1,0:T(8,128)(2,1)S(1)} %collective-permute-done.95.refs_1_), channel_id=1, source_target_pairs={{8,0},{16,8},{24,16},{28,24},{20,28},{12,20},{4,12},{0,4},{1,9},{9... | collective-permute-start | bytes 1769480 | tf_op jit(solution)/shard_map/ppermute | solution.py:782
  635.5 18.1 %collective-permute-start.106 = (bf16[2,96,896]{2,1,0:T(8,128)(2,1)S(1)}, bf16[2,96,896]{2,1,0:T(8,128)(2,1)S(1)}, u32[]{:S(2)}, u32[]{:S(2)}) collective-permute-start(bf16[2,96,896]{2,1,0:T(8,128)(2,1)S(1)} %collective-permute-done.105), channel_id=1, source_target_pairs={{8,0},{16,8},{24,16},{28,24},{20,28},{12,20},{4,12},{0,4},{1,9},{9... | collective-permute-start | bytes 1032200 | tf_op jit(solution)/shard_map/ppermute | solution.py:782
  (136 other events, 1492.3 us)

commit v5 on v4

--- a/solution.py
+++ b/solution.py
@@ -2,6 +2,7 @@
 
 import jax
 import jax.numpy as jnp
+import numpy as np
 from jax import lax
 from jax.experimental import pallas as pl
 from jax.experimental.pallas import tpu as pltpu
@@ -262,30 +263,32 @@
             jax.ShapeDtypeStruct((2, rows), F32),
             jax.ShapeDtypeStruct((rows // shares, rows), BF16),
         ],
-        compiler_params=params(16, "arbitrary"),
+        compiler_params=params(60, "arbitrary"),
         cost_estimate=SMALL,
         name="their_columns",
     )(place, w_query, w_key, w_value, gain_attn, gain_ffn, w_out)
 
 
-def join_kernel(mine_ref, own_ref, other_ref, out_ref):
-    rows = own_ref.shape[0]
-    out_ref[pl.ds(pl.multiple_of(mine_ref[0] * rows, rows), rows), :] = own_ref[...]
-    out_ref[pl.ds(pl.multiple_of((1 - mine_ref[0]) * rows, rows), rows), :] = other_ref[...]
-
-
-def join(mine, own, other):
-    rows, width = own.shape
+def join_kernel(mine_ref, *refs):
+    *parts, out_ref = refs
+    rows = parts[0].shape[0]
+    for k, part in enumerate(parts):
+        at = jnp.bitwise_xor(mine_ref[0], k)
+        out_ref[pl.ds(pl.multiple_of(at * rows, rows), rows), :] = part[...]
+
+
+def join(mine, *parts):
+    rows, width = parts[0].shape
     spec = pl.BlockSpec(memory_space=pltpu.VMEM)
     return pl.pallas_call(
         join_kernel,
-        out_shape=jax.ShapeDtypeStruct((2 * rows, width), own.dtype),
-        in_specs=[pl.BlockSpec(memory_space=pltpu.SMEM), spec, spec],
+        out_shape=jax.ShapeDtypeStruct((len(parts) * rows, width), parts[0].dtype),
+        in_specs=[pl.BlockSpec(memory_space=pltpu.SMEM)] + [spec] * len(parts),
         out_specs=spec,
         compiler_params=params(16),
         cost_estimate=SMALL,
         name="join",
-    )(mine.reshape(1), own, other)
+    )(mine.reshape(1), *parts)
 
 
 def project_kernel(col_ref, own_ref, other_ref, gains_ref, gains_c_ref, query_ref, key_ref, value_ref, there_ref, x_own_ref, x_other_ref, qkv_ref, scale_ref):
@@ -341,7 +344,7 @@
             jax.ShapeDtypeStruct((rows, width), BF16),
             jax.ShapeDtypeStruct((rows, 1), F32),
         ],
-        compiler_params=params(24, "arbitrary"),
+        compiler_params=params(60, "arbitrary"),
         cost_estimate=SMALL,
         name="project",
     )(col, own, other, gains, gains_c, w_query, w_key, w_value, there)
@@ -638,7 +641,7 @@
     return list(range(0, size, 2)) + list(range(1, size, 2))[::-1]
 
 
-def unpack_kernel(aliased, index_ref, *refs):
+def unpack_kernel(aliased, plan_ref, *refs):
     chunks = refs[0:2]
     gate_ref, up_ref, down_ref = refs[2 + aliased : 5 + aliased]
     blocks = chunks[0].shape[1] // LANES
@@ -654,15 +657,21 @@
         pl.when(pl.program_id(1) == k)(lambda k=k: write(chunks[k]))
 
 
-def unpack(index, chunks, shapes, outs):
+def unpack(plan, first, wave, chunks, shapes, outs):
     count, rows, width = chunks[0].shape
     chunk = pl.BlockSpec((1, rows, width), lambda i, d, n: (i, 0, 0))
 
+    def place(i, d, n):
+        block = n[n.shape[0] - 1]
+        return n[first + 2 * i + d], 1 - block if wave else block
+
     def wide(i, d, n):
-        return (n[2 * i + d], 0, n[2 * count])
+        expert, block = place(i, d, n)
+        return (expert, 0, block)
 
     def low(i, d, n):
-        return (n[2 * i + d], n[2 * count], 0)
+        expert, block = place(i, d, n)
+        return (expert, block, 0)
 
     aliased = len(outs)
     return pl.pallas_call(
@@ -682,7 +691,7 @@
         compiler_params=params(16, "arbitrary", "arbitrary"),
         cost_estimate=SMALL,
         name="unpack",
-    )(index, *chunks, *outs)
+    )(plan, *chunks, *outs)
 
 
 def unpack_late_kernel(col_ref, first_ref, second_ref, *outs):
@@ -726,7 +735,29 @@
     )(col, first, second)
 
 
-LATE_ROUND = 3
+def plans(ring, each):
+    size = len(ring)
+    rows = []
+    for member in range(size):
+        place = ring.index(member)
+        for col in range(2):
+            chunks = []
+            for step in range(2 * size - 1):
+                for which in range(2):
+                    sign = 1 if which == col else -1
+                    chunks.append((place - sign * step) % size)
+            experts = []
+            for start in (0, size - 1):
+                for step in range(start, start + size):
+                    for k in range(each):
+                        for which in range(2):
+                            second = col if which == 0 else 1 - col
+                            experts.append(2 * each * chunks[2 * step + which] + each * second + k)
+            rows.append(experts + chunks + [col])
+    return np.asarray(rows, np.int32)
+
+
+LATE_ROUND = 1
 
 
 def add_rounded(left, right):
@@ -772,9 +803,11 @@
         [(2 * a, 2 * b) for a, b in ways[0]] + [(2 * a + 1, 2 * b + 1) for a, b in ways[1]]
         for ways in ((rights, lefts), (lefts, rights))
     ]
-    place_of = [ring.index(k) for k in range(ring_size)]
-    place = jnp.asarray(place_of, jnp.int32)[dp % ring_size]
-    signs = [1 - 2 * col, 2 * col - 1]
+    experts_each = experts // (2 * ring_size)
+    plan = jnp.asarray(plans(ring, experts_each))
+    plan = lax.dynamic_slice(
+        plan, (2 * (dp % ring_size) + col, jnp.int32(0)), (1, plan.shape[1])
+    ).reshape(-1)
 
     def send(values, which):
         if ring_size == 1:
@@ -782,7 +815,7 @@
         return lax.ppermute(values, ("dp", "col"), routes_of[which])
 
     def chunk_at(step, which):
-        return (place - signs[which] * step) % ring_size
+        return plan[2 * experts + 2 * step + which]
 
     def across_rings(values):
         if len(starts) == 1:
@@ -820,15 +853,10 @@
     grad_y = swap(after(out_grad[:grad_cut], tokens_y), "row")
     far = project_half(tokens_y, tokens_yc)
 
-    def double(part, bit, *others):
-        if bit >= count:
-            return part
-        pairs = [(m, m ^ bit) for m in range(dp_size)]
-        came = after(lax.ppermute(part, "dp", pairs), *others)
-        return join(member // bit % 2, part, came)
-
-    out_y = double(out_y, 1)
-    where = after(where, out_y, grad_y)
+    shares = [out_y]
+    for k in range(1, count):
+        shares.append(lax.ppermute(out_y, "dp", [(m, m ^ k) for m in range(dp_size)]))
+    where = after(where, grad_y, *shares)
 
     w_sgate, w_sup, w_sdown = w_shared_gate[None], w_shared_up[None], w_shared_down[None]
     up_c = swap(after(w_up, gate_c, tokens_yc), "col")
@@ -844,10 +872,10 @@
         w_out,
         out_c,
     )
-    down_c = swap(after(w_down, up_c, attended_c), "col")
+    down_c = swap(after(w_down, tokens_yc), "col")
     rest_y = swap(after(out_grad[grad_cut:], attended_c), "row")
     attended_y = after(attended_y, before[0])
-    out_y = double(out_y, 2, attended_y)
+    out_y = join(member, *shares)
     out_yc = swap(out_y, "col")
     attended_yc = swap(attended_y, "col")
     grad_own = join(row, out_grad, jnp.concatenate([grad_y, rest_y], axis=0))
@@ -870,14 +898,8 @@
         dense = dense - gates[-1]
     gates = jnp.concatenate(gates, axis=0).astype(BF16)
 
-    each = experts // (2 * ring_size)
-    orders = []
-    for s in range(ring_size):
-        for k in range(each):
-            for which in range(2):
-                second = col if which == 0 else 1 - col
-                orders.append(2 * each * chunk_at(s, which) + each * second + k)
-    order = jnp.stack(orders + [col]).astype(jnp.int32)
+    each = experts_each
+    order = plan
     pairs_total = experts // 2
     routed = [w_gate, w_up, gate_c, up_c, w_down, down_c]
     shared = [w_sgate, w_sup, sgate_c, sup_c, w_sdown, sdown_c]
@@ -934,9 +956,40 @@
 
         return work
 
+    start = row * local_rows
+
+    def my_rows(values):
+        return lax.dynamic_slice_in_dim(values, start, local_rows, axis=0)
+
+    def their_rows(values):
+        return lax.dynamic_slice_in_dim(values, local_rows - start, local_rows, axis=0)
+
+    normed = {}
+
+    def work_hidden(order):
+        normed_grad = mixed[True, 0] + swap(mixed[True, 1], "col").astype(F32)
+        came = swap(normed_grad.astype(BF16), "row")
+        normed_grad = normed_grad + after(came, order).astype(F32)
+        scaled = normed_grad * norm_gain_ffn
+        products = jnp.sum(scaled * hidden, axis=1, keepdims=True)
+        mean = (products + swap(products, "col")) / D
+        normed["gain"] = jnp.sum(my_rows(normed_grad * hidden * scale_ffn), axis=0)
+        normed["hidden"] = (
+            grad_own.astype(F32) + scale_ffn * scaled - hidden * scale_ffn**3 * mean
+        )
+        normed["grad"] = normed["hidden"].astype(BF16)
+        normed["grad_c"] = swap(normed["grad"], "col")
+        return normed["grad"]
+
+    def work_attend(order):
+        normed["qkv"] = attend_back(
+            after(where, order), near[2], far[2], normed["grad"], normed["grad_c"], w_out, out_c
+        )
+        return normed["qkv"]
+
     tasks = [work_experts(at, at + each) for at in range(each, pairs_total, each)]
-    tasks += [work_shared, work_mix(True, 1), work_mix(True, 0)]
-    later = [work_mix(False, 1), work_mix(False, 0)]
+    tasks += [work_shared, work_mix(True, 1), work_mix(True, 0), work_mix(False, 1), work_mix(False, 0)]
+    tasks += [None] * (2 * ring_size - 3 - len(tasks)) + [work_hidden, work_attend]
     got = [None, None]
     if ring_size > 1:
         got[0] = send(sums[0], 0)
@@ -945,8 +998,9 @@
     for s in range(1, ring_size):
         for k in range(2):
             last = sums
-            if tasks:
-                last = [tasks.pop(0)(after(order, *last))]
+            task = tasks.pop(0) if tasks else None
+            if task:
+                last = [task(after(order, *last))]
             got[k] = after(got[k], *last)
             parts = [runs[at] for at in range(each * s, each * s + each)]
             mine = [p[k][p[2] : p[2] + 1] for p in parts]
@@ -954,32 +1008,16 @@
             sums[k] = add_rounded(got[k], mine)
             if s + 1 < ring_size:
                 got[k] = send(sums[k], k)
-    while tasks:
-        tasks.pop(0)(after(order, *sums))
+    for task in tasks:
+        if task:
+            task(after(order, *sums))
     sums = [across_rings(total) for total in sums]
     waves = [[total[:, :local_features] for total in sums]]
     crossed = [swap(total[:, local_features:], "col") for total in sums]
     waves.append([crossed[1], crossed[0]])
 
-    start = row * local_rows
-
-    def my_rows(values):
-        return lax.dynamic_slice_in_dim(values, start, local_rows, axis=0)
-
-    def their_rows(values):
-        return lax.dynamic_slice_in_dim(values, local_rows - start, local_rows, axis=0)
-
-    normed_grad = mixed[True, 0] + swap(mixed[True, 1], "col").astype(F32)
-    normed_grad = normed_grad + swap(normed_grad.astype(BF16), "row").astype(F32)
-    gain_ffn_part = jnp.sum(my_rows(normed_grad * hidden * scale_ffn), axis=0)
-    scaled = normed_grad * norm_gain_ffn
-    products = jnp.sum(scaled * hidden, axis=1, keepdims=True)
-    mean = (products + swap(products, "col")) / D
-    hidden_grad = grad_own.astype(F32) + scale_ffn * scaled - hidden * scale_ffn**3 * mean
-    attn_grad = hidden_grad.astype(BF16)
-    attn_grad_c = swap(attn_grad, "col")
-
-    qkv_grad = attend_back(where, near[2], far[2], attn_grad, attn_grad_c, w_out, out_c)
+    hidden_grad, attn_grad, attn_grad_c = normed["hidden"], normed["grad"], normed["grad_c"]
+    gain_ffn_part, qkv_grad = normed["gain"], normed["qkv"]
     packs = late_grads(
         where,
         near[0:2],
@@ -1015,69 +1053,62 @@
             late[k] = in_order(totals[k][0:1], others[1 - k][None], col, 0)
             late_out[k] = late_place(late[k], 0, k)
 
-    def late_finish(got, last):
-        nonlocal late_done
-        late_done += 1
-        for k in range(2):
-            values = after(got[k], *last)
-            if late_done < ring_size:
-                late[k] = add_rounded(values, late_chunk(late_done, k))
-            else:
-                late[k] = values
-                late_out[k] = late_place(values, late_done - ring_size + 1, k)
-            last = [late[k]]
-        if late_done == ring_size - 1:
-            late_turn()
+    def late_finish(k, values):
+        if late_done < ring_size:
+            late[k] = add_rounded(values, late_chunk(late_done, k))
+        else:
+            late[k] = values
+            late_out[k] = late_place(values, late_done - ring_size + 1, k)
 
     shapes = [w_gate.shape, w_up.shape, w_down.shape]
     placed = ()
 
     def place_chunks(wave, step, chunks, placed):
-        index = []
-        for k in range(each):
-            for which in range(2):
-                second = col if which == 0 else 1 - col
-                at = chunk_at(ring_size - 1 + step, which)
-                index.append(2 * each * at + each * second + k)
-        index.append(col if wave == 0 else 1 - col)
-        return unpack(jnp.stack(index).astype(jnp.int32), chunks, shapes, placed)
+        return unpack(plan, experts + 2 * each * step, wave, chunks, shapes, placed)
 
     if late_total == 0:
         late_turn()
     rounds = [(wave, step) for wave in range(2) for step in range(ring_size - 1)]
+    late_got = None
+    last = list(sums)
     for number, (wave, step) in enumerate(rounds):
         if step == 0:
-            chunks = waves[wave]
-        if number == LATE_ROUND:
-            late = [after(values, *chunks) for values in late]
-        steps = 1 if number >= LATE_ROUND else 0
-        if number >= len(rounds) - LATE_ROUND:
-            steps = 2
-        steps = min(steps, late_total - late_done)
-        got = [send(chunks[k], k) for k in range(2)]
-        late_got = [send(late[k], k) for k in range(2)] if steps else None
+            came = list(got) if number else None
+            got = list(waves[wave])
+        late_done += late_got is not None
+        chunks = [None, None]
+        for k in range(2):
+            chunks[k] = after(got[k], *last)
+            got[k] = send(chunks[k], k)
+            last = [chunks[k]]
+            if late_got is not None:
+                late_finish(k, after(late_got[k], *last))
+                last = [late[k]]
+        if late_got is not None and late_done == ring_size - 1:
+            late_turn()
+        if number >= LATE_ROUND and late_done < late_total:
+            late_got = [send(after(late[k], *chunks), k) for k in range(2)]
+        else:
+            late_got = None
+        if step == 0 and number:
+            placed = place_chunks(0, ring_size - 1, came, placed)
         placed = place_chunks(wave, step, chunks, placed)
         last = placed[0:1]
-        if number in (LATE_ROUND + 1, LATE_ROUND + 2):
-            last = [later.pop(0)(after(order, *last))]
-        if number == LATE_ROUND + 5:
+        if number == LATE_ROUND + 3:
             qkv_grad = after(qkv_grad, *last)
+    if rounds:
+        placed = place_chunks(1, ring_size - 1, [after(got[k], *last) for k in range(2)], placed)
+        last = placed[0:1]
+    while late_got is not None:
+        late_done += 1
         for k in range(2):
-            got[k] = after(got[k], *last)
-        for at in range(steps):
-            if at:
-                late_got = [send(late[k], k) for k in range(2)]
-            late_finish(late_got, got)
-        chunks = got
-        if step == ring_size - 2:
-            placed = place_chunks(wave, step + 1, chunks, placed)
-    while later:
-        later.pop(0)(order)
+            late_finish(k, after(late_got[k], *last))
+        if late_done == ring_size - 1:
+            late_turn()
+        late_got = [send(late[k], k) for k in range(2)] if late_done < late_total else None
     if not rounds:
         for wave in range(2):
             placed = place_chunks(wave, 0, waves[wave], placed)
-    while late_done < late_total:
-        late_finish([send(late[k], k) for k in range(2)], placed[0:1])
     gate_grad, up_grad, down_grad = placed
     shapes = [w.shape for w in (w_shared_gate, w_shared_up, w_shared_down)]
     shapes += [w.shape for w in (w_query, w_key, w_value, w_out)]

time: 687 us -> 724 us (1.054)
  between operations: 23.6 us -> 59.2 us
  waiting for transfers between devices: 264 us -> 242 us
  starting transfers between devices: 99.8 us -> 113 us
    ppermute x34, waiting for transfers between devices: 61.8 us -> 48.7 us  [swap(): return lax.ppermute(values, axis, [(0, 1), (1, 0)])]
    ppermute x3, waiting for transfers between devices: 21.4 us -> 12.3 us  [body(): gain_parts = gain_parts + lax.ppermute(gain_parts, 'dp', pairs)]
    ppermute x70, starting transfers between devices: 76.9 us -> 84.7 us  [send(): return lax.ppermute(values, ('dp', 'col'), routes_of[which])]
    convert_element_type x28 -> x27, other arithmetic: 23 us -> 24.1 us  [add_rounded(): return (left.astype(F32) + right.astype(F32)).astype(BF16)]
  transfers between devices with their start and end apart: 109 -> 110, of which waited for: 50 -> 50; matrix products, arithmetic and copies ran while one was open for 6% -> 7% of each run, Pallas kernels for 30% -> 29%
where the time goes in v5:
time: 724 us; the launch traced here: 714 us
  waiting for transfers between devices  242 us (33%)
  Pallas kernels  222 us (31%)
  starting transfers between devices  113 us (16%)
  between operations  59.2 us (8%)
  other arithmetic  38.5 us (5%)
  local copies, waits for them, and re-layouts  36.2 us (5%)
    ppermute x70, waiting for transfers between devices, send(): return lax.ppermute(values, ('dp', 'col'), routes_of[which])  171 us
    ppermute x70, starting transfers between devices, send(): return lax.ppermute(values, ('dp', 'col'), routes_of[which])  84.7 us
    pallas_call x9, Pallas kernels, expert_grads(): pl.pallas_call(functools.partial(expert_kernel, shared, aliased, first),...  79.7 us
    ppermute x34, waiting for transfers between devices, swap(): return lax.ppermute(values, axis, [(0, 1), (1, 0)])  48.7 us
    pallas_call x4, Pallas kernels, mix(): pl.pallas_call(functools.partial(mix_kernel, back, group), grid_spec=pltp...  39.9 us
    pallas_call x16, Pallas kernels, unpack(): pl.pallas_call(functools.partial(unpack_kernel, aliased), grid_spec=pltpu...  38.7 us
    convert_element_type x27, other arithmetic, add_rounded(): return (left.astype(F32) + right.astype(F32)).astype(BF16)  24.1 us
    unnamed x182, local copies, waits for them, and re-layouts  23.6 us
  transfers between devices with their start and end apart: 110, of which 50 were waited for; matrix products, arithmetic and copies ran while one was open for 7% of the time, Pallas kernels for 29%

profile of v5, /device:TPU:0, one launch (start us, length us, event | category | flops | bytes accessed | tf_op | source)
XLA Modules:
  0.0 713.5 jit_solution(16208272104777666173)
XLA Ops:
  4.3 3.1 their_columns.1
  10.7 3.1 collective-permute-done.2.gains_c_ref.refs_7_
  13.7 2.9 collective-permute-start.4
  18.4 4.5 project.2
  22.9 12.1 %collective-permute-done.4.refs_0_ = bf16[192,768]{1,0:T(8,128)(2,1)S(1)} collective-permute-done((bf16[192,768]{1,0:T(8,128)(2,1)}, bf16[192,768]{1,0:T(8,128)(2,1)S(1)}, u32[]{:S(2)}, u32[]{:S(2)}) %collective-permute-start.4) | collective-permute-done | bytes 294944 | tf_op jit(solution)/shard_map/ppermute | solution.py:48
  44.1 3.6 collective-permute-done.6.refs_1_
  47.8 2.7 collective-permute-start.8
  51.4 6.2 collective-permute-done.8.refs_3_
  57.6 4.8 project.3
  63.4 6.3 attend.1.refs_4_.refs_5_
  74.7 7.8 %collective-permute-done.15 = bf16[192,768]{1,0:T(8,128)(2,1)S(1)} collective-permute-done((bf16[192,768]{1,0:T(8,128)(2,1)S(1)}, bf16[192,768]{1,0:T(8,128)(2,1)S(1)}, u32[]{:S(2)}, u32[]{:S(2)}) %collective-permute-start.15) | collective-permute-done | bytes 294944 | tf_op jit(solution)/shard_map/ppermute | solution.py:48
  85.6 9.0 %hidden_before.1 = (f32[1024,768]{1,0:T(8,128)}, f32[1024,768]{1,0:T(8,128)}) custom-call(s32[3]{0:T(128)} %copy-done.57, bf16[512,768]{1,0:T(8,128)(2,1)} %refs_0_.2, bf16[512,768]{1,0:T(8,128)(2,1)} %copy-done.73, bf16[512,768]{1,0:T(8,128)(2,1)} %collective-permute-done.own_ref.refs_2_, bf16[512,768]{1,0:T(8,128)(2,1)} %copy-done.74, ...), custom_call_target="tpu_custom_call" | custom-call | flops 2415919104 | bytes 12582912 | tf_op jit(solution)/shard_map/hidden_before/pallas_call | solution.py:403
  94.6 4.0 collective-permute-done.12.refs_2_
  102.0 9.4 %hidden_after.1 = (f32[1024,768]{1,0:T(8,128)}, bf16[1024,768]{1,0:T(8,128)(2,1)}, bf16[1024,768]{1,0:T(8,128)(2,1)}, f32[1024,1]{1,0:T(8,128)}) custom-call(s32[3]{0:T(128)} %copy-done.57, f32[1024,768]{1,0:T(8,128)} %get-tuple-element.254.refs_0_, f32[1024,768]{1,0:T(8,128)} %get-tuple-element.255.refs_1_, ...), custom_call_target="tpu_custom_call" | custom-call | tf_op jit(solution)/shard_map/hidden_after/pallas_call | solution.py:425
  114.8 9.1 %expert_grads.9 = (bf16[1,1536,384]{2,1,0:T(8,128)(2,1)S(1)}, bf16[1,1536,384]{2,1,0:T(8,128)(2,1)S(1)}, bf16[8,1024,512]{2,1,0:T(8,128)(2,1)}, bf16[8,1024,256]{2,1,0:T(8,128)(2,1)S(1)}) custom-call(s32[63]{0:T(128)S(1)} %get-tuple-element.317.order_ref.plan_ref, bf16[1024,768]{1,0:T(8,128)(2,1)S(1)} %copy-done.2, bf16[1024,768]{1,0:T(8,128)(2,1)S(1)} %copy-done.3, ...), custom_call_target="tpu_custom_call" | custom-call | tf_op jit(solution)/shard_map/expert_grads/pallas_call | solution.py:548
  125.5 8.9 %expert_grads.10 = (bf16[1,1536,384]{2,1,0:T(8,128)(2,1)S(1)}, bf16[1,1536,384]{2,1,0:T(8,128)(2,1)S(1)}, bf16[8,1024,512]{2,1,0:T(8,128)(2,1)}, bf16[8,1024,256]{2,1,0:T(8,128)(2,1)S(1)}) custom-call(s32[63]{0:T(128)S(1)} %get-tuple-element.317.order_ref.plan_ref, bf16[1024,768]{1,0:T(8,128)(2,1)S(1)} %copy-done.2, ...), custom_call_target="tpu_custom_call", output_to_operand_aliasing={{2}: (18, {}), {3}: (19, {})} | custom-call | tf_op jit(solution)/shard_map/expert_grads/pallas_call | solution.py:548
  134.8 8.9 %expert_grads.11 = (bf16[1,1536,384]{2,1,0:T(8,128)(2,1)S(1)}, bf16[1,1536,384]{2,1,0:T(8,128)(2,1)S(1)}, bf16[8,1024,512]{2,1,0:T(8,128)(2,1)}, bf16[8,1024,256]{2,1,0:T(8,128)(2,1)S(1)}) custom-call(s32[63]{0:T(128)S(1)} %get-tuple-element.317.order_ref.plan_ref, bf16[1024,768]{1,0:T(8,128)(2,1)S(1)} %copy-done.2, ...), custom_call_target="tpu_custom_call", output_to_operand_aliasing={{2}: (18, {}), {3}: (19, {})} | custom-call | tf_op jit(solution)/shard_map/expert_grads/pallas_call | solution.py:548
  146.5 9.3 %expert_grads.12 = (bf16[1,1536,384]{2,1,0:T(8,128)(2,1)S(1)}, bf16[1,1536,384]{2,1,0:T(8,128)(2,1)S(1)}, bf16[8,1024,512]{2,1,0:T(8,128)(2,1)}, bf16[8,1024,256]{2,1,0:T(8,128)(2,1)S(1)}) custom-call(s32[63]{0:T(128)S(1)} %get-tuple-element.317.order_ref.plan_ref, bf16[1024,768]{1,0:T(8,128)(2,1)S(1)} %copy-done.2, ...), custom_call_target="tpu_custom_call", output_to_operand_aliasing={{2}: (18, {}), {3}: (19, {})} | custom-call | tf_op jit(solution)/shard_map/expert_grads/pallas_call | solution.py:548
  159.4 8.9 %expert_grads.13 = (bf16[1,1536,384]{2,1,0:T(8,128)(2,1)S(1)}, bf16[1,1536,384]{2,1,0:T(8,128)(2,1)S(1)}, bf16[8,1024,512]{2,1,0:T(8,128)(2,1)}, bf16[8,1024,256]{2,1,0:T(8,128)(2,1)S(1)}) custom-call(s32[63]{0:T(128)S(1)} %get-tuple-element.317.order_ref.plan_ref, bf16[1024,768]{1,0:T(8,128)(2,1)S(1)} %copy-done.2, ...), custom_call_target="tpu_custom_call", output_to_operand_aliasing={{2}: (18, {}), {3}: (19, {})} | custom-call | tf_op jit(solution)/shard_map/expert_grads/pallas_call | solution.py:548
  172.6 8.9 %expert_grads.14 = (bf16[1,1536,384]{2,1,0:T(8,128)(2,1)S(1)}, bf16[1,1536,384]{2,1,0:T(8,128)(2,1)S(1)}, bf16[8,1024,512]{2,1,0:T(8,128)(2,1)}, bf16[8,1024,256]{2,1,0:T(8,128)(2,1)S(1)}) custom-call(s32[63]{0:T(128)S(1)} %get-tuple-element.317.order_ref.plan_ref, bf16[1024,768]{1,0:T(8,128)(2,1)S(1)} %copy-done.2, ...), custom_call_target="tpu_custom_call", output_to_operand_aliasing={{2}: (18, {}), {3}: (19, {})} | custom-call | tf_op jit(solution)/shard_map/expert_grads/pallas_call | solution.py:548
  186.5 9.0 %expert_grads.15 = (bf16[1,1536,384]{2,1,0:T(8,128)(2,1)S(1)}, bf16[1,1536,384]{2,1,0:T(8,128)(2,1)S(1)}, bf16[8,1024,512]{2,1,0:T(8,128)(2,1)}, bf16[8,1024,256]{2,1,0:T(8,128)(2,1)S(1)}) custom-call(s32[63]{0:T(128)S(1)} %get-tuple-element.317.order_ref.plan_ref, bf16[1024,768]{1,0:T(8,128)(2,1)S(1)} %copy-done.2, ...), custom_call_target="tpu_custom_call", output_to_operand_aliasing={{2}: (18, {}), {3}: (19, {})} | custom-call | tf_op jit(solution)/shard_map/expert_grads/pallas_call | solution.py:548
  199.1 8.9 %expert_grads.16 = (bf16[1,1536,384]{2,1,0:T(8,128)(2,1)S(1)}, bf16[1,1536,384]{2,1,0:T(8,128)(2,1)S(1)}, bf16[8,1024,512]{2,1,0:T(8,128)(2,1)}, bf16[8,1024,256]{2,1,0:T(8,128)(2,1)S(1)}) custom-call(s32[63]{0:T(128)S(1)} %get-tuple-element.317.order_ref.plan_ref, bf16[1024,768]{1,0:T(8,128)(2,1)S(1)} %copy-done.2, ...), custom_call_target="tpu_custom_call", output_to_operand_aliasing={{2}: (18, {}), {3}: (19, {})} | custom-call | tf_op jit(solution)/shard_map/expert_grads/pallas_call | solution.py:548
  211.5 8.0 %expert_grads.17 = (bf16[1,1536,384]{2,1,0:T(8,128)(2,1)S(1)}, bf16[1,1536,384]{2,1,0:T(8,128)(2,1)S(1)}, bf16[1,1024,512]{2,1,0:T(8,128)(2,1)S(1)}, bf16[1,1024,256]{2,1,0:T(8,128)(2,1)S(1)}) custom-call(s32[63]{0:T(128)S(1)} %get-tuple-element.317.order_ref.plan_ref, bf16[1024,768]{1,0:T(8,128)(2,1)S(1)} %copy-done.2, bf16[1024,768]{1,0:T(8,128)(2,1)S(1)} %copy-done.4, ...), custom_call_target="tpu_custom_call" | custom-call | tf_op jit(solution)/shard_map/expert_grads/pallas_call | solution.py:548
  223.5 12.5 %mix.4 = bf16[1024,768]{1,0:T(8,128)(2,1)S(1)} custom-call(s32[63]{0:T(128)S(1)} %get-tuple-element.317.order_ref.plan_ref, bf16[8,1024,512]{2,1,0:T(8,128)(2,1)} %get-tuple-element.296.refs_0_, bf16[1,1024,512]{2,1,0:T(8,128)(2,1)S(1)} %get-tuple-element.303.refs_1_, ...), custom_call_target="tpu_custom_call" | custom-call | tf_op jit(solution)/shard_map/mix/pallas_call | solution.py:619
  239.9 12.5 %mix.5 = f32[1024,768]{1,0:T(8,128)S(1)} custom-call(s32[63]{0:T(128)S(1)} %get-tuple-element.317.order_ref.plan_ref, bf16[8,1024,512]{2,1,0:T(8,128)(2,1)} %get-tuple-element.296.refs_0_, bf16[1,1024,512]{2,1,0:T(8,128)(2,1)S(1)} %get-tuple-element.303.refs_1_, bf16[16,768,256]{2,1,0:T(8,128)(2,1)} %refs_16_.1, bf16[16,768,256]{2,1,0:T(8,128)(2,1)} %refs_17_.1, ...), custom_call_target="tpu_custom_call" | custom-call | tf_op jit(solution)/shard_map/mix/pallas_call | solution.py:619
  252.4 11.2 %collective-permute-done.30 = bf16[1,1536,384]{2,1,0:T(8,128)(2,1)} collective-permute-done((bf16[1,1536,384]{2,1,0:T(8,128)(2,1)S(1)}, bf16[1,1536,384]{2,1,0:T(8,128)(2,1)}, u32[]{:S(2)}, u32[]{:S(2)}) %collective-permute-start.30) | collective-permute-done | bytes 1179680 | tf_op jit(solution)/shard_map/ppermute | solution.py:815
  270.6 7.6 %mix.6 = bf16[1024,768]{1,0:T(8,128)(2,1)S(1)} custom-call(s32[63]{0:T(128)S(1)} %get-tuple-element.317.order_ref.plan_ref, bf16[8,1024,256]{2,1,0:T(8,128)(2,1)} %copy-done, bf16[1,1024,256]{2,1,0:T(8,128)(2,1)S(1)} %get-tuple-element.314.refs_1_, ...), custom_call_target="tpu_custom_call" | custom-call | tf_op jit(solution)/shard_map/mix/pallas_call | solution.py:619
  278.3 3.2 add_convert_fusion.4
  281.9 7.3 %mix.7 = f32[1024,768]{1,0:T(8,128)S(1)} custom-call(s32[63]{0:T(128)S(1)} %get-tuple-element.317.order_ref.plan_ref, bf16[8,1024,256]{2,1,0:T(8,128)(2,1)} %copy-done, bf16[1,1024,256]{2,1,0:T(8,128)(2,1)S(1)} %get-tuple-element.314.refs_1_, bf16[16,256,768]{2,1,0:T(8,128)(2,1)} %refs_9_.19, bf16[16,256,768]{2,1,0:T(8,128)(2,1)} %refs_9_.19, ...), custom_call_target="tpu_custom_call" | custom-call | tf_op jit(solution)/shard_map/mix/pallas_call | solution.py:619
  290.9 6.5 collective-permute-done.36
  297.4 3.4 multiply_reduce_fusion
  311.1 12.5 %collective-permute-done.40 = bf16[1,1536,384]{2,1,0:T(8,128)(2,1)S(1)} collective-permute-done((bf16[1,1536,384]{2,1,0:T(8,128)(2,1)S(1)}, bf16[1,1536,384]{2,1,0:T(8,128)(2,1)S(1)}, u32[]{:S(2)}, u32[]{:S(2)}) %collective-permute-start.40) | collective-permute-done | bytes 1179680 | tf_op jit(solution)/shard_map/ppermute | solution.py:815
  324.7 11.7 %attend_back.1.refs_4_ = bf16[1024,640]{1,0:T(8,128)(2,1)S(1)} custom-call(s32[3]{0:T(128)S(1)} %copy-done.58, bf16[512,640]{1,0:T(8,128)(2,1)S(1)} %copy-done.25, bf16[512,640]{1,0:T(8,128)(2,1)S(1)} %copy-done.27, bf16[1024,768]{1,0:T(8,128)(2,1)} %copy-done.5, bf16[1024,768]{1,0:T(8,128)(2,1)} %copy-done.16, bf16[768,768]{1,0:T(8,128)(2,1)} %out_ref.1, ...), custom_call_target="tpu_custom_call" | custom-call | tf_op jit(solution)/shard_map/attend_back/pallas_call | solution.py:166
  344.4 3.3 unpack.16
  347.7 7.5 %collective-permute-done.43.refs_0_ = bf16[1,768,384]{2,1,0:T(8,128)(2,1)} collective-permute-done((bf16[1,768,384]{2,1,0:T(8,128)(2,1)}, bf16[1,768,384]{2,1,0:T(8,128)(2,1)}, u32[]{:S(2)}, u32[]{:S(2)}) %collective-permute-start.43) | collective-permute-done | bytes 589856 | tf_op jit(solution)/shard_map/ppermute | solution.py:815
  369.0 9.4 %late_grads.1 = (bf16[2,768,896]{2,1,0:T(8,128)(2,1)S(1)}, bf16[2,768,896]{2,1,0:T(8,128)(2,1)}) custom-call(s32[3]{0:T(128)S(1)} %copy-done.58, bf16[512,768]{1,0:T(8,128)(2,1)S(1)} %copy-done.47, bf16[512,768]{1,0:T(8,128)(2,1)S(1)} %copy-done.48, bf16[512,768]{1,0:T(8,128)(2,1)S(1)} %copy-done.49, bf16[512,768]{1,0:T(8,128)(2,1)S(1)} %copy-done.50, ...), custom_call_target="tpu_custom_call" | custom-call | tf_op jit(solution)/shard_map/late_grads/pallas_call | solution.py:217
  399.5 3.5 unpack.17
  451.6 3.4 unpack.18
  461.6 3.3 unpack.19
  464.9 4.0 collective-permute-done.49.refs_0_
  469.8 6.5 collective-permute-done.53
  476.4 3.2 collective-permute-start.63
  485.7 3.3 collective-permute-done.62.refs_0_
  489.2 7.1 collective-permute-done.61
  504.4 9.3 %collective-permute-done.65.refs_0_ = bf16[1,768,384]{2,1,0:T(8,128)(2,1)S(1)} collective-permute-done((bf16[1,768,384]{2,1,0:T(8,128)(2,1)S(1)}, bf16[1,768,384]{2,1,0:T(8,128)(2,1)S(1)}, u32[]{:S(2)}, u32[]{:S(2)}) %collective-permute-start.65) | collective-permute-done | bytes 589856 | tf_op jit(solution)/shard_map/ppermute | solution.py:815
  513.7 6.2 collective-permute-done.64
  524.8 6.0 collective-permute-done.67
  537.0 5.1 collective-permute-done.72.refs_0_
  543.2 4.0 collective-permute-done.73.refs_1_
  555.9 6.3 collective-permute-done.70
  567.9 7.8 %collective-permute-done.55 = bf16[512,768]{1,0:T(8,128)(2,1)S(1)} collective-permute-done((bf16[512,768]{1,0:T(8,128)(2,1)S(1)}, bf16[512,768]{1,0:T(8,128)(2,1)S(1)}, u32[]{:S(2)}, u32[]{:S(2)}) %collective-permute-start.55) | collective-permute-done | bytes 786464 | tf_op jit(solution)/shard_map/ppermute | solution.py:48
  581.3 7.4 %collective-permute-done.83 = bf16[2,96,896]{2,1,0:T(8,128)(2,1)S(1)} collective-permute-done((bf16[2,96,896]{2,1,0:T(8,128)(2,1)S(1)}, bf16[2,96,896]{2,1,0:T(8,128)(2,1)S(1)}, u32[]{:S(2)}, u32[]{:S(2)}) %collective-permute-start.83) | collective-permute-done | bytes 344096 | tf_op jit(solution)/shard_map/ppermute | solution.py:815
  591.2 9.9 %collective-permute-done.58 = f32[2,768]{1,0:T(2,128)S(1)} collective-permute-done((f32[2,768]{1,0:T(2,128)S(1)}, f32[2,768]{1,0:T(2,128)S(1)}, u32[]{:S(2)}, u32[]{:S(2)}) %collective-permute-start.58) | collective-permute-done | bytes 6176 | tf_op jit(solution)/shard_map/ppermute | solution.py:1148
  610.9 2.9 collective-permute-start.91
  620.0 7.9 %collective-permute-done.90.refs_0_ = bf16[1,768,384]{2,1,0:T(8,128)(2,1)S(1)} collective-permute-done((bf16[1,768,384]{2,1,0:T(8,128)(2,1)S(1)}, bf16[1,768,384]{2,1,0:T(8,128)(2,1)S(1)}, u32[]{:S(2)}, u32[]{:S(2)}) %collective-permute-start.90) | collective-permute-done | bytes 589856 | tf_op jit(solution)/shard_map/ppermute | solution.py:815
  627.9 5.3 collective-permute-done.89
  633.2 3.5 collective-permute-start.94
  638.9 14.2 %collective-permute-done.105 = bf16[2,96,896]{2,1,0:T(8,128)(2,1)S(1)} collective-permute-done((bf16[2,96,896]{2,1,0:T(8,128)(2,1)S(1)}, bf16[2,96,896]{2,1,0:T(8,128)(2,1)S(1)}, u32[]{:S(2)}, u32[]{:S(2)}) %collective-permute-start.105) | collective-permute-done | bytes 344096 | tf_op jit(solution)/shard_map/ppermute | solution.py:815
  664.2 7.6 %collective-permute-done.96.refs_0_ = bf16[1,768,384]{2,1,0:T(8,128)(2,1)S(1)} collective-permute-done((bf16[1,768,384]{2,1,0:T(8,128)(2,1)S(1)}, bf16[1,768,384]{2,1,0:T(8,128)(2,1)S(1)}, u32[]{:S(2)}, u32[]{:S(2)}) %collective-permute-start.96) | collective-permute-done | bytes 589856 | tf_op jit(solution)/shard_map/ppermute | solution.py:815
  673.5 5.6 collective-permute-done.95
  684.4 5.8 collective-permute-done.99.refs_0_
  690.3 5.2 collective-permute-done.100.refs_1_
  700.8 6.6 collective-permute-done.101
  708.2 4.8 unpack_late.1
  (472 shorter events, 220.6 us)
Async XLA Ops:
  0.7 36.9 %collective-permute-start.17 = (bf16[16,768,256]{2,1,0:T(8,128)(2,1)}, bf16[16,768,256]{2,1,0:T(8,128)(2,1)}, u32[]{:S(2)}, u32[]{:S(2)}) collective-permute-start(bf16[16,768,256]{2,1,0:T(8,128)(2,1)} %refs_16_.1), channel_id=1, source_target_pairs={{0,1},{1,0},{2,3},{3,2},{4,5},{5,4},{6,7},{7,6},{8,9},{9,8},{10,11... | collective-permute-start | bytes 18874376 | tf_op jit(solution)/shard_map/ppermute | solution.py:48
  7.9 27.1 %collective-permute-start = (bf16[512,768]{1,0:T(8,128)(2,1)S(1)}, bf16[512,768]{1,0:T(8,128)(2,1)}, u32[]{:S(2)}, u32[]{:S(2)}) collective-permute-start(bf16[512,768]{1,0:T(8,128)(2,1)S(1)} %copy-done.64), channel_id=1, source_target_pairs={{0,2},{2,0},{1,3},{3,1},{4,6},{6,4},{5,7},{7,5},{8,10},{10,8},{9,1... | collective-permute-start | bytes 2359304 | tf_op jit(solution)/shard_map/ppermute | solution.py:48
  13.7 21.2 %collective-permute-start.4 = (bf16[192,768]{1,0:T(8,128)(2,1)}, bf16[192,768]{1,0:T(8,128)(2,1)S(1)}, u32[]{:S(2)}, u32[]{:S(2)}) collective-permute-start(bf16[192,768]{1,0:T(8,128)(2,1)} %get-tuple-element.248), channel_id=1, source_target_pairs={{0,2},{2,0},{1,3},{3,1},{4,6},{6,4},{5,7},{7,5},{8,10},{10,8},{9,1... | collective-permute-start | bytes 884744 | tf_op jit(solution)/shard_map/ppermute | solution.py:48
  37.4 74.0 %collective-permute-start.19 = (bf16[16,256,768]{2,1,0:T(8,128)(2,1)}, bf16[16,256,768]{2,1,0:T(8,128)(2,1)}, u32[]{:S(2)}, u32[]{:S(2)}) collective-permute-start(bf16[16,256,768]{2,1,0:T(8,128)(2,1)} %refs_9_.19), channel_id=1, source_target_pairs={{0,1},{1,0},{2,3},{3,2},{4,5},{5,4},{6,7},{7,6},{8,9},{9,8},{10,11... | collective-permute-start | bytes 18874376 | tf_op jit(solution)/shard_map/ppermute | solution.py:48
  38.3 73.1 %collective-permute-start.18 = (bf16[16,768,256]{2,1,0:T(8,128)(2,1)}, bf16[16,768,256]{2,1,0:T(8,128)(2,1)}, u32[]{:S(2)}, u32[]{:S(2)}) collective-permute-start(bf16[16,768,256]{2,1,0:T(8,128)(2,1)} %refs_17_.1), channel_id=1, source_target_pairs={{0,1},{1,0},{2,3},{3,2},{4,5},{5,4},{6,7},{7,6},{8,9},{9,8},{10,11... | collective-permute-start | bytes 18874376 | tf_op jit(solution)/shard_map/ppermute | solution.py:48
  74.0 24.7 %collective-permute-start.12 = (bf16[1024,384]{1,0:T(8,128)(2,1)}, bf16[1024,384]{1,0:T(8,128)(2,1)}, u32[]{:S(2)}, u32[]{:S(2)}) collective-permute-start(bf16[1024,384]{1,0:T(8,128)(2,1)} %attend.1.refs_4_.refs_5_), channel_id=1, source_target_pairs={{0,2},{2,0},{1,3},{3,1},{4,6},{6,4},{5,7},{7,5},{8,10},{10,8},{9,1... | collective-permute-start | bytes 2359304 | tf_op jit(solution)/shard_map/ppermute | solution.py:48
  82.7 28.8 %collective-permute-start.16 = (bf16[1024,768]{1,0:T(8,128)(2,1)S(1)}, bf16[1024,768]{1,0:T(8,128)(2,1)S(1)}, u32[]{:S(2)}, u32[]{:S(2)}) collective-permute-start(bf16[1024,768]{1,0:T(8,128)(2,1)S(1)} %join.3.refs_2_), channel_id=1, source_target_pairs={{0,1},{1,0},{2,3},{3,2},{4,5},{5,4},{6,7},{7,6},{8,9},{9,8},{10,11... | collective-permute-start | bytes 4718600 | tf_op jit(solution)/shard_map/ppermute | solution.py:48
  123.9 19.8 %collective-permute-start.20 = (bf16[1,1536,384]{2,1,0:T(8,128)(2,1)S(1)}, bf16[1,1536,384]{2,1,0:T(8,128)(2,1)S(1)}, u32[]{:S(2)}, u32[]{:S(2)}) collective-permute-start(bf16[1,1536,384]{2,1,0:T(8,128)(2,1)S(1)} %get-tuple-element.263), channel_id=1, source_target_pairs={{0,8},{8,16},{16,24},{24,28},{28,20},{20,12},{12,4},{4,0},{9,1},{1... | collective-permute-start | bytes 3538952 | tf_op jit(solution)/shard_map/ppermute | solution.py:815
  134.4 23.2 %collective-permute-start.22 = (bf16[1,1536,384]{2,1,0:T(8,128)(2,1)S(1)}, bf16[1,1536,384]{2,1,0:T(8,128)(2,1)S(1)}, u32[]{:S(2)}, u32[]{:S(2)}) collective-permute-start(bf16[1,1536,384]{2,1,0:T(8,128)(2,1)S(1)} %get-tuple-element.273), channel_id=1, source_target_pairs={{8,0},{16,8},{24,16},{28,24},{20,28},{12,20},{4,12},{0,4},{1,9},{9... | collective-permute-start | bytes 3538952 | tf_op jit(solution)/shard_map/ppermute | solution.py:815
  144.0 25.8 %collective-permute-start.21 = (bf16[1,1536,384]{2,1,0:T(8,128)(2,1)S(1)}, bf16[1,1536,384]{2,1,0:T(8,128)(2,1)S(1)}, u32[]{:S(2)}, u32[]{:S(2)}) collective-permute-start(bf16[1,1536,384]{2,1,0:T(8,128)(2,1)S(1)} %add_convert_fusion.13), channel_id=1, source_target_pairs={{0,8},{8,16},{16,24},{24,28},{28,20},{20,12},{12,4},{4,0},{9,1},{1... | collective-permute-start | bytes 3538952 | tf_op jit(solution)/shard_map/ppermute | solution.py:815
  157.9 25.8 %collective-permute-start.24 = (bf16[1,1536,384]{2,1,0:T(8,128)(2,1)S(1)}, bf16[1,1536,384]{2,1,0:T(8,128)(2,1)S(1)}, u32[]{:S(2)}, u32[]{:S(2)}) collective-permute-start(bf16[1,1536,384]{2,1,0:T(8,128)(2,1)S(1)} %add_convert_fusion.12), channel_id=1, source_target_pairs={{8,0},{16,8},{24,16},{28,24},{20,28},{12,20},{4,12},{0,4},{1,9},{9... | collective-permute-start | bytes 3538952 | tf_op jit(solution)/shard_map/ppermute | solution.py:815
  170.2 25.4 %collective-permute-start.23 = (bf16[1,1536,384]{2,1,0:T(8,128)(2,1)S(1)}, bf16[1,1536,384]{2,1,0:T(8,128)(2,1)S(1)}, u32[]{:S(2)}, u32[]{:S(2)}) collective-permute-start(bf16[1,1536,384]{2,1,0:T(8,128)(2,1)S(1)} %add_convert_fusion.11), channel_id=1, source_target_pairs={{0,8},{8,16},{16,24},{24,28},{28,20},{20,12},{12,4},{4,0},{9,1},{1... | collective-permute-start | bytes 3538952 | tf_op jit(solution)/shard_map/ppermute | solution.py:815
  185.0 24.0 %collective-permute-start.26 = (bf16[1,1536,384]{2,1,0:T(8,128)(2,1)}, bf16[1,1536,384]{2,1,0:T(8,128)(2,1)S(1)}, u32[]{:S(2)}, u32[]{:S(2)}) collective-permute-start(bf16[1,1536,384]{2,1,0:T(8,128)(2,1)} %add_convert_fusion.10), channel_id=1, source_target_pairs={{8,0},{16,8},{24,16},{28,24},{20,28},{12,20},{4,12},{0,4},{1,9},{9... | collective-permute-start | bytes 3538952 | tf_op jit(solution)/shard_map/ppermute | solution.py:815
  197.0 24.7 %collective-permute-start.25 = (bf16[1,1536,384]{2,1,0:T(8,128)(2,1)}, bf16[1,1536,384]{2,1,0:T(8,128)(2,1)}, u32[]{:S(2)}, u32[]{:S(2)}) collective-permute-start(bf16[1,1536,384]{2,1,0:T(8,128)(2,1)} %add_convert_fusion.9), channel_id=1, source_target_pairs={{0,8},{8,16},{16,24},{24,28},{28,20},{20,12},{12,4},{4,0},{9,1},{1... | collective-permute-start | bytes 3538952 | tf_op jit(solution)/shard_map/ppermute | solution.py:815
  210.4 27.7 %collective-permute-start.31 = (bf16[1,1536,384]{2,1,0:T(8,128)(2,1)}, bf16[1,1536,384]{2,1,0:T(8,128)(2,1)S(1)}, u32[]{:S(2)}, u32[]{:S(2)}) collective-permute-start(bf16[1,1536,384]{2,1,0:T(8,128)(2,1)} %add_convert_fusion.8), channel_id=1, source_target_pairs={{8,0},{16,8},{24,16},{28,24},{20,28},{12,20},{4,12},{0,4},{1,9},{9... | collective-permute-start | bytes 3538952 | tf_op jit(solution)/shard_map/ppermute | solution.py:815
  235.9 27.7 %collective-permute-start.35 = (bf16[1024,768]{1,0:T(8,128)(2,1)S(1)}, bf16[1024,768]{1,0:T(8,128)(2,1)S(1)}, u32[]{:S(2)}, u32[]{:S(2)}) collective-permute-start(bf16[1024,768]{1,0:T(8,128)(2,1)S(1)} %mix.4), channel_id=1, source_target_pairs={{0,1},{1,0},{2,3},{3,2},{4,5},{5,4},{6,7},{7,6},{8,9},{9,8},{10,11... | collective-permute-start | bytes 4718600 | tf_op jit(solution)/shard_map/ppermute | solution.py:48
  236.5 27.1 %collective-permute-start.30 = (bf16[1,1536,384]{2,1,0:T(8,128)(2,1)S(1)}, bf16[1,1536,384]{2,1,0:T(8,128)(2,1)}, u32[]{:S(2)}, u32[]{:S(2)}) collective-permute-start(bf16[1,1536,384]{2,1,0:T(8,128)(2,1)S(1)} %add_convert_fusion.7), channel_id=1, source_target_pairs={{0,8},{8,16},{16,24},{24,28},{28,20},{20,12},{12,4},{4,0},{9,1},{1... | collective-permute-start | bytes 3538952 | tf_op jit(solution)/shard_map/ppermute | solution.py:815
  239.4 38.8 %collective-permute-start.32 = (bf16[1,1536,384]{2,1,0:T(8,128)(2,1)}, bf16[1,1536,384]{2,1,0:T(8,128)(2,1)}, u32[]{:S(2)}, u32[]{:S(2)}) collective-permute-start(bf16[1,1536,384]{2,1,0:T(8,128)(2,1)} %add_convert_fusion.6), channel_id=1, source_target_pairs={{8,0},{16,8},{24,16},{28,24},{20,28},{12,20},{4,12},{0,4},{1,9},{9... | collective-permute-start | bytes 3538952 | tf_op jit(solution)/shard_map/ppermute | solution.py:815
  264.0 33.4 %collective-permute-start.36 = (bf16[1024,768]{1,0:T(8,128)(2,1)S(1)}, bf16[1024,768]{1,0:T(8,128)(2,1)}, u32[]{:S(2)}, u32[]{:S(2)}) collective-permute-start(bf16[1024,768]{1,0:T(8,128)(2,1)S(1)} %fusion), channel_id=1, source_target_pairs={{0,2},{2,0},{1,3},{3,1},{4,6},{6,4},{5,7},{7,5},{8,10},{10,8},{9,1... | collective-permute-start | bytes 4718600 | tf_op jit(solution)/shard_map/ppermute | solution.py:48
  268.0 22.9 %collective-permute-start.39 = (bf16[1,1536,384]{2,1,0:T(8,128)(2,1)}, bf16[1,1536,384]{2,1,0:T(8,128)(2,1)S(1)}, u32[]{:S(2)}, u32[]{:S(2)}) collective-permute-start(bf16[1,1536,384]{2,1,0:T(8,128)(2,1)} %add_convert_fusion.5), channel_id=1, source_target_pairs={{0,8},{8,16},{16,24},{24,28},{28,20},{20,12},{12,4},{4,0},{9,1},{1... | collective-permute-start | bytes 3538952 | tf_op jit(solution)/shard_map/ppermute | solution.py:815
  281.5 21.5 %collective-permute-start.41 = (bf16[1,1536,384]{2,1,0:T(8,128)(2,1)}, bf16[1,1536,384]{2,1,0:T(8,128)(2,1)}, u32[]{:S(2)}, u32[]{:S(2)}) collective-permute-start(bf16[1,1536,384]{2,1,0:T(8,128)(2,1)} %add_convert_fusion.4), channel_id=1, source_target_pairs={{8,0},{16,8},{24,16},{28,24},{20,28},{12,20},{4,12},{0,4},{1,9},{9... | collective-permute-start | bytes 3538952 | tf_op jit(solution)/shard_map/ppermute | solution.py:815
  301.3 22.3 %collective-permute-start.40 = (bf16[1,1536,384]{2,1,0:T(8,128)(2,1)S(1)}, bf16[1,1536,384]{2,1,0:T(8,128)(2,1)S(1)}, u32[]{:S(2)}, u32[]{:S(2)}) collective-permute-start(bf16[1,1536,384]{2,1,0:T(8,128)(2,1)S(1)} %add_convert_fusion.3), channel_id=1, source_target_pairs={{0,8},{8,16},{16,24},{24,28},{28,20},{20,12},{12,4},{4,0},{9,1},{1... | collective-permute-start | bytes 3538952 | tf_op jit(solution)/shard_map/ppermute | solution.py:815
  308.6 27.9 %collective-permute-start.42 = (bf16[1,1536,384]{2,1,0:T(8,128)(2,1)S(1)}, bf16[1,1536,384]{2,1,0:T(8,128)(2,1)S(1)}, u32[]{:S(2)}, u32[]{:S(2)}) collective-permute-start(bf16[1,1536,384]{2,1,0:T(8,128)(2,1)S(1)} %add_convert_fusion.1), channel_id=1, source_target_pairs={{8,0},{16,8},{24,16},{28,24},{20,28},{12,20},{4,12},{0,4},{1,9},{9... | collective-permute-start | bytes 3538952 | tf_op jit(solution)/shard_map/ppermute | solution.py:815
  341.7 39.0 %collective-permute-start.45 = (bf16[1,768,384]{2,1,0:T(8,128)(2,1)}, bf16[1,768,384]{2,1,0:T(8,128)(2,1)}, u32[]{:S(2)}, u32[]{:S(2)}) collective-permute-start(bf16[1,768,384]{2,1,0:T(8,128)(2,1)} %get-tuple-element.329.refs_1_), channel_id=1, source_target_pairs={{8,0},{16,8},{24,16},{28,24},{20,28},{12,20},{4,12},{0,4},{1,9},{9... | collective-permute-start | bytes 1769480 | tf_op jit(solution)/shard_map/ppermute | solution.py:815
  355.2 47.9 %collective-permute-start.44 = (bf16[1,768,384]{2,1,0:T(8,128)(2,1)}, bf16[1,768,384]{2,1,0:T(8,128)(2,1)}, u32[]{:S(2)}, u32[]{:S(2)}) collective-permute-start(bf16[1,768,384]{2,1,0:T(8,128)(2,1)} %collective-permute-done.43.refs_0_), channel_id=1, source_target_pairs={{0,8},{8,16},{16,24},{24,28},{28,20},{20,12},{12,4},{4,0},{9,1},{1... | collective-permute-start | bytes 1769480 | tf_op jit(solution)/shard_map/ppermute | solution.py:815
  380.7 24.4 %collective-permute-start.47 = (bf16[1,768,384]{2,1,0:T(8,128)(2,1)}, bf16[1,768,384]{2,1,0:T(8,128)(2,1)S(1)}, u32[]{:S(2)}, u32[]{:S(2)}) collective-permute-start(bf16[1,768,384]{2,1,0:T(8,128)(2,1)} %collective-permute-done.45.refs_1_), channel_id=1, source_target_pairs={{8,0},{16,8},{24,16},{28,24},{20,28},{12,20},{4,12},{0,4},{1,9},{9... | collective-permute-start | bytes 1769480 | tf_op jit(solution)/shard_map/ppermute | solution.py:815
  382.5 20.7 %collective-permute-start.48 = (bf16[2,96,896]{2,1,0:T(8,128)(2,1)}, bf16[2,96,896]{2,1,0:T(8,128)(2,1)}, u32[]{:S(2)}, u32[]{:S(2)}) collective-permute-start(bf16[2,96,896]{2,1,0:T(8,128)(2,1)} %dynamic-slice_bitcast_fusion.1), channel_id=1, source_target_pairs={{0,8},{8,16},{16,24},{24,28},{28,20},{20,12},{12,4},{4,0},{9,1},{1... | collective-permute-start | bytes 1032200 | tf_op jit(solution)/shard_map/ppermute | solution.py:815
  384.4 22.7 %collective-permute-start.74 = (bf16[2,96,896]{2,1,0:T(8,128)(2,1)}, bf16[2,96,896]{2,1,0:T(8,128)(2,1)}, u32[]{:S(2)}, u32[]{:S(2)}) collective-permute-start(bf16[2,96,896]{2,1,0:T(8,128)(2,1)} %dynamic-slice_bitcast_fusion), channel_id=1, source_target_pairs={{8,0},{16,8},{24,16},{28,24},{20,28},{12,20},{4,12},{0,4},{1,9},{9... | collective-permute-start | bytes 1032200 | tf_op jit(solution)/shard_map/ppermute | solution.py:815
  403.1 51.9 %collective-permute-start.46 = (bf16[1,768,384]{2,1,0:T(8,128)(2,1)}, bf16[1,768,384]{2,1,0:T(8,128)(2,1)}, u32[]{:S(2)}, u32[]{:S(2)}) collective-permute-start(bf16[1,768,384]{2,1,0:T(8,128)(2,1)} %collective-permute-done.44.refs_0_), channel_id=1, source_target_pairs={{0,8},{8,16},{16,24},{24,28},{28,20},{20,12},{12,4},{4,0},{9,1},{1... | collective-permute-start | bytes 1769480 | tf_op jit(solution)/shard_map/ppermute | solution.py:815
  405.1 51.2 %collective-permute-start.50 = (bf16[1,768,384]{2,1,0:T(8,128)(2,1)S(1)}, bf16[1,768,384]{2,1,0:T(8,128)(2,1)}, u32[]{:S(2)}, u32[]{:S(2)}) collective-permute-start(bf16[1,768,384]{2,1,0:T(8,128)(2,1)S(1)} %collective-permute-done.47.refs_1_), channel_id=1, source_target_pairs={{8,0},{16,8},{24,16},{28,24},{20,28},{12,20},{4,12},{0,4},{1,9},{9... | collective-permute-start | bytes 1769480 | tf_op jit(solution)/shard_map/ppermute | solution.py:815
  406.9 48.2 %collective-permute-start.51 = (bf16[2,96,896]{2,1,0:T(8,128)(2,1)}, bf16[2,96,896]{2,1,0:T(8,128)(2,1)}, u32[]{:S(2)}, u32[]{:S(2)}) collective-permute-start(bf16[2,96,896]{2,1,0:T(8,128)(2,1)} %fusion.27), channel_id=1, source_target_pairs={{0,8},{8,16},{16,24},{24,28},{28,20},{20,12},{12,4},{4,0},{9,1},{1... | collective-permute-start | bytes 1032200 | tf_op jit(solution)/shard_map/ppermute | solution.py:815
  409.0 49.3 %collective-permute-start.75 = (bf16[2,96,896]{2,1,0:T(8,128)(2,1)}, bf16[2,96,896]{2,1,0:T(8,128)(2,1)}, u32[]{:S(2)}, u32[]{:S(2)}) collective-permute-start(bf16[2,96,896]{2,1,0:T(8,128)(2,1)} %fusion.20), channel_id=1, source_target_pairs={{8,0},{16,8},{24,16},{28,24},{20,28},{12,20},{4,12},{0,4},{1,9},{9... | collective-permute-start | bytes 1032200 | tf_op jit(solution)/shard_map/ppermute | solution.py:815
  451.5 48.4 %collective-permute-start.33 = (bf16[1024,768]{1,0:T(8,128)(2,1)}, bf16[1024,768]{1,0:T(8,128)(2,1)S(1)}, u32[]{:S(2)}, u32[]{:S(2)}) collective-permute-start(bf16[1024,768]{1,0:T(8,128)(2,1)} %copy-done.28), channel_id=1, source_target_pairs={{0,1},{1,0},{2,3},{3,2},{4,5},{5,4},{6,7},{7,6},{8,9},{9,8},{10,11... | collective-permute-start | bytes 4718600 | tf_op jit(solution)/shard_map/ppermute | solution.py:48
  456.2 20.2 %collective-permute-start.52 = (bf16[1,768,384]{2,1,0:T(8,128)(2,1)}, bf16[1,768,384]{2,1,0:T(8,128)(2,1)S(1)}, u32[]{:S(2)}, u32[]{:S(2)}) collective-permute-start(bf16[1,768,384]{2,1,0:T(8,128)(2,1)} %collective-permute-done.50.refs_1_), channel_id=1, source_target_pairs={{8,0},{16,8},{24,16},{28,24},{20,28},{12,20},{4,12},{0,4},{1,9},{9... | collective-permute-start | bytes 1769480 | tf_op jit(solution)/shard_map/ppermute | solution.py:815
  458.2 18.1 %collective-permute-start.53 = (bf16[2,96,896]{2,1,0:T(8,128)(2,1)S(1)}, bf16[2,96,896]{2,1,0:T(8,128)(2,1)S(1)}, u32[]{:S(2)}, u32[]{:S(2)}) collective-permute-start(bf16[2,96,896]{2,1,0:T(8,128)(2,1)S(1)} %fusion.26), channel_id=1, source_target_pairs={{0,8},{8,16},{16,24},{24,28},{28,20},{20,12},{12,4},{4,0},{9,1},{1... | collective-permute-start | bytes 1032200 | tf_op jit(solution)/shard_map/ppermute | solution.py:815
  459.4 20.7 %collective-permute-start.76 = (bf16[2,96,896]{2,1,0:T(8,128)(2,1)S(1)}, bf16[2,96,896]{2,1,0:T(8,128)(2,1)S(1)}, u32[]{:S(2)}, u32[]{:S(2)}) collective-permute-start(bf16[2,96,896]{2,1,0:T(8,128)(2,1)S(1)} %fusion.19), channel_id=1, source_target_pairs={{8,0},{16,8},{24,16},{28,24},{20,28},{12,20},{4,12},{0,4},{1,9},{9... | collective-permute-start | bytes 1032200 | tf_op jit(solution)/shard_map/ppermute | solution.py:815
  468.9 20.0 %collective-permute-start.62 = (bf16[1,768,384]{2,1,0:T(8,128)(2,1)S(1)}, bf16[1,768,384]{2,1,0:T(8,128)(2,1)S(1)}, u32[]{:S(2)}, u32[]{:S(2)}) collective-permute-start(bf16[1,768,384]{2,1,0:T(8,128)(2,1)S(1)} %collective-permute-done.49.refs_0_), channel_id=1, source_target_pairs={{0,8},{8,16},{16,24},{24,28},{28,20},{20,12},{12,4},{4,0},{9,1},{1... | collective-permute-start | bytes 1769480 | tf_op jit(solution)/shard_map/ppermute | solution.py:815
  476.4 20.7 %collective-permute-start.63 = (bf16[1,768,384]{2,1,0:T(8,128)(2,1)S(1)}, bf16[1,768,384]{2,1,0:T(8,128)(2,1)S(1)}, u32[]{:S(2)}, u32[]{:S(2)}) collective-permute-start(bf16[1,768,384]{2,1,0:T(8,128)(2,1)S(1)} %collective-permute-done.52.refs_1_), channel_id=1, source_target_pairs={{8,0},{16,8},{24,16},{28,24},{20,28},{12,20},{4,12},{0,4},{1,9},{9... | collective-permute-start | bytes 1769480 | tf_op jit(solution)/shard_map/ppermute | solution.py:815
  489.0 45.0 %collective-permute-start.54 = (bf16[1024,768]{1,0:T(8,128)(2,1)S(1)}, bf16[1024,768]{1,0:T(8,128)(2,1)S(1)}, u32[]{:S(2)}, u32[]{:S(2)}) collective-permute-start(bf16[1024,768]{1,0:T(8,128)(2,1)S(1)} %convolution_convert_fusion), channel_id=1, source_target_pairs={{0,1},{1,0},{2,3},{3,2},{4,5},{5,4},{6,7},{7,6},{8,9},{9,8},{10,11... | collective-permute-start | bytes 4718600 | tf_op jit(solution)/shard_map/ppermute | solution.py:48
  497.2 22.9 %collective-permute-start.66 = (bf16[1,768,384]{2,1,0:T(8,128)(2,1)S(1)}, bf16[1,768,384]{2,1,0:T(8,128)(2,1)S(1)}, u32[]{:S(2)}, u32[]{:S(2)}) collective-permute-start(bf16[1,768,384]{2,1,0:T(8,128)(2,1)S(1)} %collective-permute-done.63.refs_1_), channel_id=1, source_target_pairs={{8,0},{16,8},{24,16},{28,24},{20,28},{12,20},{4,12},{0,4},{1,9},{9... | collective-permute-start | bytes 1769480 | tf_op jit(solution)/shard_map/ppermute | solution.py:815
  499.7 20.3 %collective-permute-start.64 = (bf16[2,96,896]{2,1,0:T(8,128)(2,1)S(1)}, bf16[2,96,896]{2,1,0:T(8,128)(2,1)S(1)}, u32[]{:S(2)}, u32[]{:S(2)}) collective-permute-start(bf16[2,96,896]{2,1,0:T(8,128)(2,1)S(1)} %fusion.24), channel_id=1, source_target_pairs={{0,8},{8,16},{16,24},{24,28},{28,20},{20,12},{12,4},{4,0},{9,1},{1... | collective-permute-start | bytes 1032200 | tf_op jit(solution)/shard_map/ppermute | solution.py:815
  499.9 20.5 %collective-permute-start.78 = (bf16[2,96,896]{2,1,0:T(8,128)(2,1)S(1)}, bf16[2,96,896]{2,1,0:T(8,128)(2,1)S(1)}, u32[]{:S(2)}, u32[]{:S(2)}) collective-permute-start(bf16[2,96,896]{2,1,0:T(8,128)(2,1)S(1)} %fusion.17), channel_id=1, source_target_pairs={{8,0},{16,8},{24,16},{28,24},{20,28},{12,20},{4,12},{0,4},{1,9},{9... | collective-permute-start | bytes 1032200 | tf_op jit(solution)/shard_map/ppermute | solution.py:815
  530.8 24.0 %collective-permute-start.71 = (bf16[1,768,384]{2,1,0:T(8,128)(2,1)S(1)}, bf16[1,768,384]{2,1,0:T(8,128)(2,1)S(1)}, u32[]{:S(2)}, u32[]{:S(2)}) collective-permute-start(bf16[1,768,384]{2,1,0:T(8,128)(2,1)S(1)} %collective-permute-done.68.refs_0_), channel_id=1, source_target_pairs={{0,8},{8,16},{16,24},{24,28},{28,20},{20,12},{12,4},{4,0},{9,1},{1... | collective-permute-start | bytes 1769480 | tf_op jit(solution)/shard_map/ppermute | solution.py:815
  533.0 29.4 %collective-permute-start.81 = (bf16[1,768,384]{2,1,0:T(8,128)(2,1)S(1)}, bf16[1,768,384]{2,1,0:T(8,128)(2,1)S(1)}, u32[]{:S(2)}, u32[]{:S(2)}) collective-permute-start(bf16[1,768,384]{2,1,0:T(8,128)(2,1)S(1)} %collective-permute-done.69.refs_1_), channel_id=1, source_target_pairs={{8,0},{16,8},{24,16},{28,24},{20,28},{12,20},{4,12},{0,4},{1,9},{9... | collective-permute-start | bytes 1769480 | tf_op jit(solution)/shard_map/ppermute | solution.py:815
  533.9 28.2 %collective-permute-start.70 = (bf16[2,96,896]{2,1,0:T(8,128)(2,1)S(1)}, bf16[2,96,896]{2,1,0:T(8,128)(2,1)S(1)}, u32[]{:S(2)}, u32[]{:S(2)}) collective-permute-start(bf16[2,96,896]{2,1,0:T(8,128)(2,1)S(1)} %fusion.22), channel_id=1, source_target_pairs={{0,8},{8,16},{16,24},{24,28},{28,20},{20,12},{12,4},{4,0},{9,1},{1... | collective-permute-start | bytes 1032200 | tf_op jit(solution)/shard_map/ppermute | solution.py:815
  542.1 22.0 %collective-permute-start.34 = (bf16[512,768]{1,0:T(8,128)(2,1)S(1)}, bf16[512,768]{1,0:T(8,128)(2,1)S(1)}, u32[]{:S(2)}, u32[]{:S(2)}) collective-permute-start(bf16[512,768]{1,0:T(8,128)(2,1)S(1)} %dynamic-slice_convert_fusion.1), channel_id=1, source_target_pairs={{0,2},{2,0},{1,3},{3,1},{4,6},{6,4},{5,7},{7,5},{8,10},{10,8},{9,1... | collective-permute-start | bytes 2359304 | tf_op jit(solution)/shard_map/ppermute | solution.py:48
  554.7 20.9 %collective-permute-start.55 = (bf16[512,768]{1,0:T(8,128)(2,1)S(1)}, bf16[512,768]{1,0:T(8,128)(2,1)S(1)}, u32[]{:S(2)}, u32[]{:S(2)}) collective-permute-start(bf16[512,768]{1,0:T(8,128)(2,1)S(1)} %dynamic-slice_convert_fusion), channel_id=1, source_target_pairs={{0,2},{2,0},{1,3},{3,1},{4,6},{6,4},{5,7},{7,5},{8,10},{10,8},{9,1... | collective-permute-start | bytes 2359304 | tf_op jit(solution)/shard_map/ppermute | solution.py:48
  565.7 23.0 %collective-permute-start.85 = (bf16[1,768,384]{2,1,0:T(8,128)(2,1)S(1)}, bf16[1,768,384]{2,1,0:T(8,128)(2,1)S(1)}, u32[]{:S(2)}, u32[]{:S(2)}) collective-permute-start(bf16[1,768,384]{2,1,0:T(8,128)(2,1)S(1)} %collective-permute-done.81.refs_1_), channel_id=1, source_target_pairs={{8,0},{16,8},{24,16},{28,24},{20,28},{12,20},{4,12},{0,4},{1,9},{9... | collective-permute-start | bytes 1769480 | tf_op jit(solution)/shard_map/ppermute | solution.py:815
  567.6 21.1 %collective-permute-start.83 = (bf16[2,96,896]{2,1,0:T(8,128)(2,1)S(1)}, bf16[2,96,896]{2,1,0:T(8,128)(2,1)S(1)}, u32[]{:S(2)}, u32[]{:S(2)}) collective-permute-start(bf16[2,96,896]{2,1,0:T(8,128)(2,1)S(1)} %pad_maximum_fusion.1), channel_id=1, source_target_pairs={{0,8},{8,16},{16,24},{24,28},{28,20},{20,12},{12,4},{4,0},{9,1},{1... | collective-permute-start | bytes 1032200 | tf_op jit(solution)/shard_map/ppermute | solution.py:815
  576.7 39.1 %collective-permute-start.103 = (bf16[2,96,896]{2,1,0:T(8,128)(2,1)S(1)}, bf16[2,96,896]{2,1,0:T(8,128)(2,1)S(1)}, u32[]{:S(2)}, u32[]{:S(2)}) collective-permute-start(bf16[2,96,896]{2,1,0:T(8,128)(2,1)S(1)} %pad_maximum_fusion.2), channel_id=1, source_target_pairs={{8,0},{16,8},{24,16},{28,24},{20,28},{12,20},{4,12},{0,4},{1,9},{9... | collective-permute-start | bytes 1032200 | tf_op jit(solution)/shard_map/ppermute | solution.py:815
  581.3 27.8 %collective-permute-start.87 = (bf16[1,768,384]{2,1,0:T(8,128)(2,1)S(1)}, bf16[1,768,384]{2,1,0:T(8,128)(2,1)S(1)}, u32[]{:S(2)}, u32[]{:S(2)}) collective-permute-start(bf16[1,768,384]{2,1,0:T(8,128)(2,1)S(1)} %collective-permute-done.84.refs_0_), channel_id=1, source_target_pairs={{0,8},{8,16},{16,24},{24,28},{28,20},{20,12},{12,4},{4,0},{9,1},{1... | collective-permute-start | bytes 1769480 | tf_op jit(solution)/shard_map/ppermute | solution.py:815
  588.7 22.1 %collective-permute-start.88 = (bf16[1,768,384]{2,1,0:T(8,128)(2,1)S(1)}, bf16[1,768,384]{2,1,0:T(8,128)(2,1)S(1)}, u32[]{:S(2)}, u32[]{:S(2)}) collective-permute-start(bf16[1,768,384]{2,1,0:T(8,128)(2,1)S(1)} %collective-permute-done.85.refs_1_), channel_id=1, source_target_pairs={{8,0},{16,8},{24,16},{28,24},{20,28},{12,20},{4,12},{0,4},{1,9},{9... | collective-permute-start | bytes 1769480 | tf_op jit(solution)/shard_map/ppermute | solution.py:815
  609.2 18.7 %collective-permute-start.90 = (bf16[1,768,384]{2,1,0:T(8,128)(2,1)S(1)}, bf16[1,768,384]{2,1,0:T(8,128)(2,1)S(1)}, u32[]{:S(2)}, u32[]{:S(2)}) collective-permute-start(bf16[1,768,384]{2,1,0:T(8,128)(2,1)S(1)} %collective-permute-done.87.refs_0_), channel_id=1, source_target_pairs={{0,8},{8,16},{16,24},{24,28},{28,20},{20,12},{12,4},{4,0},{9,1},{1... | collective-permute-start | bytes 1769480 | tf_op jit(solution)/shard_map/ppermute | solution.py:815
  610.9 22.4 %collective-permute-start.91 = (bf16[1,768,384]{2,1,0:T(8,128)(2,1)S(1)}, bf16[1,768,384]{2,1,0:T(8,128)(2,1)S(1)}, u32[]{:S(2)}, u32[]{:S(2)}) collective-permute-start(bf16[1,768,384]{2,1,0:T(8,128)(2,1)S(1)} %collective-permute-done.88.refs_1_), channel_id=1, source_target_pairs={{8,0},{16,8},{24,16},{28,24},{20,28},{12,20},{4,12},{0,4},{1,9},{9... | collective-permute-start | bytes 1769480 | tf_op jit(solution)/shard_map/ppermute | solution.py:815
  615.2 18.0 %collective-permute-start.89 = (bf16[2,96,896]{2,1,0:T(8,128)(2,1)S(1)}, bf16[2,96,896]{2,1,0:T(8,128)(2,1)S(1)}, u32[]{:S(2)}, u32[]{:S(2)}) collective-permute-start(bf16[2,96,896]{2,1,0:T(8,128)(2,1)S(1)} %collective-permute-done.86), channel_id=1, source_target_pairs={{0,8},{8,16},{16,24},{24,28},{28,20},{20,12},{12,4},{4,0},{9,1},{1... | collective-permute-start | bytes 1032200 | tf_op jit(solution)/shard_map/ppermute | solution.py:815
  615.9 20.9 %collective-permute-start.104 = (bf16[2,96,896]{2,1,0:T(8,128)(2,1)S(1)}, bf16[2,96,896]{2,1,0:T(8,128)(2,1)S(1)}, u32[]{:S(2)}, u32[]{:S(2)}) collective-permute-start(bf16[2,96,896]{2,1,0:T(8,128)(2,1)S(1)} %collective-permute-done.103), channel_id=1, source_target_pairs={{8,0},{16,8},{24,16},{28,24},{20,28},{12,20},{4,12},{0,4},{1,9},{9... | collective-permute-start | bytes 1032200 | tf_op jit(solution)/shard_map/ppermute | solution.py:815
  627.9 27.6 %collective-permute-start.93 = (bf16[1,768,384]{2,1,0:T(8,128)(2,1)S(1)}, bf16[1,768,384]{2,1,0:T(8,128)(2,1)S(1)}, u32[]{:S(2)}, u32[]{:S(2)}) collective-permute-start(bf16[1,768,384]{2,1,0:T(8,128)(2,1)S(1)} %collective-permute-done.90.refs_0_), channel_id=1, source_target_pairs={{0,8},{8,16},{16,24},{24,28},{28,20},{20,12},{12,4},{4,0},{9,1},{1... | collective-permute-start | bytes 1769480 | tf_op jit(solution)/shard_map/ppermute | solution.py:815
  633.2 24.1 %collective-permute-start.94 = (bf16[1,768,384]{2,1,0:T(8,128)(2,1)S(1)}, bf16[1,768,384]{2,1,0:T(8,128)(2,1)S(1)}, u32[]{:S(2)}, u32[]{:S(2)}) collective-permute-start(bf16[1,768,384]{2,1,0:T(8,128)(2,1)S(1)} %collective-permute-done.91.refs_1_), channel_id=1, source_target_pairs={{8,0},{16,8},{24,16},{28,24},{20,28},{12,20},{4,12},{0,4},{1,9},{9... | collective-permute-start | bytes 1769480 | tf_op jit(solution)/shard_map/ppermute | solution.py:815
  637.4 19.9 %collective-permute-start.92 = (bf16[2,96,896]{2,1,0:T(8,128)(2,1)S(1)}, bf16[2,96,896]{2,1,0:T(8,128)(2,1)S(1)}, u32[]{:S(2)}, u32[]{:S(2)}) collective-permute-start(bf16[2,96,896]{2,1,0:T(8,128)(2,1)S(1)} %collective-permute-done.89), channel_id=1, source_target_pairs={{0,8},{8,16},{16,24},{24,28},{28,20},{20,12},{12,4},{4,0},{9,1},{1... | collective-permute-start | bytes 1032200 | tf_op jit(solution)/shard_map/ppermute | solution.py:815
  657.3 21.9 %collective-permute-start.97 = (bf16[1,768,384]{2,1,0:T(8,128)(2,1)S(1)}, bf16[1,768,384]{2,1,0:T(8,128)(2,1)S(1)}, u32[]{:S(2)}, u32[]{:S(2)}) collective-permute-start(bf16[1,768,384]{2,1,0:T(8,128)(2,1)S(1)} %collective-permute-done.94.refs_1_), channel_id=1, source_target_pairs={{8,0},{16,8},{24,16},{28,24},{20,28},{12,20},{4,12},{0,4},{1,9},{9... | collective-permute-start | bytes 1769480 | tf_op jit(solution)/shard_map/ppermute | solution.py:815
  657.6 21.6 %collective-permute-start.95 = (bf16[2,96,896]{2,1,0:T(8,128)(2,1)S(1)}, bf16[2,96,896]{2,1,0:T(8,128)(2,1)S(1)}, u32[]{:S(2)}, u32[]{:S(2)}) collective-permute-start(bf16[2,96,896]{2,1,0:T(8,128)(2,1)S(1)} %collective-permute-done.92), channel_id=1, source_target_pairs={{0,8},{8,16},{16,24},{24,28},{28,20},{20,12},{12,4},{4,0},{9,1},{1... | collective-permute-start | bytes 1032200 | tf_op jit(solution)/shard_map/ppermute | solution.py:815
  662.1 20.0 %collective-permute-start.107 = (bf16[2,96,896]{2,1,0:T(8,128)(2,1)S(1)}, bf16[2,96,896]{2,1,0:T(8,128)(2,1)S(1)}, u32[]{:S(2)}, u32[]{:S(2)}) collective-permute-start(bf16[2,96,896]{2,1,0:T(8,128)(2,1)S(1)} %collective-permute-done.106), channel_id=1, source_target_pairs={{8,0},{16,8},{24,16},{28,24},{20,28},{12,20},{4,12},{0,4},{1,9},{9... | collective-permute-start | bytes 1032200 | tf_op jit(solution)/shard_map/ppermute | solution.py:815
  671.8 18.5 %collective-permute-start.99 = (bf16[1,768,384]{2,1,0:T(8,128)(2,1)S(1)}, bf16[1,768,384]{2,1,0:T(8,128)(2,1)S(1)}, u32[]{:S(2)}, u32[]{:S(2)}) collective-permute-start(bf16[1,768,384]{2,1,0:T(8,128)(2,1)S(1)} %collective-permute-done.96.refs_0_), channel_id=1, source_target_pairs={{0,8},{8,16},{16,24},{24,28},{28,20},{20,12},{12,4},{4,0},{9,1},{1... | collective-permute-start | bytes 1769480 | tf_op jit(solution)/shard_map/ppermute | solution.py:815
  682.1 18.3 %collective-permute-start.108 = (bf16[2,96,896]{2,1,0:T(8,128)(2,1)S(1)}, bf16[2,96,896]{2,1,0:T(8,128)(2,1)S(1)}, u32[]{:S(2)}, u32[]{:S(2)}) collective-permute-start(bf16[2,96,896]{2,1,0:T(8,128)(2,1)S(1)} %collective-permute-done.107), channel_id=1, source_target_pairs={{8,0},{16,8},{24,16},{28,24},{20,28},{12,20},{4,12},{0,4},{1,9},{9... | collective-permute-start | bytes 1032200 | tf_op jit(solution)/shard_map/ppermute | solution.py:815
  (137 other events, 1401.9 us)

commit v6 on v5

--- a/solution.py
+++ b/solution.py
@@ -172,7 +172,7 @@
             pltpu.VMEM((2 * rows, width), BF16),
             pltpu.VMEM((2 * rows, 2 * DH), F32),
         ],
-        compiler_params=params(48),
+        compiler_params=params(60),
         cost_estimate=SMALL,
         name="attend_back",
     )(place, own, other, grad, grad_c, w_out, out_c)
@@ -219,25 +219,23 @@
         out_shape=[jax.ShapeDtypeStruct((2, features, 7 * LANES), BF16)] * 2,
         in_specs=[pl.BlockSpec(memory_space=pltpu.SMEM)] + [spec] * 10,
         out_specs=[spec] * 2,
-        compiler_params=params(40),
+        compiler_params=params(60),
         cost_estimate=SMALL,
         name="late_grads",
     )(place, *near, *far, qkv_grad, attended, grad, grad_c, *shared)
 
 
 def columns_kernel(
-    place_ref, query_ref, key_ref, value_ref, gain_ref, gain_ffn_ref, w_out_ref, out_ref, gains_ref, share_ref
+    place_ref, query_ref, key_ref, value_ref, w_out_ref, out_ref, share_ref
 ):
     share_ref[...] = w_out_ref[...]
-    gains_ref[0:1, :] = gain_ref[...]
-    gains_ref[1:2, :] = gain_ffn_ref[...]
     width = GROUP_HEADS * DH
     out_ref[:, 0:width] = query_ref[...]
     out_ref[:, width : width + DH] = key_ref[...]
     out_ref[:, width + DH :] = value_ref[...]
 
 
-def their_columns(place, w_query, w_key, w_value, gain_attn, gain_ffn, w_out, shares):
+def their_columns(place, w_query, w_key, w_value, w_out, shares):
     rows = w_query.shape[0]
     width = GROUP_HEADS * DH + 2 * DH
 
@@ -250,23 +248,20 @@
             num_scalar_prefetch=1,
             grid=(1,),
             in_specs=[theirs(GROUP_HEADS * DH), theirs(DH), theirs(DH)]
-            + [pl.BlockSpec(gain_attn.shape, lambda i, c: (0, 0))] * 2
             + [pl.BlockSpec((rows // shares, rows), lambda i, c: (c[1], 0))],
             out_specs=[
                 pl.BlockSpec((rows, width), lambda i, c: (0, 0)),
-                pl.BlockSpec((2, rows), lambda i, c: (0, 0)),
                 pl.BlockSpec((rows // shares, rows), lambda i, c: (0, 0)),
             ],
         ),
         out_shape=[
             jax.ShapeDtypeStruct((rows, width), BF16),
-            jax.ShapeDtypeStruct((2, rows), F32),
             jax.ShapeDtypeStruct((rows // shares, rows), BF16),
         ],
         compiler_params=params(60, "arbitrary"),
         cost_estimate=SMALL,
         name="their_columns",
-    )(place, w_query, w_key, w_value, gain_attn, gain_ffn, w_out)
+    )(place, w_query, w_key, w_value, w_out)
 
 
 def join_kernel(mine_ref, *refs):
@@ -694,14 +689,49 @@
     )(plan, *chunks, *outs)
 
 
-def unpack_late_kernel(col_ref, first_ref, second_ref, *outs):
-    sgate, sup, sdown, query, key, value, out = outs
-    features = first_ref.shape[1]
-    flipped = col_ref[0] != 0
+def late_chunk_kernel(plan_ref, pack_ref, *refs):
+    *came, out_ref = refs
+    if came:
+        out_ref[...] = (came[0][...].astype(F32) + pack_ref[:, 0].astype(F32)).astype(BF16)
+    else:
+        out_ref[...] = pack_ref[:, 0]
+
+
+def late_chunk(plan, at, pack, came):
+    halves, _, rows, lanes = pack.shape
+    spec = pl.BlockSpec((halves, rows, lanes), lambda i, n: (0, 0, 0))
+    return pl.pallas_call(
+        late_chunk_kernel,
+        grid_spec=pltpu.PrefetchScalarGridSpec(
+            num_scalar_prefetch=1,
+            grid=(1,),
+            in_specs=[pl.BlockSpec((halves, 1, rows, lanes), lambda i, n: (0, n[at], 0, 0))]
+            + [spec] * len(came),
+            out_specs=spec,
+        ),
+        out_shape=jax.ShapeDtypeStruct((halves, rows, lanes), BF16),
+        compiler_params=params(16, "arbitrary"),
+        cost_estimate=SMALL,
+        name="late_chunk",
+    )(plan, pack, *came)
+
+
+def unpack_late_kernel(first_step, steps, plan_ref, *refs):
+    chunks = refs[0 : 2 * steps]
+    sgate, sup, sdown, query, key, value, out, all_ref = refs[2 * steps :]
+    rows, features = chunks[0].shape[1], all_ref.shape[2]
+    for k in range(2):
+        for step in range(steps):
+            at = plan_ref[first_step + 2 * step + k] * rows
+            for c in range(2):
+                all_ref[k, c, pl.ds(pl.multiple_of(at, rows), rows), :] = chunks[
+                    steps * k + step
+                ][c]
+    flipped = plan_ref[plan_ref.shape[0] - 1] != 0
     for c in range(2):
         for b in range(14):
             lanes = slice(b % 7 * LANES, (b % 7 + 1) * LANES)
-            first, second = first_ref[c, :, lanes], second_ref[c, :, lanes]
+            first, second = all_ref[0, c, :, lanes], all_ref[1, c, :, lanes]
             if b >= 7:
                 first, second = second, first
             block = jnp.where(flipped, second, first).astype(F32)
@@ -723,16 +753,20 @@
                 out[at : at + LANES, :] = block.T
 
 
-def unpack_late(col, first, second, shapes):
+def unpack_late(plan, first_step, chunks, shapes):
+    steps = len(chunks[0])
+    halves, rows, lanes = chunks[0][0].shape
     spec = pl.BlockSpec(memory_space=pltpu.VMEM)
     return pl.pallas_call(
-        unpack_late_kernel,
-        in_specs=[pl.BlockSpec(memory_space=pltpu.SMEM), spec, spec],
+        functools.partial(unpack_late_kernel, first_step, steps),
+        in_specs=[pl.BlockSpec(memory_space=pltpu.SMEM)] + [spec] * (2 * steps),
         out_specs=[spec] * len(shapes),
         out_shape=[jax.ShapeDtypeStruct(shape, F32) for shape in shapes],
+        scratch_shapes=[pltpu.VMEM((2, halves, steps * rows, lanes), BF16)],
         compiler_params=params(48),
+        cost_estimate=SMALL,
         name="unpack_late",
-    )(col, first, second)
+    )(plan, *chunks[0], *chunks[1])
 
 
 def plans(ring, each):
@@ -828,16 +862,10 @@
     tokens_c = swap(tokens_in, "col")
     count = min(ring_size, 4)
     member = dp % count
-    there, gains, out_y = their_columns(
-        jnp.stack([col, member]),
-        w_query,
-        w_key,
-        w_value,
-        norm_gain_attn[None],
-        norm_gain_ffn[None],
-        w_out,
-        count,
-    )
+    there, out_y = their_columns(
+        jnp.stack([col, member]), w_query, w_key, w_value, w_out, count
+    )
+    gains = jnp.stack([norm_gain_attn, norm_gain_ffn])
     there = swap(there, "col")
     gains_c = swap(gains, "col")
 
@@ -855,7 +883,8 @@
 
     shares = [out_y]
     for k in range(1, count):
-        shares.append(lax.ppermute(out_y, "dp", [(m, m ^ k) for m in range(dp_size)]))
+        part = out_y if k == 1 else after(out_y, far[2])
+        shares.append(lax.ppermute(part, "dp", [(m, m ^ k) for m in range(dp_size)]))
     where = after(where, grad_y, *shares)
 
     w_sgate, w_sup, w_sdown = w_shared_gate[None], w_shared_up[None], w_shared_down[None]
@@ -1032,17 +1061,9 @@
     packs = [
         pack.reshape(2, ring_size, local_features // ring_size, pack.shape[2]) for pack in packs
     ]
-
-    def late_chunk(step, which):
-        at = chunk_at(step, which)
-        return lax.dynamic_index_in_dim(packs[which], at, axis=1, keepdims=False)
-
-    def late_place(current, step, which):
-        at = chunk_at(ring_size - 1 + step, which)
-        return lax.dynamic_update_index_in_dim(late_out[which], current, at, 1)
-
-    late_out = [jnp.zeros(pack.shape, BF16) for pack in packs]
-    late = [late_chunk(0, k) for k in range(2)]
+    chunks_first = 2 * experts
+    late = [late_chunk(plan, chunks_first + k, packs[k], ()) for k in range(2)]
+    late_out = [[], []]
     late_done = 0
     late_total = 2 * (ring_size - 1)
 
@@ -1051,14 +1072,15 @@
         others = [swap(values[1], "col") for values in totals]
         for k in range(2):
             late[k] = in_order(totals[k][0:1], others[1 - k][None], col, 0)
-            late_out[k] = late_place(late[k], 0, k)
+            late_out[k].append(late[k])
 
     def late_finish(k, values):
         if late_done < ring_size:
-            late[k] = add_rounded(values, late_chunk(late_done, k))
+            at = chunks_first + 2 * late_done + k
+            late[k] = late_chunk(plan, at, packs[k], (values,))
         else:
             late[k] = values
-            late_out[k] = late_place(values, late_done - ring_size + 1, k)
+            late_out[k].append(values)
 
     shapes = [w_gate.shape, w_up.shape, w_down.shape]
     placed = ()
@@ -1112,9 +1134,7 @@
     gate_grad, up_grad, down_grad = placed
     shapes = [w.shape for w in (w_shared_gate, w_shared_up, w_shared_down)]
     shapes += [w.shape for w in (w_query, w_key, w_value, w_out)]
-    finals = unpack_late(
-        col_ref, *[out.reshape(2, local_features, out.shape[3]) for out in late_out], shapes
-    )
+    finals = unpack_late(plan, chunks_first + late_total, late_out, shapes)
     shared_gate_grad, shared_up_grad, shared_down_grad = finals[0:3]
     query_grad, key_grad, value_grad, out_proj_grad = finals[3:7]
 

time: 724 us -> 667 us (0.921)
  between operations: 59.2 us -> 2.83 us
  Pallas kernels: 222 us -> 240 us
  local copies, waits for them, and re-layouts: 36.2 us -> 24.1 us
  waiting for transfers between devices: 242 us -> 233 us
    pallas_call x1 -> x17, Pallas kernels: 4.84 us -> 18.1 us  [the longest x16 11.7 us: late_chunk(): pl.pallas_call(late_chunk_kernel, grid_spec=pltpu.PrefetchScalarGridSpec(...]
    convert_element_type x27 -> x13, other arithmetic: 24.1 us -> 19.9 us  [add_rounded(): return (left.astype(F32) + right.astype(F32)).astype(BF16)]
  transfers between devices with their start and end apart: 110 -> 110, of which waited for: 50 -> 47; matrix products, arithmetic and copies ran while one was open for 7% -> 8% of each run, Pallas kernels for 29% -> 34%
where the time goes in v6:
time: 667 us; the launch traced here: 657 us
  Pallas kernels  240 us (36%)
  waiting for transfers between devices  233 us (35%)
  starting transfers between devices  111 us (17%)
  other arithmetic  40.4 us (6%)
  local copies, waits for them, and re-layouts  24.1 us (4%)
    ppermute x70, waiting for transfers between devices, send(): return lax.ppermute(values, ('dp', 'col'), routes_of[which])  164 us
    ppermute x70, starting transfers between devices, send(): return lax.ppermute(values, ('dp', 'col'), routes_of[which])  83.4 us
    pallas_call x9, Pallas kernels, expert_grads(): pl.pallas_call(functools.partial(expert_kernel, shared, aliased, first),...  79.7 us
    ppermute x34, waiting for transfers between devices, swap(): return lax.ppermute(values, axis, [(0, 1), (1, 0)])  43.6 us
    pallas_call x4, Pallas kernels, mix(): pl.pallas_call(functools.partial(mix_kernel, back, group), grid_spec=pltp...  39.9 us
    pallas_call x16, Pallas kernels, unpack(): pl.pallas_call(functools.partial(unpack_kernel, aliased), grid_spec=pltpu...  38.2 us
    ppermute x34, starting transfers between devices, swap(): return lax.ppermute(values, axis, [(0, 1), (1, 0)])  20 us
    convert_element_type x13, other arithmetic, add_rounded(): return (left.astype(F32) + right.astype(F32)).astype(BF16)  19.9 us
  transfers between devices with their start and end apart: 110, of which 47 were waited for; matrix products, arithmetic and copies ran while one was open for 8% of the time, Pallas kernels for 34%

profile of v6, /device:TPU:0, one launch (start us, length us, event | category | flops | bytes accessed | tf_op | source)
XLA Modules:
  0.0 657.3 jit_solution(4394721177545080575)
XLA Ops:
  1.8 3.1 their_columns.1
  8.2 5.0 collective-permute-done.2.gains_c_ref.refs_7_
  13.3 2.9 collective-permute-start.4
  18.0 4.5 project.2
  22.5 9.9 %collective-permute-done.4.refs_0_ = bf16[192,768]{1,0:T(8,128)(2,1)S(1)} collective-permute-done((bf16[192,768]{1,0:T(8,128)(2,1)}, bf16[192,768]{1,0:T(8,128)(2,1)S(1)}, u32[]{:S(2)}, u32[]{:S(2)}) %collective-permute-start.4) | collective-permute-done | bytes 294944 | tf_op jit(solution)/shard_map/ppermute | solution.py:48
  39.5 4.5 project.3
  47.7 3.4 collective-permute-done.5
  51.1 3.7 collective-permute-done.9.refs_3_
  54.9 3.9 collective-permute-done.8.refs_2_
  59.9 6.2 attend.1.refs_4_.refs_5_
  66.7 3.1 collective-permute-done.10.refs_5_
  71.8 7.8 %collective-permute-done.15 = bf16[192,768]{1,0:T(8,128)(2,1)S(1)} collective-permute-done((bf16[192,768]{1,0:T(8,128)(2,1)S(1)}, bf16[192,768]{1,0:T(8,128)(2,1)S(1)}, u32[]{:S(2)}, u32[]{:S(2)}) %collective-permute-start.15) | collective-permute-done | bytes 294944 | tf_op jit(solution)/shard_map/ppermute | solution.py:48
  84.4 9.0 %hidden_before.1 = (f32[1024,768]{1,0:T(8,128)}, f32[1024,768]{1,0:T(8,128)}) custom-call(s32[3]{0:T(128)} %copy-done.49, bf16[512,768]{1,0:T(8,128)(2,1)} %refs_0_.2, bf16[512,768]{1,0:T(8,128)(2,1)} %copy-done.70, bf16[512,768]{1,0:T(8,128)(2,1)} %collective-permute-done.own_ref.refs_2_, bf16[512,768]{1,0:T(8,128)(2,1)} %copy-done.71, ...), custom_call_target="tpu_custom_call" | custom-call | flops 2415919104 | bytes 12582912 | tf_op jit(solution)/shard_map/hidden_before/pallas_call | solution.py:398
  99.1 9.4 %hidden_after.1 = (f32[1024,768]{1,0:T(8,128)}, bf16[1024,768]{1,0:T(8,128)(2,1)}, bf16[1024,768]{1,0:T(8,128)(2,1)}, f32[1024,1]{1,0:T(8,128)}) custom-call(s32[3]{0:T(128)} %copy-done.49, f32[1024,768]{1,0:T(8,128)} %get-tuple-element.254.refs_0_, f32[1024,768]{1,0:T(8,128)} %get-tuple-element.255.refs_1_, ...), custom_call_target="tpu_custom_call" | custom-call | tf_op jit(solution)/shard_map/hidden_after/pallas_call | solution.py:420
  112.0 9.1 %expert_grads.9 = (bf16[1,1536,384]{2,1,0:T(8,128)(2,1)S(1)}, bf16[1,1536,384]{2,1,0:T(8,128)(2,1)S(1)}, bf16[8,1024,512]{2,1,0:T(8,128)(2,1)}, bf16[8,1024,256]{2,1,0:T(8,128)(2,1)S(1)}) custom-call(s32[63]{0:T(128)S(1)} %fusion.18.order_ref.plan_ref, bf16[1024,768]{1,0:T(8,128)(2,1)S(1)} %copy-done.5, bf16[1024,768]{1,0:T(8,128)(2,1)S(1)} %copy-done.6, ...), custom_call_target="tpu_custom_call" | custom-call | tf_op jit(solution)/shard_map/expert_grads/pallas_call | solution.py:543
  122.6 8.9 %expert_grads.10 = (bf16[1,1536,384]{2,1,0:T(8,128)(2,1)S(1)}, bf16[1,1536,384]{2,1,0:T(8,128)(2,1)S(1)}, bf16[8,1024,512]{2,1,0:T(8,128)(2,1)}, bf16[8,1024,256]{2,1,0:T(8,128)(2,1)S(1)}) custom-call(s32[63]{0:T(128)S(1)} %fusion.18.order_ref.plan_ref, bf16[1024,768]{1,0:T(8,128)(2,1)S(1)} %copy-done.5, ...), custom_call_target="tpu_custom_call", output_to_operand_aliasing={{2}: (18, {}), {3}: (19, {})} | custom-call | tf_op jit(solution)/shard_map/expert_grads/pallas_call | solution.py:543
  131.9 8.9 %expert_grads.11 = (bf16[1,1536,384]{2,1,0:T(8,128)(2,1)S(1)}, bf16[1,1536,384]{2,1,0:T(8,128)(2,1)S(1)}, bf16[8,1024,512]{2,1,0:T(8,128)(2,1)}, bf16[8,1024,256]{2,1,0:T(8,128)(2,1)S(1)}) custom-call(s32[63]{0:T(128)S(1)} %fusion.18.order_ref.plan_ref, bf16[1024,768]{1,0:T(8,128)(2,1)S(1)} %copy-done.5, ...), custom_call_target="tpu_custom_call", output_to_operand_aliasing={{2}: (18, {}), {3}: (19, {})} | custom-call | tf_op jit(solution)/shard_map/expert_grads/pallas_call | solution.py:543
  143.6 9.3 %expert_grads.12 = (bf16[1,1536,384]{2,1,0:T(8,128)(2,1)S(1)}, bf16[1,1536,384]{2,1,0:T(8,128)(2,1)S(1)}, bf16[8,1024,512]{2,1,0:T(8,128)(2,1)}, bf16[8,1024,256]{2,1,0:T(8,128)(2,1)S(1)}) custom-call(s32[63]{0:T(128)S(1)} %fusion.18.order_ref.plan_ref, bf16[1024,768]{1,0:T(8,128)(2,1)S(1)} %copy-done.5, ...), custom_call_target="tpu_custom_call", output_to_operand_aliasing={{2}: (18, {}), {3}: (19, {})} | custom-call | tf_op jit(solution)/shard_map/expert_grads/pallas_call | solution.py:543
  156.5 8.9 %expert_grads.13 = (bf16[1,1536,384]{2,1,0:T(8,128)(2,1)S(1)}, bf16[1,1536,384]{2,1,0:T(8,128)(2,1)S(1)}, bf16[8,1024,512]{2,1,0:T(8,128)(2,1)}, bf16[8,1024,256]{2,1,0:T(8,128)(2,1)S(1)}) custom-call(s32[63]{0:T(128)S(1)} %fusion.18.order_ref.plan_ref, bf16[1024,768]{1,0:T(8,128)(2,1)S(1)} %copy-done.5, ...), custom_call_target="tpu_custom_call", output_to_operand_aliasing={{2}: (18, {}), {3}: (19, {})} | custom-call | tf_op jit(solution)/shard_map/expert_grads/pallas_call | solution.py:543
  169.7 8.9 %expert_grads.14 = (bf16[1,1536,384]{2,1,0:T(8,128)(2,1)S(1)}, bf16[1,1536,384]{2,1,0:T(8,128)(2,1)S(1)}, bf16[8,1024,512]{2,1,0:T(8,128)(2,1)}, bf16[8,1024,256]{2,1,0:T(8,128)(2,1)S(1)}) custom-call(s32[63]{0:T(128)S(1)} %fusion.18.order_ref.plan_ref, bf16[1024,768]{1,0:T(8,128)(2,1)S(1)} %copy-done.5, ...), custom_call_target="tpu_custom_call", output_to_operand_aliasing={{2}: (18, {}), {3}: (19, {})} | custom-call | tf_op jit(solution)/shard_map/expert_grads/pallas_call | solution.py:543
  183.6 9.0 %expert_grads.15 = (bf16[1,1536,384]{2,1,0:T(8,128)(2,1)S(1)}, bf16[1,1536,384]{2,1,0:T(8,128)(2,1)S(1)}, bf16[8,1024,512]{2,1,0:T(8,128)(2,1)}, bf16[8,1024,256]{2,1,0:T(8,128)(2,1)S(1)}) custom-call(s32[63]{0:T(128)S(1)} %fusion.18.order_ref.plan_ref, bf16[1024,768]{1,0:T(8,128)(2,1)S(1)} %copy-done.5, ...), custom_call_target="tpu_custom_call", output_to_operand_aliasing={{2}: (18, {}), {3}: (19, {})} | custom-call | tf_op jit(solution)/shard_map/expert_grads/pallas_call | solution.py:543
  196.2 8.9 %expert_grads.16 = (bf16[1,1536,384]{2,1,0:T(8,128)(2,1)S(1)}, bf16[1,1536,384]{2,1,0:T(8,128)(2,1)S(1)}, bf16[8,1024,512]{2,1,0:T(8,128)(2,1)}, bf16[8,1024,256]{2,1,0:T(8,128)(2,1)S(1)}) custom-call(s32[63]{0:T(128)S(1)} %fusion.18.order_ref.plan_ref, bf16[1024,768]{1,0:T(8,128)(2,1)S(1)} %copy-done.5, ...), custom_call_target="tpu_custom_call", output_to_operand_aliasing={{2}: (18, {}), {3}: (19, {})} | custom-call | tf_op jit(solution)/shard_map/expert_grads/pallas_call | solution.py:543
  208.7 8.0 %expert_grads.17 = (bf16[1,1536,384]{2,1,0:T(8,128)(2,1)S(1)}, bf16[1,1536,384]{2,1,0:T(8,128)(2,1)S(1)}, bf16[1,1024,512]{2,1,0:T(8,128)(2,1)S(1)}, bf16[1,1024,256]{2,1,0:T(8,128)(2,1)S(1)}) custom-call(s32[63]{0:T(128)S(1)} %fusion.18.order_ref.plan_ref, bf16[1024,768]{1,0:T(8,128)(2,1)S(1)} %copy-done.5, bf16[1024,768]{1,0:T(8,128)(2,1)S(1)} %copy-done.7, ...), custom_call_target="tpu_custom_call" | custom-call | tf_op jit(solution)/shard_map/expert_grads/pallas_call | solution.py:543
  220.5 12.5 %mix.4 = bf16[1024,768]{1,0:T(8,128)(2,1)S(1)} custom-call(s32[63]{0:T(128)S(1)} %fusion.18.order_ref.plan_ref, bf16[8,1024,512]{2,1,0:T(8,128)(2,1)} %get-tuple-element.296.refs_0_, bf16[1,1024,512]{2,1,0:T(8,128)(2,1)S(1)} %get-tuple-element.303.refs_1_, ...), custom_call_target="tpu_custom_call" | custom-call | tf_op jit(solution)/shard_map/mix/pallas_call | solution.py:614
  237.0 12.5 %mix.5 = f32[1024,768]{1,0:T(8,128)S(1)} custom-call(s32[63]{0:T(128)S(1)} %fusion.18.order_ref.plan_ref, bf16[8,1024,512]{2,1,0:T(8,128)(2,1)} %get-tuple-element.296.refs_0_, bf16[1,1024,512]{2,1,0:T(8,128)(2,1)S(1)} %get-tuple-element.303.refs_1_, bf16[16,768,256]{2,1,0:T(8,128)(2,1)} %refs_16_.1, bf16[16,768,256]{2,1,0:T(8,128)(2,1)} %refs_17_.1, ...), custom_call_target="tpu_custom_call" | custom-call | tf_op jit(solution)/shard_map/mix/pallas_call | solution.py:614
  249.5 11.2 %collective-permute-done.30 = bf16[1,1536,384]{2,1,0:T(8,128)(2,1)} collective-permute-done((bf16[1,1536,384]{2,1,0:T(8,128)(2,1)S(1)}, bf16[1,1536,384]{2,1,0:T(8,128)(2,1)}, u32[]{:S(2)}, u32[]{:S(2)}) %collective-permute-start.30) | collective-permute-done | bytes 1179680 | tf_op jit(solution)/shard_map/ppermute | solution.py:849
  266.9 7.6 %mix.6 = bf16[1024,768]{1,0:T(8,128)(2,1)S(1)} custom-call(s32[63]{0:T(128)S(1)} %fusion.18.order_ref.plan_ref, bf16[8,1024,256]{2,1,0:T(8,128)(2,1)} %copy-done, bf16[1,1024,256]{2,1,0:T(8,128)(2,1)S(1)} %get-tuple-element.314.refs_1_, ...), custom_call_target="tpu_custom_call" | custom-call | tf_op jit(solution)/shard_map/mix/pallas_call | solution.py:614
  274.6 3.2 add_convert_fusion.4
  278.2 7.3 %mix.7 = f32[1024,768]{1,0:T(8,128)S(1)} custom-call(s32[63]{0:T(128)S(1)} %fusion.18.order_ref.plan_ref, bf16[8,1024,256]{2,1,0:T(8,128)(2,1)} %copy-done, bf16[1,1024,256]{2,1,0:T(8,128)(2,1)S(1)} %get-tuple-element.314.refs_1_, bf16[16,256,768]{2,1,0:T(8,128)(2,1)} %refs_9_.19, bf16[16,256,768]{2,1,0:T(8,128)(2,1)} %refs_9_.19, ...), custom_call_target="tpu_custom_call" | custom-call | tf_op jit(solution)/shard_map/mix/pallas_call | solution.py:614
  287.4 7.1 %collective-permute-done.36 = bf16[1024,768]{1,0:T(8,128)(2,1)} collective-permute-done((bf16[1024,768]{1,0:T(8,128)(2,1)S(1)}, bf16[1024,768]{1,0:T(8,128)(2,1)}, u32[]{:S(2)}, u32[]{:S(2)}) %collective-permute-start.36) | collective-permute-done | bytes 1572896 | tf_op jit(solution)/shard_map/ppermute | solution.py:48
  294.5 3.4 multiply_reduce_fusion
  303.3 3.2 add_convert_fusion.1
  308.9 11.1 %collective-permute-done.40 = bf16[1,1536,384]{2,1,0:T(8,128)(2,1)} collective-permute-done((bf16[1,1536,384]{2,1,0:T(8,128)(2,1)S(1)}, bf16[1,1536,384]{2,1,0:T(8,128)(2,1)}, u32[]{:S(2)}, u32[]{:S(2)}) %collective-permute-start.40) | collective-permute-done | bytes 1179680 | tf_op jit(solution)/shard_map/ppermute | solution.py:849
  319.9 13.2 %attend_back.1.refs_4_ = bf16[1024,640]{1,0:T(8,128)(2,1)} custom-call(s32[3]{0:T(128)} %copy-done.49, bf16[512,640]{1,0:T(8,128)(2,1)} %get-tuple-element.246.own_ref, bf16[512,640]{1,0:T(8,128)(2,1)} %get-tuple-element.250.other_ref, bf16[1024,768]{1,0:T(8,128)(2,1)} %copy-done.54, bf16[1024,768]{1,0:T(8,128)(2,1)} %collective-permute-done.38.grad_c_ref.refs_7_, ...), custom_call_target="tpu_custom_call" | custom-call | tf_op jit(solution)/shard_map/attend_back/pallas_call | solution.py:166
  341.6 10.9 %collective-permute-done.43.refs_0_ = bf16[1,768,384]{2,1,0:T(8,128)(2,1)S(1)} collective-permute-done((bf16[1,768,384]{2,1,0:T(8,128)(2,1)S(1)}, bf16[1,768,384]{2,1,0:T(8,128)(2,1)S(1)}, u32[]{:S(2)}, u32[]{:S(2)}) %collective-permute-start.43) | collective-permute-done | bytes 589856 | tf_op jit(solution)/shard_map/ppermute | solution.py:849
  354.9 13.2 %late_grads.1 = (bf16[2,768,896]{2,1,0:T(8,128)(2,1)}, bf16[2,768,896]{2,1,0:T(8,128)(2,1)}) custom-call(s32[3]{0:T(128)} %copy-done.49, bf16[512,768]{1,0:T(8,128)(2,1)} %get-tuple-element.337.refs_0_, bf16[512,768]{1,0:T(8,128)(2,1)} %get-tuple-element.338.refs_1_, bf16[512,768]{1,0:T(8,128)(2,1)} %get-tuple-element.339.refs_2_, ...), custom_call_target="tpu_custom_call" | custom-call | tf_op jit(solution)/shard_map/late_grads/pallas_call | solution.py:217
  374.5 3.3 collective-permute-done.48.refs_0_
  380.6 3.1 unpack.18
  383.7 6.0 collective-permute-done.46.refs_0_
  390.5 3.8 collective-permute-done.51.refs_0_
  402.1 4.8 collective-permute-done.49.refs_0_
  407.6 6.7 %collective-permute-done.53.refs_0_ = bf16[2,96,896]{2,1,0:T(8,128)(2,1)S(1)} collective-permute-done((bf16[2,96,896]{2,1,0:T(8,128)(2,1)S(1)}, bf16[2,96,896]{2,1,0:T(8,128)(2,1)S(1)}, u32[]{:S(2)}, u32[]{:S(2)}) %collective-permute-start.53) | collective-permute-done | bytes 344096 | tf_op jit(solution)/shard_map/ppermute | solution.py:849
  420.7 10.7 %collective-permute-done.75.refs_0_ = bf16[2,96,896]{2,1,0:T(8,128)(2,1)S(1)} collective-permute-done((bf16[2,96,896]{2,1,0:T(8,128)(2,1)S(1)}, bf16[2,96,896]{2,1,0:T(8,128)(2,1)S(1)}, u32[]{:S(2)}, u32[]{:S(2)}) %collective-permute-start.75) | collective-permute-done | bytes 344096 | tf_op jit(solution)/shard_map/ppermute | solution.py:849
  445.0 14.5 %collective-permute-done.77.refs_0_ = bf16[2,96,896]{2,1,0:T(8,128)(2,1)S(1)} collective-permute-done((bf16[2,96,896]{2,1,0:T(8,128)(2,1)S(1)}, bf16[2,96,896]{2,1,0:T(8,128)(2,1)S(1)}, u32[]{:S(2)}, u32[]{:S(2)}) %collective-permute-start.77) | collective-permute-done | bytes 344096 | tf_op jit(solution)/shard_map/ppermute | solution.py:849
  471.7 5.5 collective-permute-done.67.refs_0_
  480.0 10.2 %collective-permute-done.79.refs_0_ = bf16[2,96,896]{2,1,0:T(8,128)(2,1)S(1)} collective-permute-done((bf16[2,96,896]{2,1,0:T(8,128)(2,1)S(1)}, bf16[2,96,896]{2,1,0:T(8,128)(2,1)S(1)}, u32[]{:S(2)}, u32[]{:S(2)}) %collective-permute-start.79) | collective-permute-done | bytes 344096 | tf_op jit(solution)/shard_map/ppermute | solution.py:849
  495.8 3.1 unpack.24
  498.9 7.2 %collective-permute-done.70.refs_0_ = bf16[2,96,896]{2,1,0:T(8,128)(2,1)S(1)} collective-permute-done((bf16[2,96,896]{2,1,0:T(8,128)(2,1)S(1)}, bf16[2,96,896]{2,1,0:T(8,128)(2,1)S(1)}, u32[]{:S(2)}, u32[]{:S(2)}) %collective-permute-start.70) | collective-permute-done | bytes 344096 | tf_op jit(solution)/shard_map/ppermute | solution.py:849
  520.0 3.1 unpack.25
  523.2 4.7 collective-permute-done.83.refs_1_
  530.1 5.6 collective-permute-done.103.refs_9_
  538.0 3.5 unpack.26
  541.5 2.9 collective-permute-done.87.refs_0_
  545.4 6.5 collective-permute-done.86.refs_2_
  559.4 2.8 convert_add_fusion
  564.7 3.4 collective-permute-done.90.refs_0_
  568.4 5.2 collective-permute-done.89.refs_3_
  581.2 4.9 collective-permute-done.93.refs_0_
  587.9 4.9 collective-permute-done.92.refs_4_
  605.2 3.4 collective-permute-done.96.refs_0_
  609.1 3.1 collective-permute-done.95.refs_5_
  619.5 10.3 %collective-permute-done.58 = f32[2,768]{1,0:T(2,128)S(1)} collective-permute-done((f32[2,768]{1,0:T(2,128)S(1)}, f32[2,768]{1,0:T(2,128)S(1)}, u32[]{:S(2)}, u32[]{:S(2)}) %collective-permute-start.58) | collective-permute-done | bytes 6176 | tf_op jit(solution)/shard_map/ppermute | solution.py:1168
  631.4 5.3 collective-permute-done.59
  650.4 6.5 unpack_late.1
  (453 shorter events, 226.7 us)
Async XLA Ops:
  0.7 34.4 %collective-permute-start.17 = (bf16[16,768,256]{2,1,0:T(8,128)(2,1)}, bf16[16,768,256]{2,1,0:T(8,128)(2,1)}, u32[]{:S(2)}, u32[]{:S(2)}) collective-permute-start(bf16[16,768,256]{2,1,0:T(8,128)(2,1)} %refs_16_.1), channel_id=1, source_target_pairs={{0,1},{1,0},{2,3},{3,2},{4,5},{5,4},{6,7},{7,6},{8,9},{9,8},{10,11... | collective-permute-start | bytes 18874376 | tf_op jit(solution)/shard_map/ppermute | solution.py:48
  5.4 27.1 %collective-permute-start = (bf16[512,768]{1,0:T(8,128)(2,1)S(1)}, bf16[512,768]{1,0:T(8,128)(2,1)}, u32[]{:S(2)}, u32[]{:S(2)}) collective-permute-start(bf16[512,768]{1,0:T(8,128)(2,1)S(1)} %copy-done.58), channel_id=1, source_target_pairs={{0,2},{2,0},{1,3},{3,1},{4,6},{6,4},{5,7},{7,5},{8,10},{10,8},{9,1... | collective-permute-start | bytes 2359304 | tf_op jit(solution)/shard_map/ppermute | solution.py:48
  13.3 19.1 %collective-permute-start.4 = (bf16[192,768]{1,0:T(8,128)(2,1)}, bf16[192,768]{1,0:T(8,128)(2,1)S(1)}, u32[]{:S(2)}, u32[]{:S(2)}) collective-permute-start(bf16[192,768]{1,0:T(8,128)(2,1)} %get-tuple-element.247), channel_id=1, source_target_pairs={{0,2},{2,0},{1,3},{3,1},{4,6},{6,4},{5,7},{7,5},{8,10},{10,8},{9,1... | collective-permute-start | bytes 884744 | tf_op jit(solution)/shard_map/ppermute | solution.py:48
  34.9 73.7 %collective-permute-start.19 = (bf16[16,256,768]{2,1,0:T(8,128)(2,1)}, bf16[16,256,768]{2,1,0:T(8,128)(2,1)}, u32[]{:S(2)}, u32[]{:S(2)}) collective-permute-start(bf16[16,256,768]{2,1,0:T(8,128)(2,1)} %refs_9_.19), channel_id=1, source_target_pairs={{0,1},{1,0},{2,3},{3,2},{4,5},{5,4},{6,7},{7,6},{8,9},{9,8},{10,11... | collective-permute-start | bytes 18874376 | tf_op jit(solution)/shard_map/ppermute | solution.py:48
  35.0 73.5 %collective-permute-start.18 = (bf16[16,768,256]{2,1,0:T(8,128)(2,1)}, bf16[16,768,256]{2,1,0:T(8,128)(2,1)}, u32[]{:S(2)}, u32[]{:S(2)}) collective-permute-start(bf16[16,768,256]{2,1,0:T(8,128)(2,1)} %refs_17_.1), channel_id=1, source_target_pairs={{0,1},{1,0},{2,3},{3,2},{4,5},{5,4},{6,7},{7,6},{8,9},{9,8},{10,11... | collective-permute-start | bytes 18874376 | tf_op jit(solution)/shard_map/ppermute | solution.py:48
  66.2 17.5 %collective-permute-start.11 = (bf16[768,768]{1,0:T(8,128)(2,1)}, bf16[768,768]{1,0:T(8,128)(2,1)}, u32[]{:S(2)}, u32[]{:S(2)}) collective-permute-start(bf16[768,768]{1,0:T(8,128)(2,1)} %out_ref.1), channel_id=1, source_target_pairs={{0,1},{1,0},{2,3},{3,2},{4,5},{5,4},{6,7},{7,6},{8,9},{9,8},{10,11... | collective-permute-start | bytes 3538952 | tf_op jit(solution)/shard_map/ppermute | solution.py:48
  70.1 25.6 %collective-permute-start.12 = (bf16[1024,384]{1,0:T(8,128)(2,1)}, bf16[1024,384]{1,0:T(8,128)(2,1)}, u32[]{:S(2)}, u32[]{:S(2)}) collective-permute-start(bf16[1024,384]{1,0:T(8,128)(2,1)} %attend.1.refs_4_.refs_5_), channel_id=1, source_target_pairs={{0,2},{2,0},{1,3},{3,1},{4,6},{6,4},{5,7},{7,5},{8,10},{10,8},{9,1... | collective-permute-start | bytes 2359304 | tf_op jit(solution)/shard_map/ppermute | solution.py:48
  79.8 28.7 %collective-permute-start.16 = (bf16[1024,768]{1,0:T(8,128)(2,1)S(1)}, bf16[1024,768]{1,0:T(8,128)(2,1)S(1)}, u32[]{:S(2)}, u32[]{:S(2)}) collective-permute-start(bf16[1024,768]{1,0:T(8,128)(2,1)S(1)} %join.3.refs_2_), channel_id=1, source_target_pairs={{0,1},{1,0},{2,3},{3,2},{4,5},{5,4},{6,7},{7,6},{8,9},{9,8},{10,11... | collective-permute-start | bytes 4718600 | tf_op jit(solution)/shard_map/ppermute | solution.py:48
  121.0 19.8 %collective-permute-start.20 = (bf16[1,1536,384]{2,1,0:T(8,128)(2,1)S(1)}, bf16[1,1536,384]{2,1,0:T(8,128)(2,1)S(1)}, u32[]{:S(2)}, u32[]{:S(2)}) collective-permute-start(bf16[1,1536,384]{2,1,0:T(8,128)(2,1)S(1)} %get-tuple-element.263), channel_id=1, source_target_pairs={{0,8},{8,16},{16,24},{24,28},{28,20},{20,12},{12,4},{4,0},{9,1},{1... | collective-permute-start | bytes 3538952 | tf_op jit(solution)/shard_map/ppermute | solution.py:849
  131.5 23.2 %collective-permute-start.22 = (bf16[1,1536,384]{2,1,0:T(8,128)(2,1)S(1)}, bf16[1,1536,384]{2,1,0:T(8,128)(2,1)S(1)}, u32[]{:S(2)}, u32[]{:S(2)}) collective-permute-start(bf16[1,1536,384]{2,1,0:T(8,128)(2,1)S(1)} %get-tuple-element.273), channel_id=1, source_target_pairs={{8,0},{16,8},{24,16},{28,24},{20,28},{12,20},{4,12},{0,4},{1,9},{9... | collective-permute-start | bytes 3538952 | tf_op jit(solution)/shard_map/ppermute | solution.py:849
  141.1 25.8 %collective-permute-start.21 = (bf16[1,1536,384]{2,1,0:T(8,128)(2,1)S(1)}, bf16[1,1536,384]{2,1,0:T(8,128)(2,1)S(1)}, u32[]{:S(2)}, u32[]{:S(2)}) collective-permute-start(bf16[1,1536,384]{2,1,0:T(8,128)(2,1)S(1)} %add_convert_fusion.13), channel_id=1, source_target_pairs={{0,8},{8,16},{16,24},{24,28},{28,20},{20,12},{12,4},{4,0},{9,1},{1... | collective-permute-start | bytes 3538952 | tf_op jit(solution)/shard_map/ppermute | solution.py:849
  155.0 25.8 %collective-permute-start.24 = (bf16[1,1536,384]{2,1,0:T(8,128)(2,1)S(1)}, bf16[1,1536,384]{2,1,0:T(8,128)(2,1)S(1)}, u32[]{:S(2)}, u32[]{:S(2)}) collective-permute-start(bf16[1,1536,384]{2,1,0:T(8,128)(2,1)S(1)} %add_convert_fusion.12), channel_id=1, source_target_pairs={{8,0},{16,8},{24,16},{28,24},{20,28},{12,20},{4,12},{0,4},{1,9},{9... | collective-permute-start | bytes 3538952 | tf_op jit(solution)/shard_map/ppermute | solution.py:849
  167.3 25.4 %collective-permute-start.23 = (bf16[1,1536,384]{2,1,0:T(8,128)(2,1)S(1)}, bf16[1,1536,384]{2,1,0:T(8,128)(2,1)S(1)}, u32[]{:S(2)}, u32[]{:S(2)}) collective-permute-start(bf16[1,1536,384]{2,1,0:T(8,128)(2,1)S(1)} %add_convert_fusion.11), channel_id=1, source_target_pairs={{0,8},{8,16},{16,24},{24,28},{28,20},{20,12},{12,4},{4,0},{9,1},{1... | collective-permute-start | bytes 3538952 | tf_op jit(solution)/shard_map/ppermute | solution.py:849
  182.1 24.0 %collective-permute-start.26 = (bf16[1,1536,384]{2,1,0:T(8,128)(2,1)}, bf16[1,1536,384]{2,1,0:T(8,128)(2,1)S(1)}, u32[]{:S(2)}, u32[]{:S(2)}) collective-permute-start(bf16[1,1536,384]{2,1,0:T(8,128)(2,1)} %add_convert_fusion.10), channel_id=1, source_target_pairs={{8,0},{16,8},{24,16},{28,24},{20,28},{12,20},{4,12},{0,4},{1,9},{9... | collective-permute-start | bytes 3538952 | tf_op jit(solution)/shard_map/ppermute | solution.py:849
  194.1 24.7 %collective-permute-start.25 = (bf16[1,1536,384]{2,1,0:T(8,128)(2,1)}, bf16[1,1536,384]{2,1,0:T(8,128)(2,1)}, u32[]{:S(2)}, u32[]{:S(2)}) collective-permute-start(bf16[1,1536,384]{2,1,0:T(8,128)(2,1)} %add_convert_fusion.9), channel_id=1, source_target_pairs={{0,8},{8,16},{16,24},{24,28},{28,20},{20,12},{12,4},{4,0},{9,1},{1... | collective-permute-start | bytes 3538952 | tf_op jit(solution)/shard_map/ppermute | solution.py:849
  207.5 27.7 %collective-permute-start.31 = (bf16[1,1536,384]{2,1,0:T(8,128)(2,1)}, bf16[1,1536,384]{2,1,0:T(8,128)(2,1)S(1)}, u32[]{:S(2)}, u32[]{:S(2)}) collective-permute-start(bf16[1,1536,384]{2,1,0:T(8,128)(2,1)} %add_convert_fusion.8), channel_id=1, source_target_pairs={{8,0},{16,8},{24,16},{28,24},{20,28},{12,20},{4,12},{0,4},{1,9},{9... | collective-permute-start | bytes 3538952 | tf_op jit(solution)/shard_map/ppermute | solution.py:849
  233.0 27.7 %collective-permute-start.35 = (bf16[1024,768]{1,0:T(8,128)(2,1)S(1)}, bf16[1024,768]{1,0:T(8,128)(2,1)S(1)}, u32[]{:S(2)}, u32[]{:S(2)}) collective-permute-start(bf16[1024,768]{1,0:T(8,128)(2,1)S(1)} %mix.4), channel_id=1, source_target_pairs={{0,1},{1,0},{2,3},{3,2},{4,5},{5,4},{6,7},{7,6},{8,9},{9,8},{10,11... | collective-permute-start | bytes 4718600 | tf_op jit(solution)/shard_map/ppermute | solution.py:48
  233.6 27.1 %collective-permute-start.30 = (bf16[1,1536,384]{2,1,0:T(8,128)(2,1)S(1)}, bf16[1,1536,384]{2,1,0:T(8,128)(2,1)}, u32[]{:S(2)}, u32[]{:S(2)}) collective-permute-start(bf16[1,1536,384]{2,1,0:T(8,128)(2,1)S(1)} %add_convert_fusion.7), channel_id=1, source_target_pairs={{0,8},{8,16},{16,24},{24,28},{28,20},{20,12},{12,4},{4,0},{9,1},{1... | collective-permute-start | bytes 3538952 | tf_op jit(solution)/shard_map/ppermute | solution.py:849
  236.5 38.0 %collective-permute-start.32 = (bf16[1,1536,384]{2,1,0:T(8,128)(2,1)}, bf16[1,1536,384]{2,1,0:T(8,128)(2,1)}, u32[]{:S(2)}, u32[]{:S(2)}) collective-permute-start(bf16[1,1536,384]{2,1,0:T(8,128)(2,1)} %add_convert_fusion.6), channel_id=1, source_target_pairs={{8,0},{16,8},{24,16},{28,24},{20,28},{12,20},{4,12},{0,4},{1,9},{9... | collective-permute-start | bytes 3538952 | tf_op jit(solution)/shard_map/ppermute | solution.py:849
  261.1 33.4 %collective-permute-start.36 = (bf16[1024,768]{1,0:T(8,128)(2,1)S(1)}, bf16[1024,768]{1,0:T(8,128)(2,1)}, u32[]{:S(2)}, u32[]{:S(2)}) collective-permute-start(bf16[1024,768]{1,0:T(8,128)(2,1)S(1)} %fusion), channel_id=1, source_target_pairs={{0,2},{2,0},{1,3},{3,1},{4,6},{6,4},{5,7},{7,5},{8,10},{10,8},{9,1... | collective-permute-start | bytes 4718600 | tf_op jit(solution)/shard_map/ppermute | solution.py:48
  264.4 22.9 %collective-permute-start.39 = (bf16[1,1536,384]{2,1,0:T(8,128)(2,1)}, bf16[1,1536,384]{2,1,0:T(8,128)(2,1)S(1)}, u32[]{:S(2)}, u32[]{:S(2)}) collective-permute-start(bf16[1,1536,384]{2,1,0:T(8,128)(2,1)} %add_convert_fusion.5), channel_id=1, source_target_pairs={{0,8},{8,16},{16,24},{24,28},{28,20},{20,12},{12,4},{4,0},{9,1},{1... | collective-permute-start | bytes 3538952 | tf_op jit(solution)/shard_map/ppermute | solution.py:849
  277.8 22.4 %collective-permute-start.41 = (bf16[1,1536,384]{2,1,0:T(8,128)(2,1)}, bf16[1,1536,384]{2,1,0:T(8,128)(2,1)}, u32[]{:S(2)}, u32[]{:S(2)}) collective-permute-start(bf16[1,1536,384]{2,1,0:T(8,128)(2,1)} %add_convert_fusion.4), channel_id=1, source_target_pairs={{8,0},{16,8},{24,16},{28,24},{20,28},{12,20},{4,12},{0,4},{1,9},{9... | collective-permute-start | bytes 3538952 | tf_op jit(solution)/shard_map/ppermute | solution.py:849
  298.4 21.5 %collective-permute-start.40 = (bf16[1,1536,384]{2,1,0:T(8,128)(2,1)S(1)}, bf16[1,1536,384]{2,1,0:T(8,128)(2,1)}, u32[]{:S(2)}, u32[]{:S(2)}) collective-permute-start(bf16[1,1536,384]{2,1,0:T(8,128)(2,1)S(1)} %add_convert_fusion.3), channel_id=1, source_target_pairs={{0,8},{8,16},{16,24},{24,28},{28,20},{20,12},{12,4},{4,0},{9,1},{1... | collective-permute-start | bytes 3538952 | tf_op jit(solution)/shard_map/ppermute | solution.py:849
  303.3 16.7 %collective-permute-start.38 = (bf16[1024,768]{1,0:T(8,128)(2,1)S(1)}, bf16[1024,768]{1,0:T(8,128)(2,1)}, u32[]{:S(2)}, u32[]{:S(2)}) collective-permute-start(bf16[1024,768]{1,0:T(8,128)(2,1)S(1)} %get-tuple-element.484.grad_ref.refs_6_), channel_id=1, source_target_pairs={{0,1},{1,0},{2,3},{3,2},{4,5},{5,4},{6,7},{7,6},{8,9},{9,8},{10,11... | collective-permute-start | bytes 4718600 | tf_op jit(solution)/shard_map/ppermute | solution.py:48
  306.5 26.7 %collective-permute-start.42 = (bf16[1,1536,384]{2,1,0:T(8,128)(2,1)}, bf16[1,1536,384]{2,1,0:T(8,128)(2,1)}, u32[]{:S(2)}, u32[]{:S(2)}) collective-permute-start(bf16[1,1536,384]{2,1,0:T(8,128)(2,1)} %add_convert_fusion.1), channel_id=1, source_target_pairs={{8,0},{16,8},{24,16},{28,24},{20,28},{12,20},{4,12},{0,4},{1,9},{9... | collective-permute-start | bytes 3538952 | tf_op jit(solution)/shard_map/ppermute | solution.py:849
  352.5 20.2 %collective-permute-start.44 = (bf16[1,768,384]{2,1,0:T(8,128)(2,1)S(1)}, bf16[1,768,384]{2,1,0:T(8,128)(2,1)}, u32[]{:S(2)}, u32[]{:S(2)}) collective-permute-start(bf16[1,768,384]{2,1,0:T(8,128)(2,1)S(1)} %collective-permute-done.43.refs_0_), channel_id=1, source_target_pairs={{0,8},{8,16},{16,24},{24,28},{28,20},{20,12},{12,4},{4,0},{9,1},{1... | collective-permute-start | bytes 1769480 | tf_op jit(solution)/shard_map/ppermute | solution.py:849
  353.0 25.5 %collective-permute-start.47 = (bf16[1,768,384]{2,1,0:T(8,128)(2,1)S(1)}, bf16[1,768,384]{2,1,0:T(8,128)(2,1)S(1)}, u32[]{:S(2)}, u32[]{:S(2)}) collective-permute-start(bf16[1,768,384]{2,1,0:T(8,128)(2,1)S(1)} %collective-permute-done.45.refs_1_), channel_id=1, source_target_pairs={{8,0},{16,8},{24,16},{28,24},{20,28},{12,20},{4,12},{0,4},{1,9},{9... | collective-permute-start | bytes 1769480 | tf_op jit(solution)/shard_map/ppermute | solution.py:849
  372.7 17.0 %collective-permute-start.46 = (bf16[1,768,384]{2,1,0:T(8,128)(2,1)}, bf16[1,768,384]{2,1,0:T(8,128)(2,1)S(1)}, u32[]{:S(2)}, u32[]{:S(2)}) collective-permute-start(bf16[1,768,384]{2,1,0:T(8,128)(2,1)} %collective-permute-done.44.refs_0_), channel_id=1, source_target_pairs={{0,8},{8,16},{16,24},{24,28},{28,20},{20,12},{12,4},{4,0},{9,1},{1... | collective-permute-start | bytes 1769480 | tf_op jit(solution)/shard_map/ppermute | solution.py:849
  378.5 16.5 %collective-permute-start.50 = (bf16[1,768,384]{2,1,0:T(8,128)(2,1)S(1)}, bf16[1,768,384]{2,1,0:T(8,128)(2,1)S(1)}, u32[]{:S(2)}, u32[]{:S(2)}) collective-permute-start(bf16[1,768,384]{2,1,0:T(8,128)(2,1)S(1)} %collective-permute-done.47.refs_1_), channel_id=1, source_target_pairs={{8,0},{16,8},{24,16},{28,24},{20,28},{12,20},{4,12},{0,4},{1,9},{9... | collective-permute-start | bytes 1769480 | tf_op jit(solution)/shard_map/ppermute | solution.py:849
  389.7 17.2 %collective-permute-start.49 = (bf16[1,768,384]{2,1,0:T(8,128)(2,1)S(1)}, bf16[1,768,384]{2,1,0:T(8,128)(2,1)S(1)}, u32[]{:S(2)}, u32[]{:S(2)}) collective-permute-start(bf16[1,768,384]{2,1,0:T(8,128)(2,1)S(1)} %collective-permute-done.46.refs_0_), channel_id=1, source_target_pairs={{0,8},{8,16},{16,24},{24,28},{28,20},{20,12},{12,4},{4,0},{9,1},{1... | collective-permute-start | bytes 1769480 | tf_op jit(solution)/shard_map/ppermute | solution.py:849
  395.0 20.0 %collective-permute-start.52 = (bf16[1,768,384]{2,1,0:T(8,128)(2,1)S(1)}, bf16[1,768,384]{2,1,0:T(8,128)(2,1)S(1)}, u32[]{:S(2)}, u32[]{:S(2)}) collective-permute-start(bf16[1,768,384]{2,1,0:T(8,128)(2,1)S(1)} %collective-permute-done.50.refs_1_), channel_id=1, source_target_pairs={{8,0},{16,8},{24,16},{28,24},{20,28},{12,20},{4,12},{0,4},{1,9},{9... | collective-permute-start | bytes 1769480 | tf_op jit(solution)/shard_map/ppermute | solution.py:849
  397.3 17.0 %collective-permute-start.53 = (bf16[2,96,896]{2,1,0:T(8,128)(2,1)S(1)}, bf16[2,96,896]{2,1,0:T(8,128)(2,1)S(1)}, u32[]{:S(2)}, u32[]{:S(2)}) collective-permute-start(bf16[2,96,896]{2,1,0:T(8,128)(2,1)S(1)} %late_chunk.18), channel_id=1, source_target_pairs={{0,8},{8,16},{16,24},{24,28},{28,20},{20,12},{12,4},{4,0},{9,1},{1... | collective-permute-start | bytes 1032200 | tf_op jit(solution)/shard_map/ppermute | solution.py:849
  397.9 19.9 %collective-permute-start.74 = (bf16[2,96,896]{2,1,0:T(8,128)(2,1)S(1)}, bf16[2,96,896]{2,1,0:T(8,128)(2,1)S(1)}, u32[]{:S(2)}, u32[]{:S(2)}) collective-permute-start(bf16[2,96,896]{2,1,0:T(8,128)(2,1)S(1)} %late_chunk.24), channel_id=1, source_target_pairs={{8,0},{16,8},{24,16},{28,24},{20,28},{12,20},{4,12},{0,4},{1,9},{9... | collective-permute-start | bytes 1032200 | tf_op jit(solution)/shard_map/ppermute | solution.py:849
  406.9 29.0 %collective-permute-start.62 = (bf16[1,768,384]{2,1,0:T(8,128)(2,1)S(1)}, bf16[1,768,384]{2,1,0:T(8,128)(2,1)S(1)}, u32[]{:S(2)}, u32[]{:S(2)}) collective-permute-start(bf16[1,768,384]{2,1,0:T(8,128)(2,1)S(1)} %collective-permute-done.49.refs_0_), channel_id=1, source_target_pairs={{0,8},{8,16},{16,24},{24,28},{28,20},{20,12},{12,4},{4,0},{9,1},{1... | collective-permute-start | bytes 1769480 | tf_op jit(solution)/shard_map/ppermute | solution.py:849
  415.0 22.0 %collective-permute-start.63 = (bf16[1,768,384]{2,1,0:T(8,128)(2,1)S(1)}, bf16[1,768,384]{2,1,0:T(8,128)(2,1)S(1)}, u32[]{:S(2)}, u32[]{:S(2)}) collective-permute-start(bf16[1,768,384]{2,1,0:T(8,128)(2,1)S(1)} %collective-permute-done.52.refs_1_), channel_id=1, source_target_pairs={{8,0},{16,8},{24,16},{28,24},{20,28},{12,20},{4,12},{0,4},{1,9},{9... | collective-permute-start | bytes 1769480 | tf_op jit(solution)/shard_map/ppermute | solution.py:849
  436.0 25.6 %collective-permute-start.65 = (bf16[1,768,384]{2,1,0:T(8,128)(2,1)S(1)}, bf16[1,768,384]{2,1,0:T(8,128)(2,1)S(1)}, u32[]{:S(2)}, u32[]{:S(2)}) collective-permute-start(bf16[1,768,384]{2,1,0:T(8,128)(2,1)S(1)} %collective-permute-done.62.refs_0_), channel_id=1, source_target_pairs={{0,8},{8,16},{16,24},{24,28},{28,20},{20,12},{12,4},{4,0},{9,1},{1... | collective-permute-start | bytes 1769480 | tf_op jit(solution)/shard_map/ppermute | solution.py:849
  437.0 29.2 %collective-permute-start.66 = (bf16[1,768,384]{2,1,0:T(8,128)(2,1)S(1)}, bf16[1,768,384]{2,1,0:T(8,128)(2,1)S(1)}, u32[]{:S(2)}, u32[]{:S(2)}) collective-permute-start(bf16[1,768,384]{2,1,0:T(8,128)(2,1)S(1)} %collective-permute-done.63.refs_1_), channel_id=1, source_target_pairs={{8,0},{16,8},{24,16},{28,24},{20,28},{12,20},{4,12},{0,4},{1,9},{9... | collective-permute-start | bytes 1769480 | tf_op jit(solution)/shard_map/ppermute | solution.py:849
  440.1 19.4 %collective-permute-start.77 = (bf16[2,96,896]{2,1,0:T(8,128)(2,1)S(1)}, bf16[2,96,896]{2,1,0:T(8,128)(2,1)S(1)}, u32[]{:S(2)}, u32[]{:S(2)}) collective-permute-start(bf16[2,96,896]{2,1,0:T(8,128)(2,1)S(1)} %late_chunk.27), channel_id=1, source_target_pairs={{8,0},{16,8},{24,16},{28,24},{20,28},{12,20},{4,12},{0,4},{1,9},{9... | collective-permute-start | bytes 1032200 | tf_op jit(solution)/shard_map/ppermute | solution.py:849
  441.9 23.6 %collective-permute-start.64 = (bf16[2,96,896]{2,1,0:T(8,128)(2,1)S(1)}, bf16[2,96,896]{2,1,0:T(8,128)(2,1)S(1)}, u32[]{:S(2)}, u32[]{:S(2)}) collective-permute-start(bf16[2,96,896]{2,1,0:T(8,128)(2,1)S(1)} %late_chunk.20), channel_id=1, source_target_pairs={{0,8},{8,16},{16,24},{24,28},{28,20},{20,12},{12,4},{4,0},{9,1},{1... | collective-permute-start | bytes 1032200 | tf_op jit(solution)/shard_map/ppermute | solution.py:849
  442.2 26.1 %collective-permute-start.68 = (bf16[1,768,384]{2,1,0:T(8,128)(2,1)S(1)}, bf16[1,768,384]{2,1,0:T(8,128)(2,1)S(1)}, u32[]{:S(2)}, u32[]{:S(2)}) collective-permute-start(bf16[1,768,384]{2,1,0:T(8,128)(2,1)S(1)} %copy-done.74), channel_id=1, source_target_pairs={{0,1},{1,0},{2,3},{3,2},{4,5},{5,4},{6,7},{7,6},{8,9},{9,8},{10,11... | collective-permute-start | bytes 1769480 | tf_op jit(solution)/shard_map/ppermute | solution.py:48
  459.5 19.3 %collective-permute-start.69 = (bf16[1,768,384]{2,1,0:T(8,128)(2,1)S(1)}, bf16[1,768,384]{2,1,0:T(8,128)(2,1)}, u32[]{:S(2)}, u32[]{:S(2)}) collective-permute-start(bf16[1,768,384]{2,1,0:T(8,128)(2,1)S(1)} %copy-done.73), channel_id=1, source_target_pairs={{0,1},{1,0},{2,3},{3,2},{4,5},{5,4},{6,7},{7,6},{8,9},{9,8},{10,11... | collective-permute-start | bytes 1769480 | tf_op jit(solution)/shard_map/ppermute | solution.py:48
  466.5 26.5 %collective-permute-start.73 = (bf16[1,768,384]{2,1,0:T(8,128)(2,1)S(1)}, bf16[1,768,384]{2,1,0:T(8,128)(2,1)S(1)}, u32[]{:S(2)}, u32[]{:S(2)}) collective-permute-start(bf16[1,768,384]{2,1,0:T(8,128)(2,1)S(1)} %collective-permute-done.66.refs_1_), channel_id=1, source_target_pairs={{8,0},{16,8},{24,16},{28,24},{20,28},{12,20},{4,12},{0,4},{1,9},{9... | collective-permute-start | bytes 1769480 | tf_op jit(solution)/shard_map/ppermute | solution.py:849
  468.3 25.4 %collective-permute-start.72 = (bf16[1,768,384]{2,1,0:T(8,128)(2,1)S(1)}, bf16[1,768,384]{2,1,0:T(8,128)(2,1)S(1)}, u32[]{:S(2)}, u32[]{:S(2)}) collective-permute-start(bf16[1,768,384]{2,1,0:T(8,128)(2,1)S(1)} %collective-permute-done.65.refs_0_), channel_id=1, source_target_pairs={{0,8},{8,16},{16,24},{24,28},{28,20},{20,12},{12,4},{4,0},{9,1},{1... | collective-permute-start | bytes 1769480 | tf_op jit(solution)/shard_map/ppermute | solution.py:849
  470.6 28.3 %collective-permute-start.71 = (bf16[1,768,384]{2,1,0:T(8,128)(2,1)S(1)}, bf16[1,768,384]{2,1,0:T(8,128)(2,1)S(1)}, u32[]{:S(2)}, u32[]{:S(2)}) collective-permute-start(bf16[1,768,384]{2,1,0:T(8,128)(2,1)S(1)} %collective-permute-done.68.refs_0_), channel_id=1, source_target_pairs={{0,8},{8,16},{16,24},{24,28},{28,20},{20,12},{12,4},{4,0},{9,1},{1... | collective-permute-start | bytes 1769480 | tf_op jit(solution)/shard_map/ppermute | solution.py:849
  478.8 27.3 %collective-permute-start.70 = (bf16[2,96,896]{2,1,0:T(8,128)(2,1)S(1)}, bf16[2,96,896]{2,1,0:T(8,128)(2,1)S(1)}, u32[]{:S(2)}, u32[]{:S(2)}) collective-permute-start(bf16[2,96,896]{2,1,0:T(8,128)(2,1)S(1)} %late_chunk.22), channel_id=1, source_target_pairs={{0,8},{8,16},{16,24},{24,28},{28,20},{20,12},{12,4},{4,0},{9,1},{1... | collective-permute-start | bytes 1032200 | tf_op jit(solution)/shard_map/ppermute | solution.py:849
  490.2 18.8 %collective-permute-start.81 = (bf16[1,768,384]{2,1,0:T(8,128)(2,1)}, bf16[1,768,384]{2,1,0:T(8,128)(2,1)}, u32[]{:S(2)}, u32[]{:S(2)}) collective-permute-start(bf16[1,768,384]{2,1,0:T(8,128)(2,1)} %collective-permute-done.69.refs_1_), channel_id=1, source_target_pairs={{8,0},{16,8},{24,16},{28,24},{20,28},{12,20},{4,12},{0,4},{1,9},{9... | collective-permute-start | bytes 1769480 | tf_op jit(solution)/shard_map/ppermute | solution.py:849
  507.5 46.4 %collective-permute-start.33 = (bf16[1024,768]{1,0:T(8,128)(2,1)}, bf16[1024,768]{1,0:T(8,128)(2,1)}, u32[]{:S(2)}, u32[]{:S(2)}) collective-permute-start(bf16[1024,768]{1,0:T(8,128)(2,1)} %copy-done.20), channel_id=1, source_target_pairs={{0,1},{1,0},{2,3},{3,2},{4,5},{5,4},{6,7},{7,6},{8,9},{9,8},{10,11... | collective-permute-start | bytes 4718600 | tf_op jit(solution)/shard_map/ppermute | solution.py:48
  514.6 43.1 %collective-permute-start.54 = (bf16[1024,768]{1,0:T(8,128)(2,1)}, bf16[1024,768]{1,0:T(8,128)(2,1)}, u32[]{:S(2)}, u32[]{:S(2)}) collective-permute-start(bf16[1024,768]{1,0:T(8,128)(2,1)} %convolution_convert_fusion), channel_id=1, source_target_pairs={{0,1},{1,0},{2,3},{3,2},{4,5},{5,4},{6,7},{7,6},{8,9},{9,8},{10,11... | collective-permute-start | bytes 4718600 | tf_op jit(solution)/shard_map/ppermute | solution.py:48
  518.2 17.5 %collective-permute-start.103 = (bf16[2,96,896]{2,1,0:T(8,128)(2,1)S(1)}, bf16[2,96,896]{2,1,0:T(8,128)(2,1)}, u32[]{:S(2)}, u32[]{:S(2)}) collective-permute-start(bf16[2,96,896]{2,1,0:T(8,128)(2,1)S(1)} %pad_maximum_fusion.2.refs_8_), channel_id=1, source_target_pairs={{8,0},{16,8},{24,16},{28,24},{20,28},{12,20},{4,12},{0,4},{1,9},{9... | collective-permute-start | bytes 1032200 | tf_op jit(solution)/shard_map/ppermute | solution.py:849
  527.9 16.5 %collective-permute-start.87 = (bf16[1,768,384]{2,1,0:T(8,128)(2,1)}, bf16[1,768,384]{2,1,0:T(8,128)(2,1)S(1)}, u32[]{:S(2)}, u32[]{:S(2)}) collective-permute-start(bf16[1,768,384]{2,1,0:T(8,128)(2,1)} %collective-permute-done.84.refs_0_), channel_id=1, source_target_pairs={{0,8},{8,16},{16,24},{24,28},{28,20},{20,12},{12,4},{4,0},{9,1},{1... | collective-permute-start | bytes 1769480 | tf_op jit(solution)/shard_map/ppermute | solution.py:849
  528.2 23.9 %collective-permute-start.88 = (bf16[1,768,384]{2,1,0:T(8,128)(2,1)S(1)}, bf16[1,768,384]{2,1,0:T(8,128)(2,1)S(1)}, u32[]{:S(2)}, u32[]{:S(2)}) collective-permute-start(bf16[1,768,384]{2,1,0:T(8,128)(2,1)S(1)} %collective-permute-done.85.refs_1_), channel_id=1, source_target_pairs={{8,0},{16,8},{24,16},{28,24},{20,28},{12,20},{4,12},{0,4},{1,9},{9... | collective-permute-start | bytes 1769480 | tf_op jit(solution)/shard_map/ppermute | solution.py:849
  551.8 16.3 %collective-permute-start.90 = (bf16[1,768,384]{2,1,0:T(8,128)(2,1)S(1)}, bf16[1,768,384]{2,1,0:T(8,128)(2,1)S(1)}, u32[]{:S(2)}, u32[]{:S(2)}) collective-permute-start(bf16[1,768,384]{2,1,0:T(8,128)(2,1)S(1)} %collective-permute-done.87.refs_0_), channel_id=1, source_target_pairs={{0,8},{8,16},{16,24},{24,28},{28,20},{20,12},{12,4},{4,0},{9,1},{1... | collective-permute-start | bytes 1769480 | tf_op jit(solution)/shard_map/ppermute | solution.py:849
  552.1 21.5 %collective-permute-start.91 = (bf16[1,768,384]{2,1,0:T(8,128)(2,1)S(1)}, bf16[1,768,384]{2,1,0:T(8,128)(2,1)S(1)}, u32[]{:S(2)}, u32[]{:S(2)}) collective-permute-start(bf16[1,768,384]{2,1,0:T(8,128)(2,1)S(1)} %collective-permute-done.88.refs_1_), channel_id=1, source_target_pairs={{8,0},{16,8},{24,16},{28,24},{20,28},{12,20},{4,12},{0,4},{1,9},{9... | collective-permute-start | bytes 1769480 | tf_op jit(solution)/shard_map/ppermute | solution.py:849
  556.9 38.0 %collective-permute-start.34 = (bf16[512,768]{1,0:T(8,128)(2,1)}, bf16[512,768]{1,0:T(8,128)(2,1)}, u32[]{:S(2)}, u32[]{:S(2)}) collective-permute-start(bf16[512,768]{1,0:T(8,128)(2,1)} %dynamic-slice_convert_fusion.1), channel_id=1, source_target_pairs={{0,2},{2,0},{1,3},{3,1},{4,6},{6,4},{5,7},{7,5},{8,10},{10,8},{9,1... | collective-permute-start | bytes 2359304 | tf_op jit(solution)/shard_map/ppermute | solution.py:48
  557.4 16.2 %collective-permute-start.89 = (bf16[2,96,896]{2,1,0:T(8,128)(2,1)}, bf16[2,96,896]{2,1,0:T(8,128)(2,1)}, u32[]{:S(2)}, u32[]{:S(2)}) collective-permute-start(bf16[2,96,896]{2,1,0:T(8,128)(2,1)} %collective-permute-done.86.refs_2_), channel_id=1, source_target_pairs={{0,8},{8,16},{16,24},{24,28},{28,20},{20,12},{12,4},{4,0},{9,1},{1... | collective-permute-start | bytes 1032200 | tf_op jit(solution)/shard_map/ppermute | solution.py:849
  557.7 19.2 %collective-permute-start.105 = (bf16[2,96,896]{2,1,0:T(8,128)(2,1)S(1)}, bf16[2,96,896]{2,1,0:T(8,128)(2,1)S(1)}, u32[]{:S(2)}, u32[]{:S(2)}) collective-permute-start(bf16[2,96,896]{2,1,0:T(8,128)(2,1)S(1)} %collective-permute-done.104.refs_10_), channel_id=1, source_target_pairs={{8,0},{16,8},{24,16},{28,24},{20,28},{12,20},{4,12},{0,4},{1,9},{9... | collective-permute-start | bytes 1032200 | tf_op jit(solution)/shard_map/ppermute | solution.py:849
  568.1 18.0 %collective-permute-start.93 = (bf16[1,768,384]{2,1,0:T(8,128)(2,1)S(1)}, bf16[1,768,384]{2,1,0:T(8,128)(2,1)S(1)}, u32[]{:S(2)}, u32[]{:S(2)}) collective-permute-start(bf16[1,768,384]{2,1,0:T(8,128)(2,1)S(1)} %collective-permute-done.90.refs_0_), channel_id=1, source_target_pairs={{0,8},{8,16},{16,24},{24,28},{28,20},{20,12},{12,4},{4,0},{9,1},{1... | collective-permute-start | bytes 1769480 | tf_op jit(solution)/shard_map/ppermute | solution.py:849
  573.6 19.6 %collective-permute-start.94 = (bf16[1,768,384]{2,1,0:T(8,128)(2,1)S(1)}, bf16[1,768,384]{2,1,0:T(8,128)(2,1)S(1)}, u32[]{:S(2)}, u32[]{:S(2)}) collective-permute-start(bf16[1,768,384]{2,1,0:T(8,128)(2,1)S(1)} %collective-permute-done.91.refs_1_), channel_id=1, source_target_pairs={{8,0},{16,8},{24,16},{28,24},{20,28},{12,20},{4,12},{0,4},{1,9},{9... | collective-permute-start | bytes 1769480 | tf_op jit(solution)/shard_map/ppermute | solution.py:849
  576.3 21.5 %collective-permute-start.55 = (bf16[512,768]{1,0:T(8,128)(2,1)}, bf16[512,768]{1,0:T(8,128)(2,1)}, u32[]{:S(2)}, u32[]{:S(2)}) collective-permute-start(bf16[512,768]{1,0:T(8,128)(2,1)} %dynamic-slice_convert_fusion), channel_id=1, source_target_pairs={{0,2},{2,0},{1,3},{3,1},{4,6},{6,4},{5,7},{7,5},{8,10},{10,8},{9,1... | collective-permute-start | bytes 2359304 | tf_op jit(solution)/shard_map/ppermute | solution.py:48
  593.2 19.0 %collective-permute-start.97 = (bf16[1,768,384]{2,1,0:T(8,128)(2,1)S(1)}, bf16[1,768,384]{2,1,0:T(8,128)(2,1)S(1)}, u32[]{:S(2)}, u32[]{:S(2)}) collective-permute-start(bf16[1,768,384]{2,1,0:T(8,128)(2,1)S(1)} %collective-permute-done.94.refs_1_), channel_id=1, source_target_pairs={{8,0},{16,8},{24,16},{28,24},{20,28},{12,20},{4,12},{0,4},{1,9},{9... | collective-permute-start | bytes 1769480 | tf_op jit(solution)/shard_map/ppermute | solution.py:849
  599.7 17.2 %collective-permute-start.107 = (bf16[2,96,896]{2,1,0:T(8,128)(2,1)S(1)}, bf16[2,96,896]{2,1,0:T(8,128)(2,1)S(1)}, u32[]{:S(2)}, u32[]{:S(2)}) collective-permute-start(bf16[2,96,896]{2,1,0:T(8,128)(2,1)S(1)} %collective-permute-done.106.refs_12_), channel_id=1, source_target_pairs={{8,0},{16,8},{24,16},{28,24},{20,28},{12,20},{4,12},{0,4},{1,9},{9... | collective-permute-start | bytes 1032200 | tf_op jit(solution)/shard_map/ppermute | solution.py:849
  608.6 30.5 %collective-permute-start.99 = (bf16[1,768,384]{2,1,0:T(8,128)(2,1)S(1)}, bf16[1,768,384]{2,1,0:T(8,128)(2,1)S(1)}, u32[]{:S(2)}, u32[]{:S(2)}) collective-permute-start(bf16[1,768,384]{2,1,0:T(8,128)(2,1)S(1)} %collective-permute-done.96.refs_0_), channel_id=1, source_target_pairs={{0,8},{8,16},{16,24},{24,28},{28,20},{20,12},{12,4},{4,0},{9,1},{1... | collective-permute-start | bytes 1769480 | tf_op jit(solution)/shard_map/ppermute | solution.py:849
  612.3 26.8 %collective-permute-start.100 = (bf16[1,768,384]{2,1,0:T(8,128)(2,1)S(1)}, bf16[1,768,384]{2,1,0:T(8,128)(2,1)S(1)}, u32[]{:S(2)}, u32[]{:S(2)}) collective-permute-start(bf16[1,768,384]{2,1,0:T(8,128)(2,1)S(1)} %collective-permute-done.97.refs_1_), channel_id=1, source_target_pairs={{8,0},{16,8},{24,16},{28,24},{20,28},{12,20},{4,12},{0,4},{1,9},{9... | collective-permute-start | bytes 1769480 | tf_op jit(solution)/shard_map/ppermute | solution.py:849
  616.9 24.2 %collective-permute-start.98 = (bf16[2,96,896]{2,1,0:T(8,128)(2,1)S(1)}, bf16[2,96,896]{2,1,0:T(8,128)(2,1)S(1)}, u32[]{:S(2)}, u32[]{:S(2)}) collective-permute-start(bf16[2,96,896]{2,1,0:T(8,128)(2,1)S(1)} %collective-permute-done.95.refs_5_), channel_id=1, source_target_pairs={{0,8},{8,16},{16,24},{24,28},{28,20},{20,12},{12,4},{4,0},{9,1},{1... | collective-permute-start | bytes 1032200 | tf_op jit(solution)/shard_map/ppermute | solution.py:849
  (137 other events, 1372.9 us)

commit v7 on v6

--- a/solution.py
+++ b/solution.py
@@ -564,45 +564,110 @@
     )(order, *x, *o, gates, *weights, *weights, *kept)
 
 
-def mix_kernel(back, group, order_ref, *refs):
+def mix_back_kernel(group, order_ref, *refs):
     acts_ref, shared_ref = refs[0:2]
-    each = 2 if back else 1
-    count = 2 * group * each
-    weights = refs[2 : 2 + count]
-    shared = refs[2 + count : 2 + count + 2 * each]
-    out_ref, total_ref = refs[2 + count + 2 * each :]
+    count = 8 * group
+    weights, shared = refs[2 : 2 + count], refs[2 + count : 10 + count]
+    own_ref, other_ref, total_ref = refs[10 + count :]
+    step = pl.program_id(0)
+
+    def gathered(parts, half):
+        picked = [p[0] for k in range(len(parts) // 4) for p in parts[4 * k + 2 * half :][:2]]
+        return jnp.concatenate(picked, axis=1)
+
+    acts = jnp.concatenate([acts_ref[g] for g in range(group)], axis=1)
+    for half in range(2):
+        term = dot_nt(acts, gathered(weights, half))
+
+        @pl.when(step == 0)
+        def _(half=half, term=term):
+            total_ref[half] = term + dot_nt(shared_ref[0], gathered(shared, half))
+
+        @pl.when(step > 0)
+        def _(half=half, term=term):
+            total_ref[half] += term
+
+    @pl.when(step == pl.num_programs(0) - 1)
+    def _():
+        own_ref[...] = total_ref[0]
+        other_ref[...] = total_ref[1].astype(BF16)
+
+
+def mix_back(part, order, acts, shared_acts, weights, shared_weights):
+    pairs, rows, width = acts.shape
+    rows = rows // 2
+    features = weights[0].shape[1]
+    group = 2 if pairs % 2 == 0 else 1
+
+    def spec(place):
+        return pl.BlockSpec(
+            (1, features, LANES), lambda i, o: (place(i, o)[0], 0, place(i, o)[1])
+        )
+
+    def routed(k):
+        return spec(lambda i, o: (o[2 * group * i + k], o[o.shape[0] - 1]))
+
+    def common(k):
+        return spec(lambda i, o: (0, 2 * o[o.shape[0] - 1] + k))
+
+    whole = pl.BlockSpec((rows, features), lambda i, o: (0, 0))
+    return pl.pallas_call(
+        functools.partial(mix_back_kernel, group),
+        grid_spec=pltpu.PrefetchScalarGridSpec(
+            num_scalar_prefetch=1,
+            grid=(pairs // group,),
+            in_specs=[
+                pl.BlockSpec((group, rows, width), lambda i, o: (i, part, 0)),
+                pl.BlockSpec((1, rows, width), lambda i, o: (0, part, 0)),
+            ]
+            + [routed(k) for k in range(2 * group) for _ in weights]
+            + [common(k) for k in range(2) for _ in weights],
+            out_specs=[whole, whole],
+            scratch_shapes=[pltpu.VMEM((2, rows, features), F32)],
+        ),
+        out_shape=[
+            jax.ShapeDtypeStruct((rows, features), F32),
+            jax.ShapeDtypeStruct((rows, features), BF16),
+        ],
+        compiler_params=params(48, "arbitrary"),
+        cost_estimate=SMALL,
+        name="mix_back",
+    )(order, acts, shared_acts, *weights * (2 * group), *shared_weights * 2)
+
+
+def mix_out_kernel(group, order_ref, *refs):
+    acts_ref, shared_ref = refs[0:2]
+    count = 2 * group
+    weights, shared = refs[2 : 2 + count], refs[2 + count : 4 + count]
+    out_ref, total_ref = refs[4 + count :]
     step = pl.program_id(0)
     rows = out_ref.shape[0]
     tile = 512
-    times = dot_nt if back else dot
-    along = 1 if back else 0
 
     @pl.when(step == 0)
     def _():
-        both = jnp.concatenate([w[0] for w in shared], axis=along)
+        both = jnp.concatenate([w[0] for w in shared], axis=0)
         for t in range(rows // tile):
             at = slice(t * tile, (t + 1) * tile)
-            total_ref[at, :] = times(shared_ref[0, at, :], both)
-
-    both = jnp.concatenate([w[0] for w in weights], axis=along)
+            total_ref[at, :] = dot(shared_ref[0, at, :], both)
+
+    both = jnp.concatenate([w[0] for w in weights], axis=0)
     for t in range(rows // tile):
         at = slice(t * tile, (t + 1) * tile)
         acts = jnp.concatenate([acts_ref[g, at, :] for g in range(group)], axis=1)
-        total_ref[at, :] += times(acts, both)
+        total_ref[at, :] += dot(acts, both)
 
     @pl.when(step == pl.num_programs(0) - 1)
     def _():
         out_ref[...] = total_ref[...].astype(out_ref.dtype)
 
 
-def mix(back, dtype, order, acts, shared_acts, weights, shared_weights):
+def mix_out(dtype, order, acts, shared_acts, weights, shared_weights):
     pairs, rows, width = acts.shape
-    features = weights[0].shape[1] if back else weights[0].shape[2]
+    features = weights.shape[2]
     group = 4 if pairs % 4 == 0 else 1
 
     def spec(place):
-        if back:
-            return pl.BlockSpec((1, features, LANES), lambda i, o: (place(i, o)[0], 0, place(i, o)[1]))
         return pl.BlockSpec((1, LANES, features), lambda i, o: (*place(i, o), 0))
 
     def routed(k):
@@ -612,7 +677,7 @@
         return spec(lambda i, o: (0, 2 * o[o.shape[0] - 1] + k))
 
     return pl.pallas_call(
-        functools.partial(mix_kernel, back, group),
+        functools.partial(mix_out_kernel, group),
         grid_spec=pltpu.PrefetchScalarGridSpec(
             num_scalar_prefetch=1,
             grid=(pairs // group,),
@@ -620,16 +685,112 @@
                 pl.BlockSpec((group, rows, width), lambda i, o: (i, 0, 0)),
                 pl.BlockSpec((1, rows, width), lambda i, o: (0, 0, 0)),
             ]
-            + [routed(k) for k in range(2 * group) for _ in weights]
-            + [common(k) for k in range(2) for _ in weights],
+            + [routed(k) for k in range(2 * group)]
+            + [common(k) for k in range(2)],
             out_specs=pl.BlockSpec((rows, features), lambda i, o: (0, 0)),
             scratch_shapes=[pltpu.VMEM((rows, features), F32)],
         ),
         out_shape=jax.ShapeDtypeStruct((rows, features), dtype),
         compiler_params=params(48, "arbitrary"),
         cost_estimate=SMALL,
-        name="mix",
-    )(order, acts, shared_acts, *weights * (2 * group), *shared_weights * 2)
+        name="mix_out",
+    )(order, acts, shared_acts, *[weights] * (2 * group), *[shared_weights] * 2)
+
+
+def chip_sum_kernel(own_ref, other_ref, total_ref, rounded_ref):
+    total = own_ref[...] + other_ref[...].astype(F32)
+    total_ref[...] = total
+    rounded_ref[...] = total.astype(BF16)
+
+
+def chip_sum(own, other):
+    rows, features = own.shape
+    spec = pl.BlockSpec((TOKEN_TILE, features), lambda i: (i, 0))
+    return pl.pallas_call(
+        chip_sum_kernel,
+        grid=(rows // TOKEN_TILE,),
+        out_shape=[
+            jax.ShapeDtypeStruct((rows, features), F32),
+            jax.ShapeDtypeStruct((rows, features), BF16),
+        ],
+        in_specs=[spec, spec],
+        out_specs=[spec, spec],
+        compiler_params=params(16, "arbitrary"),
+        cost_estimate=SMALL,
+        name="chip_sum",
+    )(own, other)
+
+
+def norm_back_kernel(tiles, place_ref, *refs):
+    sums, came = refs[0:2], refs[2:4]
+    hidden_ref, scale_ref, gains_ref = refs[4:7]
+    grad_ref, product_ref, gain_ref = refs[7:10]
+    step = pl.program_id(0)
+    part = (step >= tiles // 2).astype(jnp.int32)
+    terms = [sums[k][...] + came[k][...].astype(F32) for k in range(2)]
+    grad = jnp.where(part == 0, terms[0], terms[1])
+    hidden = hidden_ref[...]
+    grad_ref[...] = grad
+    product_ref[...] = jnp.sum(grad * gains_ref[1:2, :] * hidden, axis=1, keepdims=True)
+
+    @pl.when(step == 0)
+    def _():
+        gain_ref[...] = jnp.zeros_like(gain_ref)
+
+    @pl.when(part == place_ref[0])
+    def _():
+        gain_ref[...] += jnp.sum(grad * hidden * scale_ref[...], axis=0, keepdims=True)
+
+
+def norm_back(place, sums, came, hidden, scale, gains):
+    rows, features = hidden.shape
+    tiles = rows // TOKEN_TILE
+    halfwise = pl.BlockSpec((TOKEN_TILE, features), lambda i, p: (i % (tiles // 2), 0))
+    return pl.pallas_call(
+        functools.partial(norm_back_kernel, tiles),
+        grid_spec=pltpu.PrefetchScalarGridSpec(
+            num_scalar_prefetch=1,
+            grid=(tiles,),
+            in_specs=[halfwise] * 4 + [rowwise(features), rowwise(1), whole(2, features)],
+            out_specs=[rowwise(features), rowwise(1), whole(1, features)],
+        ),
+        out_shape=[
+            jax.ShapeDtypeStruct((rows, features), F32),
+            jax.ShapeDtypeStruct((rows, 1), F32),
+            jax.ShapeDtypeStruct((1, features), F32),
+        ],
+        compiler_params=params(48, "arbitrary"),
+        cost_estimate=SMALL,
+        name="norm_back",
+    )(place, *sums, *came, hidden, scale, gains)
+
+
+def norm_back_end_kernel(grad_ref, own_ref, other_ref, hidden_ref, scale_ref, gains_ref, out_grad_ref, hidden_grad_ref, rounded_ref):
+    scale = scale_ref[...]
+    mean = (own_ref[...] + other_ref[...]) * (1.0 / D)
+    result = out_grad_ref[...].astype(F32) + scale * (grad_ref[...] * gains_ref[1:2, :])
+    result = result - hidden_ref[...] * (scale * scale * scale * mean)
+    hidden_grad_ref[...] = result
+    rounded_ref[...] = result.astype(BF16)
+
+
+def norm_back_end(grad, products, products_c, hidden, scale, gains, out_grad):
+    rows, features = hidden.shape
+    tile = pl.BlockSpec((TOKEN_TILE, features), lambda i: (i, 0))
+    column = pl.BlockSpec((TOKEN_TILE, 1), lambda i: (i, 0))
+    return pl.pallas_call(
+        norm_back_end_kernel,
+        grid=(rows // TOKEN_TILE,),
+        in_specs=[tile, column, column, tile, column, pl.BlockSpec(gains.shape, lambda i: (0, 0)), tile],
+        out_specs=[tile, tile],
+        out_shape=[
+            jax.ShapeDtypeStruct((rows, features), F32),
+            jax.ShapeDtypeStruct((rows, features), BF16),
+        ],
+        compiler_params=params(48, "arbitrary"),
+        cost_estimate=SMALL,
+        name="norm_back_end",
+    )(grad, products, products_c, hidden, scale, gains, out_grad)
 
 
 def ring_of(size):
@@ -689,27 +850,71 @@
     )(plan, *chunks, *outs)
 
 
-def late_chunk_kernel(plan_ref, pack_ref, *refs):
-    *came, out_ref = refs
+def ring_sum_kernel(came_ref, mine_ref, *outs):
+    total = (came_ref[...].astype(F32) + mine_ref[...].astype(F32)).astype(BF16)
+    if len(outs) == 1:
+        outs[0][...] = total
+    else:
+        half = pl.program_id(1) // (pl.num_programs(1) // 2)
+        for k, out_ref in enumerate(outs):
+
+            @pl.when(half == k)
+            def _(out_ref=out_ref):
+                out_ref[...] = total
+
+
+def ring_sum(came, mine, halved):
+    count, rows, lanes = came.shape
+    tiles = 4
+    spec = pl.BlockSpec((1, rows // tiles, lanes), lambda i, j: (i, j, 0))
+
+    def half(k):
+        first = k * tiles // 2
+        last = tiles // 2 - 1
+        return pl.BlockSpec(
+            (1, rows // tiles, lanes), lambda i, j: (i, jnp.clip(j - first, 0, last), 0)
+        )
+
+    shapes = [jax.ShapeDtypeStruct((count, rows // 2, lanes), BF16)] * 2
+    return pl.pallas_call(
+        ring_sum_kernel,
+        grid=(count, tiles),
+        in_specs=[spec, spec],
+        out_specs=[half(0), half(1)] if halved else spec,
+        out_shape=shapes if halved else jax.ShapeDtypeStruct(came.shape, BF16),
+        compiler_params=params(16, "arbitrary", "arbitrary"),
+        cost_estimate=SMALL,
+        name="ring_sum",
+    )(came, mine)
+
+
+def late_chunk_kernel(came, plan_ref, pack_ref, *refs):
+    values = pack_ref[:, 0]
     if came:
-        out_ref[...] = (came[0][...].astype(F32) + pack_ref[:, 0].astype(F32)).astype(BF16)
+        values = (refs[0][...].astype(F32) + values.astype(F32)).astype(BF16)
+    outs = refs[came:]
+    if len(outs) == 1:
+        outs[0][...] = values
     else:
-        out_ref[...] = pack_ref[:, 0]
-
-
-def late_chunk(plan, at, pack, came):
+        for k, out_ref in enumerate(outs):
+            out_ref[...] = values[k]
+
+
+def late_chunk(plan, at, pack, came, halved):
     halves, _, rows, lanes = pack.shape
     spec = pl.BlockSpec((halves, rows, lanes), lambda i, n: (0, 0, 0))
-    return pl.pallas_call(
-        late_chunk_kernel,
+    half = pl.BlockSpec((rows, lanes), lambda i, n: (0, 0))
+    halfs = [jax.ShapeDtypeStruct((rows, lanes), BF16)] * 2
+    return pl.pallas_call(
+        functools.partial(late_chunk_kernel, len(came)),
         grid_spec=pltpu.PrefetchScalarGridSpec(
             num_scalar_prefetch=1,
             grid=(1,),
             in_specs=[pl.BlockSpec((halves, 1, rows, lanes), lambda i, n: (0, n[at], 0, 0))]
             + [spec] * len(came),
-            out_specs=spec,
+            out_specs=[half] * 2 if halved else spec,
         ),
-        out_shape=jax.ShapeDtypeStruct((halves, rows, lanes), BF16),
+        out_shape=halfs if halved else jax.ShapeDtypeStruct((halves, rows, lanes), BF16),
         compiler_params=params(16, "arbitrary"),
         cost_estimate=SMALL,
         name="late_chunk",
@@ -719,14 +924,14 @@
 def unpack_late_kernel(first_step, steps, plan_ref, *refs):
     chunks = refs[0 : 2 * steps]
     sgate, sup, sdown, query, key, value, out, all_ref = refs[2 * steps :]
-    rows, features = chunks[0].shape[1], all_ref.shape[2]
+    rows, features = chunks[0].shape[0] // 2, all_ref.shape[2]
     for k in range(2):
         for step in range(steps):
             at = plan_ref[first_step + 2 * step + k] * rows
             for c in range(2):
                 all_ref[k, c, pl.ds(pl.multiple_of(at, rows), rows), :] = chunks[
                     steps * k + step
-                ][c]
+                ][c * rows : (c + 1) * rows, :]
     flipped = plan_ref[plan_ref.shape[0] - 1] != 0
     for c in range(2):
         for b in range(14):
@@ -755,14 +960,14 @@
 
 def unpack_late(plan, first_step, chunks, shapes):
     steps = len(chunks[0])
-    halves, rows, lanes = chunks[0][0].shape
+    rows, lanes = chunks[0][0].shape[0] // 2, chunks[0][0].shape[1]
     spec = pl.BlockSpec(memory_space=pltpu.VMEM)
     return pl.pallas_call(
         functools.partial(unpack_late_kernel, first_step, steps),
         in_specs=[pl.BlockSpec(memory_space=pltpu.SMEM)] + [spec] * (2 * steps),
         out_specs=[spec] * len(shapes),
         out_shape=[jax.ShapeDtypeStruct(shape, F32) for shape in shapes],
-        scratch_shapes=[pltpu.VMEM((2, halves, steps * rows, lanes), BF16)],
+        scratch_shapes=[pltpu.VMEM((2, 2, steps * rows, lanes), BF16)],
         compiler_params=params(48),
         cost_estimate=SMALL,
         name="unpack_late",
@@ -791,11 +996,7 @@
     return np.asarray(rows, np.int32)
 
 
-LATE_ROUND = 1
-
-
-def add_rounded(left, right):
-    return (left.astype(F32) + right.astype(F32)).astype(BF16)
+LATE_ROUND = 0
 
 
 def body(
@@ -877,13 +1078,11 @@
     out_y = swap(out_y, "row")
     tokens_y = after(tokens_y, near[2], out_y)
     tokens_yc = swap(tokens_y, "col")
-    grad_cut = local_rows // 8 * 5
-    grad_y = swap(after(out_grad[:grad_cut], tokens_y), "row")
+    grad_y = swap(after(out_grad, tokens_y), "row")
     far = project_half(tokens_y, tokens_yc)
-
     shares = [out_y]
     for k in range(1, count):
-        part = out_y if k == 1 else after(out_y, far[2])
+        part = out_y if k < 3 else after(out_y, far[2])
         shares.append(lax.ppermute(part, "dp", [(m, m ^ k) for m in range(dp_size)]))
     where = after(where, grad_y, *shares)
 
@@ -902,12 +1101,11 @@
         out_c,
     )
     down_c = swap(after(w_down, tokens_yc), "col")
-    rest_y = swap(after(out_grad[grad_cut:], attended_c), "row")
     attended_y = after(attended_y, before[0])
     out_y = join(member, *shares)
     out_yc = swap(out_y, "col")
     attended_yc = swap(attended_y, "col")
-    grad_own = join(row, out_grad, jnp.concatenate([grad_y, rest_y], axis=0))
+    grad_own = join(row, out_grad, grad_y)
     grad_other = swap(grad_own, "col")
     hidden, x_own, x_other, scale_ffn = hidden_after(
         where, before, [attended_y, attended_yc], out_y, out_yc, gains, gains_c
@@ -957,8 +1155,7 @@
             nonlocal kept
             result = run(first, last, order, tuple(kept))
             kept = result[2:]
-            for at in range(first, last):
-                runs[at] = (result[0], result[1], at - first)
+            runs[first] = result[0:2]
             return kept[0]
 
         return work
@@ -969,19 +1166,26 @@
         )
         return runs["shared"][2]
 
-    def work_mix(back, half):
+    def work_back(part):
         def work(order):
-            pick = slice(2 * half, 2 * half + 2) if back else slice(4 + half, 5 + half)
-            mixed[back, half] = mix(
-                back,
+            mixed[True, part] = mix_back(
+                part, order, kept[0], runs["shared"][2], routed[:4], shared[:4]
+            )
+            return mixed[True, part][1]
+
+        return work
+
+    def work_out(half):
+        def work(order):
+            mixed[False, half] = mix_out(
                 BF16 if half else F32,
                 order,
-                kept[0 if back else 1],
-                runs["shared"][2 if back else 3],
-                routed[pick],
-                shared[pick],
+                kept[1],
+                runs["shared"][3],
+                routed[4 + half],
+                shared[4 + half],
             )
-            return mixed[back, half]
+            return mixed[False, half]
 
         return work
 
@@ -995,18 +1199,20 @@
 
     normed = {}
 
+    def row_sums(part):
+        own, other = mixed[True, part]
+        both = chip_sum(own, swap(other, "col"))
+        return both, swap(both[1], "row")
+
     def work_hidden(order):
-        normed_grad = mixed[True, 0] + swap(mixed[True, 1], "col").astype(F32)
-        came = swap(normed_grad.astype(BF16), "row")
-        normed_grad = normed_grad + after(came, order).astype(F32)
-        scaled = normed_grad * norm_gain_ffn
-        products = jnp.sum(scaled * hidden, axis=1, keepdims=True)
-        mean = (products + swap(products, "col")) / D
-        normed["gain"] = jnp.sum(my_rows(normed_grad * hidden * scale_ffn), axis=0)
-        normed["hidden"] = (
-            grad_own.astype(F32) + scale_ffn * scaled - hidden * scale_ffn**3 * mean
+        both, came = zip(*(normed["sums"][part] for part in range(2)), strict=True)
+        grads, products, normed["gain"] = norm_back(
+            where, [b[0] for b in both], [after(c, order) for c in came], hidden, scale_ffn, gains
         )
-        normed["grad"] = normed["hidden"].astype(BF16)
+        products_c = swap(products, "col")
+        normed["hidden"], normed["grad"] = norm_back_end(
+            grads, products, products_c, hidden, scale_ffn, gains, grad_own
+        )
         normed["grad_c"] = swap(normed["grad"], "col")
         return normed["grad"]
 
@@ -1016,9 +1222,31 @@
         )
         return normed["qkv"]
 
+    def work_late(order):
+        normed["packs"] = late_grads(
+            after(where, order),
+            near[0:2],
+            far[0:2],
+            normed["qkv"],
+            attended,
+            normed["grad"],
+            normed["grad_c"],
+            runs["shared"][0:2],
+        )
+        return normed["packs"][0]
+
+    def with_sums(part):
+        def work(order):
+            result = work_back(part)(order)
+            normed.setdefault("sums", {})[part] = row_sums(part)
+            return result
+
+        return work
+
     tasks = [work_experts(at, at + each) for at in range(each, pairs_total, each)]
-    tasks += [work_shared, work_mix(True, 1), work_mix(True, 0), work_mix(False, 1), work_mix(False, 0)]
-    tasks += [None] * (2 * ring_size - 3 - len(tasks)) + [work_hidden, work_attend]
+    tasks += [work_shared, with_sums(0), with_sums(1), work_out(1), work_out(0)]
+    ends = [work_hidden, work_attend, work_late]
+    tasks += [None] * (2 * ring_size - 1 - len(tasks) - len(ends)) + ends
     got = [None, None]
     if ring_size > 1:
         got[0] = send(sums[0], 0)
@@ -1030,54 +1258,47 @@
             task = tasks.pop(0) if tasks else None
             if task:
                 last = [task(after(order, *last))]
-            got[k] = after(got[k], *last)
-            parts = [runs[at] for at in range(each * s, each * s + each)]
-            mine = [p[k][p[2] : p[2] + 1] for p in parts]
-            mine = mine[0] if each == 1 else jnp.concatenate(mine, axis=0)
-            sums[k] = add_rounded(got[k], mine)
+            sums[k] = ring_sum(after(got[k], *last), runs[each * s][k], s + 1 == ring_size)
             if s + 1 < ring_size:
                 got[k] = send(sums[k], k)
+            else:
+                sums[k], got[k] = sums[k]
     for task in tasks:
         if task:
             task(after(order, *sums))
-    sums = [across_rings(total) for total in sums]
-    waves = [[total[:, :local_features] for total in sums]]
-    crossed = [swap(total[:, local_features:], "col") for total in sums]
+    if ring_size == 1:
+        got = [total[:, local_features:] for total in sums]
+        sums = [total[:, :local_features] for total in sums]
+    waves = [[across_rings(total) for total in sums]]
+    crossed = [swap(across_rings(total), "col") for total in got]
     waves.append([crossed[1], crossed[0]])
 
     hidden_grad, attn_grad, attn_grad_c = normed["hidden"], normed["grad"], normed["grad_c"]
     gain_ffn_part, qkv_grad = normed["gain"], normed["qkv"]
-    packs = late_grads(
-        where,
-        near[0:2],
-        far[0:2],
-        qkv_grad,
-        attended,
-        attn_grad,
-        attn_grad_c,
-        runs["shared"][0:2],
-    )
+    packs = normed["packs"]
 
     packs = [
         pack.reshape(2, ring_size, local_features // ring_size, pack.shape[2]) for pack in packs
     ]
     chunks_first = 2 * experts
-    late = [late_chunk(plan, chunks_first + k, packs[k], ()) for k in range(2)]
+    late_total = 2 * (ring_size - 1)
+    late = [
+        late_chunk(plan, chunks_first + k, packs[k], (), late_total == 0) for k in range(2)
+    ]
     late_out = [[], []]
     late_done = 0
-    late_total = 2 * (ring_size - 1)
 
     def late_turn():
-        totals = [across_rings(values) for values in late]
-        others = [swap(values[1], "col") for values in totals]
+        owns = [across_rings(values[0]) for values in late]
+        others = [swap(across_rings(values[1]), "col") for values in late]
         for k in range(2):
-            late[k] = in_order(totals[k][0:1], others[1 - k][None], col, 0)
+            late[k] = join(col, owns[k], others[1 - k])
             late_out[k].append(late[k])
 
     def late_finish(k, values):
         if late_done < ring_size:
             at = chunks_first + 2 * late_done + k
-            late[k] = late_chunk(plan, at, packs[k], (values,))
+            late[k] = late_chunk(plan, at, packs[k], (values,), late_done == ring_size - 1)
         else:
             late[k] = values
             late_out[k].append(values)
@@ -1092,7 +1313,7 @@
         late_turn()
     rounds = [(wave, step) for wave in range(2) for step in range(ring_size - 1)]
     late_got = None
-    last = list(sums)
+    last = []
     for number, (wave, step) in enumerate(rounds):
         if step == 0:
             came = list(got) if number else None
@@ -1100,18 +1321,17 @@
         late_done += late_got is not None
         chunks = [None, None]
         for k in range(2):
-            chunks[k] = after(got[k], *last)
+            chunks[k] = after(got[k], *last) if last else got[k]
             got[k] = send(chunks[k], k)
             last = [chunks[k]]
             if late_got is not None:
                 late_finish(k, after(late_got[k], *last))
-                last = [late[k]]
+                last = list(late[k]) if late_done == ring_size - 1 else [late[k]]
         if late_got is not None and late_done == ring_size - 1:
             late_turn()
+        late_got = None
         if number >= LATE_ROUND and late_done < late_total:
-            late_got = [send(after(late[k], *chunks), k) for k in range(2)]
-        else:
-            late_got = None
+            late_got = [send(late[k], k) for k in range(2)]
         if step == 0 and number:
             placed = place_chunks(0, ring_size - 1, came, placed)
         placed = place_chunks(wave, step, chunks, placed)
@@ -1161,7 +1381,7 @@
         my_rows(hidden_grad) + scale_attn * scaled - tokens_f32 * scale_attn**3 * mean
     ).astype(BF16)
 
-    gain_parts = jnp.stack([gain_attn_part, gain_ffn_part])
+    gain_parts = jnp.concatenate([gain_attn_part[None], gain_ffn_part], axis=0)
     bit = 1
     while bit < ring_size:
         pairs = [(g + k, g + (k ^ bit)) for g in starts for k in range(ring_size)]

time: 667 us -> 670 us (level)
  Pallas kernels: 240 us -> 281 us
  other arithmetic: 40.4 us -> 13.6 us
  starting transfers between devices: 111 us -> 101 us
    pallas_call x20 -> x38, Pallas kernels: 51.5 us -> 92.5 us  [the longest x2 31.9 us: mix_back(): pl.pallas_call(functools.partial(mix_back_kernel, group), grid_spec=pltpu...]
    convert_element_type x15 -> x1, other arithmetic: 22.6 us -> 2.36 us  [body(): block_out = (my_rows(hidden) + ffn_rows).astype(BF16)]
    ppermute x70, starting transfers between devices: 83.4 us -> 71.5 us  [send(): return lax.ppermute(values, ('dp', 'col'), routes_of[which])]
    unnamed x182 -> x166, local copies, waits for them, and re-layouts: 17.3 us -> 25.2 us
    ppermute x34 -> x35, waiting for transfers between devices: 43.6 us -> 48.2 us  [swap(): return lax.ppermute(values, axis, [(0, 1), (1, 0)])]
    ppermute x34 -> x35, starting transfers between devices: 20 us -> 18.4 us  [swap(): return lax.ppermute(values, axis, [(0, 1), (1, 0)])]
  transfers between devices with their start and end apart: 110 -> 111, of which waited for: 47 -> 51; matrix products, arithmetic and copies ran while one was open for 8% -> 3% of each run, Pallas kernels for 34% -> 40%
where the time goes in v7:
time: 670 us; the launch traced here: 660 us
  Pallas kernels  281 us (42%)
  waiting for transfers between devices  228 us (34%)
  starting transfers between devices  101 us (15%)
  local copies, waits for them, and re-layouts  28.6 us (4%)
  other arithmetic  13.6 us (2%)
    ppermute x70, waiting for transfers between devices, send(): return lax.ppermute(values, ('dp', 'col'), routes_of[which])  161 us
    pallas_call x9, Pallas kernels, expert_grads(): pl.pallas_call(functools.partial(expert_kernel, shared, aliased, first),...  78.8 us
    ppermute x70, starting transfers between devices, send(): return lax.ppermute(values, ('dp', 'col'), routes_of[which])  71.5 us
    ppermute x35, waiting for transfers between devices, swap(): return lax.ppermute(values, axis, [(0, 1), (1, 0)])  48.2 us
    pallas_call x16, Pallas kernels, unpack(): pl.pallas_call(functools.partial(unpack_kernel, aliased), grid_spec=pltpu...  38.7 us
    pallas_call x2, Pallas kernels, mix_back(): pl.pallas_call(functools.partial(mix_back_kernel, group), grid_spec=pltpu...  31.9 us
    unnamed x166, local copies, waits for them, and re-layouts  25.2 us
    pallas_call x14, Pallas kernels, ring_sum(): pl.pallas_call(ring_sum_kernel, grid=(count, tiles), in_specs=[spec, spec...  22 us
  transfers between devices with their start and end apart: 111, of which 51 were waited for; matrix products, arithmetic and copies ran while one was open for 3% of the time, Pallas kernels for 40%

profile of v7, /device:TPU:0, one launch (start us, length us, event | category | flops | bytes accessed | tf_op | source)
XLA Modules:
  0.0 660.1 jit_solution(1459552454101571849)
XLA Ops:
  1.8 3.2 their_columns.1
  5.5 2.6 collective-permute-start
  8.3 4.9 collective-permute-done.2.gains_c_ref.refs_7_
  13.2 2.9 collective-permute-start.4
  17.9 4.5 project.2
  22.4 10.1 %collective-permute-done.4.refs_0_ = bf16[192,768]{1,0:T(8,128)(2,1)S(1)} collective-permute-done((bf16[192,768]{1,0:T(8,128)(2,1)}, bf16[192,768]{1,0:T(8,128)(2,1)S(1)}, u32[]{:S(2)}, u32[]{:S(2)}) %collective-permute-start.4) | collective-permute-done | bytes 294944 | tf_op jit(solution)/shard_map/ppermute | solution.py:48
  40.8 4.5 project.3
  50.8 5.0 collective-permute-done.5.refs_1_
  57.6 6.2 attend.1.refs_4_.refs_5_
  69.6 9.0 %hidden_before.1 = (f32[1024,768]{1,0:T(8,128)}, f32[1024,768]{1,0:T(8,128)}) custom-call(s32[3]{0:T(128)} %copy-done.55, bf16[512,768]{1,0:T(8,128)(2,1)} %refs_0_.2, bf16[512,768]{1,0:T(8,128)(2,1)} %copy-done.71, bf16[512,768]{1,0:T(8,128)(2,1)} %collective-permute-done.own_ref.refs_2_, bf16[512,768]{1,0:T(8,128)(2,1)} %copy-done.72, ...), custom_call_target="tpu_custom_call" | custom-call | flops 2415919104 | bytes 12582912 | tf_op jit(solution)/shard_map/hidden_before/pallas_call | solution.py:398
  78.6 5.6 collective-permute-done.12.refs_2_
  87.5 9.4 %hidden_after.1 = (f32[1024,768]{1,0:T(8,128)}, bf16[1024,768]{1,0:T(8,128)(2,1)}, bf16[1024,768]{1,0:T(8,128)(2,1)}, f32[1024,1]{1,0:T(8,128)}) custom-call(s32[3]{0:T(128)} %copy-done.55, f32[1024,768]{1,0:T(8,128)} %get-tuple-element.250.refs_0_, f32[1024,768]{1,0:T(8,128)} %get-tuple-element.251.refs_1_, ...), custom_call_target="tpu_custom_call" | custom-call | tf_op jit(solution)/shard_map/hidden_after/pallas_call | solution.py:420
  100.4 9.3 %expert_grads.9 = (bf16[1,1536,384]{2,1,0:T(8,128)(2,1)S(1)}, bf16[1,1536,384]{2,1,0:T(8,128)(2,1)S(1)}, bf16[8,1024,512]{2,1,0:T(8,128)(2,1)}, bf16[8,1024,256]{2,1,0:T(8,128)(2,1)S(1)}) custom-call(s32[63]{0:T(128)S(1)} %fusion.14.order_ref.plan_ref, bf16[1024,768]{1,0:T(8,128)(2,1)S(1)} %copy-done.5, bf16[1024,768]{1,0:T(8,128)(2,1)S(1)} %copy-done.6, ...), custom_call_target="tpu_custom_call" | custom-call | tf_op jit(solution)/shard_map/expert_grads/pallas_call | solution.py:543
  111.2 8.8 %expert_grads.10 = (bf16[1,1536,384]{2,1,0:T(8,128)(2,1)S(1)}, bf16[1,1536,384]{2,1,0:T(8,128)(2,1)S(1)}, bf16[8,1024,512]{2,1,0:T(8,128)(2,1)}, bf16[8,1024,256]{2,1,0:T(8,128)(2,1)S(1)}) custom-call(s32[63]{0:T(128)S(1)} %fusion.14.order_ref.plan_ref, bf16[1024,768]{1,0:T(8,128)(2,1)S(1)} %copy-done.5, ...), custom_call_target="tpu_custom_call", output_to_operand_aliasing={{2}: (18, {}), {3}: (19, {})} | custom-call | tf_op jit(solution)/shard_map/expert_grads/pallas_call | solution.py:543
  120.5 8.8 %expert_grads.11 = (bf16[1,1536,384]{2,1,0:T(8,128)(2,1)S(1)}, bf16[1,1536,384]{2,1,0:T(8,128)(2,1)S(1)}, bf16[8,1024,512]{2,1,0:T(8,128)(2,1)}, bf16[8,1024,256]{2,1,0:T(8,128)(2,1)S(1)}) custom-call(s32[63]{0:T(128)S(1)} %fusion.14.order_ref.plan_ref, bf16[1024,768]{1,0:T(8,128)(2,1)S(1)} %copy-done.5, ...), custom_call_target="tpu_custom_call", output_to_operand_aliasing={{2}: (18, {}), {3}: (19, {})} | custom-call | tf_op jit(solution)/shard_map/expert_grads/pallas_call | solution.py:543
  132.2 8.8 %expert_grads.12 = (bf16[1,1536,384]{2,1,0:T(8,128)(2,1)S(1)}, bf16[1,1536,384]{2,1,0:T(8,128)(2,1)S(1)}, bf16[8,1024,512]{2,1,0:T(8,128)(2,1)}, bf16[8,1024,256]{2,1,0:T(8,128)(2,1)S(1)}) custom-call(s32[63]{0:T(128)S(1)} %fusion.14.order_ref.plan_ref, bf16[1024,768]{1,0:T(8,128)(2,1)S(1)} %copy-done.5, ...), custom_call_target="tpu_custom_call", output_to_operand_aliasing={{2}: (18, {}), {3}: (19, {})} | custom-call | tf_op jit(solution)/shard_map/expert_grads/pallas_call | solution.py:543
  146.7 8.8 %expert_grads.13 = (bf16[1,1536,384]{2,1,0:T(8,128)(2,1)S(1)}, bf16[1,1536,384]{2,1,0:T(8,128)(2,1)S(1)}, bf16[8,1024,512]{2,1,0:T(8,128)(2,1)}, bf16[8,1024,256]{2,1,0:T(8,128)(2,1)S(1)}) custom-call(s32[63]{0:T(128)S(1)} %fusion.14.order_ref.plan_ref, bf16[1024,768]{1,0:T(8,128)(2,1)S(1)} %copy-done.5, ...), custom_call_target="tpu_custom_call", output_to_operand_aliasing={{2}: (18, {}), {3}: (19, {})} | custom-call | tf_op jit(solution)/shard_map/expert_grads/pallas_call | solution.py:543
  157.0 8.8 %expert_grads.14 = (bf16[1,1536,384]{2,1,0:T(8,128)(2,1)S(1)}, bf16[1,1536,384]{2,1,0:T(8,128)(2,1)S(1)}, bf16[8,1024,512]{2,1,0:T(8,128)(2,1)}, bf16[8,1024,256]{2,1,0:T(8,128)(2,1)S(1)}) custom-call(s32[63]{0:T(128)S(1)} %fusion.14.order_ref.plan_ref, bf16[1024,768]{1,0:T(8,128)(2,1)S(1)} %copy-done.5, ...), custom_call_target="tpu_custom_call", output_to_operand_aliasing={{2}: (18, {}), {3}: (19, {})} | custom-call | tf_op jit(solution)/shard_map/expert_grads/pallas_call | solution.py:543
  167.5 3.5 ring_sum.17
  172.7 8.8 %expert_grads.15 = (bf16[1,1536,384]{2,1,0:T(8,128)(2,1)S(1)}, bf16[1,1536,384]{2,1,0:T(8,128)(2,1)S(1)}, bf16[8,1024,512]{2,1,0:T(8,128)(2,1)}, bf16[8,1024,256]{2,1,0:T(8,128)(2,1)S(1)}) custom-call(s32[63]{0:T(128)S(1)} %fusion.14.order_ref.plan_ref, bf16[1024,768]{1,0:T(8,128)(2,1)S(1)} %copy-done.5, ...), custom_call_target="tpu_custom_call", output_to_operand_aliasing={{2}: (18, {}), {3}: (19, {})} | custom-call | tf_op jit(solution)/shard_map/expert_grads/pallas_call | solution.py:543
  187.2 8.8 %expert_grads.16 = (bf16[1,1536,384]{2,1,0:T(8,128)(2,1)S(1)}, bf16[1,1536,384]{2,1,0:T(8,128)(2,1)S(1)}, bf16[8,1024,512]{2,1,0:T(8,128)(2,1)}, bf16[8,1024,256]{2,1,0:T(8,128)(2,1)S(1)}) custom-call(s32[63]{0:T(128)S(1)} %fusion.14.order_ref.plan_ref, bf16[1024,768]{1,0:T(8,128)(2,1)S(1)} %copy-done.5, ...), custom_call_target="tpu_custom_call", output_to_operand_aliasing={{2}: (18, {}), {3}: (19, {})} | custom-call | tf_op jit(solution)/shard_map/expert_grads/pallas_call | solution.py:543
  201.5 7.7 %expert_grads.17 = (bf16[1,1536,384]{2,1,0:T(8,128)(2,1)S(1)}, bf16[1,1536,384]{2,1,0:T(8,128)(2,1)S(1)}, bf16[1,1024,512]{2,1,0:T(8,128)(2,1)S(1)}, bf16[1,1024,256]{2,1,0:T(8,128)(2,1)S(1)}) custom-call(s32[63]{0:T(128)S(1)} %fusion.14.order_ref.plan_ref, bf16[1024,768]{1,0:T(8,128)(2,1)S(1)} %copy-done.5, bf16[1024,768]{1,0:T(8,128)(2,1)S(1)} %copy-done.7, ...), custom_call_target="tpu_custom_call" | custom-call | tf_op jit(solution)/shard_map/expert_grads/pallas_call | solution.py:543
  210.2 2.6 ring_sum.20
  214.0 16.0 %mix_back.2 = (f32[512,768]{1,0:T(8,128)}, bf16[512,768]{1,0:T(8,128)(2,1)}) custom-call(s32[63]{0:T(128)S(1)} %fusion.14.order_ref.plan_ref, bf16[8,1024,512]{2,1,0:T(8,128)(2,1)} %get-tuple-element.291.refs_0_, bf16[1,1024,512]{2,1,0:T(8,128)(2,1)S(1)} %get-tuple-element.298.refs_1_, bf16[16,768,256]{2,1,0:T(8,128)(2,1)} %refs_14_.3, ...), custom_call_target="tpu_custom_call" | custom-call | tf_op jit(solution)/shard_map/mix_back/pallas_call | solution.py:614
  231.8 15.9 %mix_back.3 = (f32[512,768]{1,0:T(8,128)}, bf16[512,768]{1,0:T(8,128)(2,1)}) custom-call(s32[63]{0:T(128)S(1)} %fusion.14.order_ref.plan_ref, bf16[8,1024,512]{2,1,0:T(8,128)(2,1)} %get-tuple-element.291.refs_0_, bf16[1,1024,512]{2,1,0:T(8,128)(2,1)S(1)} %get-tuple-element.298.refs_1_, bf16[16,768,256]{2,1,0:T(8,128)(2,1)} %refs_14_.3, ...), custom_call_target="tpu_custom_call" | custom-call | tf_op jit(solution)/shard_map/mix_back/pallas_call | solution.py:614
  258.0 7.2 %mix_out.2 = bf16[1024,768]{1,0:T(8,128)(2,1)S(1)} custom-call(s32[63]{0:T(128)S(1)} %fusion.14.order_ref.plan_ref, bf16[8,1024,256]{2,1,0:T(8,128)(2,1)} %copy-done, bf16[1,1024,256]{2,1,0:T(8,128)(2,1)S(1)} %get-tuple-element.311.refs_1_, ...), custom_call_target="tpu_custom_call" | custom-call | tf_op jit(solution)/shard_map/mix_out/pallas_call | solution.py:679
  268.0 7.3 %mix_out.3 = f32[1024,768]{1,0:T(8,128)S(1)} custom-call(s32[63]{0:T(128)S(1)} %fusion.14.order_ref.plan_ref, bf16[8,1024,256]{2,1,0:T(8,128)(2,1)} %copy-done, bf16[1,1024,256]{2,1,0:T(8,128)(2,1)S(1)} %get-tuple-element.311.refs_1_, bf16[16,256,768]{2,1,0:T(8,128)(2,1)} %refs_9_.17, bf16[16,256,768]{2,1,0:T(8,128)(2,1)} %refs_9_.17, ...), custom_call_target="tpu_custom_call" | custom-call | tf_op jit(solution)/shard_map/mix_out/pallas_call | solution.py:679
  275.3 3.9 ring_sum.24
  279.2 12.8 %collective-permute-done.38.refs_3_ = bf16[512,768]{1,0:T(8,128)(2,1)} collective-permute-done((bf16[512,768]{1,0:T(8,128)(2,1)}, bf16[512,768]{1,0:T(8,128)(2,1)}, u32[]{:S(2)}, u32[]{:S(2)}) %collective-permute-start.38) | collective-permute-done | bytes 786464 | tf_op jit(solution)/shard_map/ppermute | solution.py:48
  292.0 6.1 norm_back.1
  300.0 5.4 norm_back_end.1
  308.9 13.1 %attend_back.1.refs_4_ = bf16[1024,640]{1,0:T(8,128)(2,1)} custom-call(s32[3]{0:T(128)} %copy-done.55, bf16[512,640]{1,0:T(8,128)(2,1)} %get-tuple-element.242.own_ref, bf16[512,640]{1,0:T(8,128)(2,1)} %get-tuple-element.246.other_ref, bf16[1024,768]{1,0:T(8,128)(2,1)} %copy-done.16, bf16[1024,768]{1,0:T(8,128)(2,1)} %collective-permute-done.40.grad_c_ref.refs_7_, ...), custom_call_target="tpu_custom_call" | custom-call | tf_op jit(solution)/shard_map/attend_back/pallas_call | solution.py:166
  322.0 11.6 %collective-permute-done.41.came_ref = bf16[1,1536,384]{2,1,0:T(8,128)(2,1)} collective-permute-done((bf16[1,1536,384]{2,1,0:T(8,128)(2,1)}, bf16[1,1536,384]{2,1,0:T(8,128)(2,1)}, u32[]{:S(2)}, u32[]{:S(2)}) %collective-permute-start.41) | collective-permute-done | bytes 1179680 | tf_op jit(solution)/shard_map/ppermute | solution.py:1050
  337.5 13.2 %late_grads.1 = (bf16[2,768,896]{2,1,0:T(8,128)(2,1)}, bf16[2,768,896]{2,1,0:T(8,128)(2,1)}) custom-call(s32[3]{0:T(128)} %copy-done.55, bf16[512,768]{1,0:T(8,128)(2,1)} %get-tuple-element.337.refs_0_, bf16[512,768]{1,0:T(8,128)(2,1)} %get-tuple-element.338.refs_1_, bf16[512,768]{1,0:T(8,128)(2,1)} %get-tuple-element.339.refs_2_, ...), custom_call_target="tpu_custom_call" | custom-call | tf_op jit(solution)/shard_map/late_grads/pallas_call | solution.py:217
  362.2 3.5 collective-permute-done.47.refs_0_
  371.8 3.1 unpack.17
  377.0 5.1 collective-permute-done.50.refs_0_
  382.8 3.3 collective-permute-done.49.refs_1_
  392.9 5.8 collective-permute-done.52.refs_0_
  399.4 3.0 collective-permute-done.51.refs_1_
  402.5 7.2 %collective-permute-done.71.refs_0_ = bf16[2,96,896]{2,1,0:T(8,128)(2,1)S(1)} collective-permute-done((bf16[2,96,896]{2,1,0:T(8,128)(2,1)S(1)}, bf16[2,96,896]{2,1,0:T(8,128)(2,1)S(1)}, u32[]{:S(2)}, u32[]{:S(2)}) %collective-permute-start.71) | collective-permute-done | bytes 344096 | tf_op jit(solution)/shard_map/ppermute | solution.py:1050
  416.6 13.1 %collective-permute-done.72.refs_0_ = bf16[2,96,896]{2,1,0:T(8,128)(2,1)S(1)} collective-permute-done((bf16[2,96,896]{2,1,0:T(8,128)(2,1)S(1)}, bf16[2,96,896]{2,1,0:T(8,128)(2,1)S(1)}, u32[]{:S(2)}, u32[]{:S(2)}) %collective-permute-start.72) | collective-permute-done | bytes 344096 | tf_op jit(solution)/shard_map/ppermute | solution.py:1050
  433.2 6.6 %collective-permute-done.73.refs_0_ = bf16[2,96,896]{2,1,0:T(8,128)(2,1)S(1)} collective-permute-done((bf16[2,96,896]{2,1,0:T(8,128)(2,1)S(1)}, bf16[2,96,896]{2,1,0:T(8,128)(2,1)S(1)}, u32[]{:S(2)}, u32[]{:S(2)}) %collective-permute-start.73) | collective-permute-done | bytes 344096 | tf_op jit(solution)/shard_map/ppermute | solution.py:1050
  446.8 13.0 %collective-permute-done.74.refs_0_ = bf16[2,96,896]{2,1,0:T(8,128)(2,1)S(1)} collective-permute-done((bf16[2,96,896]{2,1,0:T(8,128)(2,1)S(1)}, bf16[2,96,896]{2,1,0:T(8,128)(2,1)S(1)}, u32[]{:S(2)}, u32[]{:S(2)}) %collective-permute-start.74) | collective-permute-done | bytes 344096 | tf_op jit(solution)/shard_map/ppermute | solution.py:1050
  463.6 4.4 collective-permute-done.75.refs_0_
  470.9 3.4 collective-permute-done.65.refs_0_
  475.0 5.8 collective-permute-done.76.refs_0_
  489.2 3.4 collective-permute-done.77.refs_0_
  500.0 5.3 collective-permute-done.83.refs_1_
  511.6 4.4 collective-permute-done.80.refs_1_
  521.4 7.4 %collective-permute-done.85.refs_0_ = bf16[1,768,384]{2,1,0:T(8,128)(2,1)} collective-permute-done((bf16[1,768,384]{2,1,0:T(8,128)(2,1)S(1)}, bf16[1,768,384]{2,1,0:T(8,128)(2,1)}, u32[]{:S(2)}, u32[]{:S(2)}) %collective-permute-start.85) | collective-permute-done | bytes 589856 | tf_op jit(solution)/shard_map/ppermute | solution.py:1050
  543.0 3.3 unpack.26
  550.1 4.4 collective-permute-done.87.refs_3_
  556.6 3.0 convert_add_fusion
  565.6 3.6 unpack.27
  571.0 6.8 %collective-permute-done.90.refs_4_ = bf16[192,896]{1,0:T(8,128)(2,1)S(1)} collective-permute-done((bf16[192,896]{1,0:T(8,128)(2,1)}, bf16[192,896]{1,0:T(8,128)(2,1)S(1)}, u32[]{:S(2)}, u32[]{:S(2)}) %collective-permute-start.90) | collective-permute-done | bytes 344096 | tf_op jit(solution)/shard_map/ppermute | solution.py:1050
  586.4 9.9 %collective-permute-done.107.refs_12_ = bf16[192,896]{1,0:T(8,128)(2,1)S(1)} collective-permute-done((bf16[192,896]{1,0:T(8,128)(2,1)}, bf16[192,896]{1,0:T(8,128)(2,1)S(1)}, u32[]{:S(2)}, u32[]{:S(2)}) %collective-permute-start.107) | collective-permute-done | bytes 344096 | tf_op jit(solution)/shard_map/ppermute | solution.py:1050
  598.6 3.6 unpack.28
  608.9 4.3 collective-permute-done.108.refs_13_
  613.2 12.7 %collective-permute-done.57 = f32[2,768]{1,0:T(2,128)S(1)} collective-permute-done((f32[2,768]{1,0:T(2,128)S(1)}, f32[2,768]{1,0:T(2,128)S(1)}, u32[]{:S(2)}, u32[]{:S(2)}) %collective-permute-start.57) | collective-permute-done | bytes 6176 | tf_op jit(solution)/shard_map/ppermute | solution.py:1388
  631.2 3.9 collective-permute-done.58
  638.3 2.6 fusion.2
  645.4 4.0 collective-permute-done.102.refs_1_
  653.1 6.6 unpack_late.1
  (429 shorter events, 225.6 us)
Async XLA Ops:
  0.6 34.5 %collective-permute-start.16 = (bf16[16,768,256]{2,1,0:T(8,128)(2,1)}, bf16[16,768,256]{2,1,0:T(8,128)(2,1)}, u32[]{:S(2)}, u32[]{:S(2)}) collective-permute-start(bf16[16,768,256]{2,1,0:T(8,128)(2,1)} %refs_14_.3), channel_id=1, source_target_pairs={{0,1},{1,0},{2,3},{3,2},{4,5},{5,4},{6,7},{7,6},{8,9},{9,8},{10,11... | collective-permute-start | bytes 18874376 | tf_op jit(solution)/shard_map/ppermute | solution.py:48
  5.5 27.1 %collective-permute-start = (bf16[512,768]{1,0:T(8,128)(2,1)S(1)}, bf16[512,768]{1,0:T(8,128)(2,1)}, u32[]{:S(2)}, u32[]{:S(2)}) collective-permute-start(bf16[512,768]{1,0:T(8,128)(2,1)S(1)} %copy-done.62), channel_id=1, source_target_pairs={{0,2},{2,0},{1,3},{3,1},{4,6},{6,4},{5,7},{7,5},{8,10},{10,8},{9,1... | collective-permute-start | bytes 2359304 | tf_op jit(solution)/shard_map/ppermute | solution.py:48
  13.2 19.3 %collective-permute-start.4 = (bf16[192,768]{1,0:T(8,128)(2,1)}, bf16[192,768]{1,0:T(8,128)(2,1)S(1)}, u32[]{:S(2)}, u32[]{:S(2)}) collective-permute-start(bf16[192,768]{1,0:T(8,128)(2,1)} %get-tuple-element.243), channel_id=1, source_target_pairs={{0,2},{2,0},{1,3},{3,1},{4,6},{6,4},{5,7},{7,5},{8,10},{10,8},{9,1... | collective-permute-start | bytes 884744 | tf_op jit(solution)/shard_map/ppermute | solution.py:48
  35.0 62.0 %collective-permute-start.18 = (bf16[16,256,768]{2,1,0:T(8,128)(2,1)}, bf16[16,256,768]{2,1,0:T(8,128)(2,1)}, u32[]{:S(2)}, u32[]{:S(2)}) collective-permute-start(bf16[16,256,768]{2,1,0:T(8,128)(2,1)} %refs_9_.17), channel_id=1, source_target_pairs={{0,1},{1,0},{2,3},{3,2},{4,5},{5,4},{6,7},{7,6},{8,9},{9,8},{10,11... | collective-permute-start | bytes 18874376 | tf_op jit(solution)/shard_map/ppermute | solution.py:48
  35.9 61.1 %collective-permute-start.17 = (bf16[16,768,256]{2,1,0:T(8,128)(2,1)}, bf16[16,768,256]{2,1,0:T(8,128)(2,1)}, u32[]{:S(2)}, u32[]{:S(2)}) collective-permute-start(bf16[16,768,256]{2,1,0:T(8,128)(2,1)} %refs_15_.19), channel_id=1, source_target_pairs={{0,1},{1,0},{2,3},{3,2},{4,5},{5,4},{6,7},{7,6},{8,9},{9,8},{10,11... | collective-permute-start | bytes 18874376 | tf_op jit(solution)/shard_map/ppermute | solution.py:48
  36.0 19.8 %collective-permute-start.5 = (bf16[512,768]{1,0:T(8,128)(2,1)S(1)}, bf16[512,768]{1,0:T(8,128)(2,1)S(1)}, u32[]{:S(2)}, u32[]{:S(2)}) collective-permute-start(bf16[512,768]{1,0:T(8,128)(2,1)S(1)} %copy-done.46), channel_id=1, source_target_pairs={{0,2},{2,0},{1,3},{3,1},{4,6},{6,4},{5,7},{7,5},{8,10},{10,8},{9,1... | collective-permute-start | bytes 2359304 | tf_op jit(solution)/shard_map/ppermute | solution.py:48
  50.7 17.7 %collective-permute-start.11 = (bf16[768,768]{1,0:T(8,128)(2,1)}, bf16[768,768]{1,0:T(8,128)(2,1)}, u32[]{:S(2)}, u32[]{:S(2)}) collective-permute-start(bf16[768,768]{1,0:T(8,128)(2,1)} %out_ref.1), channel_id=1, source_target_pairs={{0,1},{1,0},{2,3},{3,2},{4,5},{5,4},{6,7},{7,6},{8,9},{9,8},{10,11... | collective-permute-start | bytes 3538952 | tf_op jit(solution)/shard_map/ppermute | solution.py:48
  63.9 20.3 %collective-permute-start.12 = (bf16[1024,384]{1,0:T(8,128)(2,1)}, bf16[1024,384]{1,0:T(8,128)(2,1)}, u32[]{:S(2)}, u32[]{:S(2)}) collective-permute-start(bf16[1024,384]{1,0:T(8,128)(2,1)} %attend.1.refs_4_.refs_5_), channel_id=1, source_target_pairs={{0,2},{2,0},{1,3},{3,1},{4,6},{6,4},{5,7},{7,5},{8,10},{10,8},{9,1... | collective-permute-start | bytes 2359304 | tf_op jit(solution)/shard_map/ppermute | solution.py:48
  67.2 29.7 %collective-permute-start.15 = (bf16[1024,768]{1,0:T(8,128)(2,1)S(1)}, bf16[1024,768]{1,0:T(8,128)(2,1)S(1)}, u32[]{:S(2)}, u32[]{:S(2)}) collective-permute-start(bf16[1024,768]{1,0:T(8,128)(2,1)S(1)} %join.5.refs_2_.out_grad_ref), channel_id=1, source_target_pairs={{0,1},{1,0},{2,3},{3,2},{4,5},{5,4},{6,7},{7,6},{8,9},{9,8},{10,11... | collective-permute-start | bytes 4718600 | tf_op jit(solution)/shard_map/ppermute | solution.py:48
  109.7 19.7 %collective-permute-start.19 = (bf16[1,1536,384]{2,1,0:T(8,128)(2,1)S(1)}, bf16[1,1536,384]{2,1,0:T(8,128)(2,1)S(1)}, u32[]{:S(2)}, u32[]{:S(2)}) collective-permute-start(bf16[1,1536,384]{2,1,0:T(8,128)(2,1)S(1)} %get-tuple-element.258), channel_id=1, source_target_pairs={{0,8},{8,16},{16,24},{24,28},{28,20},{20,12},{12,4},{4,0},{9,1},{1... | collective-permute-start | bytes 3538952 | tf_op jit(solution)/shard_map/ppermute | solution.py:1050
  120.1 23.3 %collective-permute-start.21 = (bf16[1,1536,384]{2,1,0:T(8,128)(2,1)S(1)}, bf16[1,1536,384]{2,1,0:T(8,128)(2,1)S(1)}, u32[]{:S(2)}, u32[]{:S(2)}) collective-permute-start(bf16[1,1536,384]{2,1,0:T(8,128)(2,1)S(1)} %get-tuple-element.268), channel_id=1, source_target_pairs={{8,0},{16,8},{24,16},{28,24},{20,28},{12,20},{4,12},{0,4},{1,9},{9... | collective-permute-start | bytes 3538952 | tf_op jit(solution)/shard_map/ppermute | solution.py:1050
  129.7 25.8 %collective-permute-start.20 = (bf16[1,1536,384]{2,1,0:T(8,128)(2,1)S(1)}, bf16[1,1536,384]{2,1,0:T(8,128)(2,1)S(1)}, u32[]{:S(2)}, u32[]{:S(2)}) collective-permute-start(bf16[1,1536,384]{2,1,0:T(8,128)(2,1)S(1)} %ring_sum.14), channel_id=1, source_target_pairs={{0,8},{8,16},{16,24},{24,28},{28,20},{20,12},{12,4},{4,0},{9,1},{1... | collective-permute-start | bytes 3538952 | tf_op jit(solution)/shard_map/ppermute | solution.py:1050
  145.0 22.5 %collective-permute-start.23 = (bf16[1,1536,384]{2,1,0:T(8,128)(2,1)}, bf16[1,1536,384]{2,1,0:T(8,128)(2,1)}, u32[]{:S(2)}, u32[]{:S(2)}) collective-permute-start(bf16[1,1536,384]{2,1,0:T(8,128)(2,1)} %ring_sum.15), channel_id=1, source_target_pairs={{8,0},{16,8},{24,16},{28,24},{20,28},{12,20},{4,12},{0,4},{1,9},{9... | collective-permute-start | bytes 3538952 | tf_op jit(solution)/shard_map/ppermute | solution.py:1050
  156.5 25.1 %collective-permute-start.22 = (bf16[1,1536,384]{2,1,0:T(8,128)(2,1)S(1)}, bf16[1,1536,384]{2,1,0:T(8,128)(2,1)S(1)}, u32[]{:S(2)}, u32[]{:S(2)}) collective-permute-start(bf16[1,1536,384]{2,1,0:T(8,128)(2,1)S(1)} %ring_sum.16), channel_id=1, source_target_pairs={{0,8},{8,16},{16,24},{24,28},{28,20},{20,12},{12,4},{4,0},{9,1},{1... | collective-permute-start | bytes 3538952 | tf_op jit(solution)/shard_map/ppermute | solution.py:1050
  171.1 28.0 %collective-permute-start.25 = (bf16[1,1536,384]{2,1,0:T(8,128)(2,1)}, bf16[1,1536,384]{2,1,0:T(8,128)(2,1)S(1)}, u32[]{:S(2)}, u32[]{:S(2)}) collective-permute-start(bf16[1,1536,384]{2,1,0:T(8,128)(2,1)} %ring_sum.17), channel_id=1, source_target_pairs={{8,0},{16,8},{24,16},{28,24},{20,28},{12,20},{4,12},{0,4},{1,9},{9... | collective-permute-start | bytes 3538952 | tf_op jit(solution)/shard_map/ppermute | solution.py:1050
  185.7 24.5 %collective-permute-start.24 = (bf16[1,1536,384]{2,1,0:T(8,128)(2,1)}, bf16[1,1536,384]{2,1,0:T(8,128)(2,1)}, u32[]{:S(2)}, u32[]{:S(2)}) collective-permute-start(bf16[1,1536,384]{2,1,0:T(8,128)(2,1)} %ring_sum.18), channel_id=1, source_target_pairs={{0,8},{8,16},{16,24},{24,28},{28,20},{20,12},{12,4},{4,0},{9,1},{1... | collective-permute-start | bytes 3538952 | tf_op jit(solution)/shard_map/ppermute | solution.py:1050
  200.2 29.8 %collective-permute-start.30 = (bf16[1,1536,384]{2,1,0:T(8,128)(2,1)S(1)}, bf16[1,1536,384]{2,1,0:T(8,128)(2,1)S(1)}, u32[]{:S(2)}, u32[]{:S(2)}) collective-permute-start(bf16[1,1536,384]{2,1,0:T(8,128)(2,1)S(1)} %ring_sum.19), channel_id=1, source_target_pairs={{8,0},{16,8},{24,16},{28,24},{20,28},{12,20},{4,12},{0,4},{1,9},{9... | collective-permute-start | bytes 3538952 | tf_op jit(solution)/shard_map/ppermute | solution.py:1050
  212.9 35.3 %collective-permute-start.29 = (bf16[1,1536,384]{2,1,0:T(8,128)(2,1)S(1)}, bf16[1,1536,384]{2,1,0:T(8,128)(2,1)S(1)}, u32[]{:S(2)}, u32[]{:S(2)}) collective-permute-start(bf16[1,1536,384]{2,1,0:T(8,128)(2,1)S(1)} %ring_sum.20), channel_id=1, source_target_pairs={{0,8},{8,16},{16,24},{24,28},{28,20},{20,12},{12,4},{4,0},{9,1},{1... | collective-permute-start | bytes 3538952 | tf_op jit(solution)/shard_map/ppermute | solution.py:1050
  230.4 34.9 %collective-permute-start.31 = (bf16[1,1536,384]{2,1,0:T(8,128)(2,1)S(1)}, bf16[1,1536,384]{2,1,0:T(8,128)(2,1)S(1)}, u32[]{:S(2)}, u32[]{:S(2)}) collective-permute-start(bf16[1,1536,384]{2,1,0:T(8,128)(2,1)S(1)} %ring_sum.21), channel_id=1, source_target_pairs={{8,0},{16,8},{24,16},{28,24},{20,28},{12,20},{4,12},{0,4},{1,9},{9... | collective-permute-start | bytes 3538952 | tf_op jit(solution)/shard_map/ppermute | solution.py:1050
  231.8 20.3 %collective-permute-start.34 = (bf16[512,768]{1,0:T(8,128)(2,1)}, bf16[512,768]{1,0:T(8,128)(2,1)S(1)}, u32[]{:S(2)}, u32[]{:S(2)}) collective-permute-start(bf16[512,768]{1,0:T(8,128)(2,1)} %get-tuple-element.302), channel_id=1, source_target_pairs={{0,1},{1,0},{2,3},{3,2},{4,5},{5,4},{6,7},{7,6},{8,9},{9,8},{10,11... | collective-permute-start | bytes 2359304 | tf_op jit(solution)/shard_map/ppermute | solution.py:48
  250.9 24.4 %collective-permute-start.37 = (bf16[1,1536,384]{2,1,0:T(8,128)(2,1)S(1)}, bf16[1,1536,384]{2,1,0:T(8,128)(2,1)}, u32[]{:S(2)}, u32[]{:S(2)}) collective-permute-start(bf16[1,1536,384]{2,1,0:T(8,128)(2,1)S(1)} %ring_sum.22), channel_id=1, source_target_pairs={{0,8},{8,16},{16,24},{24,28},{28,20},{20,12},{12,4},{4,0},{9,1},{1... | collective-permute-start | bytes 3538952 | tf_op jit(solution)/shard_map/ppermute | solution.py:1050
  255.0 24.2 %collective-permute-start.36 = (bf16[512,768]{1,0:T(8,128)(2,1)}, bf16[512,768]{1,0:T(8,128)(2,1)}, u32[]{:S(2)}, u32[]{:S(2)}) collective-permute-start(bf16[512,768]{1,0:T(8,128)(2,1)} %get-tuple-element.319), channel_id=1, source_target_pairs={{0,2},{2,0},{1,3},{3,1},{4,6},{6,4},{5,7},{7,5},{8,10},{10,8},{9,1... | collective-permute-start | bytes 2359304 | tf_op jit(solution)/shard_map/ppermute | solution.py:48
  257.0 35.0 %collective-permute-start.38 = (bf16[512,768]{1,0:T(8,128)(2,1)}, bf16[512,768]{1,0:T(8,128)(2,1)}, u32[]{:S(2)}, u32[]{:S(2)}) collective-permute-start(bf16[512,768]{1,0:T(8,128)(2,1)} %get-tuple-element.324), channel_id=1, source_target_pairs={{0,2},{2,0},{1,3},{3,1},{4,6},{6,4},{5,7},{7,5},{8,10},{10,8},{9,1... | collective-permute-start | bytes 2359304 | tf_op jit(solution)/shard_map/ppermute | solution.py:48
  267.0 38.8 %collective-permute-start.43 = (bf16[1,1536,384]{2,1,0:T(8,128)(2,1)}, bf16[1,1536,384]{2,1,0:T(8,128)(2,1)S(1)}, u32[]{:S(2)}, u32[]{:S(2)}) collective-permute-start(bf16[1,1536,384]{2,1,0:T(8,128)(2,1)} %ring_sum.23), channel_id=1, source_target_pairs={{8,0},{16,8},{24,16},{28,24},{20,28},{12,20},{4,12},{0,4},{1,9},{9... | collective-permute-start | bytes 3538952 | tf_op jit(solution)/shard_map/ppermute | solution.py:1050
  305.5 28.1 %collective-permute-start.41 = (bf16[1,1536,384]{2,1,0:T(8,128)(2,1)}, bf16[1,1536,384]{2,1,0:T(8,128)(2,1)}, u32[]{:S(2)}, u32[]{:S(2)}) collective-permute-start(bf16[1,1536,384]{2,1,0:T(8,128)(2,1)} %ring_sum.24), channel_id=1, source_target_pairs={{0,8},{8,16},{16,24},{24,28},{28,20},{20,12},{12,4},{4,0},{9,1},{1... | collective-permute-start | bytes 3538952 | tf_op jit(solution)/shard_map/ppermute | solution.py:1050
  306.5 44.2 %collective-permute-start.44 = (bf16[1,1536,384]{2,1,0:T(8,128)(2,1)S(1)}, bf16[1,1536,384]{2,1,0:T(8,128)(2,1)}, u32[]{:S(2)}, u32[]{:S(2)}) collective-permute-start(bf16[1,1536,384]{2,1,0:T(8,128)(2,1)S(1)} %ring_sum.26), channel_id=1, source_target_pairs={{8,0},{16,8},{24,16},{28,24},{20,28},{12,20},{4,12},{0,4},{1,9},{9... | collective-permute-start | bytes 3538952 | tf_op jit(solution)/shard_map/ppermute | solution.py:1050
  337.3 22.9 %collective-permute-start.42 = (bf16[1,768,384]{2,1,0:T(8,128)(2,1)S(1)}, bf16[1,768,384]{2,1,0:T(8,128)(2,1)}, u32[]{:S(2)}, u32[]{:S(2)}) collective-permute-start(bf16[1,768,384]{2,1,0:T(8,128)(2,1)S(1)} %get-tuple-element.334.refs_0_), channel_id=1, source_target_pairs={{0,8},{8,16},{16,24},{24,28},{28,20},{20,12},{12,4},{4,0},{9,1},{1... | collective-permute-start | bytes 1769480 | tf_op jit(solution)/shard_map/ppermute | solution.py:1050
  368.7 17.4 %collective-permute-start.49 = (bf16[1,768,384]{2,1,0:T(8,128)(2,1)S(1)}, bf16[1,768,384]{2,1,0:T(8,128)(2,1)S(1)}, u32[]{:S(2)}, u32[]{:S(2)}) collective-permute-start(bf16[1,768,384]{2,1,0:T(8,128)(2,1)S(1)} %collective-permute-done.46.refs_1_), channel_id=1, source_target_pairs={{8,0},{16,8},{24,16},{28,24},{20,28},{12,20},{4,12},{0,4},{1,9},{9... | collective-permute-start | bytes 1769480 | tf_op jit(solution)/shard_map/ppermute | solution.py:1050
  388.7 21.0 %collective-permute-start.71 = (bf16[2,96,896]{2,1,0:T(8,128)(2,1)S(1)}, bf16[2,96,896]{2,1,0:T(8,128)(2,1)S(1)}, u32[]{:S(2)}, u32[]{:S(2)}) collective-permute-start(bf16[2,96,896]{2,1,0:T(8,128)(2,1)S(1)} %late_chunk.24), channel_id=1, source_target_pairs={{8,0},{16,8},{24,16},{28,24},{20,28},{12,20},{4,12},{0,4},{1,9},{9... | collective-permute-start | bytes 1032200 | tf_op jit(solution)/shard_map/ppermute | solution.py:1050
  391.3 23.3 %collective-permute-start.61 = (bf16[1,768,384]{2,1,0:T(8,128)(2,1)S(1)}, bf16[1,768,384]{2,1,0:T(8,128)(2,1)S(1)}, u32[]{:S(2)}, u32[]{:S(2)}) collective-permute-start(bf16[1,768,384]{2,1,0:T(8,128)(2,1)S(1)} %collective-permute-done.48.refs_0_), channel_id=1, source_target_pairs={{0,8},{8,16},{16,24},{24,28},{28,20},{20,12},{12,4},{4,0},{9,1},{1... | collective-permute-start | bytes 1769480 | tf_op jit(solution)/shard_map/ppermute | solution.py:1050
  402.3 29.0 %collective-permute-start.64 = (bf16[1,768,384]{2,1,0:T(8,128)(2,1)S(1)}, bf16[1,768,384]{2,1,0:T(8,128)(2,1)S(1)}, u32[]{:S(2)}, u32[]{:S(2)}) collective-permute-start(bf16[1,768,384]{2,1,0:T(8,128)(2,1)S(1)} %collective-permute-done.51.refs_1_), channel_id=1, source_target_pairs={{8,0},{16,8},{24,16},{28,24},{20,28},{12,20},{4,12},{0,4},{1,9},{9... | collective-permute-start | bytes 1769480 | tf_op jit(solution)/shard_map/ppermute | solution.py:1050
  410.4 19.3 %collective-permute-start.72 = (bf16[2,96,896]{2,1,0:T(8,128)(2,1)S(1)}, bf16[2,96,896]{2,1,0:T(8,128)(2,1)S(1)}, u32[]{:S(2)}, u32[]{:S(2)}) collective-permute-start(bf16[2,96,896]{2,1,0:T(8,128)(2,1)S(1)} %late_chunk.25), channel_id=1, source_target_pairs={{8,0},{16,8},{24,16},{28,24},{20,28},{12,20},{4,12},{0,4},{1,9},{9... | collective-permute-start | bytes 1032200 | tf_op jit(solution)/shard_map/ppermute | solution.py:1050
  410.6 20.0 %collective-permute-start.60 = (bf16[2,96,896]{2,1,0:T(8,128)(2,1)S(1)}, bf16[2,96,896]{2,1,0:T(8,128)(2,1)S(1)}, u32[]{:S(2)}, u32[]{:S(2)}) collective-permute-start(bf16[2,96,896]{2,1,0:T(8,128)(2,1)S(1)} %late_chunk.19), channel_id=1, source_target_pairs={{0,8},{8,16},{16,24},{24,28},{28,20},{20,12},{12,4},{4,0},{9,1},{1... | collective-permute-start | bytes 1032200 | tf_op jit(solution)/shard_map/ppermute | solution.py:1050
  414.6 30.2 %collective-permute-start.63 = (bf16[1,768,384]{2,1,0:T(8,128)(2,1)S(1)}, bf16[1,768,384]{2,1,0:T(8,128)(2,1)S(1)}, u32[]{:S(2)}, u32[]{:S(2)}) collective-permute-start(bf16[1,768,384]{2,1,0:T(8,128)(2,1)S(1)} %collective-permute-done.61.refs_0_), channel_id=1, source_target_pairs={{0,8},{8,16},{16,24},{24,28},{28,20},{20,12},{12,4},{4,0},{9,1},{1... | collective-permute-start | bytes 1769480 | tf_op jit(solution)/shard_map/ppermute | solution.py:1050
  431.3 30.0 %collective-permute-start.67 = (bf16[1,768,384]{2,1,0:T(8,128)(2,1)S(1)}, bf16[1,768,384]{2,1,0:T(8,128)(2,1)S(1)}, u32[]{:S(2)}, u32[]{:S(2)}) collective-permute-start(bf16[1,768,384]{2,1,0:T(8,128)(2,1)S(1)} %collective-permute-done.64.refs_1_), channel_id=1, source_target_pairs={{8,0},{16,8},{24,16},{28,24},{20,28},{12,20},{4,12},{0,4},{1,9},{9... | collective-permute-start | bytes 1769480 | tf_op jit(solution)/shard_map/ppermute | solution.py:1050
  440.5 19.3 %collective-permute-start.74 = (bf16[2,96,896]{2,1,0:T(8,128)(2,1)S(1)}, bf16[2,96,896]{2,1,0:T(8,128)(2,1)S(1)}, u32[]{:S(2)}, u32[]{:S(2)}) collective-permute-start(bf16[2,96,896]{2,1,0:T(8,128)(2,1)S(1)} %late_chunk.27), channel_id=1, source_target_pairs={{8,0},{16,8},{24,16},{28,24},{20,28},{12,20},{4,12},{0,4},{1,9},{9... | collective-permute-start | bytes 1032200 | tf_op jit(solution)/shard_map/ppermute | solution.py:1050
  440.6 20.0 %collective-permute-start.62 = (bf16[2,96,896]{2,1,0:T(8,128)(2,1)S(1)}, bf16[2,96,896]{2,1,0:T(8,128)(2,1)S(1)}, u32[]{:S(2)}, u32[]{:S(2)}) collective-permute-start(bf16[2,96,896]{2,1,0:T(8,128)(2,1)S(1)} %late_chunk.20), channel_id=1, source_target_pairs={{0,8},{8,16},{16,24},{24,28},{28,20},{20,12},{12,4},{4,0},{9,1},{1... | collective-permute-start | bytes 1032200 | tf_op jit(solution)/shard_map/ppermute | solution.py:1050
  444.8 23.9 %collective-permute-start.66 = (bf16[1,768,384]{2,1,0:T(8,128)(2,1)S(1)}, bf16[1,768,384]{2,1,0:T(8,128)(2,1)S(1)}, u32[]{:S(2)}, u32[]{:S(2)}) collective-permute-start(bf16[1,768,384]{2,1,0:T(8,128)(2,1)S(1)} %collective-permute-done.63.refs_0_), channel_id=1, source_target_pairs={{0,8},{8,16},{16,24},{24,28},{28,20},{20,12},{12,4},{4,0},{9,1},{1... | collective-permute-start | bytes 1769480 | tf_op jit(solution)/shard_map/ppermute | solution.py:1050
  463.6 20.2 %collective-permute-start.69 = (bf16[1,768,384]{2,1,0:T(8,128)(2,1)S(1)}, bf16[1,768,384]{2,1,0:T(8,128)(2,1)S(1)}, u32[]{:S(2)}, u32[]{:S(2)}) collective-permute-start(bf16[1,768,384]{2,1,0:T(8,128)(2,1)S(1)} %get-tuple-element.383), channel_id=1, source_target_pairs={{0,1},{1,0},{2,3},{3,2},{4,5},{5,4},{6,7},{7,6},{8,9},{9,8},{10,11... | collective-permute-start | bytes 1769480 | tf_op jit(solution)/shard_map/ppermute | solution.py:48
  468.7 19.9 %collective-permute-start.78 = (bf16[1,768,384]{2,1,0:T(8,128)(2,1)S(1)}, bf16[1,768,384]{2,1,0:T(8,128)(2,1)S(1)}, u32[]{:S(2)}, u32[]{:S(2)}) collective-permute-start(bf16[1,768,384]{2,1,0:T(8,128)(2,1)S(1)} %copy-done.58), channel_id=1, source_target_pairs={{0,1},{1,0},{2,3},{3,2},{4,5},{5,4},{6,7},{7,6},{8,9},{9,8},{10,11... | collective-permute-start | bytes 1769480 | tf_op jit(solution)/shard_map/ppermute | solution.py:48
  481.6 17.5 %collective-permute-start.82 = (bf16[1,768,384]{2,1,0:T(8,128)(2,1)S(1)}, bf16[1,768,384]{2,1,0:T(8,128)(2,1)S(1)}, u32[]{:S(2)}, u32[]{:S(2)}) collective-permute-start(bf16[1,768,384]{2,1,0:T(8,128)(2,1)S(1)} %collective-permute-done.66.refs_0_), channel_id=1, source_target_pairs={{0,8},{8,16},{16,24},{24,28},{28,20},{20,12},{12,4},{4,0},{9,1},{1... | collective-permute-start | bytes 1769480 | tf_op jit(solution)/shard_map/ppermute | solution.py:1050
  483.7 21.5 %collective-permute-start.83 = (bf16[1,768,384]{2,1,0:T(8,128)(2,1)S(1)}, bf16[1,768,384]{2,1,0:T(8,128)(2,1)S(1)}, u32[]{:S(2)}, u32[]{:S(2)}) collective-permute-start(bf16[1,768,384]{2,1,0:T(8,128)(2,1)S(1)} %collective-permute-done.70.refs_1_), channel_id=1, source_target_pairs={{8,0},{16,8},{24,16},{28,24},{20,28},{12,20},{4,12},{0,4},{1,9},{9... | collective-permute-start | bytes 1769480 | tf_op jit(solution)/shard_map/ppermute | solution.py:1050
  486.4 25.2 %collective-permute-start.81 = (bf16[1,768,384]{2,1,0:T(8,128)(2,1)S(1)}, bf16[1,768,384]{2,1,0:T(8,128)(2,1)S(1)}, u32[]{:S(2)}, u32[]{:S(2)}) collective-permute-start(bf16[1,768,384]{2,1,0:T(8,128)(2,1)S(1)} %collective-permute-done.69.refs_0_), channel_id=1, source_target_pairs={{0,8},{8,16},{16,24},{24,28},{28,20},{20,12},{12,4},{4,0},{9,1},{1... | collective-permute-start | bytes 1769480 | tf_op jit(solution)/shard_map/ppermute | solution.py:1050
  488.6 29.3 %collective-permute-start.86 = (bf16[1,768,384]{2,1,0:T(8,128)(2,1)S(1)}, bf16[1,768,384]{2,1,0:T(8,128)(2,1)S(1)}, u32[]{:S(2)}, u32[]{:S(2)}) collective-permute-start(bf16[1,768,384]{2,1,0:T(8,128)(2,1)S(1)} %collective-permute-done.78.refs_1_), channel_id=1, source_target_pairs={{8,0},{16,8},{24,16},{28,24},{20,28},{12,20},{4,12},{0,4},{1,9},{9... | collective-permute-start | bytes 1769480 | tf_op jit(solution)/shard_map/ppermute | solution.py:1050
  496.0 60.6 %collective-permute-start.53 = (bf16[1024,768]{1,0:T(8,128)(2,1)}, bf16[1024,768]{1,0:T(8,128)(2,1)}, u32[]{:S(2)}, u32[]{:S(2)}) collective-permute-start(bf16[1024,768]{1,0:T(8,128)(2,1)} %convolution_convert_fusion), channel_id=1, source_target_pairs={{0,1},{1,0},{2,3},{3,2},{4,5},{5,4},{6,7},{7,6},{8,9},{9,8},{10,11... | collective-permute-start | bytes 4718600 | tf_op jit(solution)/shard_map/ppermute | solution.py:48
  499.1 17.0 %collective-permute-start.80 = (bf16[192,896]{1,0:T(8,128)(2,1)S(1)}, bf16[192,896]{1,0:T(8,128)(2,1)S(1)}, u32[]{:S(2)}, u32[]{:S(2)}) collective-permute-start(bf16[192,896]{1,0:T(8,128)(2,1)S(1)} %join.6.refs_0_), channel_id=1, source_target_pairs={{0,8},{8,16},{16,24},{24,28},{28,20},{20,12},{12,4},{4,0},{9,1},{1... | collective-permute-start | bytes 1032200 | tf_op jit(solution)/shard_map/ppermute | solution.py:1050
  511.6 17.1 %collective-permute-start.85 = (bf16[1,768,384]{2,1,0:T(8,128)(2,1)S(1)}, bf16[1,768,384]{2,1,0:T(8,128)(2,1)}, u32[]{:S(2)}, u32[]{:S(2)}) collective-permute-start(bf16[1,768,384]{2,1,0:T(8,128)(2,1)S(1)} %collective-permute-done.81.refs_0_), channel_id=1, source_target_pairs={{0,8},{8,16},{16,24},{24,28},{28,20},{20,12},{12,4},{4,0},{9,1},{1... | collective-permute-start | bytes 1769480 | tf_op jit(solution)/shard_map/ppermute | solution.py:1050
  517.9 17.9 %collective-permute-start.89 = (bf16[1,768,384]{2,1,0:T(8,128)(2,1)S(1)}, bf16[1,768,384]{2,1,0:T(8,128)(2,1)}, u32[]{:S(2)}, u32[]{:S(2)}) collective-permute-start(bf16[1,768,384]{2,1,0:T(8,128)(2,1)S(1)} %collective-permute-done.86.refs_1_), channel_id=1, source_target_pairs={{8,0},{16,8},{24,16},{28,24},{20,28},{12,20},{4,12},{0,4},{1,9},{9... | collective-permute-start | bytes 1769480 | tf_op jit(solution)/shard_map/ppermute | solution.py:1050
  518.3 45.4 %collective-permute-start.32 = (bf16[1024,768]{1,0:T(8,128)(2,1)S(1)}, bf16[1024,768]{1,0:T(8,128)(2,1)}, u32[]{:S(2)}, u32[]{:S(2)}) collective-permute-start(bf16[1024,768]{1,0:T(8,128)(2,1)S(1)} %copy-done.23), channel_id=1, source_target_pairs={{0,1},{1,0},{2,3},{3,2},{4,5},{5,4},{6,7},{7,6},{8,9},{9,8},{10,11... | collective-permute-start | bytes 4718600 | tf_op jit(solution)/shard_map/ppermute | solution.py:48
  535.8 18.7 %collective-permute-start.92 = (bf16[1,768,384]{2,1,0:T(8,128)(2,1)}, bf16[1,768,384]{2,1,0:T(8,128)(2,1)S(1)}, u32[]{:S(2)}, u32[]{:S(2)}) collective-permute-start(bf16[1,768,384]{2,1,0:T(8,128)(2,1)} %collective-permute-done.89.refs_1_), channel_id=1, source_target_pairs={{8,0},{16,8},{24,16},{28,24},{20,28},{12,20},{4,12},{0,4},{1,9},{9... | collective-permute-start | bytes 1769480 | tf_op jit(solution)/shard_map/ppermute | solution.py:1050
  554.5 16.5 %collective-permute-start.91 = (bf16[1,768,384]{2,1,0:T(8,128)(2,1)}, bf16[1,768,384]{2,1,0:T(8,128)(2,1)}, u32[]{:S(2)}, u32[]{:S(2)}) collective-permute-start(bf16[1,768,384]{2,1,0:T(8,128)(2,1)} %collective-permute-done.88.refs_0_), channel_id=1, source_target_pairs={{0,8},{8,16},{16,24},{24,28},{28,20},{20,12},{12,4},{4,0},{9,1},{1... | collective-permute-start | bytes 1769480 | tf_op jit(solution)/shard_map/ppermute | solution.py:1050
  554.5 23.2 %collective-permute-start.95 = (bf16[1,768,384]{2,1,0:T(8,128)(2,1)S(1)}, bf16[1,768,384]{2,1,0:T(8,128)(2,1)}, u32[]{:S(2)}, u32[]{:S(2)}) collective-permute-start(bf16[1,768,384]{2,1,0:T(8,128)(2,1)S(1)} %collective-permute-done.92.refs_1_), channel_id=1, source_target_pairs={{8,0},{16,8},{24,16},{28,24},{20,28},{12,20},{4,12},{0,4},{1,9},{9... | collective-permute-start | bytes 1769480 | tf_op jit(solution)/shard_map/ppermute | solution.py:1050
  560.7 21.4 %collective-permute-start.54 = (bf16[512,768]{1,0:T(8,128)(2,1)}, bf16[512,768]{1,0:T(8,128)(2,1)}, u32[]{:S(2)}, u32[]{:S(2)}) collective-permute-start(bf16[512,768]{1,0:T(8,128)(2,1)} %dynamic-slice_convert_fusion), channel_id=1, source_target_pairs={{0,2},{2,0},{1,3},{3,1},{4,6},{6,4},{5,7},{7,5},{8,10},{10,8},{9,1... | collective-permute-start | bytes 2359304 | tf_op jit(solution)/shard_map/ppermute | solution.py:48
  561.7 20.0 %collective-permute-start.106 = (bf16[192,896]{1,0:T(8,128)(2,1)}, bf16[192,896]{1,0:T(8,128)(2,1)}, u32[]{:S(2)}, u32[]{:S(2)}) collective-permute-start(bf16[192,896]{1,0:T(8,128)(2,1)} %collective-permute-done.105.refs_10_), channel_id=1, source_target_pairs={{8,0},{16,8},{24,16},{28,24},{20,28},{12,20},{4,12},{0,4},{1,9},{9... | collective-permute-start | bytes 1032200 | tf_op jit(solution)/shard_map/ppermute | solution.py:1050
  571.0 31.2 %collective-permute-start.94 = (bf16[1,768,384]{2,1,0:T(8,128)(2,1)}, bf16[1,768,384]{2,1,0:T(8,128)(2,1)S(1)}, u32[]{:S(2)}, u32[]{:S(2)}) collective-permute-start(bf16[1,768,384]{2,1,0:T(8,128)(2,1)} %collective-permute-done.91.refs_0_), channel_id=1, source_target_pairs={{0,8},{8,16},{16,24},{24,28},{28,20},{20,12},{12,4},{4,0},{9,1},{1... | collective-permute-start | bytes 1769480 | tf_op jit(solution)/shard_map/ppermute | solution.py:1050
  577.8 26.5 %collective-permute-start.98 = (bf16[1,768,384]{2,1,0:T(8,128)(2,1)}, bf16[1,768,384]{2,1,0:T(8,128)(2,1)S(1)}, u32[]{:S(2)}, u32[]{:S(2)}) collective-permute-start(bf16[1,768,384]{2,1,0:T(8,128)(2,1)} %collective-permute-done.95.refs_1_), channel_id=1, source_target_pairs={{8,0},{16,8},{24,16},{28,24},{20,28},{12,20},{4,12},{0,4},{1,9},{9... | collective-permute-start | bytes 1769480 | tf_op jit(solution)/shard_map/ppermute | solution.py:1050
  580.5 25.9 %collective-permute-start.33 = (bf16[512,768]{1,0:T(8,128)(2,1)}, bf16[512,768]{1,0:T(8,128)(2,1)}, u32[]{:S(2)}, u32[]{:S(2)}) collective-permute-start(bf16[512,768]{1,0:T(8,128)(2,1)} %dynamic-slice_convert_fusion.1), channel_id=1, source_target_pairs={{0,2},{2,0},{1,3},{3,1},{4,6},{6,4},{5,7},{7,5},{8,10},{10,8},{9,1... | collective-permute-start | bytes 2359304 | tf_op jit(solution)/shard_map/ppermute | solution.py:48
  582.1 20.2 %collective-permute-start.93 = (bf16[192,896]{1,0:T(8,128)(2,1)S(1)}, bf16[192,896]{1,0:T(8,128)(2,1)S(1)}, u32[]{:S(2)}, u32[]{:S(2)}) collective-permute-start(bf16[192,896]{1,0:T(8,128)(2,1)S(1)} %collective-permute-done.90.refs_4_), channel_id=1, source_target_pairs={{0,8},{8,16},{16,24},{24,28},{28,20},{20,12},{12,4},{4,0},{9,1},{1... | collective-permute-start | bytes 1032200 | tf_op jit(solution)/shard_map/ppermute | solution.py:1050
  602.2 25.8 %collective-permute-start.97 = (bf16[1,768,384]{2,1,0:T(8,128)(2,1)S(1)}, bf16[1,768,384]{2,1,0:T(8,128)(2,1)S(1)}, u32[]{:S(2)}, u32[]{:S(2)}) collective-permute-start(bf16[1,768,384]{2,1,0:T(8,128)(2,1)S(1)} %collective-permute-done.94.refs_0_), channel_id=1, source_target_pairs={{0,8},{8,16},{16,24},{24,28},{28,20},{20,12},{12,4},{4,0},{9,1},{1... | collective-permute-start | bytes 1769480 | tf_op jit(solution)/shard_map/ppermute | solution.py:1050
  604.3 26.8 %collective-permute-start.101 = (bf16[1,768,384]{2,1,0:T(8,128)(2,1)S(1)}, bf16[1,768,384]{2,1,0:T(8,128)(2,1)S(1)}, u32[]{:S(2)}, u32[]{:S(2)}) collective-permute-start(bf16[1,768,384]{2,1,0:T(8,128)(2,1)S(1)} %collective-permute-done.98.refs_1_), channel_id=1, source_target_pairs={{8,0},{16,8},{24,16},{28,24},{20,28},{12,20},{4,12},{0,4},{1,9},{9... | collective-permute-start | bytes 1769480 | tf_op jit(solution)/shard_map/ppermute | solution.py:1050
  604.3 21.5 %collective-permute-start.57 = (f32[2,768]{1,0:T(2,128)S(1)}, f32[2,768]{1,0:T(2,128)S(1)}, u32[]{:S(2)}, u32[]{:S(2)}) collective-permute-start(f32[2,768]{1,0:T(2,128)S(1)} %fusion.16), channel_id=1, source_target_pairs={{0,8},{4,12},{8,0},{12,4},{16,24},{20,28},{24,16},{28,20},{1,9},{5... | collective-permute-start | bytes 18440 | tf_op jit(solution)/shard_map/ppermute | solution.py:1388
  606.4 22.7 %collective-permute-start.96 = (bf16[192,896]{1,0:T(8,128)(2,1)S(1)}, bf16[192,896]{1,0:T(8,128)(2,1)S(1)}, u32[]{:S(2)}, u32[]{:S(2)}) collective-permute-start(bf16[192,896]{1,0:T(8,128)(2,1)S(1)} %collective-permute-done.93.refs_5_), channel_id=1, source_target_pairs={{0,8},{8,16},{16,24},{24,28},{28,20},{20,12},{12,4},{4,0},{9,1},{1... | collective-permute-start | bytes 1032200 | tf_op jit(solution)/shard_map/ppermute | solution.py:1050
  613.1 18.0 %collective-permute-start.55 = (f32[512,1]{0,1:T(1,128)S(1)}, f32[512,1]{0,1:T(1,128)S(1)}, u32[]{:S(2)}, u32[]{:S(2)}) collective-permute-start(f32[512,1]{0,1:T(1,128)S(1)} %bitcast.75), channel_id=1, source_target_pairs={{0,1},{1,0},{2,3},{3,2},{4,5},{5,4},{6,7},{7,6},{8,9},{9,8},{10,11... | collective-permute-start | bytes 6152 | tf_op jit(solution)/shard_map/ppermute | solution.py:48
  631.1 18.3 %collective-permute-start.102 = (bf16[1,768,384]{2,1,0:T(8,128)(2,1)S(1)}, bf16[1,768,384]{2,1,0:T(8,128)(2,1)S(1)}, u32[]{:S(2)}, u32[]{:S(2)}) collective-permute-start(bf16[1,768,384]{2,1,0:T(8,128)(2,1)S(1)} %collective-permute-done.101.refs_1_), channel_id=1, source_target_pairs={{8,0},{16,8},{24,16},{28,24},{20,28},{12,20},{4,12},{0,4},{1,9},{9... | collective-permute-start | bytes 1769480 | tf_op jit(solution)/shard_map/ppermute | solution.py:1050
  (130 other events, 1137.6 us)

commit v8 on v7

--- a/solution.py
+++ b/solution.py
@@ -564,110 +564,45 @@
     )(order, *x, *o, gates, *weights, *weights, *kept)
 
 
-def mix_back_kernel(group, order_ref, *refs):
+def mix_kernel(back, group, order_ref, *refs):
     acts_ref, shared_ref = refs[0:2]
-    count = 8 * group
-    weights, shared = refs[2 : 2 + count], refs[2 + count : 10 + count]
-    own_ref, other_ref, total_ref = refs[10 + count :]
-    step = pl.program_id(0)
-
-    def gathered(parts, half):
-        picked = [p[0] for k in range(len(parts) // 4) for p in parts[4 * k + 2 * half :][:2]]
-        return jnp.concatenate(picked, axis=1)
-
-    acts = jnp.concatenate([acts_ref[g] for g in range(group)], axis=1)
-    for half in range(2):
-        term = dot_nt(acts, gathered(weights, half))
-
-        @pl.when(step == 0)
-        def _(half=half, term=term):
-            total_ref[half] = term + dot_nt(shared_ref[0], gathered(shared, half))
-
-        @pl.when(step > 0)
-        def _(half=half, term=term):
-            total_ref[half] += term
-
-    @pl.when(step == pl.num_programs(0) - 1)
-    def _():
-        own_ref[...] = total_ref[0]
-        other_ref[...] = total_ref[1].astype(BF16)
-
-
-def mix_back(part, order, acts, shared_acts, weights, shared_weights):
-    pairs, rows, width = acts.shape
-    rows = rows // 2
-    features = weights[0].shape[1]
-    group = 2 if pairs % 2 == 0 else 1
-
-    def spec(place):
-        return pl.BlockSpec(
-            (1, features, LANES), lambda i, o: (place(i, o)[0], 0, place(i, o)[1])
-        )
-
-    def routed(k):
-        return spec(lambda i, o: (o[2 * group * i + k], o[o.shape[0] - 1]))
-
-    def common(k):
-        return spec(lambda i, o: (0, 2 * o[o.shape[0] - 1] + k))
-
-    whole = pl.BlockSpec((rows, features), lambda i, o: (0, 0))
-    return pl.pallas_call(
-        functools.partial(mix_back_kernel, group),
-        grid_spec=pltpu.PrefetchScalarGridSpec(
-            num_scalar_prefetch=1,
-            grid=(pairs // group,),
-            in_specs=[
-                pl.BlockSpec((group, rows, width), lambda i, o: (i, part, 0)),
-                pl.BlockSpec((1, rows, width), lambda i, o: (0, part, 0)),
-            ]
-            + [routed(k) for k in range(2 * group) for _ in weights]
-            + [common(k) for k in range(2) for _ in weights],
-            out_specs=[whole, whole],
-            scratch_shapes=[pltpu.VMEM((2, rows, features), F32)],
-        ),
-        out_shape=[
-            jax.ShapeDtypeStruct((rows, features), F32),
-            jax.ShapeDtypeStruct((rows, features), BF16),
-        ],
-        compiler_params=params(48, "arbitrary"),
-        cost_estimate=SMALL,
-        name="mix_back",
-    )(order, acts, shared_acts, *weights * (2 * group), *shared_weights * 2)
-
-
-def mix_out_kernel(group, order_ref, *refs):
-    acts_ref, shared_ref = refs[0:2]
-    count = 2 * group
-    weights, shared = refs[2 : 2 + count], refs[2 + count : 4 + count]
-    out_ref, total_ref = refs[4 + count :]
+    each = 2 if back else 1
+    count = 2 * group * each
+    weights = refs[2 : 2 + count]
+    shared = refs[2 + count : 2 + count + 2 * each]
+    out_ref, total_ref = refs[2 + count + 2 * each :]
     step = pl.program_id(0)
     rows = out_ref.shape[0]
     tile = 512
+    times = dot_nt if back else dot
+    along = 1 if back else 0
 
     @pl.when(step == 0)
     def _():
-        both = jnp.concatenate([w[0] for w in shared], axis=0)
+        both = jnp.concatenate([w[0] for w in shared], axis=along)
         for t in range(rows // tile):
             at = slice(t * tile, (t + 1) * tile)
-            total_ref[at, :] = dot(shared_ref[0, at, :], both)
-
-    both = jnp.concatenate([w[0] for w in weights], axis=0)
+            total_ref[at, :] = times(shared_ref[0, at, :], both)
+
+    both = jnp.concatenate([w[0] for w in weights], axis=along)
     for t in range(rows // tile):
         at = slice(t * tile, (t + 1) * tile)
         acts = jnp.concatenate([acts_ref[g, at, :] for g in range(group)], axis=1)
-        total_ref[at, :] += dot(acts, both)
+        total_ref[at, :] += times(acts, both)
 
     @pl.when(step == pl.num_programs(0) - 1)
     def _():
         out_ref[...] = total_ref[...].astype(out_ref.dtype)
 
 
-def mix_out(dtype, order, acts, shared_acts, weights, shared_weights):
+def mix(back, dtype, order, acts, shared_acts, weights, shared_weights):
     pairs, rows, width = acts.shape
-    features = weights.shape[2]
+    features = weights[0].shape[1] if back else weights[0].shape[2]
     group = 4 if pairs % 4 == 0 else 1
 
     def spec(place):
+        if back:
+            return pl.BlockSpec((1, features, LANES), lambda i, o: (place(i, o)[0], 0, place(i, o)[1]))
         return pl.BlockSpec((1, LANES, features), lambda i, o: (*place(i, o), 0))
 
     def routed(k):
@@ -677,7 +612,7 @@
         return spec(lambda i, o: (0, 2 * o[o.shape[0] - 1] + k))
 
     return pl.pallas_call(
-        functools.partial(mix_out_kernel, group),
+        functools.partial(mix_kernel, back, group),
         grid_spec=pltpu.PrefetchScalarGridSpec(
             num_scalar_prefetch=1,
             grid=(pairs // group,),
@@ -685,16 +620,16 @@
                 pl.BlockSpec((group, rows, width), lambda i, o: (i, 0, 0)),
                 pl.BlockSpec((1, rows, width), lambda i, o: (0, 0, 0)),
             ]
-            + [routed(k) for k in range(2 * group)]
-            + [common(k) for k in range(2)],
+            + [routed(k) for k in range(2 * group) for _ in weights]
+            + [common(k) for k in range(2) for _ in weights],
             out_specs=pl.BlockSpec((rows, features), lambda i, o: (0, 0)),
             scratch_shapes=[pltpu.VMEM((rows, features), F32)],
         ),
         out_shape=jax.ShapeDtypeStruct((rows, features), dtype),
         compiler_params=params(48, "arbitrary"),
         cost_estimate=SMALL,
-        name="mix_out",
-    )(order, acts, shared_acts, *[weights] * (2 * group), *[shared_weights] * 2)
+        name="mix",
+    )(order, acts, shared_acts, *weights * (2 * group), *shared_weights * 2)
 
 
 def chip_sum_kernel(own_ref, other_ref, total_ref, rounded_ref):
@@ -722,13 +657,10 @@
 
 
 def norm_back_kernel(tiles, place_ref, *refs):
-    sums, came = refs[0:2], refs[2:4]
-    hidden_ref, scale_ref, gains_ref = refs[4:7]
-    grad_ref, product_ref, gain_ref = refs[7:10]
+    sum_ref, came_ref, hidden_ref, scale_ref, gains_ref, grad_ref, product_ref, gain_ref = refs
     step = pl.program_id(0)
     part = (step >= tiles // 2).astype(jnp.int32)
-    terms = [sums[k][...] + came[k][...].astype(F32) for k in range(2)]
-    grad = jnp.where(part == 0, terms[0], terms[1])
+    grad = sum_ref[...] + came_ref[...].astype(F32)
     hidden = hidden_ref[...]
     grad_ref[...] = grad
     product_ref[...] = jnp.sum(grad * gains_ref[1:2, :] * hidden, axis=1, keepdims=True)
@@ -745,13 +677,12 @@
 def norm_back(place, sums, came, hidden, scale, gains):
     rows, features = hidden.shape
     tiles = rows // TOKEN_TILE
-    halfwise = pl.BlockSpec((TOKEN_TILE, features), lambda i, p: (i % (tiles // 2), 0))
     return pl.pallas_call(
         functools.partial(norm_back_kernel, tiles),
         grid_spec=pltpu.PrefetchScalarGridSpec(
             num_scalar_prefetch=1,
             grid=(tiles,),
-            in_specs=[halfwise] * 4 + [rowwise(features), rowwise(1), whole(2, features)],
+            in_specs=[rowwise(features)] * 3 + [rowwise(1), whole(2, features)],
             out_specs=[rowwise(features), rowwise(1), whole(1, features)],
         ),
         out_shape=[
@@ -762,7 +693,7 @@
         compiler_params=params(48, "arbitrary"),
         cost_estimate=SMALL,
         name="norm_back",
-    )(place, *sums, *came, hidden, scale, gains)
+    )(place, sums, came, hidden, scale, gains)
 
 
 def norm_back_end_kernel(grad_ref, own_ref, other_ref, hidden_ref, scale_ref, gains_ref, out_grad_ref, hidden_grad_ref, rounded_ref):
@@ -996,9 +927,6 @@
     return np.asarray(rows, np.int32)
 
 
-LATE_ROUND = 0
-
-
 def body(
     tokens_in,
     norm_gain_attn,
@@ -1149,9 +1077,10 @@
     sums = [first[0], first[1]]
     runs = {}
     mixed = {}
+    normed = {}
 
     def work_experts(first, last):
-        def work(order):
+        def work(order, ties):
             nonlocal kept
             result = run(first, last, order, tuple(kept))
             kept = result[2:]
@@ -1160,30 +1089,42 @@
 
         return work
 
-    def work_shared(order):
+    def work_shared(order, ties):
         runs["shared"] = expert_grads(
             order, 0, 1, None, [x_own, x_other], [grad_own, grad_other], gates, shared, ()
         )
         return runs["shared"][2]
 
-    def work_back(part):
-        def work(order):
-            mixed[True, part] = mix_back(
-                part, order, kept[0], runs["shared"][2], routed[:4], shared[:4]
+    def work_back(half):
+        def work(order, ties):
+            mixed[True, half] = mix(
+                True,
+                BF16 if half else F32,
+                order,
+                kept[0],
+                runs["shared"][2],
+                routed[2 * half : 2 * half + 2],
+                shared[2 * half : 2 * half + 2],
             )
-            return mixed[True, part][1]
+            if half:
+                normed["other"] = swap(mixed[True, 1], "col")
+                return mixed[True, 1]
+            normed["sum"] = chip_sum(mixed[True, 0], normed["other"])
+            normed["came"] = swap(normed["sum"][1], "row")
+            return normed["sum"][1]
 
         return work
 
     def work_out(half):
-        def work(order):
-            mixed[False, half] = mix_out(
+        def work(order, ties):
+            mixed[False, half] = mix(
+                False,
                 BF16 if half else F32,
                 order,
                 kept[1],
                 runs["shared"][3],
-                routed[4 + half],
-                shared[4 + half],
+                routed[4 + half : 5 + half],
+                shared[4 + half : 5 + half],
             )
             return mixed[False, half]
 
@@ -1197,17 +1138,9 @@
     def their_rows(values):
         return lax.dynamic_slice_in_dim(values, local_rows - start, local_rows, axis=0)
 
-    normed = {}
-
-    def row_sums(part):
-        own, other = mixed[True, part]
-        both = chip_sum(own, swap(other, "col"))
-        return both, swap(both[1], "row")
-
-    def work_hidden(order):
-        both, came = zip(*(normed["sums"][part] for part in range(2)), strict=True)
+    def work_hidden(order, ties):
         grads, products, normed["gain"] = norm_back(
-            where, [b[0] for b in both], [after(c, order) for c in came], hidden, scale_ffn, gains
+            after(where, *ties), normed["sum"][0], normed["came"], hidden, scale_ffn, gains
         )
         products_c = swap(products, "col")
         normed["hidden"], normed["grad"] = norm_back_end(
@@ -1216,15 +1149,15 @@
         normed["grad_c"] = swap(normed["grad"], "col")
         return normed["grad"]
 
-    def work_attend(order):
+    def work_attend(order, ties):
         normed["qkv"] = attend_back(
-            after(where, order), near[2], far[2], normed["grad"], normed["grad_c"], w_out, out_c
+            after(where, *ties), near[2], far[2], normed["grad"], normed["grad_c"], w_out, out_c
         )
         return normed["qkv"]
 
-    def work_late(order):
+    def work_late(order, ties):
         normed["packs"] = late_grads(
-            after(where, order),
+            where,
             near[0:2],
             far[0:2],
             normed["qkv"],
@@ -1235,29 +1168,21 @@
         )
         return normed["packs"][0]
 
-    def with_sums(part):
-        def work(order):
-            result = work_back(part)(order)
-            normed.setdefault("sums", {})[part] = row_sums(part)
-            return result
-
-        return work
-
     tasks = [work_experts(at, at + each) for at in range(each, pairs_total, each)]
-    tasks += [work_shared, with_sums(0), with_sums(1), work_out(1), work_out(0)]
-    ends = [work_hidden, work_attend, work_late]
+    tasks += [work_shared, work_back(1), work_back(0), work_out(1), work_out(0)]
+    ends = [work_hidden, work_attend]
     tasks += [None] * (2 * ring_size - 1 - len(tasks) - len(ends)) + ends
     got = [None, None]
     if ring_size > 1:
         got[0] = send(sums[0], 0)
-        tasks.pop(0)(after(order, *sums))
+        tasks.pop(0)(after(order, *sums), sums)
         got[1] = send(after(sums[1], kept[0]), 1)
     for s in range(1, ring_size):
         for k in range(2):
             last = sums
             task = tasks.pop(0) if tasks else None
             if task:
-                last = [task(after(order, *last))]
+                last = [task(after(order, *last), last)]
             sums[k] = ring_sum(after(got[k], *last), runs[each * s][k], s + 1 == ring_size)
             if s + 1 < ring_size:
                 got[k] = send(sums[k], k)
@@ -1265,7 +1190,7 @@
                 sums[k], got[k] = sums[k]
     for task in tasks:
         if task:
-            task(after(order, *sums))
+            task(after(order, *sums), sums)
     if ring_size == 1:
         got = [total[:, local_features:] for total in sums]
         sums = [total[:, :local_features] for total in sums]
@@ -1275,6 +1200,7 @@
 
     hidden_grad, attn_grad, attn_grad_c = normed["hidden"], normed["grad"], normed["grad_c"]
     gain_ffn_part, qkv_grad = normed["gain"], normed["qkv"]
+    work_late(order, ())
     packs = normed["packs"]
 
     packs = [
@@ -1311,13 +1237,15 @@
 
     if late_total == 0:
         late_turn()
-    rounds = [(wave, step) for wave in range(2) for step in range(ring_size - 1)]
+    steps = ring_size - 1
     late_got = None
     last = []
-    for number, (wave, step) in enumerate(rounds):
-        if step == 0:
-            came = list(got) if number else None
-            got = list(waves[wave])
+    got = list(waves[0])
+    for number in range(2 * steps - 1):
+        wave, step = (0, number) if number < steps else (1, number - steps + 1)
+        if number == steps:
+            came = got
+            got = early
         late_done += late_got is not None
         chunks = [None, None]
         for k in range(2):
@@ -1327,19 +1255,22 @@
             if late_got is not None:
                 late_finish(k, after(late_got[k], *last))
                 last = list(late[k]) if late_done == ring_size - 1 else [late[k]]
+        if number == 0:
+            early = [send(after(waves[1][k], *chunks), k) for k in range(2)]
         if late_got is not None and late_done == ring_size - 1:
             late_turn()
         late_got = None
-        if number >= LATE_ROUND and late_done < late_total:
+        if late_done < late_total:
             late_got = [send(late[k], k) for k in range(2)]
-        if step == 0 and number:
-            placed = place_chunks(0, ring_size - 1, came, placed)
-        placed = place_chunks(wave, step, chunks, placed)
+        if number == steps:
+            placed = place_chunks(0, steps, came, placed)
+            placed = place_chunks(1, 0, waves[1], placed)
+        placed = place_chunks(wave, step, [after(chunks[0], *last), chunks[1]], placed)
         last = placed[0:1]
-        if number == LATE_ROUND + 3:
+        if number == 3:
             qkv_grad = after(qkv_grad, *last)
-    if rounds:
-        placed = place_chunks(1, ring_size - 1, [after(got[k], *last) for k in range(2)], placed)
+    if steps:
+        placed = place_chunks(1, steps, [after(got[k], *last) for k in range(2)], placed)
         last = placed[0:1]
     while late_got is not None:
         late_done += 1
@@ -1348,7 +1279,7 @@
         if late_done == ring_size - 1:
             late_turn()
         late_got = [send(late[k], k) for k in range(2)] if late_done < late_total else None
-    if not rounds:
+    if not steps:
         for wave in range(2):
             placed = place_chunks(wave, 0, waves[wave], placed)
     gate_grad, up_grad, down_grad = placed

time: 670 us -> 692 us (1.033)
  waiting for transfers between devices: 228 us -> 253 us
    ppermute x70, waiting for transfers between devices: 161 us -> 188 us  [send(): return lax.ppermute(values, ('dp', 'col'), routes_of[which])]
    ppermute x35 -> x33, waiting for transfers between devices: 48.2 us -> 35 us  [swap(): return lax.ppermute(values, axis, [(0, 1), (1, 0)])]
    ppermute x3, waiting for transfers between devices: 16.5 us -> 27.8 us  [body(): gain_parts = gain_parts + lax.ppermute(gain_parts, 'dp', pairs)]
    unnamed x166 -> x176, local copies, waits for them, and re-layouts: 25.2 us -> 28.3 us
    ppermute x35 -> x33, starting transfers between devices: 18.4 us -> 16.5 us  [swap(): return lax.ppermute(values, axis, [(0, 1), (1, 0)])]
  transfers between devices with their start and end apart: 111 -> 109, of which waited for: 51 -> 42; matrix products, arithmetic and copies ran while one was open for 3% -> 3% of each run, Pallas kernels for 40% -> 37%
where the time goes in v8:
time: 692 us; the launch traced here: 682 us
  Pallas kernels  275 us (40%)
  waiting for transfers between devices  253 us (37%)
  starting transfers between devices  101 us (15%)
  local copies, waits for them, and re-layouts  31.6 us (5%)
  other arithmetic  12.5 us (2%)
    ppermute x70, waiting for transfers between devices, send(): return lax.ppermute(values, ('dp', 'col'), routes_of[which])  188 us
    pallas_call x9, Pallas kernels, expert_grads(): pl.pallas_call(functools.partial(expert_kernel, shared, aliased, first),...  78.8 us
    ppermute x70, starting transfers between devices, send(): return lax.ppermute(values, ('dp', 'col'), routes_of[which])  75.7 us
    pallas_call x16, Pallas kernels, unpack(): pl.pallas_call(functools.partial(unpack_kernel, aliased), grid_spec=pltpu...  40 us
    pallas_call x4, Pallas kernels, mix(): pl.pallas_call(functools.partial(mix_kernel, back, group), grid_spec=pltp...  39.4 us
    ppermute x33, waiting for transfers between devices, swap(): return lax.ppermute(values, axis, [(0, 1), (1, 0)])  35 us
    unnamed x176, local copies, waits for them, and re-layouts  28.3 us
    ppermute x3, waiting for transfers between devices, body(): gain_parts = gain_parts + lax.ppermute(gain_parts, 'dp', pairs)  27.8 us
  transfers between devices with their start and end apart: 109, of which 42 were waited for; matrix products, arithmetic and copies ran while one was open for 3% of the time, Pallas kernels for 37%

profile of v8, /device:TPU:0, one launch (start us, length us, event | category | flops | bytes accessed | tf_op | source)
XLA Modules:
  0.0 681.7 jit_solution(14721402856796108416)
XLA Ops:
  1.8 3.2 their_columns.1
  5.5 2.6 collective-permute-start
  8.3 4.9 collective-permute-done.2.gains_c_ref.refs_7_
  13.2 2.9 collective-permute-start.4
  17.9 4.5 project.2
  22.4 10.1 %collective-permute-done.4.refs_0_ = bf16[192,768]{1,0:T(8,128)(2,1)S(1)} collective-permute-done((bf16[192,768]{1,0:T(8,128)(2,1)}, bf16[192,768]{1,0:T(8,128)(2,1)S(1)}, u32[]{:S(2)}, u32[]{:S(2)}) %collective-permute-start.4) | collective-permute-done | bytes 294944 | tf_op jit(solution)/shard_map/ppermute | solution.py:48
  40.8 4.5 project.3
  47.5 2.5 collective-permute-start.9
  50.8 5.0 collective-permute-done.5.refs_1_
  57.6 6.2 attend.1.refs_4_.refs_5_
  69.6 9.0 %hidden_before.1 = (f32[1024,768]{1,0:T(8,128)}, f32[1024,768]{1,0:T(8,128)}) custom-call(s32[3]{0:T(128)} %copy-done.58, bf16[512,768]{1,0:T(8,128)(2,1)} %refs_0_.2, bf16[512,768]{1,0:T(8,128)(2,1)} %copy-done.77, bf16[512,768]{1,0:T(8,128)(2,1)} %collective-permute-done.own_ref.refs_2_, bf16[512,768]{1,0:T(8,128)(2,1)} %copy-done.78, ...), custom_call_target="tpu_custom_call" | custom-call | flops 2415919104 | bytes 12582912 | tf_op jit(solution)/shard_map/hidden_before/pallas_call | solution.py:398
  78.6 5.6 collective-permute-done.12.refs_2_
  87.5 9.4 %hidden_after.1 = (f32[1024,768]{1,0:T(8,128)}, bf16[1024,768]{1,0:T(8,128)(2,1)}, bf16[1024,768]{1,0:T(8,128)(2,1)}, f32[1024,1]{1,0:T(8,128)}) custom-call(s32[3]{0:T(128)} %copy-done.58, f32[1024,768]{1,0:T(8,128)} %get-tuple-element.256.refs_0_, f32[1024,768]{1,0:T(8,128)} %get-tuple-element.257.refs_1_, ...), custom_call_target="tpu_custom_call" | custom-call | tf_op jit(solution)/shard_map/hidden_after/pallas_call | solution.py:420
  100.4 9.3 %expert_grads.9 = (bf16[1,1536,384]{2,1,0:T(8,128)(2,1)S(1)}, bf16[1,1536,384]{2,1,0:T(8,128)(2,1)S(1)}, bf16[8,1024,512]{2,1,0:T(8,128)(2,1)}, bf16[8,1024,256]{2,1,0:T(8,128)(2,1)S(1)}) custom-call(s32[63]{0:T(128)S(1)} %fusion.14.order_ref.plan_ref, bf16[1024,768]{1,0:T(8,128)(2,1)S(1)} %copy-done.5, bf16[1024,768]{1,0:T(8,128)(2,1)S(1)} %copy-done.6, ...), custom_call_target="tpu_custom_call" | custom-call | tf_op jit(solution)/shard_map/expert_grads/pallas_call | solution.py:543
  111.2 8.8 %expert_grads.10 = (bf16[1,1536,384]{2,1,0:T(8,128)(2,1)S(1)}, bf16[1,1536,384]{2,1,0:T(8,128)(2,1)S(1)}, bf16[8,1024,512]{2,1,0:T(8,128)(2,1)}, bf16[8,1024,256]{2,1,0:T(8,128)(2,1)S(1)}) custom-call(s32[63]{0:T(128)S(1)} %fusion.14.order_ref.plan_ref, bf16[1024,768]{1,0:T(8,128)(2,1)S(1)} %copy-done.5, ...), custom_call_target="tpu_custom_call", output_to_operand_aliasing={{2}: (18, {}), {3}: (19, {})} | custom-call | tf_op jit(solution)/shard_map/expert_grads/pallas_call | solution.py:543
  120.5 8.8 %expert_grads.11 = (bf16[1,1536,384]{2,1,0:T(8,128)(2,1)S(1)}, bf16[1,1536,384]{2,1,0:T(8,128)(2,1)S(1)}, bf16[8,1024,512]{2,1,0:T(8,128)(2,1)}, bf16[8,1024,256]{2,1,0:T(8,128)(2,1)S(1)}) custom-call(s32[63]{0:T(128)S(1)} %fusion.14.order_ref.plan_ref, bf16[1024,768]{1,0:T(8,128)(2,1)S(1)} %copy-done.5, ...), custom_call_target="tpu_custom_call", output_to_operand_aliasing={{2}: (18, {}), {3}: (19, {})} | custom-call | tf_op jit(solution)/shard_map/expert_grads/pallas_call | solution.py:543
  129.7 2.5 collective-permute-start.20
  132.2 8.8 %expert_grads.12 = (bf16[1,1536,384]{2,1,0:T(8,128)(2,1)S(1)}, bf16[1,1536,384]{2,1,0:T(8,128)(2,1)S(1)}, bf16[8,1024,512]{2,1,0:T(8,128)(2,1)}, bf16[8,1024,256]{2,1,0:T(8,128)(2,1)S(1)}) custom-call(s32[63]{0:T(128)S(1)} %fusion.14.order_ref.plan_ref, bf16[1024,768]{1,0:T(8,128)(2,1)S(1)} %copy-done.5, ...), custom_call_target="tpu_custom_call", output_to_operand_aliasing={{2}: (18, {}), {3}: (19, {})} | custom-call | tf_op jit(solution)/shard_map/expert_grads/pallas_call | solution.py:543
  145.4 8.8 %expert_grads.13 = (bf16[1,1536,384]{2,1,0:T(8,128)(2,1)S(1)}, bf16[1,1536,384]{2,1,0:T(8,128)(2,1)S(1)}, bf16[8,1024,512]{2,1,0:T(8,128)(2,1)}, bf16[8,1024,256]{2,1,0:T(8,128)(2,1)S(1)}) custom-call(s32[63]{0:T(128)S(1)} %fusion.14.order_ref.plan_ref, bf16[1024,768]{1,0:T(8,128)(2,1)S(1)} %copy-done.5, ...), custom_call_target="tpu_custom_call", output_to_operand_aliasing={{2}: (18, {}), {3}: (19, {})} | custom-call | tf_op jit(solution)/shard_map/expert_grads/pallas_call | solution.py:543
  155.7 2.5 collective-permute-start.22
  158.2 8.8 %expert_grads.14 = (bf16[1,1536,384]{2,1,0:T(8,128)(2,1)S(1)}, bf16[1,1536,384]{2,1,0:T(8,128)(2,1)S(1)}, bf16[8,1024,512]{2,1,0:T(8,128)(2,1)}, bf16[8,1024,256]{2,1,0:T(8,128)(2,1)S(1)}) custom-call(s32[63]{0:T(128)S(1)} %fusion.14.order_ref.plan_ref, bf16[1024,768]{1,0:T(8,128)(2,1)S(1)} %copy-done.5, ...), custom_call_target="tpu_custom_call", output_to_operand_aliasing={{2}: (18, {}), {3}: (19, {})} | custom-call | tf_op jit(solution)/shard_map/expert_grads/pallas_call | solution.py:543
  172.0 8.8 %expert_grads.15 = (bf16[1,1536,384]{2,1,0:T(8,128)(2,1)S(1)}, bf16[1,1536,384]{2,1,0:T(8,128)(2,1)S(1)}, bf16[8,1024,512]{2,1,0:T(8,128)(2,1)}, bf16[8,1024,256]{2,1,0:T(8,128)(2,1)S(1)}) custom-call(s32[63]{0:T(128)S(1)} %fusion.14.order_ref.plan_ref, bf16[1024,768]{1,0:T(8,128)(2,1)S(1)} %copy-done.5, ...), custom_call_target="tpu_custom_call", output_to_operand_aliasing={{2}: (18, {}), {3}: (19, {})} | custom-call | tf_op jit(solution)/shard_map/expert_grads/pallas_call | solution.py:543
  187.2 8.8 %expert_grads.16 = (bf16[1,1536,384]{2,1,0:T(8,128)(2,1)S(1)}, bf16[1,1536,384]{2,1,0:T(8,128)(2,1)S(1)}, bf16[8,1024,512]{2,1,0:T(8,128)(2,1)}, bf16[8,1024,256]{2,1,0:T(8,128)(2,1)S(1)}) custom-call(s32[63]{0:T(128)S(1)} %fusion.14.order_ref.plan_ref, bf16[1024,768]{1,0:T(8,128)(2,1)S(1)} %copy-done.5, ...), custom_call_target="tpu_custom_call", output_to_operand_aliasing={{2}: (18, {}), {3}: (19, {})} | custom-call | tf_op jit(solution)/shard_map/expert_grads/pallas_call | solution.py:543
  203.8 7.7 %expert_grads.17 = (bf16[1,1536,384]{2,1,0:T(8,128)(2,1)S(1)}, bf16[1,1536,384]{2,1,0:T(8,128)(2,1)S(1)}, bf16[1,1024,512]{2,1,0:T(8,128)(2,1)S(1)}, bf16[1,1024,256]{2,1,0:T(8,128)(2,1)S(1)}) custom-call(s32[63]{0:T(128)S(1)} %fusion.14.order_ref.plan_ref, bf16[1024,768]{1,0:T(8,128)(2,1)S(1)} %copy-done.5, bf16[1024,768]{1,0:T(8,128)(2,1)S(1)} %copy-done.7, ...), custom_call_target="tpu_custom_call" | custom-call | tf_op jit(solution)/shard_map/expert_grads/pallas_call | solution.py:543
  213.5 3.7 ring_sum.20
  217.1 12.4 %mix.4 = bf16[1024,768]{1,0:T(8,128)(2,1)S(1)} custom-call(s32[63]{0:T(128)S(1)} %fusion.14.order_ref.plan_ref, bf16[8,1024,512]{2,1,0:T(8,128)(2,1)} %get-tuple-element.297.refs_0_, bf16[1,1024,512]{2,1,0:T(8,128)(2,1)S(1)} %get-tuple-element.304.refs_1_, ...), custom_call_target="tpu_custom_call" | custom-call | tf_op jit(solution)/shard_map/mix/pallas_call | solution.py:614
  234.5 12.5 %mix.5.own_ref = f32[1024,768]{1,0:T(8,128)S(1)} custom-call(s32[63]{0:T(128)S(1)} %fusion.14.order_ref.plan_ref, bf16[8,1024,512]{2,1,0:T(8,128)(2,1)} %get-tuple-element.297.refs_0_, bf16[1,1024,512]{2,1,0:T(8,128)(2,1)S(1)} %get-tuple-element.304.refs_1_, bf16[16,768,256]{2,1,0:T(8,128)(2,1)} %refs_16_.1, bf16[16,768,256]{2,1,0:T(8,128)(2,1)} %refs_17_.1, ...), custom_call_target="tpu_custom_call" | custom-call | tf_op jit(solution)/shard_map/mix/pallas_call | solution.py:614
  251.6 6.1 collective-permute-done.29.came_ref
  262.1 7.2 %mix.6 = bf16[1024,768]{1,0:T(8,128)(2,1)S(1)} custom-call(s32[63]{0:T(128)S(1)} %fusion.14.order_ref.plan_ref, bf16[8,1024,256]{2,1,0:T(8,128)(2,1)} %copy-done, bf16[1,1024,256]{2,1,0:T(8,128)(2,1)S(1)} %get-tuple-element.316.refs_1_, ...), custom_call_target="tpu_custom_call" | custom-call | tf_op jit(solution)/shard_map/mix/pallas_call | solution.py:614
  269.4 3.7 ring_sum.23
  273.1 7.3 %mix.7 = f32[1024,768]{1,0:T(8,128)S(1)} custom-call(s32[63]{0:T(128)S(1)} %fusion.14.order_ref.plan_ref, bf16[8,1024,256]{2,1,0:T(8,128)(2,1)} %copy-done, bf16[1,1024,256]{2,1,0:T(8,128)(2,1)S(1)} %get-tuple-element.316.refs_1_, bf16[16,256,768]{2,1,0:T(8,128)(2,1)} %refs_9_.19, bf16[16,256,768]{2,1,0:T(8,128)(2,1)} %refs_9_.19, ...), custom_call_target="tpu_custom_call" | custom-call | tf_op jit(solution)/shard_map/mix/pallas_call | solution.py:614
  284.3 5.2 collective-permute-done.36.came_ref
  291.3 4.5 norm_back.1
  299.4 5.4 norm_back_end.1
  307.0 26.4 %collective-permute-done.39.came_ref = bf16[1,1536,384]{2,1,0:T(8,128)(2,1)S(1)} collective-permute-done((bf16[1,1536,384]{2,1,0:T(8,128)(2,1)S(1)}, bf16[1,1536,384]{2,1,0:T(8,128)(2,1)S(1)}, u32[]{:S(2)}, u32[]{:S(2)}) %collective-permute-start.39) | collective-permute-done | bytes 1179680 | tf_op jit(solution)/shard_map/ppermute | solution.py:978
  336.3 13.1 %attend_back.1.refs_4_ = bf16[1024,640]{1,0:T(8,128)(2,1)} custom-call(s32[3]{0:T(128)} %copy-done.58, bf16[512,640]{1,0:T(8,128)(2,1)} %get-tuple-element.248.own_ref, bf16[512,640]{1,0:T(8,128)(2,1)} %get-tuple-element.252.other_ref, bf16[1024,768]{1,0:T(8,128)(2,1)} %copy-done.17, bf16[1024,768]{1,0:T(8,128)(2,1)} %collective-permute-done.40.grad_c_ref.refs_7_, ...), custom_call_target="tpu_custom_call" | custom-call | tf_op jit(solution)/shard_map/attend_back/pallas_call | solution.py:166
  353.3 13.2 %late_grads.1 = (bf16[2,768,896]{2,1,0:T(8,128)(2,1)}, bf16[2,768,896]{2,1,0:T(8,128)(2,1)}) custom-call(s32[3]{0:T(128)} %copy-done.58, bf16[512,768]{1,0:T(8,128)(2,1)} %get-tuple-element.343.refs_0_, bf16[512,768]{1,0:T(8,128)(2,1)} %get-tuple-element.344.refs_1_, bf16[512,768]{1,0:T(8,128)(2,1)} %get-tuple-element.345.refs_2_, ...), custom_call_target="tpu_custom_call" | custom-call | tf_op jit(solution)/shard_map/late_grads/pallas_call | solution.py:217
  373.4 2.8 collective-permute-done.46.refs_0_
  379.9 12.6 %collective-permute-done.44.refs_0_ = bf16[2,96,896]{2,1,0:T(8,128)(2,1)S(1)} collective-permute-done((bf16[2,96,896]{2,1,0:T(8,128)(2,1)S(1)}, bf16[2,96,896]{2,1,0:T(8,128)(2,1)S(1)}, u32[]{:S(2)}, u32[]{:S(2)}) %collective-permute-start.44) | collective-permute-done | bytes 344096 | tf_op jit(solution)/shard_map/ppermute | solution.py:978
  393.2 3.2 unpack.17
  401.2 20.1 %collective-permute-done.48.refs_0_ = bf16[2,96,896]{2,1,0:T(8,128)(2,1)S(1)} collective-permute-done((bf16[2,96,896]{2,1,0:T(8,128)(2,1)S(1)}, bf16[2,96,896]{2,1,0:T(8,128)(2,1)S(1)}, u32[]{:S(2)}, u32[]{:S(2)}) %collective-permute-start.48) | collective-permute-done | bytes 344096 | tf_op jit(solution)/shard_map/ppermute | solution.py:978
  428.9 16.6 %collective-permute-done.51.refs_0_ = bf16[2,96,896]{2,1,0:T(8,128)(2,1)S(1)} collective-permute-done((bf16[2,96,896]{2,1,0:T(8,128)(2,1)S(1)}, bf16[2,96,896]{2,1,0:T(8,128)(2,1)S(1)}, u32[]{:S(2)}, u32[]{:S(2)}) %collective-permute-start.51) | collective-permute-done | bytes 344096 | tf_op jit(solution)/shard_map/ppermute | solution.py:978
  453.2 7.4 %collective-permute-done.65.refs_0_ = bf16[2,96,896]{2,1,0:T(8,128)(2,1)S(1)} collective-permute-done((bf16[2,96,896]{2,1,0:T(8,128)(2,1)S(1)}, bf16[2,96,896]{2,1,0:T(8,128)(2,1)S(1)}, u32[]{:S(2)}, u32[]{:S(2)}) %collective-permute-start.65) | collective-permute-done | bytes 344096 | tf_op jit(solution)/shard_map/ppermute | solution.py:978
  465.7 5.6 collective-permute-done.63.refs_0_
  475.2 7.1 %collective-permute-done.69.refs_0_ = bf16[2,96,896]{2,1,0:T(8,128)(2,1)S(1)} collective-permute-done((bf16[2,96,896]{2,1,0:T(8,128)(2,1)S(1)}, bf16[2,96,896]{2,1,0:T(8,128)(2,1)S(1)}, u32[]{:S(2)}, u32[]{:S(2)}) %collective-permute-start.69) | collective-permute-done | bytes 344096 | tf_op jit(solution)/shard_map/ppermute | solution.py:978
  487.3 16.3 %collective-permute-done.67.refs_0_ = bf16[2,96,896]{2,1,0:T(8,128)(2,1)S(1)} collective-permute-done((bf16[2,96,896]{2,1,0:T(8,128)(2,1)S(1)}, bf16[2,96,896]{2,1,0:T(8,128)(2,1)S(1)}, u32[]{:S(2)}, u32[]{:S(2)}) %collective-permute-start.67) | collective-permute-done | bytes 344096 | tf_op jit(solution)/shard_map/ppermute | solution.py:978
  512.7 2.6 convolution_convert_fusion
  515.3 6.7 collective-permute-done.71.refs_0_
  530.0 7.3 %collective-permute-done.83.refs_1_ = bf16[1,768,384]{2,1,0:T(8,128)(2,1)S(1)} collective-permute-done((bf16[1,768,384]{2,1,0:T(8,128)(2,1)S(1)}, bf16[1,768,384]{2,1,0:T(8,128)(2,1)S(1)}, u32[]{:S(2)}, u32[]{:S(2)}) %collective-permute-start.83) | collective-permute-done | bytes 589856 | tf_op jit(solution)/shard_map/ppermute | solution.py:978
  550.8 3.3 unpack.26
  554.1 7.1 %collective-permute-done.85.refs_0_ = bf16[1,768,384]{2,1,0:T(8,128)(2,1)} collective-permute-done((bf16[1,768,384]{2,1,0:T(8,128)(2,1)}, bf16[1,768,384]{2,1,0:T(8,128)(2,1)}, u32[]{:S(2)}, u32[]{:S(2)}) %collective-permute-start.85) | collective-permute-done | bytes 589856 | tf_op jit(solution)/shard_map/ppermute | solution.py:978
  561.8 3.4 collective-permute-done.84.refs_2_
  568.5 3.5 convert_add_fusion
  573.1 10.9 %collective-permute-done.91.refs_10_ = bf16[192,896]{1,0:T(8,128)(2,1)S(1)} collective-permute-done((bf16[192,896]{1,0:T(8,128)(2,1)}, bf16[192,896]{1,0:T(8,128)(2,1)S(1)}, u32[]{:S(2)}, u32[]{:S(2)}) %collective-permute-start.91) | collective-permute-done | bytes 344096 | tf_op jit(solution)/shard_map/ppermute | solution.py:978
  585.3 3.6 unpack.27
  595.8 4.1 collective-permute-done.95.refs_11_
  601.6 3.5 unpack.28
  608.1 5.7 collective-permute-done.93.refs_4_
  619.8 13.2 %collective-permute-done.57 = f32[2,768]{1,0:T(2,128)S(1)} collective-permute-done((f32[2,768]{1,0:T(2,128)S(1)}, f32[2,768]{1,0:T(2,128)S(1)}, u32[]{:S(2)}, u32[]{:S(2)}) %collective-permute-start.57) | collective-permute-done | bytes 6176 | tf_op jit(solution)/shard_map/ppermute | solution.py:1319
  633.2 3.5 unpack.29
  645.8 14.6 %collective-permute-done.59 = f32[2,768]{1,0:T(2,128)S(1)} collective-permute-done((f32[2,768]{1,0:T(2,128)S(1)}, f32[2,768]{1,0:T(2,128)S(1)}, u32[]{:S(2)}, u32[]{:S(2)}) %collective-permute-start.59) | collective-permute-done | bytes 6176 | tf_op jit(solution)/shard_map/ppermute | solution.py:1319
  667.5 2.6 fusion.2
  670.7 4.1 collective-permute-done.106.refs_7_
  674.8 6.5 unpack_late.1
  (434 shorter events, 206.2 us)
Async XLA Ops:
  0.6 34.5 %collective-permute-start.16 = (bf16[16,768,256]{2,1,0:T(8,128)(2,1)}, bf16[16,768,256]{2,1,0:T(8,128)(2,1)}, u32[]{:S(2)}, u32[]{:S(2)}) collective-permute-start(bf16[16,768,256]{2,1,0:T(8,128)(2,1)} %refs_16_.1), channel_id=1, source_target_pairs={{0,1},{1,0},{2,3},{3,2},{4,5},{5,4},{6,7},{7,6},{8,9},{9,8},{10,11... | collective-permute-start | bytes 18874376 | tf_op jit(solution)/shard_map/ppermute | solution.py:48
  5.5 27.1 %collective-permute-start = (bf16[512,768]{1,0:T(8,128)(2,1)S(1)}, bf16[512,768]{1,0:T(8,128)(2,1)}, u32[]{:S(2)}, u32[]{:S(2)}) collective-permute-start(bf16[512,768]{1,0:T(8,128)(2,1)S(1)} %copy-done.67), channel_id=1, source_target_pairs={{0,2},{2,0},{1,3},{3,1},{4,6},{6,4},{5,7},{7,5},{8,10},{10,8},{9,1... | collective-permute-start | bytes 2359304 | tf_op jit(solution)/shard_map/ppermute | solution.py:48
  13.2 19.3 %collective-permute-start.4 = (bf16[192,768]{1,0:T(8,128)(2,1)}, bf16[192,768]{1,0:T(8,128)(2,1)S(1)}, u32[]{:S(2)}, u32[]{:S(2)}) collective-permute-start(bf16[192,768]{1,0:T(8,128)(2,1)} %get-tuple-element.249), channel_id=1, source_target_pairs={{0,2},{2,0},{1,3},{3,1},{4,6},{6,4},{5,7},{7,5},{8,10},{10,8},{9,1... | collective-permute-start | bytes 884744 | tf_op jit(solution)/shard_map/ppermute | solution.py:48
  35.0 62.0 %collective-permute-start.18 = (bf16[16,256,768]{2,1,0:T(8,128)(2,1)}, bf16[16,256,768]{2,1,0:T(8,128)(2,1)}, u32[]{:S(2)}, u32[]{:S(2)}) collective-permute-start(bf16[16,256,768]{2,1,0:T(8,128)(2,1)} %refs_9_.19), channel_id=1, source_target_pairs={{0,1},{1,0},{2,3},{3,2},{4,5},{5,4},{6,7},{7,6},{8,9},{9,8},{10,11... | collective-permute-start | bytes 18874376 | tf_op jit(solution)/shard_map/ppermute | solution.py:48
  35.9 61.1 %collective-permute-start.17 = (bf16[16,768,256]{2,1,0:T(8,128)(2,1)}, bf16[16,768,256]{2,1,0:T(8,128)(2,1)}, u32[]{:S(2)}, u32[]{:S(2)}) collective-permute-start(bf16[16,768,256]{2,1,0:T(8,128)(2,1)} %refs_17_.1), channel_id=1, source_target_pairs={{0,1},{1,0},{2,3},{3,2},{4,5},{5,4},{6,7},{7,6},{8,9},{9,8},{10,11... | collective-permute-start | bytes 18874376 | tf_op jit(solution)/shard_map/ppermute | solution.py:48
  36.0 19.8 %collective-permute-start.5 = (bf16[512,768]{1,0:T(8,128)(2,1)S(1)}, bf16[512,768]{1,0:T(8,128)(2,1)S(1)}, u32[]{:S(2)}, u32[]{:S(2)}) collective-permute-start(bf16[512,768]{1,0:T(8,128)(2,1)S(1)} %copy-done.45), channel_id=1, source_target_pairs={{0,2},{2,0},{1,3},{3,1},{4,6},{6,4},{5,7},{7,5},{8,10},{10,8},{9,1... | collective-permute-start | bytes 2359304 | tf_op jit(solution)/shard_map/ppermute | solution.py:48
  63.9 20.3 %collective-permute-start.12 = (bf16[1024,384]{1,0:T(8,128)(2,1)}, bf16[1024,384]{1,0:T(8,128)(2,1)}, u32[]{:S(2)}, u32[]{:S(2)}) collective-permute-start(bf16[1024,384]{1,0:T(8,128)(2,1)} %attend.1.refs_4_.refs_5_), channel_id=1, source_target_pairs={{0,2},{2,0},{1,3},{3,1},{4,6},{6,4},{5,7},{7,5},{8,10},{10,8},{9,1... | collective-permute-start | bytes 2359304 | tf_op jit(solution)/shard_map/ppermute | solution.py:48
  67.2 29.7 %collective-permute-start.15 = (bf16[1024,768]{1,0:T(8,128)(2,1)S(1)}, bf16[1024,768]{1,0:T(8,128)(2,1)S(1)}, u32[]{:S(2)}, u32[]{:S(2)}) collective-permute-start(bf16[1024,768]{1,0:T(8,128)(2,1)S(1)} %join.5.refs_2_.out_grad_ref), channel_id=1, source_target_pairs={{0,1},{1,0},{2,3},{3,2},{4,5},{5,4},{6,7},{7,6},{8,9},{9,8},{10,11... | collective-permute-start | bytes 4718600 | tf_op jit(solution)/shard_map/ppermute | solution.py:48
  109.7 19.7 %collective-permute-start.19 = (bf16[1,1536,384]{2,1,0:T(8,128)(2,1)S(1)}, bf16[1,1536,384]{2,1,0:T(8,128)(2,1)S(1)}, u32[]{:S(2)}, u32[]{:S(2)}) collective-permute-start(bf16[1,1536,384]{2,1,0:T(8,128)(2,1)S(1)} %get-tuple-element.264), channel_id=1, source_target_pairs={{0,8},{8,16},{16,24},{24,28},{28,20},{20,12},{12,4},{4,0},{9,1},{1... | collective-permute-start | bytes 3538952 | tf_op jit(solution)/shard_map/ppermute | solution.py:978
  120.1 23.3 %collective-permute-start.21 = (bf16[1,1536,384]{2,1,0:T(8,128)(2,1)S(1)}, bf16[1,1536,384]{2,1,0:T(8,128)(2,1)S(1)}, u32[]{:S(2)}, u32[]{:S(2)}) collective-permute-start(bf16[1,1536,384]{2,1,0:T(8,128)(2,1)S(1)} %get-tuple-element.274), channel_id=1, source_target_pairs={{8,0},{16,8},{24,16},{28,24},{20,28},{12,20},{4,12},{0,4},{1,9},{9... | collective-permute-start | bytes 3538952 | tf_op jit(solution)/shard_map/ppermute | solution.py:978
  129.7 25.6 %collective-permute-start.20 = (bf16[1,1536,384]{2,1,0:T(8,128)(2,1)S(1)}, bf16[1,1536,384]{2,1,0:T(8,128)(2,1)S(1)}, u32[]{:S(2)}, u32[]{:S(2)}) collective-permute-start(bf16[1,1536,384]{2,1,0:T(8,128)(2,1)S(1)} %ring_sum.14), channel_id=1, source_target_pairs={{0,8},{8,16},{16,24},{24,28},{28,20},{20,12},{12,4},{4,0},{9,1},{1... | collective-permute-start | bytes 3538952 | tf_op jit(solution)/shard_map/ppermute | solution.py:978
  143.7 25.0 %collective-permute-start.23 = (bf16[1,1536,384]{2,1,0:T(8,128)(2,1)S(1)}, bf16[1,1536,384]{2,1,0:T(8,128)(2,1)S(1)}, u32[]{:S(2)}, u32[]{:S(2)}) collective-permute-start(bf16[1,1536,384]{2,1,0:T(8,128)(2,1)S(1)} %ring_sum.15), channel_id=1, source_target_pairs={{8,0},{16,8},{24,16},{28,24},{20,28},{12,20},{4,12},{0,4},{1,9},{9... | collective-permute-start | bytes 3538952 | tf_op jit(solution)/shard_map/ppermute | solution.py:978
  155.7 25.2 %collective-permute-start.22 = (bf16[1,1536,384]{2,1,0:T(8,128)(2,1)S(1)}, bf16[1,1536,384]{2,1,0:T(8,128)(2,1)S(1)}, u32[]{:S(2)}, u32[]{:S(2)}) collective-permute-start(bf16[1,1536,384]{2,1,0:T(8,128)(2,1)S(1)} %ring_sum.16), channel_id=1, source_target_pairs={{0,8},{8,16},{16,24},{24,28},{28,20},{20,12},{12,4},{4,0},{9,1},{1... | collective-permute-start | bytes 3538952 | tf_op jit(solution)/shard_map/ppermute | solution.py:978
  170.4 29.7 %collective-permute-start.25 = (bf16[1,1536,384]{2,1,0:T(8,128)(2,1)}, bf16[1,1536,384]{2,1,0:T(8,128)(2,1)S(1)}, u32[]{:S(2)}, u32[]{:S(2)}) collective-permute-start(bf16[1,1536,384]{2,1,0:T(8,128)(2,1)} %ring_sum.17), channel_id=1, source_target_pairs={{8,0},{16,8},{24,16},{28,24},{20,28},{12,20},{4,12},{0,4},{1,9},{9... | collective-permute-start | bytes 3538952 | tf_op jit(solution)/shard_map/ppermute | solution.py:978
  185.0 28.5 %collective-permute-start.24 = (bf16[1,1536,384]{2,1,0:T(8,128)(2,1)}, bf16[1,1536,384]{2,1,0:T(8,128)(2,1)}, u32[]{:S(2)}, u32[]{:S(2)}) collective-permute-start(bf16[1,1536,384]{2,1,0:T(8,128)(2,1)} %ring_sum.18), channel_id=1, source_target_pairs={{0,8},{8,16},{16,24},{24,28},{28,20},{20,12},{12,4},{4,0},{9,1},{1... | collective-permute-start | bytes 3538952 | tf_op jit(solution)/shard_map/ppermute | solution.py:978
  202.7 29.3 %collective-permute-start.30 = (bf16[1,1536,384]{2,1,0:T(8,128)(2,1)S(1)}, bf16[1,1536,384]{2,1,0:T(8,128)(2,1)S(1)}, u32[]{:S(2)}, u32[]{:S(2)}) collective-permute-start(bf16[1,1536,384]{2,1,0:T(8,128)(2,1)S(1)} %ring_sum.19), channel_id=1, source_target_pairs={{8,0},{16,8},{24,16},{28,24},{20,28},{12,20},{4,12},{0,4},{1,9},{9... | collective-permute-start | bytes 3538952 | tf_op jit(solution)/shard_map/ppermute | solution.py:978
  230.5 27.2 %collective-permute-start.29 = (bf16[1,1536,384]{2,1,0:T(8,128)(2,1)}, bf16[1,1536,384]{2,1,0:T(8,128)(2,1)}, u32[]{:S(2)}, u32[]{:S(2)}) collective-permute-start(bf16[1,1536,384]{2,1,0:T(8,128)(2,1)} %ring_sum.20), channel_id=1, source_target_pairs={{0,8},{8,16},{16,24},{24,28},{28,20},{20,12},{12,4},{4,0},{9,1},{1... | collective-permute-start | bytes 3538952 | tf_op jit(solution)/shard_map/ppermute | solution.py:978
  233.7 35.6 %collective-permute-start.32 = (bf16[1,1536,384]{2,1,0:T(8,128)(2,1)}, bf16[1,1536,384]{2,1,0:T(8,128)(2,1)}, u32[]{:S(2)}, u32[]{:S(2)}) collective-permute-start(bf16[1,1536,384]{2,1,0:T(8,128)(2,1)} %ring_sum.21), channel_id=1, source_target_pairs={{8,0},{16,8},{24,16},{28,24},{20,28},{12,20},{4,12},{0,4},{1,9},{9... | collective-permute-start | bytes 3538952 | tf_op jit(solution)/shard_map/ppermute | solution.py:978
  250.5 40.7 %collective-permute-start.37 = (bf16[1024,768]{1,0:T(8,128)(2,1)}, bf16[1024,768]{1,0:T(8,128)(2,1)S(1)}, u32[]{:S(2)}, u32[]{:S(2)}) collective-permute-start(bf16[1024,768]{1,0:T(8,128)(2,1)} %get-tuple-element.311), channel_id=1, source_target_pairs={{0,2},{2,0},{1,3},{3,1},{4,6},{6,4},{5,7},{7,5},{8,10},{10,8},{9,1... | collective-permute-start | bytes 4718600 | tf_op jit(solution)/shard_map/ppermute | solution.py:48
  259.9 22.0 %collective-permute-start.35 = (bf16[1,1536,384]{2,1,0:T(8,128)(2,1)S(1)}, bf16[1,1536,384]{2,1,0:T(8,128)(2,1)}, u32[]{:S(2)}, u32[]{:S(2)}) collective-permute-start(bf16[1,1536,384]{2,1,0:T(8,128)(2,1)S(1)} %ring_sum.22), channel_id=1, source_target_pairs={{0,8},{8,16},{16,24},{24,28},{28,20},{20,12},{12,4},{4,0},{9,1},{1... | collective-permute-start | bytes 3538952 | tf_op jit(solution)/shard_map/ppermute | solution.py:978
  304.8 31.5 %collective-permute-start.40 = (bf16[1024,768]{1,0:T(8,128)(2,1)S(1)}, bf16[1024,768]{1,0:T(8,128)(2,1)}, u32[]{:S(2)}, u32[]{:S(2)}) collective-permute-start(bf16[1024,768]{1,0:T(8,128)(2,1)S(1)} %get-tuple-element.331.grad_ref.refs_6_), channel_id=1, source_target_pairs={{0,1},{1,0},{2,3},{3,2},{4,5},{5,4},{6,7},{7,6},{8,9},{9,8},{10,11... | collective-permute-start | bytes 4718600 | tf_op jit(solution)/shard_map/ppermute | solution.py:48
  304.9 28.5 %collective-permute-start.39 = (bf16[1,1536,384]{2,1,0:T(8,128)(2,1)S(1)}, bf16[1,1536,384]{2,1,0:T(8,128)(2,1)S(1)}, u32[]{:S(2)}, u32[]{:S(2)}) collective-permute-start(bf16[1,1536,384]{2,1,0:T(8,128)(2,1)S(1)} %ring_sum.24), channel_id=1, source_target_pairs={{0,8},{8,16},{16,24},{24,28},{28,20},{20,12},{12,4},{4,0},{9,1},{1... | collective-permute-start | bytes 3538952 | tf_op jit(solution)/shard_map/ppermute | solution.py:978
  306.1 43.3 %collective-permute-start.42 = (bf16[1,1536,384]{2,1,0:T(8,128)(2,1)}, bf16[1,1536,384]{2,1,0:T(8,128)(2,1)}, u32[]{:S(2)}, u32[]{:S(2)}) collective-permute-start(bf16[1,1536,384]{2,1,0:T(8,128)(2,1)} %ring_sum.25), channel_id=1, source_target_pairs={{8,0},{16,8},{24,16},{28,24},{20,28},{12,20},{4,12},{0,4},{1,9},{9... | collective-permute-start | bytes 3538952 | tf_op jit(solution)/shard_map/ppermute | solution.py:978
  334.8 37.5 %collective-permute-start.41 = (bf16[1,768,384]{2,1,0:T(8,128)(2,1)S(1)}, bf16[1,768,384]{2,1,0:T(8,128)(2,1)}, u32[]{:S(2)}, u32[]{:S(2)}) collective-permute-start(bf16[1,768,384]{2,1,0:T(8,128)(2,1)S(1)} %get-tuple-element.340.refs_0_), channel_id=1, source_target_pairs={{0,8},{8,16},{16,24},{24,28},{28,20},{20,12},{12,4},{4,0},{9,1},{1... | collective-permute-start | bytes 1769480 | tf_op jit(solution)/shard_map/ppermute | solution.py:978
  352.6 24.3 %collective-permute-start.45 = (bf16[1,768,384]{2,1,0:T(8,128)(2,1)S(1)}, bf16[1,768,384]{2,1,0:T(8,128)(2,1)S(1)}, u32[]{:S(2)}, u32[]{:S(2)}) collective-permute-start(bf16[1,768,384]{2,1,0:T(8,128)(2,1)S(1)} %get-tuple-element.339.refs_1_), channel_id=1, source_target_pairs={{8,0},{16,8},{24,16},{28,24},{20,28},{12,20},{4,12},{0,4},{1,9},{9... | collective-permute-start | bytes 1769480 | tf_op jit(solution)/shard_map/ppermute | solution.py:978
  372.3 24.1 %collective-permute-start.43 = (bf16[1,768,384]{2,1,0:T(8,128)(2,1)}, bf16[1,768,384]{2,1,0:T(8,128)(2,1)S(1)}, u32[]{:S(2)}, u32[]{:S(2)}) collective-permute-start(bf16[1,768,384]{2,1,0:T(8,128)(2,1)} %collective-permute-done.41.refs_0_), channel_id=1, source_target_pairs={{0,8},{8,16},{16,24},{24,28},{28,20},{20,12},{12,4},{4,0},{9,1},{1... | collective-permute-start | bytes 1769480 | tf_op jit(solution)/shard_map/ppermute | solution.py:978
  376.9 21.4 %collective-permute-start.49 = (bf16[1,768,384]{2,1,0:T(8,128)(2,1)S(1)}, bf16[1,768,384]{2,1,0:T(8,128)(2,1)S(1)}, u32[]{:S(2)}, u32[]{:S(2)}) collective-permute-start(bf16[1,768,384]{2,1,0:T(8,128)(2,1)S(1)} %collective-permute-done.45.refs_1_), channel_id=1, source_target_pairs={{8,0},{16,8},{24,16},{28,24},{20,28},{12,20},{4,12},{0,4},{1,9},{9... | collective-permute-start | bytes 1769480 | tf_op jit(solution)/shard_map/ppermute | solution.py:978
  396.4 27.7 %collective-permute-start.47 = (bf16[1,768,384]{2,1,0:T(8,128)(2,1)S(1)}, bf16[1,768,384]{2,1,0:T(8,128)(2,1)S(1)}, u32[]{:S(2)}, u32[]{:S(2)}) collective-permute-start(bf16[1,768,384]{2,1,0:T(8,128)(2,1)S(1)} %collective-permute-done.43.refs_0_), channel_id=1, source_target_pairs={{0,8},{8,16},{16,24},{24,28},{28,20},{20,12},{12,4},{4,0},{9,1},{1... | collective-permute-start | bytes 1769480 | tf_op jit(solution)/shard_map/ppermute | solution.py:978
  398.3 28.1 %collective-permute-start.52 = (bf16[1,768,384]{2,1,0:T(8,128)(2,1)S(1)}, bf16[1,768,384]{2,1,0:T(8,128)(2,1)S(1)}, u32[]{:S(2)}, u32[]{:S(2)}) collective-permute-start(bf16[1,768,384]{2,1,0:T(8,128)(2,1)S(1)} %collective-permute-done.49.refs_1_), channel_id=1, source_target_pairs={{8,0},{16,8},{24,16},{28,24},{20,28},{12,20},{4,12},{0,4},{1,9},{9... | collective-permute-start | bytes 1769480 | tf_op jit(solution)/shard_map/ppermute | solution.py:978
  399.2 22.1 %collective-permute-start.48 = (bf16[2,96,896]{2,1,0:T(8,128)(2,1)S(1)}, bf16[2,96,896]{2,1,0:T(8,128)(2,1)S(1)}, u32[]{:S(2)}, u32[]{:S(2)}) collective-permute-start(bf16[2,96,896]{2,1,0:T(8,128)(2,1)S(1)} %late_chunk.19), channel_id=1, source_target_pairs={{8,0},{16,8},{24,16},{28,24},{20,28},{12,20},{4,12},{0,4},{1,9},{9... | collective-permute-start | bytes 1032200 | tf_op jit(solution)/shard_map/ppermute | solution.py:978
  399.6 26.2 %collective-permute-start.53 = (bf16[2,96,896]{2,1,0:T(8,128)(2,1)S(1)}, bf16[2,96,896]{2,1,0:T(8,128)(2,1)S(1)}, u32[]{:S(2)}, u32[]{:S(2)}) collective-permute-start(bf16[2,96,896]{2,1,0:T(8,128)(2,1)S(1)} %late_chunk.20), channel_id=1, source_target_pairs={{0,8},{8,16},{16,24},{24,28},{28,20},{20,12},{12,4},{4,0},{9,1},{1... | collective-permute-start | bytes 1032200 | tf_op jit(solution)/shard_map/ppermute | solution.py:978
  424.1 24.2 %collective-permute-start.62 = (bf16[1,768,384]{2,1,0:T(8,128)(2,1)S(1)}, bf16[1,768,384]{2,1,0:T(8,128)(2,1)S(1)}, u32[]{:S(2)}, u32[]{:S(2)}) collective-permute-start(bf16[1,768,384]{2,1,0:T(8,128)(2,1)S(1)} %collective-permute-done.47.refs_0_), channel_id=1, source_target_pairs={{0,8},{8,16},{16,24},{24,28},{28,20},{20,12},{12,4},{4,0},{9,1},{1... | collective-permute-start | bytes 1769480 | tf_op jit(solution)/shard_map/ppermute | solution.py:978
  426.5 24.6 %collective-permute-start.66 = (bf16[1,768,384]{2,1,0:T(8,128)(2,1)S(1)}, bf16[1,768,384]{2,1,0:T(8,128)(2,1)S(1)}, u32[]{:S(2)}, u32[]{:S(2)}) collective-permute-start(bf16[1,768,384]{2,1,0:T(8,128)(2,1)S(1)} %collective-permute-done.52.refs_1_), channel_id=1, source_target_pairs={{8,0},{16,8},{24,16},{28,24},{20,28},{12,20},{4,12},{0,4},{1,9},{9... | collective-permute-start | bytes 1769480 | tf_op jit(solution)/shard_map/ppermute | solution.py:978
  428.2 22.2 %collective-permute-start.61 = (bf16[2,96,896]{2,1,0:T(8,128)(2,1)S(1)}, bf16[2,96,896]{2,1,0:T(8,128)(2,1)S(1)}, u32[]{:S(2)}, u32[]{:S(2)}) collective-permute-start(bf16[2,96,896]{2,1,0:T(8,128)(2,1)S(1)} %late_chunk.22), channel_id=1, source_target_pairs={{0,8},{8,16},{16,24},{24,28},{28,20},{20,12},{12,4},{4,0},{9,1},{1... | collective-permute-start | bytes 1032200 | tf_op jit(solution)/shard_map/ppermute | solution.py:978
  451.1 22.1 %collective-permute-start.70 = (bf16[1,768,384]{2,1,0:T(8,128)(2,1)S(1)}, bf16[1,768,384]{2,1,0:T(8,128)(2,1)S(1)}, u32[]{:S(2)}, u32[]{:S(2)}) collective-permute-start(bf16[1,768,384]{2,1,0:T(8,128)(2,1)S(1)} %collective-permute-done.66.refs_1_), channel_id=1, source_target_pairs={{8,0},{16,8},{24,16},{28,24},{20,28},{12,20},{4,12},{0,4},{1,9},{9... | collective-permute-start | bytes 1769480 | tf_op jit(solution)/shard_map/ppermute | solution.py:978
  451.5 22.5 %collective-permute-start.72 = (bf16[1,768,384]{2,1,0:T(8,128)(2,1)S(1)}, bf16[1,768,384]{2,1,0:T(8,128)(2,1)S(1)}, u32[]{:S(2)}, u32[]{:S(2)}) collective-permute-start(bf16[1,768,384]{2,1,0:T(8,128)(2,1)S(1)} %copy-done.63), channel_id=1, source_target_pairs={{0,1},{1,0},{2,3},{3,2},{4,5},{5,4},{6,7},{7,6},{8,9},{9,8},{10,11... | collective-permute-start | bytes 1769480 | tf_op jit(solution)/shard_map/ppermute | solution.py:48
  451.5 19.8 %collective-permute-start.63 = (bf16[2,96,896]{2,1,0:T(8,128)(2,1)S(1)}, bf16[2,96,896]{2,1,0:T(8,128)(2,1)S(1)}, u32[]{:S(2)}, u32[]{:S(2)}) collective-permute-start(bf16[2,96,896]{2,1,0:T(8,128)(2,1)S(1)} %late_chunk.24), channel_id=1, source_target_pairs={{0,8},{8,16},{16,24},{24,28},{28,20},{20,12},{12,4},{4,0},{9,1},{1... | collective-permute-start | bytes 1032200 | tf_op jit(solution)/shard_map/ppermute | solution.py:978
  460.6 23.5 %collective-permute-start.77 = (bf16[1,768,384]{2,1,0:T(8,128)(2,1)S(1)}, bf16[1,768,384]{2,1,0:T(8,128)(2,1)S(1)}, u32[]{:S(2)}, u32[]{:S(2)}) collective-permute-start(bf16[1,768,384]{2,1,0:T(8,128)(2,1)S(1)} %copy-done.61), channel_id=1, source_target_pairs={{0,1},{1,0},{2,3},{3,2},{4,5},{5,4},{6,7},{7,6},{8,9},{9,8},{10,11... | collective-permute-start | bytes 1769480 | tf_op jit(solution)/shard_map/ppermute | solution.py:48
  464.0 21.2 %collective-permute-start.68 = (bf16[1,768,384]{2,1,0:T(8,128)(2,1)S(1)}, bf16[1,768,384]{2,1,0:T(8,128)(2,1)S(1)}, u32[]{:S(2)}, u32[]{:S(2)}) collective-permute-start(bf16[1,768,384]{2,1,0:T(8,128)(2,1)S(1)} %collective-permute-done.64.refs_0_), channel_id=1, source_target_pairs={{0,8},{8,16},{16,24},{24,28},{28,20},{20,12},{12,4},{4,0},{9,1},{1... | collective-permute-start | bytes 1769480 | tf_op jit(solution)/shard_map/ppermute | solution.py:978
  473.2 32.3 %collective-permute-start.75 = (bf16[1,768,384]{2,1,0:T(8,128)(2,1)S(1)}, bf16[1,768,384]{2,1,0:T(8,128)(2,1)S(1)}, u32[]{:S(2)}, u32[]{:S(2)}) collective-permute-start(bf16[1,768,384]{2,1,0:T(8,128)(2,1)S(1)} %collective-permute-done.70.refs_1_), channel_id=1, source_target_pairs={{8,0},{16,8},{24,16},{28,24},{20,28},{12,20},{4,12},{0,4},{1,9},{9... | collective-permute-start | bytes 1769480 | tf_op jit(solution)/shard_map/ppermute | solution.py:978
  474.0 36.7 %collective-permute-start.73 = (bf16[1,768,384]{2,1,0:T(8,128)(2,1)S(1)}, bf16[1,768,384]{2,1,0:T(8,128)(2,1)S(1)}, u32[]{:S(2)}, u32[]{:S(2)}) collective-permute-start(bf16[1,768,384]{2,1,0:T(8,128)(2,1)S(1)} %collective-permute-done.72.refs_0_), channel_id=1, source_target_pairs={{0,8},{8,16},{16,24},{24,28},{28,20},{20,12},{12,4},{4,0},{9,1},{1... | collective-permute-start | bytes 1769480 | tf_op jit(solution)/shard_map/ppermute | solution.py:978
  482.3 21.2 %collective-permute-start.67 = (bf16[2,96,896]{2,1,0:T(8,128)(2,1)S(1)}, bf16[2,96,896]{2,1,0:T(8,128)(2,1)S(1)}, u32[]{:S(2)}, u32[]{:S(2)}) collective-permute-start(bf16[2,96,896]{2,1,0:T(8,128)(2,1)S(1)} %late_chunk.26), channel_id=1, source_target_pairs={{0,8},{8,16},{16,24},{24,28},{28,20},{20,12},{12,4},{4,0},{9,1},{1... | collective-permute-start | bytes 1032200 | tf_op jit(solution)/shard_map/ppermute | solution.py:978
  484.1 23.7 %collective-permute-start.74 = (bf16[2,96,896]{2,1,0:T(8,128)(2,1)S(1)}, bf16[2,96,896]{2,1,0:T(8,128)(2,1)S(1)}, u32[]{:S(2)}, u32[]{:S(2)}) collective-permute-start(bf16[2,96,896]{2,1,0:T(8,128)(2,1)S(1)} %late_chunk.27), channel_id=1, source_target_pairs={{8,0},{16,8},{24,16},{28,24},{20,28},{12,20},{4,12},{0,4},{1,9},{9... | collective-permute-start | bytes 1032200 | tf_op jit(solution)/shard_map/ppermute | solution.py:978
  485.1 37.5 %collective-permute-start.78 = (bf16[1,768,384]{2,1,0:T(8,128)(2,1)S(1)}, bf16[1,768,384]{2,1,0:T(8,128)(2,1)S(1)}, u32[]{:S(2)}, u32[]{:S(2)}) collective-permute-start(bf16[1,768,384]{2,1,0:T(8,128)(2,1)S(1)} %collective-permute-done.77.refs_1_), channel_id=1, source_target_pairs={{8,0},{16,8},{24,16},{28,24},{20,28},{12,20},{4,12},{0,4},{1,9},{9... | collective-permute-start | bytes 1769480 | tf_op jit(solution)/shard_map/ppermute | solution.py:978
  503.6 20.8 %collective-permute-start.82 = (bf16[1,768,384]{2,1,0:T(8,128)(2,1)S(1)}, bf16[1,768,384]{2,1,0:T(8,128)(2,1)S(1)}, u32[]{:S(2)}, u32[]{:S(2)}) collective-permute-start(bf16[1,768,384]{2,1,0:T(8,128)(2,1)S(1)} %collective-permute-done.68.refs_0_), channel_id=1, source_target_pairs={{0,8},{8,16},{16,24},{24,28},{28,20},{20,12},{12,4},{4,0},{9,1},{1... | collective-permute-start | bytes 1769480 | tf_op jit(solution)/shard_map/ppermute | solution.py:978
  510.7 19.3 %collective-permute-start.81 = (bf16[1,768,384]{2,1,0:T(8,128)(2,1)S(1)}, bf16[1,768,384]{2,1,0:T(8,128)(2,1)}, u32[]{:S(2)}, u32[]{:S(2)}) collective-permute-start(bf16[1,768,384]{2,1,0:T(8,128)(2,1)S(1)} %collective-permute-done.73.refs_0_), channel_id=1, source_target_pairs={{0,8},{8,16},{16,24},{24,28},{28,20},{20,12},{12,4},{4,0},{9,1},{1... | collective-permute-start | bytes 1769480 | tf_op jit(solution)/shard_map/ppermute | solution.py:978
  521.9 46.3 %collective-permute-start.54 = (bf16[1024,768]{1,0:T(8,128)(2,1)}, bf16[1024,768]{1,0:T(8,128)(2,1)}, u32[]{:S(2)}, u32[]{:S(2)}) collective-permute-start(bf16[1024,768]{1,0:T(8,128)(2,1)} %convolution_convert_fusion), channel_id=1, source_target_pairs={{0,1},{1,0},{2,3},{3,2},{4,5},{5,4},{6,7},{7,6},{8,9},{9,8},{10,11... | collective-permute-start | bytes 4718600 | tf_op jit(solution)/shard_map/ppermute | solution.py:48
  524.4 21.2 %collective-permute-start.88 = (bf16[1,768,384]{2,1,0:T(8,128)(2,1)S(1)}, bf16[1,768,384]{2,1,0:T(8,128)(2,1)}, u32[]{:S(2)}, u32[]{:S(2)}) collective-permute-start(bf16[1,768,384]{2,1,0:T(8,128)(2,1)S(1)} %collective-permute-done.78.refs_1_), channel_id=1, source_target_pairs={{8,0},{16,8},{24,16},{28,24},{20,28},{12,20},{4,12},{0,4},{1,9},{9... | collective-permute-start | bytes 1769480 | tf_op jit(solution)/shard_map/ppermute | solution.py:978
  530.0 62.0 %collective-permute-start.33 = (bf16[1024,768]{1,0:T(8,128)(2,1)S(1)}, bf16[1024,768]{1,0:T(8,128)(2,1)}, u32[]{:S(2)}, u32[]{:S(2)}) collective-permute-start(bf16[1024,768]{1,0:T(8,128)(2,1)S(1)} %copy-done.24), channel_id=1, source_target_pairs={{0,1},{1,0},{2,3},{3,2},{4,5},{5,4},{6,7},{7,6},{8,9},{9,8},{10,11... | collective-permute-start | bytes 4718600 | tf_op jit(solution)/shard_map/ppermute | solution.py:48
  545.6 19.6 %collective-permute-start.92 = (bf16[1,768,384]{2,1,0:T(8,128)(2,1)}, bf16[1,768,384]{2,1,0:T(8,128)(2,1)}, u32[]{:S(2)}, u32[]{:S(2)}) collective-permute-start(bf16[1,768,384]{2,1,0:T(8,128)(2,1)} %collective-permute-done.88.refs_1_), channel_id=1, source_target_pairs={{8,0},{16,8},{24,16},{28,24},{20,28},{12,20},{4,12},{0,4},{1,9},{9... | collective-permute-start | bytes 1769480 | tf_op jit(solution)/shard_map/ppermute | solution.py:978
  561.2 27.7 %collective-permute-start.90 = (bf16[1,768,384]{2,1,0:T(8,128)(2,1)}, bf16[1,768,384]{2,1,0:T(8,128)(2,1)S(1)}, u32[]{:S(2)}, u32[]{:S(2)}) collective-permute-start(bf16[1,768,384]{2,1,0:T(8,128)(2,1)} %collective-permute-done.85.refs_0_), channel_id=1, source_target_pairs={{0,8},{8,16},{16,24},{24,28},{28,20},{20,12},{12,4},{4,0},{9,1},{1... | collective-permute-start | bytes 1769480 | tf_op jit(solution)/shard_map/ppermute | solution.py:978
  565.2 25.8 %collective-permute-start.96 = (bf16[1,768,384]{2,1,0:T(8,128)(2,1)}, bf16[1,768,384]{2,1,0:T(8,128)(2,1)}, u32[]{:S(2)}, u32[]{:S(2)}) collective-permute-start(bf16[1,768,384]{2,1,0:T(8,128)(2,1)} %collective-permute-done.92.refs_1_), channel_id=1, source_target_pairs={{8,0},{16,8},{24,16},{28,24},{20,28},{12,20},{4,12},{0,4},{1,9},{9... | collective-permute-start | bytes 1769480 | tf_op jit(solution)/shard_map/ppermute | solution.py:978
  568.3 21.7 %collective-permute-start.89 = (bf16[192,896]{1,0:T(8,128)(2,1)}, bf16[192,896]{1,0:T(8,128)(2,1)}, u32[]{:S(2)}, u32[]{:S(2)}) collective-permute-start(bf16[192,896]{1,0:T(8,128)(2,1)} %collective-permute-done.84.refs_2_), channel_id=1, source_target_pairs={{0,8},{8,16},{16,24},{24,28},{28,20},{20,12},{12,4},{4,0},{9,1},{1... | collective-permute-start | bytes 1032200 | tf_op jit(solution)/shard_map/ppermute | solution.py:978
  584.0 31.7 %collective-permute-start.55 = (bf16[512,768]{1,0:T(8,128)(2,1)}, bf16[512,768]{1,0:T(8,128)(2,1)}, u32[]{:S(2)}, u32[]{:S(2)}) collective-permute-start(bf16[512,768]{1,0:T(8,128)(2,1)} %dynamic-slice_convert_fusion), channel_id=1, source_target_pairs={{0,2},{2,0},{1,3},{3,1},{4,6},{6,4},{5,7},{7,5},{8,10},{10,8},{9,1... | collective-permute-start | bytes 2359304 | tf_op jit(solution)/shard_map/ppermute | solution.py:48
  591.0 22.8 %collective-permute-start.93 = (bf16[192,896]{1,0:T(8,128)(2,1)}, bf16[192,896]{1,0:T(8,128)(2,1)}, u32[]{:S(2)}, u32[]{:S(2)}) collective-permute-start(bf16[192,896]{1,0:T(8,128)(2,1)} %collective-permute-done.89.refs_3_), channel_id=1, source_target_pairs={{0,8},{8,16},{16,24},{24,28},{28,20},{20,12},{12,4},{4,0},{9,1},{1... | collective-permute-start | bytes 1032200 | tf_op jit(solution)/shard_map/ppermute | solution.py:978
  592.0 22.8 %collective-permute-start.100 = (bf16[1,768,384]{2,1,0:T(8,128)(2,1)}, bf16[1,768,384]{2,1,0:T(8,128)(2,1)S(1)}, u32[]{:S(2)}, u32[]{:S(2)}) collective-permute-start(bf16[1,768,384]{2,1,0:T(8,128)(2,1)} %collective-permute-done.96.refs_1_), channel_id=1, source_target_pairs={{8,0},{16,8},{24,16},{28,24},{20,28},{12,20},{4,12},{0,4},{1,9},{9... | collective-permute-start | bytes 1769480 | tf_op jit(solution)/shard_map/ppermute | solution.py:978
  600.6 39.9 %collective-permute-start.34 = (bf16[512,768]{1,0:T(8,128)(2,1)}, bf16[512,768]{1,0:T(8,128)(2,1)}, u32[]{:S(2)}, u32[]{:S(2)}) collective-permute-start(bf16[512,768]{1,0:T(8,128)(2,1)} %dynamic-slice_convert_fusion.1), channel_id=1, source_target_pairs={{0,2},{2,0},{1,3},{3,1},{4,6},{6,4},{5,7},{7,5},{8,10},{10,8},{9,1... | collective-permute-start | bytes 2359304 | tf_op jit(solution)/shard_map/ppermute | solution.py:48
  613.8 22.9 %collective-permute-start.98 = (bf16[1,768,384]{2,1,0:T(8,128)(2,1)}, bf16[1,768,384]{2,1,0:T(8,128)(2,1)S(1)}, u32[]{:S(2)}, u32[]{:S(2)}) collective-permute-start(bf16[1,768,384]{2,1,0:T(8,128)(2,1)} %collective-permute-done.94.refs_0_), channel_id=1, source_target_pairs={{0,8},{8,16},{16,24},{24,28},{28,20},{20,12},{12,4},{4,0},{9,1},{1... | collective-permute-start | bytes 1769480 | tf_op jit(solution)/shard_map/ppermute | solution.py:978
  614.7 23.8 %collective-permute-start.97 = (bf16[192,896]{1,0:T(8,128)(2,1)}, bf16[192,896]{1,0:T(8,128)(2,1)S(1)}, u32[]{:S(2)}, u32[]{:S(2)}) collective-permute-start(bf16[192,896]{1,0:T(8,128)(2,1)} %collective-permute-done.93.refs_4_), channel_id=1, source_target_pairs={{0,8},{8,16},{16,24},{24,28},{28,20},{20,12},{12,4},{4,0},{9,1},{1... | collective-permute-start | bytes 1032200 | tf_op jit(solution)/shard_map/ppermute | solution.py:978
  615.7 23.0 %collective-permute-start.104 = (bf16[1,768,384]{2,1,0:T(8,128)(2,1)S(1)}, bf16[1,768,384]{2,1,0:T(8,128)(2,1)S(1)}, u32[]{:S(2)}, u32[]{:S(2)}) collective-permute-start(bf16[1,768,384]{2,1,0:T(8,128)(2,1)S(1)} %collective-permute-done.100.refs_1_), channel_id=1, source_target_pairs={{8,0},{16,8},{24,16},{28,24},{20,28},{12,20},{4,12},{0,4},{1,9},{9... | collective-permute-start | bytes 1769480 | tf_op jit(solution)/shard_map/ppermute | solution.py:978
  638.5 24.8 %collective-permute-start.102 = (bf16[1,768,384]{2,1,0:T(8,128)(2,1)S(1)}, bf16[1,768,384]{2,1,0:T(8,128)(2,1)S(1)}, u32[]{:S(2)}, u32[]{:S(2)}) collective-permute-start(bf16[1,768,384]{2,1,0:T(8,128)(2,1)S(1)} %collective-permute-done.98.refs_0_), channel_id=1, source_target_pairs={{0,8},{8,16},{16,24},{24,28},{28,20},{20,12},{12,4},{4,0},{9,1},{1... | collective-permute-start | bytes 1769480 | tf_op jit(solution)/shard_map/ppermute | solution.py:978
  638.7 24.6 %collective-permute-start.105 = (bf16[1,768,384]{2,1,0:T(8,128)(2,1)S(1)}, bf16[1,768,384]{2,1,0:T(8,128)(2,1)S(1)}, u32[]{:S(2)}, u32[]{:S(2)}) collective-permute-start(bf16[1,768,384]{2,1,0:T(8,128)(2,1)S(1)} %collective-permute-done.104.refs_1_), channel_id=1, source_target_pairs={{8,0},{16,8},{24,16},{28,24},{20,28},{12,20},{4,12},{0,4},{1,9},{9... | collective-permute-start | bytes 1769480 | tf_op jit(solution)/shard_map/ppermute | solution.py:978
  642.9 22.5 %collective-permute-start.101 = (bf16[192,896]{1,0:T(8,128)(2,1)S(1)}, bf16[192,896]{1,0:T(8,128)(2,1)S(1)}, u32[]{:S(2)}, u32[]{:S(2)}) collective-permute-start(bf16[192,896]{1,0:T(8,128)(2,1)S(1)} %collective-permute-done.97.refs_5_), channel_id=1, source_target_pairs={{0,8},{8,16},{16,24},{24,28},{28,20},{20,12},{12,4},{4,0},{9,1},{1... | collective-permute-start | bytes 1032200 | tf_op jit(solution)/shard_map/ppermute | solution.py:978
  643.1 23.9 %collective-permute-start.107 = (bf16[192,896]{1,0:T(8,128)(2,1)S(1)}, bf16[192,896]{1,0:T(8,128)(2,1)S(1)}, u32[]{:S(2)}, u32[]{:S(2)}) collective-permute-start(bf16[192,896]{1,0:T(8,128)(2,1)S(1)} %collective-permute-done.103.refs_13_), channel_id=1, source_target_pairs={{8,0},{16,8},{24,16},{28,24},{20,28},{12,20},{4,12},{0,4},{1,9},{9... | collective-permute-start | bytes 1032200 | tf_op jit(solution)/shard_map/ppermute | solution.py:978
  (133 other events, 1171.6 us)

commit v9 on v8

--- a/solution.py
+++ b/solution.py
@@ -19,6 +19,7 @@
 F32 = jnp.float32
 BF16 = jnp.bfloat16
 MIB = 1024 * 1024
+GAIN_ROWS = 16
 SMALL = pl.CostEstimate(flops=0, bytes_accessed=0, transcendentals=0)
 
 
@@ -852,10 +853,34 @@
     )(plan, pack, *came)
 
 
+def late_join_kernel(col_ref, own_ref, other_ref, gains_ref, out_ref):
+    rows = own_ref.shape[0]
+    features = gains_ref.shape[1]
+    out_ref[pl.ds(pl.multiple_of(col_ref[0] * rows, rows), rows), :] = own_ref[...]
+    out_ref[pl.ds(pl.multiple_of((1 - col_ref[0]) * rows, rows), rows), :] = other_ref[...]
+    out_ref[2 * rows :, :] = jnp.zeros((GAIN_ROWS, own_ref.shape[1]), BF16)
+    pad = jnp.zeros((GAIN_ROWS - 2, features), F32)
+    out_ref[2 * rows :, 0:features] = jnp.concatenate([gains_ref[...], pad], axis=0).astype(BF16)
+
+
+def late_join(col, own, other, gains):
+    rows, lanes = own.shape
+    spec = pl.BlockSpec(memory_space=pltpu.VMEM)
+    return pl.pallas_call(
+        late_join_kernel,
+        out_shape=jax.ShapeDtypeStruct((2 * rows + GAIN_ROWS, lanes), BF16),
+        in_specs=[pl.BlockSpec(memory_space=pltpu.SMEM)] + [spec] * 3,
+        out_specs=spec,
+        compiler_params=params(16),
+        cost_estimate=SMALL,
+        name="late_join",
+    )(col, own, other, gains)
+
+
 def unpack_late_kernel(first_step, steps, plan_ref, *refs):
     chunks = refs[0 : 2 * steps]
-    sgate, sup, sdown, query, key, value, out, all_ref = refs[2 * steps :]
-    rows, features = chunks[0].shape[0] // 2, all_ref.shape[2]
+    sgate, sup, sdown, query, key, value, out, gains, all_ref, gain_ref = refs[2 * steps :]
+    rows, features = (chunks[0].shape[0] - GAIN_ROWS) // 2, all_ref.shape[2]
     for k in range(2):
         for step in range(steps):
             at = plan_ref[first_step + 2 * step + k] * rows
@@ -863,6 +888,14 @@
                 all_ref[k, c, pl.ds(pl.multiple_of(at, rows), rows), :] = chunks[
                     steps * k + step
                 ][c * rows : (c + 1) * rows, :]
+    for step in range(steps):
+        at = plan_ref[first_step + 2 * step] * GAIN_ROWS
+        gain_ref[pl.ds(pl.multiple_of(at, GAIN_ROWS), GAIN_ROWS), :] = chunks[step][2 * rows :, :]
+    total = jnp.zeros((GAIN_ROWS, features), F32)
+    for step in range(steps):
+        rows_of = slice(step * GAIN_ROWS, (step + 1) * GAIN_ROWS)
+        total = total + gain_ref[rows_of, 0:features].astype(F32)
+    gains[...] = total[0:2]
     flipped = plan_ref[plan_ref.shape[0] - 1] != 0
     for c in range(2):
         for b in range(14):
@@ -891,14 +924,17 @@
 
 def unpack_late(plan, first_step, chunks, shapes):
     steps = len(chunks[0])
-    rows, lanes = chunks[0][0].shape[0] // 2, chunks[0][0].shape[1]
+    rows, lanes = (chunks[0][0].shape[0] - GAIN_ROWS) // 2, chunks[0][0].shape[1]
     spec = pl.BlockSpec(memory_space=pltpu.VMEM)
     return pl.pallas_call(
         functools.partial(unpack_late_kernel, first_step, steps),
         in_specs=[pl.BlockSpec(memory_space=pltpu.SMEM)] + [spec] * (2 * steps),
         out_specs=[spec] * len(shapes),
         out_shape=[jax.ShapeDtypeStruct(shape, F32) for shape in shapes],
-        scratch_shapes=[pltpu.VMEM((2, 2, steps * rows, lanes), BF16)],
+        scratch_shapes=[
+            pltpu.VMEM((2, 2, steps * rows, lanes), BF16),
+            pltpu.VMEM((steps * GAIN_ROWS, lanes), BF16),
+        ],
         compiler_params=params(48),
         cost_estimate=SMALL,
         name="unpack_late",
@@ -1085,7 +1121,7 @@
             result = run(first, last, order, tuple(kept))
             kept = result[2:]
             runs[first] = result[0:2]
-            return kept[0]
+            return [kept[0]]
 
         return work
 
@@ -1093,7 +1129,7 @@
         runs["shared"] = expert_grads(
             order, 0, 1, None, [x_own, x_other], [grad_own, grad_other], gates, shared, ()
         )
-        return runs["shared"][2]
+        return [runs["shared"][2]]
 
     def work_back(half):
         def work(order, ties):
@@ -1108,10 +1144,10 @@
             )
             if half:
                 normed["other"] = swap(mixed[True, 1], "col")
-                return mixed[True, 1]
+                return [mixed[True, 1]]
             normed["sum"] = chip_sum(mixed[True, 0], normed["other"])
             normed["came"] = swap(normed["sum"][1], "row")
-            return normed["sum"][1]
+            return [mixed[True, 0]]
 
         return work
 
@@ -1126,7 +1162,7 @@
                 routed[4 + half : 5 + half],
                 shared[4 + half : 5 + half],
             )
-            return mixed[False, half]
+            return [mixed[False, half]] + ([] if half else [normed["sum"][1]])
 
         return work
 
@@ -1147,17 +1183,17 @@
             grads, products, products_c, hidden, scale_ffn, gains, grad_own
         )
         normed["grad_c"] = swap(normed["grad"], "col")
-        return normed["grad"]
+        return [normed["grad"]]
 
     def work_attend(order, ties):
         normed["qkv"] = attend_back(
             after(where, *ties), near[2], far[2], normed["grad"], normed["grad_c"], w_out, out_c
         )
-        return normed["qkv"]
+        return [normed["qkv"]]
 
     def work_late(order, ties):
         normed["packs"] = late_grads(
-            where,
+            after(where, *ties),
             near[0:2],
             far[0:2],
             normed["qkv"],
@@ -1166,12 +1202,11 @@
             normed["grad_c"],
             runs["shared"][0:2],
         )
-        return normed["packs"][0]
+        return normed["packs"]
 
     tasks = [work_experts(at, at + each) for at in range(each, pairs_total, each)]
     tasks += [work_shared, work_back(1), work_back(0), work_out(1), work_out(0)]
-    ends = [work_hidden, work_attend]
-    tasks += [None] * (2 * ring_size - 1 - len(tasks) - len(ends)) + ends
+    later = [work_hidden, work_attend, work_late]
     got = [None, None]
     if ring_size > 1:
         got[0] = send(sums[0], 0)
@@ -1182,7 +1217,7 @@
             last = sums
             task = tasks.pop(0) if tasks else None
             if task:
-                last = [task(after(order, *last), last)]
+                last = task(after(order, *last), last)
             sums[k] = ring_sum(after(got[k], *last), runs[each * s][k], s + 1 == ring_size)
             if s + 1 < ring_size:
                 got[k] = send(sums[k], k)
@@ -1198,19 +1233,48 @@
     crossed = [swap(across_rings(total), "col") for total in got]
     waves.append([crossed[1], crossed[0]])
 
-    hidden_grad, attn_grad, attn_grad_c = normed["hidden"], normed["grad"], normed["grad_c"]
-    gain_ffn_part, qkv_grad = normed["gain"], normed["qkv"]
-    work_late(order, ())
-    packs = normed["packs"]
-
-    packs = [
-        pack.reshape(2, ring_size, local_features // ring_size, pack.shape[2]) for pack in packs
-    ]
     chunks_first = 2 * experts
     late_total = 2 * (ring_size - 1)
-    late = [
-        late_chunk(plan, chunks_first + k, packs[k], (), late_total == 0) for k in range(2)
-    ]
+    packs, late = [None, None], [None, None]
+
+    def late_begin():
+        for k in range(2):
+            pack = normed["packs"][k]
+            packs[k] = pack.reshape(2, ring_size, local_features // ring_size, pack.shape[2])
+            late[k] = late_chunk(plan, chunks_first + k, packs[k], (), late_total == 0)
+
+    def back_to_tokens(ties):
+        hidden_grad = normed["hidden"]
+        qkv_grad = after(normed["qkv"], *ties)
+        ffn_sum = mixed[False, 0] + swap(mixed[False, 1], "col").astype(F32)
+        ffn_rows = my_rows(ffn_sum) + swap(their_rows(ffn_sum).astype(BF16), "row").astype(F32)
+        block_out = (my_rows(hidden) + ffn_rows).astype(BF16)
+        here = jnp.concatenate(
+            [halves(w, 1, col)[0] for w in (w_query, w_key, w_value)], axis=1
+        )
+        tokens_back = dot_nt(qkv_grad, here) + swap(
+            dot_nt(qkv_grad, there).astype(BF16), "col"
+        ).astype(F32)
+        tokens_back = my_rows(tokens_back) + swap(
+            their_rows(tokens_back).astype(BF16), "row"
+        ).astype(F32)
+        scale_attn = near[3]
+        tokens_f32 = tokens_in.astype(F32)
+        gain_attn_part = jnp.sum(tokens_back * tokens_f32 * scale_attn, axis=0)
+        scaled = tokens_back * norm_gain_attn
+        products = jnp.sum(scaled * tokens_f32, axis=1, keepdims=True)
+        mean = (products + swap(products, "col")) / D
+        tokens_grad = (
+            my_rows(hidden_grad) + scale_attn * scaled - tokens_f32 * scale_attn**3 * mean
+        ).astype(BF16)
+
+        gain_parts = jnp.concatenate([gain_attn_part[None], normed["gain"]], axis=0)
+        normed["gains"] = across_rings(gain_parts + swap(gain_parts, "row"))
+        normed["outs"] = (block_out, tokens_grad)
+
+    def gain_sums():
+        return normed["gains"]
+
     late_out = [[], []]
     late_done = 0
 
@@ -1218,7 +1282,7 @@
         owns = [across_rings(values[0]) for values in late]
         others = [swap(across_rings(values[1]), "col") for values in late]
         for k in range(2):
-            late[k] = join(col, owns[k], others[1 - k])
+            late[k] = late_join(col_ref, owns[k], others[1 - k], gain_sums())
             late_out[k].append(late[k])
 
     def late_finish(k, values):
@@ -1235,8 +1299,6 @@
     def place_chunks(wave, step, chunks, placed):
         return unpack(plan, experts + 2 * each * step, wave, chunks, shapes, placed)
 
-    if late_total == 0:
-        late_turn()
     steps = ring_size - 1
     late_got = None
     last = []
@@ -1246,21 +1308,26 @@
         if number == steps:
             came = got
             got = early
-        late_done += late_got is not None
         chunks = [None, None]
         for k in range(2):
             chunks[k] = after(got[k], *last) if last else got[k]
             got[k] = send(chunks[k], k)
             last = [chunks[k]]
-            if late_got is not None:
+        if number == 0:
+            early = [send(after(waves[1][k], *chunks), k) for k in range(2)]
+        if late_got is not None:
+            late_done += 1
+            for k in range(2):
                 late_finish(k, after(late_got[k], *last))
                 last = list(late[k]) if late_done == ring_size - 1 else [late[k]]
-        if number == 0:
-            early = [send(after(waves[1][k], *chunks), k) for k in range(2)]
-        if late_got is not None and late_done == ring_size - 1:
-            late_turn()
+            if late_done == ring_size - 1:
+                late_turn()
+        if number < len(later):
+            last = later[number](after(order, *last), last)
         late_got = None
-        if late_done < late_total:
+        if number + 1 >= len(later) and late_done < late_total:
+            if late_done == 0:
+                late_begin()
             late_got = [send(late[k], k) for k in range(2)]
         if number == steps:
             placed = place_chunks(0, steps, came, placed)
@@ -1268,10 +1335,16 @@
         placed = place_chunks(wave, step, [after(chunks[0], *last), chunks[1]], placed)
         last = placed[0:1]
         if number == 3:
-            qkv_grad = after(qkv_grad, *last)
+            back_to_tokens(last)
     if steps:
         placed = place_chunks(1, steps, [after(got[k], *last) for k in range(2)], placed)
         last = placed[0:1]
+    else:
+        for work in later:
+            work(order, ())
+        late_begin()
+        back_to_tokens(())
+        late_turn()
     while late_got is not None:
         late_done += 1
         for k in range(2):
@@ -1284,51 +1357,20 @@
             placed = place_chunks(wave, 0, waves[wave], placed)
     gate_grad, up_grad, down_grad = placed
     shapes = [w.shape for w in (w_shared_gate, w_shared_up, w_shared_down)]
-    shapes += [w.shape for w in (w_query, w_key, w_value, w_out)]
+    shapes += [w.shape for w in (w_query, w_key, w_value, w_out)] + [gains.shape]
     finals = unpack_late(plan, chunks_first + late_total, late_out, shapes)
     shared_gate_grad, shared_up_grad, shared_down_grad = finals[0:3]
-    query_grad, key_grad, value_grad, out_proj_grad = finals[3:7]
-
-    ffn_sum = mixed[False, 0] + swap(mixed[False, 1], "col").astype(F32)
-    ffn_rows = my_rows(ffn_sum) + swap(their_rows(ffn_sum).astype(BF16), "row").astype(F32)
-    block_out = (my_rows(hidden) + ffn_rows).astype(BF16)
-
-    here = jnp.concatenate(
-        [halves(w, 1, col)[0] for w in (w_query, w_key, w_value)], axis=1
-    )
-    tokens_back = dot_nt(qkv_grad, here) + swap(
-        dot_nt(qkv_grad, there).astype(BF16), "col"
-    ).astype(F32)
-    tokens_back = my_rows(tokens_back) + swap(
-        their_rows(tokens_back).astype(BF16), "row"
-    ).astype(F32)
-    scale_attn = near[3]
-    tokens_f32 = tokens_in.astype(F32)
-    gain_attn_part = jnp.sum(tokens_back * tokens_f32 * scale_attn, axis=0)
-    scaled = tokens_back * norm_gain_attn
-    products = jnp.sum(scaled * tokens_f32, axis=1, keepdims=True)
-    mean = (products + swap(products, "col")) / D
-    tokens_grad = (
-        my_rows(hidden_grad) + scale_attn * scaled - tokens_f32 * scale_attn**3 * mean
-    ).astype(BF16)
-
-    gain_parts = jnp.concatenate([gain_attn_part[None], gain_ffn_part], axis=0)
-    bit = 1
-    while bit < ring_size:
-        pairs = [(g + k, g + (k ^ bit)) for g in starts for k in range(ring_size)]
-        gain_parts = gain_parts + lax.ppermute(gain_parts, "dp", pairs)
-        bit *= 2
-    gain_parts = across_rings(gain_parts + swap(gain_parts, "row"))
+    query_grad, key_grad, value_grad, out_proj_grad, gain_grads = finals[3:8]
+
 
     return (
-        block_out,
-        tokens_grad,
-        gain_parts[0],
+        *normed["outs"],
+        gain_grads[0],
         query_grad,
         key_grad,
         value_grad,
         out_proj_grad,
-        gain_parts[1],
+        gain_grads[1],
         gate_grad,
         up_grad,
         down_grad,

time: 692 us -> 690 us (level)
    ppermute x3 -> x0, waiting for transfers between devices: 27.8 us -> none  [body(): gain_parts = gain_parts + lax.ppermute(gain_parts, 'dp', pairs)]
    ppermute x70, waiting for transfers between devices: 188 us -> 214 us  [send(): return lax.ppermute(values, ('dp', 'col'), routes_of[which])]
    unnamed x176 -> x172, local copies, waits for them, and re-layouts: 28.3 us -> 28.2 us
  transfers between devices with their start and end apart: 109 -> 106, of which waited for: 42 -> 38; matrix products, arithmetic and copies ran while one was open for 3% -> 3% of each run, Pallas kernels for 37% -> 37%
where the time goes in v9:
time: 690 us; the launch traced here: 680 us
  Pallas kernels  278 us (40%)
  waiting for transfers between devices  254 us (37%)
  starting transfers between devices  100 us (14%)
  local copies, waits for them, and re-layouts  30.6 us (4%)
  other arithmetic  9.72 us (1%)
    ppermute x70, waiting for transfers between devices, send(): return lax.ppermute(values, ('dp', 'col'), routes_of[which])  214 us
    ppermute x70, starting transfers between devices, send(): return lax.ppermute(values, ('dp', 'col'), routes_of[which])  79.1 us
    pallas_call x9, Pallas kernels, expert_grads(): pl.pallas_call(functools.partial(expert_kernel, shared, aliased, first),...  79.1 us
    pallas_call x16, Pallas kernels, unpack(): pl.pallas_call(functools.partial(unpack_kernel, aliased), grid_spec=pltpu...  40.8 us
    pallas_call x4, Pallas kernels, mix(): pl.pallas_call(functools.partial(mix_kernel, back, group), grid_spec=pltp...  39.4 us
    ppermute x33, waiting for transfers between devices, swap(): return lax.ppermute(values, axis, [(0, 1), (1, 0)])  37.8 us
    unnamed x172, local copies, waits for them, and re-layouts  28.2 us
    pallas_call x14, Pallas kernels, ring_sum(): pl.pallas_call(ring_sum_kernel, grid=(count, tiles), in_specs=[spec, spec...  21.9 us
  transfers between devices with their start and end apart: 106, of which 38 were waited for; matrix products, arithmetic and copies ran while one was open for 3% of the time, Pallas kernels for 37%

profile of v9, /device:TPU:0, one launch (start us, length us, event | category | flops | bytes accessed | tf_op | source)
XLA Modules:
  0.0 680.1 jit_solution(18303496320816200673)
XLA Ops:
  1.8 3.2 their_columns.1
  5.5 2.6 collective-permute-start
  8.3 4.9 collective-permute-done.2.gains_c_ref.refs_7_
  13.2 2.9 collective-permute-start.4
  17.9 4.5 project.2
  22.4 10.1 %collective-permute-done.4.refs_0_ = bf16[192,768]{1,0:T(8,128)(2,1)S(1)} collective-permute-done((bf16[192,768]{1,0:T(8,128)(2,1)}, bf16[192,768]{1,0:T(8,128)(2,1)S(1)}, u32[]{:S(2)}, u32[]{:S(2)}) %collective-permute-start.4) | collective-permute-done | bytes 294944 | tf_op jit(solution)/shard_map/ppermute | solution.py:49
  32.5 2.5 collective-permute-done.8.other_ref.refs_3_
  40.8 4.5 project.3
  47.5 2.5 collective-permute-start.9
  51.4 4.4 collective-permute-done.5.refs_1_
  58.3 6.2 attend.1.refs_4_.refs_5_
  70.0 9.0 %hidden_before.1 = (f32[1024,768]{1,0:T(8,128)}, f32[1024,768]{1,0:T(8,128)}) custom-call(s32[3]{0:T(128)} %copy-done.57, bf16[512,768]{1,0:T(8,128)(2,1)} %refs_0_.2, bf16[512,768]{1,0:T(8,128)(2,1)} %copy-done.76, bf16[512,768]{1,0:T(8,128)(2,1)} %collective-permute-done.own_ref.refs_2_, bf16[512,768]{1,0:T(8,128)(2,1)} %copy-done.77, ...), custom_call_target="tpu_custom_call" | custom-call | flops 2415919104 | bytes 12582912 | tf_op jit(solution)/shard_map/hidden_before/pallas_call | solution.py:399
  79.1 6.3 collective-permute-done.12.refs_2_
  88.8 9.4 %hidden_after.1 = (f32[1024,768]{1,0:T(8,128)}, bf16[1024,768]{1,0:T(8,128)(2,1)}, bf16[1024,768]{1,0:T(8,128)(2,1)}, f32[1024,1]{1,0:T(8,128)}) custom-call(s32[3]{0:T(128)} %copy-done.57, f32[1024,768]{1,0:T(8,128)} %get-tuple-element.258.refs_0_, f32[1024,768]{1,0:T(8,128)} %get-tuple-element.259.refs_1_, ...), custom_call_target="tpu_custom_call" | custom-call | tf_op jit(solution)/shard_map/hidden_after/pallas_call | solution.py:421
  101.6 9.3 %expert_grads.9 = (bf16[1,1536,384]{2,1,0:T(8,128)(2,1)S(1)}, bf16[1,1536,384]{2,1,0:T(8,128)(2,1)S(1)}, bf16[8,1024,512]{2,1,0:T(8,128)(2,1)}, bf16[8,1024,256]{2,1,0:T(8,128)(2,1)S(1)}) custom-call(s32[63]{0:T(128)S(1)} %fusion.14.order_ref.plan_ref, bf16[1024,768]{1,0:T(8,128)(2,1)S(1)} %copy-done.7, bf16[1024,768]{1,0:T(8,128)(2,1)S(1)} %copy-done.8, ...), custom_call_target="tpu_custom_call" | custom-call | tf_op jit(solution)/shard_map/expert_grads/pallas_call | solution.py:544
  112.5 8.9 %expert_grads.10 = (bf16[1,1536,384]{2,1,0:T(8,128)(2,1)S(1)}, bf16[1,1536,384]{2,1,0:T(8,128)(2,1)S(1)}, bf16[8,1024,512]{2,1,0:T(8,128)(2,1)}, bf16[8,1024,256]{2,1,0:T(8,128)(2,1)S(1)}) custom-call(s32[63]{0:T(128)S(1)} %fusion.14.order_ref.plan_ref, bf16[1024,768]{1,0:T(8,128)(2,1)S(1)} %copy-done.7, ...), custom_call_target="tpu_custom_call", output_to_operand_aliasing={{2}: (18, {}), {3}: (19, {})} | custom-call | tf_op jit(solution)/shard_map/expert_grads/pallas_call | solution.py:544
  121.8 8.9 %expert_grads.11 = (bf16[1,1536,384]{2,1,0:T(8,128)(2,1)S(1)}, bf16[1,1536,384]{2,1,0:T(8,128)(2,1)S(1)}, bf16[8,1024,512]{2,1,0:T(8,128)(2,1)}, bf16[8,1024,256]{2,1,0:T(8,128)(2,1)S(1)}) custom-call(s32[63]{0:T(128)S(1)} %fusion.14.order_ref.plan_ref, bf16[1024,768]{1,0:T(8,128)(2,1)S(1)} %copy-done.7, ...), custom_call_target="tpu_custom_call", output_to_operand_aliasing={{2}: (18, {}), {3}: (19, {})} | custom-call | tf_op jit(solution)/shard_map/expert_grads/pallas_call | solution.py:544
  131.0 2.4 collective-permute-start.20
  133.4 8.9 %expert_grads.12 = (bf16[1,1536,384]{2,1,0:T(8,128)(2,1)S(1)}, bf16[1,1536,384]{2,1,0:T(8,128)(2,1)S(1)}, bf16[8,1024,512]{2,1,0:T(8,128)(2,1)}, bf16[8,1024,256]{2,1,0:T(8,128)(2,1)S(1)}) custom-call(s32[63]{0:T(128)S(1)} %fusion.14.order_ref.plan_ref, bf16[1024,768]{1,0:T(8,128)(2,1)S(1)} %copy-done.7, ...), custom_call_target="tpu_custom_call", output_to_operand_aliasing={{2}: (18, {}), {3}: (19, {})} | custom-call | tf_op jit(solution)/shard_map/expert_grads/pallas_call | solution.py:544
  146.6 8.9 %expert_grads.13 = (bf16[1,1536,384]{2,1,0:T(8,128)(2,1)S(1)}, bf16[1,1536,384]{2,1,0:T(8,128)(2,1)S(1)}, bf16[8,1024,512]{2,1,0:T(8,128)(2,1)}, bf16[8,1024,256]{2,1,0:T(8,128)(2,1)S(1)}) custom-call(s32[63]{0:T(128)S(1)} %fusion.14.order_ref.plan_ref, bf16[1024,768]{1,0:T(8,128)(2,1)S(1)} %copy-done.7, ...), custom_call_target="tpu_custom_call", output_to_operand_aliasing={{2}: (18, {}), {3}: (19, {})} | custom-call | tf_op jit(solution)/shard_map/expert_grads/pallas_call | solution.py:544
  159.4 8.9 %expert_grads.14 = (bf16[1,1536,384]{2,1,0:T(8,128)(2,1)S(1)}, bf16[1,1536,384]{2,1,0:T(8,128)(2,1)S(1)}, bf16[8,1024,512]{2,1,0:T(8,128)(2,1)}, bf16[8,1024,256]{2,1,0:T(8,128)(2,1)S(1)}) custom-call(s32[63]{0:T(128)S(1)} %fusion.14.order_ref.plan_ref, bf16[1024,768]{1,0:T(8,128)(2,1)S(1)} %copy-done.7, ...), custom_call_target="tpu_custom_call", output_to_operand_aliasing={{2}: (18, {}), {3}: (19, {})} | custom-call | tf_op jit(solution)/shard_map/expert_grads/pallas_call | solution.py:544
  172.9 8.9 %expert_grads.15 = (bf16[1,1536,384]{2,1,0:T(8,128)(2,1)S(1)}, bf16[1,1536,384]{2,1,0:T(8,128)(2,1)S(1)}, bf16[8,1024,512]{2,1,0:T(8,128)(2,1)}, bf16[8,1024,256]{2,1,0:T(8,128)(2,1)S(1)}) custom-call(s32[63]{0:T(128)S(1)} %fusion.14.order_ref.plan_ref, bf16[1024,768]{1,0:T(8,128)(2,1)S(1)} %copy-done.7, ...), custom_call_target="tpu_custom_call", output_to_operand_aliasing={{2}: (18, {}), {3}: (19, {})} | custom-call | tf_op jit(solution)/shard_map/expert_grads/pallas_call | solution.py:544
  186.9 8.9 %expert_grads.16 = (bf16[1,1536,384]{2,1,0:T(8,128)(2,1)S(1)}, bf16[1,1536,384]{2,1,0:T(8,128)(2,1)S(1)}, bf16[8,1024,512]{2,1,0:T(8,128)(2,1)}, bf16[8,1024,256]{2,1,0:T(8,128)(2,1)S(1)}) custom-call(s32[63]{0:T(128)S(1)} %fusion.14.order_ref.plan_ref, bf16[1024,768]{1,0:T(8,128)(2,1)S(1)} %copy-done.7, ...), custom_call_target="tpu_custom_call", output_to_operand_aliasing={{2}: (18, {}), {3}: (19, {})} | custom-call | tf_op jit(solution)/shard_map/expert_grads/pallas_call | solution.py:544
  204.9 7.7 %expert_grads.17 = (bf16[1,1536,384]{2,1,0:T(8,128)(2,1)S(1)}, bf16[1,1536,384]{2,1,0:T(8,128)(2,1)S(1)}, bf16[1,1024,512]{2,1,0:T(8,128)(2,1)S(1)}, bf16[1,1024,256]{2,1,0:T(8,128)(2,1)S(1)}) custom-call(s32[63]{0:T(128)S(1)} %fusion.14.order_ref.plan_ref, bf16[1024,768]{1,0:T(8,128)(2,1)S(1)} %copy-done.7, bf16[1024,768]{1,0:T(8,128)(2,1)S(1)} %copy-done.9, ...), custom_call_target="tpu_custom_call" | custom-call | tf_op jit(solution)/shard_map/expert_grads/pallas_call | solution.py:544
  214.6 3.5 ring_sum.20
  219.4 12.4 %mix.4 = bf16[1024,768]{1,0:T(8,128)(2,1)S(1)} custom-call(s32[63]{0:T(128)S(1)} %fusion.14.order_ref.plan_ref, bf16[8,1024,512]{2,1,0:T(8,128)(2,1)} %get-tuple-element.299.refs_0_, bf16[1,1024,512]{2,1,0:T(8,128)(2,1)S(1)} %get-tuple-element.306.refs_1_, ...), custom_call_target="tpu_custom_call" | custom-call | tf_op jit(solution)/shard_map/mix/pallas_call | solution.py:615
  234.7 12.5 %mix.5.own_ref = f32[1024,768]{1,0:T(8,128)S(1)} custom-call(s32[63]{0:T(128)S(1)} %fusion.14.order_ref.plan_ref, bf16[8,1024,512]{2,1,0:T(8,128)(2,1)} %get-tuple-element.299.refs_0_, bf16[1,1024,512]{2,1,0:T(8,128)(2,1)S(1)} %get-tuple-element.306.refs_1_, bf16[16,768,256]{2,1,0:T(8,128)(2,1)} %refs_16_.1, bf16[16,768,256]{2,1,0:T(8,128)(2,1)} %refs_17_.1, ...), custom_call_target="tpu_custom_call" | custom-call | tf_op jit(solution)/shard_map/mix/pallas_call | solution.py:615
  247.3 2.7 ring_sum.22
  251.2 7.2 %mix.6 = bf16[1024,768]{1,0:T(8,128)(2,1)S(1)} custom-call(s32[63]{0:T(128)S(1)} %fusion.14.order_ref.plan_ref, bf16[8,1024,256]{2,1,0:T(8,128)(2,1)} %copy-done, bf16[1,1024,256]{2,1,0:T(8,128)(2,1)S(1)} %get-tuple-element.317.refs_1_, ...), custom_call_target="tpu_custom_call" | custom-call | tf_op jit(solution)/shard_map/mix/pallas_call | solution.py:615
  259.6 3.7 ring_sum.23
  267.3 7.3 %mix.7 = f32[1024,768]{1,0:T(8,128)S(1)} custom-call(s32[63]{0:T(128)S(1)} %fusion.14.order_ref.plan_ref, bf16[8,1024,256]{2,1,0:T(8,128)(2,1)} %copy-done, bf16[1,1024,256]{2,1,0:T(8,128)(2,1)S(1)} %get-tuple-element.317.refs_1_, bf16[16,256,768]{2,1,0:T(8,128)(2,1)} %refs_9_.19, bf16[16,256,768]{2,1,0:T(8,128)(2,1)} %refs_9_.19, ...), custom_call_target="tpu_custom_call" | custom-call | tf_op jit(solution)/shard_map/mix/pallas_call | solution.py:615
  274.6 2.8 ring_sum.24
  280.9 24.0 %collective-permute-done.38.came_ref = bf16[1,1536,384]{2,1,0:T(8,128)(2,1)S(1)} collective-permute-done((bf16[1,1536,384]{2,1,0:T(8,128)(2,1)S(1)}, bf16[1,1536,384]{2,1,0:T(8,128)(2,1)S(1)}, u32[]{:S(2)}, u32[]{:S(2)}) %collective-permute-start.38) | collective-permute-done | bytes 1179680 | tf_op jit(solution)/shard_map/ppermute | solution.py:1014
  307.7 4.5 norm_back.1
  315.8 5.3 norm_back_end.1
  325.4 11.3 %collective-permute-done.42.refs_0_ = bf16[1,768,384]{2,1,0:T(8,128)(2,1)S(1)} collective-permute-done((bf16[1,768,384]{2,1,0:T(8,128)(2,1)S(1)}, bf16[1,768,384]{2,1,0:T(8,128)(2,1)S(1)}, u32[]{:S(2)}, u32[]{:S(2)}) %collective-permute-start.42) | collective-permute-done | bytes 589856 | tf_op jit(solution)/shard_map/ppermute | solution.py:1014
  338.9 13.2 %attend_back.1.refs_4_ = bf16[1024,640]{1,0:T(8,128)(2,1)} custom-call(s32[3]{0:T(128)} %copy-done.57, bf16[512,640]{1,0:T(8,128)(2,1)} %get-tuple-element.250.own_ref, bf16[512,640]{1,0:T(8,128)(2,1)} %get-tuple-element.254.other_ref, bf16[1024,768]{1,0:T(8,128)(2,1)} %copy-done.17, bf16[1024,768]{1,0:T(8,128)(2,1)} %collective-permute-done.43.grad_c_ref.refs_7_, ...), custom_call_target="tpu_custom_call" | custom-call | tf_op jit(solution)/shard_map/attend_back/pallas_call | solution.py:167
  356.2 13.1 %late_grads.1 = (bf16[2,768,896]{2,1,0:T(8,128)(2,1)}, bf16[2,768,896]{2,1,0:T(8,128)(2,1)}) custom-call(s32[3]{0:T(128)} %copy-done.57, bf16[512,768]{1,0:T(8,128)(2,1)} %get-tuple-element.353.refs_0_, bf16[512,768]{1,0:T(8,128)(2,1)} %get-tuple-element.354.refs_1_, bf16[512,768]{1,0:T(8,128)(2,1)} %get-tuple-element.355.refs_2_, ...), custom_call_target="tpu_custom_call" | custom-call | tf_op jit(solution)/shard_map/late_grads/pallas_call | solution.py:218
  369.3 3.5 unpack.18
  378.7 17.7 %collective-permute-done.48.refs_0_ = bf16[2,96,896]{2,1,0:T(8,128)(2,1)S(1)} collective-permute-done((bf16[2,96,896]{2,1,0:T(8,128)(2,1)S(1)}, bf16[2,96,896]{2,1,0:T(8,128)(2,1)S(1)}, u32[]{:S(2)}, u32[]{:S(2)}) %collective-permute-start.48) | collective-permute-done | bytes 344096 | tf_op jit(solution)/shard_map/ppermute | solution.py:1014
  399.9 3.2 unpack.19
  405.2 2.6 convolution_convert_fusion
  410.6 8.9 %collective-permute-done.58.refs_0_ = bf16[1,768,384]{2,1,0:T(8,128)(2,1)S(1)} collective-permute-done((bf16[1,768,384]{2,1,0:T(8,128)(2,1)S(1)}, bf16[1,768,384]{2,1,0:T(8,128)(2,1)S(1)}, u32[]{:S(2)}, u32[]{:S(2)}) %collective-permute-start.58) | collective-permute-done | bytes 589856 | tf_op jit(solution)/shard_map/ppermute | solution.py:1014
  427.8 17.7 %collective-permute-done.63.refs_0_ = bf16[2,96,896]{2,1,0:T(8,128)(2,1)S(1)} collective-permute-done((bf16[2,96,896]{2,1,0:T(8,128)(2,1)S(1)}, bf16[2,96,896]{2,1,0:T(8,128)(2,1)S(1)}, u32[]{:S(2)}, u32[]{:S(2)}) %collective-permute-start.63) | collective-permute-done | bytes 344096 | tf_op jit(solution)/shard_map/ppermute | solution.py:1014
  458.4 8.2 %collective-permute-done.69.refs_0_ = bf16[2,96,896]{2,1,0:T(8,128)(2,1)} collective-permute-done((bf16[2,96,896]{2,1,0:T(8,128)(2,1)}, bf16[2,96,896]{2,1,0:T(8,128)(2,1)}, u32[]{:S(2)}, u32[]{:S(2)}) %collective-permute-start.69) | collective-permute-done | bytes 344096 | tf_op jit(solution)/shard_map/ppermute | solution.py:1014
  476.0 3.0 convert_add_fusion
  480.9 17.0 %collective-permute-done.73.refs_0_ = bf16[2,96,896]{2,1,0:T(8,128)(2,1)S(1)} collective-permute-done((bf16[2,96,896]{2,1,0:T(8,128)(2,1)S(1)}, bf16[2,96,896]{2,1,0:T(8,128)(2,1)S(1)}, u32[]{:S(2)}, u32[]{:S(2)}) %collective-permute-start.73) | collective-permute-done | bytes 344096 | tf_op jit(solution)/shard_map/ppermute | solution.py:1014
  500.7 3.3 unpack.24
  504.0 3.3 unpack.25
  512.9 16.6 %collective-permute-done.70.refs_0_ = bf16[2,96,896]{2,1,0:T(8,128)(2,1)S(1)} collective-permute-done((bf16[2,96,896]{2,1,0:T(8,128)(2,1)S(1)}, bf16[2,96,896]{2,1,0:T(8,128)(2,1)S(1)}, u32[]{:S(2)}, u32[]{:S(2)}) %collective-permute-start.70) | collective-permute-done | bytes 344096 | tf_op jit(solution)/shard_map/ppermute | solution.py:1014
  539.4 2.7 fusion.5
  542.1 14.1 %collective-permute-done.76.refs_0_ = bf16[2,96,896]{2,1,0:T(8,128)(2,1)S(1)} collective-permute-done((bf16[2,96,896]{2,1,0:T(8,128)(2,1)}, bf16[2,96,896]{2,1,0:T(8,128)(2,1)S(1)}, u32[]{:S(2)}, u32[]{:S(2)}) %collective-permute-start.76) | collective-permute-done | bytes 344096 | tf_op jit(solution)/shard_map/ppermute | solution.py:1014
  558.4 3.2 unpack.27
  566.4 19.3 %collective-permute-done.83.refs_1_ = bf16[208,896]{1,0:T(8,128)(2,1)S(1)} collective-permute-done((bf16[208,896]{1,0:T(8,128)(2,1)S(1)}, bf16[208,896]{1,0:T(8,128)(2,1)S(1)}, u32[]{:S(2)}, u32[]{:S(2)}) %collective-permute-start.83) | collective-permute-done | bytes 372768 | tf_op jit(solution)/shard_map/ppermute | solution.py:1014
  585.7 3.3 unpack.28
  589.2 2.4 collective-permute-start.92
  593.6 19.6 %collective-permute-done.86.refs_2_ = bf16[208,896]{1,0:T(8,128)(2,1)S(1)} collective-permute-done((bf16[208,896]{1,0:T(8,128)(2,1)S(1)}, bf16[208,896]{1,0:T(8,128)(2,1)S(1)}, u32[]{:S(2)}, u32[]{:S(2)}) %collective-permute-start.86) | collective-permute-done | bytes 372768 | tf_op jit(solution)/shard_map/ppermute | solution.py:1014
  619.8 4.9 collective-permute-done.91.refs_3_
  630.4 7.0 %collective-permute-done.96.refs_0_ = bf16[1,768,384]{2,1,0:T(8,128)(2,1)S(1)} collective-permute-done((bf16[1,768,384]{2,1,0:T(8,128)(2,1)S(1)}, bf16[1,768,384]{2,1,0:T(8,128)(2,1)S(1)}, u32[]{:S(2)}, u32[]{:S(2)}) %collective-permute-start.96) | collective-permute-done | bytes 589856 | tf_op jit(solution)/shard_map/ppermute | solution.py:1014
  639.5 5.2 collective-permute-done.95.refs_4_
  646.8 8.1 %collective-permute-done.99.refs_5_ = bf16[208,896]{1,0:T(8,128)(2,1)S(1)} collective-permute-done((bf16[208,896]{1,0:T(8,128)(2,1)S(1)}, bf16[208,896]{1,0:T(8,128)(2,1)S(1)}, u32[]{:S(2)}, u32[]{:S(2)}) %collective-permute-start.99) | collective-permute-done | bytes 372768 | tf_op jit(solution)/shard_map/ppermute | solution.py:1014
  658.1 6.0 collective-permute-done.100.refs_6_
  667.5 2.6 fusion.2
  673.4 5.7 unpack_late.1
  (421 shorter events, 190.4 us)
Async XLA Ops:
  0.6 34.5 %collective-permute-start.16 = (bf16[16,768,256]{2,1,0:T(8,128)(2,1)}, bf16[16,768,256]{2,1,0:T(8,128)(2,1)}, u32[]{:S(2)}, u32[]{:S(2)}) collective-permute-start(bf16[16,768,256]{2,1,0:T(8,128)(2,1)} %refs_16_.1), channel_id=1, source_target_pairs={{0,1},{1,0},{2,3},{3,2},{4,5},{5,4},{6,7},{7,6},{8,9},{9,8},{10,11... | collective-permute-start | bytes 18874376 | tf_op jit(solution)/shard_map/ppermute | solution.py:49
  5.5 27.1 %collective-permute-start = (bf16[512,768]{1,0:T(8,128)(2,1)S(1)}, bf16[512,768]{1,0:T(8,128)(2,1)}, u32[]{:S(2)}, u32[]{:S(2)}) collective-permute-start(bf16[512,768]{1,0:T(8,128)(2,1)S(1)} %copy-done.65), channel_id=1, source_target_pairs={{0,2},{2,0},{1,3},{3,1},{4,6},{6,4},{5,7},{7,5},{8,10},{10,8},{9,1... | collective-permute-start | bytes 2359304 | tf_op jit(solution)/shard_map/ppermute | solution.py:49
  13.2 19.3 %collective-permute-start.4 = (bf16[192,768]{1,0:T(8,128)(2,1)}, bf16[192,768]{1,0:T(8,128)(2,1)S(1)}, u32[]{:S(2)}, u32[]{:S(2)}) collective-permute-start(bf16[192,768]{1,0:T(8,128)(2,1)} %get-tuple-element.251), channel_id=1, source_target_pairs={{0,2},{2,0},{1,3},{3,1},{4,6},{6,4},{5,7},{7,5},{8,10},{10,8},{9,1... | collective-permute-start | bytes 884744 | tf_op jit(solution)/shard_map/ppermute | solution.py:49
  35.0 63.2 %collective-permute-start.18 = (bf16[16,256,768]{2,1,0:T(8,128)(2,1)}, bf16[16,256,768]{2,1,0:T(8,128)(2,1)}, u32[]{:S(2)}, u32[]{:S(2)}) collective-permute-start(bf16[16,256,768]{2,1,0:T(8,128)(2,1)} %refs_9_.19), channel_id=1, source_target_pairs={{0,1},{1,0},{2,3},{3,2},{4,5},{5,4},{6,7},{7,6},{8,9},{9,8},{10,11... | collective-permute-start | bytes 18874376 | tf_op jit(solution)/shard_map/ppermute | solution.py:49
  35.9 62.3 %collective-permute-start.17 = (bf16[16,768,256]{2,1,0:T(8,128)(2,1)}, bf16[16,768,256]{2,1,0:T(8,128)(2,1)}, u32[]{:S(2)}, u32[]{:S(2)}) collective-permute-start(bf16[16,768,256]{2,1,0:T(8,128)(2,1)} %refs_17_.1), channel_id=1, source_target_pairs={{0,1},{1,0},{2,3},{3,2},{4,5},{5,4},{6,7},{7,6},{8,9},{9,8},{10,11... | collective-permute-start | bytes 18874376 | tf_op jit(solution)/shard_map/ppermute | solution.py:49
  36.0 19.8 %collective-permute-start.5 = (bf16[512,768]{1,0:T(8,128)(2,1)S(1)}, bf16[512,768]{1,0:T(8,128)(2,1)S(1)}, u32[]{:S(2)}, u32[]{:S(2)}) collective-permute-start(bf16[512,768]{1,0:T(8,128)(2,1)S(1)} %copy-done.40), channel_id=1, source_target_pairs={{0,2},{2,0},{1,3},{3,1},{4,6},{6,4},{5,7},{7,5},{8,10},{10,8},{9,1... | collective-permute-start | bytes 2359304 | tf_op jit(solution)/shard_map/ppermute | solution.py:49
  65.1 20.3 %collective-permute-start.12 = (bf16[1024,384]{1,0:T(8,128)(2,1)}, bf16[1024,384]{1,0:T(8,128)(2,1)}, u32[]{:S(2)}, u32[]{:S(2)}) collective-permute-start(bf16[1024,384]{1,0:T(8,128)(2,1)} %attend.1.refs_4_.refs_5_), channel_id=1, source_target_pairs={{0,2},{2,0},{1,3},{3,1},{4,6},{6,4},{5,7},{7,5},{8,10},{10,8},{9,1... | collective-permute-start | bytes 2359304 | tf_op jit(solution)/shard_map/ppermute | solution.py:49
  67.7 30.4 %collective-permute-start.15 = (bf16[1024,768]{1,0:T(8,128)(2,1)S(1)}, bf16[1024,768]{1,0:T(8,128)(2,1)S(1)}, u32[]{:S(2)}, u32[]{:S(2)}) collective-permute-start(bf16[1024,768]{1,0:T(8,128)(2,1)S(1)} %join.3.refs_2_.out_grad_ref), channel_id=1, source_target_pairs={{0,1},{1,0},{2,3},{3,2},{4,5},{5,4},{6,7},{7,6},{8,9},{9,8},{10,11... | collective-permute-start | bytes 4718600 | tf_op jit(solution)/shard_map/ppermute | solution.py:49
  110.9 19.8 %collective-permute-start.19 = (bf16[1,1536,384]{2,1,0:T(8,128)(2,1)S(1)}, bf16[1,1536,384]{2,1,0:T(8,128)(2,1)S(1)}, u32[]{:S(2)}, u32[]{:S(2)}) collective-permute-start(bf16[1,1536,384]{2,1,0:T(8,128)(2,1)S(1)} %get-tuple-element.266), channel_id=1, source_target_pairs={{0,8},{8,16},{16,24},{24,28},{28,20},{20,12},{12,4},{4,0},{9,1},{1... | collective-permute-start | bytes 3538952 | tf_op jit(solution)/shard_map/ppermute | solution.py:1014
  121.3 23.2 %collective-permute-start.21 = (bf16[1,1536,384]{2,1,0:T(8,128)(2,1)S(1)}, bf16[1,1536,384]{2,1,0:T(8,128)(2,1)S(1)}, u32[]{:S(2)}, u32[]{:S(2)}) collective-permute-start(bf16[1,1536,384]{2,1,0:T(8,128)(2,1)S(1)} %get-tuple-element.276), channel_id=1, source_target_pairs={{8,0},{16,8},{24,16},{28,24},{20,28},{12,20},{4,12},{0,4},{1,9},{9... | collective-permute-start | bytes 3538952 | tf_op jit(solution)/shard_map/ppermute | solution.py:1014
  131.0 25.6 %collective-permute-start.20 = (bf16[1,1536,384]{2,1,0:T(8,128)(2,1)S(1)}, bf16[1,1536,384]{2,1,0:T(8,128)(2,1)S(1)}, u32[]{:S(2)}, u32[]{:S(2)}) collective-permute-start(bf16[1,1536,384]{2,1,0:T(8,128)(2,1)S(1)} %ring_sum.14), channel_id=1, source_target_pairs={{0,8},{8,16},{16,24},{24,28},{28,20},{20,12},{12,4},{4,0},{9,1},{1... | collective-permute-start | bytes 3538952 | tf_op jit(solution)/shard_map/ppermute | solution.py:1014
  144.9 25.5 %collective-permute-start.23 = (bf16[1,1536,384]{2,1,0:T(8,128)(2,1)S(1)}, bf16[1,1536,384]{2,1,0:T(8,128)(2,1)S(1)}, u32[]{:S(2)}, u32[]{:S(2)}) collective-permute-start(bf16[1,1536,384]{2,1,0:T(8,128)(2,1)S(1)} %ring_sum.15), channel_id=1, source_target_pairs={{8,0},{16,8},{24,16},{28,24},{20,28},{12,20},{4,12},{0,4},{1,9},{9... | collective-permute-start | bytes 3538952 | tf_op jit(solution)/shard_map/ppermute | solution.py:1014
  157.0 26.8 %collective-permute-start.22 = (bf16[1,1536,384]{2,1,0:T(8,128)(2,1)S(1)}, bf16[1,1536,384]{2,1,0:T(8,128)(2,1)S(1)}, u32[]{:S(2)}, u32[]{:S(2)}) collective-permute-start(bf16[1,1536,384]{2,1,0:T(8,128)(2,1)S(1)} %ring_sum.16), channel_id=1, source_target_pairs={{0,8},{8,16},{16,24},{24,28},{28,20},{20,12},{12,4},{4,0},{9,1},{1... | collective-permute-start | bytes 3538952 | tf_op jit(solution)/shard_map/ppermute | solution.py:1014
  172.1 25.7 %collective-permute-start.25 = (bf16[1,1536,384]{2,1,0:T(8,128)(2,1)}, bf16[1,1536,384]{2,1,0:T(8,128)(2,1)S(1)}, u32[]{:S(2)}, u32[]{:S(2)}) collective-permute-start(bf16[1,1536,384]{2,1,0:T(8,128)(2,1)} %ring_sum.17), channel_id=1, source_target_pairs={{8,0},{16,8},{24,16},{28,24},{20,28},{12,20},{4,12},{0,4},{1,9},{9... | collective-permute-start | bytes 3538952 | tf_op jit(solution)/shard_map/ppermute | solution.py:1014
  185.4 29.2 %collective-permute-start.24 = (bf16[1,1536,384]{2,1,0:T(8,128)(2,1)}, bf16[1,1536,384]{2,1,0:T(8,128)(2,1)}, u32[]{:S(2)}, u32[]{:S(2)}) collective-permute-start(bf16[1,1536,384]{2,1,0:T(8,128)(2,1)} %ring_sum.18), channel_id=1, source_target_pairs={{0,8},{8,16},{16,24},{24,28},{28,20},{20,12},{12,4},{4,0},{9,1},{1... | collective-permute-start | bytes 3538952 | tf_op jit(solution)/shard_map/ppermute | solution.py:1014
  199.6 32.3 %collective-permute-start.30 = (bf16[1,1536,384]{2,1,0:T(8,128)(2,1)}, bf16[1,1536,384]{2,1,0:T(8,128)(2,1)S(1)}, u32[]{:S(2)}, u32[]{:S(2)}) collective-permute-start(bf16[1,1536,384]{2,1,0:T(8,128)(2,1)} %ring_sum.19), channel_id=1, source_target_pairs={{8,0},{16,8},{24,16},{28,24},{20,28},{12,20},{4,12},{0,4},{1,9},{9... | collective-permute-start | bytes 3538952 | tf_op jit(solution)/shard_map/ppermute | solution.py:1014
  218.1 29.1 %collective-permute-start.29 = (bf16[1,1536,384]{2,1,0:T(8,128)(2,1)}, bf16[1,1536,384]{2,1,0:T(8,128)(2,1)}, u32[]{:S(2)}, u32[]{:S(2)}) collective-permute-start(bf16[1,1536,384]{2,1,0:T(8,128)(2,1)} %ring_sum.20), channel_id=1, source_target_pairs={{0,8},{8,16},{16,24},{24,28},{28,20},{20,12},{12,4},{4,0},{9,1},{1... | collective-permute-start | bytes 3538952 | tf_op jit(solution)/shard_map/ppermute | solution.py:1014
  233.6 26.1 %collective-permute-start.31 = (bf16[1,1536,384]{2,1,0:T(8,128)(2,1)}, bf16[1,1536,384]{2,1,0:T(8,128)(2,1)}, u32[]{:S(2)}, u32[]{:S(2)}) collective-permute-start(bf16[1,1536,384]{2,1,0:T(8,128)(2,1)} %ring_sum.21), channel_id=1, source_target_pairs={{8,0},{16,8},{24,16},{28,24},{20,28},{12,20},{4,12},{0,4},{1,9},{9... | collective-permute-start | bytes 3538952 | tf_op jit(solution)/shard_map/ppermute | solution.py:1014
  234.7 29.4 %collective-permute-start.36 = (bf16[1024,768]{1,0:T(8,128)(2,1)S(1)}, bf16[1024,768]{1,0:T(8,128)(2,1)S(1)}, u32[]{:S(2)}, u32[]{:S(2)}) collective-permute-start(bf16[1024,768]{1,0:T(8,128)(2,1)S(1)} %mix.4), channel_id=1, source_target_pairs={{0,1},{1,0},{2,3},{3,2},{4,5},{5,4},{6,7},{7,6},{8,9},{9,8},{10,11... | collective-permute-start | bytes 4718600 | tf_op jit(solution)/shard_map/ppermute | solution.py:49
  249.9 24.7 %collective-permute-start.35 = (bf16[1,1536,384]{2,1,0:T(8,128)(2,1)S(1)}, bf16[1,1536,384]{2,1,0:T(8,128)(2,1)}, u32[]{:S(2)}, u32[]{:S(2)}) collective-permute-start(bf16[1,1536,384]{2,1,0:T(8,128)(2,1)S(1)} %ring_sum.22), channel_id=1, source_target_pairs={{0,8},{8,16},{16,24},{24,28},{28,20},{20,12},{12,4},{4,0},{9,1},{1... | collective-permute-start | bytes 3538952 | tf_op jit(solution)/shard_map/ppermute | solution.py:1014
  266.2 41.4 %collective-permute-start.39 = (bf16[1024,768]{1,0:T(8,128)(2,1)S(1)}, bf16[1024,768]{1,0:T(8,128)(2,1)S(1)}, u32[]{:S(2)}, u32[]{:S(2)}) collective-permute-start(bf16[1024,768]{1,0:T(8,128)(2,1)S(1)} %get-tuple-element.321), channel_id=1, source_target_pairs={{0,2},{2,0},{1,3},{3,1},{4,6},{6,4},{5,7},{7,5},{8,10},{10,8},{9,1... | collective-permute-start | bytes 4718600 | tf_op jit(solution)/shard_map/ppermute | solution.py:49
  277.5 27.4 %collective-permute-start.38 = (bf16[1,1536,384]{2,1,0:T(8,128)(2,1)S(1)}, bf16[1,1536,384]{2,1,0:T(8,128)(2,1)S(1)}, u32[]{:S(2)}, u32[]{:S(2)}) collective-permute-start(bf16[1,1536,384]{2,1,0:T(8,128)(2,1)S(1)} %ring_sum.24), channel_id=1, source_target_pairs={{0,8},{8,16},{16,24},{24,28},{28,20},{20,12},{12,4},{4,0},{9,1},{1... | collective-permute-start | bytes 3538952 | tf_op jit(solution)/shard_map/ppermute | solution.py:1014
  280.1 26.2 %collective-permute-start.37 = (bf16[1,1536,384]{2,1,0:T(8,128)(2,1)S(1)}, bf16[1,1536,384]{2,1,0:T(8,128)(2,1)S(1)}, u32[]{:S(2)}, u32[]{:S(2)}) collective-permute-start(bf16[1,1536,384]{2,1,0:T(8,128)(2,1)S(1)} %ring_sum.25), channel_id=1, source_target_pairs={{8,0},{16,8},{24,16},{28,24},{20,28},{12,20},{4,12},{0,4},{1,9},{9... | collective-permute-start | bytes 3538952 | tf_op jit(solution)/shard_map/ppermute | solution.py:1014
  354.2 18.7 %collective-permute-start.45 = (bf16[1,768,384]{2,1,0:T(8,128)(2,1)}, bf16[1,768,384]{2,1,0:T(8,128)(2,1)S(1)}, u32[]{:S(2)}, u32[]{:S(2)}) collective-permute-start(bf16[1,768,384]{2,1,0:T(8,128)(2,1)} %collective-permute-done.44.refs_0_), channel_id=1, source_target_pairs={{0,8},{8,16},{16,24},{24,28},{28,20},{20,12},{12,4},{4,0},{9,1},{1... | collective-permute-start | bytes 1769480 | tf_op jit(solution)/shard_map/ppermute | solution.py:1014
  356.1 18.8 %collective-permute-start.49 = (bf16[1,768,384]{2,1,0:T(8,128)(2,1)}, bf16[1,768,384]{2,1,0:T(8,128)(2,1)}, u32[]{:S(2)}, u32[]{:S(2)}) collective-permute-start(bf16[1,768,384]{2,1,0:T(8,128)(2,1)} %collective-permute-done.46.refs_1_), channel_id=1, source_target_pairs={{8,0},{16,8},{24,16},{28,24},{20,28},{12,20},{4,12},{0,4},{1,9},{9... | collective-permute-start | bytes 1769480 | tf_op jit(solution)/shard_map/ppermute | solution.py:1014
  372.9 30.2 %collective-permute-start.55 = (bf16[1,768,384]{2,1,0:T(8,128)(2,1)S(1)}, bf16[1,768,384]{2,1,0:T(8,128)(2,1)S(1)}, u32[]{:S(2)}, u32[]{:S(2)}) collective-permute-start(bf16[1,768,384]{2,1,0:T(8,128)(2,1)S(1)} %collective-permute-done.45.refs_0_), channel_id=1, source_target_pairs={{0,8},{8,16},{16,24},{24,28},{28,20},{20,12},{12,4},{4,0},{9,1},{1... | collective-permute-start | bytes 1769480 | tf_op jit(solution)/shard_map/ppermute | solution.py:1014
  374.9 28.5 %collective-permute-start.54 = (bf16[1,768,384]{2,1,0:T(8,128)(2,1)}, bf16[1,768,384]{2,1,0:T(8,128)(2,1)S(1)}, u32[]{:S(2)}, u32[]{:S(2)}) collective-permute-start(bf16[1,768,384]{2,1,0:T(8,128)(2,1)} %collective-permute-done.49.refs_1_), channel_id=1, source_target_pairs={{8,0},{16,8},{24,16},{28,24},{20,28},{12,20},{4,12},{0,4},{1,9},{9... | collective-permute-start | bytes 1769480 | tf_op jit(solution)/shard_map/ppermute | solution.py:1014
  375.9 20.4 %collective-permute-start.48 = (bf16[2,96,896]{2,1,0:T(8,128)(2,1)S(1)}, bf16[2,96,896]{2,1,0:T(8,128)(2,1)S(1)}, u32[]{:S(2)}, u32[]{:S(2)}) collective-permute-start(bf16[2,96,896]{2,1,0:T(8,128)(2,1)S(1)} %late_chunk.17), channel_id=1, source_target_pairs={{0,8},{8,16},{16,24},{24,28},{28,20},{20,12},{12,4},{4,0},{9,1},{1... | collective-permute-start | bytes 1032200 | tf_op jit(solution)/shard_map/ppermute | solution.py:1014
  378.2 19.2 %collective-permute-start.47 = (bf16[2,96,896]{2,1,0:T(8,128)(2,1)S(1)}, bf16[2,96,896]{2,1,0:T(8,128)(2,1)S(1)}, u32[]{:S(2)}, u32[]{:S(2)}) collective-permute-start(bf16[2,96,896]{2,1,0:T(8,128)(2,1)S(1)} %late_chunk.16), channel_id=1, source_target_pairs={{8,0},{16,8},{24,16},{28,24},{20,28},{12,20},{4,12},{0,4},{1,9},{9... | collective-permute-start | bytes 1032200 | tf_op jit(solution)/shard_map/ppermute | solution.py:1014
  403.4 18.8 %collective-permute-start.57 = (bf16[1,768,384]{2,1,0:T(8,128)(2,1)S(1)}, bf16[1,768,384]{2,1,0:T(8,128)(2,1)S(1)}, u32[]{:S(2)}, u32[]{:S(2)}) collective-permute-start(bf16[1,768,384]{2,1,0:T(8,128)(2,1)S(1)} %collective-permute-done.54.refs_1_), channel_id=1, source_target_pairs={{8,0},{16,8},{24,16},{28,24},{20,28},{12,20},{4,12},{0,4},{1,9},{9... | collective-permute-start | bytes 1769480 | tf_op jit(solution)/shard_map/ppermute | solution.py:1014
  407.8 64.6 %collective-permute-start.50 = (bf16[1024,768]{1,0:T(8,128)(2,1)}, bf16[1024,768]{1,0:T(8,128)(2,1)}, u32[]{:S(2)}, u32[]{:S(2)}) collective-permute-start(bf16[1024,768]{1,0:T(8,128)(2,1)} %convolution_convert_fusion), channel_id=1, source_target_pairs={{0,1},{1,0},{2,3},{3,2},{4,5},{5,4},{6,7},{7,6},{8,9},{9,8},{10,11... | collective-permute-start | bytes 4718600 | tf_op jit(solution)/shard_map/ppermute | solution.py:49
  422.3 23.5 %collective-permute-start.61 = (bf16[1,768,384]{2,1,0:T(8,128)(2,1)S(1)}, bf16[1,768,384]{2,1,0:T(8,128)(2,1)S(1)}, u32[]{:S(2)}, u32[]{:S(2)}) collective-permute-start(bf16[1,768,384]{2,1,0:T(8,128)(2,1)S(1)} %collective-permute-done.57.refs_1_), channel_id=1, source_target_pairs={{8,0},{16,8},{24,16},{28,24},{20,28},{12,20},{4,12},{0,4},{1,9},{9... | collective-permute-start | bytes 1769480 | tf_op jit(solution)/shard_map/ppermute | solution.py:1014
  423.7 25.2 %collective-permute-start.62 = (bf16[1,768,384]{2,1,0:T(8,128)(2,1)S(1)}, bf16[1,768,384]{2,1,0:T(8,128)(2,1)S(1)}, u32[]{:S(2)}, u32[]{:S(2)}) collective-permute-start(bf16[1,768,384]{2,1,0:T(8,128)(2,1)S(1)} %collective-permute-done.58.refs_0_), channel_id=1, source_target_pairs={{0,8},{8,16},{16,24},{24,28},{28,20},{20,12},{12,4},{4,0},{9,1},{1... | collective-permute-start | bytes 1769480 | tf_op jit(solution)/shard_map/ppermute | solution.py:1014
  424.3 21.2 %collective-permute-start.63 = (bf16[2,96,896]{2,1,0:T(8,128)(2,1)S(1)}, bf16[2,96,896]{2,1,0:T(8,128)(2,1)S(1)}, u32[]{:S(2)}, u32[]{:S(2)}) collective-permute-start(bf16[2,96,896]{2,1,0:T(8,128)(2,1)S(1)} %late_chunk.21), channel_id=1, source_target_pairs={{8,0},{16,8},{24,16},{28,24},{20,28},{12,20},{4,12},{0,4},{1,9},{9... | collective-permute-start | bytes 1032200 | tf_op jit(solution)/shard_map/ppermute | solution.py:1014
  427.2 27.7 %collective-permute-start.60 = (bf16[2,96,896]{2,1,0:T(8,128)(2,1)}, bf16[2,96,896]{2,1,0:T(8,128)(2,1)}, u32[]{:S(2)}, u32[]{:S(2)}) collective-permute-start(bf16[2,96,896]{2,1,0:T(8,128)(2,1)} %late_chunk.22), channel_id=1, source_target_pairs={{0,8},{8,16},{16,24},{24,28},{28,20},{20,12},{12,4},{4,0},{9,1},{1... | collective-permute-start | bytes 1032200 | tf_op jit(solution)/shard_map/ppermute | solution.py:1014
  445.5 24.9 %collective-permute-start.68 = (bf16[1,768,384]{2,1,0:T(8,128)(2,1)}, bf16[1,768,384]{2,1,0:T(8,128)(2,1)}, u32[]{:S(2)}, u32[]{:S(2)}) collective-permute-start(bf16[1,768,384]{2,1,0:T(8,128)(2,1)} %collective-permute-done.67.refs_0_), channel_id=1, source_target_pairs={{0,8},{8,16},{16,24},{24,28},{28,20},{20,12},{12,4},{4,0},{9,1},{1... | collective-permute-start | bytes 1769480 | tf_op jit(solution)/shard_map/ppermute | solution.py:1014
  445.8 26.6 %collective-permute-start.66 = (bf16[1,768,384]{2,1,0:T(8,128)(2,1)}, bf16[1,768,384]{2,1,0:T(8,128)(2,1)}, u32[]{:S(2)}, u32[]{:S(2)}) collective-permute-start(bf16[1,768,384]{2,1,0:T(8,128)(2,1)} %collective-permute-done.65.refs_1_), channel_id=1, source_target_pairs={{8,0},{16,8},{24,16},{28,24},{20,28},{12,20},{4,12},{0,4},{1,9},{9... | collective-permute-start | bytes 1769480 | tf_op jit(solution)/shard_map/ppermute | solution.py:1014
  466.6 31.9 %collective-permute-start.74 = (bf16[1,768,384]{2,1,0:T(8,128)(2,1)S(1)}, bf16[1,768,384]{2,1,0:T(8,128)(2,1)S(1)}, u32[]{:S(2)}, u32[]{:S(2)}) collective-permute-start(bf16[1,768,384]{2,1,0:T(8,128)(2,1)S(1)} %collective-permute-done.62.refs_0_), channel_id=1, source_target_pairs={{0,8},{8,16},{16,24},{24,28},{28,20},{20,12},{12,4},{4,0},{9,1},{1... | collective-permute-start | bytes 1769480 | tf_op jit(solution)/shard_map/ppermute | solution.py:1014
  470.4 28.2 %collective-permute-start.75 = (bf16[1,768,384]{2,1,0:T(8,128)(2,1)S(1)}, bf16[1,768,384]{2,1,0:T(8,128)(2,1)S(1)}, u32[]{:S(2)}, u32[]{:S(2)}) collective-permute-start(bf16[1,768,384]{2,1,0:T(8,128)(2,1)S(1)} %copy-done.42), channel_id=1, source_target_pairs={{8,0},{16,8},{24,16},{28,24},{20,28},{12,20},{4,12},{0,4},{1,9},{9... | collective-permute-start | bytes 1769480 | tf_op jit(solution)/shard_map/ppermute | solution.py:1014
  472.4 34.9 %collective-permute-start.72 = (bf16[1,768,384]{2,1,0:T(8,128)(2,1)}, bf16[1,768,384]{2,1,0:T(8,128)(2,1)S(1)}, u32[]{:S(2)}, u32[]{:S(2)}) collective-permute-start(bf16[1,768,384]{2,1,0:T(8,128)(2,1)} %collective-permute-done.68.refs_0_), channel_id=1, source_target_pairs={{0,8},{8,16},{16,24},{24,28},{28,20},{20,12},{12,4},{4,0},{9,1},{1... | collective-permute-start | bytes 1769480 | tf_op jit(solution)/shard_map/ppermute | solution.py:1014
  472.4 35.7 %collective-permute-start.71 = (bf16[1,768,384]{2,1,0:T(8,128)(2,1)}, bf16[1,768,384]{2,1,0:T(8,128)(2,1)S(1)}, u32[]{:S(2)}, u32[]{:S(2)}) collective-permute-start(bf16[1,768,384]{2,1,0:T(8,128)(2,1)} %collective-permute-done.66.refs_1_), channel_id=1, source_target_pairs={{8,0},{16,8},{24,16},{28,24},{20,28},{12,20},{4,12},{0,4},{1,9},{9... | collective-permute-start | bytes 1769480 | tf_op jit(solution)/shard_map/ppermute | solution.py:1014
  474.5 23.4 %collective-permute-start.73 = (bf16[2,96,896]{2,1,0:T(8,128)(2,1)S(1)}, bf16[2,96,896]{2,1,0:T(8,128)(2,1)S(1)}, u32[]{:S(2)}, u32[]{:S(2)}) collective-permute-start(bf16[2,96,896]{2,1,0:T(8,128)(2,1)S(1)} %late_chunk.25), channel_id=1, source_target_pairs={{8,0},{16,8},{24,16},{28,24},{20,28},{12,20},{4,12},{0,4},{1,9},{9... | collective-permute-start | bytes 1032200 | tf_op jit(solution)/shard_map/ppermute | solution.py:1014
  507.3 26.5 %collective-permute-start.78 = (bf16[1,768,384]{2,1,0:T(8,128)(2,1)S(1)}, bf16[1,768,384]{2,1,0:T(8,128)(2,1)S(1)}, u32[]{:S(2)}, u32[]{:S(2)}) collective-permute-start(bf16[1,768,384]{2,1,0:T(8,128)(2,1)S(1)} %collective-permute-done.72.refs_0_), channel_id=1, source_target_pairs={{0,8},{8,16},{16,24},{24,28},{28,20},{20,12},{12,4},{4,0},{9,1},{1... | collective-permute-start | bytes 1769480 | tf_op jit(solution)/shard_map/ppermute | solution.py:1014
  508.1 26.1 %collective-permute-start.77 = (bf16[1,768,384]{2,1,0:T(8,128)(2,1)S(1)}, bf16[1,768,384]{2,1,0:T(8,128)(2,1)}, u32[]{:S(2)}, u32[]{:S(2)}) collective-permute-start(bf16[1,768,384]{2,1,0:T(8,128)(2,1)S(1)} %collective-permute-done.71.refs_1_), channel_id=1, source_target_pairs={{8,0},{16,8},{24,16},{28,24},{20,28},{12,20},{4,12},{0,4},{1,9},{9... | collective-permute-start | bytes 1769480 | tf_op jit(solution)/shard_map/ppermute | solution.py:1014
  510.3 27.4 %collective-permute-start.51 = (bf16[512,768]{1,0:T(8,128)(2,1)}, bf16[512,768]{1,0:T(8,128)(2,1)}, u32[]{:S(2)}, u32[]{:S(2)}) collective-permute-start(bf16[512,768]{1,0:T(8,128)(2,1)} %dynamic-slice_convert_fusion), channel_id=1, source_target_pairs={{0,2},{2,0},{1,3},{3,1},{4,6},{6,4},{5,7},{7,5},{8,10},{10,8},{9,1... | collective-permute-start | bytes 2359304 | tf_op jit(solution)/shard_map/ppermute | solution.py:49
  511.8 19.2 %collective-permute-start.79 = (bf16[2,96,896]{2,1,0:T(8,128)(2,1)S(1)}, bf16[2,96,896]{2,1,0:T(8,128)(2,1)S(1)}, u32[]{:S(2)}, u32[]{:S(2)}) collective-permute-start(bf16[2,96,896]{2,1,0:T(8,128)(2,1)S(1)} %late_chunk.27), channel_id=1, source_target_pairs={{8,0},{16,8},{24,16},{28,24},{20,28},{12,20},{4,12},{0,4},{1,9},{9... | collective-permute-start | bytes 1032200 | tf_op jit(solution)/shard_map/ppermute | solution.py:1014
  533.9 27.7 %collective-permute-start.85 = (bf16[1,768,384]{2,1,0:T(8,128)(2,1)S(1)}, bf16[1,768,384]{2,1,0:T(8,128)(2,1)}, u32[]{:S(2)}, u32[]{:S(2)}) collective-permute-start(bf16[1,768,384]{2,1,0:T(8,128)(2,1)S(1)} %collective-permute-done.78.refs_0_), channel_id=1, source_target_pairs={{0,8},{8,16},{16,24},{24,28},{28,20},{20,12},{12,4},{4,0},{9,1},{1... | collective-permute-start | bytes 1769480 | tf_op jit(solution)/shard_map/ppermute | solution.py:1014
  534.2 27.8 %collective-permute-start.84 = (bf16[1,768,384]{2,1,0:T(8,128)(2,1)}, bf16[1,768,384]{2,1,0:T(8,128)(2,1)}, u32[]{:S(2)}, u32[]{:S(2)}) collective-permute-start(bf16[1,768,384]{2,1,0:T(8,128)(2,1)} %collective-permute-done.77.refs_1_), channel_id=1, source_target_pairs={{8,0},{16,8},{24,16},{28,24},{20,28},{12,20},{4,12},{0,4},{1,9},{9... | collective-permute-start | bytes 1769480 | tf_op jit(solution)/shard_map/ppermute | solution.py:1014
  536.1 83.2 %collective-permute-start.32 = (bf16[1024,768]{1,0:T(8,128)(2,1)}, bf16[1024,768]{1,0:T(8,128)(2,1)S(1)}, u32[]{:S(2)}, u32[]{:S(2)}) collective-permute-start(bf16[1024,768]{1,0:T(8,128)(2,1)} %copy-done.23), channel_id=1, source_target_pairs={{0,1},{1,0},{2,3},{3,2},{4,5},{5,4},{6,7},{7,6},{8,9},{9,8},{10,11... | collective-permute-start | bytes 4718600 | tf_op jit(solution)/shard_map/ppermute | solution.py:49
  537.3 19.0 %collective-permute-start.76 = (bf16[2,96,896]{2,1,0:T(8,128)(2,1)}, bf16[2,96,896]{2,1,0:T(8,128)(2,1)S(1)}, u32[]{:S(2)}, u32[]{:S(2)}) collective-permute-start(bf16[2,96,896]{2,1,0:T(8,128)(2,1)} %copy-done.48), channel_id=1, source_target_pairs={{0,8},{8,16},{16,24},{24,28},{28,20},{20,12},{12,4},{4,0},{9,1},{1... | collective-permute-start | bytes 1032200 | tf_op jit(solution)/shard_map/ppermute | solution.py:1014
  537.7 19.9 %collective-permute-start.80 = (bf16[2,96,896]{2,1,0:T(8,128)(2,1)}, bf16[2,96,896]{2,1,0:T(8,128)(2,1)S(1)}, u32[]{:S(2)}, u32[]{:S(2)}) collective-permute-start(bf16[2,96,896]{2,1,0:T(8,128)(2,1)} %copy-done.47), channel_id=1, source_target_pairs={{8,0},{16,8},{24,16},{28,24},{20,28},{12,20},{4,12},{0,4},{1,9},{9... | collective-permute-start | bytes 1032200 | tf_op jit(solution)/shard_map/ppermute | solution.py:1014
  562.0 27.0 %collective-permute-start.88 = (bf16[1,768,384]{2,1,0:T(8,128)(2,1)}, bf16[1,768,384]{2,1,0:T(8,128)(2,1)S(1)}, u32[]{:S(2)}, u32[]{:S(2)}) collective-permute-start(bf16[1,768,384]{2,1,0:T(8,128)(2,1)} %collective-permute-done.85.refs_0_), channel_id=1, source_target_pairs={{0,8},{8,16},{16,24},{24,28},{28,20},{20,12},{12,4},{4,0},{9,1},{1... | collective-permute-start | bytes 1769480 | tf_op jit(solution)/shard_map/ppermute | solution.py:1014
  562.3 26.9 %collective-permute-start.87 = (bf16[1,768,384]{2,1,0:T(8,128)(2,1)}, bf16[1,768,384]{2,1,0:T(8,128)(2,1)S(1)}, u32[]{:S(2)}, u32[]{:S(2)}) collective-permute-start(bf16[1,768,384]{2,1,0:T(8,128)(2,1)} %collective-permute-done.84.refs_1_), channel_id=1, source_target_pairs={{8,0},{16,8},{24,16},{28,24},{20,28},{12,20},{4,12},{0,4},{1,9},{9... | collective-permute-start | bytes 1769480 | tf_op jit(solution)/shard_map/ppermute | solution.py:1014
  564.2 21.4 %collective-permute-start.83 = (bf16[208,896]{1,0:T(8,128)(2,1)S(1)}, bf16[208,896]{1,0:T(8,128)(2,1)S(1)}, u32[]{:S(2)}, u32[]{:S(2)}) collective-permute-start(bf16[208,896]{1,0:T(8,128)(2,1)S(1)} %late_join.2.refs_0_), channel_id=1, source_target_pairs={{0,8},{8,16},{16,24},{24,28},{28,20},{20,12},{12,4},{4,0},{9,1},{1... | collective-permute-start | bytes 1118216 | tf_op jit(solution)/shard_map/ppermute | solution.py:1014
  564.5 21.2 %collective-permute-start.90 = (bf16[208,896]{1,0:T(8,128)(2,1)S(1)}, bf16[208,896]{1,0:T(8,128)(2,1)S(1)}, u32[]{:S(2)}, u32[]{:S(2)}) collective-permute-start(bf16[208,896]{1,0:T(8,128)(2,1)S(1)} %late_join.3.refs_8_), channel_id=1, source_target_pairs={{8,0},{16,8},{24,16},{28,24},{20,28},{12,20},{4,12},{0,4},{1,9},{9... | collective-permute-start | bytes 1118216 | tf_op jit(solution)/shard_map/ppermute | solution.py:1014
  589.0 28.3 %collective-permute-start.93 = (bf16[1,768,384]{2,1,0:T(8,128)(2,1)S(1)}, bf16[1,768,384]{2,1,0:T(8,128)(2,1)S(1)}, u32[]{:S(2)}, u32[]{:S(2)}) collective-permute-start(bf16[1,768,384]{2,1,0:T(8,128)(2,1)S(1)} %collective-permute-done.88.refs_0_), channel_id=1, source_target_pairs={{0,8},{8,16},{16,24},{24,28},{28,20},{20,12},{12,4},{4,0},{9,1},{1... | collective-permute-start | bytes 1769480 | tf_op jit(solution)/shard_map/ppermute | solution.py:1014
  589.2 28.1 %collective-permute-start.92 = (bf16[1,768,384]{2,1,0:T(8,128)(2,1)S(1)}, bf16[1,768,384]{2,1,0:T(8,128)(2,1)S(1)}, u32[]{:S(2)}, u32[]{:S(2)}) collective-permute-start(bf16[1,768,384]{2,1,0:T(8,128)(2,1)S(1)} %collective-permute-done.87.refs_1_), channel_id=1, source_target_pairs={{8,0},{16,8},{24,16},{28,24},{20,28},{12,20},{4,12},{0,4},{1,9},{9... | collective-permute-start | bytes 1769480 | tf_op jit(solution)/shard_map/ppermute | solution.py:1014
  591.6 21.6 %collective-permute-start.86 = (bf16[208,896]{1,0:T(8,128)(2,1)S(1)}, bf16[208,896]{1,0:T(8,128)(2,1)S(1)}, u32[]{:S(2)}, u32[]{:S(2)}) collective-permute-start(bf16[208,896]{1,0:T(8,128)(2,1)S(1)} %collective-permute-done.83.refs_1_), channel_id=1, source_target_pairs={{0,8},{8,16},{16,24},{24,28},{28,20},{20,12},{12,4},{4,0},{9,1},{1... | collective-permute-start | bytes 1118216 | tf_op jit(solution)/shard_map/ppermute | solution.py:1014
  591.6 21.6 %collective-permute-start.94 = (bf16[208,896]{1,0:T(8,128)(2,1)S(1)}, bf16[208,896]{1,0:T(8,128)(2,1)S(1)}, u32[]{:S(2)}, u32[]{:S(2)}) collective-permute-start(bf16[208,896]{1,0:T(8,128)(2,1)S(1)} %collective-permute-done.90.refs_9_), channel_id=1, source_target_pairs={{8,0},{16,8},{24,16},{28,24},{20,28},{12,20},{4,12},{0,4},{1,9},{9... | collective-permute-start | bytes 1118216 | tf_op jit(solution)/shard_map/ppermute | solution.py:1014
  617.3 20.0 %collective-permute-start.96 = (bf16[1,768,384]{2,1,0:T(8,128)(2,1)S(1)}, bf16[1,768,384]{2,1,0:T(8,128)(2,1)S(1)}, u32[]{:S(2)}, u32[]{:S(2)}) collective-permute-start(bf16[1,768,384]{2,1,0:T(8,128)(2,1)S(1)} %collective-permute-done.93.refs_0_), channel_id=1, source_target_pairs={{0,8},{8,16},{16,24},{24,28},{28,20},{20,12},{12,4},{4,0},{9,1},{1... | collective-permute-start | bytes 1769480 | tf_op jit(solution)/shard_map/ppermute | solution.py:1014
  617.3 20.1 %collective-permute-start.98 = (bf16[1,768,384]{2,1,0:T(8,128)(2,1)S(1)}, bf16[1,768,384]{2,1,0:T(8,128)(2,1)S(1)}, u32[]{:S(2)}, u32[]{:S(2)}) collective-permute-start(bf16[1,768,384]{2,1,0:T(8,128)(2,1)S(1)} %collective-permute-done.92.refs_1_), channel_id=1, source_target_pairs={{8,0},{16,8},{24,16},{28,24},{20,28},{12,20},{4,12},{0,4},{1,9},{9... | collective-permute-start | bytes 1769480 | tf_op jit(solution)/shard_map/ppermute | solution.py:1014
  624.7 20.1 %collective-permute-start.95 = (bf16[208,896]{1,0:T(8,128)(2,1)S(1)}, bf16[208,896]{1,0:T(8,128)(2,1)S(1)}, u32[]{:S(2)}, u32[]{:S(2)}) collective-permute-start(bf16[208,896]{1,0:T(8,128)(2,1)S(1)} %collective-permute-done.91.refs_3_), channel_id=1, source_target_pairs={{0,8},{8,16},{16,24},{24,28},{28,20},{20,12},{12,4},{4,0},{9,1},{1... | collective-permute-start | bytes 1118216 | tf_op jit(solution)/shard_map/ppermute | solution.py:1014
  624.8 20.5 %collective-permute-start.102 = (bf16[208,896]{1,0:T(8,128)(2,1)S(1)}, bf16[208,896]{1,0:T(8,128)(2,1)S(1)}, u32[]{:S(2)}, u32[]{:S(2)}) collective-permute-start(bf16[208,896]{1,0:T(8,128)(2,1)S(1)} %collective-permute-done.97.refs_11_), channel_id=1, source_target_pairs={{8,0},{16,8},{24,16},{28,24},{20,28},{12,20},{4,12},{0,4},{1,9},{9... | collective-permute-start | bytes 1118216 | tf_op jit(solution)/shard_map/ppermute | solution.py:1014
  626.9 30.0 %collective-permute-start.33 = (bf16[512,768]{1,0:T(8,128)(2,1)S(1)}, bf16[512,768]{1,0:T(8,128)(2,1)S(1)}, u32[]{:S(2)}, u32[]{:S(2)}) collective-permute-start(bf16[512,768]{1,0:T(8,128)(2,1)S(1)} %dynamic-slice_convert_fusion.1), channel_id=1, source_target_pairs={{0,2},{2,0},{1,3},{3,1},{4,6},{6,4},{5,7},{7,5},{8,10},{10,8},{9,1... | collective-permute-start | bytes 2359304 | tf_op jit(solution)/shard_map/ppermute | solution.py:49
  (128 other events, 1067.1 us)

commit v10 on v9

--- a/solution.py
+++ b/solution.py
@@ -20,6 +20,8 @@
 BF16 = jnp.bfloat16
 MIB = 1024 * 1024
 GAIN_ROWS = 16
+RING = 8
+LATE_BLOCKS = 5
 SMALL = pl.CostEstimate(flops=0, bytes_accessed=0, transcendentals=0)
 
 
@@ -179,6 +181,11 @@
     )(place, own, other, grad, grad_c, w_out, out_c)
 
 
+def unit_slices(unit, share):
+    row, lane = divmod(unit, 3)
+    return slice(row * share, (row + 1) * share), slice(lane * LANES, (lane + 1) * LANES)
+
+
 def late_kernel(place_ref, *refs):
     near, near_c, far, far_c, qkv_ref, attended_ref, grad_ref, grad_c_ref = refs[0:8]
     shared = refs[8:10]
@@ -188,21 +195,28 @@
     far_rows = pl.ds(pl.multiple_of((1 - place_ref[0]) * rows, rows), rows)
     split = 7 * LANES
 
+    chunks = outs[0].shape[0]
+    share = features // chunks
+
     def store(h, at, values):
         values = values.astype(BF16)
-        for part in range(2):
-            low, high = max(at, part * split), min(at + values.shape[1], (part + 1) * split)
-            if low < high:
-                piece = values[:, low - at : high - at]
-                to = slice(low - part * split, high - part * split)
-
-                @pl.when(place_ref[2] == 0)
-                def _(part=part, to=to, piece=piece):
-                    outs[part][h, :, to] = piece
-
-                @pl.when(place_ref[2] != 0)
-                def _(part=part, to=to, piece=piece):
-                    outs[1 - part][h, :, to] = piece
+        for b in range(values.shape[1] // LANES):
+            part, unit = divmod(at // LANES + b, split // LANES)
+            to_rows, to_lanes = unit_slices(h * (split // LANES) + unit, share)
+
+            def write(out_ref, b=b, to_rows=to_rows, to_lanes=to_lanes):
+                for chunk in range(chunks):
+                    out_ref[chunk, to_rows, to_lanes] = values[
+                        chunk * share : (chunk + 1) * share, b * LANES : (b + 1) * LANES
+                    ]
+
+            pl.when(place_ref[2] == 0)(lambda part=part, write=write: write(outs[part]))
+            pl.when(place_ref[2] != 0)(lambda part=part, write=write: write(outs[1 - part]))
+
+    for out_ref in outs:
+        to_rows, to_lanes = unit_slices(2 * (split // LANES), share)
+        for chunk in range(chunks):
+            out_ref[chunk, to_rows, to_lanes] = jnp.zeros((share, LANES), BF16)
 
     for h, (x, y, grad) in enumerate(((near, far, grad_ref), (near_c, far_c, grad_c_ref))):
         for k in range(2):
@@ -214,10 +228,11 @@
 
 def late_grads(place, near, far, qkv_grad, attended, grad, grad_c, shared):
     features = near[0].shape[1]
+    rows = LATE_BLOCKS * (features // RING)
     spec = pl.BlockSpec(memory_space=pltpu.VMEM)
     return pl.pallas_call(
         late_kernel,
-        out_shape=[jax.ShapeDtypeStruct((2, features, 7 * LANES), BF16)] * 2,
+        out_shape=[jax.ShapeDtypeStruct((RING, rows, 3 * LANES), BF16)] * 2,
         in_specs=[pl.BlockSpec(memory_space=pltpu.SMEM)] + [spec] * 10,
         out_specs=[spec] * 2,
         compiler_params=params(60),
@@ -633,13 +648,20 @@
     )(order, acts, shared_acts, *weights * (2 * group), *shared_weights * 2)
 
 
-def chip_sum_kernel(own_ref, other_ref, total_ref, rounded_ref):
+def chip_sum_kernel(own_ref, other_ref, hidden_ref, gains_ref, total_ref, rounded_ref, product_ref):
     total = own_ref[...] + other_ref[...].astype(F32)
     total_ref[...] = total
     rounded_ref[...] = total.astype(BF16)
-
-
-def chip_sum(own, other):
+    product_ref[...] = lax.dot_general(
+        jnp.ones((8, total.shape[1]), F32),
+        total * gains_ref[1:2, :] * hidden_ref[...],
+        (((1,), (1,)), ((), ())),
+        precision=lax.Precision.HIGHEST,
+        preferred_element_type=F32,
+    )
+
+
+def chip_sum(own, other, hidden, gains):
     rows, features = own.shape
     spec = pl.BlockSpec((TOKEN_TILE, features), lambda i: (i, 0))
     return pl.pallas_call(
@@ -648,23 +670,37 @@
         out_shape=[
             jax.ShapeDtypeStruct((rows, features), F32),
             jax.ShapeDtypeStruct((rows, features), BF16),
+            jax.ShapeDtypeStruct((8, rows), F32),
         ],
-        in_specs=[spec, spec],
-        out_specs=[spec, spec],
-        compiler_params=params(16, "arbitrary"),
+        in_specs=[spec, spec, spec, pl.BlockSpec(gains.shape, lambda i: (0, 0))],
+        out_specs=[spec, spec, pl.BlockSpec((8, TOKEN_TILE), lambda i: (0, i))],
+        compiler_params=params(24, "arbitrary"),
         cost_estimate=SMALL,
         name="chip_sum",
-    )(own, other)
+    )(own, other, hidden, gains)
 
 
 def norm_back_kernel(tiles, place_ref, *refs):
-    sum_ref, came_ref, hidden_ref, scale_ref, gains_ref, grad_ref, product_ref, gain_ref = refs
+    sum_ref, came_ref, hidden_ref, scale_ref, out_grad_ref, gains_ref = refs[0:6]
+    products = refs[6:10]
+    hidden_grad_ref, rounded_ref, gain_ref = refs[10:13]
     step = pl.program_id(0)
     part = (step >= tiles // 2).astype(jnp.int32)
     grad = sum_ref[...] + came_ref[...].astype(F32)
     hidden = hidden_ref[...]
-    grad_ref[...] = grad
-    product_ref[...] = jnp.sum(grad * gains_ref[1:2, :] * hidden, axis=1, keepdims=True)
+    scale = scale_ref[...]
+    total = (products[0][...] + products[1][...]) + (products[2][...] + products[3][...])
+    mean = lax.dot_general(
+        total,
+        jnp.full((8, LANES), 1.0 / (8 * D), F32),
+        (((0,), (0,)), ((), ())),
+        precision=lax.Precision.HIGHEST,
+        preferred_element_type=F32,
+    )[:, 0:1]
+    result = out_grad_ref[...].astype(F32) + scale * (grad * gains_ref[1:2, :])
+    result = result - hidden * (scale * scale * scale * mean)
+    hidden_grad_ref[...] = result
+    rounded_ref[...] = result.astype(BF16)
 
     @pl.when(step == 0)
     def _():
@@ -672,57 +708,32 @@
 
     @pl.when(part == place_ref[0])
     def _():
-        gain_ref[...] += jnp.sum(grad * hidden * scale_ref[...], axis=0, keepdims=True)
-
-
-def norm_back(place, sums, came, hidden, scale, gains):
+        gain_ref[...] += jnp.sum(grad * hidden * scale, axis=0, keepdims=True)
+
+
+def norm_back(place, sums, came, hidden, scale, out_grad, gains, products):
     rows, features = hidden.shape
     tiles = rows // TOKEN_TILE
+    lanes = pl.BlockSpec((8, TOKEN_TILE), lambda i, p: (0, i))
     return pl.pallas_call(
         functools.partial(norm_back_kernel, tiles),
         grid_spec=pltpu.PrefetchScalarGridSpec(
             num_scalar_prefetch=1,
             grid=(tiles,),
-            in_specs=[rowwise(features)] * 3 + [rowwise(1), whole(2, features)],
-            out_specs=[rowwise(features), rowwise(1), whole(1, features)],
+            in_specs=[rowwise(features)] * 3
+            + [rowwise(1), rowwise(features), whole(2, features)]
+            + [lanes] * 4,
+            out_specs=[rowwise(features)] * 2 + [whole(1, features)],
         ),
         out_shape=[
             jax.ShapeDtypeStruct((rows, features), F32),
-            jax.ShapeDtypeStruct((rows, 1), F32),
+            jax.ShapeDtypeStruct((rows, features), BF16),
             jax.ShapeDtypeStruct((1, features), F32),
         ],
         compiler_params=params(48, "arbitrary"),
         cost_estimate=SMALL,
         name="norm_back",
-    )(place, sums, came, hidden, scale, gains)
-
-
-def norm_back_end_kernel(grad_ref, own_ref, other_ref, hidden_ref, scale_ref, gains_ref, out_grad_ref, hidden_grad_ref, rounded_ref):
-    scale = scale_ref[...]
-    mean = (own_ref[...] + other_ref[...]) * (1.0 / D)
-    result = out_grad_ref[...].astype(F32) + scale * (grad_ref[...] * gains_ref[1:2, :])
-    result = result - hidden_ref[...] * (scale * scale * scale * mean)
-    hidden_grad_ref[...] = result
-    rounded_ref[...] = result.astype(BF16)
-
-
-def norm_back_end(grad, products, products_c, hidden, scale, gains, out_grad):
-    rows, features = hidden.shape
-    tile = pl.BlockSpec((TOKEN_TILE, features), lambda i: (i, 0))
-    column = pl.BlockSpec((TOKEN_TILE, 1), lambda i: (i, 0))
-    return pl.pallas_call(
-        norm_back_end_kernel,
-        grid=(rows // TOKEN_TILE,),
-        in_specs=[tile, column, column, tile, column, pl.BlockSpec(gains.shape, lambda i: (0, 0)), tile],
-        out_specs=[tile, tile],
-        out_shape=[
-            jax.ShapeDtypeStruct((rows, features), F32),
-            jax.ShapeDtypeStruct((rows, features), BF16),
-        ],
-        compiler_params=params(48, "arbitrary"),
-        cost_estimate=SMALL,
-        name="norm_back_end",
-    )(grad, products, products_c, hidden, scale, gains, out_grad)
+    )(place, sums, came, hidden, scale, out_grad, gains, *products)
 
 
 def ring_of(size):
@@ -732,33 +743,33 @@
 def unpack_kernel(aliased, plan_ref, *refs):
     chunks = refs[0:2]
     gate_ref, up_ref, down_ref = refs[2 + aliased : 5 + aliased]
-    blocks = chunks[0].shape[1] // LANES
+    rows = gate_ref.shape[1]
 
     def write(chunk_ref):
-        gate_ref[0] = chunk_ref[0, :, 0:LANES].astype(F32)
-        up_ref[0] = chunk_ref[0, :, LANES : 2 * LANES].astype(F32)
-        for b in range(blocks):
-            at = slice(b * LANES, (b + 1) * LANES)
-            down_ref[0, :, at] = chunk_ref[0, at, 2 * LANES :].astype(F32)
+        first = chunk_ref.shape[0] - rows
+        gate_ref[0] = chunk_ref[first:, 0:LANES].astype(F32)
+        up_ref[0] = chunk_ref[first:, LANES : 2 * LANES].astype(F32)
+        for b in range(rows // LANES):
+            at = slice(first + b * LANES, first + (b + 1) * LANES)
+            down_ref[0, :, b * LANES : (b + 1) * LANES] = chunk_ref[at, 2 * LANES :].astype(F32)
 
     for k in range(2):
-        pl.when(pl.program_id(1) == k)(lambda k=k: write(chunks[k]))
+        pl.when(pl.program_id(0) == k)(lambda k=k: write(chunks[k]))
 
 
 def unpack(plan, first, wave, chunks, shapes, outs):
-    count, rows, width = chunks[0].shape
-    chunk = pl.BlockSpec((1, rows, width), lambda i, d, n: (i, 0, 0))
-
-    def place(i, d, n):
+    rows = shapes[0][1]
+
+    def place(d, n):
         block = n[n.shape[0] - 1]
-        return n[first + 2 * i + d], 1 - block if wave else block
-
-    def wide(i, d, n):
-        expert, block = place(i, d, n)
+        return n[first + d], 1 - block if wave else block
+
+    def wide(d, n):
+        expert, block = place(d, n)
         return (expert, 0, block)
 
-    def low(i, d, n):
-        expert, block = place(i, d, n)
+    def low(d, n):
+        expert, block = place(d, n)
         return (expert, block, 0)
 
     aliased = len(outs)
@@ -766,8 +777,9 @@
         functools.partial(unpack_kernel, aliased),
         grid_spec=pltpu.PrefetchScalarGridSpec(
             num_scalar_prefetch=1,
-            grid=(count, 2),
-            in_specs=[chunk, chunk] + [pl.BlockSpec(memory_space=pl.ANY)] * aliased,
+            grid=(2,),
+            in_specs=[pl.BlockSpec(chunk.shape, lambda d, n: (0, 0)) for chunk in chunks]
+            + [pl.BlockSpec(memory_space=pl.ANY)] * aliased,
             out_specs=[
                 pl.BlockSpec((1, rows, LANES), wide),
                 pl.BlockSpec((1, rows, LANES), wide),
@@ -776,7 +788,7 @@
         ),
         out_shape=[jax.ShapeDtypeStruct(shape, F32) for shape in shapes],
         input_output_aliases={3 + k: k for k in range(aliased)},
-        compiler_params=params(16, "arbitrary", "arbitrary"),
+        compiler_params=params(16, "arbitrary"),
         cost_estimate=SMALL,
         name="unpack",
     )(plan, *chunks, *outs)
@@ -820,82 +832,145 @@
     )(came, mine)
 
 
-def late_chunk_kernel(came, plan_ref, pack_ref, *refs):
-    values = pack_ref[:, 0]
-    if came:
-        values = (refs[0][...].astype(F32) + values.astype(F32)).astype(BF16)
-    outs = refs[came:]
-    if len(outs) == 1:
-        outs[0][...] = values
-    else:
-        for k, out_ref in enumerate(outs):
-            out_ref[...] = values[k]
-
-
-def late_chunk(plan, at, pack, came, halved):
-    halves, _, rows, lanes = pack.shape
-    spec = pl.BlockSpec((halves, rows, lanes), lambda i, n: (0, 0, 0))
-    half = pl.BlockSpec((rows, lanes), lambda i, n: (0, 0))
-    halfs = [jax.ShapeDtypeStruct((rows, lanes), BF16)] * 2
-    return pl.pallas_call(
-        functools.partial(late_chunk_kernel, len(came)),
+def late_load_kernel(plan_ref, pack_ref, main_ref, out_ref):
+    rows = pack_ref.shape[1]
+    out_ref[0:rows, :] = pack_ref[0]
+    out_ref[rows:, :] = main_ref[...]
+
+
+def late_load(plan, at, pack, main):
+    rows, lanes = pack.shape[1:]
+    total = rows + main.shape[0]
+    return pl.pallas_call(
+        late_load_kernel,
         grid_spec=pltpu.PrefetchScalarGridSpec(
             num_scalar_prefetch=1,
             grid=(1,),
-            in_specs=[pl.BlockSpec((halves, 1, rows, lanes), lambda i, n: (0, n[at], 0, 0))]
-            + [spec] * len(came),
-            out_specs=[half] * 2 if halved else spec,
+            in_specs=[
+                pl.BlockSpec((1, rows, lanes), lambda i, n: (n[at], 0, 0)),
+                pl.BlockSpec(main.shape, lambda i, n: (0, 0)),
+            ],
+            out_specs=pl.BlockSpec((total, lanes), lambda i, n: (0, 0)),
         ),
-        out_shape=halfs if halved else jax.ShapeDtypeStruct((halves, rows, lanes), BF16),
+        out_shape=jax.ShapeDtypeStruct((total, lanes), BF16),
         compiler_params=params(16, "arbitrary"),
         cost_estimate=SMALL,
-        name="late_chunk",
-    )(plan, pack, *came)
-
-
-def late_join_kernel(col_ref, own_ref, other_ref, gains_ref, out_ref):
-    rows = own_ref.shape[0]
-    features = gains_ref.shape[1]
-    out_ref[pl.ds(pl.multiple_of(col_ref[0] * rows, rows), rows), :] = own_ref[...]
-    out_ref[pl.ds(pl.multiple_of((1 - col_ref[0]) * rows, rows), rows), :] = other_ref[...]
-    out_ref[2 * rows :, :] = jnp.zeros((GAIN_ROWS, own_ref.shape[1]), BF16)
-    pad = jnp.zeros((GAIN_ROWS - 2, features), F32)
-    out_ref[2 * rows :, 0:features] = jnp.concatenate([gains_ref[...], pad], axis=0).astype(BF16)
-
-
-def late_join(col, own, other, gains):
-    rows, lanes = own.shape
-    spec = pl.BlockSpec(memory_space=pltpu.VMEM)
+        name="late_load",
+    )(plan, pack, main)
+
+
+def late_add_kernel(plan_ref, pack_ref, came_ref, *outs):
+    total = (came_ref[...].astype(F32) + pack_ref[0].astype(F32)).astype(BF16)
+    for out_ref in outs:
+        out_ref[...] = total
+
+
+def late_add(plan, at, pack, came, copied=False):
+    rows, lanes = pack.shape[1:]
+    spec = pl.BlockSpec((rows, lanes), lambda i, n: (0, 0))
+    shape = jax.ShapeDtypeStruct(came.shape, BF16)
+    return pl.pallas_call(
+        late_add_kernel,
+        grid_spec=pltpu.PrefetchScalarGridSpec(
+            num_scalar_prefetch=1,
+            grid=(1,),
+            in_specs=[pl.BlockSpec((1, rows, lanes), lambda i, n: (n[at], 0, 0)), spec],
+            out_specs=[spec] * 2 if copied else spec,
+        ),
+        out_shape=[shape, jax.ShapeDtypeStruct((rows, lanes), BF16)] if copied else shape,
+        input_output_aliases={2: 0},
+        compiler_params=params(16, "arbitrary"),
+        cost_estimate=SMALL,
+        name="late_add",
+    )(plan, pack, came)
+
+
+def late_main_kernel(main_ref, all_ref, out_ref):
+    out_ref[...] = main_ref[...]
+
+
+def late_main(rows_all, main):
+    lanes = main.shape[1]
+    share = main.shape[0] // RING
+    first = (rows_all.shape[0] - main.shape[0]) // share
+    return pl.pallas_call(
+        late_main_kernel,
+        grid=(RING,),
+        in_specs=[
+            pl.BlockSpec((share, lanes), lambda i: (i, 0)),
+            pl.BlockSpec(memory_space=pl.ANY),
+        ],
+        out_specs=pl.BlockSpec((share, lanes), lambda i: (first + i, 0)),
+        out_shape=jax.ShapeDtypeStruct(rows_all.shape, BF16),
+        input_output_aliases={1: 0},
+        compiler_params=params(16, "arbitrary"),
+        cost_estimate=SMALL,
+        name="late_main",
+    )(main, rows_all)
+
+
+def late_join_kernel(col_ref, mine_ref, other_ref, gains_ref, out_ref):
+    units = 7
+    share = mine_ref.shape[0] // LATE_BLOCKS
+    to_rows, to_lanes = unit_slices(2 * units, share)
+    blocks = gains_ref.shape[1] // LANES
+    gains = [
+        gains_ref[g : g + 1, b * LANES : (b + 1) * LANES] for g in range(2) for b in range(blocks)
+    ]
+    gains = jnp.concatenate(gains + [jnp.zeros((share - len(gains), LANES), F32)], axis=0)
+    own = [mine_ref[unit_slices(b, share)] for b in range(units)]
+    other = [other_ref[unit_slices(units + b, share)] for b in range(units)]
+    for b in range(units):
+        first, second = own[b], other[b]
+        flipped = col_ref[0] != 0
+        out_ref[unit_slices(b, share)] = jnp.where(flipped, second, first)
+        out_ref[unit_slices(units + b, share)] = jnp.where(flipped, first, second)
+    out_ref[to_rows, to_lanes] = gains.astype(BF16)
+
+
+def late_join(col, rows_all, other, gains):
+    rows, lanes = other.shape
+    spec = pl.BlockSpec((rows, lanes), lambda i, c: (0, 0))
     return pl.pallas_call(
         late_join_kernel,
-        out_shape=jax.ShapeDtypeStruct((2 * rows + GAIN_ROWS, lanes), BF16),
-        in_specs=[pl.BlockSpec(memory_space=pltpu.SMEM)] + [spec] * 3,
-        out_specs=spec,
-        compiler_params=params(16),
+        grid_spec=pltpu.PrefetchScalarGridSpec(
+            num_scalar_prefetch=1,
+            grid=(1,),
+            in_specs=[spec, spec, pl.BlockSpec(gains.shape, lambda i, c: (0, 0))],
+            out_specs=spec,
+        ),
+        out_shape=jax.ShapeDtypeStruct(rows_all.shape, BF16),
+        input_output_aliases={1: 0},
+        compiler_params=params(16, "arbitrary"),
         cost_estimate=SMALL,
         name="late_join",
-    )(col, own, other, gains)
+    )(col, rows_all, other, gains)
 
 
 def unpack_late_kernel(first_step, steps, plan_ref, *refs):
     chunks = refs[0 : 2 * steps]
     sgate, sup, sdown, query, key, value, out, gains, all_ref, gain_ref = refs[2 * steps :]
-    rows, features = (chunks[0].shape[0] - GAIN_ROWS) // 2, all_ref.shape[2]
+    share, features = chunks[0].shape[0] // LATE_BLOCKS, all_ref.shape[2]
     for k in range(2):
         for step in range(steps):
-            at = plan_ref[first_step + 2 * step + k] * rows
-            for c in range(2):
-                all_ref[k, c, pl.ds(pl.multiple_of(at, rows), rows), :] = chunks[
-                    steps * k + step
-                ][c * rows : (c + 1) * rows, :]
+            at = plan_ref[first_step + 2 * step + k]
+            chunk = chunks[steps * k + step]
+            to_rows = pl.ds(pl.multiple_of(at * share, share), share)
+            for unit in range(14):
+                lanes = slice(unit % 7 * LANES, (unit % 7 + 1) * LANES)
+                all_ref[k, unit // 7, to_rows, lanes] = chunk[unit_slices(unit, share)]
+            if k == 0:
+                to_rows = pl.ds(pl.multiple_of(at * GAIN_ROWS, GAIN_ROWS), GAIN_ROWS)
+                rows, lanes = unit_slices(14, share)
+                gain_ref[to_rows, :] = chunk[rows.start : rows.start + GAIN_ROWS, lanes]
+    total = jnp.zeros((GAIN_ROWS, LANES), F32)
     for step in range(steps):
-        at = plan_ref[first_step + 2 * step] * GAIN_ROWS
-        gain_ref[pl.ds(pl.multiple_of(at, GAIN_ROWS), GAIN_ROWS), :] = chunks[step][2 * rows :, :]
-    total = jnp.zeros((GAIN_ROWS, features), F32)
-    for step in range(steps):
-        rows_of = slice(step * GAIN_ROWS, (step + 1) * GAIN_ROWS)
-        total = total + gain_ref[rows_of, 0:features].astype(F32)
-    gains[...] = total[0:2]
+        total = total + gain_ref[step * GAIN_ROWS : (step + 1) * GAIN_ROWS, :].astype(F32)
+    blocks = features // LANES
+    for row in range(2 * blocks):
+        gains[row // blocks : row // blocks + 1, row % blocks * LANES : (row % blocks + 1) * LANES] = (
+            total[row : row + 1, :]
+        )
     flipped = plan_ref[plan_ref.shape[0] - 1] != 0
     for c in range(2):
         for b in range(14):
@@ -924,18 +999,23 @@
 
 def unpack_late(plan, first_step, chunks, shapes):
     steps = len(chunks[0])
-    rows, lanes = (chunks[0][0].shape[0] - GAIN_ROWS) // 2, chunks[0][0].shape[1]
-    spec = pl.BlockSpec(memory_space=pltpu.VMEM)
+    features = shapes[0][0]
+    share = features // steps
+    chunk = pl.BlockSpec((LATE_BLOCKS * share, 3 * LANES), lambda i, n: (0, 0))
     return pl.pallas_call(
         functools.partial(unpack_late_kernel, first_step, steps),
-        in_specs=[pl.BlockSpec(memory_space=pltpu.SMEM)] + [spec] * (2 * steps),
-        out_specs=[spec] * len(shapes),
+        grid_spec=pltpu.PrefetchScalarGridSpec(
+            num_scalar_prefetch=1,
+            grid=(1,),
+            in_specs=[chunk] * (2 * steps),
+            out_specs=[pl.BlockSpec(shape, lambda i, n: (0, 0)) for shape in shapes],
+            scratch_shapes=[
+                pltpu.VMEM((2, 2, features, 7 * LANES), BF16),
+                pltpu.VMEM((steps * GAIN_ROWS, LANES), BF16),
+            ],
+        ),
         out_shape=[jax.ShapeDtypeStruct(shape, F32) for shape in shapes],
-        scratch_shapes=[
-            pltpu.VMEM((2, 2, steps * rows, lanes), BF16),
-            pltpu.VMEM((steps * GAIN_ROWS, lanes), BF16),
-        ],
-        compiler_params=params(48),
+        compiler_params=params(48, "arbitrary"),
         cost_estimate=SMALL,
         name="unpack_late",
     )(plan, *chunks[0], *chunks[1])
@@ -991,7 +1071,7 @@
     group_width = GROUP_HEADS * DH
     col_ref = col.reshape(1)
 
-    ring_size = min(8, dp_size)
+    ring_size = RING
     ring = ring_of(ring_size)
     starts = range(0, dp_size, ring_size)
     rights = [
@@ -1009,8 +1089,6 @@
     ).reshape(-1)
 
     def send(values, which):
-        if ring_size == 1:
-            return values
         return lax.ppermute(values, ("dp", "col"), routes_of[which])
 
     def chunk_at(step, which):
@@ -1025,7 +1103,7 @@
     where = jnp.stack([row, seq_lengths[0], col])
     tokens_y = swap(tokens_in, "row")
     tokens_c = swap(tokens_in, "col")
-    count = min(ring_size, 4)
+    count = 4
     member = dp % count
     there, out_y = their_columns(
         jnp.stack([col, member]), w_query, w_key, w_value, w_out, count
@@ -1145,8 +1223,12 @@
             if half:
                 normed["other"] = swap(mixed[True, 1], "col")
                 return [mixed[True, 1]]
-            normed["sum"] = chip_sum(mixed[True, 0], normed["other"])
-            normed["came"] = swap(normed["sum"][1], "row")
+            total, rounded, product = chip_sum(mixed[True, 0], normed["other"], hidden, gains)
+            product_c = swap(product, "col")
+            normed["sum"] = total
+            normed["tie"] = rounded
+            normed["came"] = swap(rounded, "row")
+            normed["products"] = [product, product_c, swap(product, "row"), swap(product_c, "row")]
             return [mixed[True, 0]]
 
         return work
@@ -1162,7 +1244,7 @@
                 routed[4 + half : 5 + half],
                 shared[4 + half : 5 + half],
             )
-            return [mixed[False, half]] + ([] if half else [normed["sum"][1]])
+            return [mixed[False, half]] + ([] if half else [normed["tie"]])
 
         return work
 
@@ -1175,12 +1257,15 @@
         return lax.dynamic_slice_in_dim(values, local_rows - start, local_rows, axis=0)
 
     def work_hidden(order, ties):
-        grads, products, normed["gain"] = norm_back(
-            after(where, *ties), normed["sum"][0], normed["came"], hidden, scale_ffn, gains
-        )
-        products_c = swap(products, "col")
-        normed["hidden"], normed["grad"] = norm_back_end(
-            grads, products, products_c, hidden, scale_ffn, gains, grad_own
+        normed["hidden"], normed["grad"], normed["gain"] = norm_back(
+            after(where, *ties),
+            normed["sum"],
+            normed["came"],
+            hidden,
+            scale_ffn,
+            grad_own,
+            gains,
+            normed["products"],
         )
         normed["grad_c"] = swap(normed["grad"], "col")
         return [normed["grad"]]
@@ -1206,12 +1291,11 @@
 
     tasks = [work_experts(at, at + each) for at in range(each, pairs_total, each)]
     tasks += [work_shared, work_back(1), work_back(0), work_out(1), work_out(0)]
-    later = [work_hidden, work_attend, work_late]
+    later = [[work_hidden, work_attend], [work_late]]
     got = [None, None]
-    if ring_size > 1:
-        got[0] = send(sums[0], 0)
-        tasks.pop(0)(after(order, *sums), sums)
-        got[1] = send(after(sums[1], kept[0]), 1)
+    got[0] = send(sums[0], 0)
+    tasks.pop(0)(after(order, *sums), sums)
+    got[1] = send(after(sums[1], kept[0]), 1)
     for s in range(1, ring_size):
         for k in range(2):
             last = sums
@@ -1223,25 +1307,11 @@
                 got[k] = send(sums[k], k)
             else:
                 sums[k], got[k] = sums[k]
-    for task in tasks:
-        if task:
-            task(after(order, *sums), sums)
-    if ring_size == 1:
-        got = [total[:, local_features:] for total in sums]
-        sums = [total[:, :local_features] for total in sums]
-    waves = [[across_rings(total) for total in sums]]
     crossed = [swap(across_rings(total), "col") for total in got]
-    waves.append([crossed[1], crossed[0]])
+    waves = [[across_rings(total)[0] for total in sums], [crossed[1][0], crossed[0][0]]]
 
     chunks_first = 2 * experts
     late_total = 2 * (ring_size - 1)
-    packs, late = [None, None], [None, None]
-
-    def late_begin():
-        for k in range(2):
-            pack = normed["packs"][k]
-            packs[k] = pack.reshape(2, ring_size, local_features // ring_size, pack.shape[2])
-            late[k] = late_chunk(plan, chunks_first + k, packs[k], (), late_total == 0)
 
     def back_to_tokens(ties):
         hidden_grad = normed["hidden"]
@@ -1272,89 +1342,83 @@
         normed["gains"] = across_rings(gain_parts + swap(gain_parts, "row"))
         normed["outs"] = (block_out, tokens_grad)
 
-    def gain_sums():
-        return normed["gains"]
-
-    late_out = [[], []]
-    late_done = 0
-
-    def late_turn():
-        owns = [across_rings(values[0]) for values in late]
-        others = [swap(across_rings(values[1]), "col") for values in late]
-        for k in range(2):
-            late[k] = late_join(col_ref, owns[k], others[1 - k], gain_sums())
-            late_out[k].append(late[k])
-
-    def late_finish(k, values):
-        if late_done < ring_size:
-            at = chunks_first + 2 * late_done + k
-            late[k] = late_chunk(plan, at, packs[k], (values,), late_done == ring_size - 1)
-        else:
-            late[k] = values
-            late_out[k].append(values)
-
     shapes = [w_gate.shape, w_up.shape, w_down.shape]
     placed = ()
-
-    def place_chunks(wave, step, chunks, placed):
-        return unpack(plan, experts + 2 * each * step, wave, chunks, shapes, placed)
-
-    steps = ring_size - 1
-    late_got = None
-    last = []
-    got = list(waves[0])
-    for number in range(2 * steps - 1):
-        wave, step = (0, number) if number < steps else (1, number - steps + 1)
-        if number == steps:
-            came = got
-            got = early
-        chunks = [None, None]
+    late_out = [[], []]
+    late_start = len(later)
+    last, got = [], [None, None]
+    moves = [(wave, step) for wave in range(2) for step in range(wave, ring_size - 1)]
+    for number, (wave, step) in enumerate(moves):
+        late_step = number - late_start
+        current = [None, None]
+        copies = [None, None]
         for k in range(2):
-            chunks[k] = after(got[k], *last) if last else got[k]
-            got[k] = send(chunks[k], k)
-            last = [chunks[k]]
+            if number == 0:
+                current[k] = after(waves[0][k], *last) if last else waves[0][k]
+                got[k] = send(current[k], k)
+                last = [current[k]]
+                continue
+            current[k] = after(got[k], *last)
+            if late_step < 0:
+                got[k] = send(current[k], k)
+                last = [current[k]]
+                continue
+            at = chunks_first + 2 * late_step + k
+            if late_step == 0:
+                current[k] = late_load(plan, at, normed["packs"][k], current[k])
+            elif late_step < ring_size - 1:
+                current[k] = late_add(plan, at, normed["packs"][k], current[k])
+            elif late_step == ring_size - 1:
+                current[k], copies[k] = late_add(plan, at, normed["packs"][k], current[k], True)
+            last = [current[k]]
+            if not (wave == 1 and step == 1) and late_step != ring_size - 1:
+                got[k] = send(current[k], k)
+                if late_step >= ring_size:
+                    late_out[k].append(current[k])
+        switch = wave == 1 and step == 1
+        if switch or late_step == ring_size - 1:
+            if late_step == ring_size - 1:
+                others = [swap(across_rings(values), "col") for values in copies]
+                current = [
+                    late_join(col_ref, current[k], others[1 - k], normed["gains"])
+                    for k in range(2)
+                ]
+            if switch:
+                placed = unpack(
+                    plan, experts + 2 * (ring_size - 1), 0, current, shapes, placed
+                )
+                placed = unpack(plan, experts, 1, waves[1], shapes, placed)
+                current = [late_main(after(current[k], placed[0]), early[k]) for k in range(2)]
+            for k in range(2):
+                got[k] = send(current[k], k)
+                if late_step >= ring_size - 1:
+                    late_out[k].append(current[k])
+            last = [current[1]]
         if number == 0:
-            early = [send(after(waves[1][k], *chunks), k) for k in range(2)]
-        if late_got is not None:
-            late_done += 1
-            for k in range(2):
-                late_finish(k, after(late_got[k], *last))
-                last = list(late[k]) if late_done == ring_size - 1 else [late[k]]
-            if late_done == ring_size - 1:
-                late_turn()
+            early = [send(after(waves[1][k], *current), k) for k in range(2)]
         if number < len(later):
-            last = later[number](after(order, *last), last)
-        late_got = None
-        if number + 1 >= len(later) and late_done < late_total:
-            if late_done == 0:
-                late_begin()
-            late_got = [send(late[k], k) for k in range(2)]
-        if number == steps:
-            placed = place_chunks(0, steps, came, placed)
-            placed = place_chunks(1, 0, waves[1], placed)
-        placed = place_chunks(wave, step, [after(chunks[0], *last), chunks[1]], placed)
+            for work in later[number]:
+                if number == 1:
+                    last = [*last, *early]
+                last = work(after(order, *last), last)
+        placed = unpack(
+            plan, experts + 2 * step, wave, [after(current[0], *last), current[1]], shapes, placed
+        )
         last = placed[0:1]
         if number == 3:
             back_to_tokens(last)
-    if steps:
-        placed = place_chunks(1, steps, [after(got[k], *last) for k in range(2)], placed)
-        last = placed[0:1]
-    else:
-        for work in later:
-            work(order, ())
-        late_begin()
-        back_to_tokens(())
-        late_turn()
-    while late_got is not None:
-        late_done += 1
+    for late_step in range(len(moves) - late_start, late_total + 1):
         for k in range(2):
-            late_finish(k, after(late_got[k], *last))
-        if late_done == ring_size - 1:
-            late_turn()
-        late_got = [send(late[k], k) for k in range(2)] if late_done < late_total else None
-    if not steps:
-        for wave in range(2):
-            placed = place_chunks(wave, 0, waves[wave], placed)
+            values = after(got[k], *last)
+            late_out[k].append(values)
+            if late_step < late_total:
+                got[k] = send(values[: LATE_BLOCKS * (local_features // ring_size)], k)
+            last = [values]
+        if late_step == len(moves) - late_start:
+            whole_chunks = [late_out[k][-1] for k in range(2)]
+            placed = unpack(
+                plan, experts + 2 * (ring_size - 1), 1, whole_chunks, shapes, placed
+            )
     gate_grad, up_grad, down_grad = placed
     shapes = [w.shape for w in (w_shared_gate, w_shared_up, w_shared_down)]
     shapes += [w.shape for w in (w_query, w_key, w_value, w_out)] + [gains.shape]

time: 690 us -> 698 us (1.012)
  Pallas kernels: 278 us -> 306 us
  starting transfers between devices: 100 us -> 78.5 us
  waiting for transfers between devices: 254 us -> 264 us
  local copies, waits for them, and re-layouts: 30.6 us -> 23.6 us
    ppermute x70 -> x48, starting transfers between devices: 79.1 us -> 54.2 us  [send(): return lax.ppermute(values, ('dp', 'col'), routes_of[which])]
    pallas_call x20 -> x21, Pallas kernels: 34.5 us -> 45.2 us  [the longest x14 20.2 us: late_add(): pl.pallas_call(late_add_kernel, grid_spec=pltpu.PrefetchScalarGridSpec(nu...]
    ppermute x70 -> x48, waiting for transfers between devices: 214 us -> 222 us  [send(): return lax.ppermute(values, ('dp', 'col'), routes_of[which])]
    unnamed x172 -> x166, local copies, waits for them, and re-layouts: 28.2 us -> 21.1 us
    ppermute x33 -> x35, starting transfers between devices: 15.6 us -> 18.7 us  [swap(): return lax.ppermute(values, axis, [(0, 1), (1, 0)])]
    ppermute x33 -> x35, waiting for transfers between devices: 37.8 us -> 40.2 us  [swap(): return lax.ppermute(values, axis, [(0, 1), (1, 0)])]
  transfers between devices with their start and end apart: 106 -> 86, of which waited for: 38 -> 36; matrix products, arithmetic and copies ran while one was open for 3% -> 2% of each run, Pallas kernels for 37% -> 41%
where the time goes in v10:
time: 698 us; the launch traced here: 688 us
  Pallas kernels  306 us (44%)
  waiting for transfers between devices  264 us (38%)
  starting transfers between devices  78.5 us (11%)
  local copies, waits for them, and re-layouts  23.6 us (3%)
  other arithmetic  8.32 us (1%)
    ppermute x48, waiting for transfers between devices, send(): return lax.ppermute(values, ('dp', 'col'), routes_of[which])  222 us
    pallas_call x9, Pallas kernels, expert_grads(): pl.pallas_call(functools.partial(expert_kernel, shared, aliased, first),...  78.8 us
    ppermute x48, starting transfers between devices, send(): return lax.ppermute(values, ('dp', 'col'), routes_of[which])  54.2 us
    pallas_call x16, Pallas kernels, unpack(): pl.pallas_call(functools.partial(unpack_kernel, aliased), grid_spec=pltpu...  44 us
    ppermute x35, waiting for transfers between devices, swap(): return lax.ppermute(values, axis, [(0, 1), (1, 0)])  40.2 us
    pallas_call x4, Pallas kernels, mix(): pl.pallas_call(functools.partial(mix_kernel, back, group), grid_spec=pltp...  39.4 us
    pallas_call x14, Pallas kernels, ring_sum(): pl.pallas_call(ring_sum_kernel, grid=(count, tiles), in_specs=[spec, spec...  28.7 us
    unnamed x166, local copies, waits for them, and re-layouts  21.1 us
  transfers between devices with their start and end apart: 86, of which 36 were waited for; matrix products, arithmetic and copies ran while one was open for 2% of the time, Pallas kernels for 41%

profile of v10, /device:TPU:0, one launch (start us, length us, event | category | flops | bytes accessed | tf_op | source)
XLA Modules:
  0.0 688.1 jit_solution(2050955944900356660)
XLA Ops:
  1.8 3.2 their_columns.1
  5.5 2.6 collective-permute-start
  8.3 4.9 collective-permute-done.2.gains_c_ref.refs_7_
  13.2 2.9 collective-permute-start.4
  17.9 4.5 project.2
  22.4 10.1 %collective-permute-done.4.refs_0_ = bf16[192,768]{1,0:T(8,128)(2,1)S(1)} collective-permute-done((bf16[192,768]{1,0:T(8,128)(2,1)}, bf16[192,768]{1,0:T(8,128)(2,1)S(1)}, u32[]{:S(2)}, u32[]{:S(2)}) %collective-permute-start.4) | collective-permute-done | bytes 294944 | tf_op jit(solution)/shard_map/ppermute | solution.py:51
  40.8 4.5 project.3
  50.8 5.0 collective-permute-done.5.refs_1_
  57.6 6.3 attend.1.refs_4_.refs_5_
  69.6 9.0 %hidden_before.1 = (f32[1024,768]{1,0:T(8,128)}, f32[1024,768]{1,0:T(8,128)}) custom-call(s32[3]{0:T(128)} %copy-done.59, bf16[512,768]{1,0:T(8,128)(2,1)} %refs_0_.2, bf16[512,768]{1,0:T(8,128)(2,1)} %copy-done.72, bf16[512,768]{1,0:T(8,128)(2,1)} %collective-permute-done.own_ref.refs_2_, bf16[512,768]{1,0:T(8,128)(2,1)} %copy-done.73, ...), custom_call_target="tpu_custom_call" | custom-call | flops 2415919104 | bytes 12582912 | tf_op jit(solution)/shard_map/hidden_before/pallas_call | solution.py:414
  78.6 5.6 collective-permute-done.12.refs_2_
  87.6 9.4 %hidden_after.1 = (f32[1024,768]{1,0:T(8,128)}, bf16[1024,768]{1,0:T(8,128)(2,1)}, bf16[1024,768]{1,0:T(8,128)(2,1)}, f32[1024,1]{1,0:T(8,128)}) custom-call(s32[3]{0:T(128)} %copy-done.59, f32[1024,768]{1,0:T(8,128)} %get-tuple-element.237.refs_0_, f32[1024,768]{1,0:T(8,128)} %get-tuple-element.238.refs_1_, ...), custom_call_target="tpu_custom_call" | custom-call | tf_op jit(solution)/shard_map/hidden_after/pallas_call | solution.py:436
  100.4 9.3 %expert_grads.9 = (bf16[1,1536,384]{2,1,0:T(8,128)(2,1)S(1)}, bf16[1,1536,384]{2,1,0:T(8,128)(2,1)S(1)}, bf16[8,1024,512]{2,1,0:T(8,128)(2,1)}, bf16[8,1024,256]{2,1,0:T(8,128)(2,1)S(1)}) custom-call(s32[63]{0:T(128)S(1)} %fusion.14.order_ref.plan_ref, bf16[1024,768]{1,0:T(8,128)(2,1)S(1)} %copy-done.6, bf16[1024,768]{1,0:T(8,128)(2,1)S(1)} %copy-done.7, ...), custom_call_target="tpu_custom_call" | custom-call | tf_op jit(solution)/shard_map/expert_grads/pallas_call | solution.py:559
  111.3 8.8 %expert_grads.10 = (bf16[1,1536,384]{2,1,0:T(8,128)(2,1)S(1)}, bf16[1,1536,384]{2,1,0:T(8,128)(2,1)S(1)}, bf16[8,1024,512]{2,1,0:T(8,128)(2,1)}, bf16[8,1024,256]{2,1,0:T(8,128)(2,1)S(1)}) custom-call(s32[63]{0:T(128)S(1)} %fusion.14.order_ref.plan_ref, bf16[1024,768]{1,0:T(8,128)(2,1)S(1)} %copy-done.6, ...), custom_call_target="tpu_custom_call", output_to_operand_aliasing={{2}: (18, {}), {3}: (19, {})} | custom-call | tf_op jit(solution)/shard_map/expert_grads/pallas_call | solution.py:559
  120.6 8.8 %expert_grads.11 = (bf16[1,1536,384]{2,1,0:T(8,128)(2,1)S(1)}, bf16[1,1536,384]{2,1,0:T(8,128)(2,1)S(1)}, bf16[8,1024,512]{2,1,0:T(8,128)(2,1)}, bf16[8,1024,256]{2,1,0:T(8,128)(2,1)S(1)}) custom-call(s32[63]{0:T(128)S(1)} %fusion.14.order_ref.plan_ref, bf16[1024,768]{1,0:T(8,128)(2,1)S(1)} %copy-done.6, ...), custom_call_target="tpu_custom_call", output_to_operand_aliasing={{2}: (18, {}), {3}: (19, {})} | custom-call | tf_op jit(solution)/shard_map/expert_grads/pallas_call | solution.py:559
  129.8 2.5 collective-permute-start.20
  132.3 8.8 %expert_grads.12 = (bf16[1,1536,384]{2,1,0:T(8,128)(2,1)S(1)}, bf16[1,1536,384]{2,1,0:T(8,128)(2,1)S(1)}, bf16[8,1024,512]{2,1,0:T(8,128)(2,1)}, bf16[8,1024,256]{2,1,0:T(8,128)(2,1)S(1)}) custom-call(s32[63]{0:T(128)S(1)} %fusion.14.order_ref.plan_ref, bf16[1024,768]{1,0:T(8,128)(2,1)S(1)} %copy-done.6, ...), custom_call_target="tpu_custom_call", output_to_operand_aliasing={{2}: (18, {}), {3}: (19, {})} | custom-call | tf_op jit(solution)/shard_map/expert_grads/pallas_call | solution.py:559
  146.7 8.8 %expert_grads.13 = (bf16[1,1536,384]{2,1,0:T(8,128)(2,1)S(1)}, bf16[1,1536,384]{2,1,0:T(8,128)(2,1)S(1)}, bf16[8,1024,512]{2,1,0:T(8,128)(2,1)}, bf16[8,1024,256]{2,1,0:T(8,128)(2,1)S(1)}) custom-call(s32[63]{0:T(128)S(1)} %fusion.14.order_ref.plan_ref, bf16[1024,768]{1,0:T(8,128)(2,1)S(1)} %copy-done.6, ...), custom_call_target="tpu_custom_call", output_to_operand_aliasing={{2}: (18, {}), {3}: (19, {})} | custom-call | tf_op jit(solution)/shard_map/expert_grads/pallas_call | solution.py:559
  156.8 8.8 %expert_grads.14 = (bf16[1,1536,384]{2,1,0:T(8,128)(2,1)S(1)}, bf16[1,1536,384]{2,1,0:T(8,128)(2,1)S(1)}, bf16[8,1024,512]{2,1,0:T(8,128)(2,1)}, bf16[8,1024,256]{2,1,0:T(8,128)(2,1)S(1)}) custom-call(s32[63]{0:T(128)S(1)} %fusion.14.order_ref.plan_ref, bf16[1024,768]{1,0:T(8,128)(2,1)S(1)} %copy-done.6, ...), custom_call_target="tpu_custom_call", output_to_operand_aliasing={{2}: (18, {}), {3}: (19, {})} | custom-call | tf_op jit(solution)/shard_map/expert_grads/pallas_call | solution.py:559
  171.4 8.8 %expert_grads.15 = (bf16[1,1536,384]{2,1,0:T(8,128)(2,1)S(1)}, bf16[1,1536,384]{2,1,0:T(8,128)(2,1)S(1)}, bf16[8,1024,512]{2,1,0:T(8,128)(2,1)}, bf16[8,1024,256]{2,1,0:T(8,128)(2,1)S(1)}) custom-call(s32[63]{0:T(128)S(1)} %fusion.14.order_ref.plan_ref, bf16[1024,768]{1,0:T(8,128)(2,1)S(1)} %copy-done.6, ...), custom_call_target="tpu_custom_call", output_to_operand_aliasing={{2}: (18, {}), {3}: (19, {})} | custom-call | tf_op jit(solution)/shard_map/expert_grads/pallas_call | solution.py:559
  183.3 8.8 %expert_grads.16 = (bf16[1,1536,384]{2,1,0:T(8,128)(2,1)S(1)}, bf16[1,1536,384]{2,1,0:T(8,128)(2,1)S(1)}, bf16[8,1024,512]{2,1,0:T(8,128)(2,1)}, bf16[8,1024,256]{2,1,0:T(8,128)(2,1)S(1)}) custom-call(s32[63]{0:T(128)S(1)} %fusion.14.order_ref.plan_ref, bf16[1024,768]{1,0:T(8,128)(2,1)S(1)} %copy-done.6, ...), custom_call_target="tpu_custom_call", output_to_operand_aliasing={{2}: (18, {}), {3}: (19, {})} | custom-call | tf_op jit(solution)/shard_map/expert_grads/pallas_call | solution.py:559
  195.2 3.9 ring_sum.19
  204.8 7.7 %expert_grads.17 = (bf16[1,1536,384]{2,1,0:T(8,128)(2,1)S(1)}, bf16[1,1536,384]{2,1,0:T(8,128)(2,1)S(1)}, bf16[1,1024,512]{2,1,0:T(8,128)(2,1)S(1)}, bf16[1,1024,256]{2,1,0:T(8,128)(2,1)S(1)}) custom-call(s32[63]{0:T(128)S(1)} %fusion.14.order_ref.plan_ref, bf16[1024,768]{1,0:T(8,128)(2,1)S(1)} %copy-done.6, bf16[1024,768]{1,0:T(8,128)(2,1)S(1)} %copy-done.8, ...), custom_call_target="tpu_custom_call" | custom-call | tf_op jit(solution)/shard_map/expert_grads/pallas_call | solution.py:559
  213.5 2.6 ring_sum.20
  217.3 12.4 %mix.4 = bf16[1024,768]{1,0:T(8,128)(2,1)S(1)} custom-call(s32[63]{0:T(128)S(1)} %fusion.14.order_ref.plan_ref, bf16[8,1024,512]{2,1,0:T(8,128)(2,1)} %get-tuple-element.278.refs_0_, bf16[1,1024,512]{2,1,0:T(8,128)(2,1)S(1)} %get-tuple-element.285.refs_1_, ...), custom_call_target="tpu_custom_call" | custom-call | tf_op jit(solution)/shard_map/mix/pallas_call | solution.py:630
  232.7 12.5 %mix.5.own_ref = f32[1024,768]{1,0:T(8,128)S(1)} custom-call(s32[63]{0:T(128)S(1)} %fusion.14.order_ref.plan_ref, bf16[8,1024,512]{2,1,0:T(8,128)(2,1)} %get-tuple-element.278.refs_0_, bf16[1,1024,512]{2,1,0:T(8,128)(2,1)S(1)} %get-tuple-element.285.refs_1_, bf16[16,768,256]{2,1,0:T(8,128)(2,1)} %refs_16_.1, bf16[16,768,256]{2,1,0:T(8,128)(2,1)} %refs_17_.1, ...), custom_call_target="tpu_custom_call" | custom-call | tf_op jit(solution)/shard_map/mix/pallas_call | solution.py:630
  245.3 3.8 ring_sum.22
  250.1 7.2 %mix.6 = bf16[1024,768]{1,0:T(8,128)(2,1)S(1)} custom-call(s32[63]{0:T(128)S(1)} %fusion.14.order_ref.plan_ref, bf16[8,1024,256]{2,1,0:T(8,128)(2,1)} %copy-done, bf16[1,1024,256]{2,1,0:T(8,128)(2,1)S(1)} %get-tuple-element.296.refs_1_, ...), custom_call_target="tpu_custom_call" | custom-call | tf_op jit(solution)/shard_map/mix/pallas_call | solution.py:630
  257.4 3.9 ring_sum.23
  264.1 4.4 chip_sum.1
  271.3 7.3 %mix.7 = f32[1024,768]{1,0:T(8,128)S(1)} custom-call(s32[63]{0:T(128)S(1)} %fusion.14.order_ref.plan_ref, bf16[8,1024,256]{2,1,0:T(8,128)(2,1)} %copy-done, bf16[1,1024,256]{2,1,0:T(8,128)(2,1)S(1)} %get-tuple-element.296.refs_1_, bf16[16,256,768]{2,1,0:T(8,128)(2,1)} %refs_9_.19, bf16[16,256,768]{2,1,0:T(8,128)(2,1)} %refs_9_.19, ...), custom_call_target="tpu_custom_call" | custom-call | tf_op jit(solution)/shard_map/mix/pallas_call | solution.py:630
  278.6 2.8 ring_sum.24
  286.1 23.7 %collective-permute-done.38.came_ref = bf16[1,1536,384]{2,1,0:T(8,128)(2,1)S(1)} collective-permute-done((bf16[1,1536,384]{2,1,0:T(8,128)(2,1)S(1)}, bf16[1,1536,384]{2,1,0:T(8,128)(2,1)S(1)}, u32[]{:S(2)}, u32[]{:S(2)}) %collective-permute-start.38) | collective-permute-done | bytes 1179680 | tf_op jit(solution)/shard_map/ppermute | solution.py:1092
  313.5 6.6 norm_back.1
  327.1 13.1 %attend_back.1.refs_4_ = bf16[1024,640]{1,0:T(8,128)(2,1)} custom-call(s32[3]{0:T(128)} %copy-done.59, bf16[512,640]{1,0:T(8,128)(2,1)} %get-tuple-element.229.own_ref, bf16[512,640]{1,0:T(8,128)(2,1)} %get-tuple-element.233.other_ref, bf16[1024,768]{1,0:T(8,128)(2,1)} %copy-done.18, bf16[1024,768]{1,0:T(8,128)(2,1)} %collective-permute-done.43.grad_c_ref.refs_7_, ...), custom_call_target="tpu_custom_call" | custom-call | tf_op jit(solution)/shard_map/attend_back/pallas_call | solution.py:169
  340.2 3.3 unpack.16
  345.5 3.5 collective-permute-done.47.main_ref
  351.2 13.9 %late_grads.1 = (bf16[8,480,384]{2,1,0:T(8,128)(2,1)}, bf16[8,480,384]{2,1,0:T(8,128)(2,1)}) custom-call(s32[3]{0:T(128)} %copy-done.59, bf16[512,768]{1,0:T(8,128)(2,1)} %get-tuple-element.329.refs_0_, bf16[512,768]{1,0:T(8,128)(2,1)} %get-tuple-element.330.refs_1_, bf16[512,768]{1,0:T(8,128)(2,1)} %get-tuple-element.331.refs_2_, ...), custom_call_target="tpu_custom_call" | custom-call | tf_op jit(solution)/shard_map/late_grads/pallas_call | solution.py:233
  365.1 3.6 unpack.17
  377.1 16.6 %collective-permute-done.51.came_ref = bf16[1248,384]{1,0:T(8,128)(2,1)S(1)} collective-permute-done((bf16[1248,384]{1,0:T(8,128)(2,1)S(1)}, bf16[1248,384]{1,0:T(8,128)(2,1)S(1)}, u32[]{:S(2)}, u32[]{:S(2)}) %collective-permute-start.51) | collective-permute-done | bytes 958496 | tf_op jit(solution)/shard_map/ppermute | solution.py:1092
  399.6 18.6 %collective-permute-done.57.came_ref = bf16[1248,384]{1,0:T(8,128)(2,1)S(1)} collective-permute-done((bf16[1248,384]{1,0:T(8,128)(2,1)S(1)}, bf16[1248,384]{1,0:T(8,128)(2,1)S(1)}, u32[]{:S(2)}, u32[]{:S(2)}) %collective-permute-start.57) | collective-permute-done | bytes 958496 | tf_op jit(solution)/shard_map/ppermute | solution.py:1092
  423.9 18.4 %collective-permute-done.58.came_ref = bf16[1248,384]{1,0:T(8,128)(2,1)S(1)} collective-permute-done((bf16[1248,384]{1,0:T(8,128)(2,1)S(1)}, bf16[1248,384]{1,0:T(8,128)(2,1)S(1)}, u32[]{:S(2)}, u32[]{:S(2)}) %collective-permute-start.58) | collective-permute-done | bytes 958496 | tf_op jit(solution)/shard_map/ppermute | solution.py:1092
  448.0 17.7 %collective-permute-done.60.came_ref = bf16[1248,384]{1,0:T(8,128)(2,1)S(1)} collective-permute-done((bf16[1248,384]{1,0:T(8,128)(2,1)S(1)}, bf16[1248,384]{1,0:T(8,128)(2,1)S(1)}, u32[]{:S(2)}, u32[]{:S(2)}) %collective-permute-start.60) | collective-permute-done | bytes 958496 | tf_op jit(solution)/shard_map/ppermute | solution.py:1092
  470.3 2.6 convolution_convert_fusion
  475.0 13.2 %collective-permute-done.62.came_ref = bf16[1248,384]{1,0:T(8,128)(2,1)} collective-permute-done((bf16[1248,384]{1,0:T(8,128)(2,1)S(1)}, bf16[1248,384]{1,0:T(8,128)(2,1)}, u32[]{:S(2)}, u32[]{:S(2)}) %collective-permute-start.62) | collective-permute-done | bytes 958496 | tf_op jit(solution)/shard_map/ppermute | solution.py:1092
  492.9 3.6 unpack.23
  496.5 3.3 unpack.24
  499.8 2.6 late_main.2.refs_0_
  502.7 2.6 late_main.3.refs_1_
  508.6 3.8 unpack.25
  512.4 11.2 %collective-permute-done.65.came_ref = bf16[1248,384]{1,0:T(8,128)(2,1)} collective-permute-done((bf16[1248,384]{1,0:T(8,128)(2,1)}, bf16[1248,384]{1,0:T(8,128)(2,1)}, u32[]{:S(2)}, u32[]{:S(2)}) %collective-permute-start.65) | collective-permute-done | bytes 958496 | tf_op jit(solution)/shard_map/ppermute | solution.py:1092
  530.6 2.9 convert_add_fusion
  537.4 3.8 unpack.26
  541.3 5.9 collective-permute-done.66.came_ref
  547.2 2.6 late_add.26
  564.5 3.6 unpack.27
  568.1 16.3 %collective-permute-done.71.refs_0_.refs_1_ = bf16[1248,384]{1,0:T(8,128)(2,1)S(1)} collective-permute-done((bf16[1248,384]{1,0:T(8,128)(2,1)}, bf16[1248,384]{1,0:T(8,128)(2,1)S(1)}, u32[]{:S(2)}, u32[]{:S(2)}) %collective-permute-start.71) | collective-permute-done | bytes 958496 | tf_op jit(solution)/shard_map/ppermute | solution.py:1092
  589.0 18.7 %collective-permute-done.73.refs_0_.refs_2_ = bf16[1248,384]{1,0:T(8,128)(2,1)S(1)} collective-permute-done((bf16[1248,384]{1,0:T(8,128)(2,1)S(1)}, bf16[1248,384]{1,0:T(8,128)(2,1)S(1)}, u32[]{:S(2)}, u32[]{:S(2)}) %collective-permute-start.73) | collective-permute-done | bytes 958496 | tf_op jit(solution)/shard_map/ppermute | solution.py:1092
  611.9 18.5 %collective-permute-done.75.refs_0_.refs_3_ = bf16[1248,384]{1,0:T(8,128)(2,1)S(1)} collective-permute-done((bf16[1248,384]{1,0:T(8,128)(2,1)S(1)}, bf16[1248,384]{1,0:T(8,128)(2,1)S(1)}, u32[]{:S(2)}, u32[]{:S(2)}) %collective-permute-start.75) | collective-permute-done | bytes 958496 | tf_op jit(solution)/shard_map/ppermute | solution.py:1092
  636.3 15.8 %collective-permute-done.77.refs_4_.refs_0_ = bf16[1248,384]{1,0:T(8,128)(2,1)S(1)} collective-permute-done((bf16[1248,384]{1,0:T(8,128)(2,1)S(1)}, bf16[1248,384]{1,0:T(8,128)(2,1)S(1)}, u32[]{:S(2)}, u32[]{:S(2)}) %collective-permute-start.77) | collective-permute-done | bytes 958496 | tf_op jit(solution)/shard_map/ppermute | solution.py:1092
  654.3 6.6 collective-permute-done.79.refs_5_
  664.2 5.3 collective-permute-done.81.refs_6_
  673.4 2.6 fusion.2
  679.6 7.5 %unpack_late.1 = (f32[768,512]{1,0:T(8,128)}, f32[768,512]{1,0:T(8,128)}, f32[512,768]{1,0:T(8,128)}, f32[768,768]{1,0:T(8,128)}, f32[768,256]{1,0:T(8,128)}, /*...) custom-call(s32[63]{0:T(128)S(1)} %fusion.14.order_ref.plan_ref, bf16[1248,384]{1,0:T(8,128)(2,1)} %late_join.2.refs_0_, ...), custom_call_target="tpu_custom_call" | custom-call | tf_op jit(solution)/shard_map/unpack_late/pallas_call | solution.py:1005
  (378 shorter events, 183.4 us)
Async XLA Ops:
  0.6 34.5 %collective-permute-start.16 = (bf16[16,768,256]{2,1,0:T(8,128)(2,1)}, bf16[16,768,256]{2,1,0:T(8,128)(2,1)}, u32[]{:S(2)}, u32[]{:S(2)}) collective-permute-start(bf16[16,768,256]{2,1,0:T(8,128)(2,1)} %refs_16_.1), channel_id=1, source_target_pairs={{0,1},{1,0},{2,3},{3,2},{4,5},{5,4},{6,7},{7,6},{8,9},{9,8},{10,11... | collective-permute-start | bytes 18874376 | tf_op jit(solution)/shard_map/ppermute | solution.py:51
  4.9 11.2 %collective-permute-start.3 = (bf16[768,640]{1,0:T(8,128)(2,1)}, bf16[768,640]{1,0:T(8,128)(2,1)S(1)}, u32[]{:S(2)}, u32[]{:S(2)}) collective-permute-start(bf16[768,640]{1,0:T(8,128)(2,1)} %get-tuple-element.228), channel_id=1, source_target_pairs={{0,1},{1,0},{2,3},{3,2},{4,5},{5,4},{6,7},{7,6},{8,9},{9,8},{10,11... | collective-permute-start | bytes 2949128 | tf_op jit(solution)/shard_map/ppermute | solution.py:51
  5.0 11.1 %collective-permute-start.1 = (bf16[512,768]{1,0:T(8,128)(2,1)S(1)}, bf16[512,768]{1,0:T(8,128)(2,1)S(1)}, u32[]{:S(2)}, u32[]{:S(2)}) collective-permute-start(bf16[512,768]{1,0:T(8,128)(2,1)S(1)} %copy-done.62), channel_id=1, source_target_pairs={{0,1},{1,0},{2,3},{3,2},{4,5},{5,4},{6,7},{7,6},{8,9},{9,8},{10,11... | collective-permute-start | bytes 2359304 | tf_op jit(solution)/shard_map/ppermute | solution.py:51
  5.5 27.1 %collective-permute-start = (bf16[512,768]{1,0:T(8,128)(2,1)S(1)}, bf16[512,768]{1,0:T(8,128)(2,1)}, u32[]{:S(2)}, u32[]{:S(2)}) collective-permute-start(bf16[512,768]{1,0:T(8,128)(2,1)S(1)} %copy-done.62), channel_id=1, source_target_pairs={{0,2},{2,0},{1,3},{3,1},{4,6},{6,4},{5,7},{7,5},{8,10},{10,8},{9,1... | collective-permute-start | bytes 2359304 | tf_op jit(solution)/shard_map/ppermute | solution.py:51
  13.2 19.3 %collective-permute-start.4 = (bf16[192,768]{1,0:T(8,128)(2,1)}, bf16[192,768]{1,0:T(8,128)(2,1)S(1)}, u32[]{:S(2)}, u32[]{:S(2)}) collective-permute-start(bf16[192,768]{1,0:T(8,128)(2,1)} %get-tuple-element.230), channel_id=1, source_target_pairs={{0,2},{2,0},{1,3},{3,1},{4,6},{6,4},{5,7},{7,5},{8,10},{10,8},{9,1... | collective-permute-start | bytes 884744 | tf_op jit(solution)/shard_map/ppermute | solution.py:51
  35.0 62.0 %collective-permute-start.18 = (bf16[16,256,768]{2,1,0:T(8,128)(2,1)}, bf16[16,256,768]{2,1,0:T(8,128)(2,1)}, u32[]{:S(2)}, u32[]{:S(2)}) collective-permute-start(bf16[16,256,768]{2,1,0:T(8,128)(2,1)} %refs_9_.19), channel_id=1, source_target_pairs={{0,1},{1,0},{2,3},{3,2},{4,5},{5,4},{6,7},{7,6},{8,9},{9,8},{10,11... | collective-permute-start | bytes 18874376 | tf_op jit(solution)/shard_map/ppermute | solution.py:51
  35.9 61.2 %collective-permute-start.17 = (bf16[16,768,256]{2,1,0:T(8,128)(2,1)}, bf16[16,768,256]{2,1,0:T(8,128)(2,1)}, u32[]{:S(2)}, u32[]{:S(2)}) collective-permute-start(bf16[16,768,256]{2,1,0:T(8,128)(2,1)} %refs_17_.1), channel_id=1, source_target_pairs={{0,1},{1,0},{2,3},{3,2},{4,5},{5,4},{6,7},{7,6},{8,9},{9,8},{10,11... | collective-permute-start | bytes 18874376 | tf_op jit(solution)/shard_map/ppermute | solution.py:51
  36.0 19.8 %collective-permute-start.5 = (bf16[512,768]{1,0:T(8,128)(2,1)S(1)}, bf16[512,768]{1,0:T(8,128)(2,1)S(1)}, u32[]{:S(2)}, u32[]{:S(2)}) collective-permute-start(bf16[512,768]{1,0:T(8,128)(2,1)S(1)} %copy-done.43), channel_id=1, source_target_pairs={{0,2},{2,0},{1,3},{3,1},{4,6},{6,4},{5,7},{7,5},{8,10},{10,8},{9,1... | collective-permute-start | bytes 2359304 | tf_op jit(solution)/shard_map/ppermute | solution.py:51
  39.3 11.5 %collective-permute-start.7 = (bf16[192,768]{1,0:T(8,128)(2,1)S(1)}, bf16[192,768]{1,0:T(8,128)(2,1)S(1)}, u32[]{:S(2)}, u32[]{:S(2)}) collective-permute-start(bf16[192,768]{1,0:T(8,128)(2,1)S(1)} %collective-permute-done.4.refs_0_), channel_id=1, source_target_pairs={{0,8},{4,12},{8,0},{12,4},{16,24},{20,28},{24,16},{28,20},{1,9},{5... | collective-permute-start | bytes 884744 | tf_op jit(solution)/shard_map/ppermute | solution.py:1128
  50.7 17.8 %collective-permute-start.11 = (bf16[768,768]{1,0:T(8,128)(2,1)}, bf16[768,768]{1,0:T(8,128)(2,1)}, u32[]{:S(2)}, u32[]{:S(2)}) collective-permute-start(bf16[768,768]{1,0:T(8,128)(2,1)} %out_ref.1), channel_id=1, source_target_pairs={{0,1},{1,0},{2,3},{3,2},{4,5},{5,4},{6,7},{7,6},{8,9},{9,8},{10,11... | collective-permute-start | bytes 3538952 | tf_op jit(solution)/shard_map/ppermute | solution.py:51
  63.9 20.3 %collective-permute-start.12 = (bf16[1024,384]{1,0:T(8,128)(2,1)}, bf16[1024,384]{1,0:T(8,128)(2,1)}, u32[]{:S(2)}, u32[]{:S(2)}) collective-permute-start(bf16[1024,384]{1,0:T(8,128)(2,1)} %attend.1.refs_4_.refs_5_), channel_id=1, source_target_pairs={{0,2},{2,0},{1,3},{3,1},{4,6},{6,4},{5,7},{7,5},{8,10},{10,8},{9,1... | collective-permute-start | bytes 2359304 | tf_op jit(solution)/shard_map/ppermute | solution.py:51
  67.3 29.7 %collective-permute-start.15 = (bf16[1024,768]{1,0:T(8,128)(2,1)S(1)}, bf16[1024,768]{1,0:T(8,128)(2,1)S(1)}, u32[]{:S(2)}, u32[]{:S(2)}) collective-permute-start(bf16[1024,768]{1,0:T(8,128)(2,1)S(1)} %join.3.refs_2_.refs_4_), channel_id=1, source_target_pairs={{0,1},{1,0},{2,3},{3,2},{4,5},{5,4},{6,7},{7,6},{8,9},{9,8},{10,11... | collective-permute-start | bytes 4718600 | tf_op jit(solution)/shard_map/ppermute | solution.py:51
  68.5 15.8 %collective-permute-start.14 = (bf16[768,768]{1,0:T(8,128)(2,1)}, bf16[768,768]{1,0:T(8,128)(2,1)}, u32[]{:S(2)}, u32[]{:S(2)}) collective-permute-start(bf16[768,768]{1,0:T(8,128)(2,1)} %join.2.refs_4_), channel_id=1, source_target_pairs={{0,1},{1,0},{2,3},{3,2},{4,5},{5,4},{6,7},{7,6},{8,9},{9,8},{10,11... | collective-permute-start | bytes 3538952 | tf_op jit(solution)/shard_map/ppermute | solution.py:51
  109.7 19.7 %collective-permute-start.19 = (bf16[1,1536,384]{2,1,0:T(8,128)(2,1)S(1)}, bf16[1,1536,384]{2,1,0:T(8,128)(2,1)S(1)}, u32[]{:S(2)}, u32[]{:S(2)}) collective-permute-start(bf16[1,1536,384]{2,1,0:T(8,128)(2,1)S(1)} %get-tuple-element.245), channel_id=1, source_target_pairs={{0,8},{8,16},{16,24},{24,28},{28,20},{20,12},{12,4},{4,0},{9,1},{1... | collective-permute-start | bytes 3538952 | tf_op jit(solution)/shard_map/ppermute | solution.py:1092
  120.1 23.3 %collective-permute-start.21 = (bf16[1,1536,384]{2,1,0:T(8,128)(2,1)S(1)}, bf16[1,1536,384]{2,1,0:T(8,128)(2,1)S(1)}, u32[]{:S(2)}, u32[]{:S(2)}) collective-permute-start(bf16[1,1536,384]{2,1,0:T(8,128)(2,1)S(1)} %get-tuple-element.255), channel_id=1, source_target_pairs={{8,0},{16,8},{24,16},{28,24},{20,28},{12,20},{4,12},{0,4},{1,9},{9... | collective-permute-start | bytes 3538952 | tf_op jit(solution)/shard_map/ppermute | solution.py:1092
  129.8 25.8 %collective-permute-start.20 = (bf16[1,1536,384]{2,1,0:T(8,128)(2,1)S(1)}, bf16[1,1536,384]{2,1,0:T(8,128)(2,1)S(1)}, u32[]{:S(2)}, u32[]{:S(2)}) collective-permute-start(bf16[1,1536,384]{2,1,0:T(8,128)(2,1)S(1)} %ring_sum.14), channel_id=1, source_target_pairs={{0,8},{8,16},{16,24},{24,28},{28,20},{20,12},{12,4},{4,0},{9,1},{1... | collective-permute-start | bytes 3538952 | tf_op jit(solution)/shard_map/ppermute | solution.py:1092
  145.1 23.1 %collective-permute-start.23 = (bf16[1,1536,384]{2,1,0:T(8,128)(2,1)}, bf16[1,1536,384]{2,1,0:T(8,128)(2,1)S(1)}, u32[]{:S(2)}, u32[]{:S(2)}) collective-permute-start(bf16[1,1536,384]{2,1,0:T(8,128)(2,1)} %ring_sum.15), channel_id=1, source_target_pairs={{8,0},{16,8},{24,16},{28,24},{20,28},{12,20},{4,12},{0,4},{1,9},{9... | collective-permute-start | bytes 3538952 | tf_op jit(solution)/shard_map/ppermute | solution.py:1092
  155.9 24.4 %collective-permute-start.22 = (bf16[1,1536,384]{2,1,0:T(8,128)(2,1)S(1)}, bf16[1,1536,384]{2,1,0:T(8,128)(2,1)S(1)}, u32[]{:S(2)}, u32[]{:S(2)}) collective-permute-start(bf16[1,1536,384]{2,1,0:T(8,128)(2,1)S(1)} %ring_sum.16), channel_id=1, source_target_pairs={{0,8},{8,16},{16,24},{24,28},{28,20},{20,12},{12,4},{4,0},{9,1},{1... | collective-permute-start | bytes 3538952 | tf_op jit(solution)/shard_map/ppermute | solution.py:1092
  169.8 25.4 %collective-permute-start.25 = (bf16[1,1536,384]{2,1,0:T(8,128)(2,1)}, bf16[1,1536,384]{2,1,0:T(8,128)(2,1)}, u32[]{:S(2)}, u32[]{:S(2)}) collective-permute-start(bf16[1,1536,384]{2,1,0:T(8,128)(2,1)} %ring_sum.17), channel_id=1, source_target_pairs={{8,0},{16,8},{24,16},{28,24},{20,28},{12,20},{4,12},{0,4},{1,9},{9... | collective-permute-start | bytes 3538952 | tf_op jit(solution)/shard_map/ppermute | solution.py:1092
  182.2 31.3 %collective-permute-start.24 = (bf16[1,1536,384]{2,1,0:T(8,128)(2,1)}, bf16[1,1536,384]{2,1,0:T(8,128)(2,1)}, u32[]{:S(2)}, u32[]{:S(2)}) collective-permute-start(bf16[1,1536,384]{2,1,0:T(8,128)(2,1)} %ring_sum.18), channel_id=1, source_target_pairs={{0,8},{8,16},{16,24},{24,28},{28,20},{20,12},{12,4},{4,0},{9,1},{1... | collective-permute-start | bytes 3538952 | tf_op jit(solution)/shard_map/ppermute | solution.py:1092
  199.1 30.6 %collective-permute-start.30 = (bf16[1,1536,384]{2,1,0:T(8,128)(2,1)}, bf16[1,1536,384]{2,1,0:T(8,128)(2,1)S(1)}, u32[]{:S(2)}, u32[]{:S(2)}) collective-permute-start(bf16[1,1536,384]{2,1,0:T(8,128)(2,1)} %ring_sum.19), channel_id=1, source_target_pairs={{8,0},{16,8},{24,16},{28,24},{20,28},{12,20},{4,12},{0,4},{1,9},{9... | collective-permute-start | bytes 3538952 | tf_op jit(solution)/shard_map/ppermute | solution.py:1092
  216.1 29.1 %collective-permute-start.29 = (bf16[1,1536,384]{2,1,0:T(8,128)(2,1)S(1)}, bf16[1,1536,384]{2,1,0:T(8,128)(2,1)}, u32[]{:S(2)}, u32[]{:S(2)}) collective-permute-start(bf16[1,1536,384]{2,1,0:T(8,128)(2,1)S(1)} %ring_sum.20), channel_id=1, source_target_pairs={{0,8},{8,16},{16,24},{24,28},{28,20},{20,12},{12,4},{4,0},{9,1},{1... | collective-permute-start | bytes 3538952 | tf_op jit(solution)/shard_map/ppermute | solution.py:1092
  231.4 26.0 %collective-permute-start.31 = (bf16[1,1536,384]{2,1,0:T(8,128)(2,1)}, bf16[1,1536,384]{2,1,0:T(8,128)(2,1)}, u32[]{:S(2)}, u32[]{:S(2)}) collective-permute-start(bf16[1,1536,384]{2,1,0:T(8,128)(2,1)} %ring_sum.21), channel_id=1, source_target_pairs={{8,0},{16,8},{24,16},{28,24},{20,28},{12,20},{4,12},{0,4},{1,9},{9... | collective-permute-start | bytes 3538952 | tf_op jit(solution)/shard_map/ppermute | solution.py:1092
  232.7 29.5 %collective-permute-start.36 = (bf16[1024,768]{1,0:T(8,128)(2,1)S(1)}, bf16[1024,768]{1,0:T(8,128)(2,1)}, u32[]{:S(2)}, u32[]{:S(2)}) collective-permute-start(bf16[1024,768]{1,0:T(8,128)(2,1)S(1)} %mix.4), channel_id=1, source_target_pairs={{0,1},{1,0},{2,3},{3,2},{4,5},{5,4},{6,7},{7,6},{8,9},{9,8},{10,11... | collective-permute-start | bytes 4718600 | tf_op jit(solution)/shard_map/ppermute | solution.py:51
  249.0 29.5 %collective-permute-start.35 = (bf16[1,1536,384]{2,1,0:T(8,128)(2,1)}, bf16[1,1536,384]{2,1,0:T(8,128)(2,1)}, u32[]{:S(2)}, u32[]{:S(2)}) collective-permute-start(bf16[1,1536,384]{2,1,0:T(8,128)(2,1)} %ring_sum.22), channel_id=1, source_target_pairs={{0,8},{8,16},{16,24},{24,28},{28,20},{20,12},{12,4},{4,0},{9,1},{1... | collective-permute-start | bytes 3538952 | tf_op jit(solution)/shard_map/ppermute | solution.py:1092
  261.3 21.3 %collective-permute-start.34 = (bf16[1,1536,384]{2,1,0:T(8,128)(2,1)}, bf16[1,1536,384]{2,1,0:T(8,128)(2,1)S(1)}, u32[]{:S(2)}, u32[]{:S(2)}) collective-permute-start(bf16[1,1536,384]{2,1,0:T(8,128)(2,1)} %ring_sum.23), channel_id=1, source_target_pairs={{8,0},{16,8},{24,16},{28,24},{20,28},{12,20},{4,12},{0,4},{1,9},{9... | collective-permute-start | bytes 3538952 | tf_op jit(solution)/shard_map/ppermute | solution.py:1092
  270.2 43.3 %collective-permute-start.39 = (bf16[1024,768]{1,0:T(8,128)(2,1)S(1)}, bf16[1024,768]{1,0:T(8,128)(2,1)S(1)}, u32[]{:S(2)}, u32[]{:S(2)}) collective-permute-start(bf16[1024,768]{1,0:T(8,128)(2,1)S(1)} %get-tuple-element.300), channel_id=1, source_target_pairs={{0,2},{2,0},{1,3},{3,1},{4,6},{6,4},{5,7},{7,5},{8,10},{10,8},{9,1... | collective-permute-start | bytes 4718600 | tf_op jit(solution)/shard_map/ppermute | solution.py:51
  281.4 28.4 %collective-permute-start.38 = (bf16[1,1536,384]{2,1,0:T(8,128)(2,1)S(1)}, bf16[1,1536,384]{2,1,0:T(8,128)(2,1)S(1)}, u32[]{:S(2)}, u32[]{:S(2)}) collective-permute-start(bf16[1,1536,384]{2,1,0:T(8,128)(2,1)S(1)} %ring_sum.24), channel_id=1, source_target_pairs={{0,8},{8,16},{16,24},{24,28},{28,20},{20,12},{12,4},{4,0},{9,1},{1... | collective-permute-start | bytes 3538952 | tf_op jit(solution)/shard_map/ppermute | solution.py:1092
  283.0 28.6 %collective-permute-start.37 = (bf16[1,1536,384]{2,1,0:T(8,128)(2,1)S(1)}, bf16[1,1536,384]{2,1,0:T(8,128)(2,1)S(1)}, u32[]{:S(2)}, u32[]{:S(2)}) collective-permute-start(bf16[1,1536,384]{2,1,0:T(8,128)(2,1)S(1)} %ring_sum.25), channel_id=1, source_target_pairs={{8,0},{16,8},{24,16},{28,24},{20,28},{12,20},{4,12},{0,4},{1,9},{9... | collective-permute-start | bytes 3538952 | tf_op jit(solution)/shard_map/ppermute | solution.py:1092
  284.0 29.5 %collective-permute-start.41 = (f32[8,1024]{1,0:T(8,128)S(1)}, f32[8,1024]{1,0:T(8,128)S(1)}, u32[]{:S(2)}, u32[]{:S(2)}) collective-permute-start(f32[8,1024]{1,0:T(8,128)S(1)} %get-tuple-element.315.refs_6_), channel_id=1, source_target_pairs={{0,2},{2,0},{1,3},{3,1},{4,6},{6,4},{5,7},{7,5},{8,10},{10,8},{9,1... | collective-permute-start | bytes 98312 | tf_op jit(solution)/shard_map/ppermute | solution.py:51
  285.2 28.3 %collective-permute-start.42 = (f32[8,1024]{1,0:T(8,128)S(1)}, f32[8,1024]{1,0:T(8,128)S(1)}, u32[]{:S(2)}, u32[]{:S(2)}) collective-permute-start(f32[8,1024]{1,0:T(8,128)S(1)} %collective-permute-done.40.refs_7_), channel_id=1, source_target_pairs={{0,2},{2,0},{1,3},{3,1},{4,6},{6,4},{5,7},{7,5},{8,10},{10,8},{9,1... | collective-permute-start | bytes 98312 | tf_op jit(solution)/shard_map/ppermute | solution.py:51
  320.7 22.8 %collective-permute-start.45 = (bf16[768,384]{1,0:T(8,128)(2,1)}, bf16[768,384]{1,0:T(8,128)(2,1)}, u32[]{:S(2)}, u32[]{:S(2)}) collective-permute-start(bf16[768,384]{1,0:T(8,128)(2,1)} %bitcast.20.refs_0_), channel_id=1, source_target_pairs={{0,8},{8,16},{16,24},{24,28},{28,20},{20,12},{12,4},{4,0},{9,1},{1... | collective-permute-start | bytes 1769480 | tf_op jit(solution)/shard_map/ppermute | solution.py:1092
  322.1 22.4 %collective-permute-start.44 = (bf16[768,384]{1,0:T(8,128)(2,1)}, bf16[768,384]{1,0:T(8,128)(2,1)}, u32[]{:S(2)}, u32[]{:S(2)}) collective-permute-start(bf16[768,384]{1,0:T(8,128)(2,1)} %bitcast.19.refs_1_), channel_id=1, source_target_pairs={{8,0},{16,8},{24,16},{28,24},{20,28},{12,20},{4,12},{0,4},{1,9},{9... | collective-permute-start | bytes 1769480 | tf_op jit(solution)/shard_map/ppermute | solution.py:1092
  324.5 24.5 %collective-permute-start.47 = (bf16[768,384]{1,0:T(8,128)(2,1)}, bf16[768,384]{1,0:T(8,128)(2,1)S(1)}, u32[]{:S(2)}, u32[]{:S(2)}) collective-permute-start(bf16[768,384]{1,0:T(8,128)(2,1)} %bitcast.21.refs_0_), channel_id=1, source_target_pairs={{0,8},{8,16},{16,24},{24,28},{28,20},{20,12},{12,4},{4,0},{9,1},{1... | collective-permute-start | bytes 1769480 | tf_op jit(solution)/shard_map/ppermute | solution.py:1092
  325.9 25.3 %collective-permute-start.49 = (bf16[768,384]{1,0:T(8,128)(2,1)}, bf16[768,384]{1,0:T(8,128)(2,1)S(1)}, u32[]{:S(2)}, u32[]{:S(2)}) collective-permute-start(bf16[768,384]{1,0:T(8,128)(2,1)} %bitcast.22.refs_1_), channel_id=1, source_target_pairs={{8,0},{16,8},{24,16},{28,24},{20,28},{12,20},{4,12},{0,4},{1,9},{9... | collective-permute-start | bytes 1769480 | tf_op jit(solution)/shard_map/ppermute | solution.py:1092
  343.5 25.2 %collective-permute-start.50 = (bf16[768,384]{1,0:T(8,128)(2,1)}, bf16[768,384]{1,0:T(8,128)(2,1)S(1)}, u32[]{:S(2)}, u32[]{:S(2)}) collective-permute-start(bf16[768,384]{1,0:T(8,128)(2,1)} %collective-permute-done.45.refs_0_), channel_id=1, source_target_pairs={{0,8},{8,16},{16,24},{24,28},{28,20},{20,12},{12,4},{4,0},{9,1},{1... | collective-permute-start | bytes 1769480 | tf_op jit(solution)/shard_map/ppermute | solution.py:1092
  344.5 27.9 %collective-permute-start.52 = (bf16[768,384]{1,0:T(8,128)(2,1)}, bf16[768,384]{1,0:T(8,128)(2,1)}, u32[]{:S(2)}, u32[]{:S(2)}) collective-permute-start(bf16[768,384]{1,0:T(8,128)(2,1)} %collective-permute-done.44.refs_1_), channel_id=1, source_target_pairs={{8,0},{16,8},{24,16},{28,24},{20,28},{12,20},{4,12},{0,4},{1,9},{9... | collective-permute-start | bytes 1769480 | tf_op jit(solution)/shard_map/ppermute | solution.py:1092
  371.2 22.5 %collective-permute-start.51 = (bf16[1248,384]{1,0:T(8,128)(2,1)S(1)}, bf16[1248,384]{1,0:T(8,128)(2,1)S(1)}, u32[]{:S(2)}, u32[]{:S(2)}) collective-permute-start(bf16[1248,384]{1,0:T(8,128)(2,1)S(1)} %late_load.2.refs_0_), channel_id=1, source_target_pairs={{0,8},{8,16},{16,24},{24,28},{28,20},{20,12},{12,4},{4,0},{9,1},{1... | collective-permute-start | bytes 2875400 | tf_op jit(solution)/shard_map/ppermute | solution.py:1092
  374.2 22.6 %collective-permute-start.53 = (bf16[1248,384]{1,0:T(8,128)(2,1)S(1)}, bf16[1248,384]{1,0:T(8,128)(2,1)S(1)}, u32[]{:S(2)}, u32[]{:S(2)}) collective-permute-start(bf16[1248,384]{1,0:T(8,128)(2,1)S(1)} %late_load.3.refs_1_), channel_id=1, source_target_pairs={{8,0},{16,8},{24,16},{28,24},{20,28},{12,20},{4,12},{0,4},{1,9},{9... | collective-permute-start | bytes 2875400 | tf_op jit(solution)/shard_map/ppermute | solution.py:1092
  394.5 23.7 %collective-permute-start.57 = (bf16[1248,384]{1,0:T(8,128)(2,1)S(1)}, bf16[1248,384]{1,0:T(8,128)(2,1)S(1)}, u32[]{:S(2)}, u32[]{:S(2)}) collective-permute-start(bf16[1248,384]{1,0:T(8,128)(2,1)S(1)} %late_add.14.refs_0_), channel_id=1, source_target_pairs={{0,8},{8,16},{16,24},{24,28},{28,20},{20,12},{12,4},{4,0},{9,1},{1... | collective-permute-start | bytes 2875400 | tf_op jit(solution)/shard_map/ppermute | solution.py:1092
  397.4 23.6 %collective-permute-start.59 = (bf16[1248,384]{1,0:T(8,128)(2,1)S(1)}, bf16[1248,384]{1,0:T(8,128)(2,1)S(1)}, u32[]{:S(2)}, u32[]{:S(2)}) collective-permute-start(bf16[1248,384]{1,0:T(8,128)(2,1)S(1)} %late_add.15.refs_1_), channel_id=1, source_target_pairs={{8,0},{16,8},{24,16},{28,24},{20,28},{12,20},{4,12},{0,4},{1,9},{9... | collective-permute-start | bytes 2875400 | tf_op jit(solution)/shard_map/ppermute | solution.py:1092
  418.9 23.4 %collective-permute-start.58 = (bf16[1248,384]{1,0:T(8,128)(2,1)S(1)}, bf16[1248,384]{1,0:T(8,128)(2,1)S(1)}, u32[]{:S(2)}, u32[]{:S(2)}) collective-permute-start(bf16[1248,384]{1,0:T(8,128)(2,1)S(1)} %late_add.16.refs_0_), channel_id=1, source_target_pairs={{0,8},{8,16},{16,24},{24,28},{28,20},{20,12},{12,4},{4,0},{9,1},{1... | collective-permute-start | bytes 2875400 | tf_op jit(solution)/shard_map/ppermute | solution.py:1092
  421.8 22.8 %collective-permute-start.61 = (bf16[1248,384]{1,0:T(8,128)(2,1)S(1)}, bf16[1248,384]{1,0:T(8,128)(2,1)S(1)}, u32[]{:S(2)}, u32[]{:S(2)}) collective-permute-start(bf16[1248,384]{1,0:T(8,128)(2,1)S(1)} %late_add.17.refs_1_), channel_id=1, source_target_pairs={{8,0},{16,8},{24,16},{28,24},{20,28},{12,20},{4,12},{0,4},{1,9},{9... | collective-permute-start | bytes 2875400 | tf_op jit(solution)/shard_map/ppermute | solution.py:1092
  443.1 22.6 %collective-permute-start.60 = (bf16[1248,384]{1,0:T(8,128)(2,1)S(1)}, bf16[1248,384]{1,0:T(8,128)(2,1)S(1)}, u32[]{:S(2)}, u32[]{:S(2)}) collective-permute-start(bf16[1248,384]{1,0:T(8,128)(2,1)S(1)} %late_add.18.refs_0_), channel_id=1, source_target_pairs={{0,8},{8,16},{16,24},{24,28},{28,20},{20,12},{12,4},{4,0},{9,1},{1... | collective-permute-start | bytes 2875400 | tf_op jit(solution)/shard_map/ppermute | solution.py:1092
  445.3 24.0 %collective-permute-start.63 = (bf16[1248,384]{1,0:T(8,128)(2,1)S(1)}, bf16[1248,384]{1,0:T(8,128)(2,1)S(1)}, u32[]{:S(2)}, u32[]{:S(2)}) collective-permute-start(bf16[1248,384]{1,0:T(8,128)(2,1)S(1)} %late_add.19.refs_1_), channel_id=1, source_target_pairs={{8,0},{16,8},{24,16},{28,24},{20,28},{12,20},{4,12},{0,4},{1,9},{9... | collective-permute-start | bytes 2875400 | tf_op jit(solution)/shard_map/ppermute | solution.py:1092
  466.4 21.8 %collective-permute-start.62 = (bf16[1248,384]{1,0:T(8,128)(2,1)S(1)}, bf16[1248,384]{1,0:T(8,128)(2,1)}, u32[]{:S(2)}, u32[]{:S(2)}) collective-permute-start(bf16[1248,384]{1,0:T(8,128)(2,1)S(1)} %late_add.20.refs_0_), channel_id=1, source_target_pairs={{0,8},{8,16},{16,24},{24,28},{28,20},{20,12},{12,4},{4,0},{9,1},{1... | collective-permute-start | bytes 2875400 | tf_op jit(solution)/shard_map/ppermute | solution.py:1092
  470.0 20.5 %collective-permute-start.64 = (bf16[1248,384]{1,0:T(8,128)(2,1)S(1)}, bf16[1248,384]{1,0:T(8,128)(2,1)}, u32[]{:S(2)}, u32[]{:S(2)}) collective-permute-start(bf16[1248,384]{1,0:T(8,128)(2,1)S(1)} %late_add.21.refs_1_), channel_id=1, source_target_pairs={{8,0},{16,8},{24,16},{28,24},{20,28},{12,20},{4,12},{0,4},{1,9},{9... | collective-permute-start | bytes 2875400 | tf_op jit(solution)/shard_map/ppermute | solution.py:1092
  472.9 57.7 %collective-permute-start.54 = (bf16[1024,768]{1,0:T(8,128)(2,1)}, bf16[1024,768]{1,0:T(8,128)(2,1)}, u32[]{:S(2)}, u32[]{:S(2)}) collective-permute-start(bf16[1024,768]{1,0:T(8,128)(2,1)} %convolution_convert_fusion), channel_id=1, source_target_pairs={{0,1},{1,0},{2,3},{3,2},{4,5},{5,4},{6,7},{7,6},{8,9},{9,8},{10,11... | collective-permute-start | bytes 4718600 | tf_op jit(solution)/shard_map/ppermute | solution.py:51
  502.4 21.2 %collective-permute-start.65 = (bf16[1248,384]{1,0:T(8,128)(2,1)}, bf16[1248,384]{1,0:T(8,128)(2,1)}, u32[]{:S(2)}, u32[]{:S(2)}) collective-permute-start(bf16[1248,384]{1,0:T(8,128)(2,1)} %late_main.2.refs_0_), channel_id=1, source_target_pairs={{0,8},{8,16},{16,24},{24,28},{28,20},{20,12},{12,4},{4,0},{9,1},{1... | collective-permute-start | bytes 2875400 | tf_op jit(solution)/shard_map/ppermute | solution.py:1092
  505.3 22.4 %collective-permute-start.67 = (bf16[1248,384]{1,0:T(8,128)(2,1)}, bf16[1248,384]{1,0:T(8,128)(2,1)}, u32[]{:S(2)}, u32[]{:S(2)}) collective-permute-start(bf16[1248,384]{1,0:T(8,128)(2,1)} %late_main.3.refs_1_), channel_id=1, source_target_pairs={{8,0},{16,8},{24,16},{28,24},{20,28},{12,20},{4,12},{0,4},{1,9},{9... | collective-permute-start | bytes 2875400 | tf_op jit(solution)/shard_map/ppermute | solution.py:1092
  526.0 21.2 %collective-permute-start.66 = (bf16[1248,384]{1,0:T(8,128)(2,1)}, bf16[1248,384]{1,0:T(8,128)(2,1)}, u32[]{:S(2)}, u32[]{:S(2)}) collective-permute-start(bf16[1248,384]{1,0:T(8,128)(2,1)} %late_add.24.refs_0_), channel_id=1, source_target_pairs={{0,8},{8,16},{16,24},{24,28},{28,20},{20,12},{12,4},{4,0},{9,1},{1... | collective-permute-start | bytes 2875400 | tf_op jit(solution)/shard_map/ppermute | solution.py:1092
  530.1 19.8 %collective-permute-start.68 = (bf16[1248,384]{1,0:T(8,128)(2,1)}, bf16[1248,384]{1,0:T(8,128)(2,1)}, u32[]{:S(2)}, u32[]{:S(2)}) collective-permute-start(bf16[1248,384]{1,0:T(8,128)(2,1)} %late_add.25.refs_1_), channel_id=1, source_target_pairs={{8,0},{16,8},{24,16},{28,24},{20,28},{12,20},{4,12},{0,4},{1,9},{9... | collective-permute-start | bytes 2875400 | tf_op jit(solution)/shard_map/ppermute | solution.py:1092
  536.1 16.7 %collective-permute-start.55 = (bf16[512,768]{1,0:T(8,128)(2,1)}, bf16[512,768]{1,0:T(8,128)(2,1)}, u32[]{:S(2)}, u32[]{:S(2)}) collective-permute-start(bf16[512,768]{1,0:T(8,128)(2,1)} %dynamic-slice_convert_fusion), channel_id=1, source_target_pairs={{0,2},{2,0},{1,3},{3,1},{4,6},{6,4},{5,7},{7,5},{8,10},{10,8},{9,1... | collective-permute-start | bytes 2359304 | tf_op jit(solution)/shard_map/ppermute | solution.py:51
  560.2 24.1 %collective-permute-start.71 = (bf16[1248,384]{1,0:T(8,128)(2,1)}, bf16[1248,384]{1,0:T(8,128)(2,1)S(1)}, u32[]{:S(2)}, u32[]{:S(2)}) collective-permute-start(bf16[1248,384]{1,0:T(8,128)(2,1)} %late_join.2.refs_0_), channel_id=1, source_target_pairs={{0,8},{8,16},{16,24},{24,28},{28,20},{20,12},{12,4},{4,0},{9,1},{1... | collective-permute-start | bytes 2875400 | tf_op jit(solution)/shard_map/ppermute | solution.py:1092
  564.5 22.2 %collective-permute-start.74 = (bf16[1248,384]{1,0:T(8,128)(2,1)}, bf16[1248,384]{1,0:T(8,128)(2,1)S(1)}, u32[]{:S(2)}, u32[]{:S(2)}) collective-permute-start(bf16[1248,384]{1,0:T(8,128)(2,1)} %late_join.3.refs_1_.refs_8_), channel_id=1, source_target_pairs={{8,0},{16,8},{24,16},{28,24},{20,28},{12,20},{4,12},{0,4},{1,9},{9... | collective-permute-start | bytes 2875400 | tf_op jit(solution)/shard_map/ppermute | solution.py:1092
  584.3 23.4 %collective-permute-start.73 = (bf16[1248,384]{1,0:T(8,128)(2,1)S(1)}, bf16[1248,384]{1,0:T(8,128)(2,1)S(1)}, u32[]{:S(2)}, u32[]{:S(2)}) collective-permute-start(bf16[1248,384]{1,0:T(8,128)(2,1)S(1)} %collective-permute-done.71.refs_0_.refs_1_), channel_id=1, source_target_pairs={{0,8},{8,16},{16,24},{24,28},{28,20},{20,12},{12,4},{4,0},{9,1},{1... | collective-permute-start | bytes 2875400 | tf_op jit(solution)/shard_map/ppermute | solution.py:1092
  586.7 23.0 %collective-permute-start.76 = (bf16[1248,384]{1,0:T(8,128)(2,1)S(1)}, bf16[1248,384]{1,0:T(8,128)(2,1)S(1)}, u32[]{:S(2)}, u32[]{:S(2)}) collective-permute-start(bf16[1248,384]{1,0:T(8,128)(2,1)S(1)} %collective-permute-done.74.refs_1_.refs_9_), channel_id=1, source_target_pairs={{8,0},{16,8},{24,16},{28,24},{20,28},{12,20},{4,12},{0,4},{1,9},{9... | collective-permute-start | bytes 2875400 | tf_op jit(solution)/shard_map/ppermute | solution.py:1092
  586.7 45.7 %collective-permute-start.32 = (bf16[1024,768]{1,0:T(8,128)(2,1)S(1)}, bf16[1024,768]{1,0:T(8,128)(2,1)S(1)}, u32[]{:S(2)}, u32[]{:S(2)}) collective-permute-start(bf16[1024,768]{1,0:T(8,128)(2,1)S(1)} %copy-done.28), channel_id=1, source_target_pairs={{0,1},{1,0},{2,3},{3,2},{4,5},{5,4},{6,7},{7,6},{8,9},{9,8},{10,11... | collective-permute-start | bytes 4718600 | tf_op jit(solution)/shard_map/ppermute | solution.py:51
  607.8 22.6 %collective-permute-start.75 = (bf16[1248,384]{1,0:T(8,128)(2,1)S(1)}, bf16[1248,384]{1,0:T(8,128)(2,1)S(1)}, u32[]{:S(2)}, u32[]{:S(2)}) collective-permute-start(bf16[1248,384]{1,0:T(8,128)(2,1)S(1)} %collective-permute-done.73.refs_0_.refs_2_), channel_id=1, source_target_pairs={{0,8},{8,16},{16,24},{24,28},{28,20},{20,12},{12,4},{4,0},{9,1},{1... | collective-permute-start | bytes 2875400 | tf_op jit(solution)/shard_map/ppermute | solution.py:1092
  609.7 22.1 %collective-permute-start.78 = (bf16[1248,384]{1,0:T(8,128)(2,1)S(1)}, bf16[1248,384]{1,0:T(8,128)(2,1)S(1)}, u32[]{:S(2)}, u32[]{:S(2)}) collective-permute-start(bf16[1248,384]{1,0:T(8,128)(2,1)S(1)} %collective-permute-done.76.refs_1_.refs_10_), channel_id=1, source_target_pairs={{8,0},{16,8},{24,16},{28,24},{20,28},{12,20},{4,12},{0,4},{1,9},{9... | collective-permute-start | bytes 2875400 | tf_op jit(solution)/shard_map/ppermute | solution.py:1092
  630.4 21.7 %collective-permute-start.77 = (bf16[1248,384]{1,0:T(8,128)(2,1)S(1)}, bf16[1248,384]{1,0:T(8,128)(2,1)S(1)}, u32[]{:S(2)}, u32[]{:S(2)}) collective-permute-start(bf16[1248,384]{1,0:T(8,128)(2,1)S(1)} %collective-permute-done.75.refs_0_.refs_3_), channel_id=1, source_target_pairs={{0,8},{8,16},{16,24},{24,28},{28,20},{20,12},{12,4},{4,0},{9,1},{1... | collective-permute-start | bytes 2875400 | tf_op jit(solution)/shard_map/ppermute | solution.py:1092
  631.8 21.4 %collective-permute-start.80 = (bf16[1248,384]{1,0:T(8,128)(2,1)S(1)}, bf16[1248,384]{1,0:T(8,128)(2,1)S(1)}, u32[]{:S(2)}, u32[]{:S(2)}) collective-permute-start(bf16[1248,384]{1,0:T(8,128)(2,1)S(1)} %collective-permute-done.78.refs_1_.refs_11_), channel_id=1, source_target_pairs={{8,0},{16,8},{24,16},{28,24},{20,28},{12,20},{4,12},{0,4},{1,9},{9... | collective-permute-start | bytes 2875400 | tf_op jit(solution)/shard_map/ppermute | solution.py:1092
  633.0 30.0 %collective-permute-start.33 = (bf16[512,768]{1,0:T(8,128)(2,1)S(1)}, bf16[512,768]{1,0:T(8,128)(2,1)S(1)}, u32[]{:S(2)}, u32[]{:S(2)}) collective-permute-start(bf16[512,768]{1,0:T(8,128)(2,1)S(1)} %dynamic-slice_convert_fusion.1), channel_id=1, source_target_pairs={{0,2},{2,0},{1,3},{3,1},{4,6},{6,4},{5,7},{7,5},{8,10},{10,8},{9,1... | collective-permute-start | bytes 2359304 | tf_op jit(solution)/shard_map/ppermute | solution.py:51
  663.0 10.5 %collective-permute-start.56 = (f32[512,1]{0,1:T(1,128)S(1)}, f32[512,1]{0,1:T(1,128)S(1)}, u32[]{:S(2)}, u32[]{:S(2)}) collective-permute-start(f32[512,1]{0,1:T(1,128)S(1)} %bitcast.57), channel_id=1, source_target_pairs={{0,1},{1,0},{2,3},{3,2},{4,5},{5,4},{6,7},{7,6},{8,9},{9,8},{10,11... | collective-permute-start | bytes 6152 | tf_op jit(solution)/shard_map/ppermute | solution.py:51
  (105 other events, 796.4 us)

commit v11 on v10

--- a/solution.py
+++ b/solution.py
@@ -807,10 +807,11 @@
                 out_ref[...] = total
 
 
-def ring_sum(came, mine, halved):
+def ring_sum(came, mine, first, halved):
     count, rows, lanes = came.shape
     tiles = 4
     spec = pl.BlockSpec((1, rows // tiles, lanes), lambda i, j: (i, j, 0))
+    term = pl.BlockSpec((1, rows // tiles, lanes), lambda i, j: (first + i, j, 0))
 
     def half(k):
         first = k * tiles // 2
@@ -823,7 +824,7 @@
     return pl.pallas_call(
         ring_sum_kernel,
         grid=(count, tiles),
-        in_specs=[spec, spec],
+        in_specs=[spec, term],
         out_specs=[half(0), half(1)] if halved else spec,
         out_shape=shapes if halved else jax.ShapeDtypeStruct(came.shape, BF16),
         compiler_params=params(16, "arbitrary", "arbitrary"),
@@ -885,32 +886,9 @@
     )(plan, pack, came)
 
 
-def late_main_kernel(main_ref, all_ref, out_ref):
-    out_ref[...] = main_ref[...]
-
-
-def late_main(rows_all, main):
-    lanes = main.shape[1]
-    share = main.shape[0] // RING
-    first = (rows_all.shape[0] - main.shape[0]) // share
-    return pl.pallas_call(
-        late_main_kernel,
-        grid=(RING,),
-        in_specs=[
-            pl.BlockSpec((share, lanes), lambda i: (i, 0)),
-            pl.BlockSpec(memory_space=pl.ANY),
-        ],
-        out_specs=pl.BlockSpec((share, lanes), lambda i: (first + i, 0)),
-        out_shape=jax.ShapeDtypeStruct(rows_all.shape, BF16),
-        input_output_aliases={1: 0},
-        compiler_params=params(16, "arbitrary"),
-        cost_estimate=SMALL,
-        name="late_main",
-    )(main, rows_all)
-
-
-def late_join_kernel(col_ref, mine_ref, other_ref, gains_ref, out_ref):
+def late_join_kernel(col_ref, mine_ref, other_ref, gains_ref, main_ref, out_ref):
     units = 7
+    out_ref[mine_ref.shape[0] :, :] = main_ref[...]
     share = mine_ref.shape[0] // LATE_BLOCKS
     to_rows, to_lanes = unit_slices(2 * units, share)
     blocks = gains_ref.shape[1] // LANES
@@ -928,23 +906,26 @@
     out_ref[to_rows, to_lanes] = gains.astype(BF16)
 
 
-def late_join(col, rows_all, other, gains):
-    rows, lanes = other.shape
-    spec = pl.BlockSpec((rows, lanes), lambda i, c: (0, 0))
+def late_join(col, mine, other, gains, main):
+    rows, lanes = mine.shape
+    total = rows + main.shape[0]
+
+    def all_of(*shape):
+        return pl.BlockSpec(shape, lambda i, c: (0, 0))
+
     return pl.pallas_call(
         late_join_kernel,
         grid_spec=pltpu.PrefetchScalarGridSpec(
             num_scalar_prefetch=1,
             grid=(1,),
-            in_specs=[spec, spec, pl.BlockSpec(gains.shape, lambda i, c: (0, 0))],
-            out_specs=spec,
+            in_specs=[all_of(rows, lanes)] * 2 + [all_of(*gains.shape), all_of(*main.shape)],
+            out_specs=all_of(total, lanes),
         ),
-        out_shape=jax.ShapeDtypeStruct(rows_all.shape, BF16),
-        input_output_aliases={1: 0},
+        out_shape=jax.ShapeDtypeStruct((total, lanes), BF16),
         compiler_params=params(16, "arbitrary"),
         cost_estimate=SMALL,
         name="late_join",
-    )(col, rows_all, other, gains)
+    )(col, mine, other, gains, main)
 
 
 def unpack_late_kernel(first_step, steps, plan_ref, *refs):
@@ -1186,7 +1167,7 @@
             kept,
         )
 
-    first = run(0, each, order, ())
+    first = run(0, 1, order, ())
     kept = first[2:]
     sums = [first[0], first[1]]
     runs = {}
@@ -1198,7 +1179,8 @@
             nonlocal kept
             result = run(first, last, order, tuple(kept))
             kept = result[2:]
-            runs[first] = result[0:2]
+            for at in range(first, last):
+                runs[at] = (*result[0:2], at - first)
             return [kept[0]]
 
         return work
@@ -1244,7 +1226,7 @@
                 routed[4 + half : 5 + half],
                 shared[4 + half : 5 + half],
             )
-            return [mixed[False, half]] + ([] if half else [normed["tie"]])
+            return [mixed[False, half]]
 
         return work
 
@@ -1289,9 +1271,13 @@
         )
         return normed["packs"]
 
-    tasks = [work_experts(at, at + each) for at in range(each, pairs_total, each)]
-    tasks += [work_shared, work_back(1), work_back(0), work_out(1), work_out(0)]
-    later = [[work_hidden, work_attend], [work_late]]
+    def work_tie(order, ties):
+        return [normed["tie"]]
+
+    tasks = [work_experts(at, min(at + 2, pairs_total)) for at in range(1, pairs_total, 2)]
+    tasks += [work_shared, work_back(1), work_back(0), None, work_out(0), work_tie]
+    ends = [work_hidden, work_attend, work_late]
+    tasks += [None] * (2 * ring_size - 2 - len(tasks) - len(ends)) + ends
     got = [None, None]
     got[0] = send(sums[0], 0)
     tasks.pop(0)(after(order, *sums), sums)
@@ -1302,7 +1288,8 @@
             task = tasks.pop(0) if tasks else None
             if task:
                 last = task(after(order, *last), last)
-            sums[k] = ring_sum(after(got[k], *last), runs[each * s][k], s + 1 == ring_size)
+            mine = runs[s]
+            sums[k] = ring_sum(after(got[k], *last), mine[k], mine[2], s + 1 == ring_size)
             if s + 1 < ring_size:
                 got[k] = send(sums[k], k)
             else:
@@ -1316,9 +1303,6 @@
     def back_to_tokens(ties):
         hidden_grad = normed["hidden"]
         qkv_grad = after(normed["qkv"], *ties)
-        ffn_sum = mixed[False, 0] + swap(mixed[False, 1], "col").astype(F32)
-        ffn_rows = my_rows(ffn_sum) + swap(their_rows(ffn_sum).astype(BF16), "row").astype(F32)
-        block_out = (my_rows(hidden) + ffn_rows).astype(BF16)
         here = jnp.concatenate(
             [halves(w, 1, col)[0] for w in (w_query, w_key, w_value)], axis=1
         )
@@ -1340,85 +1324,68 @@
 
         gain_parts = jnp.concatenate([gain_attn_part[None], normed["gain"]], axis=0)
         normed["gains"] = across_rings(gain_parts + swap(gain_parts, "row"))
-        normed["outs"] = (block_out, tokens_grad)
+        normed["tokens_grad"] = tokens_grad
+
+    def block_rows(ties):
+        ffn_sum = after(mixed[False, 0], *ties) + swap(mixed[False, 1], "col").astype(F32)
+        ffn_rows = my_rows(ffn_sum) + swap(their_rows(ffn_sum).astype(BF16), "row").astype(F32)
+        block_out = (my_rows(hidden) + ffn_rows).astype(BF16)
+        normed["block_out"] = block_out
 
     shapes = [w_gate.shape, w_up.shape, w_down.shape]
     placed = ()
     late_out = [[], []]
-    late_start = len(later)
     last, got = [], [None, None]
-    moves = [(wave, step) for wave in range(2) for step in range(wave, ring_size - 1)]
+    moves = [(wave, step) for wave in range(2) for step in range(ring_size - 1)]
     for number, (wave, step) in enumerate(moves):
-        late_step = number - late_start
         current = [None, None]
         copies = [None, None]
+        turn = number == ring_size - 1
         for k in range(2):
+            at = chunks_first + 2 * number + k
+            pack = normed["packs"][k]
             if number == 0:
-                current[k] = after(waves[0][k], *last) if last else waves[0][k]
+                current[k] = late_load(plan, at, pack, after(waves[0][k], *last))
+            elif number < ring_size - 1:
+                current[k] = late_add(plan, at, pack, after(got[k], *last))
+            elif turn:
+                current[k], copies[k] = late_add(plan, at, pack, after(got[k], *last), True)
+            else:
+                current[k] = after(got[k], *last)
+            last = [current[k]]
+            if not turn:
                 got[k] = send(current[k], k)
-                last = [current[k]]
-                continue
-            current[k] = after(got[k], *last)
-            if late_step < 0:
+        if turn:
+            placed = unpack(plan, experts + 2 * (ring_size - 1), 0, current, shapes, placed)
+            others = [swap(across_rings(values), "col") for values in copies]
+            for k in range(2):
+                current[k] = late_join(
+                    col_ref, after(copies[k], *last), others[1 - k], normed["gains"], waves[1][k]
+                )
                 got[k] = send(current[k], k)
-                last = [current[k]]
-                continue
-            at = chunks_first + 2 * late_step + k
-            if late_step == 0:
-                current[k] = late_load(plan, at, normed["packs"][k], current[k])
-            elif late_step < ring_size - 1:
-                current[k] = late_add(plan, at, normed["packs"][k], current[k])
-            elif late_step == ring_size - 1:
-                current[k], copies[k] = late_add(plan, at, normed["packs"][k], current[k], True)
-            last = [current[k]]
-            if not (wave == 1 and step == 1) and late_step != ring_size - 1:
-                got[k] = send(current[k], k)
-                if late_step >= ring_size:
-                    late_out[k].append(current[k])
-        switch = wave == 1 and step == 1
-        if switch or late_step == ring_size - 1:
-            if late_step == ring_size - 1:
-                others = [swap(across_rings(values), "col") for values in copies]
-                current = [
-                    late_join(col_ref, current[k], others[1 - k], normed["gains"])
-                    for k in range(2)
-                ]
-            if switch:
-                placed = unpack(
-                    plan, experts + 2 * (ring_size - 1), 0, current, shapes, placed
-                )
-                placed = unpack(plan, experts, 1, waves[1], shapes, placed)
-                current = [late_main(after(current[k], placed[0]), early[k]) for k in range(2)]
+                last = work_out(1)(after(order, current[k]), ()) if k == 0 else [current[k]]
+        if number >= ring_size - 1:
             for k in range(2):
-                got[k] = send(current[k], k)
-                if late_step >= ring_size - 1:
-                    late_out[k].append(current[k])
-            last = [current[1]]
-        if number == 0:
-            early = [send(after(waves[1][k], *current), k) for k in range(2)]
-        if number < len(later):
-            for work in later[number]:
-                if number == 1:
-                    last = [*last, *early]
-                last = work(after(order, *last), last)
+                late_out[k].append(current[k])
         placed = unpack(
             plan, experts + 2 * step, wave, [after(current[0], *last), current[1]], shapes, placed
         )
         last = placed[0:1]
-        if number == 3:
+        if number == 2:
             back_to_tokens(last)
-    for late_step in range(len(moves) - late_start, late_total + 1):
-        for k in range(2):
-            values = after(got[k], *last)
-            late_out[k].append(values)
-            if late_step < late_total:
-                got[k] = send(values[: LATE_BLOCKS * (local_features // ring_size)], k)
-            last = [values]
-        if late_step == len(moves) - late_start:
-            whole_chunks = [late_out[k][-1] for k in range(2)]
-            placed = unpack(
-                plan, experts + 2 * (ring_size - 1), 1, whole_chunks, shapes, placed
-            )
+        if number == ring_size + 1:
+            block_rows(last)
+    for k in range(2):
+        late_out[k].append(after(got[k], *last))
+        last = [late_out[k][-1]]
+    placed = unpack(
+        plan,
+        experts + 2 * (ring_size - 1),
+        1,
+        [late_out[k][-1] for k in range(2)],
+        shapes,
+        placed,
+    )
     gate_grad, up_grad, down_grad = placed
     shapes = [w.shape for w in (w_shared_gate, w_shared_up, w_shared_down)]
     shapes += [w.shape for w in (w_query, w_key, w_value, w_out)] + [gains.shape]
@@ -1428,7 +1395,8 @@
 
 
     return (
-        *normed["outs"],
+        normed["block_out"],
+        normed["tokens_grad"],
         gain_grads[0],
         query_grad,
         key_grad,

time: 698 us -> 705 us (1.010)
  waiting for transfers between devices: 264 us -> 295 us
  Pallas kernels: 306 us -> 284 us
  starting transfers between devices: 78.5 us -> 60.3 us
  local copies, waits for them, and re-layouts: 23.6 us -> 37.7 us
    ppermute x48 -> x42, waiting for transfers between devices: 222 us -> 256 us  [send(): return lax.ppermute(values, ('dp', 'col'), routes_of[which])]
    ppermute x48 -> x42, starting transfers between devices: 54.2 us -> 35.9 us  [send(): return lax.ppermute(values, ('dp', 'col'), routes_of[which])]
    unnamed x166 -> x208, local copies, waits for them, and re-layouts: 21.1 us -> 35.3 us
    pallas_call x9 -> x6, Pallas kernels: 78.8 us -> 72.3 us  [expert_grads(): pl.pallas_call(functools.partial(expert_kernel, shared, aliased, first),...]
    pallas_call x16 -> x14, Pallas kernels: 33.9 us -> 27.8 us  [ring_sum(): pl.pallas_call(ring_sum_kernel, grid=(count, tiles), in_specs=[spec, term...]
  transfers between devices with their start and end apart: 86 -> 80, of which waited for: 36 -> 41; matrix products, arithmetic and copies ran while one was open for 2% -> 2% of each run, Pallas kernels for 41% -> 37%
where the time goes in v11:
time: 705 us; the launch traced here: 695 us
  waiting for transfers between devices  295 us (42%)
  Pallas kernels  284 us (40%)
  starting transfers between devices  60.3 us (9%)
  local copies, waits for them, and re-layouts  37.7 us (5%)
  other arithmetic  8.65 us (1%)
    ppermute x42, waiting for transfers between devices, send(): return lax.ppermute(values, ('dp', 'col'), routes_of[which])  256 us
    pallas_call x6, Pallas kernels, expert_grads(): pl.pallas_call(functools.partial(expert_kernel, shared, aliased, first),...  72.3 us
    pallas_call x4, Pallas kernels, mix(): pl.pallas_call(functools.partial(mix_kernel, back, group), grid_spec=pltp...  39.9 us
    pallas_call x16, Pallas kernels, unpack(): pl.pallas_call(functools.partial(unpack_kernel, aliased), grid_spec=pltpu...  38.4 us
    ppermute x35, waiting for transfers between devices, swap(): return lax.ppermute(values, axis, [(0, 1), (1, 0)])  37.2 us
    ppermute x42, starting transfers between devices, send(): return lax.ppermute(values, ('dp', 'col'), routes_of[which])  35.9 us
    unnamed x208, local copies, waits for them, and re-layouts  35.3 us
    pallas_call x14, Pallas kernels, ring_sum(): pl.pallas_call(ring_sum_kernel, grid=(count, tiles), in_specs=[spec, term...  27.8 us
  transfers between devices with their start and end apart: 80, of which 41 were waited for; matrix products, arithmetic and copies ran while one was open for 2% of the time, Pallas kernels for 37%

profile of v11, /device:TPU:0, one launch (start us, length us, event | category | flops | bytes accessed | tf_op | source)
XLA Modules:
  0.0 694.6 jit_solution(12552136256502050711)
XLA Ops:
  1.8 3.1 their_columns.1
  5.3 2.6 collective-permute-start
  8.2 5.0 collective-permute-done.2.gains_c_ref.refs_7_
  13.3 2.9 collective-permute-start.4
  18.0 4.5 project.2
  22.5 9.9 %collective-permute-done.4.refs_0_ = bf16[192,768]{1,0:T(8,128)(2,1)S(1)} collective-permute-done((bf16[192,768]{1,0:T(8,128)(2,1)}, bf16[192,768]{1,0:T(8,128)(2,1)S(1)}, u32[]{:S(2)}, u32[]{:S(2)}) %collective-permute-start.4) | collective-permute-done | bytes 294944 | tf_op jit(solution)/shard_map/ppermute | solution.py:51
  40.7 4.5 project.3
  47.4 2.5 collective-permute-start.9
  50.7 5.0 collective-permute-done.5.refs_1_
  57.5 6.3 attend.1.refs_4_.refs_5_
  69.5 9.0 %hidden_before.1 = (f32[1024,768]{1,0:T(8,128)}, f32[1024,768]{1,0:T(8,128)}) custom-call(s32[3]{0:T(128)} %copy-done.76, bf16[512,768]{1,0:T(8,128)(2,1)} %refs_0_.2, bf16[512,768]{1,0:T(8,128)(2,1)} %copy-done.93, bf16[512,768]{1,0:T(8,128)(2,1)} %collective-permute-done.own_ref.refs_2_, bf16[512,768]{1,0:T(8,128)(2,1)} %copy-done.94, ...), custom_call_target="tpu_custom_call" | custom-call | flops 2415919104 | bytes 12582912 | tf_op jit(solution)/shard_map/hidden_before/pallas_call | solution.py:414
  78.5 5.6 collective-permute-done.12.refs_2_
  87.5 9.4 %hidden_after.1 = (f32[1024,768]{1,0:T(8,128)}, bf16[1024,768]{1,0:T(8,128)(2,1)}, bf16[1024,768]{1,0:T(8,128)(2,1)}, f32[1024,1]{1,0:T(8,128)}) custom-call(s32[3]{0:T(128)} %copy-done.76, f32[1024,768]{1,0:T(8,128)} %get-tuple-element.218.refs_0_, f32[1024,768]{1,0:T(8,128)} %get-tuple-element.219.refs_1_, ...), custom_call_target="tpu_custom_call" | custom-call | tf_op jit(solution)/shard_map/hidden_after/pallas_call | solution.py:436
  100.3 9.0 %expert_grads.6 = (bf16[1,1536,384]{2,1,0:T(8,128)(2,1)S(1)}, bf16[1,1536,384]{2,1,0:T(8,128)(2,1)S(1)}, bf16[8,1024,512]{2,1,0:T(8,128)(2,1)}, bf16[8,1024,256]{2,1,0:T(8,128)(2,1)S(1)}) custom-call(s32[63]{0:T(128)S(1)} %fusion.14.order_ref.plan_ref, bf16[1024,768]{1,0:T(8,128)(2,1)S(1)} %copy-done.9, bf16[1024,768]{1,0:T(8,128)(2,1)S(1)} %copy-done.10, ...), custom_call_target="tpu_custom_call" | custom-call | tf_op jit(solution)/shard_map/expert_grads/pallas_call | solution.py:559
  112.9 15.2 %expert_grads.7 = (bf16[2,1536,384]{2,1,0:T(8,128)(2,1)S(1)}, bf16[2,1536,384]{2,1,0:T(8,128)(2,1)S(1)}, bf16[8,1024,512]{2,1,0:T(8,128)(2,1)}, bf16[8,1024,256]{2,1,0:T(8,128)(2,1)}) custom-call(s32[63]{0:T(128)S(1)} %fusion.14.order_ref.plan_ref, bf16[1024,768]{1,0:T(8,128)(2,1)S(1)} %copy-done.9, ...), custom_call_target="tpu_custom_call", output_to_operand_aliasing={{2}: (18, {}), {3}: (19, {})} | custom-call | tf_op jit(solution)/shard_map/expert_grads/pallas_call | solution.py:559
  128.6 15.6 %expert_grads.8 = (bf16[2,1536,384]{2,1,0:T(8,128)(2,1)S(1)}, bf16[2,1536,384]{2,1,0:T(8,128)(2,1)S(1)}, bf16[8,1024,512]{2,1,0:T(8,128)(2,1)}, bf16[8,1024,256]{2,1,0:T(8,128)(2,1)}) custom-call(s32[63]{0:T(128)S(1)} %fusion.14.order_ref.plan_ref, bf16[1024,768]{1,0:T(8,128)(2,1)S(1)} %copy-done.9, ...), custom_call_target="tpu_custom_call", output_to_operand_aliasing={{2}: (18, {}), {3}: (19, {})} | custom-call | tf_op jit(solution)/shard_map/expert_grads/pallas_call | solution.py:559
  148.3 15.4 %expert_grads.9 = (bf16[2,1536,384]{2,1,0:T(8,128)(2,1)S(1)}, bf16[2,1536,384]{2,1,0:T(8,128)(2,1)S(1)}, bf16[8,1024,512]{2,1,0:T(8,128)(2,1)}, bf16[8,1024,256]{2,1,0:T(8,128)(2,1)}) custom-call(s32[63]{0:T(128)S(1)} %fusion.14.order_ref.plan_ref, bf16[1024,768]{1,0:T(8,128)(2,1)S(1)} %copy-done.9, ...), custom_call_target="tpu_custom_call", output_to_operand_aliasing={{2}: (18, {}), {3}: (19, {})} | custom-call | tf_op jit(solution)/shard_map/expert_grads/pallas_call | solution.py:559
  169.2 8.8 %expert_grads.10 = (bf16[1,1536,384]{2,1,0:T(8,128)(2,1)S(1)}, bf16[1,1536,384]{2,1,0:T(8,128)(2,1)S(1)}, bf16[8,1024,512]{2,1,0:T(8,128)(2,1)}, bf16[8,1024,256]{2,1,0:T(8,128)(2,1)S(1)}) custom-call(s32[63]{0:T(128)S(1)} %fusion.14.order_ref.plan_ref, bf16[1024,768]{1,0:T(8,128)(2,1)S(1)} %copy-done.9, ...), custom_call_target="tpu_custom_call", output_to_operand_aliasing={{2}: (18, {}), {3}: (19, {})} | custom-call | tf_op jit(solution)/shard_map/expert_grads/pallas_call | solution.py:559
  180.1 3.2 copy-done.39
  186.6 8.3 %expert_grads.11 = (bf16[1,1536,384]{2,1,0:T(8,128)(2,1)S(1)}, bf16[1,1536,384]{2,1,0:T(8,128)(2,1)S(1)}, bf16[1,1024,512]{2,1,0:T(8,128)(2,1)S(1)}, bf16[1,1024,256]{2,1,0:T(8,128)(2,1)S(1)}) custom-call(s32[63]{0:T(128)S(1)} %fusion.14.order_ref.plan_ref, bf16[1024,768]{1,0:T(8,128)(2,1)S(1)} %copy-done.9, bf16[1024,768]{1,0:T(8,128)(2,1)S(1)} %copy-done.11, ...), custom_call_target="tpu_custom_call" | custom-call | tf_op jit(solution)/shard_map/expert_grads/pallas_call | solution.py:559
  196.8 12.8 %mix.4 = bf16[1024,768]{1,0:T(8,128)(2,1)S(1)} custom-call(s32[63]{0:T(128)S(1)} %fusion.14.order_ref.plan_ref, bf16[8,1024,512]{2,1,0:T(8,128)(2,1)} %get-tuple-element.244.refs_0_, bf16[1,1024,512]{2,1,0:T(8,128)(2,1)S(1)} %get-tuple-element.250.refs_1_, ...), custom_call_target="tpu_custom_call" | custom-call | tf_op jit(solution)/shard_map/mix/pallas_call | solution.py:630
  209.7 3.5 ring_sum.18
  214.8 12.5 %mix.5.own_ref = f32[1024,768]{1,0:T(8,128)S(1)} custom-call(s32[63]{0:T(128)S(1)} %fusion.14.order_ref.plan_ref, bf16[8,1024,512]{2,1,0:T(8,128)(2,1)} %get-tuple-element.244.refs_0_, bf16[1,1024,512]{2,1,0:T(8,128)(2,1)S(1)} %get-tuple-element.250.refs_1_, bf16[16,768,256]{2,1,0:T(8,128)(2,1)} %refs_16_.1, bf16[16,768,256]{2,1,0:T(8,128)(2,1)} %refs_17_.1, ...), custom_call_target="tpu_custom_call" | custom-call | tf_op jit(solution)/shard_map/mix/pallas_call | solution.py:630
  234.9 4.8 chip_sum.1
  244.5 7.4 %mix.6 = f32[1024,768]{1,0:T(8,128)S(1)} custom-call(s32[63]{0:T(128)S(1)} %fusion.14.order_ref.plan_ref, bf16[8,1024,256]{2,1,0:T(8,128)(2,1)} %copy-done.7, bf16[1,1024,256]{2,1,0:T(8,128)(2,1)S(1)} %get-tuple-element.261.refs_1_, bf16[16,256,768]{2,1,0:T(8,128)(2,1)} %refs_9_.13, bf16[16,256,768]{2,1,0:T(8,128)(2,1)} %refs_9_.13, ...), custom_call_target="tpu_custom_call" | custom-call | tf_op jit(solution)/shard_map/mix/pallas_call | solution.py:630
  252.2 3.5 ring_sum.22
  258.0 4.4 collective-permute-done.29.came_ref
  262.8 11.2 %collective-permute-done.33.came_ref = bf16[1,1536,384]{2,1,0:T(8,128)(2,1)S(1)} collective-permute-done((bf16[1,1536,384]{2,1,0:T(8,128)(2,1)S(1)}, bf16[1,1536,384]{2,1,0:T(8,128)(2,1)S(1)}, u32[]{:S(2)}, u32[]{:S(2)}) %collective-permute-start.33) | collective-permute-done | bytes 1179680 | tf_op jit(solution)/shard_map/ppermute | solution.py:1073
  277.4 6.9 norm_back.1
  286.5 26.4 %collective-permute-done.31.came_ref = bf16[1,1536,384]{2,1,0:T(8,128)(2,1)S(1)} collective-permute-done((bf16[1,1536,384]{2,1,0:T(8,128)(2,1)S(1)}, bf16[1,1536,384]{2,1,0:T(8,128)(2,1)S(1)}, u32[]{:S(2)}, u32[]{:S(2)}) %collective-permute-start.31) | collective-permute-done | bytes 1179680 | tf_op jit(solution)/shard_map/ppermute | solution.py:1073
  316.5 13.1 %attend_back.1.refs_4_ = bf16[1024,640]{1,0:T(8,128)(2,1)} custom-call(s32[3]{0:T(128)} %copy-done.76, bf16[512,640]{1,0:T(8,128)(2,1)} %get-tuple-element.210.own_ref, bf16[512,640]{1,0:T(8,128)(2,1)} %get-tuple-element.214.other_ref, bf16[1024,768]{1,0:T(8,128)(2,1)} %copy-done.41, bf16[1024,768]{1,0:T(8,128)(2,1)} %collective-permute-done.39.grad_c_ref.refs_7_, ...), custom_call_target="tpu_custom_call" | custom-call | tf_op jit(solution)/shard_map/attend_back/pallas_call | solution.py:169
  329.6 3.5 ring_sum.25
  333.2 13.9 %late_grads.1 = (bf16[8,480,384]{2,1,0:T(8,128)(2,1)}, bf16[8,480,384]{2,1,0:T(8,128)(2,1)}) custom-call(s32[3]{0:T(128)} %copy-done.76, bf16[512,768]{1,0:T(8,128)(2,1)} %get-tuple-element.277.refs_0_, bf16[512,768]{1,0:T(8,128)(2,1)} %get-tuple-element.278.refs_1_, bf16[512,768]{1,0:T(8,128)(2,1)} %get-tuple-element.279.refs_2_, ...), custom_call_target="tpu_custom_call" | custom-call | tf_op jit(solution)/shard_map/late_grads/pallas_call | solution.py:233
  360.0 16.5 %collective-permute-done.41.came_ref = bf16[1248,384]{1,0:T(8,128)(2,1)S(1)} collective-permute-done((bf16[1248,384]{1,0:T(8,128)(2,1)S(1)}, bf16[1248,384]{1,0:T(8,128)(2,1)S(1)}, u32[]{:S(2)}, u32[]{:S(2)}) %collective-permute-start.41) | collective-permute-done | bytes 958496 | tf_op jit(solution)/shard_map/ppermute | solution.py:1073
  382.2 18.7 %collective-permute-done.43.came_ref = bf16[1248,384]{1,0:T(8,128)(2,1)S(1)} collective-permute-done((bf16[1248,384]{1,0:T(8,128)(2,1)S(1)}, bf16[1248,384]{1,0:T(8,128)(2,1)S(1)}, u32[]{:S(2)}, u32[]{:S(2)}) %collective-permute-start.43) | collective-permute-done | bytes 958496 | tf_op jit(solution)/shard_map/ppermute | solution.py:1073
  406.6 18.0 %collective-permute-done.45.came_ref = bf16[1248,384]{1,0:T(8,128)(2,1)S(1)} collective-permute-done((bf16[1248,384]{1,0:T(8,128)(2,1)S(1)}, bf16[1248,384]{1,0:T(8,128)(2,1)S(1)}, u32[]{:S(2)}, u32[]{:S(2)}) %collective-permute-start.45) | collective-permute-done | bytes 958496 | tf_op jit(solution)/shard_map/ppermute | solution.py:1073
  430.8 16.5 %collective-permute-done.47.came_ref = bf16[1248,384]{1,0:T(8,128)(2,1)S(1)} collective-permute-done((bf16[1248,384]{1,0:T(8,128)(2,1)S(1)}, bf16[1248,384]{1,0:T(8,128)(2,1)S(1)}, u32[]{:S(2)}, u32[]{:S(2)}) %collective-permute-start.47) | collective-permute-done | bytes 958496 | tf_op jit(solution)/shard_map/ppermute | solution.py:1073
  448.4 3.6 collective-permute-done.50.came_ref
  453.1 2.6 convolution_convert_fusion
  457.8 11.4 %collective-permute-done.49.came_ref = bf16[1248,384]{1,0:T(8,128)(2,1)} collective-permute-done((bf16[1248,384]{1,0:T(8,128)(2,1)S(1)}, bf16[1248,384]{1,0:T(8,128)(2,1)}, u32[]{:S(2)}, u32[]{:S(2)}) %collective-permute-start.49) | collective-permute-done | bytes 958496 | tf_op jit(solution)/shard_map/ppermute | solution.py:1073
  477.6 3.8 unpack.21
  481.4 11.5 %collective-permute-done.51.came_ref = bf16[1248,384]{1,0:T(8,128)(2,1)} collective-permute-done((bf16[1248,384]{1,0:T(8,128)(2,1)}, bf16[1248,384]{1,0:T(8,128)(2,1)}, u32[]{:S(2)}, u32[]{:S(2)}) %collective-permute-start.51) | collective-permute-done | bytes 958496 | tf_op jit(solution)/shard_map/ppermute | solution.py:1073
  497.6 2.5 collective-permute-start.55
  500.1 2.9 convert_add_fusion.1
  507.5 3.8 unpack.22
  511.4 4.7 collective-permute-done.53.came_ref
  516.1 2.7 late_add.26
  524.7 2.6 collective-permute-done.59
  527.6 7.2 %mix.7 = bf16[1024,768]{1,0:T(8,128)(2,1)S(1)} custom-call(s32[63]{0:T(128)S(1)} %fusion.14.order_ref.plan_ref, bf16[8,1024,256]{2,1,0:T(8,128)(2,1)} %copy-done.7, bf16[1,1024,256]{2,1,0:T(8,128)(2,1)S(1)} %copy-done.57, bf16[16,256,768]{2,1,0:T(8,128)(2,1)} %collective-permute-done.18.refs_10_.refs_16_.refs_2_.refs_3_.refs_4_.refs_5_.refs_6_.refs_7_.refs_8_.refs_9_, ...), custom_call_target="tpu_custom_call" | custom-call | tf_op jit(solution)/shard_map/mix/pallas_call | solution.py:630
  537.0 3.6 unpack.23
  544.8 10.6 %collective-permute-done.65.refs_1_.refs_9_ = bf16[1248,384]{1,0:T(8,128)(2,1)S(1)} collective-permute-done((bf16[1248,384]{1,0:T(8,128)(2,1)S(1)}, bf16[1248,384]{1,0:T(8,128)(2,1)S(1)}, u32[]{:S(2)}, u32[]{:S(2)}) %collective-permute-start.65) | collective-permute-done | bytes 958496 | tf_op jit(solution)/shard_map/ppermute | solution.py:1073
  559.2 6.9 collective-permute-done.64.refs_0_.refs_2_
  566.2 10.7 %collective-permute-done.66.refs_1_.refs_10_ = bf16[1248,384]{1,0:T(8,128)(2,1)S(1)} collective-permute-done((bf16[1248,384]{1,0:T(8,128)(2,1)S(1)}, bf16[1248,384]{1,0:T(8,128)(2,1)S(1)}, u32[]{:S(2)}, u32[]{:S(2)}) %collective-permute-start.66) | collective-permute-done | bytes 958496 | tf_op jit(solution)/shard_map/ppermute | solution.py:1073
  580.6 7.3 %collective-permute-done.70.refs_0_.refs_3_ = bf16[1248,384]{1,0:T(8,128)(2,1)S(1)} collective-permute-done((bf16[1248,384]{1,0:T(8,128)(2,1)S(1)}, bf16[1248,384]{1,0:T(8,128)(2,1)S(1)}, u32[]{:S(2)}, u32[]{:S(2)}) %collective-permute-start.70) | collective-permute-done | bytes 958496 | tf_op jit(solution)/shard_map/ppermute | solution.py:1073
  587.9 10.2 %collective-permute-done.72.refs_1_.refs_11_ = bf16[1248,384]{1,0:T(8,128)(2,1)S(1)} collective-permute-done((bf16[1248,384]{1,0:T(8,128)(2,1)S(1)}, bf16[1248,384]{1,0:T(8,128)(2,1)S(1)}, u32[]{:S(2)}, u32[]{:S(2)}) %collective-permute-start.72) | collective-permute-done | bytes 958496 | tf_op jit(solution)/shard_map/ppermute | solution.py:1073
  602.0 7.3 %collective-permute-done.71.refs_0_.refs_4_ = bf16[1248,384]{1,0:T(8,128)(2,1)S(1)} collective-permute-done((bf16[1248,384]{1,0:T(8,128)(2,1)S(1)}, bf16[1248,384]{1,0:T(8,128)(2,1)S(1)}, u32[]{:S(2)}, u32[]{:S(2)}) %collective-permute-start.71) | collective-permute-done | bytes 958496 | tf_op jit(solution)/shard_map/ppermute | solution.py:1073
  609.3 9.5 %collective-permute-done.74.refs_1_.refs_12_ = bf16[1248,384]{1,0:T(8,128)(2,1)S(1)} collective-permute-done((bf16[1248,384]{1,0:T(8,128)(2,1)S(1)}, bf16[1248,384]{1,0:T(8,128)(2,1)S(1)}, u32[]{:S(2)}, u32[]{:S(2)}) %collective-permute-start.74) | collective-permute-done | bytes 958496 | tf_op jit(solution)/shard_map/ppermute | solution.py:1073
  622.6 8.1 %collective-permute-done.73.refs_0_.refs_5_ = bf16[1248,384]{1,0:T(8,128)(2,1)S(1)} collective-permute-done((bf16[1248,384]{1,0:T(8,128)(2,1)S(1)}, bf16[1248,384]{1,0:T(8,128)(2,1)S(1)}, u32[]{:S(2)}, u32[]{:S(2)}) %collective-permute-start.73) | collective-permute-done | bytes 958496 | tf_op jit(solution)/shard_map/ppermute | solution.py:1073
  630.7 11.9 %collective-permute-done.76.refs_1_.refs_13_ = bf16[1248,384]{1,0:T(8,128)(2,1)S(1)} collective-permute-done((bf16[1248,384]{1,0:T(8,128)(2,1)S(1)}, bf16[1248,384]{1,0:T(8,128)(2,1)S(1)}, u32[]{:S(2)}, u32[]{:S(2)}) %collective-permute-start.76) | collective-permute-done | bytes 958496 | tf_op jit(solution)/shard_map/ppermute | solution.py:1073
  646.5 6.1 collective-permute-done.75.refs_0_.refs_6_
  652.5 13.6 %collective-permute-done.78.refs_1_.refs_14_ = bf16[1248,384]{1,0:T(8,128)(2,1)S(1)} collective-permute-done((bf16[1248,384]{1,0:T(8,128)(2,1)S(1)}, bf16[1248,384]{1,0:T(8,128)(2,1)S(1)}, u32[]{:S(2)}, u32[]{:S(2)}) %collective-permute-start.78) | collective-permute-done | bytes 958496 | tf_op jit(solution)/shard_map/ppermute | solution.py:1073
  667.7 2.7 fusion.4
  675.1 5.1 collective-permute-done.79.refs_15_.refs_1_
  681.2 7.8 %unpack_late.1 = (f32[768,512]{1,0:T(8,128)}, f32[768,512]{1,0:T(8,128)}, f32[512,768]{1,0:T(8,128)}, f32[768,768]{1,0:T(8,128)}, f32[768,256]{1,0:T(8,128)}, /*...) custom-call(s32[63]{0:T(128)S(1)} %fusion.14.order_ref.plan_ref, ...), custom_call_target="tpu_custom_call" | custom-call | tf_op jit(solution)/shard_map/unpack_late/pallas_call | solution.py:986
  (401 shorter events, 171.6 us)
Async XLA Ops:
  0.7 34.4 %collective-permute-start.16 = (bf16[16,768,256]{2,1,0:T(8,128)(2,1)}, bf16[16,768,256]{2,1,0:T(8,128)(2,1)}, u32[]{:S(2)}, u32[]{:S(2)}) collective-permute-start(bf16[16,768,256]{2,1,0:T(8,128)(2,1)} %refs_16_.1), channel_id=1, source_target_pairs={{0,1},{1,0},{2,3},{3,2},{4,5},{5,4},{6,7},{7,6},{8,9},{9,8},{10,11... | collective-permute-start | bytes 18874376 | tf_op jit(solution)/shard_map/ppermute | solution.py:51
  5.3 27.1 %collective-permute-start = (bf16[512,768]{1,0:T(8,128)(2,1)S(1)}, bf16[512,768]{1,0:T(8,128)(2,1)}, u32[]{:S(2)}, u32[]{:S(2)}) collective-permute-start(bf16[512,768]{1,0:T(8,128)(2,1)S(1)} %copy-done.81), channel_id=1, source_target_pairs={{0,2},{2,0},{1,3},{3,1},{4,6},{6,4},{5,7},{7,5},{8,10},{10,8},{9,1... | collective-permute-start | bytes 2359304 | tf_op jit(solution)/shard_map/ppermute | solution.py:51
  13.3 19.1 %collective-permute-start.4 = (bf16[192,768]{1,0:T(8,128)(2,1)}, bf16[192,768]{1,0:T(8,128)(2,1)S(1)}, u32[]{:S(2)}, u32[]{:S(2)}) collective-permute-start(bf16[192,768]{1,0:T(8,128)(2,1)} %get-tuple-element.211), channel_id=1, source_target_pairs={{0,2},{2,0},{1,3},{3,1},{4,6},{6,4},{5,7},{7,5},{8,10},{10,8},{9,1... | collective-permute-start | bytes 884744 | tf_op jit(solution)/shard_map/ppermute | solution.py:51
  34.9 62.0 %collective-permute-start.18 = (bf16[16,256,768]{2,1,0:T(8,128)(2,1)}, bf16[16,256,768]{2,1,0:T(8,128)(2,1)}, u32[]{:S(2)}, u32[]{:S(2)}) collective-permute-start(bf16[16,256,768]{2,1,0:T(8,128)(2,1)} %refs_9_.13), channel_id=1, source_target_pairs={{0,1},{1,0},{2,3},{3,2},{4,5},{5,4},{6,7},{7,6},{8,9},{9,8},{10,11... | collective-permute-start | bytes 18874376 | tf_op jit(solution)/shard_map/ppermute | solution.py:51
  35.8 61.1 %collective-permute-start.17 = (bf16[16,768,256]{2,1,0:T(8,128)(2,1)}, bf16[16,768,256]{2,1,0:T(8,128)(2,1)}, u32[]{:S(2)}, u32[]{:S(2)}) collective-permute-start(bf16[16,768,256]{2,1,0:T(8,128)(2,1)} %refs_17_.1), channel_id=1, source_target_pairs={{0,1},{1,0},{2,3},{3,2},{4,5},{5,4},{6,7},{7,6},{8,9},{9,8},{10,11... | collective-permute-start | bytes 18874376 | tf_op jit(solution)/shard_map/ppermute | solution.py:51
  35.9 19.8 %collective-permute-start.5 = (bf16[512,768]{1,0:T(8,128)(2,1)S(1)}, bf16[512,768]{1,0:T(8,128)(2,1)S(1)}, u32[]{:S(2)}, u32[]{:S(2)}) collective-permute-start(bf16[512,768]{1,0:T(8,128)(2,1)S(1)} %copy-done.66), channel_id=1, source_target_pairs={{0,2},{2,0},{1,3},{3,1},{4,6},{6,4},{5,7},{7,5},{8,10},{10,8},{9,1... | collective-permute-start | bytes 2359304 | tf_op jit(solution)/shard_map/ppermute | solution.py:51
  50.6 17.8 %collective-permute-start.11 = (bf16[768,768]{1,0:T(8,128)(2,1)}, bf16[768,768]{1,0:T(8,128)(2,1)}, u32[]{:S(2)}, u32[]{:S(2)}) collective-permute-start(bf16[768,768]{1,0:T(8,128)(2,1)} %out_ref.1), channel_id=1, source_target_pairs={{0,1},{1,0},{2,3},{3,2},{4,5},{5,4},{6,7},{7,6},{8,9},{9,8},{10,11... | collective-permute-start | bytes 3538952 | tf_op jit(solution)/shard_map/ppermute | solution.py:51
  63.8 20.3 %collective-permute-start.12 = (bf16[1024,384]{1,0:T(8,128)(2,1)}, bf16[1024,384]{1,0:T(8,128)(2,1)}, u32[]{:S(2)}, u32[]{:S(2)}) collective-permute-start(bf16[1024,384]{1,0:T(8,128)(2,1)} %attend.1.refs_4_.refs_5_), channel_id=1, source_target_pairs={{0,2},{2,0},{1,3},{3,1},{4,6},{6,4},{5,7},{7,5},{8,10},{10,8},{9,1... | collective-permute-start | bytes 2359304 | tf_op jit(solution)/shard_map/ppermute | solution.py:51
  67.2 29.7 %collective-permute-start.15 = (bf16[1024,768]{1,0:T(8,128)(2,1)S(1)}, bf16[1024,768]{1,0:T(8,128)(2,1)S(1)}, u32[]{:S(2)}, u32[]{:S(2)}) collective-permute-start(bf16[1024,768]{1,0:T(8,128)(2,1)S(1)} %join.3.refs_2_.refs_4_), channel_id=1, source_target_pairs={{0,1},{1,0},{2,3},{3,2},{4,5},{5,4},{6,7},{7,6},{8,9},{9,8},{10,11... | collective-permute-start | bytes 4718600 | tf_op jit(solution)/shard_map/ppermute | solution.py:51
  111.3 32.9 %collective-permute-start.19 = (bf16[1,1536,384]{2,1,0:T(8,128)(2,1)S(1)}, bf16[1,1536,384]{2,1,0:T(8,128)(2,1)S(1)}, u32[]{:S(2)}, u32[]{:S(2)}) collective-permute-start(bf16[1,1536,384]{2,1,0:T(8,128)(2,1)S(1)} %get-tuple-element.226), channel_id=1, source_target_pairs={{0,8},{8,16},{16,24},{24,28},{28,20},{20,12},{12,4},{4,0},{9,1},{1... | collective-permute-start | bytes 3538952 | tf_op jit(solution)/shard_map/ppermute | solution.py:1073
  128.1 35.6 %collective-permute-start.21 = (bf16[1,1536,384]{2,1,0:T(8,128)(2,1)S(1)}, bf16[1,1536,384]{2,1,0:T(8,128)(2,1)S(1)}, u32[]{:S(2)}, u32[]{:S(2)}) collective-permute-start(bf16[1,1536,384]{2,1,0:T(8,128)(2,1)S(1)} %get-tuple-element.236), channel_id=1, source_target_pairs={{8,0},{16,8},{24,16},{28,24},{20,28},{12,20},{4,12},{0,4},{1,9},{9... | collective-permute-start | bytes 3538952 | tf_op jit(solution)/shard_map/ppermute | solution.py:1073
  146.7 33.3 %collective-permute-start.20 = (bf16[1,1536,384]{2,1,0:T(8,128)(2,1)}, bf16[1,1536,384]{2,1,0:T(8,128)(2,1)S(1)}, u32[]{:S(2)}, u32[]{:S(2)}) collective-permute-start(bf16[1,1536,384]{2,1,0:T(8,128)(2,1)} %ring_sum.14), channel_id=1, source_target_pairs={{0,8},{8,16},{16,24},{24,28},{28,20},{20,12},{12,4},{4,0},{9,1},{1... | collective-permute-start | bytes 3538952 | tf_op jit(solution)/shard_map/ppermute | solution.py:1073
  167.4 27.6 %collective-permute-start.23 = (bf16[1,1536,384]{2,1,0:T(8,128)(2,1)S(1)}, bf16[1,1536,384]{2,1,0:T(8,128)(2,1)S(1)}, u32[]{:S(2)}, u32[]{:S(2)}) collective-permute-start(bf16[1,1536,384]{2,1,0:T(8,128)(2,1)S(1)} %ring_sum.15), channel_id=1, source_target_pairs={{8,0},{16,8},{24,16},{28,24},{20,28},{12,20},{4,12},{0,4},{1,9},{9... | collective-permute-start | bytes 3538952 | tf_op jit(solution)/shard_map/ppermute | solution.py:1073
  167.9 18.6 %collective-permute-start.24 = (bf16[1,768,512]{2,1,0:T(8,128)(2,1)S(1)}, bf16[1,768,512]{2,1,0:T(8,128)(2,1)S(1)}, u32[]{:S(2)}, u32[]{:S(2)}) collective-permute-start(bf16[1,768,512]{2,1,0:T(8,128)(2,1)S(1)} %bitcast.29), channel_id=1, source_target_pairs={{0,1},{1,0},{2,3},{3,2},{4,5},{5,4},{6,7},{7,6},{8,9},{9,8},{10,11... | collective-permute-start | bytes 2359304 | tf_op jit(solution)/shard_map/ppermute | solution.py:51
  167.9 18.6 %collective-permute-start.25 = (bf16[1,768,512]{2,1,0:T(8,128)(2,1)S(1)}, bf16[1,768,512]{2,1,0:T(8,128)(2,1)S(1)}, u32[]{:S(2)}, u32[]{:S(2)}) collective-permute-start(bf16[1,768,512]{2,1,0:T(8,128)(2,1)S(1)} %bitcast.34), channel_id=1, source_target_pairs={{0,1},{1,0},{2,3},{3,2},{4,5},{5,4},{6,7},{7,6},{8,9},{9,8},{10,11... | collective-permute-start | bytes 2359304 | tf_op jit(solution)/shard_map/ppermute | solution.py:51
  168.4 18.1 %collective-permute-start.26 = (bf16[1,512,768]{2,1,0:T(8,128)(2,1)S(1)}, bf16[1,512,768]{2,1,0:T(8,128)(2,1)S(1)}, u32[]{:S(2)}, u32[]{:S(2)}) collective-permute-start(bf16[1,512,768]{2,1,0:T(8,128)(2,1)S(1)} %bitcast.39), channel_id=1, source_target_pairs={{0,1},{1,0},{2,3},{3,2},{4,5},{5,4},{6,7},{7,6},{8,9},{9,8},{10,11... | collective-permute-start | bytes 2359304 | tf_op jit(solution)/shard_map/ppermute | solution.py:51
  184.9 24.8 %collective-permute-start.22 = (bf16[1,1536,384]{2,1,0:T(8,128)(2,1)}, bf16[1,1536,384]{2,1,0:T(8,128)(2,1)}, u32[]{:S(2)}, u32[]{:S(2)}) collective-permute-start(bf16[1,1536,384]{2,1,0:T(8,128)(2,1)} %ring_sum.16), channel_id=1, source_target_pairs={{0,8},{8,16},{16,24},{24,28},{28,20},{20,12},{12,4},{4,0},{9,1},{1... | collective-permute-start | bytes 3538952 | tf_op jit(solution)/shard_map/ppermute | solution.py:1073
  196.3 32.7 %collective-permute-start.28 = (bf16[1,1536,384]{2,1,0:T(8,128)(2,1)S(1)}, bf16[1,1536,384]{2,1,0:T(8,128)(2,1)S(1)}, u32[]{:S(2)}, u32[]{:S(2)}) collective-permute-start(bf16[1,1536,384]{2,1,0:T(8,128)(2,1)S(1)} %ring_sum.17), channel_id=1, source_target_pairs={{8,0},{16,8},{24,16},{28,24},{20,28},{12,20},{4,12},{0,4},{1,9},{9... | collective-permute-start | bytes 3538952 | tf_op jit(solution)/shard_map/ppermute | solution.py:1073
  209.6 23.2 %collective-permute-start.30 = (bf16[1024,768]{1,0:T(8,128)(2,1)S(1)}, bf16[1024,768]{1,0:T(8,128)(2,1)}, u32[]{:S(2)}, u32[]{:S(2)}) collective-permute-start(bf16[1024,768]{1,0:T(8,128)(2,1)S(1)} %mix.4), channel_id=1, source_target_pairs={{0,1},{1,0},{2,3},{3,2},{4,5},{5,4},{6,7},{7,6},{8,9},{9,8},{10,11... | collective-permute-start | bytes 4718600 | tf_op jit(solution)/shard_map/ppermute | solution.py:51
  213.2 27.5 %collective-permute-start.27 = (bf16[1,1536,384]{2,1,0:T(8,128)(2,1)}, bf16[1,1536,384]{2,1,0:T(8,128)(2,1)}, u32[]{:S(2)}, u32[]{:S(2)}) collective-permute-start(bf16[1,1536,384]{2,1,0:T(8,128)(2,1)} %ring_sum.18), channel_id=1, source_target_pairs={{0,8},{8,16},{16,24},{24,28},{28,20},{20,12},{12,4},{4,0},{9,1},{1... | collective-permute-start | bytes 3538952 | tf_op jit(solution)/shard_map/ppermute | solution.py:1073
  232.4 19.8 %collective-permute-start.32 = (bf16[1,1536,384]{2,1,0:T(8,128)(2,1)}, bf16[1,1536,384]{2,1,0:T(8,128)(2,1)}, u32[]{:S(2)}, u32[]{:S(2)}) collective-permute-start(bf16[1,1536,384]{2,1,0:T(8,128)(2,1)} %ring_sum.19), channel_id=1, source_target_pairs={{8,0},{16,8},{24,16},{28,24},{20,28},{12,20},{4,12},{0,4},{1,9},{9... | collective-permute-start | bytes 3538952 | tf_op jit(solution)/shard_map/ppermute | solution.py:1073
  239.7 37.8 %collective-permute-start.34 = (bf16[1024,768]{1,0:T(8,128)(2,1)}, bf16[1024,768]{1,0:T(8,128)(2,1)}, u32[]{:S(2)}, u32[]{:S(2)}) collective-permute-start(bf16[1024,768]{1,0:T(8,128)(2,1)} %get-tuple-element.262), channel_id=1, source_target_pairs={{0,2},{2,0},{1,3},{3,1},{4,6},{6,4},{5,7},{7,5},{8,10},{10,8},{9,1... | collective-permute-start | bytes 4718600 | tf_op jit(solution)/shard_map/ppermute | solution.py:51
  242.9 19.5 %collective-permute-start.29 = (bf16[1,1536,384]{2,1,0:T(8,128)(2,1)S(1)}, bf16[1,1536,384]{2,1,0:T(8,128)(2,1)S(1)}, u32[]{:S(2)}, u32[]{:S(2)}) collective-permute-start(bf16[1,1536,384]{2,1,0:T(8,128)(2,1)S(1)} %ring_sum.20), channel_id=1, source_target_pairs={{0,8},{8,16},{16,24},{24,28},{28,20},{20,12},{12,4},{4,0},{9,1},{1... | collective-permute-start | bytes 3538952 | tf_op jit(solution)/shard_map/ppermute | solution.py:1073
  255.7 18.4 %collective-permute-start.33 = (bf16[1,1536,384]{2,1,0:T(8,128)(2,1)S(1)}, bf16[1,1536,384]{2,1,0:T(8,128)(2,1)S(1)}, u32[]{:S(2)}, u32[]{:S(2)}) collective-permute-start(bf16[1,1536,384]{2,1,0:T(8,128)(2,1)S(1)} %ring_sum.22), channel_id=1, source_target_pairs={{8,0},{16,8},{24,16},{28,24},{20,28},{12,20},{4,12},{0,4},{1,9},{9... | collective-permute-start | bytes 3538952 | tf_op jit(solution)/shard_map/ppermute | solution.py:1073
  255.8 21.2 %collective-permute-start.36 = (f32[8,1024]{1,0:T(8,128)S(1)}, f32[8,1024]{1,0:T(8,128)S(1)}, u32[]{:S(2)}, u32[]{:S(2)}) collective-permute-start(f32[8,1024]{1,0:T(8,128)S(1)} %get-tuple-element.271.refs_6_), channel_id=1, source_target_pairs={{0,2},{2,0},{1,3},{3,1},{4,6},{6,4},{5,7},{7,5},{8,10},{10,8},{9,1... | collective-permute-start | bytes 98312 | tf_op jit(solution)/shard_map/ppermute | solution.py:51
  257.0 20.4 %collective-permute-start.37 = (f32[8,1024]{1,0:T(8,128)S(1)}, f32[8,1024]{1,0:T(8,128)S(1)}, u32[]{:S(2)}, u32[]{:S(2)}) collective-permute-start(f32[8,1024]{1,0:T(8,128)S(1)} %collective-permute-done.35.refs_7_), channel_id=1, source_target_pairs={{0,2},{2,0},{1,3},{3,1},{4,6},{6,4},{5,7},{7,5},{8,10},{10,8},{9,1... | collective-permute-start | bytes 98312 | tf_op jit(solution)/shard_map/ppermute | solution.py:51
  284.3 32.2 %collective-permute-start.39 = (bf16[1024,768]{1,0:T(8,128)(2,1)S(1)}, bf16[1024,768]{1,0:T(8,128)(2,1)}, u32[]{:S(2)}, u32[]{:S(2)}) collective-permute-start(bf16[1024,768]{1,0:T(8,128)(2,1)S(1)} %get-tuple-element.272.grad_ref.refs_6_), channel_id=1, source_target_pairs={{0,1},{1,0},{2,3},{3,2},{4,5},{5,4},{6,7},{7,6},{8,9},{9,8},{10,11... | collective-permute-start | bytes 4718600 | tf_op jit(solution)/shard_map/ppermute | solution.py:51
  284.3 28.6 %collective-permute-start.31 = (bf16[1,1536,384]{2,1,0:T(8,128)(2,1)S(1)}, bf16[1,1536,384]{2,1,0:T(8,128)(2,1)S(1)}, u32[]{:S(2)}, u32[]{:S(2)}) collective-permute-start(bf16[1,1536,384]{2,1,0:T(8,128)(2,1)S(1)} %ring_sum.21), channel_id=1, source_target_pairs={{0,8},{8,16},{16,24},{24,28},{28,20},{20,12},{12,4},{4,0},{9,1},{1... | collective-permute-start | bytes 3538952 | tf_op jit(solution)/shard_map/ppermute | solution.py:1073
  286.0 43.6 %collective-permute-start.38 = (bf16[1,1536,384]{2,1,0:T(8,128)(2,1)}, bf16[1,1536,384]{2,1,0:T(8,128)(2,1)}, u32[]{:S(2)}, u32[]{:S(2)}) collective-permute-start(bf16[1,1536,384]{2,1,0:T(8,128)(2,1)} %ring_sum.23), channel_id=1, source_target_pairs={{8,0},{16,8},{24,16},{28,24},{20,28},{12,20},{4,12},{0,4},{1,9},{9... | collective-permute-start | bytes 3538952 | tf_op jit(solution)/shard_map/ppermute | solution.py:1073
  314.5 32.6 %collective-permute-start.40 = (bf16[1,1536,384]{2,1,0:T(8,128)(2,1)}, bf16[1,1536,384]{2,1,0:T(8,128)(2,1)}, u32[]{:S(2)}, u32[]{:S(2)}) collective-permute-start(bf16[1,1536,384]{2,1,0:T(8,128)(2,1)} %ring_sum.24), channel_id=1, source_target_pairs={{0,8},{8,16},{16,24},{24,28},{28,20},{20,12},{12,4},{4,0},{9,1},{1... | collective-permute-start | bytes 3538952 | tf_op jit(solution)/shard_map/ppermute | solution.py:1073
  333.1 21.6 %collective-permute-start.42 = (bf16[1,1536,384]{2,1,0:T(8,128)(2,1)}, bf16[1,1536,384]{2,1,0:T(8,128)(2,1)}, u32[]{:S(2)}, u32[]{:S(2)}) collective-permute-start(bf16[1,1536,384]{2,1,0:T(8,128)(2,1)} %ring_sum.25), channel_id=1, source_target_pairs={{8,0},{16,8},{24,16},{28,24},{20,28},{12,20},{4,12},{0,4},{1,9},{9... | collective-permute-start | bytes 3538952 | tf_op jit(solution)/shard_map/ppermute | solution.py:1073
  352.8 23.8 %collective-permute-start.41 = (bf16[1248,384]{1,0:T(8,128)(2,1)S(1)}, bf16[1248,384]{1,0:T(8,128)(2,1)S(1)}, u32[]{:S(2)}, u32[]{:S(2)}) collective-permute-start(bf16[1248,384]{1,0:T(8,128)(2,1)S(1)} %late_load.2.refs_0_), channel_id=1, source_target_pairs={{0,8},{8,16},{16,24},{24,28},{28,20},{20,12},{12,4},{4,0},{9,1},{1... | collective-permute-start | bytes 2875400 | tf_op jit(solution)/shard_map/ppermute | solution.py:1073
  357.8 21.6 %collective-permute-start.44 = (bf16[1248,384]{1,0:T(8,128)(2,1)S(1)}, bf16[1248,384]{1,0:T(8,128)(2,1)S(1)}, u32[]{:S(2)}, u32[]{:S(2)}) collective-permute-start(bf16[1248,384]{1,0:T(8,128)(2,1)S(1)} %late_load.3.refs_1_), channel_id=1, source_target_pairs={{8,0},{16,8},{24,16},{28,24},{20,28},{12,20},{4,12},{0,4},{1,9},{9... | collective-permute-start | bytes 2875400 | tf_op jit(solution)/shard_map/ppermute | solution.py:1073
  377.3 23.7 %collective-permute-start.43 = (bf16[1248,384]{1,0:T(8,128)(2,1)S(1)}, bf16[1248,384]{1,0:T(8,128)(2,1)S(1)}, u32[]{:S(2)}, u32[]{:S(2)}) collective-permute-start(bf16[1248,384]{1,0:T(8,128)(2,1)S(1)} %late_add.14.refs_0_), channel_id=1, source_target_pairs={{0,8},{8,16},{16,24},{24,28},{28,20},{20,12},{12,4},{4,0},{9,1},{1... | collective-permute-start | bytes 2875400 | tf_op jit(solution)/shard_map/ppermute | solution.py:1073
  380.1 23.1 %collective-permute-start.46 = (bf16[1248,384]{1,0:T(8,128)(2,1)S(1)}, bf16[1248,384]{1,0:T(8,128)(2,1)S(1)}, u32[]{:S(2)}, u32[]{:S(2)}) collective-permute-start(bf16[1248,384]{1,0:T(8,128)(2,1)S(1)} %late_add.15.refs_1_), channel_id=1, source_target_pairs={{8,0},{16,8},{24,16},{28,24},{20,28},{12,20},{4,12},{0,4},{1,9},{9... | collective-permute-start | bytes 2875400 | tf_op jit(solution)/shard_map/ppermute | solution.py:1073
  401.7 22.9 %collective-permute-start.45 = (bf16[1248,384]{1,0:T(8,128)(2,1)S(1)}, bf16[1248,384]{1,0:T(8,128)(2,1)S(1)}, u32[]{:S(2)}, u32[]{:S(2)}) collective-permute-start(bf16[1248,384]{1,0:T(8,128)(2,1)S(1)} %late_add.16.refs_0_), channel_id=1, source_target_pairs={{0,8},{8,16},{16,24},{24,28},{28,20},{20,12},{12,4},{4,0},{9,1},{1... | collective-permute-start | bytes 2875400 | tf_op jit(solution)/shard_map/ppermute | solution.py:1073
  403.9 24.1 %collective-permute-start.48 = (bf16[1248,384]{1,0:T(8,128)(2,1)S(1)}, bf16[1248,384]{1,0:T(8,128)(2,1)S(1)}, u32[]{:S(2)}, u32[]{:S(2)}) collective-permute-start(bf16[1248,384]{1,0:T(8,128)(2,1)S(1)} %late_add.17.refs_1_), channel_id=1, source_target_pairs={{8,0},{16,8},{24,16},{28,24},{20,28},{12,20},{4,12},{0,4},{1,9},{9... | collective-permute-start | bytes 2875400 | tf_op jit(solution)/shard_map/ppermute | solution.py:1073
  425.3 22.0 %collective-permute-start.47 = (bf16[1248,384]{1,0:T(8,128)(2,1)S(1)}, bf16[1248,384]{1,0:T(8,128)(2,1)S(1)}, u32[]{:S(2)}, u32[]{:S(2)}) collective-permute-start(bf16[1248,384]{1,0:T(8,128)(2,1)S(1)} %late_add.18.refs_0_), channel_id=1, source_target_pairs={{0,8},{8,16},{16,24},{24,28},{28,20},{20,12},{12,4},{4,0},{9,1},{1... | collective-permute-start | bytes 2875400 | tf_op jit(solution)/shard_map/ppermute | solution.py:1073
  428.7 23.3 %collective-permute-start.50 = (bf16[1248,384]{1,0:T(8,128)(2,1)S(1)}, bf16[1248,384]{1,0:T(8,128)(2,1)S(1)}, u32[]{:S(2)}, u32[]{:S(2)}) collective-permute-start(bf16[1248,384]{1,0:T(8,128)(2,1)S(1)} %late_add.19.refs_1_), channel_id=1, source_target_pairs={{8,0},{16,8},{24,16},{28,24},{20,28},{12,20},{4,12},{0,4},{1,9},{9... | collective-permute-start | bytes 2875400 | tf_op jit(solution)/shard_map/ppermute | solution.py:1073
  448.0 21.2 %collective-permute-start.49 = (bf16[1248,384]{1,0:T(8,128)(2,1)S(1)}, bf16[1248,384]{1,0:T(8,128)(2,1)}, u32[]{:S(2)}, u32[]{:S(2)}) collective-permute-start(bf16[1248,384]{1,0:T(8,128)(2,1)S(1)} %late_add.20.refs_0_), channel_id=1, source_target_pairs={{0,8},{8,16},{16,24},{24,28},{28,20},{20,12},{12,4},{4,0},{9,1},{1... | collective-permute-start | bytes 2875400 | tf_op jit(solution)/shard_map/ppermute | solution.py:1073
  452.7 19.2 %collective-permute-start.52 = (bf16[1248,384]{1,0:T(8,128)(2,1)S(1)}, bf16[1248,384]{1,0:T(8,128)(2,1)}, u32[]{:S(2)}, u32[]{:S(2)}) collective-permute-start(bf16[1248,384]{1,0:T(8,128)(2,1)S(1)} %late_add.21.refs_1_), channel_id=1, source_target_pairs={{8,0},{16,8},{24,16},{28,24},{20,28},{12,20},{4,12},{0,4},{1,9},{9... | collective-permute-start | bytes 2875400 | tf_op jit(solution)/shard_map/ppermute | solution.py:1073
  455.7 44.4 %collective-permute-start.57 = (bf16[1024,768]{1,0:T(8,128)(2,1)}, bf16[1024,768]{1,0:T(8,128)(2,1)}, u32[]{:S(2)}, u32[]{:S(2)}) collective-permute-start(bf16[1024,768]{1,0:T(8,128)(2,1)} %convolution_convert_fusion), channel_id=1, source_target_pairs={{0,1},{1,0},{2,3},{3,2},{4,5},{5,4},{6,7},{7,6},{8,9},{9,8},{10,11... | collective-permute-start | bytes 4718600 | tf_op jit(solution)/shard_map/ppermute | solution.py:51
  471.6 21.2 %collective-permute-start.51 = (bf16[1248,384]{1,0:T(8,128)(2,1)}, bf16[1248,384]{1,0:T(8,128)(2,1)}, u32[]{:S(2)}, u32[]{:S(2)}) collective-permute-start(bf16[1248,384]{1,0:T(8,128)(2,1)} %late_add.22.refs_0_), channel_id=1, source_target_pairs={{0,8},{8,16},{16,24},{24,28},{28,20},{20,12},{12,4},{4,0},{9,1},{1... | collective-permute-start | bytes 2875400 | tf_op jit(solution)/shard_map/ppermute | solution.py:1073
  474.3 21.0 %collective-permute-start.54 = (bf16[1248,384]{1,0:T(8,128)(2,1)}, bf16[1248,384]{1,0:T(8,128)(2,1)}, u32[]{:S(2)}, u32[]{:S(2)}) collective-permute-start(bf16[1248,384]{1,0:T(8,128)(2,1)} %late_add.23.refs_1_), channel_id=1, source_target_pairs={{8,0},{16,8},{24,16},{28,24},{20,28},{12,20},{4,12},{0,4},{1,9},{9... | collective-permute-start | bytes 2875400 | tf_op jit(solution)/shard_map/ppermute | solution.py:1073
  495.2 20.8 %collective-permute-start.53 = (bf16[1248,384]{1,0:T(8,128)(2,1)}, bf16[1248,384]{1,0:T(8,128)(2,1)}, u32[]{:S(2)}, u32[]{:S(2)}) collective-permute-start(bf16[1248,384]{1,0:T(8,128)(2,1)} %late_add.24.refs_0_), channel_id=1, source_target_pairs={{0,8},{8,16},{16,24},{24,28},{28,20},{20,12},{12,4},{4,0},{9,1},{1... | collective-permute-start | bytes 2875400 | tf_op jit(solution)/shard_map/ppermute | solution.py:1073
  497.6 21.1 %collective-permute-start.55 = (bf16[1248,384]{1,0:T(8,128)(2,1)}, bf16[1248,384]{1,0:T(8,128)(2,1)}, u32[]{:S(2)}, u32[]{:S(2)}) collective-permute-start(bf16[1248,384]{1,0:T(8,128)(2,1)} %late_add.25.refs_1_), channel_id=1, source_target_pairs={{8,0},{16,8},{24,16},{28,24},{20,28},{12,20},{4,12},{0,4},{1,9},{9... | collective-permute-start | bytes 2875400 | tf_op jit(solution)/shard_map/ppermute | solution.py:1073
  506.9 27.9 %collective-permute-start.63 = (bf16[1,768,384]{2,1,0:T(8,128)(2,1)}, bf16[1,768,384]{2,1,0:T(8,128)(2,1)S(1)}, u32[]{:S(2)}, u32[]{:S(2)}) collective-permute-start(bf16[1,768,384]{2,1,0:T(8,128)(2,1)} %copy-done.78), channel_id=1, source_target_pairs={{0,1},{1,0},{2,3},{3,2},{4,5},{5,4},{6,7},{7,6},{8,9},{9,8},{10,11... | collective-permute-start | bytes 1769480 | tf_op jit(solution)/shard_map/ppermute | solution.py:51
  507.0 20.3 %collective-permute-start.60 = (bf16[1,768,384]{2,1,0:T(8,128)(2,1)}, bf16[1,768,384]{2,1,0:T(8,128)(2,1)S(1)}, u32[]{:S(2)}, u32[]{:S(2)}) collective-permute-start(bf16[1,768,384]{2,1,0:T(8,128)(2,1)} %copy-done.79), channel_id=1, source_target_pairs={{0,1},{1,0},{2,3},{3,2},{4,5},{5,4},{6,7},{7,6},{8,9},{9,8},{10,11... | collective-permute-start | bytes 1769480 | tf_op jit(solution)/shard_map/ppermute | solution.py:51
  518.7 16.1 %collective-permute-start.62 = (bf16[480,384]{1,0:T(8,128)(2,1)S(1)}, bf16[480,384]{1,0:T(8,128)(2,1)S(1)}, u32[]{:S(2)}, u32[]{:S(2)}) collective-permute-start(bf16[480,384]{1,0:T(8,128)(2,1)S(1)} %get-tuple-element.335.mine_ref), channel_id=1, source_target_pairs={{0,1},{1,0},{2,3},{3,2},{4,5},{5,4},{6,7},{7,6},{8,9},{9,8},{10,11... | collective-permute-start | bytes 1105928 | tf_op jit(solution)/shard_map/ppermute | solution.py:51
  527.5 17.3 %collective-permute-start.61 = (bf16[1248,384]{1,0:T(8,128)(2,1)S(1)}, bf16[1248,384]{1,0:T(8,128)(2,1)S(1)}, u32[]{:S(2)}, u32[]{:S(2)}) collective-permute-start(bf16[1248,384]{1,0:T(8,128)(2,1)S(1)} %late_join.2.refs_0_), channel_id=1, source_target_pairs={{0,8},{8,16},{16,24},{24,28},{28,20},{20,12},{12,4},{4,0},{9,1},{1... | collective-permute-start | bytes 2875400 | tf_op jit(solution)/shard_map/ppermute | solution.py:1073
  535.0 20.4 %collective-permute-start.65 = (bf16[1248,384]{1,0:T(8,128)(2,1)S(1)}, bf16[1248,384]{1,0:T(8,128)(2,1)S(1)}, u32[]{:S(2)}, u32[]{:S(2)}) collective-permute-start(bf16[1248,384]{1,0:T(8,128)(2,1)S(1)} %late_join.3.refs_1_.refs_8_), channel_id=1, source_target_pairs={{8,0},{16,8},{24,16},{28,24},{20,28},{12,20},{4,12},{0,4},{1,9},{9... | collective-permute-start | bytes 2875400 | tf_op jit(solution)/shard_map/ppermute | solution.py:1073
  544.8 21.4 %collective-permute-start.64 = (bf16[1248,384]{1,0:T(8,128)(2,1)S(1)}, bf16[1248,384]{1,0:T(8,128)(2,1)S(1)}, u32[]{:S(2)}, u32[]{:S(2)}) collective-permute-start(bf16[1248,384]{1,0:T(8,128)(2,1)S(1)} %collective-permute-done.61.refs_0_.refs_1_), channel_id=1, source_target_pairs={{0,8},{8,16},{16,24},{24,28},{28,20},{20,12},{12,4},{4,0},{9,1},{1... | collective-permute-start | bytes 2875400 | tf_op jit(solution)/shard_map/ppermute | solution.py:1073
  555.4 21.4 %collective-permute-start.66 = (bf16[1248,384]{1,0:T(8,128)(2,1)S(1)}, bf16[1248,384]{1,0:T(8,128)(2,1)S(1)}, u32[]{:S(2)}, u32[]{:S(2)}) collective-permute-start(bf16[1248,384]{1,0:T(8,128)(2,1)S(1)} %collective-permute-done.65.refs_1_.refs_9_), channel_id=1, source_target_pairs={{8,0},{16,8},{24,16},{28,24},{20,28},{12,20},{4,12},{0,4},{1,9},{9... | collective-permute-start | bytes 2875400 | tf_op jit(solution)/shard_map/ppermute | solution.py:1073
  566.2 21.8 %collective-permute-start.70 = (bf16[1248,384]{1,0:T(8,128)(2,1)S(1)}, bf16[1248,384]{1,0:T(8,128)(2,1)S(1)}, u32[]{:S(2)}, u32[]{:S(2)}) collective-permute-start(bf16[1248,384]{1,0:T(8,128)(2,1)S(1)} %collective-permute-done.64.refs_0_.refs_2_), channel_id=1, source_target_pairs={{0,8},{8,16},{16,24},{24,28},{28,20},{20,12},{12,4},{4,0},{9,1},{1... | collective-permute-start | bytes 2875400 | tf_op jit(solution)/shard_map/ppermute | solution.py:1073
  576.8 21.4 %collective-permute-start.72 = (bf16[1248,384]{1,0:T(8,128)(2,1)S(1)}, bf16[1248,384]{1,0:T(8,128)(2,1)S(1)}, u32[]{:S(2)}, u32[]{:S(2)}) collective-permute-start(bf16[1248,384]{1,0:T(8,128)(2,1)S(1)} %collective-permute-done.66.refs_1_.refs_10_), channel_id=1, source_target_pairs={{8,0},{16,8},{24,16},{28,24},{20,28},{12,20},{4,12},{0,4},{1,9},{9... | collective-permute-start | bytes 2875400 | tf_op jit(solution)/shard_map/ppermute | solution.py:1073
  587.9 21.4 %collective-permute-start.71 = (bf16[1248,384]{1,0:T(8,128)(2,1)S(1)}, bf16[1248,384]{1,0:T(8,128)(2,1)S(1)}, u32[]{:S(2)}, u32[]{:S(2)}) collective-permute-start(bf16[1248,384]{1,0:T(8,128)(2,1)S(1)} %collective-permute-done.70.refs_0_.refs_3_), channel_id=1, source_target_pairs={{0,8},{8,16},{16,24},{24,28},{28,20},{20,12},{12,4},{4,0},{9,1},{1... | collective-permute-start | bytes 2875400 | tf_op jit(solution)/shard_map/ppermute | solution.py:1073
  598.2 20.6 %collective-permute-start.74 = (bf16[1248,384]{1,0:T(8,128)(2,1)S(1)}, bf16[1248,384]{1,0:T(8,128)(2,1)S(1)}, u32[]{:S(2)}, u32[]{:S(2)}) collective-permute-start(bf16[1248,384]{1,0:T(8,128)(2,1)S(1)} %collective-permute-done.72.refs_1_.refs_11_), channel_id=1, source_target_pairs={{8,0},{16,8},{24,16},{28,24},{20,28},{12,20},{4,12},{0,4},{1,9},{9... | collective-permute-start | bytes 2875400 | tf_op jit(solution)/shard_map/ppermute | solution.py:1073
  599.9 42.7 %collective-permute-start.67 = (bf16[1024,768]{1,0:T(8,128)(2,1)S(1)}, bf16[1024,768]{1,0:T(8,128)(2,1)S(1)}, u32[]{:S(2)}, u32[]{:S(2)}) collective-permute-start(bf16[1024,768]{1,0:T(8,128)(2,1)S(1)} %mix.7), channel_id=1, source_target_pairs={{0,1},{1,0},{2,3},{3,2},{4,5},{5,4},{6,7},{7,6},{8,9},{9,8},{10,11... | collective-permute-start | bytes 4718600 | tf_op jit(solution)/shard_map/ppermute | solution.py:51
  609.3 21.4 %collective-permute-start.73 = (bf16[1248,384]{1,0:T(8,128)(2,1)S(1)}, bf16[1248,384]{1,0:T(8,128)(2,1)S(1)}, u32[]{:S(2)}, u32[]{:S(2)}) collective-permute-start(bf16[1248,384]{1,0:T(8,128)(2,1)S(1)} %collective-permute-done.71.refs_0_.refs_4_), channel_id=1, source_target_pairs={{0,8},{8,16},{16,24},{24,28},{28,20},{20,12},{12,4},{4,0},{9,1},{1... | collective-permute-start | bytes 2875400 | tf_op jit(solution)/shard_map/ppermute | solution.py:1073
  618.8 23.8 %collective-permute-start.76 = (bf16[1248,384]{1,0:T(8,128)(2,1)S(1)}, bf16[1248,384]{1,0:T(8,128)(2,1)S(1)}, u32[]{:S(2)}, u32[]{:S(2)}) collective-permute-start(bf16[1248,384]{1,0:T(8,128)(2,1)S(1)} %collective-permute-done.74.refs_1_.refs_12_), channel_id=1, source_target_pairs={{8,0},{16,8},{24,16},{28,24},{20,28},{12,20},{4,12},{0,4},{1,9},{9... | collective-permute-start | bytes 2875400 | tf_op jit(solution)/shard_map/ppermute | solution.py:1073
  630.7 21.8 %collective-permute-start.75 = (bf16[1248,384]{1,0:T(8,128)(2,1)S(1)}, bf16[1248,384]{1,0:T(8,128)(2,1)S(1)}, u32[]{:S(2)}, u32[]{:S(2)}) collective-permute-start(bf16[1248,384]{1,0:T(8,128)(2,1)S(1)} %collective-permute-done.73.refs_0_.refs_5_), channel_id=1, source_target_pairs={{0,8},{8,16},{16,24},{24,28},{28,20},{20,12},{12,4},{4,0},{9,1},{1... | collective-permute-start | bytes 2875400 | tf_op jit(solution)/shard_map/ppermute | solution.py:1073
  642.6 23.5 %collective-permute-start.78 = (bf16[1248,384]{1,0:T(8,128)(2,1)S(1)}, bf16[1248,384]{1,0:T(8,128)(2,1)S(1)}, u32[]{:S(2)}, u32[]{:S(2)}) collective-permute-start(bf16[1248,384]{1,0:T(8,128)(2,1)S(1)} %collective-permute-done.76.refs_1_.refs_13_), channel_id=1, source_target_pairs={{8,0},{16,8},{24,16},{28,24},{20,28},{12,20},{4,12},{0,4},{1,9},{9... | collective-permute-start | bytes 2875400 | tf_op jit(solution)/shard_map/ppermute | solution.py:1073
  643.2 27.2 %collective-permute-start.68 = (bf16[512,768]{1,0:T(8,128)(2,1)S(1)}, bf16[512,768]{1,0:T(8,128)(2,1)S(1)}, u32[]{:S(2)}, u32[]{:S(2)}) collective-permute-start(bf16[512,768]{1,0:T(8,128)(2,1)S(1)} %dynamic-slice_convert_fusion), channel_id=1, source_target_pairs={{0,2},{2,0},{1,3},{3,1},{4,6},{6,4},{5,7},{7,5},{8,10},{10,8},{9,1... | collective-permute-start | bytes 2359304 | tf_op jit(solution)/shard_map/ppermute | solution.py:51
  652.5 22.6 %collective-permute-start.77 = (bf16[1248,384]{1,0:T(8,128)(2,1)S(1)}, bf16[1248,384]{1,0:T(8,128)(2,1)S(1)}, u32[]{:S(2)}, u32[]{:S(2)}) collective-permute-start(bf16[1248,384]{1,0:T(8,128)(2,1)S(1)} %collective-permute-done.75.refs_0_.refs_6_), channel_id=1, source_target_pairs={{0,8},{8,16},{16,24},{24,28},{28,20},{20,12},{12,4},{4,0},{9,1},{1... | collective-permute-start | bytes 2875400 | tf_op jit(solution)/shard_map/ppermute | solution.py:1073
  (120 other events, 987.9 us)

commit v12 on v11

--- a/solution.py
+++ b/solution.py
@@ -124,8 +124,10 @@
 
 
 def attend_back_kernel(
-    place_ref, own_ref, other_ref, grad_ref, grad_c_ref, out_ref, out_c_ref, result_ref, all_ref, total_ref
+    place_ref, own_ref, other_ref, *refs
 ):
+    grad_refs, grad_c_refs = refs[0:2], refs[2:4]
+    out_ref, out_c_ref, result_ref, all_ref, total_ref = refs[4:9]
     gather_rows(place_ref, own_ref, other_ref, all_ref)
     rows = own_ref.shape[0]
     block = 256
@@ -138,8 +140,10 @@
         key = all_ref[0:keys, width : width + DH]
         value = all_ref[0:keys, width + DH : width + 2 * DH]
         probs = key_probs(query, key, first, place_ref[1])
-        grad = dot_nt(grad_ref[first:keys, :], out_ref[group, :])
-        grad = (grad + dot_nt(grad_c_ref[first:keys, :], out_c_ref[group, :])).astype(BF16)
+        half, in_half = divmod(first, rows)
+        piece = slice(in_half, in_half + block)
+        grad = dot_nt(grad_refs[half][piece, :], out_ref[group, :])
+        grad = (grad + dot_nt(grad_c_refs[half][piece, :], out_c_ref[group, :])).astype(BF16)
         grad = jnp.concatenate(
             [grad[:, h * DH : (h + 1) * DH] for h in range(GROUP_HEADS)], axis=0
         )
@@ -169,7 +173,7 @@
     return pl.pallas_call(
         attend_back_kernel,
         out_shape=jax.ShapeDtypeStruct((2 * rows, width), BF16),
-        in_specs=[pl.BlockSpec(memory_space=pltpu.SMEM)] + [spec] * 6,
+        in_specs=[pl.BlockSpec(memory_space=pltpu.SMEM)] + [spec] * 8,
         out_specs=spec,
         scratch_shapes=[
             pltpu.VMEM((2 * rows, width), BF16),
@@ -178,7 +182,7 @@
         compiler_params=params(60),
         cost_estimate=SMALL,
         name="attend_back",
-    )(place, own, other, grad, grad_c, w_out, out_c)
+    )(place, own, other, *grad, *grad_c, w_out, out_c)
 
 
 def unit_slices(unit, share):
@@ -187,9 +191,8 @@
 
 
 def late_kernel(place_ref, *refs):
-    near, near_c, far, far_c, qkv_ref, attended_ref, grad_ref, grad_c_ref = refs[0:8]
-    shared = refs[8:10]
-    outs = refs[10:12]
+    near, near_c, far, far_c, qkv_ref, attended_ref = refs[0:6]
+    grad_refs, grad_c_refs, shared, outs = refs[6:8], refs[8:10], refs[10:12], refs[12:14]
     rows, features = near.shape
     own_rows = pl.ds(pl.multiple_of(place_ref[0] * rows, rows), rows)
     far_rows = pl.ds(pl.multiple_of((1 - place_ref[0]) * rows, rows), rows)
@@ -218,12 +221,13 @@
         for chunk in range(chunks):
             out_ref[chunk, to_rows, to_lanes] = jnp.zeros((share, LANES), BF16)
 
-    for h, (x, y, grad) in enumerate(((near, far, grad_ref), (near_c, far_c, grad_c_ref))):
+    for h, (x, y, grad) in enumerate(((near, far, grad_refs), (near_c, far_c, grad_c_refs))):
         for k in range(2):
             store(h, 3 * LANES * k, shared[k][0, h * features : (h + 1) * features, :])
         project = dot_tn(x[...], qkv_ref[own_rows, :]) + dot_tn(y[...], qkv_ref[far_rows, :])
         store(h, 6 * LANES, project)
-        store(h, 11 * LANES, dot_tn(grad[...], attended_ref[...]))
+        out = [dot_tn(grad[k][...], attended_ref[k * rows : (k + 1) * rows, :]) for k in range(2)]
+        store(h, 11 * LANES, out[0] + out[1])
 
 
 def late_grads(place, near, far, qkv_grad, attended, grad, grad_c, shared):
@@ -233,12 +237,12 @@
     return pl.pallas_call(
         late_kernel,
         out_shape=[jax.ShapeDtypeStruct((RING, rows, 3 * LANES), BF16)] * 2,
-        in_specs=[pl.BlockSpec(memory_space=pltpu.SMEM)] + [spec] * 10,
+        in_specs=[pl.BlockSpec(memory_space=pltpu.SMEM)] + [spec] * 12,
         out_specs=[spec] * 2,
         compiler_params=params(60),
         cost_estimate=SMALL,
         name="late_grads",
-    )(place, *near, *far, qkv_grad, attended, grad, grad_c, *shared)
+    )(place, *near, *far, qkv_grad, attended, *grad, *grad_c, *shared)
 
 
 def columns_kernel(
@@ -580,15 +584,15 @@
     )(order, *x, *o, gates, *weights, *weights, *kept)
 
 
-def mix_kernel(back, group, order_ref, *refs):
+def mix_kernel(back, group, pieces, order_ref, *refs):
     acts_ref, shared_ref = refs[0:2]
     each = 2 if back else 1
     count = 2 * group * each
     weights = refs[2 : 2 + count]
     shared = refs[2 + count : 2 + count + 2 * each]
-    out_ref, total_ref = refs[2 + count + 2 * each :]
+    *outs, total_ref = refs[2 + count + 2 * each :]
     step = pl.program_id(0)
-    rows = out_ref.shape[0]
+    rows = total_ref.shape[0]
     tile = 512
     times = dot_nt if back else dot
     along = 1 if back else 0
@@ -608,10 +612,12 @@
 
     @pl.when(step == pl.num_programs(0) - 1)
     def _():
-        out_ref[...] = total_ref[...].astype(out_ref.dtype)
-
-
-def mix(back, dtype, order, acts, shared_acts, weights, shared_weights):
+        part = rows // pieces
+        for k, out_ref in enumerate(outs):
+            out_ref[...] = total_ref[k * part : (k + 1) * part, :].astype(out_ref.dtype)
+
+
+def mix(back, dtype, pieces, order, acts, shared_acts, weights, shared_weights):
     pairs, rows, width = acts.shape
     features = weights[0].shape[1] if back else weights[0].shape[2]
     group = 4 if pairs % 4 == 0 else 1
@@ -627,8 +633,8 @@
     def common(k):
         return spec(lambda i, o: (0, 2 * o[o.shape[0] - 1] + k))
 
-    return pl.pallas_call(
-        functools.partial(mix_kernel, back, group),
+    outs = pl.pallas_call(
+        functools.partial(mix_kernel, back, group, pieces),
         grid_spec=pltpu.PrefetchScalarGridSpec(
             num_scalar_prefetch=1,
             grid=(pairs // group,),
@@ -638,18 +644,21 @@
             ]
             + [routed(k) for k in range(2 * group) for _ in weights]
             + [common(k) for k in range(2) for _ in weights],
-            out_specs=pl.BlockSpec((rows, features), lambda i, o: (0, 0)),
+            out_specs=[pl.BlockSpec((rows // pieces, features), lambda i, o: (0, 0))] * pieces,
             scratch_shapes=[pltpu.VMEM((rows, features), F32)],
         ),
-        out_shape=jax.ShapeDtypeStruct((rows, features), dtype),
+        out_shape=[jax.ShapeDtypeStruct((rows // pieces, features), dtype)] * pieces,
         compiler_params=params(48, "arbitrary"),
         cost_estimate=SMALL,
         name="mix",
     )(order, acts, shared_acts, *weights * (2 * group), *shared_weights * 2)
-
-
-def chip_sum_kernel(own_ref, other_ref, hidden_ref, gains_ref, total_ref, rounded_ref, product_ref):
-    total = own_ref[...] + other_ref[...].astype(F32)
+    return outs if pieces > 1 else outs[0]
+
+
+def chip_sum_kernel(tiles, own_ref, first_ref, second_ref, hidden_ref, gains_ref, total_ref, rounded_ref, product_ref):
+    is_first = pl.program_id(0) < tiles // 2
+    other = jnp.where(is_first, first_ref[...], second_ref[...])
+    total = own_ref[...] + other.astype(F32)
     total_ref[...] = total
     rounded_ref[...] = total.astype(BF16)
     product_ref[...] = lax.dot_general(
@@ -664,26 +673,28 @@
 def chip_sum(own, other, hidden, gains):
     rows, features = own.shape
     spec = pl.BlockSpec((TOKEN_TILE, features), lambda i: (i, 0))
-    return pl.pallas_call(
-        chip_sum_kernel,
-        grid=(rows // TOKEN_TILE,),
+    tiles = rows // TOKEN_TILE
+    piece = pl.BlockSpec((TOKEN_TILE, features), lambda i: (i % (tiles // 2), 0))
+    return pl.pallas_call(
+        functools.partial(chip_sum_kernel, tiles),
+        grid=(tiles,),
         out_shape=[
             jax.ShapeDtypeStruct((rows, features), F32),
             jax.ShapeDtypeStruct((rows, features), BF16),
             jax.ShapeDtypeStruct((8, rows), F32),
         ],
-        in_specs=[spec, spec, spec, pl.BlockSpec(gains.shape, lambda i: (0, 0))],
+        in_specs=[spec, piece, piece, spec, pl.BlockSpec(gains.shape, lambda i: (0, 0))],
         out_specs=[spec, spec, pl.BlockSpec((8, TOKEN_TILE), lambda i: (0, i))],
         compiler_params=params(24, "arbitrary"),
         cost_estimate=SMALL,
         name="chip_sum",
-    )(own, other, hidden, gains)
+    )(own, *other, hidden, gains)
 
 
 def norm_back_kernel(tiles, place_ref, *refs):
     sum_ref, came_ref, hidden_ref, scale_ref, out_grad_ref, gains_ref = refs[0:6]
     products = refs[6:10]
-    hidden_grad_ref, rounded_ref, gain_ref = refs[10:13]
+    hidden_grad_ref, first_ref, second_ref, gain_ref = refs[10:14]
     step = pl.program_id(0)
     part = (step >= tiles // 2).astype(jnp.int32)
     grad = sum_ref[...] + came_ref[...].astype(F32)
@@ -700,7 +711,11 @@
     result = out_grad_ref[...].astype(F32) + scale * (grad * gains_ref[1:2, :])
     result = result - hidden * (scale * scale * scale * mean)
     hidden_grad_ref[...] = result
-    rounded_ref[...] = result.astype(BF16)
+    for k, rounded_ref in enumerate((first_ref, second_ref)):
+
+        @pl.when(part == k)
+        def _(rounded_ref=rounded_ref):
+            rounded_ref[...] = result.astype(BF16)
 
     @pl.when(step == 0)
     def _():
@@ -715,6 +730,13 @@
     rows, features = hidden.shape
     tiles = rows // TOKEN_TILE
     lanes = pl.BlockSpec((8, TOKEN_TILE), lambda i, p: (0, i))
+
+    def piece(k):
+        last = tiles // 2 - 1
+        return pl.BlockSpec(
+            (TOKEN_TILE, features), lambda i, p: (jnp.clip(i - k * tiles // 2, 0, last), 0)
+        )
+
     return pl.pallas_call(
         functools.partial(norm_back_kernel, tiles),
         grid_spec=pltpu.PrefetchScalarGridSpec(
@@ -723,11 +745,12 @@
             in_specs=[rowwise(features)] * 3
             + [rowwise(1), rowwise(features), whole(2, features)]
             + [lanes] * 4,
-            out_specs=[rowwise(features)] * 2 + [whole(1, features)],
+            out_specs=[rowwise(features), piece(0), piece(1), whole(1, features)],
         ),
         out_shape=[
             jax.ShapeDtypeStruct((rows, features), F32),
-            jax.ShapeDtypeStruct((rows, features), BF16),
+            jax.ShapeDtypeStruct((rows // 2, features), BF16),
+            jax.ShapeDtypeStruct((rows // 2, features), BF16),
             jax.ShapeDtypeStruct((1, features), F32),
         ],
         compiler_params=params(48, "arbitrary"),
@@ -1196,6 +1219,7 @@
             mixed[True, half] = mix(
                 True,
                 BF16 if half else F32,
+                1 + half,
                 order,
                 kept[0],
                 runs["shared"][2],
@@ -1203,9 +1227,11 @@
                 shared[2 * half : 2 * half + 2],
             )
             if half:
-                normed["other"] = swap(mixed[True, 1], "col")
-                return [mixed[True, 1]]
-            total, rounded, product = chip_sum(mixed[True, 0], normed["other"], hidden, gains)
+                normed["other"] = [swap(part, "col") for part in mixed[True, 1]]
+                return list(mixed[True, 1])
+            total, rounded, product = chip_sum(
+                mixed[True, 0], normed["other"], hidden, gains
+            )
             product_c = swap(product, "col")
             normed["sum"] = total
             normed["tie"] = rounded
@@ -1220,6 +1246,7 @@
             mixed[False, half] = mix(
                 False,
                 BF16 if half else F32,
+                1,
                 order,
                 kept[1],
                 runs["shared"][3],
@@ -1239,7 +1266,7 @@
         return lax.dynamic_slice_in_dim(values, local_rows - start, local_rows, axis=0)
 
     def work_hidden(order, ties):
-        normed["hidden"], normed["grad"], normed["gain"] = norm_back(
+        normed["hidden"], *grad, normed["gain"] = norm_back(
             after(where, *ties),
             normed["sum"],
             normed["came"],
@@ -1249,8 +1276,9 @@
             gains,
             normed["products"],
         )
-        normed["grad_c"] = swap(normed["grad"], "col")
-        return [normed["grad"]]
+        normed["grad"] = grad
+        normed["grad_c"] = [swap(part, "col") for part in grad]
+        return grad
 
     def work_attend(order, ties):
         normed["qkv"] = attend_back(

time: 705 us -> 693 us (0.983)
  waiting for transfers between devices: 295 us -> 272 us
  starting transfers between devices: 60.3 us -> 69.8 us
    ppermute x42, waiting for transfers between devices: 256 us -> 228 us  [send(): return lax.ppermute(values, ('dp', 'col'), routes_of[which])]
    ppermute x42, starting transfers between devices: 35.9 us -> 44.5 us  [send(): return lax.ppermute(values, ('dp', 'col'), routes_of[which])]
    ppermute x35 -> x37, waiting for transfers between devices: 37.2 us -> 41.5 us  [swap(): return lax.ppermute(values, axis, [(0, 1), (1, 0)])]
    ppermute x35 -> x37, starting transfers between devices: 18.8 us -> 19.8 us  [swap(): return lax.ppermute(values, axis, [(0, 1), (1, 0)])]
    unnamed x208 -> x216, local copies, waits for them, and re-layouts: 35.3 us -> 35.8 us
  transfers between devices with their start and end apart: 80 -> 82, of which waited for: 41 -> 38; matrix products, arithmetic and copies ran while one was open for 2% -> 2% of each run, Pallas kernels for 37% -> 39%
where the time goes in v12:
time: 693 us; the launch traced here: 683 us
  Pallas kernels  285 us (41%)
  waiting for transfers between devices  272 us (39%)
  starting transfers between devices  69.8 us (10%)
  local copies, waits for them, and re-layouts  38.2 us (6%)
  other arithmetic  9.79 us (1%)
    ppermute x42, waiting for transfers between devices, send(): return lax.ppermute(values, ('dp', 'col'), routes_of[which])  228 us
    pallas_call x6, Pallas kernels, expert_grads(): pl.pallas_call(functools.partial(expert_kernel, shared, aliased, first),...  72.6 us
    ppermute x42, starting transfers between devices, send(): return lax.ppermute(values, ('dp', 'col'), routes_of[which])  44.5 us
    ppermute x37, waiting for transfers between devices, swap(): return lax.ppermute(values, axis, [(0, 1), (1, 0)])  41.5 us
    pallas_call x4, Pallas kernels, mix(): pl.pallas_call(functools.partial(mix_kernel, back, group, pieces), grid_s...  39.7 us
    pallas_call x16, Pallas kernels, unpack(): pl.pallas_call(functools.partial(unpack_kernel, aliased), grid_spec=pltpu...  38.5 us
    unnamed x216, local copies, waits for them, and re-layouts  35.8 us
    pallas_call x14, Pallas kernels, ring_sum(): pl.pallas_call(ring_sum_kernel, grid=(count, tiles), in_specs=[spec, term...  27 us
  transfers between devices with their start and end apart: 82, of which 38 were waited for; matrix products, arithmetic and copies ran while one was open for 2% of the time, Pallas kernels for 39%

profile of v12, /device:TPU:0, one launch (start us, length us, event | category | flops | bytes accessed | tf_op | source)
XLA Modules:
  0.0 682.7 jit_solution(4173993362509631867)
XLA Ops:
  1.8 3.1 their_columns.1
  5.4 2.6 collective-permute-start
  8.2 5.0 collective-permute-done.2.gains_c_ref.refs_7_
  13.3 2.9 collective-permute-start.4
  18.0 4.5 project.2
  22.4 10.0 %collective-permute-done.4.refs_0_ = bf16[192,768]{1,0:T(8,128)(2,1)S(1)} collective-permute-done((bf16[192,768]{1,0:T(8,128)(2,1)}, bf16[192,768]{1,0:T(8,128)(2,1)S(1)}, u32[]{:S(2)}, u32[]{:S(2)}) %collective-permute-start.4) | collective-permute-done | bytes 294944 | tf_op jit(solution)/shard_map/ppermute | solution.py:51
  32.4 2.5 collective-permute-done.8.other_ref.refs_3_
  40.8 4.5 project.3
  47.4 2.5 collective-permute-start.9
  50.7 5.0 collective-permute-done.5.refs_1_
  57.5 6.3 attend.1.refs_4_.refs_5_
  69.5 9.0 %hidden_before.1 = (f32[1024,768]{1,0:T(8,128)}, f32[1024,768]{1,0:T(8,128)}) custom-call(s32[3]{0:T(128)} %copy-done.77, bf16[512,768]{1,0:T(8,128)(2,1)} %refs_0_.2, bf16[512,768]{1,0:T(8,128)(2,1)} %copy-done.97, bf16[512,768]{1,0:T(8,128)(2,1)} %collective-permute-done.own_ref.refs_2_, bf16[512,768]{1,0:T(8,128)(2,1)} %copy-done.98, ...), custom_call_target="tpu_custom_call" | custom-call | flops 2415919104 | bytes 12582912 | tf_op jit(solution)/shard_map/hidden_before/pallas_call | solution.py:418
  78.5 5.6 collective-permute-done.12.refs_2_
  87.5 9.4 %hidden_after.1 = (f32[1024,768]{1,0:T(8,128)}, bf16[1024,768]{1,0:T(8,128)(2,1)}, bf16[1024,768]{1,0:T(8,128)(2,1)}, f32[1024,1]{1,0:T(8,128)}) custom-call(s32[3]{0:T(128)} %copy-done.77, f32[1024,768]{1,0:T(8,128)} %get-tuple-element.221.refs_0_, f32[1024,768]{1,0:T(8,128)} %get-tuple-element.222.refs_1_, ...), custom_call_target="tpu_custom_call" | custom-call | tf_op jit(solution)/shard_map/hidden_after/pallas_call | solution.py:440
  100.3 9.0 %expert_grads.6 = (bf16[1,1536,384]{2,1,0:T(8,128)(2,1)S(1)}, bf16[1,1536,384]{2,1,0:T(8,128)(2,1)S(1)}, bf16[8,1024,512]{2,1,0:T(8,128)(2,1)}, bf16[8,1024,256]{2,1,0:T(8,128)(2,1)S(1)}) custom-call(s32[63]{0:T(128)S(1)} %fusion.14.order_ref.plan_ref, bf16[1024,768]{1,0:T(8,128)(2,1)S(1)} %copy-done.9, bf16[1024,768]{1,0:T(8,128)(2,1)S(1)} %copy-done.10, ...), custom_call_target="tpu_custom_call" | custom-call | tf_op jit(solution)/shard_map/expert_grads/pallas_call | solution.py:563
  112.9 15.2 %expert_grads.7 = (bf16[2,1536,384]{2,1,0:T(8,128)(2,1)S(1)}, bf16[2,1536,384]{2,1,0:T(8,128)(2,1)S(1)}, bf16[8,1024,512]{2,1,0:T(8,128)(2,1)}, bf16[8,1024,256]{2,1,0:T(8,128)(2,1)}) custom-call(s32[63]{0:T(128)S(1)} %fusion.14.order_ref.plan_ref, bf16[1024,768]{1,0:T(8,128)(2,1)S(1)} %copy-done.9, ...), custom_call_target="tpu_custom_call", output_to_operand_aliasing={{2}: (18, {}), {3}: (19, {})} | custom-call | tf_op jit(solution)/shard_map/expert_grads/pallas_call | solution.py:563
  128.7 15.6 %expert_grads.8 = (bf16[2,1536,384]{2,1,0:T(8,128)(2,1)S(1)}, bf16[2,1536,384]{2,1,0:T(8,128)(2,1)S(1)}, bf16[8,1024,512]{2,1,0:T(8,128)(2,1)}, bf16[8,1024,256]{2,1,0:T(8,128)(2,1)}) custom-call(s32[63]{0:T(128)S(1)} %fusion.14.order_ref.plan_ref, bf16[1024,768]{1,0:T(8,128)(2,1)S(1)} %copy-done.9, ...), custom_call_target="tpu_custom_call", output_to_operand_aliasing={{2}: (18, {}), {3}: (19, {})} | custom-call | tf_op jit(solution)/shard_map/expert_grads/pallas_call | solution.py:563
  148.4 15.6 %expert_grads.9 = (bf16[2,1536,384]{2,1,0:T(8,128)(2,1)S(1)}, bf16[2,1536,384]{2,1,0:T(8,128)(2,1)S(1)}, bf16[8,1024,512]{2,1,0:T(8,128)(2,1)}, bf16[8,1024,256]{2,1,0:T(8,128)(2,1)}) custom-call(s32[63]{0:T(128)S(1)} %fusion.14.order_ref.plan_ref, bf16[1024,768]{1,0:T(8,128)(2,1)S(1)} %copy-done.9, ...), custom_call_target="tpu_custom_call", output_to_operand_aliasing={{2}: (18, {}), {3}: (19, {})} | custom-call | tf_op jit(solution)/shard_map/expert_grads/pallas_call | solution.py:563
  169.4 8.8 %expert_grads.10 = (bf16[1,1536,384]{2,1,0:T(8,128)(2,1)S(1)}, bf16[1,1536,384]{2,1,0:T(8,128)(2,1)S(1)}, bf16[8,1024,512]{2,1,0:T(8,128)(2,1)}, bf16[8,1024,256]{2,1,0:T(8,128)(2,1)S(1)}) custom-call(s32[63]{0:T(128)S(1)} %fusion.14.order_ref.plan_ref, bf16[1024,768]{1,0:T(8,128)(2,1)S(1)} %copy-done.9, ...), custom_call_target="tpu_custom_call", output_to_operand_aliasing={{2}: (18, {}), {3}: (19, {})} | custom-call | tf_op jit(solution)/shard_map/expert_grads/pallas_call | solution.py:563
  180.3 3.2 copy-done.39
  186.8 8.3 %expert_grads.11 = (bf16[1,1536,384]{2,1,0:T(8,128)(2,1)S(1)}, bf16[1,1536,384]{2,1,0:T(8,128)(2,1)S(1)}, bf16[1,1024,512]{2,1,0:T(8,128)(2,1)S(1)}, bf16[1,1024,256]{2,1,0:T(8,128)(2,1)S(1)}) custom-call(s32[63]{0:T(128)S(1)} %fusion.14.order_ref.plan_ref, bf16[1024,768]{1,0:T(8,128)(2,1)S(1)} %copy-done.9, bf16[1024,768]{1,0:T(8,128)(2,1)S(1)} %copy-done.11, ...), custom_call_target="tpu_custom_call" | custom-call | tf_op jit(solution)/shard_map/expert_grads/pallas_call | solution.py:563
  197.0 12.6 %mix.4 = (bf16[512,768]{1,0:T(8,128)(2,1)S(1)}, bf16[512,768]{1,0:T(8,128)(2,1)S(1)}) custom-call(s32[63]{0:T(128)S(1)} %fusion.14.order_ref.plan_ref, bf16[8,1024,512]{2,1,0:T(8,128)(2,1)} %get-tuple-element.247.refs_0_, bf16[1,1024,512]{2,1,0:T(8,128)(2,1)S(1)} %get-tuple-element.253.refs_1_, ...), custom_call_target="tpu_custom_call" | custom-call | tf_op jit(solution)/shard_map/mix/pallas_call | solution.py:636
  209.7 3.8 ring_sum.18
  215.0 12.5 %mix.5.own_ref = f32[1024,768]{1,0:T(8,128)S(1)} custom-call(s32[63]{0:T(128)S(1)} %fusion.14.order_ref.plan_ref, bf16[8,1024,512]{2,1,0:T(8,128)(2,1)} %get-tuple-element.247.refs_0_, bf16[1,1024,512]{2,1,0:T(8,128)(2,1)S(1)} %get-tuple-element.253.refs_1_, bf16[16,768,256]{2,1,0:T(8,128)(2,1)} %refs_16_.1, bf16[16,768,256]{2,1,0:T(8,128)(2,1)} %refs_17_.1, ...), custom_call_target="tpu_custom_call" | custom-call | tf_op jit(solution)/shard_map/mix/pallas_call | solution.py:636
  233.6 3.0 collective-permute-done.30.first_ref
  238.5 3.5 chip_sum.1
  246.9 7.4 %mix.6 = f32[1024,768]{1,0:T(8,128)S(1)} custom-call(s32[63]{0:T(128)S(1)} %fusion.14.order_ref.plan_ref, bf16[8,1024,256]{2,1,0:T(8,128)(2,1)} %copy-done.7, bf16[1,1024,256]{2,1,0:T(8,128)(2,1)S(1)} %get-tuple-element.266.refs_1_, bf16[16,256,768]{2,1,0:T(8,128)(2,1)} %refs_9_.13, bf16[16,256,768]{2,1,0:T(8,128)(2,1)} %refs_9_.13, ...), custom_call_target="tpu_custom_call" | custom-call | tf_op jit(solution)/shard_map/mix/pallas_call | solution.py:636
  255.2 10.4 %collective-permute-done.29.came_ref = bf16[1,1536,384]{2,1,0:T(8,128)(2,1)} collective-permute-done((bf16[1,1536,384]{2,1,0:T(8,128)(2,1)}, bf16[1,1536,384]{2,1,0:T(8,128)(2,1)}, u32[]{:S(2)}, u32[]{:S(2)}) %collective-permute-start.29) | collective-permute-done | bytes 1179680 | tf_op jit(solution)/shard_map/ppermute | solution.py:1096
  269.6 8.7 %collective-permute-done.34.came_ref = bf16[1,1536,384]{2,1,0:T(8,128)(2,1)S(1)} collective-permute-done((bf16[1,1536,384]{2,1,0:T(8,128)(2,1)S(1)}, bf16[1,1536,384]{2,1,0:T(8,128)(2,1)S(1)}, u32[]{:S(2)}, u32[]{:S(2)}) %collective-permute-start.34) | collective-permute-done | bytes 1179680 | tf_op jit(solution)/shard_map/ppermute | solution.py:1096
  285.7 6.9 %norm_back.1 = (f32[1024,768]{1,0:T(8,128)}, bf16[512,768]{1,0:T(8,128)(2,1)S(1)}, bf16[512,768]{1,0:T(8,128)(2,1)S(1)}, f32[1,768]{1,0:T(1,128)S(1)}) custom-call(s32[3]{0:T(128)S(1)} %copy-done.78, f32[1024,768]{1,0:T(8,128)} %copy-done.52, bf16[1024,768]{1,0:T(8,128)(2,1)S(1)} %collective-permute-done.35.refs_1_, ...), custom_call_target="tpu_custom_call" | custom-call | tf_op jit(solution)/shard_map/norm_back/pallas_call | solution.py:740
  297.2 13.1 %attend_back.1.refs_4_ = bf16[1024,640]{1,0:T(8,128)(2,1)} custom-call(s32[3]{0:T(128)} %copy-done.77, bf16[512,640]{1,0:T(8,128)(2,1)} %get-tuple-element.213.own_ref, bf16[512,640]{1,0:T(8,128)(2,1)} %get-tuple-element.217.other_ref, bf16[512,768]{1,0:T(8,128)(2,1)} %copy-done.53, bf16[512,768]{1,0:T(8,128)(2,1)} %copy-done.54, ...), custom_call_target="tpu_custom_call" | custom-call | tf_op jit(solution)/shard_map/attend_back/pallas_call | solution.py:173
  310.3 3.5 ring_sum.25
  314.4 16.5 %late_grads.1 = (bf16[8,480,384]{2,1,0:T(8,128)(2,1)}, bf16[8,480,384]{2,1,0:T(8,128)(2,1)}) custom-call(s32[3]{0:T(128)} %copy-done.77, bf16[512,768]{1,0:T(8,128)(2,1)} %get-tuple-element.283.refs_0_, bf16[512,768]{1,0:T(8,128)(2,1)} %get-tuple-element.284.refs_1_, bf16[512,768]{1,0:T(8,128)(2,1)} %get-tuple-element.285.refs_2_, ...), custom_call_target="tpu_custom_call" | custom-call | tf_op jit(solution)/shard_map/late_grads/pallas_call | solution.py:237
  330.9 2.5 ring_sum.26
  343.9 14.8 %collective-permute-done.43.came_ref = bf16[1248,384]{1,0:T(8,128)(2,1)S(1)} collective-permute-done((bf16[1248,384]{1,0:T(8,128)(2,1)S(1)}, bf16[1248,384]{1,0:T(8,128)(2,1)S(1)}, u32[]{:S(2)}, u32[]{:S(2)}) %collective-permute-start.43) | collective-permute-done | bytes 958496 | tf_op jit(solution)/shard_map/ppermute | solution.py:1096
  365.3 16.9 %collective-permute-done.45.came_ref = bf16[1248,384]{1,0:T(8,128)(2,1)S(1)} collective-permute-done((bf16[1248,384]{1,0:T(8,128)(2,1)S(1)}, bf16[1248,384]{1,0:T(8,128)(2,1)S(1)}, u32[]{:S(2)}, u32[]{:S(2)}) %collective-permute-start.45) | collective-permute-done | bytes 958496 | tf_op jit(solution)/shard_map/ppermute | solution.py:1096
  387.9 19.0 %collective-permute-done.47.came_ref = bf16[1248,384]{1,0:T(8,128)(2,1)S(1)} collective-permute-done((bf16[1248,384]{1,0:T(8,128)(2,1)S(1)}, bf16[1248,384]{1,0:T(8,128)(2,1)S(1)}, u32[]{:S(2)}, u32[]{:S(2)}) %collective-permute-start.47) | collective-permute-done | bytes 958496 | tf_op jit(solution)/shard_map/ppermute | solution.py:1096
  412.5 18.4 %collective-permute-done.49.came_ref = bf16[1248,384]{1,0:T(8,128)(2,1)S(1)} collective-permute-done((bf16[1248,384]{1,0:T(8,128)(2,1)S(1)}, bf16[1248,384]{1,0:T(8,128)(2,1)S(1)}, u32[]{:S(2)}, u32[]{:S(2)}) %collective-permute-start.49) | collective-permute-done | bytes 958496 | tf_op jit(solution)/shard_map/ppermute | solution.py:1096
  434.5 2.6 convolution_convert_fusion
  439.1 15.0 %collective-permute-done.51.came_ref = bf16[1248,384]{1,0:T(8,128)(2,1)} collective-permute-done((bf16[1248,384]{1,0:T(8,128)(2,1)S(1)}, bf16[1248,384]{1,0:T(8,128)(2,1)}, u32[]{:S(2)}, u32[]{:S(2)}) %collective-permute-start.51) | collective-permute-done | bytes 958496 | tf_op jit(solution)/shard_map/ppermute | solution.py:1096
  463.4 3.8 unpack.21
  467.2 11.1 %collective-permute-done.53.came_ref = bf16[1248,384]{1,0:T(8,128)(2,1)} collective-permute-done((bf16[1248,384]{1,0:T(8,128)(2,1)}, bf16[1248,384]{1,0:T(8,128)(2,1)}, u32[]{:S(2)}, u32[]{:S(2)}) %collective-permute-start.53) | collective-permute-done | bytes 958496 | tf_op jit(solution)/shard_map/ppermute | solution.py:1096
  485.3 2.9 convert_add_fusion.1
  492.8 3.8 unpack.22
  496.6 5.1 collective-permute-done.55.came_ref
  501.7 2.7 late_add.26
  514.6 7.2 %mix.7 = bf16[1024,768]{1,0:T(8,128)(2,1)S(1)} custom-call(s32[63]{0:T(128)S(1)} %fusion.14.order_ref.plan_ref, bf16[8,1024,256]{2,1,0:T(8,128)(2,1)} %copy-done.7, bf16[1,1024,256]{2,1,0:T(8,128)(2,1)S(1)} %copy-done.58, bf16[16,256,768]{2,1,0:T(8,128)(2,1)} %collective-permute-done.18.refs_10_.refs_16_.refs_2_.refs_3_.refs_4_.refs_5_.refs_6_.refs_7_.refs_8_.refs_9_, ...), custom_call_target="tpu_custom_call" | custom-call | tf_op jit(solution)/shard_map/mix/pallas_call | solution.py:636
  522.6 3.6 unpack.23
  528.3 2.6 collective-permute-done.63.refs_0_.refs_1_
  532.9 9.5 %collective-permute-done.67.refs_1_.refs_9_ = bf16[1248,384]{1,0:T(8,128)(2,1)S(1)} collective-permute-done((bf16[1248,384]{1,0:T(8,128)(2,1)S(1)}, bf16[1248,384]{1,0:T(8,128)(2,1)S(1)}, u32[]{:S(2)}, u32[]{:S(2)}) %collective-permute-start.67) | collective-permute-done | bytes 958496 | tf_op jit(solution)/shard_map/ppermute | solution.py:1096
  544.6 7.7 %collective-permute-done.66.refs_0_.refs_2_ = bf16[1248,384]{1,0:T(8,128)(2,1)S(1)} collective-permute-done((bf16[1248,384]{1,0:T(8,128)(2,1)S(1)}, bf16[1248,384]{1,0:T(8,128)(2,1)S(1)}, u32[]{:S(2)}, u32[]{:S(2)}) %collective-permute-start.66) | collective-permute-done | bytes 958496 | tf_op jit(solution)/shard_map/ppermute | solution.py:1096
  554.3 9.5 %collective-permute-done.68.refs_1_.refs_10_ = bf16[1248,384]{1,0:T(8,128)(2,1)S(1)} collective-permute-done((bf16[1248,384]{1,0:T(8,128)(2,1)S(1)}, bf16[1248,384]{1,0:T(8,128)(2,1)S(1)}, u32[]{:S(2)}, u32[]{:S(2)}) %collective-permute-start.68) | collective-permute-done | bytes 958496 | tf_op jit(solution)/shard_map/ppermute | solution.py:1096
  566.0 7.7 %collective-permute-done.72.refs_0_.refs_3_ = bf16[1248,384]{1,0:T(8,128)(2,1)S(1)} collective-permute-done((bf16[1248,384]{1,0:T(8,128)(2,1)S(1)}, bf16[1248,384]{1,0:T(8,128)(2,1)S(1)}, u32[]{:S(2)}, u32[]{:S(2)}) %collective-permute-start.72) | collective-permute-done | bytes 958496 | tf_op jit(solution)/shard_map/ppermute | solution.py:1096
  575.7 10.2 %collective-permute-done.74.refs_1_.refs_11_ = bf16[1248,384]{1,0:T(8,128)(2,1)S(1)} collective-permute-done((bf16[1248,384]{1,0:T(8,128)(2,1)S(1)}, bf16[1248,384]{1,0:T(8,128)(2,1)S(1)}, u32[]{:S(2)}, u32[]{:S(2)}) %collective-permute-start.74) | collective-permute-done | bytes 958496 | tf_op jit(solution)/shard_map/ppermute | solution.py:1096
  588.0 7.1 %collective-permute-done.73.refs_0_.refs_4_ = bf16[1248,384]{1,0:T(8,128)(2,1)S(1)} collective-permute-done((bf16[1248,384]{1,0:T(8,128)(2,1)S(1)}, bf16[1248,384]{1,0:T(8,128)(2,1)S(1)}, u32[]{:S(2)}, u32[]{:S(2)}) %collective-permute-start.73) | collective-permute-done | bytes 958496 | tf_op jit(solution)/shard_map/ppermute | solution.py:1096
  597.1 10.9 %collective-permute-done.76.refs_1_.refs_12_ = bf16[1248,384]{1,0:T(8,128)(2,1)S(1)} collective-permute-done((bf16[1248,384]{1,0:T(8,128)(2,1)S(1)}, bf16[1248,384]{1,0:T(8,128)(2,1)S(1)}, u32[]{:S(2)}, u32[]{:S(2)}) %collective-permute-start.76) | collective-permute-done | bytes 958496 | tf_op jit(solution)/shard_map/ppermute | solution.py:1096
  610.1 6.4 collective-permute-done.75.refs_0_.refs_5_
  618.8 12.1 %collective-permute-done.78.refs_1_.refs_13_ = bf16[1248,384]{1,0:T(8,128)(2,1)S(1)} collective-permute-done((bf16[1248,384]{1,0:T(8,128)(2,1)S(1)}, bf16[1248,384]{1,0:T(8,128)(2,1)S(1)}, u32[]{:S(2)}, u32[]{:S(2)}) %collective-permute-start.78) | collective-permute-done | bytes 958496 | tf_op jit(solution)/shard_map/ppermute | solution.py:1096
  634.6 4.1 collective-permute-done.77.refs_0_.refs_6_
  638.7 2.5 collective-permute-start.79
  641.2 13.3 %collective-permute-done.80.refs_1_.refs_14_ = bf16[1248,384]{1,0:T(8,128)(2,1)S(1)} collective-permute-done((bf16[1248,384]{1,0:T(8,128)(2,1)S(1)}, bf16[1248,384]{1,0:T(8,128)(2,1)S(1)}, u32[]{:S(2)}, u32[]{:S(2)}) %collective-permute-start.80) | collective-permute-done | bytes 958496 | tf_op jit(solution)/shard_map/ppermute | solution.py:1096
  655.9 2.7 fusion.4
  662.0 6.6 collective-permute-done.81.refs_15_.refs_1_
  669.6 7.8 %unpack_late.1 = (f32[768,512]{1,0:T(8,128)}, f32[768,512]{1,0:T(8,128)}, f32[512,768]{1,0:T(8,128)}, f32[768,768]{1,0:T(8,128)}, f32[768,256]{1,0:T(8,128)}, /*...) custom-call(s32[63]{0:T(128)S(1)} %fusion.14.order_ref.plan_ref, ...), custom_call_target="tpu_custom_call" | custom-call | tf_op jit(solution)/shard_map/unpack_late/pallas_call | solution.py:1009
  (413 shorter events, 179.6 us)
Async XLA Ops:
  0.7 34.4 %collective-permute-start.16 = (bf16[16,768,256]{2,1,0:T(8,128)(2,1)}, bf16[16,768,256]{2,1,0:T(8,128)(2,1)}, u32[]{:S(2)}, u32[]{:S(2)}) collective-permute-start(bf16[16,768,256]{2,1,0:T(8,128)(2,1)} %refs_16_.1), channel_id=1, source_target_pairs={{0,1},{1,0},{2,3},{3,2},{4,5},{5,4},{6,7},{7,6},{8,9},{9,8},{10,11... | collective-permute-start | bytes 18874376 | tf_op jit(solution)/shard_map/ppermute | solution.py:51
  5.4 27.1 %collective-permute-start = (bf16[512,768]{1,0:T(8,128)(2,1)S(1)}, bf16[512,768]{1,0:T(8,128)(2,1)}, u32[]{:S(2)}, u32[]{:S(2)}) collective-permute-start(bf16[512,768]{1,0:T(8,128)(2,1)S(1)} %copy-done.84), channel_id=1, source_target_pairs={{0,2},{2,0},{1,3},{3,1},{4,6},{6,4},{5,7},{7,5},{8,10},{10,8},{9,1... | collective-permute-start | bytes 2359304 | tf_op jit(solution)/shard_map/ppermute | solution.py:51
  13.3 19.1 %collective-permute-start.4 = (bf16[192,768]{1,0:T(8,128)(2,1)}, bf16[192,768]{1,0:T(8,128)(2,1)S(1)}, u32[]{:S(2)}, u32[]{:S(2)}) collective-permute-start(bf16[192,768]{1,0:T(8,128)(2,1)} %get-tuple-element.214), channel_id=1, source_target_pairs={{0,2},{2,0},{1,3},{3,1},{4,6},{6,4},{5,7},{7,5},{8,10},{10,8},{9,1... | collective-permute-start | bytes 884744 | tf_op jit(solution)/shard_map/ppermute | solution.py:51
  34.9 62.0 %collective-permute-start.18 = (bf16[16,256,768]{2,1,0:T(8,128)(2,1)}, bf16[16,256,768]{2,1,0:T(8,128)(2,1)}, u32[]{:S(2)}, u32[]{:S(2)}) collective-permute-start(bf16[16,256,768]{2,1,0:T(8,128)(2,1)} %refs_9_.13), channel_id=1, source_target_pairs={{0,1},{1,0},{2,3},{3,2},{4,5},{5,4},{6,7},{7,6},{8,9},{9,8},{10,11... | collective-permute-start | bytes 18874376 | tf_op jit(solution)/shard_map/ppermute | solution.py:51
  35.8 61.1 %collective-permute-start.17 = (bf16[16,768,256]{2,1,0:T(8,128)(2,1)}, bf16[16,768,256]{2,1,0:T(8,128)(2,1)}, u32[]{:S(2)}, u32[]{:S(2)}) collective-permute-start(bf16[16,768,256]{2,1,0:T(8,128)(2,1)} %refs_17_.1), channel_id=1, source_target_pairs={{0,1},{1,0},{2,3},{3,2},{4,5},{5,4},{6,7},{7,6},{8,9},{9,8},{10,11... | collective-permute-start | bytes 18874376 | tf_op jit(solution)/shard_map/ppermute | solution.py:51
  35.9 19.8 %collective-permute-start.5 = (bf16[512,768]{1,0:T(8,128)(2,1)S(1)}, bf16[512,768]{1,0:T(8,128)(2,1)S(1)}, u32[]{:S(2)}, u32[]{:S(2)}) collective-permute-start(bf16[512,768]{1,0:T(8,128)(2,1)S(1)} %copy-done.67), channel_id=1, source_target_pairs={{0,2},{2,0},{1,3},{3,1},{4,6},{6,4},{5,7},{7,5},{8,10},{10,8},{9,1... | collective-permute-start | bytes 2359304 | tf_op jit(solution)/shard_map/ppermute | solution.py:51
  39.2 11.5 %collective-permute-start.7 = (bf16[192,768]{1,0:T(8,128)(2,1)S(1)}, bf16[192,768]{1,0:T(8,128)(2,1)S(1)}, u32[]{:S(2)}, u32[]{:S(2)}) collective-permute-start(bf16[192,768]{1,0:T(8,128)(2,1)S(1)} %collective-permute-done.4.refs_0_), channel_id=1, source_target_pairs={{0,8},{4,12},{8,0},{12,4},{16,24},{20,28},{24,16},{28,20},{1,9},{5... | collective-permute-start | bytes 884744 | tf_op jit(solution)/shard_map/ppermute | solution.py:1132
  50.6 17.8 %collective-permute-start.11 = (bf16[768,768]{1,0:T(8,128)(2,1)}, bf16[768,768]{1,0:T(8,128)(2,1)}, u32[]{:S(2)}, u32[]{:S(2)}) collective-permute-start(bf16[768,768]{1,0:T(8,128)(2,1)} %refs_4_.5), channel_id=1, source_target_pairs={{0,1},{1,0},{2,3},{3,2},{4,5},{5,4},{6,7},{7,6},{8,9},{9,8},{10,11... | collective-permute-start | bytes 3538952 | tf_op jit(solution)/shard_map/ppermute | solution.py:51
  63.8 20.3 %collective-permute-start.12 = (bf16[1024,384]{1,0:T(8,128)(2,1)}, bf16[1024,384]{1,0:T(8,128)(2,1)}, u32[]{:S(2)}, u32[]{:S(2)}) collective-permute-start(bf16[1024,384]{1,0:T(8,128)(2,1)} %attend.1.refs_4_.refs_5_), channel_id=1, source_target_pairs={{0,2},{2,0},{1,3},{3,1},{4,6},{6,4},{5,7},{7,5},{8,10},{10,8},{9,1... | collective-permute-start | bytes 2359304 | tf_op jit(solution)/shard_map/ppermute | solution.py:51
  67.2 29.7 %collective-permute-start.15 = (bf16[1024,768]{1,0:T(8,128)(2,1)S(1)}, bf16[1024,768]{1,0:T(8,128)(2,1)S(1)}, u32[]{:S(2)}, u32[]{:S(2)}) collective-permute-start(bf16[1024,768]{1,0:T(8,128)(2,1)S(1)} %join.3.refs_2_.refs_4_), channel_id=1, source_target_pairs={{0,1},{1,0},{2,3},{3,2},{4,5},{5,4},{6,7},{7,6},{8,9},{9,8},{10,11... | collective-permute-start | bytes 4718600 | tf_op jit(solution)/shard_map/ppermute | solution.py:51
  68.4 15.8 %collective-permute-start.14 = (bf16[768,768]{1,0:T(8,128)(2,1)}, bf16[768,768]{1,0:T(8,128)(2,1)}, u32[]{:S(2)}, u32[]{:S(2)}) collective-permute-start(bf16[768,768]{1,0:T(8,128)(2,1)} %join.2.refs_4_), channel_id=1, source_target_pairs={{0,1},{1,0},{2,3},{3,2},{4,5},{5,4},{6,7},{7,6},{8,9},{9,8},{10,11... | collective-permute-start | bytes 3538952 | tf_op jit(solution)/shard_map/ppermute | solution.py:51
  111.4 32.9 %collective-permute-start.19 = (bf16[1,1536,384]{2,1,0:T(8,128)(2,1)S(1)}, bf16[1,1536,384]{2,1,0:T(8,128)(2,1)S(1)}, u32[]{:S(2)}, u32[]{:S(2)}) collective-permute-start(bf16[1,1536,384]{2,1,0:T(8,128)(2,1)S(1)} %get-tuple-element.229), channel_id=1, source_target_pairs={{0,8},{8,16},{16,24},{24,28},{28,20},{20,12},{12,4},{4,0},{9,1},{1... | collective-permute-start | bytes 3538952 | tf_op jit(solution)/shard_map/ppermute | solution.py:1096
  128.2 35.8 %collective-permute-start.21 = (bf16[1,1536,384]{2,1,0:T(8,128)(2,1)S(1)}, bf16[1,1536,384]{2,1,0:T(8,128)(2,1)S(1)}, u32[]{:S(2)}, u32[]{:S(2)}) collective-permute-start(bf16[1,1536,384]{2,1,0:T(8,128)(2,1)S(1)} %get-tuple-element.239), channel_id=1, source_target_pairs={{8,0},{16,8},{24,16},{28,24},{20,28},{12,20},{4,12},{0,4},{1,9},{9... | collective-permute-start | bytes 3538952 | tf_op jit(solution)/shard_map/ppermute | solution.py:1096
  146.8 33.5 %collective-permute-start.20 = (bf16[1,1536,384]{2,1,0:T(8,128)(2,1)}, bf16[1,1536,384]{2,1,0:T(8,128)(2,1)S(1)}, u32[]{:S(2)}, u32[]{:S(2)}) collective-permute-start(bf16[1,1536,384]{2,1,0:T(8,128)(2,1)} %ring_sum.14), channel_id=1, source_target_pairs={{0,8},{8,16},{16,24},{24,28},{28,20},{20,12},{12,4},{4,0},{9,1},{1... | collective-permute-start | bytes 3538952 | tf_op jit(solution)/shard_map/ppermute | solution.py:1096
  167.6 27.6 %collective-permute-start.23 = (bf16[1,1536,384]{2,1,0:T(8,128)(2,1)S(1)}, bf16[1,1536,384]{2,1,0:T(8,128)(2,1)S(1)}, u32[]{:S(2)}, u32[]{:S(2)}) collective-permute-start(bf16[1,1536,384]{2,1,0:T(8,128)(2,1)S(1)} %ring_sum.15), channel_id=1, source_target_pairs={{8,0},{16,8},{24,16},{28,24},{20,28},{12,20},{4,12},{0,4},{1,9},{9... | collective-permute-start | bytes 3538952 | tf_op jit(solution)/shard_map/ppermute | solution.py:1096
  168.1 18.7 %collective-permute-start.24 = (bf16[1,768,512]{2,1,0:T(8,128)(2,1)S(1)}, bf16[1,768,512]{2,1,0:T(8,128)(2,1)S(1)}, u32[]{:S(2)}, u32[]{:S(2)}) collective-permute-start(bf16[1,768,512]{2,1,0:T(8,128)(2,1)S(1)} %bitcast.29), channel_id=1, source_target_pairs={{0,1},{1,0},{2,3},{3,2},{4,5},{5,4},{6,7},{7,6},{8,9},{9,8},{10,11... | collective-permute-start | bytes 2359304 | tf_op jit(solution)/shard_map/ppermute | solution.py:51
  168.1 18.6 %collective-permute-start.25 = (bf16[1,768,512]{2,1,0:T(8,128)(2,1)S(1)}, bf16[1,768,512]{2,1,0:T(8,128)(2,1)S(1)}, u32[]{:S(2)}, u32[]{:S(2)}) collective-permute-start(bf16[1,768,512]{2,1,0:T(8,128)(2,1)S(1)} %bitcast.34), channel_id=1, source_target_pairs={{0,1},{1,0},{2,3},{3,2},{4,5},{5,4},{6,7},{7,6},{8,9},{9,8},{10,11... | collective-permute-start | bytes 2359304 | tf_op jit(solution)/shard_map/ppermute | solution.py:51
  168.6 18.2 %collective-permute-start.26 = (bf16[1,512,768]{2,1,0:T(8,128)(2,1)S(1)}, bf16[1,512,768]{2,1,0:T(8,128)(2,1)S(1)}, u32[]{:S(2)}, u32[]{:S(2)}) collective-permute-start(bf16[1,512,768]{2,1,0:T(8,128)(2,1)S(1)} %bitcast.39), channel_id=1, source_target_pairs={{0,1},{1,0},{2,3},{3,2},{4,5},{5,4},{6,7},{7,6},{8,9},{9,8},{10,11... | collective-permute-start | bytes 2359304 | tf_op jit(solution)/shard_map/ppermute | solution.py:51
  185.2 24.5 %collective-permute-start.22 = (bf16[1,1536,384]{2,1,0:T(8,128)(2,1)}, bf16[1,1536,384]{2,1,0:T(8,128)(2,1)}, u32[]{:S(2)}, u32[]{:S(2)}) collective-permute-start(bf16[1,1536,384]{2,1,0:T(8,128)(2,1)} %ring_sum.16), channel_id=1, source_target_pairs={{0,8},{8,16},{16,24},{24,28},{28,20},{20,12},{12,4},{4,0},{9,1},{1... | collective-permute-start | bytes 3538952 | tf_op jit(solution)/shard_map/ppermute | solution.py:1096
  196.6 32.6 %collective-permute-start.28 = (bf16[1,1536,384]{2,1,0:T(8,128)(2,1)S(1)}, bf16[1,1536,384]{2,1,0:T(8,128)(2,1)S(1)}, u32[]{:S(2)}, u32[]{:S(2)}) collective-permute-start(bf16[1,1536,384]{2,1,0:T(8,128)(2,1)S(1)} %ring_sum.17), channel_id=1, source_target_pairs={{8,0},{16,8},{24,16},{28,24},{20,28},{12,20},{4,12},{0,4},{1,9},{9... | collective-permute-start | bytes 3538952 | tf_op jit(solution)/shard_map/ppermute | solution.py:1096
  213.5 28.6 %collective-permute-start.27 = (bf16[1,1536,384]{2,1,0:T(8,128)(2,1)}, bf16[1,1536,384]{2,1,0:T(8,128)(2,1)S(1)}, u32[]{:S(2)}, u32[]{:S(2)}) collective-permute-start(bf16[1,1536,384]{2,1,0:T(8,128)(2,1)} %ring_sum.18), channel_id=1, source_target_pairs={{0,8},{8,16},{16,24},{24,28},{28,20},{20,12},{12,4},{4,0},{9,1},{1... | collective-permute-start | bytes 3538952 | tf_op jit(solution)/shard_map/ppermute | solution.py:1096
  232.6 21.7 %collective-permute-start.33 = (bf16[1,1536,384]{2,1,0:T(8,128)(2,1)}, bf16[1,1536,384]{2,1,0:T(8,128)(2,1)S(1)}, u32[]{:S(2)}, u32[]{:S(2)}) collective-permute-start(bf16[1,1536,384]{2,1,0:T(8,128)(2,1)} %ring_sum.19), channel_id=1, source_target_pairs={{8,0},{16,8},{24,16},{28,24},{20,28},{12,20},{4,12},{0,4},{1,9},{9... | collective-permute-start | bytes 3538952 | tf_op jit(solution)/shard_map/ppermute | solution.py:1096
  244.3 21.4 %collective-permute-start.29 = (bf16[1,1536,384]{2,1,0:T(8,128)(2,1)}, bf16[1,1536,384]{2,1,0:T(8,128)(2,1)}, u32[]{:S(2)}, u32[]{:S(2)}) collective-permute-start(bf16[1,1536,384]{2,1,0:T(8,128)(2,1)} %ring_sum.20), channel_id=1, source_target_pairs={{0,8},{8,16},{16,24},{24,28},{28,20},{20,12},{12,4},{4,0},{9,1},{1... | collective-permute-start | bytes 3538952 | tf_op jit(solution)/shard_map/ppermute | solution.py:1096
  245.8 39.9 %collective-permute-start.35 = (bf16[1024,768]{1,0:T(8,128)(2,1)}, bf16[1024,768]{1,0:T(8,128)(2,1)S(1)}, u32[]{:S(2)}, u32[]{:S(2)}) collective-permute-start(bf16[1024,768]{1,0:T(8,128)(2,1)} %get-tuple-element.267), channel_id=1, source_target_pairs={{0,2},{2,0},{1,3},{3,1},{4,6},{6,4},{5,7},{7,5},{8,10},{10,8},{9,1... | collective-permute-start | bytes 4718600 | tf_op jit(solution)/shard_map/ppermute | solution.py:51
  254.7 23.6 %collective-permute-start.34 = (bf16[1,1536,384]{2,1,0:T(8,128)(2,1)S(1)}, bf16[1,1536,384]{2,1,0:T(8,128)(2,1)S(1)}, u32[]{:S(2)}, u32[]{:S(2)}) collective-permute-start(bf16[1,1536,384]{2,1,0:T(8,128)(2,1)S(1)} %ring_sum.22), channel_id=1, source_target_pairs={{8,0},{16,8},{24,16},{28,24},{20,28},{12,20},{4,12},{0,4},{1,9},{9... | collective-permute-start | bytes 3538952 | tf_op jit(solution)/shard_map/ppermute | solution.py:1096
  268.0 25.1 %collective-permute-start.32 = (bf16[1,1536,384]{2,1,0:T(8,128)(2,1)S(1)}, bf16[1,1536,384]{2,1,0:T(8,128)(2,1)S(1)}, u32[]{:S(2)}, u32[]{:S(2)}) collective-permute-start(bf16[1,1536,384]{2,1,0:T(8,128)(2,1)S(1)} %ring_sum.21), channel_id=1, source_target_pairs={{0,8},{8,16},{16,24},{24,28},{28,20},{20,12},{12,4},{4,0},{9,1},{1... | collective-permute-start | bytes 3538952 | tf_op jit(solution)/shard_map/ppermute | solution.py:1096
  280.0 30.3 %collective-permute-start.39 = (bf16[1,1536,384]{2,1,0:T(8,128)(2,1)}, bf16[1,1536,384]{2,1,0:T(8,128)(2,1)}, u32[]{:S(2)}, u32[]{:S(2)}) collective-permute-start(bf16[1,1536,384]{2,1,0:T(8,128)(2,1)} %ring_sum.23), channel_id=1, source_target_pairs={{8,0},{16,8},{24,16},{28,24},{20,28},{12,20},{4,12},{0,4},{1,9},{9... | collective-permute-start | bytes 3538952 | tf_op jit(solution)/shard_map/ppermute | solution.py:1096
  294.8 36.1 %collective-permute-start.42 = (bf16[1,1536,384]{2,1,0:T(8,128)(2,1)}, bf16[1,1536,384]{2,1,0:T(8,128)(2,1)}, u32[]{:S(2)}, u32[]{:S(2)}) collective-permute-start(bf16[1,1536,384]{2,1,0:T(8,128)(2,1)} %ring_sum.24), channel_id=1, source_target_pairs={{0,8},{8,16},{16,24},{24,28},{28,20},{20,12},{12,4},{4,0},{9,1},{1... | collective-permute-start | bytes 3538952 | tf_op jit(solution)/shard_map/ppermute | solution.py:1096
  313.8 24.3 %collective-permute-start.44 = (bf16[1,1536,384]{2,1,0:T(8,128)(2,1)}, bf16[1,1536,384]{2,1,0:T(8,128)(2,1)}, u32[]{:S(2)}, u32[]{:S(2)}) collective-permute-start(bf16[1,1536,384]{2,1,0:T(8,128)(2,1)} %ring_sum.25), channel_id=1, source_target_pairs={{8,0},{16,8},{24,16},{28,24},{20,28},{12,20},{4,12},{0,4},{1,9},{9... | collective-permute-start | bytes 3538952 | tf_op jit(solution)/shard_map/ppermute | solution.py:1096
  336.6 22.0 %collective-permute-start.43 = (bf16[1248,384]{1,0:T(8,128)(2,1)S(1)}, bf16[1248,384]{1,0:T(8,128)(2,1)S(1)}, u32[]{:S(2)}, u32[]{:S(2)}) collective-permute-start(bf16[1248,384]{1,0:T(8,128)(2,1)S(1)} %late_load.2.refs_0_), channel_id=1, source_target_pairs={{0,8},{8,16},{16,24},{24,28},{28,20},{20,12},{12,4},{4,0},{9,1},{1... | collective-permute-start | bytes 2875400 | tf_op jit(solution)/shard_map/ppermute | solution.py:1096
  341.2 20.7 %collective-permute-start.46 = (bf16[1248,384]{1,0:T(8,128)(2,1)S(1)}, bf16[1248,384]{1,0:T(8,128)(2,1)S(1)}, u32[]{:S(2)}, u32[]{:S(2)}) collective-permute-start(bf16[1248,384]{1,0:T(8,128)(2,1)S(1)} %late_load.3.refs_1_), channel_id=1, source_target_pairs={{8,0},{16,8},{24,16},{28,24},{20,28},{12,20},{4,12},{0,4},{1,9},{9... | collective-permute-start | bytes 2875400 | tf_op jit(solution)/shard_map/ppermute | solution.py:1096
  359.4 22.8 %collective-permute-start.45 = (bf16[1248,384]{1,0:T(8,128)(2,1)S(1)}, bf16[1248,384]{1,0:T(8,128)(2,1)S(1)}, u32[]{:S(2)}, u32[]{:S(2)}) collective-permute-start(bf16[1248,384]{1,0:T(8,128)(2,1)S(1)} %late_add.14.refs_0_), channel_id=1, source_target_pairs={{0,8},{8,16},{16,24},{24,28},{28,20},{20,12},{12,4},{4,0},{9,1},{1... | collective-permute-start | bytes 2875400 | tf_op jit(solution)/shard_map/ppermute | solution.py:1096
  362.6 21.8 %collective-permute-start.48 = (bf16[1248,384]{1,0:T(8,128)(2,1)S(1)}, bf16[1248,384]{1,0:T(8,128)(2,1)S(1)}, u32[]{:S(2)}, u32[]{:S(2)}) collective-permute-start(bf16[1248,384]{1,0:T(8,128)(2,1)S(1)} %late_add.15.refs_1_), channel_id=1, source_target_pairs={{8,0},{16,8},{24,16},{28,24},{20,28},{12,20},{4,12},{0,4},{1,9},{9... | collective-permute-start | bytes 2875400 | tf_op jit(solution)/shard_map/ppermute | solution.py:1096
  382.9 23.9 %collective-permute-start.47 = (bf16[1248,384]{1,0:T(8,128)(2,1)S(1)}, bf16[1248,384]{1,0:T(8,128)(2,1)S(1)}, u32[]{:S(2)}, u32[]{:S(2)}) collective-permute-start(bf16[1248,384]{1,0:T(8,128)(2,1)S(1)} %late_add.16.refs_0_), channel_id=1, source_target_pairs={{0,8},{8,16},{16,24},{24,28},{28,20},{20,12},{12,4},{4,0},{9,1},{1... | collective-permute-start | bytes 2875400 | tf_op jit(solution)/shard_map/ppermute | solution.py:1096
  385.1 23.9 %collective-permute-start.50 = (bf16[1248,384]{1,0:T(8,128)(2,1)S(1)}, bf16[1248,384]{1,0:T(8,128)(2,1)S(1)}, u32[]{:S(2)}, u32[]{:S(2)}) collective-permute-start(bf16[1248,384]{1,0:T(8,128)(2,1)S(1)} %late_add.17.refs_1_), channel_id=1, source_target_pairs={{8,0},{16,8},{24,16},{28,24},{20,28},{12,20},{4,12},{0,4},{1,9},{9... | collective-permute-start | bytes 2875400 | tf_op jit(solution)/shard_map/ppermute | solution.py:1096
  407.6 23.3 %collective-permute-start.49 = (bf16[1248,384]{1,0:T(8,128)(2,1)S(1)}, bf16[1248,384]{1,0:T(8,128)(2,1)S(1)}, u32[]{:S(2)}, u32[]{:S(2)}) collective-permute-start(bf16[1248,384]{1,0:T(8,128)(2,1)S(1)} %late_add.18.refs_0_), channel_id=1, source_target_pairs={{0,8},{8,16},{16,24},{24,28},{28,20},{20,12},{12,4},{4,0},{9,1},{1... | collective-permute-start | bytes 2875400 | tf_op jit(solution)/shard_map/ppermute | solution.py:1096
  409.8 23.3 %collective-permute-start.52 = (bf16[1248,384]{1,0:T(8,128)(2,1)S(1)}, bf16[1248,384]{1,0:T(8,128)(2,1)S(1)}, u32[]{:S(2)}, u32[]{:S(2)}) collective-permute-start(bf16[1248,384]{1,0:T(8,128)(2,1)S(1)} %late_add.19.refs_1_), channel_id=1, source_target_pairs={{8,0},{16,8},{24,16},{28,24},{20,28},{12,20},{4,12},{0,4},{1,9},{9... | collective-permute-start | bytes 2875400 | tf_op jit(solution)/shard_map/ppermute | solution.py:1096
  431.6 22.6 %collective-permute-start.51 = (bf16[1248,384]{1,0:T(8,128)(2,1)S(1)}, bf16[1248,384]{1,0:T(8,128)(2,1)}, u32[]{:S(2)}, u32[]{:S(2)}) collective-permute-start(bf16[1248,384]{1,0:T(8,128)(2,1)S(1)} %late_add.20.refs_0_), channel_id=1, source_target_pairs={{0,8},{8,16},{16,24},{24,28},{28,20},{20,12},{12,4},{4,0},{9,1},{1... | collective-permute-start | bytes 2875400 | tf_op jit(solution)/shard_map/ppermute | solution.py:1096
  433.8 24.2 %collective-permute-start.54 = (bf16[1248,384]{1,0:T(8,128)(2,1)S(1)}, bf16[1248,384]{1,0:T(8,128)(2,1)}, u32[]{:S(2)}, u32[]{:S(2)}) collective-permute-start(bf16[1248,384]{1,0:T(8,128)(2,1)S(1)} %late_add.21.refs_1_), channel_id=1, source_target_pairs={{8,0},{16,8},{24,16},{28,24},{20,28},{12,20},{4,12},{0,4},{1,9},{9... | collective-permute-start | bytes 2875400 | tf_op jit(solution)/shard_map/ppermute | solution.py:1096
  437.1 48.2 %collective-permute-start.59 = (bf16[1024,768]{1,0:T(8,128)(2,1)}, bf16[1024,768]{1,0:T(8,128)(2,1)}, u32[]{:S(2)}, u32[]{:S(2)}) collective-permute-start(bf16[1024,768]{1,0:T(8,128)(2,1)} %convolution_convert_fusion), channel_id=1, source_target_pairs={{0,1},{1,0},{2,3},{3,2},{4,5},{5,4},{6,7},{7,6},{8,9},{9,8},{10,11... | collective-permute-start | bytes 4718600 | tf_op jit(solution)/shard_map/ppermute | solution.py:51
  456.6 21.8 %collective-permute-start.53 = (bf16[1248,384]{1,0:T(8,128)(2,1)}, bf16[1248,384]{1,0:T(8,128)(2,1)}, u32[]{:S(2)}, u32[]{:S(2)}) collective-permute-start(bf16[1248,384]{1,0:T(8,128)(2,1)} %late_add.22.refs_0_), channel_id=1, source_target_pairs={{0,8},{8,16},{16,24},{24,28},{28,20},{20,12},{12,4},{4,0},{9,1},{1... | collective-permute-start | bytes 2875400 | tf_op jit(solution)/shard_map/ppermute | solution.py:1096
  460.3 21.8 %collective-permute-start.56 = (bf16[1248,384]{1,0:T(8,128)(2,1)}, bf16[1248,384]{1,0:T(8,128)(2,1)}, u32[]{:S(2)}, u32[]{:S(2)}) collective-permute-start(bf16[1248,384]{1,0:T(8,128)(2,1)} %late_add.23.refs_1_), channel_id=1, source_target_pairs={{8,0},{16,8},{24,16},{28,24},{20,28},{12,20},{4,12},{0,4},{1,9},{9... | collective-permute-start | bytes 2875400 | tf_op jit(solution)/shard_map/ppermute | solution.py:1096
  480.7 21.0 %collective-permute-start.55 = (bf16[1248,384]{1,0:T(8,128)(2,1)}, bf16[1248,384]{1,0:T(8,128)(2,1)}, u32[]{:S(2)}, u32[]{:S(2)}) collective-permute-start(bf16[1248,384]{1,0:T(8,128)(2,1)} %late_add.24.refs_0_), channel_id=1, source_target_pairs={{0,8},{8,16},{16,24},{24,28},{28,20},{20,12},{12,4},{4,0},{9,1},{1... | collective-permute-start | bytes 2875400 | tf_op jit(solution)/shard_map/ppermute | solution.py:1096
  484.5 19.9 %collective-permute-start.57 = (bf16[1248,384]{1,0:T(8,128)(2,1)}, bf16[1248,384]{1,0:T(8,128)(2,1)}, u32[]{:S(2)}, u32[]{:S(2)}) collective-permute-start(bf16[1248,384]{1,0:T(8,128)(2,1)} %late_add.25.refs_1_), channel_id=1, source_target_pairs={{8,0},{16,8},{24,16},{28,24},{20,28},{12,20},{4,12},{0,4},{1,9},{9... | collective-permute-start | bytes 2875400 | tf_op jit(solution)/shard_map/ppermute | solution.py:1096
  490.8 16.5 %collective-permute-start.60 = (bf16[512,768]{1,0:T(8,128)(2,1)}, bf16[512,768]{1,0:T(8,128)(2,1)}, u32[]{:S(2)}, u32[]{:S(2)}) collective-permute-start(bf16[512,768]{1,0:T(8,128)(2,1)} %dynamic-slice_convert_fusion.1), channel_id=1, source_target_pairs={{0,2},{2,0},{1,3},{3,1},{4,6},{6,4},{5,7},{7,5},{8,10},{10,8},{9,1... | collective-permute-start | bytes 2359304 | tf_op jit(solution)/shard_map/ppermute | solution.py:51
  492.2 20.8 %collective-permute-start.62 = (bf16[1,768,384]{2,1,0:T(8,128)(2,1)}, bf16[1,768,384]{2,1,0:T(8,128)(2,1)S(1)}, u32[]{:S(2)}, u32[]{:S(2)}) collective-permute-start(bf16[1,768,384]{2,1,0:T(8,128)(2,1)} %copy-done.83), channel_id=1, source_target_pairs={{0,1},{1,0},{2,3},{3,2},{4,5},{5,4},{6,7},{7,6},{8,9},{9,8},{10,11... | collective-permute-start | bytes 1769480 | tf_op jit(solution)/shard_map/ppermute | solution.py:51
  492.3 29.5 %collective-permute-start.65 = (bf16[1,768,384]{2,1,0:T(8,128)(2,1)}, bf16[1,768,384]{2,1,0:T(8,128)(2,1)S(1)}, u32[]{:S(2)}, u32[]{:S(2)}) collective-permute-start(bf16[1,768,384]{2,1,0:T(8,128)(2,1)} %copy-done.82), channel_id=1, source_target_pairs={{0,1},{1,0},{2,3},{3,2},{4,5},{5,4},{6,7},{7,6},{8,9},{9,8},{10,11... | collective-permute-start | bytes 1769480 | tf_op jit(solution)/shard_map/ppermute | solution.py:51
  506.7 15.1 %collective-permute-start.64 = (bf16[480,384]{1,0:T(8,128)(2,1)S(1)}, bf16[480,384]{1,0:T(8,128)(2,1)S(1)}, u32[]{:S(2)}, u32[]{:S(2)}) collective-permute-start(bf16[480,384]{1,0:T(8,128)(2,1)S(1)} %get-tuple-element.341.mine_ref), channel_id=1, source_target_pairs={{0,1},{1,0},{2,3},{3,2},{4,5},{5,4},{6,7},{7,6},{8,9},{9,8},{10,11... | collective-permute-start | bytes 1105928 | tf_op jit(solution)/shard_map/ppermute | solution.py:51
  513.1 17.8 %collective-permute-start.63 = (bf16[1248,384]{1,0:T(8,128)(2,1)S(1)}, bf16[1248,384]{1,0:T(8,128)(2,1)S(1)}, u32[]{:S(2)}, u32[]{:S(2)}) collective-permute-start(bf16[1248,384]{1,0:T(8,128)(2,1)S(1)} %late_join.2.refs_0_), channel_id=1, source_target_pairs={{0,8},{8,16},{16,24},{24,28},{28,20},{20,12},{12,4},{4,0},{9,1},{1... | collective-permute-start | bytes 2875400 | tf_op jit(solution)/shard_map/ppermute | solution.py:1096
  522.0 20.5 %collective-permute-start.67 = (bf16[1248,384]{1,0:T(8,128)(2,1)S(1)}, bf16[1248,384]{1,0:T(8,128)(2,1)S(1)}, u32[]{:S(2)}, u32[]{:S(2)}) collective-permute-start(bf16[1248,384]{1,0:T(8,128)(2,1)S(1)} %late_join.3.refs_1_.refs_8_), channel_id=1, source_target_pairs={{8,0},{16,8},{24,16},{28,24},{20,28},{12,20},{4,12},{0,4},{1,9},{9... | collective-permute-start | bytes 2875400 | tf_op jit(solution)/shard_map/ppermute | solution.py:1096
  530.9 21.4 %collective-permute-start.66 = (bf16[1248,384]{1,0:T(8,128)(2,1)S(1)}, bf16[1248,384]{1,0:T(8,128)(2,1)S(1)}, u32[]{:S(2)}, u32[]{:S(2)}) collective-permute-start(bf16[1248,384]{1,0:T(8,128)(2,1)S(1)} %collective-permute-done.63.refs_0_.refs_1_), channel_id=1, source_target_pairs={{0,8},{8,16},{16,24},{24,28},{28,20},{20,12},{12,4},{4,0},{9,1},{1... | collective-permute-start | bytes 2875400 | tf_op jit(solution)/shard_map/ppermute | solution.py:1096
  542.4 21.4 %collective-permute-start.68 = (bf16[1248,384]{1,0:T(8,128)(2,1)S(1)}, bf16[1248,384]{1,0:T(8,128)(2,1)S(1)}, u32[]{:S(2)}, u32[]{:S(2)}) collective-permute-start(bf16[1248,384]{1,0:T(8,128)(2,1)S(1)} %collective-permute-done.67.refs_1_.refs_9_), channel_id=1, source_target_pairs={{8,0},{16,8},{24,16},{28,24},{20,28},{12,20},{4,12},{0,4},{1,9},{9... | collective-permute-start | bytes 2875400 | tf_op jit(solution)/shard_map/ppermute | solution.py:1096
  552.3 21.4 %collective-permute-start.72 = (bf16[1248,384]{1,0:T(8,128)(2,1)S(1)}, bf16[1248,384]{1,0:T(8,128)(2,1)S(1)}, u32[]{:S(2)}, u32[]{:S(2)}) collective-permute-start(bf16[1248,384]{1,0:T(8,128)(2,1)S(1)} %collective-permute-done.66.refs_0_.refs_2_), channel_id=1, source_target_pairs={{0,8},{8,16},{16,24},{24,28},{28,20},{20,12},{12,4},{4,0},{9,1},{1... | collective-permute-start | bytes 2875400 | tf_op jit(solution)/shard_map/ppermute | solution.py:1096
  563.8 22.1 %collective-permute-start.74 = (bf16[1248,384]{1,0:T(8,128)(2,1)S(1)}, bf16[1248,384]{1,0:T(8,128)(2,1)S(1)}, u32[]{:S(2)}, u32[]{:S(2)}) collective-permute-start(bf16[1248,384]{1,0:T(8,128)(2,1)S(1)} %collective-permute-done.68.refs_1_.refs_10_), channel_id=1, source_target_pairs={{8,0},{16,8},{24,16},{28,24},{20,28},{12,20},{4,12},{0,4},{1,9},{9... | collective-permute-start | bytes 2875400 | tf_op jit(solution)/shard_map/ppermute | solution.py:1096
  573.7 21.4 %collective-permute-start.73 = (bf16[1248,384]{1,0:T(8,128)(2,1)S(1)}, bf16[1248,384]{1,0:T(8,128)(2,1)S(1)}, u32[]{:S(2)}, u32[]{:S(2)}) collective-permute-start(bf16[1248,384]{1,0:T(8,128)(2,1)S(1)} %collective-permute-done.72.refs_0_.refs_3_), channel_id=1, source_target_pairs={{0,8},{8,16},{16,24},{24,28},{28,20},{20,12},{12,4},{4,0},{9,1},{1... | collective-permute-start | bytes 2875400 | tf_op jit(solution)/shard_map/ppermute | solution.py:1096
  585.9 22.1 %collective-permute-start.76 = (bf16[1248,384]{1,0:T(8,128)(2,1)S(1)}, bf16[1248,384]{1,0:T(8,128)(2,1)S(1)}, u32[]{:S(2)}, u32[]{:S(2)}) collective-permute-start(bf16[1248,384]{1,0:T(8,128)(2,1)S(1)} %collective-permute-done.74.refs_1_.refs_11_), channel_id=1, source_target_pairs={{8,0},{16,8},{24,16},{28,24},{20,28},{12,20},{4,12},{0,4},{1,9},{9... | collective-permute-start | bytes 2875400 | tf_op jit(solution)/shard_map/ppermute | solution.py:1096
  585.9 44.9 %collective-permute-start.69 = (bf16[1024,768]{1,0:T(8,128)(2,1)S(1)}, bf16[1024,768]{1,0:T(8,128)(2,1)S(1)}, u32[]{:S(2)}, u32[]{:S(2)}) collective-permute-start(bf16[1024,768]{1,0:T(8,128)(2,1)S(1)} %mix.7), channel_id=1, source_target_pairs={{0,1},{1,0},{2,3},{3,2},{4,5},{5,4},{6,7},{7,6},{8,9},{9,8},{10,11... | collective-permute-start | bytes 4718600 | tf_op jit(solution)/shard_map/ppermute | solution.py:51
  595.1 21.4 %collective-permute-start.75 = (bf16[1248,384]{1,0:T(8,128)(2,1)S(1)}, bf16[1248,384]{1,0:T(8,128)(2,1)S(1)}, u32[]{:S(2)}, u32[]{:S(2)}) collective-permute-start(bf16[1248,384]{1,0:T(8,128)(2,1)S(1)} %collective-permute-done.73.refs_0_.refs_4_), channel_id=1, source_target_pairs={{0,8},{8,16},{16,24},{24,28},{28,20},{20,12},{12,4},{4,0},{9,1},{1... | collective-permute-start | bytes 2875400 | tf_op jit(solution)/shard_map/ppermute | solution.py:1096
  608.0 22.8 %collective-permute-start.78 = (bf16[1248,384]{1,0:T(8,128)(2,1)S(1)}, bf16[1248,384]{1,0:T(8,128)(2,1)S(1)}, u32[]{:S(2)}, u32[]{:S(2)}) collective-permute-start(bf16[1248,384]{1,0:T(8,128)(2,1)S(1)} %collective-permute-done.76.refs_1_.refs_12_), channel_id=1, source_target_pairs={{8,0},{16,8},{24,16},{28,24},{20,28},{12,20},{4,12},{0,4},{1,9},{9... | collective-permute-start | bytes 2875400 | tf_op jit(solution)/shard_map/ppermute | solution.py:1096
  616.5 22.2 %collective-permute-start.77 = (bf16[1248,384]{1,0:T(8,128)(2,1)S(1)}, bf16[1248,384]{1,0:T(8,128)(2,1)S(1)}, u32[]{:S(2)}, u32[]{:S(2)}) collective-permute-start(bf16[1248,384]{1,0:T(8,128)(2,1)S(1)} %collective-permute-done.75.refs_0_.refs_5_), channel_id=1, source_target_pairs={{0,8},{8,16},{16,24},{24,28},{28,20},{20,12},{12,4},{4,0},{9,1},{1... | collective-permute-start | bytes 2875400 | tf_op jit(solution)/shard_map/ppermute | solution.py:1096
  630.8 23.6 %collective-permute-start.80 = (bf16[1248,384]{1,0:T(8,128)(2,1)S(1)}, bf16[1248,384]{1,0:T(8,128)(2,1)S(1)}, u32[]{:S(2)}, u32[]{:S(2)}) collective-permute-start(bf16[1248,384]{1,0:T(8,128)(2,1)S(1)} %collective-permute-done.78.refs_1_.refs_13_), channel_id=1, source_target_pairs={{8,0},{16,8},{24,16},{28,24},{20,28},{12,20},{4,12},{0,4},{1,9},{9... | collective-permute-start | bytes 2875400 | tf_op jit(solution)/shard_map/ppermute | solution.py:1096
  631.5 27.2 %collective-permute-start.70 = (bf16[512,768]{1,0:T(8,128)(2,1)S(1)}, bf16[512,768]{1,0:T(8,128)(2,1)S(1)}, u32[]{:S(2)}, u32[]{:S(2)}) collective-permute-start(bf16[512,768]{1,0:T(8,128)(2,1)S(1)} %dynamic-slice_convert_fusion), channel_id=1, source_target_pairs={{0,2},{2,0},{1,3},{3,1},{4,6},{6,4},{5,7},{7,5},{8,10},{10,8},{9,1... | collective-permute-start | bytes 2359304 | tf_op jit(solution)/shard_map/ppermute | solution.py:51
  638.7 23.3 %collective-permute-start.79 = (bf16[1248,384]{1,0:T(8,128)(2,1)S(1)}, bf16[1248,384]{1,0:T(8,128)(2,1)S(1)}, u32[]{:S(2)}, u32[]{:S(2)}) collective-permute-start(bf16[1248,384]{1,0:T(8,128)(2,1)S(1)} %collective-permute-done.77.refs_0_.refs_6_), channel_id=1, source_target_pairs={{0,8},{8,16},{16,24},{24,28},{28,20},{20,12},{12,4},{4,0},{9,1},{1... | collective-permute-start | bytes 2875400 | tf_op jit(solution)/shard_map/ppermute | solution.py:1096
  654.5 14.1 %collective-permute-start.81 = (bf16[1248,384]{1,0:T(8,128)(2,1)S(1)}, bf16[1248,384]{1,0:T(8,128)(2,1)S(1)}, u32[]{:S(2)}, u32[]{:S(2)}) collective-permute-start(bf16[1248,384]{1,0:T(8,128)(2,1)S(1)} %collective-permute-done.80.refs_1_.refs_14_), channel_id=1, source_target_pairs={{8,0},{16,8},{24,16},{28,24},{20,28},{12,20},{4,12},{0,4},{1,9},{9... | collective-permute-start | bytes 2875400 | tf_op jit(solution)/shard_map/ppermute | solution.py:1096
  (126 other events, 1000.5 us)

commit v13 on v12

--- a/solution.py
+++ b/solution.py
@@ -832,7 +832,7 @@
 
 def ring_sum(came, mine, first, halved):
     count, rows, lanes = came.shape
-    tiles = 4
+    tiles = 2
     spec = pl.BlockSpec((1, rows // tiles, lanes), lambda i, j: (i, j, 0))
     term = pl.BlockSpec((1, rows // tiles, lanes), lambda i, j: (first + i, j, 0))
 
@@ -850,7 +850,7 @@
         in_specs=[spec, term],
         out_specs=[half(0), half(1)] if halved else spec,
         out_shape=shapes if halved else jax.ShapeDtypeStruct(came.shape, BF16),
-        compiler_params=params(16, "arbitrary", "arbitrary"),
+        compiler_params=params(60, "arbitrary", "arbitrary"),
         cost_estimate=SMALL,
         name="ring_sum",
     )(came, mine)
@@ -1303,7 +1303,7 @@
         return [normed["tie"]]
 
     tasks = [work_experts(at, min(at + 2, pairs_total)) for at in range(1, pairs_total, 2)]
-    tasks += [work_shared, work_back(1), work_back(0), None, work_out(0), work_tie]
+    tasks += [work_shared, work_back(1), work_back(0), None, None, work_tie]
     ends = [work_hidden, work_attend, work_late]
     tasks += [None] * (2 * ring_size - 2 - len(tasks) - len(ends)) + ends
     got = [None, None]
@@ -1383,6 +1383,8 @@
             last = [current[k]]
             if not turn:
                 got[k] = send(current[k], k)
+            if number == 0 and k == 0:
+                last = work_out(0)(after(order, *last), ())
         if turn:
             placed = unpack(plan, experts + 2 * (ring_size - 1), 0, current, shapes, placed)
             others = [swap(across_rings(values), "col") for values in copies]
@@ -1399,8 +1401,10 @@
             plan, experts + 2 * step, wave, [after(current[0], *last), current[1]], shapes, placed
         )
         last = placed[0:1]
-        if number == 2:
+        if number == 0:
             back_to_tokens(last)
+        if number == 4:
+            last = [*last, normed["gains"]]
         if number == ring_size + 1:
             block_rows(last)
     for k in range(2):

time: 693 us -> 727 us (1.049)
  local copies, waits for them, and re-layouts: 38.2 us -> 66 us
  Pallas kernels: 285 us -> 306 us
  waiting for transfers between devices: 272 us -> 253 us
    unnamed x216 -> x210, local copies, waits for them, and re-layouts: 35.8 us -> 63.5 us
    ppermute x42, waiting for transfers between devices: 228 us -> 211 us  [send(): return lax.ppermute(values, ('dp', 'col'), routes_of[which])]
    pallas_call x14, Pallas kernels: 27 us -> 36.9 us  [ring_sum(): pl.pallas_call(ring_sum_kernel, grid=(count, tiles), in_specs=[spec, term...]
  transfers between devices with their start and end apart: 82 -> 82, of which waited for: 38 -> 39; matrix products, arithmetic and copies ran while one was open for 2% -> 3% of each run, Pallas kernels for 39% -> 40%
where the time goes in v13:
time: 727 us; the launch traced here: 718 us
  Pallas kernels  306 us (42%)
  waiting for transfers between devices  253 us (35%)
  starting transfers between devices  71.6 us (10%)
  local copies, waits for them, and re-layouts  66 us (9%)
  other arithmetic  11.9 us (2%)
    ppermute x42, waiting for transfers between devices, send(): return lax.ppermute(values, ('dp', 'col'), routes_of[which])  211 us
    pallas_call x6, Pallas kernels, expert_grads(): pl.pallas_call(functools.partial(expert_kernel, shared, aliased, first),...  72.4 us
    unnamed x210, local copies, waits for them, and re-layouts  63.5 us
    ppermute x42, starting transfers between devices, send(): return lax.ppermute(values, ('dp', 'col'), routes_of[which])  46.7 us
    pallas_call x16, Pallas kernels, unpack(): pl.pallas_call(functools.partial(unpack_kernel, aliased), grid_spec=pltpu...  43.4 us
    pallas_call x4, Pallas kernels, mix(): pl.pallas_call(functools.partial(mix_kernel, back, group, pieces), grid_s...  41 us
    ppermute x37, waiting for transfers between devices, swap(): return lax.ppermute(values, axis, [(0, 1), (1, 0)])  40.7 us
    pallas_call x14, Pallas kernels, ring_sum(): pl.pallas_call(ring_sum_kernel, grid=(count, tiles), in_specs=[spec, term...  36.9 us
  transfers between devices with their start and end apart: 82, of which 39 were waited for; matrix products, arithmetic and copies ran while one was open for 3% of the time, Pallas kernels for 40%

profile of v13, /device:TPU:0, one launch (start us, length us, event | category | flops | bytes accessed | tf_op | source)
XLA Modules:
  0.0 717.8 jit_solution(4145630105945914399)
XLA Ops:
  1.8 3.1 their_columns.1
  5.4 2.6 collective-permute-start
  8.2 5.0 collective-permute-done.2.gains_c_ref.refs_7_
  13.3 2.9 collective-permute-start.4
  18.0 4.5 project.2
  22.5 9.9 %collective-permute-done.4.refs_0_ = bf16[192,768]{1,0:T(8,128)(2,1)S(1)} collective-permute-done((bf16[192,768]{1,0:T(8,128)(2,1)}, bf16[192,768]{1,0:T(8,128)(2,1)S(1)}, u32[]{:S(2)}, u32[]{:S(2)}) %collective-permute-start.4) | collective-permute-done | bytes 294944 | tf_op jit(solution)/shard_map/ppermute | solution.py:51
  40.8 4.5 project.3
  50.7 5.0 collective-permute-done.5.refs_1_
  57.5 6.3 attend.1.refs_4_.refs_5_
  69.5 9.0 %hidden_before.1 = (f32[1024,768]{1,0:T(8,128)}, f32[1024,768]{1,0:T(8,128)}) custom-call(s32[3]{0:T(128)} %copy-done.76, bf16[512,768]{1,0:T(8,128)(2,1)} %refs_0_.2, bf16[512,768]{1,0:T(8,128)(2,1)} %copy-done.93, bf16[512,768]{1,0:T(8,128)(2,1)} %collective-permute-done.own_ref.refs_2_, bf16[512,768]{1,0:T(8,128)(2,1)} %copy-done.94, ...), custom_call_target="tpu_custom_call" | custom-call | flops 2415919104 | bytes 12582912 | tf_op jit(solution)/shard_map/hidden_before/pallas_call | solution.py:418
  78.5 5.6 collective-permute-done.12.refs_2_
  87.5 9.4 %hidden_after.1 = (f32[1024,768]{1,0:T(8,128)}, bf16[1024,768]{1,0:T(8,128)(2,1)}, bf16[1024,768]{1,0:T(8,128)(2,1)}, f32[1024,1]{1,0:T(8,128)}) custom-call(s32[3]{0:T(128)} %copy-done.76, f32[1024,768]{1,0:T(8,128)} %get-tuple-element.221.refs_0_, f32[1024,768]{1,0:T(8,128)} %get-tuple-element.222.refs_1_, ...), custom_call_target="tpu_custom_call" | custom-call | tf_op jit(solution)/shard_map/hidden_after/pallas_call | solution.py:440
  100.3 9.5 %expert_grads.6 = (bf16[1,1536,384]{2,1,0:T(8,128)(2,1)S(1)}, bf16[1,1536,384]{2,1,0:T(8,128)(2,1)}, bf16[8,1024,512]{2,1,0:T(8,128)(2,1)}, bf16[8,1024,256]{2,1,0:T(8,128)(2,1)S(1)}) custom-call(s32[63]{0:T(128)S(1)} %fusion.14.order_ref.plan_ref, bf16[1024,768]{1,0:T(8,128)(2,1)S(1)} %copy-done.10, bf16[1024,768]{1,0:T(8,128)(2,1)S(1)} %copy-done.14, ...), custom_call_target="tpu_custom_call" | custom-call | tf_op jit(solution)/shard_map/expert_grads/pallas_call | solution.py:563
  113.4 15.1 %expert_grads.7 = (bf16[2,1536,384]{2,1,0:T(8,128)(2,1)S(1)}, bf16[2,1536,384]{2,1,0:T(8,128)(2,1)S(1)}, bf16[8,1024,512]{2,1,0:T(8,128)(2,1)}, bf16[8,1024,256]{2,1,0:T(8,128)(2,1)}) custom-call(s32[63]{0:T(128)S(1)} %fusion.14.order_ref.plan_ref, bf16[1024,768]{1,0:T(8,128)(2,1)S(1)} %copy-done.10, ...), custom_call_target="tpu_custom_call", output_to_operand_aliasing={{2}: (18, {}), {3}: (19, {})} | custom-call | tf_op jit(solution)/shard_map/expert_grads/pallas_call | solution.py:563
  131.8 15.1 %expert_grads.8 = (bf16[2,1536,384]{2,1,0:T(8,128)(2,1)S(1)}, bf16[2,1536,384]{2,1,0:T(8,128)(2,1)S(1)}, bf16[8,1024,512]{2,1,0:T(8,128)(2,1)}, bf16[8,1024,256]{2,1,0:T(8,128)(2,1)}) custom-call(s32[63]{0:T(128)S(1)} %fusion.14.order_ref.plan_ref, bf16[1024,768]{1,0:T(8,128)(2,1)S(1)} %copy-done.10, ...), custom_call_target="tpu_custom_call", output_to_operand_aliasing={{2}: (18, {}), {3}: (19, {})} | custom-call | tf_op jit(solution)/shard_map/expert_grads/pallas_call | solution.py:563
  150.7 2.6 ring_sum.14
  157.7 15.7 %expert_grads.9 = (bf16[2,1536,384]{2,1,0:T(8,128)(2,1)S(1)}, bf16[2,1536,384]{2,1,0:T(8,128)(2,1)S(1)}, bf16[8,1024,512]{2,1,0:T(8,128)(2,1)}, bf16[8,1024,256]{2,1,0:T(8,128)(2,1)}) custom-call(s32[63]{0:T(128)S(1)} %fusion.14.order_ref.plan_ref, bf16[1024,768]{1,0:T(8,128)(2,1)S(1)} %copy-done.11, ...), custom_call_target="tpu_custom_call", output_to_operand_aliasing={{2}: (18, {}), {3}: (19, {})} | custom-call | tf_op jit(solution)/shard_map/expert_grads/pallas_call | solution.py:563
  184.7 8.8 %expert_grads.10 = (bf16[1,1536,384]{2,1,0:T(8,128)(2,1)S(1)}, bf16[1,1536,384]{2,1,0:T(8,128)(2,1)S(1)}, bf16[8,1024,512]{2,1,0:T(8,128)(2,1)}, bf16[8,1024,256]{2,1,0:T(8,128)(2,1)S(1)}) custom-call(s32[63]{0:T(128)S(1)} %fusion.14.order_ref.plan_ref, bf16[1024,768]{1,0:T(8,128)(2,1)S(1)} %copy-done.12, ...), custom_call_target="tpu_custom_call", output_to_operand_aliasing={{2}: (18, {}), {3}: (19, {})} | custom-call | tf_op jit(solution)/shard_map/expert_grads/pallas_call | solution.py:563
  197.6 2.7 ring_sum.16
  206.7 8.1 %expert_grads.11 = (bf16[1,1536,384]{2,1,0:T(8,128)(2,1)S(1)}, bf16[1,1536,384]{2,1,0:T(8,128)(2,1)S(1)}, bf16[1,1024,512]{2,1,0:T(8,128)(2,1)S(1)}, bf16[1,1024,256]{2,1,0:T(8,128)(2,1)S(1)}) custom-call(s32[63]{0:T(128)S(1)} %fusion.14.order_ref.plan_ref, bf16[1024,768]{1,0:T(8,128)(2,1)S(1)} %copy-done.13, bf16[1024,768]{1,0:T(8,128)(2,1)S(1)} %copy-done.17, ...), custom_call_target="tpu_custom_call" | custom-call | tf_op jit(solution)/shard_map/expert_grads/pallas_call | solution.py:563
  218.7 2.6 ring_sum.17
  221.7 13.6 %mix.4 = (bf16[512,768]{1,0:T(8,128)(2,1)}, bf16[512,768]{1,0:T(8,128)(2,1)S(1)}) custom-call(s32[63]{0:T(128)S(1)} %fusion.14.order_ref.plan_ref, bf16[8,1024,512]{2,1,0:T(8,128)(2,1)} %get-tuple-element.247.refs_0_, bf16[1,1024,512]{2,1,0:T(8,128)(2,1)S(1)} %copy-done.38, ...), custom_call_target="tpu_custom_call" | custom-call | tf_op jit(solution)/shard_map/mix/pallas_call | solution.py:636
  236.2 2.7 ring_sum.18
  241.7 12.5 %mix.5.own_ref = f32[1024,768]{1,0:T(8,128)S(1)} custom-call(s32[63]{0:T(128)S(1)} %fusion.14.order_ref.plan_ref, bf16[8,1024,512]{2,1,0:T(8,128)(2,1)} %get-tuple-element.247.refs_0_, bf16[1,1024,512]{2,1,0:T(8,128)(2,1)S(1)} %copy-done.39, bf16[16,768,256]{2,1,0:T(8,128)(2,1)} %refs_16_.1, bf16[16,768,256]{2,1,0:T(8,128)(2,1)} %refs_17_.1, ...), custom_call_target="tpu_custom_call" | custom-call | tf_op jit(solution)/shard_map/mix/pallas_call | solution.py:636
  267.3 3.5 chip_sum.1
  273.5 11.5 %collective-permute-done.33.came_ref = bf16[1,1536,384]{2,1,0:T(8,128)(2,1)} collective-permute-done((bf16[1,1536,384]{2,1,0:T(8,128)(2,1)}, bf16[1,1536,384]{2,1,0:T(8,128)(2,1)}, u32[]{:S(2)}, u32[]{:S(2)}) %collective-permute-start.33) | collective-permute-done | bytes 1179680 | tf_op jit(solution)/shard_map/ppermute | solution.py:1096
  292.2 22.9 %collective-permute-done.34.came_ref = bf16[1,1536,384]{2,1,0:T(8,128)(2,1)} collective-permute-done((bf16[1,1536,384]{2,1,0:T(8,128)(2,1)}, bf16[1,1536,384]{2,1,0:T(8,128)(2,1)}, u32[]{:S(2)}, u32[]{:S(2)}) %collective-permute-start.34) | collective-permute-done | bytes 1179680 | tf_op jit(solution)/shard_map/ppermute | solution.py:1096
  315.1 2.6 ring_sum.23
  325.4 6.6 norm_back.1
  332.5 2.6 ring_sum.24
  339.2 13.1 %attend_back.1.refs_4_ = bf16[1024,640]{1,0:T(8,128)(2,1)} custom-call(s32[3]{0:T(128)} %copy-done.76, bf16[512,640]{1,0:T(8,128)(2,1)} %get-tuple-element.213.own_ref, bf16[512,640]{1,0:T(8,128)(2,1)} %get-tuple-element.217.other_ref, bf16[512,768]{1,0:T(8,128)(2,1)} %copy-done.52, bf16[512,768]{1,0:T(8,128)(2,1)} %copy-done.53, ...), custom_call_target="tpu_custom_call" | custom-call | tf_op jit(solution)/shard_map/attend_back/pallas_call | solution.py:173
  354.8 16.4 %late_grads.1 = (bf16[8,480,384]{2,1,0:T(8,128)(2,1)}, bf16[8,480,384]{2,1,0:T(8,128)(2,1)}) custom-call(s32[3]{0:T(128)} %copy-done.76, bf16[512,768]{1,0:T(8,128)(2,1)} %get-tuple-element.280.refs_0_, bf16[512,768]{1,0:T(8,128)(2,1)} %get-tuple-element.281.refs_1_, bf16[512,768]{1,0:T(8,128)(2,1)} %get-tuple-element.282.refs_2_, ...), custom_call_target="tpu_custom_call" | custom-call | tf_op jit(solution)/shard_map/late_grads/pallas_call | solution.py:237
  371.2 2.9 ring_sum.26
  381.6 2.9 ring_sum.27
  385.6 7.6 %mix.6 = f32[1024,768]{1,0:T(8,128)S(1)} custom-call(s32[63]{0:T(128)S(1)} %fusion.14.order_ref.plan_ref, bf16[8,1024,256]{2,1,0:T(8,128)(2,1)} %copy-done.8, bf16[1,1024,256]{2,1,0:T(8,128)(2,1)S(1)} %copy-done.57, bf16[16,256,768]{2,1,0:T(8,128)(2,1)} %refs_9_.13, bf16[16,256,768]{2,1,0:T(8,128)(2,1)} %refs_9_.13, bf16[16,256,768]{2,1,0:T(8,128)(2,1)} %refs_9_.13, ...), custom_call_target="tpu_custom_call" | custom-call | tf_op jit(solution)/shard_map/mix/pallas_call | solution.py:636
  393.9 4.0 unpack.16
  401.7 12.1 %collective-permute-done.46.came_ref = bf16[1248,384]{1,0:T(8,128)(2,1)S(1)} collective-permute-done((bf16[1248,384]{1,0:T(8,128)(2,1)S(1)}, bf16[1248,384]{1,0:T(8,128)(2,1)S(1)}, u32[]{:S(2)}, u32[]{:S(2)}) %collective-permute-start.46) | collective-permute-done | bytes 958496 | tf_op jit(solution)/shard_map/ppermute | solution.py:1096
  417.2 3.3 unpack.17
  424.9 5.5 collective-permute-done.48.came_ref
  434.9 3.8 unpack.18
  438.8 4.5 collective-permute-done.47.came_ref
  448.1 3.7 collective-permute-done.50.came_ref
  455.1 3.6 convert_add_fusion.1
  461.0 3.8 unpack.19
  483.2 3.8 unpack.20
  487.0 4.8 collective-permute-done.51.came_ref
  499.1 3.6 unpack.21
  502.6 15.1 %collective-permute-done.56.came_ref = bf16[1248,384]{1,0:T(8,128)(2,1)S(1)} collective-permute-done((bf16[1248,384]{1,0:T(8,128)(2,1)}, bf16[1248,384]{1,0:T(8,128)(2,1)S(1)}, u32[]{:S(2)}, u32[]{:S(2)}) %collective-permute-start.56) | collective-permute-done | bytes 958496 | tf_op jit(solution)/shard_map/ppermute | solution.py:1096
  524.4 18.2 %collective-permute-done.58.came_ref = bf16[1248,384]{1,0:T(8,128)(2,1)S(1)} collective-permute-done((bf16[1248,384]{1,0:T(8,128)(2,1)S(1)}, bf16[1248,384]{1,0:T(8,128)(2,1)S(1)}, u32[]{:S(2)}, u32[]{:S(2)}) %collective-permute-start.58) | collective-permute-done | bytes 958496 | tf_op jit(solution)/shard_map/ppermute | solution.py:1096
  548.4 7.4 %mix.7 = bf16[1024,768]{1,0:T(8,128)(2,1)S(1)} custom-call(s32[63]{0:T(128)S(1)} %fusion.14.order_ref.plan_ref, bf16[8,1024,256]{2,1,0:T(8,128)(2,1)} %copy-done.8, bf16[1,1024,256]{2,1,0:T(8,128)(2,1)S(1)} %copy-done.57, bf16[16,256,768]{2,1,0:T(8,128)(2,1)} %collective-permute-done.18.refs_10_.refs_16_.refs_2_.refs_3_.refs_4_.refs_5_.refs_6_.refs_7_.refs_8_.refs_9_, ...), custom_call_target="tpu_custom_call" | custom-call | tf_op jit(solution)/shard_map/mix/pallas_call | solution.py:636
  560.3 2.9 collective-permute-done.63.refs_0_.refs_1_
  565.6 11.3 %collective-permute-done.67.refs_1_.refs_9_ = bf16[1248,384]{1,0:T(8,128)(2,1)S(1)} collective-permute-done((bf16[1248,384]{1,0:T(8,128)(2,1)S(1)}, bf16[1248,384]{1,0:T(8,128)(2,1)S(1)}, u32[]{:S(2)}, u32[]{:S(2)}) %collective-permute-start.67) | collective-permute-done | bytes 958496 | tf_op jit(solution)/shard_map/ppermute | solution.py:1096
  579.0 5.6 collective-permute-done.66.refs_0_.refs_2_
  587.0 11.5 %collective-permute-done.68.refs_1_.refs_10_ = bf16[1248,384]{1,0:T(8,128)(2,1)S(1)} collective-permute-done((bf16[1248,384]{1,0:T(8,128)(2,1)S(1)}, bf16[1248,384]{1,0:T(8,128)(2,1)S(1)}, u32[]{:S(2)}, u32[]{:S(2)}) %collective-permute-start.68) | collective-permute-done | bytes 958496 | tf_op jit(solution)/shard_map/ppermute | solution.py:1096
  600.7 5.3 collective-permute-done.72.refs_0_.refs_3_
  608.4 12.5 %collective-permute-done.74.refs_1_.refs_11_ = bf16[1248,384]{1,0:T(8,128)(2,1)S(1)} collective-permute-done((bf16[1248,384]{1,0:T(8,128)(2,1)S(1)}, bf16[1248,384]{1,0:T(8,128)(2,1)S(1)}, u32[]{:S(2)}, u32[]{:S(2)}) %collective-permute-start.74) | collective-permute-done | bytes 958496 | tf_op jit(solution)/shard_map/ppermute | solution.py:1096
  623.0 4.4 collective-permute-done.73.refs_0_.refs_4_
  629.8 13.2 %collective-permute-done.76.refs_1_.refs_12_ = bf16[1248,384]{1,0:T(8,128)(2,1)S(1)} collective-permute-done((bf16[1248,384]{1,0:T(8,128)(2,1)S(1)}, bf16[1248,384]{1,0:T(8,128)(2,1)S(1)}, u32[]{:S(2)}, u32[]{:S(2)}) %collective-permute-start.76) | collective-permute-done | bytes 958496 | tf_op jit(solution)/shard_map/ppermute | solution.py:1096
  645.1 3.7 collective-permute-done.75.refs_0_.refs_5_
  651.2 14.7 %collective-permute-done.78.refs_1_.refs_13_ = bf16[1248,384]{1,0:T(8,128)(2,1)S(1)} collective-permute-done((bf16[1248,384]{1,0:T(8,128)(2,1)S(1)}, bf16[1248,384]{1,0:T(8,128)(2,1)S(1)}, u32[]{:S(2)}, u32[]{:S(2)}) %collective-permute-start.78) | collective-permute-done | bytes 958496 | tf_op jit(solution)/shard_map/ppermute | solution.py:1096
  672.6 17.1 %collective-permute-done.80.refs_1_.refs_14_ = bf16[1248,384]{1,0:T(8,128)(2,1)S(1)} collective-permute-done((bf16[1248,384]{1,0:T(8,128)(2,1)S(1)}, bf16[1248,384]{1,0:T(8,128)(2,1)S(1)}, u32[]{:S(2)}, u32[]{:S(2)}) %collective-permute-start.80) | collective-permute-done | bytes 958496 | tf_op jit(solution)/shard_map/ppermute | solution.py:1096
  691.2 2.7 fusion.4
  697.3 6.5 collective-permute-done.81.refs_15_.refs_1_
  704.7 7.8 %unpack_late.1 = (f32[768,512]{1,0:T(8,128)}, f32[768,512]{1,0:T(8,128)}, f32[512,768]{1,0:T(8,128)}, f32[768,768]{1,0:T(8,128)}, f32[768,256]{1,0:T(8,128)}, /*...) custom-call(s32[63]{0:T(128)S(1)} %fusion.14.order_ref.plan_ref, ...), custom_call_target="tpu_custom_call" | custom-call | tf_op jit(solution)/shard_map/unpack_late/pallas_call | solution.py:1009
  (407 shorter events, 229.6 us)
Async XLA Ops:
  0.7 34.4 %collective-permute-start.16 = (bf16[16,768,256]{2,1,0:T(8,128)(2,1)}, bf16[16,768,256]{2,1,0:T(8,128)(2,1)}, u32[]{:S(2)}, u32[]{:S(2)}) collective-permute-start(bf16[16,768,256]{2,1,0:T(8,128)(2,1)} %refs_16_.1), channel_id=1, source_target_pairs={{0,1},{1,0},{2,3},{3,2},{4,5},{5,4},{6,7},{7,6},{8,9},{9,8},{10,11... | collective-permute-start | bytes 18874376 | tf_op jit(solution)/shard_map/ppermute | solution.py:51
  5.4 27.1 %collective-permute-start = (bf16[512,768]{1,0:T(8,128)(2,1)S(1)}, bf16[512,768]{1,0:T(8,128)(2,1)}, u32[]{:S(2)}, u32[]{:S(2)}) collective-permute-start(bf16[512,768]{1,0:T(8,128)(2,1)S(1)} %copy-done.79), channel_id=1, source_target_pairs={{0,2},{2,0},{1,3},{3,1},{4,6},{6,4},{5,7},{7,5},{8,10},{10,8},{9,1... | collective-permute-start | bytes 2359304 | tf_op jit(solution)/shard_map/ppermute | solution.py:51
  13.3 19.1 %collective-permute-start.4 = (bf16[192,768]{1,0:T(8,128)(2,1)}, bf16[192,768]{1,0:T(8,128)(2,1)S(1)}, u32[]{:S(2)}, u32[]{:S(2)}) collective-permute-start(bf16[192,768]{1,0:T(8,128)(2,1)} %get-tuple-element.214), channel_id=1, source_target_pairs={{0,2},{2,0},{1,3},{3,1},{4,6},{6,4},{5,7},{7,5},{8,10},{10,8},{9,1... | collective-permute-start | bytes 884744 | tf_op jit(solution)/shard_map/ppermute | solution.py:51
  34.9 62.0 %collective-permute-start.18 = (bf16[16,256,768]{2,1,0:T(8,128)(2,1)}, bf16[16,256,768]{2,1,0:T(8,128)(2,1)}, u32[]{:S(2)}, u32[]{:S(2)}) collective-permute-start(bf16[16,256,768]{2,1,0:T(8,128)(2,1)} %refs_9_.13), channel_id=1, source_target_pairs={{0,1},{1,0},{2,3},{3,2},{4,5},{5,4},{6,7},{7,6},{8,9},{9,8},{10,11... | collective-permute-start | bytes 18874376 | tf_op jit(solution)/shard_map/ppermute | solution.py:51
  35.8 61.1 %collective-permute-start.17 = (bf16[16,768,256]{2,1,0:T(8,128)(2,1)}, bf16[16,768,256]{2,1,0:T(8,128)(2,1)}, u32[]{:S(2)}, u32[]{:S(2)}) collective-permute-start(bf16[16,768,256]{2,1,0:T(8,128)(2,1)} %refs_17_.1), channel_id=1, source_target_pairs={{0,1},{1,0},{2,3},{3,2},{4,5},{5,4},{6,7},{7,6},{8,9},{9,8},{10,11... | collective-permute-start | bytes 18874376 | tf_op jit(solution)/shard_map/ppermute | solution.py:51
  35.9 19.8 %collective-permute-start.5 = (bf16[512,768]{1,0:T(8,128)(2,1)S(1)}, bf16[512,768]{1,0:T(8,128)(2,1)S(1)}, u32[]{:S(2)}, u32[]{:S(2)}) collective-permute-start(bf16[512,768]{1,0:T(8,128)(2,1)S(1)} %copy-done.64), channel_id=1, source_target_pairs={{0,2},{2,0},{1,3},{3,1},{4,6},{6,4},{5,7},{7,5},{8,10},{10,8},{9,1... | collective-permute-start | bytes 2359304 | tf_op jit(solution)/shard_map/ppermute | solution.py:51
  39.3 11.4 %collective-permute-start.6 = (bf16[192,768]{1,0:T(8,128)(2,1)S(1)}, bf16[192,768]{1,0:T(8,128)(2,1)S(1)}, u32[]{:S(2)}, u32[]{:S(2)}) collective-permute-start(bf16[192,768]{1,0:T(8,128)(2,1)S(1)} %collective-permute-done.4.refs_0_), channel_id=1, source_target_pairs={{0,4},{4,0},{8,12},{12,8},{16,20},{20,16},{24,28},{28,24},{1,5},{5... | collective-permute-start | bytes 884744 | tf_op jit(solution)/shard_map/ppermute | solution.py:1132
  50.6 17.8 %collective-permute-start.11 = (bf16[768,768]{1,0:T(8,128)(2,1)}, bf16[768,768]{1,0:T(8,128)(2,1)}, u32[]{:S(2)}, u32[]{:S(2)}) collective-permute-start(bf16[768,768]{1,0:T(8,128)(2,1)} %refs_4_.4), channel_id=1, source_target_pairs={{0,1},{1,0},{2,3},{3,2},{4,5},{5,4},{6,7},{7,6},{8,9},{9,8},{10,11... | collective-permute-start | bytes 3538952 | tf_op jit(solution)/shard_map/ppermute | solution.py:51
  63.8 20.3 %collective-permute-start.12 = (bf16[1024,384]{1,0:T(8,128)(2,1)}, bf16[1024,384]{1,0:T(8,128)(2,1)}, u32[]{:S(2)}, u32[]{:S(2)}) collective-permute-start(bf16[1024,384]{1,0:T(8,128)(2,1)} %attend.1.refs_4_.refs_5_), channel_id=1, source_target_pairs={{0,2},{2,0},{1,3},{3,1},{4,6},{6,4},{5,7},{7,5},{8,10},{10,8},{9,1... | collective-permute-start | bytes 2359304 | tf_op jit(solution)/shard_map/ppermute | solution.py:51
  67.2 29.7 %collective-permute-start.15 = (bf16[1024,768]{1,0:T(8,128)(2,1)S(1)}, bf16[1024,768]{1,0:T(8,128)(2,1)S(1)}, u32[]{:S(2)}, u32[]{:S(2)}) collective-permute-start(bf16[1024,768]{1,0:T(8,128)(2,1)S(1)} %join.3.refs_2_.refs_4_), channel_id=1, source_target_pairs={{0,1},{1,0},{2,3},{3,2},{4,5},{5,4},{6,7},{7,6},{8,9},{9,8},{10,11... | collective-permute-start | bytes 4718600 | tf_op jit(solution)/shard_map/ppermute | solution.py:51
  68.4 15.8 %collective-permute-start.14 = (bf16[768,768]{1,0:T(8,128)(2,1)}, bf16[768,768]{1,0:T(8,128)(2,1)}, u32[]{:S(2)}, u32[]{:S(2)}) collective-permute-start(bf16[768,768]{1,0:T(8,128)(2,1)} %join.2.refs_4_), channel_id=1, source_target_pairs={{0,1},{1,0},{2,3},{3,2},{4,5},{5,4},{6,7},{7,6},{8,9},{9,8},{10,11... | collective-permute-start | bytes 3538952 | tf_op jit(solution)/shard_map/ppermute | solution.py:51
  111.8 37.9 %collective-permute-start.19 = (bf16[1,1536,384]{2,1,0:T(8,128)(2,1)S(1)}, bf16[1,1536,384]{2,1,0:T(8,128)(2,1)S(1)}, u32[]{:S(2)}, u32[]{:S(2)}) collective-permute-start(bf16[1,1536,384]{2,1,0:T(8,128)(2,1)S(1)} %get-tuple-element.229), channel_id=1, source_target_pairs={{0,8},{8,16},{16,24},{24,28},{28,20},{20,12},{12,4},{4,0},{9,1},{1... | collective-permute-start | bytes 3538952 | tf_op jit(solution)/shard_map/ppermute | solution.py:1096
  131.3 44.8 %collective-permute-start.21 = (bf16[1,1536,384]{2,1,0:T(8,128)(2,1)}, bf16[1,1536,384]{2,1,0:T(8,128)(2,1)}, u32[]{:S(2)}, u32[]{:S(2)}) collective-permute-start(bf16[1,1536,384]{2,1,0:T(8,128)(2,1)} %get-tuple-element.239), channel_id=1, source_target_pairs={{8,0},{16,8},{24,16},{28,24},{20,28},{12,20},{4,12},{0,4},{1,9},{9... | collective-permute-start | bytes 3538952 | tf_op jit(solution)/shard_map/ppermute | solution.py:1096
  153.3 44.3 %collective-permute-start.20 = (bf16[1,1536,384]{2,1,0:T(8,128)(2,1)}, bf16[1,1536,384]{2,1,0:T(8,128)(2,1)}, u32[]{:S(2)}, u32[]{:S(2)}) collective-permute-start(bf16[1,1536,384]{2,1,0:T(8,128)(2,1)} %ring_sum.14), channel_id=1, source_target_pairs={{0,8},{8,16},{16,24},{24,28},{28,20},{20,12},{12,4},{4,0},{9,1},{1... | collective-permute-start | bytes 3538952 | tf_op jit(solution)/shard_map/ppermute | solution.py:1096
  178.8 39.9 %collective-permute-start.23 = (bf16[1,1536,384]{2,1,0:T(8,128)(2,1)}, bf16[1,1536,384]{2,1,0:T(8,128)(2,1)}, u32[]{:S(2)}, u32[]{:S(2)}) collective-permute-start(bf16[1,1536,384]{2,1,0:T(8,128)(2,1)} %ring_sum.15), channel_id=1, source_target_pairs={{8,0},{16,8},{24,16},{28,24},{20,28},{12,20},{4,12},{0,4},{1,9},{9... | collective-permute-start | bytes 3538952 | tf_op jit(solution)/shard_map/ppermute | solution.py:1096
  179.2 22.7 %collective-permute-start.24 = (bf16[1,768,512]{2,1,0:T(8,128)(2,1)}, bf16[1,768,512]{2,1,0:T(8,128)(2,1)}, u32[]{:S(2)}, u32[]{:S(2)}) collective-permute-start(bf16[1,768,512]{2,1,0:T(8,128)(2,1)} %bitcast.29), channel_id=1, source_target_pairs={{0,1},{1,0},{2,3},{3,2},{4,5},{5,4},{6,7},{7,6},{8,9},{9,8},{10,11... | collective-permute-start | bytes 2359304 | tf_op jit(solution)/shard_map/ppermute | solution.py:51
  179.2 22.7 %collective-permute-start.25 = (bf16[1,768,512]{2,1,0:T(8,128)(2,1)}, bf16[1,768,512]{2,1,0:T(8,128)(2,1)}, u32[]{:S(2)}, u32[]{:S(2)}) collective-permute-start(bf16[1,768,512]{2,1,0:T(8,128)(2,1)} %bitcast.34), channel_id=1, source_target_pairs={{0,1},{1,0},{2,3},{3,2},{4,5},{5,4},{6,7},{7,6},{8,9},{9,8},{10,11... | collective-permute-start | bytes 2359304 | tf_op jit(solution)/shard_map/ppermute | solution.py:51
  179.7 22.2 %collective-permute-start.26 = (bf16[1,512,768]{2,1,0:T(8,128)(2,1)}, bf16[1,512,768]{2,1,0:T(8,128)(2,1)}, u32[]{:S(2)}, u32[]{:S(2)}) collective-permute-start(bf16[1,512,768]{2,1,0:T(8,128)(2,1)} %bitcast.39), channel_id=1, source_target_pairs={{0,1},{1,0},{2,3},{3,2},{4,5},{5,4},{6,7},{7,6},{8,9},{9,8},{10,11... | collective-permute-start | bytes 2359304 | tf_op jit(solution)/shard_map/ppermute | solution.py:51
  200.3 35.0 %collective-permute-start.22 = (bf16[1,1536,384]{2,1,0:T(8,128)(2,1)}, bf16[1,1536,384]{2,1,0:T(8,128)(2,1)}, u32[]{:S(2)}, u32[]{:S(2)}) collective-permute-start(bf16[1,1536,384]{2,1,0:T(8,128)(2,1)} %ring_sum.16), channel_id=1, source_target_pairs={{0,8},{8,16},{16,24},{24,28},{28,20},{20,12},{12,4},{4,0},{9,1},{1... | collective-permute-start | bytes 3538952 | tf_op jit(solution)/shard_map/ppermute | solution.py:1096
  221.3 34.5 %collective-permute-start.28 = (bf16[1,1536,384]{2,1,0:T(8,128)(2,1)}, bf16[1,1536,384]{2,1,0:T(8,128)(2,1)}, u32[]{:S(2)}, u32[]{:S(2)}) collective-permute-start(bf16[1,1536,384]{2,1,0:T(8,128)(2,1)} %ring_sum.17), channel_id=1, source_target_pairs={{8,0},{16,8},{24,16},{28,24},{20,28},{12,20},{4,12},{0,4},{1,9},{9... | collective-permute-start | bytes 3538952 | tf_op jit(solution)/shard_map/ppermute | solution.py:1096
  238.8 20.5 %collective-permute-start.27 = (bf16[1,1536,384]{2,1,0:T(8,128)(2,1)}, bf16[1,1536,384]{2,1,0:T(8,128)(2,1)}, u32[]{:S(2)}, u32[]{:S(2)}) collective-permute-start(bf16[1,1536,384]{2,1,0:T(8,128)(2,1)} %ring_sum.18), channel_id=1, source_target_pairs={{0,8},{8,16},{16,24},{24,28},{28,20},{20,12},{12,4},{4,0},{9,1},{1... | collective-permute-start | bytes 3538952 | tf_op jit(solution)/shard_map/ppermute | solution.py:1096
  258.4 26.6 %collective-permute-start.33 = (bf16[1,1536,384]{2,1,0:T(8,128)(2,1)}, bf16[1,1536,384]{2,1,0:T(8,128)(2,1)}, u32[]{:S(2)}, u32[]{:S(2)}) collective-permute-start(bf16[1,1536,384]{2,1,0:T(8,128)(2,1)} %ring_sum.19), channel_id=1, source_target_pairs={{8,0},{16,8},{24,16},{28,24},{20,28},{12,20},{4,12},{0,4},{1,9},{9... | collective-permute-start | bytes 3538952 | tf_op jit(solution)/shard_map/ppermute | solution.py:1096
  261.9 25.7 %collective-permute-start.29 = (bf16[1,1536,384]{2,1,0:T(8,128)(2,1)}, bf16[1,1536,384]{2,1,0:T(8,128)(2,1)}, u32[]{:S(2)}, u32[]{:S(2)}) collective-permute-start(bf16[1,1536,384]{2,1,0:T(8,128)(2,1)} %ring_sum.20), channel_id=1, source_target_pairs={{0,8},{8,16},{16,24},{24,28},{28,20},{20,12},{12,4},{4,0},{9,1},{1... | collective-permute-start | bytes 3538952 | tf_op jit(solution)/shard_map/ppermute | solution.py:1096
  272.4 50.4 %collective-permute-start.35 = (bf16[1024,768]{1,0:T(8,128)(2,1)}, bf16[1024,768]{1,0:T(8,128)(2,1)S(1)}, u32[]{:S(2)}, u32[]{:S(2)}) collective-permute-start(bf16[1024,768]{1,0:T(8,128)(2,1)} %get-tuple-element.264), channel_id=1, source_target_pairs={{0,2},{2,0},{1,3},{3,1},{4,6},{6,4},{5,7},{7,5},{8,10},{10,8},{9,1... | collective-permute-start | bytes 4718600 | tf_op jit(solution)/shard_map/ppermute | solution.py:51
  287.6 27.5 %collective-permute-start.34 = (bf16[1,1536,384]{2,1,0:T(8,128)(2,1)}, bf16[1,1536,384]{2,1,0:T(8,128)(2,1)}, u32[]{:S(2)}, u32[]{:S(2)}) collective-permute-start(bf16[1,1536,384]{2,1,0:T(8,128)(2,1)} %ring_sum.22), channel_id=1, source_target_pairs={{8,0},{16,8},{24,16},{28,24},{20,28},{12,20},{4,12},{0,4},{1,9},{9... | collective-permute-start | bytes 3538952 | tf_op jit(solution)/shard_map/ppermute | solution.py:1096
  290.2 42.4 %collective-permute-start.32 = (bf16[1,1536,384]{2,1,0:T(8,128)(2,1)}, bf16[1,1536,384]{2,1,0:T(8,128)(2,1)}, u32[]{:S(2)}, u32[]{:S(2)}) collective-permute-start(bf16[1,1536,384]{2,1,0:T(8,128)(2,1)} %ring_sum.21), channel_id=1, source_target_pairs={{0,8},{8,16},{16,24},{24,28},{28,20},{20,12},{12,4},{4,0},{9,1},{1... | collective-permute-start | bytes 3538952 | tf_op jit(solution)/shard_map/ppermute | solution.py:1096
  317.7 34.6 %collective-permute-start.39 = (bf16[1,1536,384]{2,1,0:T(8,128)(2,1)}, bf16[1,1536,384]{2,1,0:T(8,128)(2,1)}, u32[]{:S(2)}, u32[]{:S(2)}) collective-permute-start(bf16[1,1536,384]{2,1,0:T(8,128)(2,1)} %ring_sum.23), channel_id=1, source_target_pairs={{8,0},{16,8},{24,16},{28,24},{20,28},{12,20},{4,12},{0,4},{1,9},{9... | collective-permute-start | bytes 3538952 | tf_op jit(solution)/shard_map/ppermute | solution.py:1096
  335.1 36.1 %collective-permute-start.42 = (bf16[1,1536,384]{2,1,0:T(8,128)(2,1)}, bf16[1,1536,384]{2,1,0:T(8,128)(2,1)}, u32[]{:S(2)}, u32[]{:S(2)}) collective-permute-start(bf16[1,1536,384]{2,1,0:T(8,128)(2,1)} %ring_sum.24), channel_id=1, source_target_pairs={{0,8},{8,16},{16,24},{24,28},{28,20},{20,12},{12,4},{4,0},{9,1},{1... | collective-permute-start | bytes 3538952 | tf_op jit(solution)/shard_map/ppermute | solution.py:1096
  354.8 25.8 %collective-permute-start.44 = (bf16[1,1536,384]{2,1,0:T(8,128)(2,1)}, bf16[1,1536,384]{2,1,0:T(8,128)(2,1)S(1)}, u32[]{:S(2)}, u32[]{:S(2)}) collective-permute-start(bf16[1,1536,384]{2,1,0:T(8,128)(2,1)} %ring_sum.25), channel_id=1, source_target_pairs={{8,0},{16,8},{24,16},{28,24},{20,28},{12,20},{4,12},{0,4},{1,9},{9... | collective-permute-start | bytes 3538952 | tf_op jit(solution)/shard_map/ppermute | solution.py:1096
  378.6 19.3 %collective-permute-start.43 = (bf16[1248,384]{1,0:T(8,128)(2,1)}, bf16[1248,384]{1,0:T(8,128)(2,1)}, u32[]{:S(2)}, u32[]{:S(2)}) collective-permute-start(bf16[1248,384]{1,0:T(8,128)(2,1)} %late_load.2.refs_0_), channel_id=1, source_target_pairs={{0,8},{8,16},{16,24},{24,28},{28,20},{20,12},{12,4},{4,0},{9,1},{1... | collective-permute-start | bytes 2875400 | tf_op jit(solution)/shard_map/ppermute | solution.py:1096
  393.8 20.0 %collective-permute-start.46 = (bf16[1248,384]{1,0:T(8,128)(2,1)S(1)}, bf16[1248,384]{1,0:T(8,128)(2,1)S(1)}, u32[]{:S(2)}, u32[]{:S(2)}) collective-permute-start(bf16[1248,384]{1,0:T(8,128)(2,1)S(1)} %late_load.3.refs_1_), channel_id=1, source_target_pairs={{8,0},{16,8},{24,16},{28,24},{20,28},{12,20},{4,12},{0,4},{1,9},{9... | collective-permute-start | bytes 2875400 | tf_op jit(solution)/shard_map/ppermute | solution.py:1096
  400.3 20.2 %collective-permute-start.45 = (bf16[1248,384]{1,0:T(8,128)(2,1)}, bf16[1248,384]{1,0:T(8,128)(2,1)}, u32[]{:S(2)}, u32[]{:S(2)}) collective-permute-start(bf16[1248,384]{1,0:T(8,128)(2,1)} %late_add.14.refs_0_), channel_id=1, source_target_pairs={{0,8},{8,16},{16,24},{24,28},{28,20},{20,12},{12,4},{4,0},{9,1},{1... | collective-permute-start | bytes 2875400 | tf_op jit(solution)/shard_map/ppermute | solution.py:1096
  414.5 15.9 %collective-permute-start.48 = (bf16[1248,384]{1,0:T(8,128)(2,1)S(1)}, bf16[1248,384]{1,0:T(8,128)(2,1)}, u32[]{:S(2)}, u32[]{:S(2)}) collective-permute-start(bf16[1248,384]{1,0:T(8,128)(2,1)S(1)} %late_add.15.refs_1_), channel_id=1, source_target_pairs={{8,0},{16,8},{24,16},{28,24},{20,28},{12,20},{4,12},{0,4},{1,9},{9... | collective-permute-start | bytes 2875400 | tf_op jit(solution)/shard_map/ppermute | solution.py:1096
  417.1 38.0 %collective-permute-start.53 = (bf16[1024,768]{1,0:T(8,128)(2,1)}, bf16[1024,768]{1,0:T(8,128)(2,1)}, u32[]{:S(2)}, u32[]{:S(2)}) collective-permute-start(bf16[1024,768]{1,0:T(8,128)(2,1)} %convolution_convert_fusion), channel_id=1, source_target_pairs={{0,1},{1,0},{2,3},{3,2},{4,5},{5,4},{6,7},{7,6},{8,9},{9,8},{10,11... | collective-permute-start | bytes 4718600 | tf_op jit(solution)/shard_map/ppermute | solution.py:51
  422.8 20.4 %collective-permute-start.47 = (bf16[1248,384]{1,0:T(8,128)(2,1)}, bf16[1248,384]{1,0:T(8,128)(2,1)}, u32[]{:S(2)}, u32[]{:S(2)}) collective-permute-start(bf16[1248,384]{1,0:T(8,128)(2,1)} %late_add.16.refs_0_), channel_id=1, source_target_pairs={{0,8},{8,16},{16,24},{24,28},{28,20},{20,12},{12,4},{4,0},{9,1},{1... | collective-permute-start | bytes 2875400 | tf_op jit(solution)/shard_map/ppermute | solution.py:1096
  432.8 19.0 %collective-permute-start.50 = (bf16[1248,384]{1,0:T(8,128)(2,1)}, bf16[1248,384]{1,0:T(8,128)(2,1)}, u32[]{:S(2)}, u32[]{:S(2)}) collective-permute-start(bf16[1248,384]{1,0:T(8,128)(2,1)} %late_add.17.refs_1_), channel_id=1, source_target_pairs={{8,0},{16,8},{24,16},{28,24},{20,28},{12,20},{4,12},{0,4},{1,9},{9... | collective-permute-start | bytes 2875400 | tf_op jit(solution)/shard_map/ppermute | solution.py:1096
  445.6 21.5 %collective-permute-start.49 = (bf16[1248,384]{1,0:T(8,128)(2,1)}, bf16[1248,384]{1,0:T(8,128)(2,1)}, u32[]{:S(2)}, u32[]{:S(2)}) collective-permute-start(bf16[1248,384]{1,0:T(8,128)(2,1)} %late_add.18.refs_0_), channel_id=1, source_target_pairs={{0,8},{8,16},{16,24},{24,28},{28,20},{20,12},{12,4},{4,0},{9,1},{1... | collective-permute-start | bytes 2875400 | tf_op jit(solution)/shard_map/ppermute | solution.py:1096
  454.1 17.9 %collective-permute-start.52 = (bf16[1248,384]{1,0:T(8,128)(2,1)}, bf16[1248,384]{1,0:T(8,128)(2,1)}, u32[]{:S(2)}, u32[]{:S(2)}) collective-permute-start(bf16[1248,384]{1,0:T(8,128)(2,1)} %late_add.19.refs_1_), channel_id=1, source_target_pairs={{8,0},{16,8},{24,16},{28,24},{20,28},{12,20},{4,12},{0,4},{1,9},{9... | collective-permute-start | bytes 2875400 | tf_op jit(solution)/shard_map/ppermute | solution.py:1096
  459.8 17.1 %collective-permute-start.54 = (bf16[512,768]{1,0:T(8,128)(2,1)}, bf16[512,768]{1,0:T(8,128)(2,1)}, u32[]{:S(2)}, u32[]{:S(2)}) collective-permute-start(bf16[512,768]{1,0:T(8,128)(2,1)} %dynamic-slice_convert_fusion.1), channel_id=1, source_target_pairs={{0,2},{2,0},{1,3},{3,1},{4,6},{6,4},{5,7},{7,5},{8,10},{10,8},{9,1... | collective-permute-start | bytes 2359304 | tf_op jit(solution)/shard_map/ppermute | solution.py:51
  469.5 22.3 %collective-permute-start.51 = (bf16[1248,384]{1,0:T(8,128)(2,1)}, bf16[1248,384]{1,0:T(8,128)(2,1)}, u32[]{:S(2)}, u32[]{:S(2)}) collective-permute-start(bf16[1248,384]{1,0:T(8,128)(2,1)} %late_add.20.refs_0_), channel_id=1, source_target_pairs={{0,8},{8,16},{16,24},{24,28},{28,20},{20,12},{12,4},{4,0},{9,1},{1... | collective-permute-start | bytes 2875400 | tf_op jit(solution)/shard_map/ppermute | solution.py:1096
  474.4 22.3 %collective-permute-start.57 = (bf16[1248,384]{1,0:T(8,128)(2,1)}, bf16[1248,384]{1,0:T(8,128)(2,1)}, u32[]{:S(2)}, u32[]{:S(2)}) collective-permute-start(bf16[1248,384]{1,0:T(8,128)(2,1)} %late_add.21.refs_1_), channel_id=1, source_target_pairs={{8,0},{16,8},{24,16},{28,24},{20,28},{12,20},{4,12},{0,4},{1,9},{9... | collective-permute-start | bytes 2875400 | tf_op jit(solution)/shard_map/ppermute | solution.py:1096
  494.2 23.5 %collective-permute-start.56 = (bf16[1248,384]{1,0:T(8,128)(2,1)}, bf16[1248,384]{1,0:T(8,128)(2,1)S(1)}, u32[]{:S(2)}, u32[]{:S(2)}) collective-permute-start(bf16[1248,384]{1,0:T(8,128)(2,1)} %late_add.22.refs_0_), channel_id=1, source_target_pairs={{0,8},{8,16},{16,24},{24,28},{28,20},{20,12},{12,4},{4,0},{9,1},{1... | collective-permute-start | bytes 2875400 | tf_op jit(solution)/shard_map/ppermute | solution.py:1096
  499.1 21.8 %collective-permute-start.59 = (bf16[1248,384]{1,0:T(8,128)(2,1)}, bf16[1248,384]{1,0:T(8,128)(2,1)S(1)}, u32[]{:S(2)}, u32[]{:S(2)}) collective-permute-start(bf16[1248,384]{1,0:T(8,128)(2,1)} %late_add.23.refs_1_), channel_id=1, source_target_pairs={{8,0},{16,8},{24,16},{28,24},{20,28},{12,20},{4,12},{0,4},{1,9},{9... | collective-permute-start | bytes 2875400 | tf_op jit(solution)/shard_map/ppermute | solution.py:1096
  518.5 24.1 %collective-permute-start.58 = (bf16[1248,384]{1,0:T(8,128)(2,1)S(1)}, bf16[1248,384]{1,0:T(8,128)(2,1)S(1)}, u32[]{:S(2)}, u32[]{:S(2)}) collective-permute-start(bf16[1248,384]{1,0:T(8,128)(2,1)S(1)} %late_add.24.refs_0_), channel_id=1, source_target_pairs={{0,8},{8,16},{16,24},{24,28},{28,20},{20,12},{12,4},{4,0},{9,1},{1... | collective-permute-start | bytes 2875400 | tf_op jit(solution)/shard_map/ppermute | solution.py:1096
  521.6 21.7 %collective-permute-start.60 = (bf16[1248,384]{1,0:T(8,128)(2,1)S(1)}, bf16[1248,384]{1,0:T(8,128)(2,1)S(1)}, u32[]{:S(2)}, u32[]{:S(2)}) collective-permute-start(bf16[1248,384]{1,0:T(8,128)(2,1)S(1)} %late_add.25.refs_1_), channel_id=1, source_target_pairs={{8,0},{16,8},{24,16},{28,24},{20,28},{12,20},{4,12},{0,4},{1,9},{9... | collective-permute-start | bytes 2875400 | tf_op jit(solution)/shard_map/ppermute | solution.py:1096
  521.7 23.0 %collective-permute-start.62 = (bf16[1,768,384]{2,1,0:T(8,128)(2,1)S(1)}, bf16[1,768,384]{2,1,0:T(8,128)(2,1)S(1)}, u32[]{:S(2)}, u32[]{:S(2)}) collective-permute-start(bf16[1,768,384]{2,1,0:T(8,128)(2,1)S(1)} %copy-done.104), channel_id=1, source_target_pairs={{0,1},{1,0},{2,3},{3,2},{4,5},{5,4},{6,7},{7,6},{8,9},{9,8},{10,11... | collective-permute-start | bytes 1769480 | tf_op jit(solution)/shard_map/ppermute | solution.py:51
  521.8 34.1 %collective-permute-start.65 = (bf16[1,768,384]{2,1,0:T(8,128)(2,1)S(1)}, bf16[1,768,384]{2,1,0:T(8,128)(2,1)S(1)}, u32[]{:S(2)}, u32[]{:S(2)}) collective-permute-start(bf16[1,768,384]{2,1,0:T(8,128)(2,1)S(1)} %copy-done.103), channel_id=1, source_target_pairs={{0,1},{1,0},{2,3},{3,2},{4,5},{5,4},{6,7},{7,6},{8,9},{9,8},{10,11... | collective-permute-start | bytes 1769480 | tf_op jit(solution)/shard_map/ppermute | solution.py:51
  544.2 11.7 %collective-permute-start.64 = (bf16[480,384]{1,0:T(8,128)(2,1)S(1)}, bf16[480,384]{1,0:T(8,128)(2,1)S(1)}, u32[]{:S(2)}, u32[]{:S(2)}) collective-permute-start(bf16[480,384]{1,0:T(8,128)(2,1)S(1)} %get-tuple-element.344.mine_ref), channel_id=1, source_target_pairs={{0,1},{1,0},{2,3},{3,2},{4,5},{5,4},{6,7},{7,6},{8,9},{9,8},{10,11... | collective-permute-start | bytes 1105928 | tf_op jit(solution)/shard_map/ppermute | solution.py:51
  546.0 17.3 %collective-permute-start.63 = (bf16[1248,384]{1,0:T(8,128)(2,1)S(1)}, bf16[1248,384]{1,0:T(8,128)(2,1)S(1)}, u32[]{:S(2)}, u32[]{:S(2)}) collective-permute-start(bf16[1248,384]{1,0:T(8,128)(2,1)S(1)} %late_join.2.refs_0_), channel_id=1, source_target_pairs={{0,8},{8,16},{16,24},{24,28},{28,20},{20,12},{12,4},{4,0},{9,1},{1... | collective-permute-start | bytes 2875400 | tf_op jit(solution)/shard_map/ppermute | solution.py:1096
  556.0 20.9 %collective-permute-start.67 = (bf16[1248,384]{1,0:T(8,128)(2,1)S(1)}, bf16[1248,384]{1,0:T(8,128)(2,1)S(1)}, u32[]{:S(2)}, u32[]{:S(2)}) collective-permute-start(bf16[1248,384]{1,0:T(8,128)(2,1)S(1)} %late_join.3.refs_1_.refs_8_), channel_id=1, source_target_pairs={{8,0},{16,8},{24,16},{28,24},{20,28},{12,20},{4,12},{0,4},{1,9},{9... | collective-permute-start | bytes 2875400 | tf_op jit(solution)/shard_map/ppermute | solution.py:1096
  563.2 21.4 %collective-permute-start.66 = (bf16[1248,384]{1,0:T(8,128)(2,1)S(1)}, bf16[1248,384]{1,0:T(8,128)(2,1)S(1)}, u32[]{:S(2)}, u32[]{:S(2)}) collective-permute-start(bf16[1248,384]{1,0:T(8,128)(2,1)S(1)} %collective-permute-done.63.refs_0_.refs_1_), channel_id=1, source_target_pairs={{0,8},{8,16},{16,24},{24,28},{28,20},{20,12},{12,4},{4,0},{9,1},{1... | collective-permute-start | bytes 2875400 | tf_op jit(solution)/shard_map/ppermute | solution.py:1096
  576.9 21.6 %collective-permute-start.68 = (bf16[1248,384]{1,0:T(8,128)(2,1)S(1)}, bf16[1248,384]{1,0:T(8,128)(2,1)S(1)}, u32[]{:S(2)}, u32[]{:S(2)}) collective-permute-start(bf16[1248,384]{1,0:T(8,128)(2,1)S(1)} %collective-permute-done.67.refs_1_.refs_9_), channel_id=1, source_target_pairs={{8,0},{16,8},{24,16},{28,24},{20,28},{12,20},{4,12},{0,4},{1,9},{9... | collective-permute-start | bytes 2875400 | tf_op jit(solution)/shard_map/ppermute | solution.py:1096
  584.6 21.4 %collective-permute-start.72 = (bf16[1248,384]{1,0:T(8,128)(2,1)S(1)}, bf16[1248,384]{1,0:T(8,128)(2,1)S(1)}, u32[]{:S(2)}, u32[]{:S(2)}) collective-permute-start(bf16[1248,384]{1,0:T(8,128)(2,1)S(1)} %collective-permute-done.66.refs_0_.refs_2_), channel_id=1, source_target_pairs={{0,8},{8,16},{16,24},{24,28},{28,20},{20,12},{12,4},{4,0},{9,1},{1... | collective-permute-start | bytes 2875400 | tf_op jit(solution)/shard_map/ppermute | solution.py:1096
  598.5 22.4 %collective-permute-start.74 = (bf16[1248,384]{1,0:T(8,128)(2,1)S(1)}, bf16[1248,384]{1,0:T(8,128)(2,1)S(1)}, u32[]{:S(2)}, u32[]{:S(2)}) collective-permute-start(bf16[1248,384]{1,0:T(8,128)(2,1)S(1)} %collective-permute-done.68.refs_1_.refs_10_), channel_id=1, source_target_pairs={{8,0},{16,8},{24,16},{28,24},{20,28},{12,20},{4,12},{0,4},{1,9},{9... | collective-permute-start | bytes 2875400 | tf_op jit(solution)/shard_map/ppermute | solution.py:1096
  606.0 21.4 %collective-permute-start.73 = (bf16[1248,384]{1,0:T(8,128)(2,1)S(1)}, bf16[1248,384]{1,0:T(8,128)(2,1)S(1)}, u32[]{:S(2)}, u32[]{:S(2)}) collective-permute-start(bf16[1248,384]{1,0:T(8,128)(2,1)S(1)} %collective-permute-done.72.refs_0_.refs_3_), channel_id=1, source_target_pairs={{0,8},{8,16},{16,24},{24,28},{28,20},{20,12},{12,4},{4,0},{9,1},{1... | collective-permute-start | bytes 2875400 | tf_op jit(solution)/shard_map/ppermute | solution.py:1096
  620.9 22.1 %collective-permute-start.76 = (bf16[1248,384]{1,0:T(8,128)(2,1)S(1)}, bf16[1248,384]{1,0:T(8,128)(2,1)S(1)}, u32[]{:S(2)}, u32[]{:S(2)}) collective-permute-start(bf16[1248,384]{1,0:T(8,128)(2,1)S(1)} %collective-permute-done.74.refs_1_.refs_11_), channel_id=1, source_target_pairs={{8,0},{16,8},{24,16},{28,24},{20,28},{12,20},{4,12},{0,4},{1,9},{9... | collective-permute-start | bytes 2875400 | tf_op jit(solution)/shard_map/ppermute | solution.py:1096
  620.9 45.0 %collective-permute-start.69 = (bf16[1024,768]{1,0:T(8,128)(2,1)S(1)}, bf16[1024,768]{1,0:T(8,128)(2,1)S(1)}, u32[]{:S(2)}, u32[]{:S(2)}) collective-permute-start(bf16[1024,768]{1,0:T(8,128)(2,1)S(1)} %mix.7), channel_id=1, source_target_pairs={{0,1},{1,0},{2,3},{3,2},{4,5},{5,4},{6,7},{7,6},{8,9},{9,8},{10,11... | collective-permute-start | bytes 4718600 | tf_op jit(solution)/shard_map/ppermute | solution.py:51
  627.4 21.4 %collective-permute-start.75 = (bf16[1248,384]{1,0:T(8,128)(2,1)S(1)}, bf16[1248,384]{1,0:T(8,128)(2,1)S(1)}, u32[]{:S(2)}, u32[]{:S(2)}) collective-permute-start(bf16[1248,384]{1,0:T(8,128)(2,1)S(1)} %collective-permute-done.73.refs_0_.refs_4_), channel_id=1, source_target_pairs={{0,8},{8,16},{16,24},{24,28},{28,20},{20,12},{12,4},{4,0},{9,1},{1... | collective-permute-start | bytes 2875400 | tf_op jit(solution)/shard_map/ppermute | solution.py:1096
  643.0 22.9 %collective-permute-start.78 = (bf16[1248,384]{1,0:T(8,128)(2,1)S(1)}, bf16[1248,384]{1,0:T(8,128)(2,1)S(1)}, u32[]{:S(2)}, u32[]{:S(2)}) collective-permute-start(bf16[1248,384]{1,0:T(8,128)(2,1)S(1)} %collective-permute-done.76.refs_1_.refs_12_), channel_id=1, source_target_pairs={{8,0},{16,8},{24,16},{28,24},{20,28},{12,20},{4,12},{0,4},{1,9},{9... | collective-permute-start | bytes 2875400 | tf_op jit(solution)/shard_map/ppermute | solution.py:1096
  648.8 21.4 %collective-permute-start.77 = (bf16[1248,384]{1,0:T(8,128)(2,1)S(1)}, bf16[1248,384]{1,0:T(8,128)(2,1)S(1)}, u32[]{:S(2)}, u32[]{:S(2)}) collective-permute-start(bf16[1248,384]{1,0:T(8,128)(2,1)S(1)} %collective-permute-done.75.refs_0_.refs_5_), channel_id=1, source_target_pairs={{0,8},{8,16},{16,24},{24,28},{28,20},{20,12},{12,4},{4,0},{9,1},{1... | collective-permute-start | bytes 2875400 | tf_op jit(solution)/shard_map/ppermute | solution.py:1096
  665.9 23.8 %collective-permute-start.80 = (bf16[1248,384]{1,0:T(8,128)(2,1)S(1)}, bf16[1248,384]{1,0:T(8,128)(2,1)S(1)}, u32[]{:S(2)}, u32[]{:S(2)}) collective-permute-start(bf16[1248,384]{1,0:T(8,128)(2,1)S(1)} %collective-permute-done.78.refs_1_.refs_13_), channel_id=1, source_target_pairs={{8,0},{16,8},{24,16},{28,24},{20,28},{12,20},{4,12},{0,4},{1,9},{9... | collective-permute-start | bytes 2875400 | tf_op jit(solution)/shard_map/ppermute | solution.py:1096
  666.5 27.4 %collective-permute-start.70 = (bf16[512,768]{1,0:T(8,128)(2,1)S(1)}, bf16[512,768]{1,0:T(8,128)(2,1)S(1)}, u32[]{:S(2)}, u32[]{:S(2)}) collective-permute-start(bf16[512,768]{1,0:T(8,128)(2,1)S(1)} %dynamic-slice_convert_fusion), channel_id=1, source_target_pairs={{0,2},{2,0},{1,3},{3,1},{4,6},{6,4},{5,7},{7,5},{8,10},{10,8},{9,1... | collective-permute-start | bytes 2359304 | tf_op jit(solution)/shard_map/ppermute | solution.py:51
  670.2 27.1 %collective-permute-start.79 = (bf16[1248,384]{1,0:T(8,128)(2,1)S(1)}, bf16[1248,384]{1,0:T(8,128)(2,1)S(1)}, u32[]{:S(2)}, u32[]{:S(2)}) collective-permute-start(bf16[1248,384]{1,0:T(8,128)(2,1)S(1)} %collective-permute-done.77.refs_0_.refs_6_), channel_id=1, source_target_pairs={{0,8},{8,16},{16,24},{24,28},{28,20},{20,12},{12,4},{4,0},{9,1},{1... | collective-permute-start | bytes 2875400 | tf_op jit(solution)/shard_map/ppermute | solution.py:1096
  689.7 14.0 %collective-permute-start.81 = (bf16[1248,384]{1,0:T(8,128)(2,1)S(1)}, bf16[1248,384]{1,0:T(8,128)(2,1)S(1)}, u32[]{:S(2)}, u32[]{:S(2)}) collective-permute-start(bf16[1248,384]{1,0:T(8,128)(2,1)S(1)} %collective-permute-done.80.refs_1_.refs_14_), channel_id=1, source_target_pairs={{8,0},{16,8},{24,16},{28,24},{20,28},{12,20},{4,12},{0,4},{1,9},{9... | collective-permute-start | bytes 2875400 | tf_op jit(solution)/shard_map/ppermute | solution.py:1096
  (123 other events, 717.8 us)

commit v14 on v12

--- a/solution.py
+++ b/solution.py
@@ -856,62 +856,42 @@
     )(came, mine)
 
 
-def late_load_kernel(plan_ref, pack_ref, main_ref, out_ref):
-    rows = pack_ref.shape[1]
-    out_ref[0:rows, :] = pack_ref[0]
-    out_ref[rows:, :] = main_ref[...]
-
-
-def late_load(plan, at, pack, main):
+def late_add_kernel(came, plan_ref, pack_ref, *refs):
+    values = pack_ref[0]
+    if came:
+        values = (refs[0][...].astype(F32) + values.astype(F32)).astype(BF16)
+    refs[came][...] = values
+
+
+def late_chunk(plan, at, pack, *came):
     rows, lanes = pack.shape[1:]
-    total = rows + main.shape[0]
-    return pl.pallas_call(
-        late_load_kernel,
+    spec = pl.BlockSpec((rows, lanes), lambda i, n: (0, 0))
+    return pl.pallas_call(
+        functools.partial(late_add_kernel, len(came)),
         grid_spec=pltpu.PrefetchScalarGridSpec(
             num_scalar_prefetch=1,
             grid=(1,),
-            in_specs=[
-                pl.BlockSpec((1, rows, lanes), lambda i, n: (n[at], 0, 0)),
-                pl.BlockSpec(main.shape, lambda i, n: (0, 0)),
-            ],
-            out_specs=pl.BlockSpec((total, lanes), lambda i, n: (0, 0)),
+            in_specs=[pl.BlockSpec((1, rows, lanes), lambda i, n: (n[at], 0, 0))]
+            + [spec] * len(came),
+            out_specs=spec,
         ),
-        out_shape=jax.ShapeDtypeStruct((total, lanes), BF16),
+        out_shape=jax.ShapeDtypeStruct((rows, lanes), BF16),
         compiler_params=params(16, "arbitrary"),
         cost_estimate=SMALL,
-        name="late_load",
-    )(plan, pack, main)
-
-
-def late_add_kernel(plan_ref, pack_ref, came_ref, *outs):
-    total = (came_ref[...].astype(F32) + pack_ref[0].astype(F32)).astype(BF16)
-    for out_ref in outs:
-        out_ref[...] = total
-
-
-def late_add(plan, at, pack, came, copied=False):
-    rows, lanes = pack.shape[1:]
-    spec = pl.BlockSpec((rows, lanes), lambda i, n: (0, 0))
-    shape = jax.ShapeDtypeStruct(came.shape, BF16)
-    return pl.pallas_call(
-        late_add_kernel,
-        grid_spec=pltpu.PrefetchScalarGridSpec(
-            num_scalar_prefetch=1,
-            grid=(1,),
-            in_specs=[pl.BlockSpec((1, rows, lanes), lambda i, n: (n[at], 0, 0)), spec],
-            out_specs=[spec] * 2 if copied else spec,
-        ),
-        out_shape=[shape, jax.ShapeDtypeStruct((rows, lanes), BF16)] if copied else shape,
-        input_output_aliases={2: 0},
-        compiler_params=params(16, "arbitrary"),
-        cost_estimate=SMALL,
-        name="late_add",
-    )(plan, pack, came)
-
-
-def late_join_kernel(col_ref, mine_ref, other_ref, gains_ref, main_ref, out_ref):
+        name="late_chunk",
+    )(plan, pack, *came)
+
+
+def late_pick(plan, at, pack):
+    return late_chunk(plan, at, pack)
+
+
+def late_add(plan, at, pack, came):
+    return late_chunk(plan, at, pack, came)
+
+
+def late_join_kernel(col_ref, mine_ref, other_ref, gains_ref, out_ref):
     units = 7
-    out_ref[mine_ref.shape[0] :, :] = main_ref[...]
     share = mine_ref.shape[0] // LATE_BLOCKS
     to_rows, to_lanes = unit_slices(2 * units, share)
     blocks = gains_ref.shape[1] // LANES
@@ -929,9 +909,8 @@
     out_ref[to_rows, to_lanes] = gains.astype(BF16)
 
 
-def late_join(col, mine, other, gains, main):
+def late_join(col, mine, other, gains):
     rows, lanes = mine.shape
-    total = rows + main.shape[0]
 
     def all_of(*shape):
         return pl.BlockSpec(shape, lambda i, c: (0, 0))
@@ -941,14 +920,14 @@
         grid_spec=pltpu.PrefetchScalarGridSpec(
             num_scalar_prefetch=1,
             grid=(1,),
-            in_specs=[all_of(rows, lanes)] * 2 + [all_of(*gains.shape), all_of(*main.shape)],
-            out_specs=all_of(total, lanes),
+            in_specs=[all_of(rows, lanes)] * 2 + [all_of(*gains.shape)],
+            out_specs=all_of(rows, lanes),
         ),
-        out_shape=jax.ShapeDtypeStruct((total, lanes), BF16),
+        out_shape=jax.ShapeDtypeStruct((rows, lanes), BF16),
         compiler_params=params(16, "arbitrary"),
         cost_estimate=SMALL,
         name="late_join",
-    )(col, mine, other, gains, main)
+    )(col, mine, other, gains)
 
 
 def unpack_late_kernel(first_step, steps, plan_ref, *refs):
@@ -1303,7 +1282,7 @@
         return [normed["tie"]]
 
     tasks = [work_experts(at, min(at + 2, pairs_total)) for at in range(1, pairs_total, 2)]
-    tasks += [work_shared, work_back(1), work_back(0), None, work_out(0), work_tie]
+    tasks += [work_shared, work_back(1), work_back(0), work_out(1), work_out(0), work_tie]
     ends = [work_hidden, work_attend, work_late]
     tasks += [None] * (2 * ring_size - 2 - len(tasks) - len(ends)) + ends
     got = [None, None]
@@ -1362,58 +1341,64 @@
 
     shapes = [w_gate.shape, w_up.shape, w_down.shape]
     placed = ()
-    late_out = [[], []]
+    late, late_out, late_done = [None, None], [[], []], 0
+
+    def late_turn():
+        others = [swap(across_rings(values), "col") for values in late]
+        for k in range(2):
+            late[k] = late_join(col_ref, across_rings(late[k]), others[1 - k], normed["gains"])
+            late_out[k].append(late[k])
+
+    def late_finish(k, values):
+        if late_done < ring_size:
+            at = chunks_first + 2 * late_done + k
+            late[k] = late_add(plan, at, normed["packs"][k], values)
+        else:
+            late[k] = values
+            late_out[k].append(values)
+
+    late = [late_pick(plan, chunks_first + k, normed["packs"][k]) for k in range(2)]
+    late_got = None
     last, got = [], [None, None]
     moves = [(wave, step) for wave in range(2) for step in range(ring_size - 1)]
     for number, (wave, step) in enumerate(moves):
-        current = [None, None]
-        copies = [None, None]
-        turn = number == ring_size - 1
+        if step == 0:
+            came = list(got)
+            got = list(waves[wave])
+        late_done += late_got is not None
+        chunks = [None, None]
         for k in range(2):
-            at = chunks_first + 2 * number + k
-            pack = normed["packs"][k]
-            if number == 0:
-                current[k] = late_load(plan, at, pack, after(waves[0][k], *last))
-            elif number < ring_size - 1:
-                current[k] = late_add(plan, at, pack, after(got[k], *last))
-            elif turn:
-                current[k], copies[k] = late_add(plan, at, pack, after(got[k], *last), True)
-            else:
-                current[k] = after(got[k], *last)
-            last = [current[k]]
-            if not turn:
-                got[k] = send(current[k], k)
-        if turn:
-            placed = unpack(plan, experts + 2 * (ring_size - 1), 0, current, shapes, placed)
-            others = [swap(across_rings(values), "col") for values in copies]
-            for k in range(2):
-                current[k] = late_join(
-                    col_ref, after(copies[k], *last), others[1 - k], normed["gains"], waves[1][k]
-                )
-                got[k] = send(current[k], k)
-                last = work_out(1)(after(order, current[k]), ()) if k == 0 else [current[k]]
-        if number >= ring_size - 1:
-            for k in range(2):
-                late_out[k].append(current[k])
-        placed = unpack(
-            plan, experts + 2 * step, wave, [after(current[0], *last), current[1]], shapes, placed
-        )
+            chunks[k] = after(got[k], *last) if last else got[k]
+            got[k] = send(chunks[k], k)
+            last = [chunks[k]]
+            if late_got is not None:
+                late_finish(k, after(late_got[k], *last))
+                last = [late[k]]
+        if late_done == ring_size - 1 and late_got is not None:
+            late_turn()
+        late_got = [send(late[k], k) for k in range(2)] if late_done < late_total else None
+        if wave and step == 0:
+            placed = unpack(plan, experts + 2 * (ring_size - 1), 0, came, shapes, placed)
+        placed = unpack(plan, experts + 2 * step, wave, chunks, shapes, placed)
         last = placed[0:1]
-        if number == 2:
+        if number == 3:
             back_to_tokens(last)
-        if number == ring_size + 1:
+        if number == 9:
             block_rows(last)
-    for k in range(2):
-        late_out[k].append(after(got[k], *last))
-        last = [late_out[k][-1]]
     placed = unpack(
         plan,
         experts + 2 * (ring_size - 1),
         1,
-        [late_out[k][-1] for k in range(2)],
+        [after(got[k], *last) for k in range(2)],
         shapes,
         placed,
     )
+    last = placed[0:1]
+    while late_got is not None:
+        late_done += 1
+        for k in range(2):
+            late_finish(k, after(late_got[k], *last))
+        late_got = [send(late[k], k) for k in range(2)] if late_done < late_total else None
     gate_grad, up_grad, down_grad = placed
     shapes = [w.shape for w in (w_shared_gate, w_shared_up, w_shared_down)]
     shapes += [w.shape for w in (w_query, w_key, w_value, w_out)] + [gains.shape]

time: 693 us -> 684 us (0.987)
  starting transfers between devices: 69.8 us -> 102 us
  waiting for transfers between devices: 272 us -> 246 us
  local copies, waits for them, and re-layouts: 38.2 us -> 29.7 us
    ppermute x42 -> x70, starting transfers between devices: 44.5 us -> 77.7 us  [send(): return lax.ppermute(values, ('dp', 'col'), routes_of[which])]
    ppermute x42 -> x70, waiting for transfers between devices: 228 us -> 209 us  [send(): return lax.ppermute(values, ('dp', 'col'), routes_of[which])]
    unnamed x216 -> x196, local copies, waits for them, and re-layouts: 35.8 us -> 27.2 us
  transfers between devices with their start and end apart: 82 -> 110, of which waited for: 38 -> 44; matrix products, arithmetic and copies ran while one was open for 2% -> 3% of each run, Pallas kernels for 39% -> 39%
where the time goes in v14:
time: 684 us; the launch traced here: 675 us
  Pallas kernels  279 us (41%)
  waiting for transfers between devices  246 us (36%)
  starting transfers between devices  102 us (15%)
  local copies, waits for them, and re-layouts  29.7 us (4%)
  other arithmetic  10.3 us (2%)
    ppermute x70, waiting for transfers between devices, send(): return lax.ppermute(values, ('dp', 'col'), routes_of[which])  209 us
    ppermute x70, starting transfers between devices, send(): return lax.ppermute(values, ('dp', 'col'), routes_of[which])  77.7 us
    pallas_call x6, Pallas kernels, expert_grads(): pl.pallas_call(functools.partial(expert_kernel, shared, aliased, first),...  72.1 us
    pallas_call x4, Pallas kernels, mix(): pl.pallas_call(functools.partial(mix_kernel, back, group, pieces), grid_s...  40.5 us
    pallas_call x16, Pallas kernels, unpack(): pl.pallas_call(functools.partial(unpack_kernel, aliased), grid_spec=pltpu...  37.4 us
    ppermute x37, waiting for transfers between devices, swap(): return lax.ppermute(values, axis, [(0, 1), (1, 0)])  34.9 us
    pallas_call x14, Pallas kernels, ring_sum(): pl.pallas_call(ring_sum_kernel, grid=(count, tiles), in_specs=[spec, term...  28.1 us
    unnamed x196, local copies, waits for them, and re-layouts  27.2 us
  transfers between devices with their start and end apart: 110, of which 44 were waited for; matrix products, arithmetic and copies ran while one was open for 3% of the time, Pallas kernels for 39%

profile of v14, /device:TPU:0, one launch (start us, length us, event | category | flops | bytes accessed | tf_op | source)
XLA Modules:
  0.0 674.7 jit_solution(2579917531419843461)
XLA Ops:
  1.8 3.1 their_columns.1
  5.4 2.6 collective-permute-start
  8.2 5.0 collective-permute-done.2.gains_c_ref.refs_7_
  13.3 2.9 collective-permute-start.4
  18.0 4.5 project.2
  22.5 9.9 %collective-permute-done.4.refs_0_ = bf16[192,768]{1,0:T(8,128)(2,1)S(1)} collective-permute-done((bf16[192,768]{1,0:T(8,128)(2,1)}, bf16[192,768]{1,0:T(8,128)(2,1)S(1)}, u32[]{:S(2)}, u32[]{:S(2)}) %collective-permute-start.4) | collective-permute-done | bytes 294944 | tf_op jit(solution)/shard_map/ppermute | solution.py:51
  32.4 2.5 collective-permute-done.8.other_ref.refs_3_
  40.8 4.5 project.3
  47.4 2.5 collective-permute-start.9
  50.7 5.0 collective-permute-done.5.refs_1_
  57.5 6.3 attend.1.refs_4_.refs_5_
  69.5 9.0 %hidden_before.1 = (f32[1024,768]{1,0:T(8,128)}, f32[1024,768]{1,0:T(8,128)}) custom-call(s32[3]{0:T(128)} %copy-done.70, bf16[512,768]{1,0:T(8,128)(2,1)} %refs_0_.2, bf16[512,768]{1,0:T(8,128)(2,1)} %copy-done.86, bf16[512,768]{1,0:T(8,128)(2,1)} %collective-permute-done.own_ref.refs_2_, bf16[512,768]{1,0:T(8,128)(2,1)} %copy-done.87, ...), custom_call_target="tpu_custom_call" | custom-call | flops 2415919104 | bytes 12582912 | tf_op jit(solution)/shard_map/hidden_before/pallas_call | solution.py:418
  78.5 5.6 collective-permute-done.12.refs_2_
  87.5 9.4 %hidden_after.1 = (f32[1024,768]{1,0:T(8,128)}, bf16[1024,768]{1,0:T(8,128)(2,1)}, bf16[1024,768]{1,0:T(8,128)(2,1)}, f32[1024,1]{1,0:T(8,128)}) custom-call(s32[3]{0:T(128)} %copy-done.70, f32[1024,768]{1,0:T(8,128)} %get-tuple-element.229.refs_0_, f32[1024,768]{1,0:T(8,128)} %get-tuple-element.230.refs_1_, ...), custom_call_target="tpu_custom_call" | custom-call | tf_op jit(solution)/shard_map/hidden_after/pallas_call | solution.py:440
  100.3 9.0 %expert_grads.6 = (bf16[1,1536,384]{2,1,0:T(8,128)(2,1)S(1)}, bf16[1,1536,384]{2,1,0:T(8,128)(2,1)S(1)}, bf16[8,1024,512]{2,1,0:T(8,128)(2,1)}, bf16[8,1024,256]{2,1,0:T(8,128)(2,1)S(1)}) custom-call(s32[63]{0:T(128)S(1)} %fusion.14.order_ref.plan_ref, bf16[1024,768]{1,0:T(8,128)(2,1)S(1)} %copy-done.8, bf16[1024,768]{1,0:T(8,128)(2,1)S(1)} %copy-done.9, ...), custom_call_target="tpu_custom_call" | custom-call | tf_op jit(solution)/shard_map/expert_grads/pallas_call | solution.py:563
  112.9 15.2 %expert_grads.7 = (bf16[2,1536,384]{2,1,0:T(8,128)(2,1)S(1)}, bf16[2,1536,384]{2,1,0:T(8,128)(2,1)S(1)}, bf16[8,1024,512]{2,1,0:T(8,128)(2,1)}, bf16[8,1024,256]{2,1,0:T(8,128)(2,1)}) custom-call(s32[63]{0:T(128)S(1)} %fusion.14.order_ref.plan_ref, bf16[1024,768]{1,0:T(8,128)(2,1)S(1)} %copy-done.8, ...), custom_call_target="tpu_custom_call", output_to_operand_aliasing={{2}: (18, {}), {3}: (19, {})} | custom-call | tf_op jit(solution)/shard_map/expert_grads/pallas_call | solution.py:563
  128.6 15.6 %expert_grads.8 = (bf16[2,1536,384]{2,1,0:T(8,128)(2,1)S(1)}, bf16[2,1536,384]{2,1,0:T(8,128)(2,1)S(1)}, bf16[8,1024,512]{2,1,0:T(8,128)(2,1)}, bf16[8,1024,256]{2,1,0:T(8,128)(2,1)}) custom-call(s32[63]{0:T(128)S(1)} %fusion.14.order_ref.plan_ref, bf16[1024,768]{1,0:T(8,128)(2,1)S(1)} %copy-done.8, ...), custom_call_target="tpu_custom_call", output_to_operand_aliasing={{2}: (18, {}), {3}: (19, {})} | custom-call | tf_op jit(solution)/shard_map/expert_grads/pallas_call | solution.py:563
  148.4 15.6 %expert_grads.9 = (bf16[2,1536,384]{2,1,0:T(8,128)(2,1)S(1)}, bf16[2,1536,384]{2,1,0:T(8,128)(2,1)S(1)}, bf16[8,1024,512]{2,1,0:T(8,128)(2,1)}, bf16[8,1024,256]{2,1,0:T(8,128)(2,1)}) custom-call(s32[63]{0:T(128)S(1)} %fusion.14.order_ref.plan_ref, bf16[1024,768]{1,0:T(8,128)(2,1)S(1)} %copy-done.8, ...), custom_call_target="tpu_custom_call", output_to_operand_aliasing={{2}: (18, {}), {3}: (19, {})} | custom-call | tf_op jit(solution)/shard_map/expert_grads/pallas_call | solution.py:563
  169.4 9.0 %expert_grads.10 = (bf16[1,1536,384]{2,1,0:T(8,128)(2,1)S(1)}, bf16[1,1536,384]{2,1,0:T(8,128)(2,1)S(1)}, bf16[8,1024,512]{2,1,0:T(8,128)(2,1)}, bf16[8,1024,256]{2,1,0:T(8,128)(2,1)S(1)}) custom-call(s32[63]{0:T(128)S(1)} %fusion.14.order_ref.plan_ref, bf16[1024,768]{1,0:T(8,128)(2,1)S(1)} %copy-done.8, ...), custom_call_target="tpu_custom_call", output_to_operand_aliasing={{2}: (18, {}), {3}: (19, {})} | custom-call | tf_op jit(solution)/shard_map/expert_grads/pallas_call | solution.py:563
  184.4 7.7 %expert_grads.11 = (bf16[1,1536,384]{2,1,0:T(8,128)(2,1)S(1)}, bf16[1,1536,384]{2,1,0:T(8,128)(2,1)S(1)}, bf16[1,1024,512]{2,1,0:T(8,128)(2,1)S(1)}, bf16[1,1024,256]{2,1,0:T(8,128)(2,1)S(1)}) custom-call(s32[63]{0:T(128)S(1)} %fusion.14.order_ref.plan_ref, bf16[1024,768]{1,0:T(8,128)(2,1)S(1)} %copy-done.8, bf16[1024,768]{1,0:T(8,128)(2,1)S(1)} %copy-done.10, ...), custom_call_target="tpu_custom_call" | custom-call | tf_op jit(solution)/shard_map/expert_grads/pallas_call | solution.py:563
  194.9 13.3 %mix.4 = (bf16[512,768]{1,0:T(8,128)(2,1)}, bf16[512,768]{1,0:T(8,128)(2,1)S(1)}) custom-call(s32[63]{0:T(128)S(1)} %fusion.14.order_ref.plan_ref, bf16[8,1024,512]{2,1,0:T(8,128)(2,1)} %get-tuple-element.255.refs_0_, bf16[1,1024,512]{2,1,0:T(8,128)(2,1)S(1)} %get-tuple-element.261.refs_1_, ...), custom_call_target="tpu_custom_call" | custom-call | tf_op jit(solution)/shard_map/mix/pallas_call | solution.py:636
  208.3 3.8 ring_sum.18
  213.5 12.5 %mix.5.own_ref = f32[1024,768]{1,0:T(8,128)S(1)} custom-call(s32[63]{0:T(128)S(1)} %fusion.14.order_ref.plan_ref, bf16[8,1024,512]{2,1,0:T(8,128)(2,1)} %get-tuple-element.255.refs_0_, bf16[1,1024,512]{2,1,0:T(8,128)(2,1)S(1)} %get-tuple-element.261.refs_1_, bf16[16,768,256]{2,1,0:T(8,128)(2,1)} %refs_16_.1, bf16[16,768,256]{2,1,0:T(8,128)(2,1)} %refs_17_.1, ...), custom_call_target="tpu_custom_call" | custom-call | tf_op jit(solution)/shard_map/mix/pallas_call | solution.py:636
  226.0 3.9 ring_sum.19
  231.0 7.5 %mix.6 = bf16[1024,768]{1,0:T(8,128)(2,1)S(1)} custom-call(s32[63]{0:T(128)S(1)} %fusion.14.order_ref.plan_ref, bf16[8,1024,256]{2,1,0:T(8,128)(2,1)} %copy-done.6, bf16[1,1024,256]{2,1,0:T(8,128)(2,1)S(1)} %get-tuple-element.273.refs_1_, ...), custom_call_target="tpu_custom_call" | custom-call | tf_op jit(solution)/shard_map/mix/pallas_call | solution.py:636
  241.6 3.5 chip_sum.1
  249.8 7.3 %mix.7 = f32[1024,768]{1,0:T(8,128)S(1)} custom-call(s32[63]{0:T(128)S(1)} %fusion.14.order_ref.plan_ref, bf16[8,1024,256]{2,1,0:T(8,128)(2,1)} %copy-done.6, bf16[1,1024,256]{2,1,0:T(8,128)(2,1)S(1)} %get-tuple-element.273.refs_1_, bf16[16,256,768]{2,1,0:T(8,128)(2,1)} %refs_9_.13, bf16[16,256,768]{2,1,0:T(8,128)(2,1)} %refs_9_.13, ...), custom_call_target="tpu_custom_call" | custom-call | tf_op jit(solution)/shard_map/mix/pallas_call | solution.py:636
  258.1 10.7 %collective-permute-done.31.came_ref = bf16[1,1536,384]{2,1,0:T(8,128)(2,1)} collective-permute-done((bf16[1,1536,384]{2,1,0:T(8,128)(2,1)}, bf16[1,1536,384]{2,1,0:T(8,128)(2,1)}, u32[]{:S(2)}, u32[]{:S(2)}) %collective-permute-start.31) | collective-permute-done | bytes 1179680 | tf_op jit(solution)/shard_map/ppermute | solution.py:1075
  272.7 8.5 %collective-permute-done.30.came_ref = bf16[1,1536,384]{2,1,0:T(8,128)(2,1)S(1)} collective-permute-done((bf16[1,1536,384]{2,1,0:T(8,128)(2,1)S(1)}, bf16[1,1536,384]{2,1,0:T(8,128)(2,1)S(1)}, u32[]{:S(2)}, u32[]{:S(2)}) %collective-permute-start.30) | collective-permute-done | bytes 1179680 | tf_op jit(solution)/shard_map/ppermute | solution.py:1075
  288.6 6.6 norm_back.1
  300.2 13.1 %attend_back.1.refs_4_ = bf16[1024,640]{1,0:T(8,128)(2,1)} custom-call(s32[3]{0:T(128)} %copy-done.70, bf16[512,640]{1,0:T(8,128)(2,1)} %get-tuple-element.221.own_ref, bf16[512,640]{1,0:T(8,128)(2,1)} %get-tuple-element.225.other_ref, bf16[512,768]{1,0:T(8,128)(2,1)} %copy-done.40, bf16[512,768]{1,0:T(8,128)(2,1)} %copy-done.41, ...), custom_call_target="tpu_custom_call" | custom-call | tf_op jit(solution)/shard_map/attend_back/pallas_call | solution.py:173
  316.2 16.2 %late_grads.1 = (bf16[8,480,384]{2,1,0:T(8,128)(2,1)}, bf16[8,480,384]{2,1,0:T(8,128)(2,1)}) custom-call(s32[3]{0:T(128)} %copy-done.70, bf16[512,768]{1,0:T(8,128)(2,1)} %get-tuple-element.292.refs_0_, bf16[512,768]{1,0:T(8,128)(2,1)} %get-tuple-element.293.refs_1_, bf16[512,768]{1,0:T(8,128)(2,1)} %get-tuple-element.294.refs_2_, ...), custom_call_target="tpu_custom_call" | custom-call | tf_op jit(solution)/shard_map/late_grads/pallas_call | solution.py:237
  332.4 3.3 ring_sum.26
  343.2 8.6 %collective-permute-done.45.refs_0_ = bf16[768,384]{1,0:T(8,128)(2,1)S(1)} collective-permute-done((bf16[768,384]{1,0:T(8,128)(2,1)S(1)}, bf16[768,384]{1,0:T(8,128)(2,1)S(1)}, u32[]{:S(2)}, u32[]{:S(2)}) %collective-permute-start.45) | collective-permute-done | bytes 589856 | tf_op jit(solution)/shard_map/ppermute | solution.py:1075
  360.6 6.2 collective-permute-done.46.refs_0_
  368.2 4.2 collective-permute-done.51.refs_0_
  378.3 6.2 collective-permute-done.49.refs_0_
  384.5 7.9 %collective-permute-done.54.refs_0_ = bf16[480,384]{1,0:T(8,128)(2,1)S(1)} collective-permute-done((bf16[480,384]{1,0:T(8,128)(2,1)S(1)}, bf16[480,384]{1,0:T(8,128)(2,1)S(1)}, u32[]{:S(2)}, u32[]{:S(2)}) %collective-permute-start.54) | collective-permute-done | bytes 368672 | tf_op jit(solution)/shard_map/ppermute | solution.py:1075
  395.2 2.6 convolution_convert_fusion
  402.5 6.8 %collective-permute-done.71.refs_0_ = bf16[480,384]{1,0:T(8,128)(2,1)S(1)} collective-permute-done((bf16[480,384]{1,0:T(8,128)(2,1)S(1)}, bf16[480,384]{1,0:T(8,128)(2,1)S(1)}, u32[]{:S(2)}, u32[]{:S(2)}) %collective-permute-start.71) | collective-permute-done | bytes 368672 | tf_op jit(solution)/shard_map/ppermute | solution.py:1075
  411.1 4.2 collective-permute-done.52.refs_0_
  416.8 6.3 collective-permute-done.57.refs_0_
  425.0 5.0 collective-permute-done.72.refs_0_
  436.4 10.7 %collective-permute-done.73.refs_0_ = bf16[480,384]{1,0:T(8,128)(2,1)} collective-permute-done((bf16[480,384]{1,0:T(8,128)(2,1)}, bf16[480,384]{1,0:T(8,128)(2,1)}, u32[]{:S(2)}, u32[]{:S(2)}) %collective-permute-start.73) | collective-permute-done | bytes 368672 | tf_op jit(solution)/shard_map/ppermute | solution.py:1075
  449.4 3.6 unpack.20
  458.5 2.9 convert_add_fusion.1
  464.9 10.7 %collective-permute-done.62.refs_0_ = bf16[480,384]{1,0:T(8,128)(2,1)S(1)} collective-permute-done((bf16[480,384]{1,0:T(8,128)(2,1)S(1)}, bf16[480,384]{1,0:T(8,128)(2,1)S(1)}, u32[]{:S(2)}, u32[]{:S(2)}) %collective-permute-start.62) | collective-permute-done | bytes 368672 | tf_op jit(solution)/shard_map/ppermute | solution.py:1075
  476.1 3.3 unpack.21
  504.5 12.1 %collective-permute-done.67.refs_1_ = bf16[768,384]{1,0:T(8,128)(2,1)S(1)} collective-permute-done((bf16[768,384]{1,0:T(8,128)(2,1)S(1)}, bf16[768,384]{1,0:T(8,128)(2,1)S(1)}, u32[]{:S(2)}, u32[]{:S(2)}) %collective-permute-start.67) | collective-permute-done | bytes 589856 | tf_op jit(solution)/shard_map/ppermute | solution.py:1075
  516.6 10.2 %collective-permute-done.66.refs_0_ = bf16[768,384]{1,0:T(8,128)(2,1)S(1)} collective-permute-done((bf16[768,384]{1,0:T(8,128)(2,1)S(1)}, bf16[768,384]{1,0:T(8,128)(2,1)S(1)}, u32[]{:S(2)}, u32[]{:S(2)}) %collective-permute-start.66) | collective-permute-done | bytes 589856 | tf_op jit(solution)/shard_map/ppermute | solution.py:1075
  528.9 3.3 unpack.24
  537.6 8.2 %collective-permute-done.68.refs_0_ = bf16[768,384]{1,0:T(8,128)(2,1)S(1)} collective-permute-done((bf16[768,384]{1,0:T(8,128)(2,1)S(1)}, bf16[768,384]{1,0:T(8,128)(2,1)S(1)}, u32[]{:S(2)}, u32[]{:S(2)}) %collective-permute-start.68) | collective-permute-done | bytes 589856 | tf_op jit(solution)/shard_map/ppermute | solution.py:1075
  555.7 5.6 collective-permute-done.88.refs_0_
  562.7 6.6 collective-permute-done.87.refs_3_
  571.1 2.8 collective-permute-done.103.refs_9_
  576.0 14.0 %collective-permute-done.104.refs_10_ = bf16[480,384]{1,0:T(8,128)(2,1)S(1)} collective-permute-done((bf16[480,384]{1,0:T(8,128)(2,1)S(1)}, bf16[480,384]{1,0:T(8,128)(2,1)S(1)}, u32[]{:S(2)}, u32[]{:S(2)}) %collective-permute-start.104) | collective-permute-done | bytes 368672 | tf_op jit(solution)/shard_map/ppermute | solution.py:1075
  595.3 3.1 collective-permute-done.105.refs_11_
  600.4 17.7 %collective-permute-done.106.refs_12_ = bf16[480,384]{1,0:T(8,128)(2,1)S(1)} collective-permute-done((bf16[480,384]{1,0:T(8,128)(2,1)S(1)}, bf16[480,384]{1,0:T(8,128)(2,1)S(1)}, u32[]{:S(2)}, u32[]{:S(2)}) %collective-permute-start.106) | collective-permute-done | bytes 368672 | tf_op jit(solution)/shard_map/ppermute | solution.py:1075
  629.0 8.5 %collective-permute-done.96.refs_0_ = bf16[768,384]{1,0:T(8,128)(2,1)S(1)} collective-permute-done((bf16[768,384]{1,0:T(8,128)(2,1)S(1)}, bf16[768,384]{1,0:T(8,128)(2,1)S(1)}, u32[]{:S(2)}, u32[]{:S(2)}) %collective-permute-start.96) | collective-permute-done | bytes 589856 | tf_op jit(solution)/shard_map/ppermute | solution.py:1075
  639.6 5.3 collective-permute-done.95.refs_6_
  649.3 2.7 fusion.4
  655.4 5.8 collective-permute-done.99.refs_0_
  664.7 3.0 collective-permute-done.109.refs_15_
  667.9 5.8 unpack_late.1
  (449 shorter events, 213.2 us)
Async XLA Ops:
  0.7 34.4 %collective-permute-start.16 = (bf16[16,768,256]{2,1,0:T(8,128)(2,1)}, bf16[16,768,256]{2,1,0:T(8,128)(2,1)}, u32[]{:S(2)}, u32[]{:S(2)}) collective-permute-start(bf16[16,768,256]{2,1,0:T(8,128)(2,1)} %refs_16_.1), channel_id=1, source_target_pairs={{0,1},{1,0},{2,3},{3,2},{4,5},{5,4},{6,7},{7,6},{8,9},{9,8},{10,11... | collective-permute-start | bytes 18874376 | tf_op jit(solution)/shard_map/ppermute | solution.py:51
  5.4 27.1 %collective-permute-start = (bf16[512,768]{1,0:T(8,128)(2,1)S(1)}, bf16[512,768]{1,0:T(8,128)(2,1)}, u32[]{:S(2)}, u32[]{:S(2)}) collective-permute-start(bf16[512,768]{1,0:T(8,128)(2,1)S(1)} %copy-done.74), channel_id=1, source_target_pairs={{0,2},{2,0},{1,3},{3,1},{4,6},{6,4},{5,7},{7,5},{8,10},{10,8},{9,1... | collective-permute-start | bytes 2359304 | tf_op jit(solution)/shard_map/ppermute | solution.py:51
  13.3 19.1 %collective-permute-start.4 = (bf16[192,768]{1,0:T(8,128)(2,1)}, bf16[192,768]{1,0:T(8,128)(2,1)S(1)}, u32[]{:S(2)}, u32[]{:S(2)}) collective-permute-start(bf16[192,768]{1,0:T(8,128)(2,1)} %get-tuple-element.222), channel_id=1, source_target_pairs={{0,2},{2,0},{1,3},{3,1},{4,6},{6,4},{5,7},{7,5},{8,10},{10,8},{9,1... | collective-permute-start | bytes 884744 | tf_op jit(solution)/shard_map/ppermute | solution.py:51
  34.9 62.0 %collective-permute-start.18 = (bf16[16,256,768]{2,1,0:T(8,128)(2,1)}, bf16[16,256,768]{2,1,0:T(8,128)(2,1)}, u32[]{:S(2)}, u32[]{:S(2)}) collective-permute-start(bf16[16,256,768]{2,1,0:T(8,128)(2,1)} %refs_9_.13), channel_id=1, source_target_pairs={{0,1},{1,0},{2,3},{3,2},{4,5},{5,4},{6,7},{7,6},{8,9},{9,8},{10,11... | collective-permute-start | bytes 18874376 | tf_op jit(solution)/shard_map/ppermute | solution.py:51
  35.8 61.1 %collective-permute-start.17 = (bf16[16,768,256]{2,1,0:T(8,128)(2,1)}, bf16[16,768,256]{2,1,0:T(8,128)(2,1)}, u32[]{:S(2)}, u32[]{:S(2)}) collective-permute-start(bf16[16,768,256]{2,1,0:T(8,128)(2,1)} %refs_17_.1), channel_id=1, source_target_pairs={{0,1},{1,0},{2,3},{3,2},{4,5},{5,4},{6,7},{7,6},{8,9},{9,8},{10,11... | collective-permute-start | bytes 18874376 | tf_op jit(solution)/shard_map/ppermute | solution.py:51
  35.9 19.8 %collective-permute-start.5 = (bf16[512,768]{1,0:T(8,128)(2,1)S(1)}, bf16[512,768]{1,0:T(8,128)(2,1)S(1)}, u32[]{:S(2)}, u32[]{:S(2)}) collective-permute-start(bf16[512,768]{1,0:T(8,128)(2,1)S(1)} %copy-done.54), channel_id=1, source_target_pairs={{0,2},{2,0},{1,3},{3,1},{4,6},{6,4},{5,7},{7,5},{8,10},{10,8},{9,1... | collective-permute-start | bytes 2359304 | tf_op jit(solution)/shard_map/ppermute | solution.py:51
  50.6 17.8 %collective-permute-start.11 = (bf16[768,768]{1,0:T(8,128)(2,1)}, bf16[768,768]{1,0:T(8,128)(2,1)}, u32[]{:S(2)}, u32[]{:S(2)}) collective-permute-start(bf16[768,768]{1,0:T(8,128)(2,1)} %refs_4_.5), channel_id=1, source_target_pairs={{0,1},{1,0},{2,3},{3,2},{4,5},{5,4},{6,7},{7,6},{8,9},{9,8},{10,11... | collective-permute-start | bytes 3538952 | tf_op jit(solution)/shard_map/ppermute | solution.py:51
  63.8 20.3 %collective-permute-start.12 = (bf16[1024,384]{1,0:T(8,128)(2,1)}, bf16[1024,384]{1,0:T(8,128)(2,1)}, u32[]{:S(2)}, u32[]{:S(2)}) collective-permute-start(bf16[1024,384]{1,0:T(8,128)(2,1)} %attend.1.refs_4_.refs_5_), channel_id=1, source_target_pairs={{0,2},{2,0},{1,3},{3,1},{4,6},{6,4},{5,7},{7,5},{8,10},{10,8},{9,1... | collective-permute-start | bytes 2359304 | tf_op jit(solution)/shard_map/ppermute | solution.py:51
  67.2 29.7 %collective-permute-start.15 = (bf16[1024,768]{1,0:T(8,128)(2,1)S(1)}, bf16[1024,768]{1,0:T(8,128)(2,1)S(1)}, u32[]{:S(2)}, u32[]{:S(2)}) collective-permute-start(bf16[1024,768]{1,0:T(8,128)(2,1)S(1)} %join.3.refs_2_.refs_4_), channel_id=1, source_target_pairs={{0,1},{1,0},{2,3},{3,2},{4,5},{5,4},{6,7},{7,6},{8,9},{9,8},{10,11... | collective-permute-start | bytes 4718600 | tf_op jit(solution)/shard_map/ppermute | solution.py:51
  111.4 32.9 %collective-permute-start.19 = (bf16[1,1536,384]{2,1,0:T(8,128)(2,1)S(1)}, bf16[1,1536,384]{2,1,0:T(8,128)(2,1)S(1)}, u32[]{:S(2)}, u32[]{:S(2)}) collective-permute-start(bf16[1,1536,384]{2,1,0:T(8,128)(2,1)S(1)} %get-tuple-element.237), channel_id=1, source_target_pairs={{0,8},{8,16},{16,24},{24,28},{28,20},{20,12},{12,4},{4,0},{9,1},{1... | collective-permute-start | bytes 3538952 | tf_op jit(solution)/shard_map/ppermute | solution.py:1075
  128.1 35.9 %collective-permute-start.21 = (bf16[1,1536,384]{2,1,0:T(8,128)(2,1)S(1)}, bf16[1,1536,384]{2,1,0:T(8,128)(2,1)S(1)}, u32[]{:S(2)}, u32[]{:S(2)}) collective-permute-start(bf16[1,1536,384]{2,1,0:T(8,128)(2,1)S(1)} %get-tuple-element.247), channel_id=1, source_target_pairs={{8,0},{16,8},{24,16},{28,24},{20,28},{12,20},{4,12},{0,4},{1,9},{9... | collective-permute-start | bytes 3538952 | tf_op jit(solution)/shard_map/ppermute | solution.py:1075
  146.8 33.6 %collective-permute-start.20 = (bf16[1,1536,384]{2,1,0:T(8,128)(2,1)}, bf16[1,1536,384]{2,1,0:T(8,128)(2,1)S(1)}, u32[]{:S(2)}, u32[]{:S(2)}) collective-permute-start(bf16[1,1536,384]{2,1,0:T(8,128)(2,1)} %ring_sum.14), channel_id=1, source_target_pairs={{0,8},{8,16},{16,24},{24,28},{28,20},{20,12},{12,4},{4,0},{9,1},{1... | collective-permute-start | bytes 3538952 | tf_op jit(solution)/shard_map/ppermute | solution.py:1075
  167.6 25.5 %collective-permute-start.23 = (bf16[1,1536,384]{2,1,0:T(8,128)(2,1)S(1)}, bf16[1,1536,384]{2,1,0:T(8,128)(2,1)S(1)}, u32[]{:S(2)}, u32[]{:S(2)}) collective-permute-start(bf16[1,1536,384]{2,1,0:T(8,128)(2,1)S(1)} %ring_sum.15), channel_id=1, source_target_pairs={{8,0},{16,8},{24,16},{28,24},{20,28},{12,20},{4,12},{0,4},{1,9},{9... | collective-permute-start | bytes 3538952 | tf_op jit(solution)/shard_map/ppermute | solution.py:1075
  182.8 25.5 %collective-permute-start.22 = (bf16[1,1536,384]{2,1,0:T(8,128)(2,1)}, bf16[1,1536,384]{2,1,0:T(8,128)(2,1)}, u32[]{:S(2)}, u32[]{:S(2)}) collective-permute-start(bf16[1,1536,384]{2,1,0:T(8,128)(2,1)} %ring_sum.16), channel_id=1, source_target_pairs={{0,8},{8,16},{16,24},{24,28},{28,20},{20,12},{12,4},{4,0},{9,1},{1... | collective-permute-start | bytes 3538952 | tf_op jit(solution)/shard_map/ppermute | solution.py:1075
  194.2 31.9 %collective-permute-start.28 = (bf16[1,1536,384]{2,1,0:T(8,128)(2,1)S(1)}, bf16[1,1536,384]{2,1,0:T(8,128)(2,1)}, u32[]{:S(2)}, u32[]{:S(2)}) collective-permute-start(bf16[1,1536,384]{2,1,0:T(8,128)(2,1)S(1)} %ring_sum.17), channel_id=1, source_target_pairs={{8,0},{16,8},{24,16},{28,24},{20,28},{12,20},{4,12},{0,4},{1,9},{9... | collective-permute-start | bytes 3538952 | tf_op jit(solution)/shard_map/ppermute | solution.py:1075
  212.0 33.1 %collective-permute-start.27 = (bf16[1,1536,384]{2,1,0:T(8,128)(2,1)}, bf16[1,1536,384]{2,1,0:T(8,128)(2,1)S(1)}, u32[]{:S(2)}, u32[]{:S(2)}) collective-permute-start(bf16[1,1536,384]{2,1,0:T(8,128)(2,1)} %ring_sum.18), channel_id=1, source_target_pairs={{0,8},{8,16},{16,24},{24,28},{28,20},{20,12},{12,4},{4,0},{9,1},{1... | collective-permute-start | bytes 3538952 | tf_op jit(solution)/shard_map/ppermute | solution.py:1075
  229.9 27.2 %collective-permute-start.29 = (bf16[1,1536,384]{2,1,0:T(8,128)(2,1)}, bf16[1,1536,384]{2,1,0:T(8,128)(2,1)S(1)}, u32[]{:S(2)}, u32[]{:S(2)}) collective-permute-start(bf16[1,1536,384]{2,1,0:T(8,128)(2,1)} %ring_sum.19), channel_id=1, source_target_pairs={{8,0},{16,8},{24,16},{28,24},{20,28},{12,20},{4,12},{0,4},{1,9},{9... | collective-permute-start | bytes 3538952 | tf_op jit(solution)/shard_map/ppermute | solution.py:1075
  247.3 21.6 %collective-permute-start.31 = (bf16[1,1536,384]{2,1,0:T(8,128)(2,1)}, bf16[1,1536,384]{2,1,0:T(8,128)(2,1)}, u32[]{:S(2)}, u32[]{:S(2)}) collective-permute-start(bf16[1,1536,384]{2,1,0:T(8,128)(2,1)} %ring_sum.20), channel_id=1, source_target_pairs={{0,8},{8,16},{16,24},{24,28},{28,20},{20,12},{12,4},{4,0},{9,1},{1... | collective-permute-start | bytes 3538952 | tf_op jit(solution)/shard_map/ppermute | solution.py:1075
  248.8 39.8 %collective-permute-start.36 = (bf16[1024,768]{1,0:T(8,128)(2,1)}, bf16[1024,768]{1,0:T(8,128)(2,1)S(1)}, u32[]{:S(2)}, u32[]{:S(2)}) collective-permute-start(bf16[1024,768]{1,0:T(8,128)(2,1)} %get-tuple-element.277), channel_id=1, source_target_pairs={{0,2},{2,0},{1,3},{3,1},{4,6},{6,4},{5,7},{7,5},{8,10},{10,8},{9,1... | collective-permute-start | bytes 4718600 | tf_op jit(solution)/shard_map/ppermute | solution.py:51
  257.5 23.6 %collective-permute-start.30 = (bf16[1,1536,384]{2,1,0:T(8,128)(2,1)S(1)}, bf16[1,1536,384]{2,1,0:T(8,128)(2,1)S(1)}, u32[]{:S(2)}, u32[]{:S(2)}) collective-permute-start(bf16[1,1536,384]{2,1,0:T(8,128)(2,1)S(1)} %ring_sum.21), channel_id=1, source_target_pairs={{8,0},{16,8},{24,16},{28,24},{20,28},{12,20},{4,12},{0,4},{1,9},{9... | collective-permute-start | bytes 3538952 | tf_op jit(solution)/shard_map/ppermute | solution.py:1075
  271.3 24.5 %collective-permute-start.35 = (bf16[1,1536,384]{2,1,0:T(8,128)(2,1)S(1)}, bf16[1,1536,384]{2,1,0:T(8,128)(2,1)S(1)}, u32[]{:S(2)}, u32[]{:S(2)}) collective-permute-start(bf16[1,1536,384]{2,1,0:T(8,128)(2,1)S(1)} %ring_sum.22), channel_id=1, source_target_pairs={{0,8},{8,16},{16,24},{24,28},{28,20},{20,12},{12,4},{4,0},{9,1},{1... | collective-permute-start | bytes 3538952 | tf_op jit(solution)/shard_map/ppermute | solution.py:1075
  282.9 30.5 %collective-permute-start.34 = (bf16[1,1536,384]{2,1,0:T(8,128)(2,1)}, bf16[1,1536,384]{2,1,0:T(8,128)(2,1)}, u32[]{:S(2)}, u32[]{:S(2)}) collective-permute-start(bf16[1,1536,384]{2,1,0:T(8,128)(2,1)} %ring_sum.23), channel_id=1, source_target_pairs={{8,0},{16,8},{24,16},{28,24},{20,28},{12,20},{4,12},{0,4},{1,9},{9... | collective-permute-start | bytes 3538952 | tf_op jit(solution)/shard_map/ppermute | solution.py:1075
  297.4 34.9 %collective-permute-start.43 = (bf16[1,1536,384]{2,1,0:T(8,128)(2,1)}, bf16[1,1536,384]{2,1,0:T(8,128)(2,1)}, u32[]{:S(2)}, u32[]{:S(2)}) collective-permute-start(bf16[1,1536,384]{2,1,0:T(8,128)(2,1)} %ring_sum.24), channel_id=1, source_target_pairs={{0,8},{8,16},{16,24},{24,28},{28,20},{20,12},{12,4},{4,0},{9,1},{1... | collective-permute-start | bytes 3538952 | tf_op jit(solution)/shard_map/ppermute | solution.py:1075
  315.6 21.6 %collective-permute-start.42 = (bf16[1,1536,384]{2,1,0:T(8,128)(2,1)S(1)}, bf16[1,1536,384]{2,1,0:T(8,128)(2,1)S(1)}, u32[]{:S(2)}, u32[]{:S(2)}) collective-permute-start(bf16[1,1536,384]{2,1,0:T(8,128)(2,1)S(1)} %ring_sum.25), channel_id=1, source_target_pairs={{8,0},{16,8},{24,16},{28,24},{20,28},{12,20},{4,12},{0,4},{1,9},{9... | collective-permute-start | bytes 3538952 | tf_op jit(solution)/shard_map/ppermute | solution.py:1075
  338.5 18.0 %collective-permute-start.47 = (bf16[768,384]{1,0:T(8,128)(2,1)S(1)}, bf16[768,384]{1,0:T(8,128)(2,1)S(1)}, u32[]{:S(2)}, u32[]{:S(2)}) collective-permute-start(bf16[768,384]{1,0:T(8,128)(2,1)S(1)} %bitcast.46), channel_id=1, source_target_pairs={{8,0},{16,8},{24,16},{28,24},{20,28},{12,20},{4,12},{0,4},{1,9},{9... | collective-permute-start | bytes 1769480 | tf_op jit(solution)/shard_map/ppermute | solution.py:1075
  356.4 16.6 %collective-permute-start.50 = (bf16[768,384]{1,0:T(8,128)(2,1)S(1)}, bf16[768,384]{1,0:T(8,128)(2,1)S(1)}, u32[]{:S(2)}, u32[]{:S(2)}) collective-permute-start(bf16[768,384]{1,0:T(8,128)(2,1)S(1)} %collective-permute-done.47.refs_1_), channel_id=1, source_target_pairs={{8,0},{16,8},{24,16},{28,24},{20,28},{12,20},{4,12},{0,4},{1,9},{9... | collective-permute-start | bytes 1769480 | tf_op jit(solution)/shard_map/ppermute | solution.py:1075
  366.8 17.8 %collective-permute-start.49 = (bf16[768,384]{1,0:T(8,128)(2,1)S(1)}, bf16[768,384]{1,0:T(8,128)(2,1)S(1)}, u32[]{:S(2)}, u32[]{:S(2)}) collective-permute-start(bf16[768,384]{1,0:T(8,128)(2,1)S(1)} %collective-permute-done.46.refs_0_), channel_id=1, source_target_pairs={{0,8},{8,16},{16,24},{24,28},{28,20},{20,12},{12,4},{4,0},{9,1},{1... | collective-permute-start | bytes 1769480 | tf_op jit(solution)/shard_map/ppermute | solution.py:1075
  373.0 20.1 %collective-permute-start.53 = (bf16[768,384]{1,0:T(8,128)(2,1)S(1)}, bf16[768,384]{1,0:T(8,128)(2,1)S(1)}, u32[]{:S(2)}, u32[]{:S(2)}) collective-permute-start(bf16[768,384]{1,0:T(8,128)(2,1)S(1)} %collective-permute-done.50.refs_1_), channel_id=1, source_target_pairs={{8,0},{16,8},{24,16},{28,24},{20,28},{12,20},{4,12},{0,4},{1,9},{9... | collective-permute-start | bytes 1769480 | tf_op jit(solution)/shard_map/ppermute | solution.py:1075
  373.6 18.9 %collective-permute-start.54 = (bf16[480,384]{1,0:T(8,128)(2,1)S(1)}, bf16[480,384]{1,0:T(8,128)(2,1)S(1)}, u32[]{:S(2)}, u32[]{:S(2)}) collective-permute-start(bf16[480,384]{1,0:T(8,128)(2,1)S(1)} %late_chunk.18), channel_id=1, source_target_pairs={{0,8},{8,16},{16,24},{24,28},{28,20},{20,12},{12,4},{4,0},{9,1},{1... | collective-permute-start | bytes 1105928 | tf_op jit(solution)/shard_map/ppermute | solution.py:1075
  375.7 22.1 %collective-permute-start.70 = (bf16[480,384]{1,0:T(8,128)(2,1)S(1)}, bf16[480,384]{1,0:T(8,128)(2,1)S(1)}, u32[]{:S(2)}, u32[]{:S(2)}) collective-permute-start(bf16[480,384]{1,0:T(8,128)(2,1)S(1)} %late_chunk.24), channel_id=1, source_target_pairs={{8,0},{16,8},{24,16},{28,24},{20,28},{12,20},{4,12},{0,4},{1,9},{9... | collective-permute-start | bytes 1105928 | tf_op jit(solution)/shard_map/ppermute | solution.py:1075
  397.8 60.7 %collective-permute-start.78 = (bf16[1024,768]{1,0:T(8,128)(2,1)}, bf16[1024,768]{1,0:T(8,128)(2,1)}, u32[]{:S(2)}, u32[]{:S(2)}) collective-permute-start(bf16[1024,768]{1,0:T(8,128)(2,1)} %convolution_convert_fusion), channel_id=1, source_target_pairs={{0,1},{1,0},{2,3},{3,2},{4,5},{5,4},{6,7},{7,6},{8,9},{9,8},{10,11... | collective-permute-start | bytes 4718600 | tf_op jit(solution)/shard_map/ppermute | solution.py:51
  400.5 23.3 %collective-permute-start.56 = (bf16[768,384]{1,0:T(8,128)(2,1)S(1)}, bf16[768,384]{1,0:T(8,128)(2,1)}, u32[]{:S(2)}, u32[]{:S(2)}) collective-permute-start(bf16[768,384]{1,0:T(8,128)(2,1)S(1)} %collective-permute-done.53.refs_1_), channel_id=1, source_target_pairs={{8,0},{16,8},{24,16},{28,24},{20,28},{12,20},{4,12},{0,4},{1,9},{9... | collective-permute-start | bytes 1769480 | tf_op jit(solution)/shard_map/ppermute | solution.py:1075
  401.0 22.1 %collective-permute-start.57 = (bf16[480,384]{1,0:T(8,128)(2,1)S(1)}, bf16[480,384]{1,0:T(8,128)(2,1)S(1)}, u32[]{:S(2)}, u32[]{:S(2)}) collective-permute-start(bf16[480,384]{1,0:T(8,128)(2,1)S(1)} %late_chunk.19), channel_id=1, source_target_pairs={{0,8},{8,16},{16,24},{24,28},{28,20},{20,12},{12,4},{4,0},{9,1},{1... | collective-permute-start | bytes 1105928 | tf_op jit(solution)/shard_map/ppermute | solution.py:1075
  410.7 19.3 %collective-permute-start.72 = (bf16[480,384]{1,0:T(8,128)(2,1)}, bf16[480,384]{1,0:T(8,128)(2,1)}, u32[]{:S(2)}, u32[]{:S(2)}) collective-permute-start(bf16[480,384]{1,0:T(8,128)(2,1)} %late_chunk.26), channel_id=1, source_target_pairs={{8,0},{16,8},{24,16},{28,24},{20,28},{12,20},{4,12},{0,4},{1,9},{9... | collective-permute-start | bytes 1105928 | tf_op jit(solution)/shard_map/ppermute | solution.py:1075
  415.3 37.7 %collective-permute-start.55 = (bf16[768,384]{1,0:T(8,128)(2,1)}, bf16[768,384]{1,0:T(8,128)(2,1)}, u32[]{:S(2)}, u32[]{:S(2)}) collective-permute-start(bf16[768,384]{1,0:T(8,128)(2,1)} %collective-permute-done.52.refs_0_), channel_id=1, source_target_pairs={{0,8},{8,16},{16,24},{24,28},{28,20},{20,12},{12,4},{4,0},{9,1},{1... | collective-permute-start | bytes 1769480 | tf_op jit(solution)/shard_map/ppermute | solution.py:1075
  423.8 33.9 %collective-permute-start.59 = (bf16[768,384]{1,0:T(8,128)(2,1)}, bf16[768,384]{1,0:T(8,128)(2,1)}, u32[]{:S(2)}, u32[]{:S(2)}) collective-permute-start(bf16[768,384]{1,0:T(8,128)(2,1)} %collective-permute-done.56.refs_1_), channel_id=1, source_target_pairs={{8,0},{16,8},{24,16},{28,24},{20,28},{12,20},{4,12},{0,4},{1,9},{9... | collective-permute-start | bytes 1769480 | tf_op jit(solution)/shard_map/ppermute | solution.py:1075
  432.8 21.8 %collective-permute-start.60 = (bf16[480,384]{1,0:T(8,128)(2,1)S(1)}, bf16[480,384]{1,0:T(8,128)(2,1)}, u32[]{:S(2)}, u32[]{:S(2)}) collective-permute-start(bf16[480,384]{1,0:T(8,128)(2,1)S(1)} %late_chunk.20), channel_id=1, source_target_pairs={{0,8},{8,16},{16,24},{24,28},{28,20},{20,12},{12,4},{4,0},{9,1},{1... | collective-permute-start | bytes 1105928 | tf_op jit(solution)/shard_map/ppermute | solution.py:1075
  453.0 22.6 %collective-permute-start.58 = (bf16[768,384]{1,0:T(8,128)(2,1)}, bf16[768,384]{1,0:T(8,128)(2,1)S(1)}, u32[]{:S(2)}, u32[]{:S(2)}) collective-permute-start(bf16[768,384]{1,0:T(8,128)(2,1)} %collective-permute-done.55.refs_0_), channel_id=1, source_target_pairs={{0,8},{8,16},{16,24},{24,28},{28,20},{20,12},{12,4},{4,0},{9,1},{1... | collective-permute-start | bytes 1769480 | tf_op jit(solution)/shard_map/ppermute | solution.py:1075
  456.2 19.4 %collective-permute-start.62 = (bf16[480,384]{1,0:T(8,128)(2,1)S(1)}, bf16[480,384]{1,0:T(8,128)(2,1)S(1)}, u32[]{:S(2)}, u32[]{:S(2)}) collective-permute-start(bf16[480,384]{1,0:T(8,128)(2,1)S(1)} %late_chunk.21), channel_id=1, source_target_pairs={{0,8},{8,16},{16,24},{24,28},{28,20},{20,12},{12,4},{4,0},{9,1},{1... | collective-permute-start | bytes 1105928 | tf_op jit(solution)/shard_map/ppermute | solution.py:1075
  457.7 23.1 %collective-permute-start.61 = (bf16[768,384]{1,0:T(8,128)(2,1)}, bf16[768,384]{1,0:T(8,128)(2,1)S(1)}, u32[]{:S(2)}, u32[]{:S(2)}) collective-permute-start(bf16[768,384]{1,0:T(8,128)(2,1)} %collective-permute-done.59.refs_1_), channel_id=1, source_target_pairs={{8,0},{16,8},{24,16},{28,24},{20,28},{12,20},{4,12},{0,4},{1,9},{9... | collective-permute-start | bytes 1769480 | tf_op jit(solution)/shard_map/ppermute | solution.py:1075
  462.4 32.3 %collective-permute-start.79 = (bf16[512,768]{1,0:T(8,128)(2,1)}, bf16[512,768]{1,0:T(8,128)(2,1)}, u32[]{:S(2)}, u32[]{:S(2)}) collective-permute-start(bf16[512,768]{1,0:T(8,128)(2,1)} %dynamic-slice_convert_fusion.1), channel_id=1, source_target_pairs={{0,2},{2,0},{1,3},{3,1},{4,6},{6,4},{5,7},{7,5},{8,10},{10,8},{9,1... | collective-permute-start | bytes 2359304 | tf_op jit(solution)/shard_map/ppermute | solution.py:51
  464.3 18.8 %collective-permute-start.75 = (bf16[480,384]{1,0:T(8,128)(2,1)S(1)}, bf16[480,384]{1,0:T(8,128)(2,1)S(1)}, u32[]{:S(2)}, u32[]{:S(2)}) collective-permute-start(bf16[480,384]{1,0:T(8,128)(2,1)S(1)} %late_chunk.29), channel_id=1, source_target_pairs={{8,0},{16,8},{24,16},{28,24},{20,28},{12,20},{4,12},{0,4},{1,9},{9... | collective-permute-start | bytes 1105928 | tf_op jit(solution)/shard_map/ppermute | solution.py:1075
  475.6 18.4 %collective-permute-start.64 = (bf16[1,768,384]{2,1,0:T(8,128)(2,1)}, bf16[1,768,384]{2,1,0:T(8,128)(2,1)}, u32[]{:S(2)}, u32[]{:S(2)}) collective-permute-start(bf16[1,768,384]{2,1,0:T(8,128)(2,1)} %get-tuple-element.346), channel_id=1, source_target_pairs={{0,1},{1,0},{2,3},{3,2},{4,5},{5,4},{6,7},{7,6},{8,9},{9,8},{10,11... | collective-permute-start | bytes 1769480 | tf_op jit(solution)/shard_map/ppermute | solution.py:51
  498.3 33.9 %collective-permute-start.63 = (bf16[768,384]{1,0:T(8,128)(2,1)}, bf16[768,384]{1,0:T(8,128)(2,1)S(1)}, u32[]{:S(2)}, u32[]{:S(2)}) collective-permute-start(bf16[768,384]{1,0:T(8,128)(2,1)} %bitcast.19.refs_0_), channel_id=1, source_target_pairs={{0,8},{8,16},{16,24},{24,28},{28,20},{20,12},{12,4},{4,0},{9,1},{1... | collective-permute-start | bytes 1769480 | tf_op jit(solution)/shard_map/ppermute | solution.py:1075
  500.3 26.5 %collective-permute-start.66 = (bf16[768,384]{1,0:T(8,128)(2,1)S(1)}, bf16[768,384]{1,0:T(8,128)(2,1)S(1)}, u32[]{:S(2)}, u32[]{:S(2)}) collective-permute-start(bf16[768,384]{1,0:T(8,128)(2,1)S(1)} %copy-done.57), channel_id=1, source_target_pairs={{0,8},{8,16},{16,24},{24,28},{28,20},{20,12},{12,4},{4,0},{9,1},{1... | collective-permute-start | bytes 1769480 | tf_op jit(solution)/shard_map/ppermute | solution.py:1075
  502.3 31.1 %collective-permute-start.69 = (bf16[768,384]{1,0:T(8,128)(2,1)}, bf16[768,384]{1,0:T(8,128)(2,1)S(1)}, u32[]{:S(2)}, u32[]{:S(2)}) collective-permute-start(bf16[768,384]{1,0:T(8,128)(2,1)} %bitcast.22.refs_1_), channel_id=1, source_target_pairs={{8,0},{16,8},{24,16},{28,24},{20,28},{12,20},{4,12},{0,4},{1,9},{9... | collective-permute-start | bytes 1769480 | tf_op jit(solution)/shard_map/ppermute | solution.py:1075
  502.5 31.0 %collective-permute-start.81 = (bf16[480,384]{1,0:T(8,128)(2,1)S(1)}, bf16[480,384]{1,0:T(8,128)(2,1)S(1)}, u32[]{:S(2)}, u32[]{:S(2)}) collective-permute-start(bf16[480,384]{1,0:T(8,128)(2,1)S(1)} %late_join.2.refs_0_), channel_id=1, source_target_pairs={{0,8},{8,16},{16,24},{24,28},{28,20},{20,12},{12,4},{4,0},{9,1},{1... | collective-permute-start | bytes 1105928 | tf_op jit(solution)/shard_map/ppermute | solution.py:1075
  549.8 19.5 %collective-permute-start.91 = (bf16[768,384]{1,0:T(8,128)(2,1)S(1)}, bf16[768,384]{1,0:T(8,128)(2,1)S(1)}, u32[]{:S(2)}, u32[]{:S(2)}) collective-permute-start(bf16[768,384]{1,0:T(8,128)(2,1)S(1)} %collective-permute-done.82.refs_1_), channel_id=1, source_target_pairs={{8,0},{16,8},{24,16},{28,24},{20,28},{12,20},{4,12},{0,4},{1,9},{9... | collective-permute-start | bytes 1769480 | tf_op jit(solution)/shard_map/ppermute | solution.py:1075
  551.5 71.8 %collective-permute-start.84 = (bf16[1024,768]{1,0:T(8,128)(2,1)S(1)}, bf16[1024,768]{1,0:T(8,128)(2,1)S(1)}, u32[]{:S(2)}, u32[]{:S(2)}) collective-permute-start(bf16[1024,768]{1,0:T(8,128)(2,1)S(1)} %copy-done.45), channel_id=1, source_target_pairs={{0,1},{1,0},{2,3},{3,2},{4,5},{5,4},{6,7},{7,6},{8,9},{9,8},{10,11... | collective-permute-start | bytes 4718600 | tf_op jit(solution)/shard_map/ppermute | solution.py:51
  551.5 17.8 %collective-permute-start.87 = (bf16[480,384]{1,0:T(8,128)(2,1)S(1)}, bf16[480,384]{1,0:T(8,128)(2,1)S(1)}, u32[]{:S(2)}, u32[]{:S(2)}) collective-permute-start(bf16[480,384]{1,0:T(8,128)(2,1)S(1)} %collective-permute-done.83.refs_2_), channel_id=1, source_target_pairs={{0,8},{8,16},{16,24},{24,28},{28,20},{20,12},{12,4},{4,0},{9,1},{1... | collective-permute-start | bytes 1105928 | tf_op jit(solution)/shard_map/ppermute | solution.py:1075
  551.9 22.1 %collective-permute-start.103 = (bf16[480,384]{1,0:T(8,128)(2,1)S(1)}, bf16[480,384]{1,0:T(8,128)(2,1)S(1)}, u32[]{:S(2)}, u32[]{:S(2)}) collective-permute-start(bf16[480,384]{1,0:T(8,128)(2,1)S(1)} %late_join.3.refs_8_), channel_id=1, source_target_pairs={{8,0},{16,8},{24,16},{28,24},{20,28},{12,20},{4,12},{0,4},{1,9},{9... | collective-permute-start | bytes 1105928 | tf_op jit(solution)/shard_map/ppermute | solution.py:1075
  561.3 31.9 %collective-permute-start.90 = (bf16[768,384]{1,0:T(8,128)(2,1)S(1)}, bf16[768,384]{1,0:T(8,128)(2,1)S(1)}, u32[]{:S(2)}, u32[]{:S(2)}) collective-permute-start(bf16[768,384]{1,0:T(8,128)(2,1)S(1)} %collective-permute-done.88.refs_0_), channel_id=1, source_target_pairs={{0,8},{8,16},{16,24},{24,28},{28,20},{20,12},{12,4},{4,0},{9,1},{1... | collective-permute-start | bytes 1769480 | tf_op jit(solution)/shard_map/ppermute | solution.py:1075
  569.2 24.9 %collective-permute-start.94 = (bf16[768,384]{1,0:T(8,128)(2,1)S(1)}, bf16[768,384]{1,0:T(8,128)(2,1)S(1)}, u32[]{:S(2)}, u32[]{:S(2)}) collective-permute-start(bf16[768,384]{1,0:T(8,128)(2,1)S(1)} %collective-permute-done.91.refs_1_), channel_id=1, source_target_pairs={{8,0},{16,8},{24,16},{28,24},{20,28},{12,20},{4,12},{0,4},{1,9},{9... | collective-permute-start | bytes 1769480 | tf_op jit(solution)/shard_map/ppermute | solution.py:1075
  575.6 18.5 %collective-permute-start.89 = (bf16[480,384]{1,0:T(8,128)(2,1)S(1)}, bf16[480,384]{1,0:T(8,128)(2,1)S(1)}, u32[]{:S(2)}, u32[]{:S(2)}) collective-permute-start(bf16[480,384]{1,0:T(8,128)(2,1)S(1)} %collective-permute-done.87.refs_3_), channel_id=1, source_target_pairs={{0,8},{8,16},{16,24},{24,28},{28,20},{20,12},{12,4},{4,0},{9,1},{1... | collective-permute-start | bytes 1105928 | tf_op jit(solution)/shard_map/ppermute | solution.py:1075
  593.2 28.1 %collective-permute-start.93 = (bf16[768,384]{1,0:T(8,128)(2,1)S(1)}, bf16[768,384]{1,0:T(8,128)(2,1)S(1)}, u32[]{:S(2)}, u32[]{:S(2)}) collective-permute-start(bf16[768,384]{1,0:T(8,128)(2,1)S(1)} %collective-permute-done.90.refs_0_), channel_id=1, source_target_pairs={{0,8},{8,16},{16,24},{24,28},{28,20},{20,12},{12,4},{4,0},{9,1},{1... | collective-permute-start | bytes 1769480 | tf_op jit(solution)/shard_map/ppermute | solution.py:1075
  594.1 28.1 %collective-permute-start.97 = (bf16[768,384]{1,0:T(8,128)(2,1)S(1)}, bf16[768,384]{1,0:T(8,128)(2,1)S(1)}, u32[]{:S(2)}, u32[]{:S(2)}) collective-permute-start(bf16[768,384]{1,0:T(8,128)(2,1)S(1)} %collective-permute-done.94.refs_1_), channel_id=1, source_target_pairs={{8,0},{16,8},{24,16},{28,24},{20,28},{12,20},{4,12},{0,4},{1,9},{9... | collective-permute-start | bytes 1769480 | tf_op jit(solution)/shard_map/ppermute | solution.py:1075
  598.3 19.7 %collective-permute-start.106 = (bf16[480,384]{1,0:T(8,128)(2,1)S(1)}, bf16[480,384]{1,0:T(8,128)(2,1)S(1)}, u32[]{:S(2)}, u32[]{:S(2)}) collective-permute-start(bf16[480,384]{1,0:T(8,128)(2,1)S(1)} %collective-permute-done.105.refs_11_), channel_id=1, source_target_pairs={{8,0},{16,8},{24,16},{28,24},{20,28},{12,20},{4,12},{0,4},{1,9},{9... | collective-permute-start | bytes 1105928 | tf_op jit(solution)/shard_map/ppermute | solution.py:1075
  600.1 22.1 %collective-permute-start.92 = (bf16[480,384]{1,0:T(8,128)(2,1)S(1)}, bf16[480,384]{1,0:T(8,128)(2,1)S(1)}, u32[]{:S(2)}, u32[]{:S(2)}) collective-permute-start(bf16[480,384]{1,0:T(8,128)(2,1)S(1)} %collective-permute-done.89.refs_4_), channel_id=1, source_target_pairs={{0,8},{8,16},{16,24},{24,28},{28,20},{20,12},{12,4},{4,0},{9,1},{1... | collective-permute-start | bytes 1105928 | tf_op jit(solution)/shard_map/ppermute | solution.py:1075
  622.2 24.2 %collective-permute-start.100 = (bf16[768,384]{1,0:T(8,128)(2,1)S(1)}, bf16[768,384]{1,0:T(8,128)(2,1)S(1)}, u32[]{:S(2)}, u32[]{:S(2)}) collective-permute-start(bf16[768,384]{1,0:T(8,128)(2,1)S(1)} %collective-permute-done.97.refs_1_), channel_id=1, source_target_pairs={{8,0},{16,8},{24,16},{28,24},{20,28},{12,20},{4,12},{0,4},{1,9},{9... | collective-permute-start | bytes 1769480 | tf_op jit(solution)/shard_map/ppermute | solution.py:1075
  623.8 21.2 %collective-permute-start.95 = (bf16[480,384]{1,0:T(8,128)(2,1)S(1)}, bf16[480,384]{1,0:T(8,128)(2,1)S(1)}, u32[]{:S(2)}, u32[]{:S(2)}) collective-permute-start(bf16[480,384]{1,0:T(8,128)(2,1)S(1)} %collective-permute-done.92.refs_5_), channel_id=1, source_target_pairs={{0,8},{8,16},{16,24},{24,28},{28,20},{20,12},{12,4},{4,0},{9,1},{1... | collective-permute-start | bytes 1105928 | tf_op jit(solution)/shard_map/ppermute | solution.py:1075
  624.8 27.2 %collective-permute-start.85 = (bf16[512,768]{1,0:T(8,128)(2,1)S(1)}, bf16[512,768]{1,0:T(8,128)(2,1)S(1)}, u32[]{:S(2)}, u32[]{:S(2)}) collective-permute-start(bf16[512,768]{1,0:T(8,128)(2,1)S(1)} %dynamic-slice_convert_fusion), channel_id=1, source_target_pairs={{0,2},{2,0},{1,3},{3,1},{4,6},{6,4},{5,7},{7,5},{8,10},{10,8},{9,1... | collective-permute-start | bytes 2359304 | tf_op jit(solution)/shard_map/ppermute | solution.py:51
  627.3 21.2 %collective-permute-start.108 = (bf16[480,384]{1,0:T(8,128)(2,1)S(1)}, bf16[480,384]{1,0:T(8,128)(2,1)S(1)}, u32[]{:S(2)}, u32[]{:S(2)}) collective-permute-start(bf16[480,384]{1,0:T(8,128)(2,1)S(1)} %collective-permute-done.107.refs_13_), channel_id=1, source_target_pairs={{8,0},{16,8},{24,16},{28,24},{20,28},{12,20},{4,12},{0,4},{1,9},{9... | collective-permute-start | bytes 1105928 | tf_op jit(solution)/shard_map/ppermute | solution.py:1075
  647.0 20.9 %collective-permute-start.98 = (bf16[480,384]{1,0:T(8,128)(2,1)S(1)}, bf16[480,384]{1,0:T(8,128)(2,1)S(1)}, u32[]{:S(2)}, u32[]{:S(2)}) collective-permute-start(bf16[480,384]{1,0:T(8,128)(2,1)S(1)} %collective-permute-done.95.refs_6_), channel_id=1, source_target_pairs={{0,8},{8,16},{16,24},{24,28},{28,20},{20,12},{12,4},{4,0},{9,1},{1... | collective-permute-start | bytes 1105928 | tf_op jit(solution)/shard_map/ppermute | solution.py:1075
  648.4 19.2 %collective-permute-start.109 = (bf16[480,384]{1,0:T(8,128)(2,1)S(1)}, bf16[480,384]{1,0:T(8,128)(2,1)S(1)}, u32[]{:S(2)}, u32[]{:S(2)}) collective-permute-start(bf16[480,384]{1,0:T(8,128)(2,1)S(1)} %collective-permute-done.108.refs_14_), channel_id=1, source_target_pairs={{8,0},{16,8},{24,16},{28,24},{20,28},{12,20},{4,12},{0,4},{1,9},{9... | collective-permute-start | bytes 1105928 | tf_op jit(solution)/shard_map/ppermute | solution.py:1075
  (144 other events, 1254.4 us)

commit v15 on v14

--- a/solution.py
+++ b/solution.py
@@ -1316,9 +1316,9 @@
         tokens_back = dot_nt(qkv_grad, here) + swap(
             dot_nt(qkv_grad, there).astype(BF16), "col"
         ).astype(F32)
-        tokens_back = my_rows(tokens_back) + swap(
-            their_rows(tokens_back).astype(BF16), "row"
-        ).astype(F32)
+        came = swap(their_rows(tokens_back).astype(BF16), "row")
+        normed["tokens_came"] = came
+        tokens_back = my_rows(tokens_back) + came.astype(F32)
         scale_attn = near[3]
         tokens_f32 = tokens_in.astype(F32)
         gain_attn_part = jnp.sum(tokens_back * tokens_f32 * scale_attn, axis=0)
@@ -1364,7 +1364,7 @@
     for number, (wave, step) in enumerate(moves):
         if step == 0:
             came = list(got)
-            got = list(waves[wave])
+            got = [after(waves[wave][k], came[k]) if wave else waves[wave][k] for k in range(2)]
         late_done += late_got is not None
         chunks = [None, None]
         for k in range(2):
@@ -1379,9 +1379,17 @@
         late_got = [send(late[k], k) for k in range(2)] if late_done < late_total else None
         if wave and step == 0:
             placed = unpack(plan, experts + 2 * (ring_size - 1), 0, came, shapes, placed)
+        ties = {
+            1: [*waves[1], *late],
+            5: [normed.get("tokens_came")],
+            6: [normed.get("gains")],
+            7: late,
+            8: late,
+        }
+        chunks = [after(chunks[0], *ties.get(number, ())), chunks[1]]
         placed = unpack(plan, experts + 2 * step, wave, chunks, shapes, placed)
         last = placed[0:1]
-        if number == 3:
+        if number == 2:
             back_to_tokens(last)
         if number == 9:
             block_rows(last)

time: 684 us -> 681 us (level)
  waiting for transfers between devices: 246 us -> 238 us
    ppermute x70, waiting for transfers between devices: 209 us -> 199 us  [send(): return lax.ppermute(values, ('dp', 'col'), routes_of[which])]
    unnamed x196 -> x188, local copies, waits for them, and re-layouts: 27.2 us -> 25.9 us
  transfers between devices with their start and end apart: 110 -> 110, of which waited for: 44 -> 45; matrix products, arithmetic and copies ran while one was open for 3% -> 2% of each run, Pallas kernels for 39% -> 40%
where the time goes in v15:
time: 681 us; the launch traced here: 671 us
  Pallas kernels  283 us (42%)
  waiting for transfers between devices  238 us (35%)
  starting transfers between devices  103 us (15%)
  local copies, waits for them, and re-layouts  28.4 us (4%)
  other arithmetic  10 us (1%)
    ppermute x70, waiting for transfers between devices, send(): return lax.ppermute(values, ('dp', 'col'), routes_of[which])  199 us
    ppermute x70, starting transfers between devices, send(): return lax.ppermute(values, ('dp', 'col'), routes_of[which])  77.8 us
    pallas_call x6, Pallas kernels, expert_grads(): pl.pallas_call(functools.partial(expert_kernel, shared, aliased, first),...  72.1 us
    pallas_call x4, Pallas kernels, mix(): pl.pallas_call(functools.partial(mix_kernel, back, group, pieces), grid_s...  40.3 us
    pallas_call x16, Pallas kernels, unpack(): pl.pallas_call(functools.partial(unpack_kernel, aliased), grid_spec=pltpu...  40.1 us
    ppermute x37, waiting for transfers between devices, swap(): return lax.ppermute(values, axis, [(0, 1), (1, 0)])  37.3 us
    pallas_call x14, Pallas kernels, ring_sum(): pl.pallas_call(ring_sum_kernel, grid=(count, tiles), in_specs=[spec, term...  30.3 us
    unnamed x188, local copies, waits for them, and re-layouts  25.9 us
  transfers between devices with their start and end apart: 110, of which 45 were waited for; matrix products, arithmetic and copies ran while one was open for 2% of the time, Pallas kernels for 40%

profile of v15, /device:TPU:0, one launch (start us, length us, event | category | flops | bytes accessed | tf_op | source)
XLA Modules:
  0.0 671.1 jit_solution(5206583370451207368)
XLA Ops:
  1.8 3.1 their_columns.1
  5.4 2.6 collective-permute-start
  8.2 5.0 collective-permute-done.2.gains_c_ref.refs_7_
  13.3 2.9 collective-permute-start.4
  18.0 4.5 project.2
  22.5 9.9 %collective-permute-done.4.refs_0_ = bf16[192,768]{1,0:T(8,128)(2,1)S(1)} collective-permute-done((bf16[192,768]{1,0:T(8,128)(2,1)}, bf16[192,768]{1,0:T(8,128)(2,1)S(1)}, u32[]{:S(2)}, u32[]{:S(2)}) %collective-permute-start.4) | collective-permute-done | bytes 294944 | tf_op jit(solution)/shard_map/ppermute | solution.py:51
  40.8 4.5 project.3
  50.7 5.0 collective-permute-done.5.refs_1_
  57.5 6.2 attend.1.refs_4_.refs_5_
  69.5 9.0 %hidden_before.1 = (f32[1024,768]{1,0:T(8,128)}, f32[1024,768]{1,0:T(8,128)}) custom-call(s32[3]{0:T(128)} %copy-done.66, bf16[512,768]{1,0:T(8,128)(2,1)} %refs_0_.2, bf16[512,768]{1,0:T(8,128)(2,1)} %copy-done.82, bf16[512,768]{1,0:T(8,128)(2,1)} %collective-permute-done.own_ref.refs_2_, bf16[512,768]{1,0:T(8,128)(2,1)} %copy-done.83, ...), custom_call_target="tpu_custom_call" | custom-call | flops 2415919104 | bytes 12582912 | tf_op jit(solution)/shard_map/hidden_before/pallas_call | solution.py:418
  78.5 5.6 collective-permute-done.12.refs_2_
  87.5 9.4 %hidden_after.1 = (f32[1024,768]{1,0:T(8,128)}, bf16[1024,768]{1,0:T(8,128)(2,1)}, bf16[1024,768]{1,0:T(8,128)(2,1)}, f32[1024,1]{1,0:T(8,128)}) custom-call(s32[3]{0:T(128)} %copy-done.66, f32[1024,768]{1,0:T(8,128)} %get-tuple-element.236.refs_0_, f32[1024,768]{1,0:T(8,128)} %get-tuple-element.237.refs_1_, ...), custom_call_target="tpu_custom_call" | custom-call | tf_op jit(solution)/shard_map/hidden_after/pallas_call | solution.py:440
  100.3 9.0 %expert_grads.6 = (bf16[1,1536,384]{2,1,0:T(8,128)(2,1)S(1)}, bf16[1,1536,384]{2,1,0:T(8,128)(2,1)S(1)}, bf16[8,1024,512]{2,1,0:T(8,128)(2,1)}, bf16[8,1024,256]{2,1,0:T(8,128)(2,1)S(1)}) custom-call(s32[63]{0:T(128)S(1)} %fusion.14.order_ref.plan_ref, bf16[1024,768]{1,0:T(8,128)(2,1)S(1)} %copy-done.8, bf16[1024,768]{1,0:T(8,128)(2,1)S(1)} %copy-done.9, ...), custom_call_target="tpu_custom_call" | custom-call | tf_op jit(solution)/shard_map/expert_grads/pallas_call | solution.py:563
  112.9 15.2 %expert_grads.7 = (bf16[2,1536,384]{2,1,0:T(8,128)(2,1)S(1)}, bf16[2,1536,384]{2,1,0:T(8,128)(2,1)S(1)}, bf16[8,1024,512]{2,1,0:T(8,128)(2,1)}, bf16[8,1024,256]{2,1,0:T(8,128)(2,1)}) custom-call(s32[63]{0:T(128)S(1)} %fusion.14.order_ref.plan_ref, bf16[1024,768]{1,0:T(8,128)(2,1)S(1)} %copy-done.8, ...), custom_call_target="tpu_custom_call", output_to_operand_aliasing={{2}: (18, {}), {3}: (19, {})} | custom-call | tf_op jit(solution)/shard_map/expert_grads/pallas_call | solution.py:563
  128.6 15.6 %expert_grads.8 = (bf16[2,1536,384]{2,1,0:T(8,128)(2,1)S(1)}, bf16[2,1536,384]{2,1,0:T(8,128)(2,1)S(1)}, bf16[8,1024,512]{2,1,0:T(8,128)(2,1)}, bf16[8,1024,256]{2,1,0:T(8,128)(2,1)}) custom-call(s32[63]{0:T(128)S(1)} %fusion.14.order_ref.plan_ref, bf16[1024,768]{1,0:T(8,128)(2,1)S(1)} %copy-done.8, ...), custom_call_target="tpu_custom_call", output_to_operand_aliasing={{2}: (18, {}), {3}: (19, {})} | custom-call | tf_op jit(solution)/shard_map/expert_grads/pallas_call | solution.py:563
  148.4 15.6 %expert_grads.9 = (bf16[2,1536,384]{2,1,0:T(8,128)(2,1)S(1)}, bf16[2,1536,384]{2,1,0:T(8,128)(2,1)S(1)}, bf16[8,1024,512]{2,1,0:T(8,128)(2,1)}, bf16[8,1024,256]{2,1,0:T(8,128)(2,1)}) custom-call(s32[63]{0:T(128)S(1)} %fusion.14.order_ref.plan_ref, bf16[1024,768]{1,0:T(8,128)(2,1)S(1)} %copy-done.8, ...), custom_call_target="tpu_custom_call", output_to_operand_aliasing={{2}: (18, {}), {3}: (19, {})} | custom-call | tf_op jit(solution)/shard_map/expert_grads/pallas_call | solution.py:563
  169.5 9.0 %expert_grads.10 = (bf16[1,1536,384]{2,1,0:T(8,128)(2,1)S(1)}, bf16[1,1536,384]{2,1,0:T(8,128)(2,1)S(1)}, bf16[8,1024,512]{2,1,0:T(8,128)(2,1)}, bf16[8,1024,256]{2,1,0:T(8,128)(2,1)S(1)}) custom-call(s32[63]{0:T(128)S(1)} %fusion.14.order_ref.plan_ref, bf16[1024,768]{1,0:T(8,128)(2,1)S(1)} %copy-done.8, ...), custom_call_target="tpu_custom_call", output_to_operand_aliasing={{2}: (18, {}), {3}: (19, {})} | custom-call | tf_op jit(solution)/shard_map/expert_grads/pallas_call | solution.py:563
  184.5 7.7 %expert_grads.11 = (bf16[1,1536,384]{2,1,0:T(8,128)(2,1)S(1)}, bf16[1,1536,384]{2,1,0:T(8,128)(2,1)S(1)}, bf16[1,1024,512]{2,1,0:T(8,128)(2,1)S(1)}, bf16[1,1024,256]{2,1,0:T(8,128)(2,1)S(1)}) custom-call(s32[63]{0:T(128)S(1)} %fusion.14.order_ref.plan_ref, bf16[1024,768]{1,0:T(8,128)(2,1)S(1)} %copy-done.8, bf16[1024,768]{1,0:T(8,128)(2,1)S(1)} %copy-done.10, ...), custom_call_target="tpu_custom_call" | custom-call | tf_op jit(solution)/shard_map/expert_grads/pallas_call | solution.py:563
  195.4 13.3 %mix.4 = (bf16[512,768]{1,0:T(8,128)(2,1)}, bf16[512,768]{1,0:T(8,128)(2,1)S(1)}) custom-call(s32[63]{0:T(128)S(1)} %fusion.14.order_ref.plan_ref, bf16[8,1024,512]{2,1,0:T(8,128)(2,1)} %get-tuple-element.262.refs_0_, bf16[1,1024,512]{2,1,0:T(8,128)(2,1)S(1)} %get-tuple-element.268.refs_1_, ...), custom_call_target="tpu_custom_call" | custom-call | tf_op jit(solution)/shard_map/mix/pallas_call | solution.py:636
  208.8 3.8 ring_sum.18
  214.1 12.5 %mix.5.own_ref = f32[1024,768]{1,0:T(8,128)S(1)} custom-call(s32[63]{0:T(128)S(1)} %fusion.14.order_ref.plan_ref, bf16[8,1024,512]{2,1,0:T(8,128)(2,1)} %get-tuple-element.262.refs_0_, bf16[1,1024,512]{2,1,0:T(8,128)(2,1)S(1)} %get-tuple-element.268.refs_1_, bf16[16,768,256]{2,1,0:T(8,128)(2,1)} %refs_16_.1, bf16[16,768,256]{2,1,0:T(8,128)(2,1)} %refs_17_.1, ...), custom_call_target="tpu_custom_call" | custom-call | tf_op jit(solution)/shard_map/mix/pallas_call | solution.py:636
  226.6 3.9 ring_sum.19
  231.5 7.3 %mix.6 = bf16[1024,768]{1,0:T(8,128)(2,1)S(1)} custom-call(s32[63]{0:T(128)S(1)} %fusion.14.order_ref.plan_ref, bf16[8,1024,256]{2,1,0:T(8,128)(2,1)} %copy-done.6, bf16[1,1024,256]{2,1,0:T(8,128)(2,1)S(1)} %get-tuple-element.280.refs_1_, ...), custom_call_target="tpu_custom_call" | custom-call | tf_op jit(solution)/shard_map/mix/pallas_call | solution.py:636
  244.0 3.5 chip_sum.1
  250.3 7.3 %mix.7 = f32[1024,768]{1,0:T(8,128)S(1)} custom-call(s32[63]{0:T(128)S(1)} %fusion.14.order_ref.plan_ref, bf16[8,1024,256]{2,1,0:T(8,128)(2,1)} %copy-done.6, bf16[1,1024,256]{2,1,0:T(8,128)(2,1)S(1)} %get-tuple-element.280.refs_1_, bf16[16,256,768]{2,1,0:T(8,128)(2,1)} %refs_9_.13, bf16[16,256,768]{2,1,0:T(8,128)(2,1)} %refs_9_.13, ...), custom_call_target="tpu_custom_call" | custom-call | tf_op jit(solution)/shard_map/mix/pallas_call | solution.py:636
  257.6 3.2 ring_sum.21
  265.3 22.2 %collective-permute-done.30.came_ref = bf16[1,1536,384]{2,1,0:T(8,128)(2,1)S(1)} collective-permute-done((bf16[1,1536,384]{2,1,0:T(8,128)(2,1)S(1)}, bf16[1,1536,384]{2,1,0:T(8,128)(2,1)S(1)}, u32[]{:S(2)}, u32[]{:S(2)}) %collective-permute-start.30) | collective-permute-done | bytes 1179680 | tf_op jit(solution)/shard_map/ppermute | solution.py:1075
  294.9 6.7 norm_back.1
  306.7 13.1 %attend_back.1.refs_4_ = bf16[1024,640]{1,0:T(8,128)(2,1)} custom-call(s32[3]{0:T(128)} %copy-done.66, bf16[512,640]{1,0:T(8,128)(2,1)} %get-tuple-element.228.own_ref, bf16[512,640]{1,0:T(8,128)(2,1)} %get-tuple-element.232.other_ref, bf16[512,768]{1,0:T(8,128)(2,1)} %copy-done.40, bf16[512,768]{1,0:T(8,128)(2,1)} %copy-done.41, ...), custom_call_target="tpu_custom_call" | custom-call | tf_op jit(solution)/shard_map/attend_back/pallas_call | solution.py:173
  322.5 16.2 %late_grads.1 = (bf16[8,480,384]{2,1,0:T(8,128)(2,1)}, bf16[8,480,384]{2,1,0:T(8,128)(2,1)}) custom-call(s32[3]{0:T(128)} %copy-done.66, bf16[512,768]{1,0:T(8,128)(2,1)} %get-tuple-element.299.refs_0_, bf16[512,768]{1,0:T(8,128)(2,1)} %get-tuple-element.300.refs_1_, bf16[512,768]{1,0:T(8,128)(2,1)} %get-tuple-element.301.refs_2_, ...), custom_call_target="tpu_custom_call" | custom-call | tf_op jit(solution)/shard_map/late_grads/pallas_call | solution.py:237
  338.8 2.6 ring_sum.26
  349.7 5.4 collective-permute-done.45.refs_0_
  357.2 5.8 collective-permute-done.48.refs_0_
  371.2 7.1 %collective-permute-done.46.refs_0_ = bf16[768,384]{1,0:T(8,128)(2,1)S(1)} collective-permute-done((bf16[768,384]{1,0:T(8,128)(2,1)S(1)}, bf16[768,384]{1,0:T(8,128)(2,1)S(1)}, u32[]{:S(2)}, u32[]{:S(2)}) %collective-permute-start.46) | collective-permute-done | bytes 589856 | tf_op jit(solution)/shard_map/ppermute | solution.py:1075
  378.2 3.9 collective-permute-done.53.refs_0_
  385.0 2.6 convolution_convert_fusion
  391.6 11.3 %collective-permute-done.51.refs_0_ = bf16[768,384]{1,0:T(8,128)(2,1)} collective-permute-done((bf16[768,384]{1,0:T(8,128)(2,1)S(1)}, bf16[768,384]{1,0:T(8,128)(2,1)}, u32[]{:S(2)}, u32[]{:S(2)}) %collective-permute-start.51) | collective-permute-done | bytes 589856 | tf_op jit(solution)/shard_map/ppermute | solution.py:1075
  405.4 5.3 collective-permute-done.56.refs_0_
  419.7 12.2 %collective-permute-done.72.refs_0_ = bf16[480,384]{1,0:T(8,128)(2,1)} collective-permute-done((bf16[480,384]{1,0:T(8,128)(2,1)S(1)}, bf16[480,384]{1,0:T(8,128)(2,1)}, u32[]{:S(2)}, u32[]{:S(2)}) %collective-permute-start.72) | collective-permute-done | bytes 368672 | tf_op jit(solution)/shard_map/ppermute | solution.py:1075
  435.2 3.6 unpack.19
  442.9 2.9 convert_add_fusion.1
  450.6 3.3 unpack.20
  454.3 6.6 collective-permute-done.64.refs_0_
  463.6 3.2 collective-permute-done.74.refs_0_
  469.9 3.6 unpack.21
  475.0 6.5 collective-permute-done.68.refs_0_
  495.2 3.3 unpack.22
  499.0 2.9 collective-permute-done.70.refs_0_
  509.6 3.3 unpack.24
  513.0 7.9 %collective-permute-done.69.refs_0_ = bf16[768,384]{1,0:T(8,128)(2,1)S(1)} collective-permute-done((bf16[768,384]{1,0:T(8,128)(2,1)}, bf16[768,384]{1,0:T(8,128)(2,1)S(1)}, u32[]{:S(2)}, u32[]{:S(2)}) %collective-permute-start.69) | collective-permute-done | bytes 589856 | tf_op jit(solution)/shard_map/ppermute | solution.py:1075
  521.5 3.7 collective-permute-done.81.refs_1_
  528.7 16.0 %collective-permute-done.82.refs_9_ = bf16[480,384]{1,0:T(8,128)(2,1)S(1)} collective-permute-done((bf16[480,384]{1,0:T(8,128)(2,1)S(1)}, bf16[480,384]{1,0:T(8,128)(2,1)S(1)}, u32[]{:S(2)}, u32[]{:S(2)}) %collective-permute-start.82) | collective-permute-done | bytes 368672 | tf_op jit(solution)/shard_map/ppermute | solution.py:1075
  551.9 10.1 %collective-permute-done.90.refs_0_ = bf16[768,384]{1,0:T(8,128)(2,1)S(1)} collective-permute-done((bf16[768,384]{1,0:T(8,128)(2,1)S(1)}, bf16[768,384]{1,0:T(8,128)(2,1)S(1)}, u32[]{:S(2)}, u32[]{:S(2)}) %collective-permute-start.90) | collective-permute-done | bytes 589856 | tf_op jit(solution)/shard_map/ppermute | solution.py:1075
  563.4 3.6 collective-permute-done.89.refs_3_
  570.6 16.7 %collective-permute-done.104.refs_10_ = bf16[480,384]{1,0:T(8,128)(2,1)S(1)} collective-permute-done((bf16[480,384]{1,0:T(8,128)(2,1)S(1)}, bf16[480,384]{1,0:T(8,128)(2,1)S(1)}, u32[]{:S(2)}, u32[]{:S(2)}) %collective-permute-start.104) | collective-permute-done | bytes 368672 | tf_op jit(solution)/shard_map/ppermute | solution.py:1075
  593.0 3.9 collective-permute-done.105.refs_11_
  598.9 16.4 %collective-permute-done.106.refs_12_ = bf16[480,384]{1,0:T(8,128)(2,1)S(1)} collective-permute-done((bf16[480,384]{1,0:T(8,128)(2,1)S(1)}, bf16[480,384]{1,0:T(8,128)(2,1)S(1)}, u32[]{:S(2)}, u32[]{:S(2)}) %collective-permute-start.106) | collective-permute-done | bytes 368672 | tf_op jit(solution)/shard_map/ppermute | solution.py:1075
  623.2 3.0 collective-permute-done.107.refs_13_
  628.2 7.1 %collective-permute-done.98.refs_0_ = bf16[768,384]{1,0:T(8,128)(2,1)S(1)} collective-permute-done((bf16[768,384]{1,0:T(8,128)(2,1)S(1)}, bf16[768,384]{1,0:T(8,128)(2,1)S(1)}, u32[]{:S(2)}, u32[]{:S(2)}) %collective-permute-start.98) | collective-permute-done | bytes 589856 | tf_op jit(solution)/shard_map/ppermute | solution.py:1075
  637.4 4.0 collective-permute-done.97.refs_6_
  646.2 2.7 fusion.4
  652.1 5.4 collective-permute-done.101.refs_0_
  660.7 3.3 collective-permute-done.109.refs_15_
  664.2 5.8 unpack_late.1
  (441 shorter events, 210.5 us)
Async XLA Ops:
  0.7 34.4 %collective-permute-start.16 = (bf16[16,768,256]{2,1,0:T(8,128)(2,1)}, bf16[16,768,256]{2,1,0:T(8,128)(2,1)}, u32[]{:S(2)}, u32[]{:S(2)}) collective-permute-start(bf16[16,768,256]{2,1,0:T(8,128)(2,1)} %refs_16_.1), channel_id=1, source_target_pairs={{0,1},{1,0},{2,3},{3,2},{4,5},{5,4},{6,7},{7,6},{8,9},{9,8},{10,11... | collective-permute-start | bytes 18874376 | tf_op jit(solution)/shard_map/ppermute | solution.py:51
  5.4 27.1 %collective-permute-start = (bf16[512,768]{1,0:T(8,128)(2,1)S(1)}, bf16[512,768]{1,0:T(8,128)(2,1)}, u32[]{:S(2)}, u32[]{:S(2)}) collective-permute-start(bf16[512,768]{1,0:T(8,128)(2,1)S(1)} %copy-done.70), channel_id=1, source_target_pairs={{0,2},{2,0},{1,3},{3,1},{4,6},{6,4},{5,7},{7,5},{8,10},{10,8},{9,1... | collective-permute-start | bytes 2359304 | tf_op jit(solution)/shard_map/ppermute | solution.py:51
  13.3 19.1 %collective-permute-start.4 = (bf16[192,768]{1,0:T(8,128)(2,1)}, bf16[192,768]{1,0:T(8,128)(2,1)S(1)}, u32[]{:S(2)}, u32[]{:S(2)}) collective-permute-start(bf16[192,768]{1,0:T(8,128)(2,1)} %get-tuple-element.229), channel_id=1, source_target_pairs={{0,2},{2,0},{1,3},{3,1},{4,6},{6,4},{5,7},{7,5},{8,10},{10,8},{9,1... | collective-permute-start | bytes 884744 | tf_op jit(solution)/shard_map/ppermute | solution.py:51
  34.9 62.0 %collective-permute-start.18 = (bf16[16,256,768]{2,1,0:T(8,128)(2,1)}, bf16[16,256,768]{2,1,0:T(8,128)(2,1)}, u32[]{:S(2)}, u32[]{:S(2)}) collective-permute-start(bf16[16,256,768]{2,1,0:T(8,128)(2,1)} %refs_9_.13), channel_id=1, source_target_pairs={{0,1},{1,0},{2,3},{3,2},{4,5},{5,4},{6,7},{7,6},{8,9},{9,8},{10,11... | collective-permute-start | bytes 18874376 | tf_op jit(solution)/shard_map/ppermute | solution.py:51
  35.8 61.1 %collective-permute-start.17 = (bf16[16,768,256]{2,1,0:T(8,128)(2,1)}, bf16[16,768,256]{2,1,0:T(8,128)(2,1)}, u32[]{:S(2)}, u32[]{:S(2)}) collective-permute-start(bf16[16,768,256]{2,1,0:T(8,128)(2,1)} %refs_17_.1), channel_id=1, source_target_pairs={{0,1},{1,0},{2,3},{3,2},{4,5},{5,4},{6,7},{7,6},{8,9},{9,8},{10,11... | collective-permute-start | bytes 18874376 | tf_op jit(solution)/shard_map/ppermute | solution.py:51
  35.9 19.8 %collective-permute-start.5 = (bf16[512,768]{1,0:T(8,128)(2,1)S(1)}, bf16[512,768]{1,0:T(8,128)(2,1)S(1)}, u32[]{:S(2)}, u32[]{:S(2)}) collective-permute-start(bf16[512,768]{1,0:T(8,128)(2,1)S(1)} %copy-done.56), channel_id=1, source_target_pairs={{0,2},{2,0},{1,3},{3,1},{4,6},{6,4},{5,7},{7,5},{8,10},{10,8},{9,1... | collective-permute-start | bytes 2359304 | tf_op jit(solution)/shard_map/ppermute | solution.py:51
  63.8 20.3 %collective-permute-start.12 = (bf16[1024,384]{1,0:T(8,128)(2,1)}, bf16[1024,384]{1,0:T(8,128)(2,1)}, u32[]{:S(2)}, u32[]{:S(2)}) collective-permute-start(bf16[1024,384]{1,0:T(8,128)(2,1)} %attend.1.refs_4_.refs_5_), channel_id=1, source_target_pairs={{0,2},{2,0},{1,3},{3,1},{4,6},{6,4},{5,7},{7,5},{8,10},{10,8},{9,1... | collective-permute-start | bytes 2359304 | tf_op jit(solution)/shard_map/ppermute | solution.py:51
  67.2 29.7 %collective-permute-start.15 = (bf16[1024,768]{1,0:T(8,128)(2,1)S(1)}, bf16[1024,768]{1,0:T(8,128)(2,1)S(1)}, u32[]{:S(2)}, u32[]{:S(2)}) collective-permute-start(bf16[1024,768]{1,0:T(8,128)(2,1)S(1)} %join.3.refs_2_.refs_4_), channel_id=1, source_target_pairs={{0,1},{1,0},{2,3},{3,2},{4,5},{5,4},{6,7},{7,6},{8,9},{9,8},{10,11... | collective-permute-start | bytes 4718600 | tf_op jit(solution)/shard_map/ppermute | solution.py:51
  111.3 32.9 %collective-permute-start.19 = (bf16[1,1536,384]{2,1,0:T(8,128)(2,1)S(1)}, bf16[1,1536,384]{2,1,0:T(8,128)(2,1)S(1)}, u32[]{:S(2)}, u32[]{:S(2)}) collective-permute-start(bf16[1,1536,384]{2,1,0:T(8,128)(2,1)S(1)} %get-tuple-element.244), channel_id=1, source_target_pairs={{0,8},{8,16},{16,24},{24,28},{28,20},{20,12},{12,4},{4,0},{9,1},{1... | collective-permute-start | bytes 3538952 | tf_op jit(solution)/shard_map/ppermute | solution.py:1075
  128.1 35.9 %collective-permute-start.21 = (bf16[1,1536,384]{2,1,0:T(8,128)(2,1)S(1)}, bf16[1,1536,384]{2,1,0:T(8,128)(2,1)S(1)}, u32[]{:S(2)}, u32[]{:S(2)}) collective-permute-start(bf16[1,1536,384]{2,1,0:T(8,128)(2,1)S(1)} %get-tuple-element.254), channel_id=1, source_target_pairs={{8,0},{16,8},{24,16},{28,24},{20,28},{12,20},{4,12},{0,4},{1,9},{9... | collective-permute-start | bytes 3538952 | tf_op jit(solution)/shard_map/ppermute | solution.py:1075
  146.9 33.6 %collective-permute-start.20 = (bf16[1,1536,384]{2,1,0:T(8,128)(2,1)}, bf16[1,1536,384]{2,1,0:T(8,128)(2,1)S(1)}, u32[]{:S(2)}, u32[]{:S(2)}) collective-permute-start(bf16[1,1536,384]{2,1,0:T(8,128)(2,1)} %ring_sum.14), channel_id=1, source_target_pairs={{0,8},{8,16},{16,24},{24,28},{28,20},{20,12},{12,4},{4,0},{9,1},{1... | collective-permute-start | bytes 3538952 | tf_op jit(solution)/shard_map/ppermute | solution.py:1075
  167.7 25.6 %collective-permute-start.23 = (bf16[1,1536,384]{2,1,0:T(8,128)(2,1)S(1)}, bf16[1,1536,384]{2,1,0:T(8,128)(2,1)S(1)}, u32[]{:S(2)}, u32[]{:S(2)}) collective-permute-start(bf16[1,1536,384]{2,1,0:T(8,128)(2,1)S(1)} %ring_sum.15), channel_id=1, source_target_pairs={{8,0},{16,8},{24,16},{28,24},{20,28},{12,20},{4,12},{0,4},{1,9},{9... | collective-permute-start | bytes 3538952 | tf_op jit(solution)/shard_map/ppermute | solution.py:1075
  182.9 25.9 %collective-permute-start.22 = (bf16[1,1536,384]{2,1,0:T(8,128)(2,1)}, bf16[1,1536,384]{2,1,0:T(8,128)(2,1)}, u32[]{:S(2)}, u32[]{:S(2)}) collective-permute-start(bf16[1,1536,384]{2,1,0:T(8,128)(2,1)} %ring_sum.16), channel_id=1, source_target_pairs={{0,8},{8,16},{16,24},{24,28},{28,20},{20,12},{12,4},{4,0},{9,1},{1... | collective-permute-start | bytes 3538952 | tf_op jit(solution)/shard_map/ppermute | solution.py:1075
  195.0 31.6 %collective-permute-start.28 = (bf16[1,1536,384]{2,1,0:T(8,128)(2,1)}, bf16[1,1536,384]{2,1,0:T(8,128)(2,1)}, u32[]{:S(2)}, u32[]{:S(2)}) collective-permute-start(bf16[1,1536,384]{2,1,0:T(8,128)(2,1)} %ring_sum.17), channel_id=1, source_target_pairs={{8,0},{16,8},{24,16},{28,24},{20,28},{12,20},{4,12},{0,4},{1,9},{9... | collective-permute-start | bytes 3538952 | tf_op jit(solution)/shard_map/ppermute | solution.py:1075
  212.5 26.3 %collective-permute-start.27 = (bf16[1,1536,384]{2,1,0:T(8,128)(2,1)}, bf16[1,1536,384]{2,1,0:T(8,128)(2,1)S(1)}, u32[]{:S(2)}, u32[]{:S(2)}) collective-permute-start(bf16[1,1536,384]{2,1,0:T(8,128)(2,1)} %ring_sum.18), channel_id=1, source_target_pairs={{0,8},{8,16},{16,24},{24,28},{28,20},{20,12},{12,4},{4,0},{9,1},{1... | collective-permute-start | bytes 3538952 | tf_op jit(solution)/shard_map/ppermute | solution.py:1075
  230.5 27.1 %collective-permute-start.29 = (bf16[1,1536,384]{2,1,0:T(8,128)(2,1)}, bf16[1,1536,384]{2,1,0:T(8,128)(2,1)}, u32[]{:S(2)}, u32[]{:S(2)}) collective-permute-start(bf16[1,1536,384]{2,1,0:T(8,128)(2,1)} %ring_sum.19), channel_id=1, source_target_pairs={{8,0},{16,8},{24,16},{28,24},{20,28},{12,20},{4,12},{0,4},{1,9},{9... | collective-permute-start | bytes 3538952 | tf_op jit(solution)/shard_map/ppermute | solution.py:1075
  240.6 20.8 %collective-permute-start.31 = (bf16[1,1536,384]{2,1,0:T(8,128)(2,1)}, bf16[1,1536,384]{2,1,0:T(8,128)(2,1)}, u32[]{:S(2)}, u32[]{:S(2)}) collective-permute-start(bf16[1,1536,384]{2,1,0:T(8,128)(2,1)} %ring_sum.20), channel_id=1, source_target_pairs={{0,8},{8,16},{16,24},{24,28},{28,20},{20,12},{12,4},{4,0},{9,1},{1... | collective-permute-start | bytes 3538952 | tf_op jit(solution)/shard_map/ppermute | solution.py:1075
  249.2 45.7 %collective-permute-start.36 = (bf16[1024,768]{1,0:T(8,128)(2,1)}, bf16[1024,768]{1,0:T(8,128)(2,1)S(1)}, u32[]{:S(2)}, u32[]{:S(2)}) collective-permute-start(bf16[1024,768]{1,0:T(8,128)(2,1)} %get-tuple-element.284), channel_id=1, source_target_pairs={{0,2},{2,0},{1,3},{3,1},{4,6},{6,4},{5,7},{7,5},{8,10},{10,8},{9,1... | collective-permute-start | bytes 4718600 | tf_op jit(solution)/shard_map/ppermute | solution.py:51
  260.8 26.8 %collective-permute-start.30 = (bf16[1,1536,384]{2,1,0:T(8,128)(2,1)S(1)}, bf16[1,1536,384]{2,1,0:T(8,128)(2,1)S(1)}, u32[]{:S(2)}, u32[]{:S(2)}) collective-permute-start(bf16[1,1536,384]{2,1,0:T(8,128)(2,1)S(1)} %ring_sum.21), channel_id=1, source_target_pairs={{8,0},{16,8},{24,16},{28,24},{20,28},{12,20},{4,12},{0,4},{1,9},{9... | collective-permute-start | bytes 3538952 | tf_op jit(solution)/shard_map/ppermute | solution.py:1075
  263.7 38.3 %collective-permute-start.35 = (bf16[1,1536,384]{2,1,0:T(8,128)(2,1)S(1)}, bf16[1,1536,384]{2,1,0:T(8,128)(2,1)S(1)}, u32[]{:S(2)}, u32[]{:S(2)}) collective-permute-start(bf16[1,1536,384]{2,1,0:T(8,128)(2,1)S(1)} %ring_sum.22), channel_id=1, source_target_pairs={{0,8},{8,16},{16,24},{24,28},{28,20},{20,12},{12,4},{4,0},{9,1},{1... | collective-permute-start | bytes 3538952 | tf_op jit(solution)/shard_map/ppermute | solution.py:1075
  289.3 30.5 %collective-permute-start.34 = (bf16[1,1536,384]{2,1,0:T(8,128)(2,1)}, bf16[1,1536,384]{2,1,0:T(8,128)(2,1)}, u32[]{:S(2)}, u32[]{:S(2)}) collective-permute-start(bf16[1,1536,384]{2,1,0:T(8,128)(2,1)} %ring_sum.23), channel_id=1, source_target_pairs={{8,0},{16,8},{24,16},{28,24},{20,28},{12,20},{4,12},{0,4},{1,9},{9... | collective-permute-start | bytes 3538952 | tf_op jit(solution)/shard_map/ppermute | solution.py:1075
  303.8 35.0 %collective-permute-start.43 = (bf16[1,1536,384]{2,1,0:T(8,128)(2,1)}, bf16[1,1536,384]{2,1,0:T(8,128)(2,1)}, u32[]{:S(2)}, u32[]{:S(2)}) collective-permute-start(bf16[1,1536,384]{2,1,0:T(8,128)(2,1)} %ring_sum.24), channel_id=1, source_target_pairs={{0,8},{8,16},{16,24},{24,28},{28,20},{20,12},{12,4},{4,0},{9,1},{1... | collective-permute-start | bytes 3538952 | tf_op jit(solution)/shard_map/ppermute | solution.py:1075
  322.0 21.0 %collective-permute-start.42 = (bf16[1,1536,384]{2,1,0:T(8,128)(2,1)S(1)}, bf16[1,1536,384]{2,1,0:T(8,128)(2,1)S(1)}, u32[]{:S(2)}, u32[]{:S(2)}) collective-permute-start(bf16[1,1536,384]{2,1,0:T(8,128)(2,1)S(1)} %ring_sum.25), channel_id=1, source_target_pairs={{8,0},{16,8},{24,16},{28,24},{20,28},{12,20},{4,12},{0,4},{1,9},{9... | collective-permute-start | bytes 3538952 | tf_op jit(solution)/shard_map/ppermute | solution.py:1075
  345.9 20.2 %collective-permute-start.50 = (bf16[768,384]{1,0:T(8,128)(2,1)S(1)}, bf16[768,384]{1,0:T(8,128)(2,1)S(1)}, u32[]{:S(2)}, u32[]{:S(2)}) collective-permute-start(bf16[768,384]{1,0:T(8,128)(2,1)S(1)} %bitcast.46), channel_id=1, source_target_pairs={{8,0},{16,8},{24,16},{28,24},{20,28},{12,20},{4,12},{0,4},{1,9},{9... | collective-permute-start | bytes 1769480 | tf_op jit(solution)/shard_map/ppermute | solution.py:1075
  349.7 19.3 %collective-permute-start.44 = (bf16[1,768,384]{2,1,0:T(8,128)(2,1)S(1)}, bf16[1,768,384]{2,1,0:T(8,128)(2,1)}, u32[]{:S(2)}, u32[]{:S(2)}) collective-permute-start(bf16[1,768,384]{2,1,0:T(8,128)(2,1)S(1)} %get-tuple-element.312), channel_id=1, source_target_pairs={{0,1},{1,0},{2,3},{3,2},{4,5},{5,4},{6,7},{7,6},{8,9},{9,8},{10,11... | collective-permute-start | bytes 1769480 | tf_op jit(solution)/shard_map/ppermute | solution.py:51
  387.5 55.4 %collective-permute-start.61 = (bf16[1024,768]{1,0:T(8,128)(2,1)}, bf16[1024,768]{1,0:T(8,128)(2,1)}, u32[]{:S(2)}, u32[]{:S(2)}) collective-permute-start(bf16[1024,768]{1,0:T(8,128)(2,1)} %convolution_convert_fusion), channel_id=1, source_target_pairs={{0,1},{1,0},{2,3},{3,2},{4,5},{5,4},{6,7},{7,6},{8,9},{9,8},{10,11... | collective-permute-start | bytes 4718600 | tf_op jit(solution)/shard_map/ppermute | solution.py:51
  389.1 23.0 %collective-permute-start.55 = (bf16[768,384]{1,0:T(8,128)(2,1)S(1)}, bf16[768,384]{1,0:T(8,128)(2,1)}, u32[]{:S(2)}, u32[]{:S(2)}) collective-permute-start(bf16[768,384]{1,0:T(8,128)(2,1)S(1)} %collective-permute-done.52.refs_1_), channel_id=1, source_target_pairs={{8,0},{16,8},{24,16},{28,24},{20,28},{12,20},{4,12},{0,4},{1,9},{9... | collective-permute-start | bytes 1769480 | tf_op jit(solution)/shard_map/ppermute | solution.py:1075
  389.6 21.2 %collective-permute-start.56 = (bf16[480,384]{1,0:T(8,128)(2,1)S(1)}, bf16[480,384]{1,0:T(8,128)(2,1)S(1)}, u32[]{:S(2)}, u32[]{:S(2)}) collective-permute-start(bf16[480,384]{1,0:T(8,128)(2,1)S(1)} %late_chunk.20), channel_id=1, source_target_pairs={{0,8},{8,16},{16,24},{24,28},{28,20},{20,12},{12,4},{4,0},{9,1},{1... | collective-permute-start | bytes 1105928 | tf_op jit(solution)/shard_map/ppermute | solution.py:1075
  391.1 22.7 %collective-permute-start.71 = (bf16[480,384]{1,0:T(8,128)(2,1)S(1)}, bf16[480,384]{1,0:T(8,128)(2,1)}, u32[]{:S(2)}, u32[]{:S(2)}) collective-permute-start(bf16[480,384]{1,0:T(8,128)(2,1)S(1)} %late_chunk.19), channel_id=1, source_target_pairs={{8,0},{16,8},{24,16},{28,24},{20,28},{12,20},{4,12},{0,4},{1,9},{9... | collective-permute-start | bytes 1105928 | tf_op jit(solution)/shard_map/ppermute | solution.py:1075
  402.9 35.8 %collective-permute-start.54 = (bf16[768,384]{1,0:T(8,128)(2,1)}, bf16[768,384]{1,0:T(8,128)(2,1)}, u32[]{:S(2)}, u32[]{:S(2)}) collective-permute-start(bf16[768,384]{1,0:T(8,128)(2,1)} %collective-permute-done.51.refs_0_), channel_id=1, source_target_pairs={{0,8},{8,16},{16,24},{24,28},{28,20},{20,12},{12,4},{4,0},{9,1},{1... | collective-permute-start | bytes 1769480 | tf_op jit(solution)/shard_map/ppermute | solution.py:1075
  412.1 30.3 %collective-permute-start.58 = (bf16[768,384]{1,0:T(8,128)(2,1)}, bf16[768,384]{1,0:T(8,128)(2,1)}, u32[]{:S(2)}, u32[]{:S(2)}) collective-permute-start(bf16[768,384]{1,0:T(8,128)(2,1)} %collective-permute-done.55.refs_1_), channel_id=1, source_target_pairs={{8,0},{16,8},{24,16},{28,24},{20,28},{12,20},{4,12},{0,4},{1,9},{9... | collective-permute-start | bytes 1769480 | tf_op jit(solution)/shard_map/ppermute | solution.py:1075
  417.4 21.8 %collective-permute-start.59 = (bf16[480,384]{1,0:T(8,128)(2,1)}, bf16[480,384]{1,0:T(8,128)(2,1)}, u32[]{:S(2)}, u32[]{:S(2)}) collective-permute-start(bf16[480,384]{1,0:T(8,128)(2,1)} %late_chunk.21), channel_id=1, source_target_pairs={{0,8},{8,16},{16,24},{24,28},{28,20},{20,12},{12,4},{4,0},{9,1},{1... | collective-permute-start | bytes 1105928 | tf_op jit(solution)/shard_map/ppermute | solution.py:1075
  440.8 20.1 %collective-permute-start.64 = (bf16[480,384]{1,0:T(8,128)(2,1)S(1)}, bf16[480,384]{1,0:T(8,128)(2,1)S(1)}, u32[]{:S(2)}, u32[]{:S(2)}) collective-permute-start(bf16[480,384]{1,0:T(8,128)(2,1)S(1)} %late_chunk.22), channel_id=1, source_target_pairs={{0,8},{8,16},{16,24},{24,28},{28,20},{20,12},{12,4},{4,0},{9,1},{1... | collective-permute-start | bytes 1105928 | tf_op jit(solution)/shard_map/ppermute | solution.py:1075
  442.4 19.1 %collective-permute-start.63 = (bf16[768,384]{1,0:T(8,128)(2,1)}, bf16[768,384]{1,0:T(8,128)(2,1)}, u32[]{:S(2)}, u32[]{:S(2)}) collective-permute-start(bf16[768,384]{1,0:T(8,128)(2,1)} %collective-permute-done.58.refs_1_), channel_id=1, source_target_pairs={{8,0},{16,8},{24,16},{28,24},{20,28},{12,20},{4,12},{0,4},{1,9},{9... | collective-permute-start | bytes 1769480 | tf_op jit(solution)/shard_map/ppermute | solution.py:1075
  446.9 23.0 %collective-permute-start.62 = (bf16[512,768]{1,0:T(8,128)(2,1)}, bf16[512,768]{1,0:T(8,128)(2,1)}, u32[]{:S(2)}, u32[]{:S(2)}) collective-permute-start(bf16[512,768]{1,0:T(8,128)(2,1)} %dynamic-slice_convert_fusion.1), channel_id=1, source_target_pairs={{0,2},{2,0},{1,3},{3,1},{4,6},{6,4},{5,7},{7,5},{8,10},{10,8},{9,1... | collective-permute-start | bytes 2359304 | tf_op jit(solution)/shard_map/ppermute | solution.py:51
  448.7 18.1 %collective-permute-start.74 = (bf16[480,384]{1,0:T(8,128)(2,1)S(1)}, bf16[480,384]{1,0:T(8,128)(2,1)S(1)}, u32[]{:S(2)}, u32[]{:S(2)}) collective-permute-start(bf16[480,384]{1,0:T(8,128)(2,1)S(1)} %late_chunk.28), channel_id=1, source_target_pairs={{8,0},{16,8},{24,16},{28,24},{20,28},{12,20},{4,12},{0,4},{1,9},{9... | collective-permute-start | bytes 1105928 | tf_op jit(solution)/shard_map/ppermute | solution.py:1075
  453.9 19.7 %collective-permute-start.60 = (bf16[768,384]{1,0:T(8,128)(2,1)}, bf16[768,384]{1,0:T(8,128)(2,1)}, u32[]{:S(2)}, u32[]{:S(2)}) collective-permute-start(bf16[768,384]{1,0:T(8,128)(2,1)} %collective-permute-done.57.refs_0_), channel_id=1, source_target_pairs={{0,8},{8,16},{16,24},{24,28},{28,20},{20,12},{12,4},{4,0},{9,1},{1... | collective-permute-start | bytes 1769480 | tf_op jit(solution)/shard_map/ppermute | solution.py:1075
  461.5 22.3 %collective-permute-start.67 = (bf16[768,384]{1,0:T(8,128)(2,1)}, bf16[768,384]{1,0:T(8,128)(2,1)}, u32[]{:S(2)}, u32[]{:S(2)}) collective-permute-start(bf16[768,384]{1,0:T(8,128)(2,1)} %collective-permute-done.63.refs_1_), channel_id=1, source_target_pairs={{8,0},{16,8},{24,16},{28,24},{20,28},{12,20},{4,12},{0,4},{1,9},{9... | collective-permute-start | bytes 1769480 | tf_op jit(solution)/shard_map/ppermute | solution.py:1075
  463.2 18.4 %collective-permute-start.68 = (bf16[480,384]{1,0:T(8,128)(2,1)S(1)}, bf16[480,384]{1,0:T(8,128)(2,1)}, u32[]{:S(2)}, u32[]{:S(2)}) collective-permute-start(bf16[480,384]{1,0:T(8,128)(2,1)S(1)} %late_chunk.23), channel_id=1, source_target_pairs={{0,8},{8,16},{16,24},{24,28},{28,20},{20,12},{12,4},{4,0},{9,1},{1... | collective-permute-start | bytes 1105928 | tf_op jit(solution)/shard_map/ppermute | solution.py:1075
  468.2 19.3 %collective-permute-start.75 = (bf16[480,384]{1,0:T(8,128)(2,1)}, bf16[480,384]{1,0:T(8,128)(2,1)}, u32[]{:S(2)}, u32[]{:S(2)}) collective-permute-start(bf16[480,384]{1,0:T(8,128)(2,1)} %late_chunk.29), channel_id=1, source_target_pairs={{8,0},{16,8},{24,16},{28,24},{20,28},{12,20},{4,12},{0,4},{1,9},{9... | collective-permute-start | bytes 1105928 | tf_op jit(solution)/shard_map/ppermute | solution.py:1075
  473.6 25.4 %collective-permute-start.65 = (bf16[768,384]{1,0:T(8,128)(2,1)}, bf16[768,384]{1,0:T(8,128)(2,1)S(1)}, u32[]{:S(2)}, u32[]{:S(2)}) collective-permute-start(bf16[768,384]{1,0:T(8,128)(2,1)} %collective-permute-done.60.refs_0_), channel_id=1, source_target_pairs={{0,8},{8,16},{16,24},{24,28},{28,20},{20,12},{12,4},{4,0},{9,1},{1... | collective-permute-start | bytes 1769480 | tf_op jit(solution)/shard_map/ppermute | solution.py:1075
  483.5 18.5 %collective-permute-start.70 = (bf16[480,384]{1,0:T(8,128)(2,1)S(1)}, bf16[480,384]{1,0:T(8,128)(2,1)S(1)}, u32[]{:S(2)}, u32[]{:S(2)}) collective-permute-start(bf16[480,384]{1,0:T(8,128)(2,1)S(1)} %late_chunk.24), channel_id=1, source_target_pairs={{0,8},{8,16},{16,24},{24,28},{28,20},{20,12},{12,4},{4,0},{9,1},{1... | collective-permute-start | bytes 1105928 | tf_op jit(solution)/shard_map/ppermute | solution.py:1075
  505.3 19.8 %collective-permute-start.83 = (bf16[768,384]{1,0:T(8,128)(2,1)}, bf16[768,384]{1,0:T(8,128)(2,1)S(1)}, u32[]{:S(2)}, u32[]{:S(2)}) collective-permute-start(bf16[768,384]{1,0:T(8,128)(2,1)} %bitcast.22.refs_1_), channel_id=1, source_target_pairs={{8,0},{16,8},{24,16},{28,24},{20,28},{12,20},{4,12},{0,4},{1,9},{9... | collective-permute-start | bytes 1769480 | tf_op jit(solution)/shard_map/ppermute | solution.py:1075
  506.9 18.3 %collective-permute-start.81 = (bf16[480,384]{1,0:T(8,128)(2,1)S(1)}, bf16[480,384]{1,0:T(8,128)(2,1)S(1)}, u32[]{:S(2)}, u32[]{:S(2)}) collective-permute-start(bf16[480,384]{1,0:T(8,128)(2,1)S(1)} %late_join.2.refs_0_), channel_id=1, source_target_pairs={{0,8},{8,16},{16,24},{24,28},{28,20},{20,12},{12,4},{4,0},{9,1},{1... | collective-permute-start | bytes 1105928 | tf_op jit(solution)/shard_map/ppermute | solution.py:1075
  520.8 26.0 %collective-permute-start.80 = (bf16[768,384]{1,0:T(8,128)(2,1)S(1)}, bf16[768,384]{1,0:T(8,128)(2,1)S(1)}, u32[]{:S(2)}, u32[]{:S(2)}) collective-permute-start(bf16[768,384]{1,0:T(8,128)(2,1)S(1)} %collective-permute-done.69.refs_0_), channel_id=1, source_target_pairs={{0,8},{8,16},{16,24},{24,28},{28,20},{20,12},{12,4},{4,0},{9,1},{1... | collective-permute-start | bytes 1769480 | tf_op jit(solution)/shard_map/ppermute | solution.py:1075
  525.1 22.6 %collective-permute-start.84 = (bf16[768,384]{1,0:T(8,128)(2,1)S(1)}, bf16[768,384]{1,0:T(8,128)(2,1)S(1)}, u32[]{:S(2)}, u32[]{:S(2)}) collective-permute-start(bf16[768,384]{1,0:T(8,128)(2,1)S(1)} %collective-permute-done.83.refs_1_), channel_id=1, source_target_pairs={{8,0},{16,8},{24,16},{28,24},{20,28},{12,20},{4,12},{0,4},{1,9},{9... | collective-permute-start | bytes 1769480 | tf_op jit(solution)/shard_map/ppermute | solution.py:1075
  526.7 18.0 %collective-permute-start.82 = (bf16[480,384]{1,0:T(8,128)(2,1)S(1)}, bf16[480,384]{1,0:T(8,128)(2,1)S(1)}, u32[]{:S(2)}, u32[]{:S(2)}) collective-permute-start(bf16[480,384]{1,0:T(8,128)(2,1)S(1)} %late_join.3.refs_8_), channel_id=1, source_target_pairs={{8,0},{16,8},{24,16},{28,24},{20,28},{12,20},{4,12},{0,4},{1,9},{9... | collective-permute-start | bytes 1105928 | tf_op jit(solution)/shard_map/ppermute | solution.py:1075
  527.8 19.9 %collective-permute-start.85 = (bf16[480,384]{1,0:T(8,128)(2,1)S(1)}, bf16[480,384]{1,0:T(8,128)(2,1)S(1)}, u32[]{:S(2)}, u32[]{:S(2)}) collective-permute-start(bf16[480,384]{1,0:T(8,128)(2,1)S(1)} %collective-permute-done.81.refs_1_), channel_id=1, source_target_pairs={{0,8},{8,16},{16,24},{24,28},{28,20},{20,12},{12,4},{4,0},{9,1},{1... | collective-permute-start | bytes 1105928 | tf_op jit(solution)/shard_map/ppermute | solution.py:1075
  547.7 19.3 %collective-permute-start.93 = (bf16[768,384]{1,0:T(8,128)(2,1)S(1)}, bf16[768,384]{1,0:T(8,128)(2,1)S(1)}, u32[]{:S(2)}, u32[]{:S(2)}) collective-permute-start(bf16[768,384]{1,0:T(8,128)(2,1)S(1)} %collective-permute-done.84.refs_1_), channel_id=1, source_target_pairs={{8,0},{16,8},{24,16},{28,24},{20,28},{12,20},{4,12},{0,4},{1,9},{9... | collective-permute-start | bytes 1769480 | tf_op jit(solution)/shard_map/ppermute | solution.py:1075
  548.9 72.2 %collective-permute-start.86 = (bf16[1024,768]{1,0:T(8,128)(2,1)S(1)}, bf16[1024,768]{1,0:T(8,128)(2,1)S(1)}, u32[]{:S(2)}, u32[]{:S(2)}) collective-permute-start(bf16[1024,768]{1,0:T(8,128)(2,1)S(1)} %copy-done.45), channel_id=1, source_target_pairs={{0,1},{1,0},{2,3},{3,2},{4,5},{5,4},{6,7},{7,6},{8,9},{9,8},{10,11... | collective-permute-start | bytes 4718600 | tf_op jit(solution)/shard_map/ppermute | solution.py:51
  562.0 29.0 %collective-permute-start.92 = (bf16[768,384]{1,0:T(8,128)(2,1)S(1)}, bf16[768,384]{1,0:T(8,128)(2,1)S(1)}, u32[]{:S(2)}, u32[]{:S(2)}) collective-permute-start(bf16[768,384]{1,0:T(8,128)(2,1)S(1)} %collective-permute-done.90.refs_0_), channel_id=1, source_target_pairs={{0,8},{8,16},{16,24},{24,28},{28,20},{20,12},{12,4},{4,0},{9,1},{1... | collective-permute-start | bytes 1769480 | tf_op jit(solution)/shard_map/ppermute | solution.py:1075
  567.0 24.4 %collective-permute-start.96 = (bf16[768,384]{1,0:T(8,128)(2,1)S(1)}, bf16[768,384]{1,0:T(8,128)(2,1)S(1)}, u32[]{:S(2)}, u32[]{:S(2)}) collective-permute-start(bf16[768,384]{1,0:T(8,128)(2,1)S(1)} %collective-permute-done.93.refs_1_), channel_id=1, source_target_pairs={{8,0},{16,8},{24,16},{28,24},{20,28},{12,20},{4,12},{0,4},{1,9},{9... | collective-permute-start | bytes 1769480 | tf_op jit(solution)/shard_map/ppermute | solution.py:1075
  568.6 18.7 %collective-permute-start.104 = (bf16[480,384]{1,0:T(8,128)(2,1)S(1)}, bf16[480,384]{1,0:T(8,128)(2,1)S(1)}, u32[]{:S(2)}, u32[]{:S(2)}) collective-permute-start(bf16[480,384]{1,0:T(8,128)(2,1)S(1)} %collective-permute-done.82.refs_9_), channel_id=1, source_target_pairs={{8,0},{16,8},{24,16},{28,24},{20,28},{12,20},{4,12},{0,4},{1,9},{9... | collective-permute-start | bytes 1105928 | tf_op jit(solution)/shard_map/ppermute | solution.py:1075
  569.9 21.5 %collective-permute-start.91 = (bf16[480,384]{1,0:T(8,128)(2,1)S(1)}, bf16[480,384]{1,0:T(8,128)(2,1)S(1)}, u32[]{:S(2)}, u32[]{:S(2)}) collective-permute-start(bf16[480,384]{1,0:T(8,128)(2,1)S(1)} %collective-permute-done.89.refs_3_), channel_id=1, source_target_pairs={{0,8},{8,16},{16,24},{24,28},{28,20},{20,12},{12,4},{4,0},{9,1},{1... | collective-permute-start | bytes 1105928 | tf_op jit(solution)/shard_map/ppermute | solution.py:1075
  591.0 28.1 %collective-permute-start.95 = (bf16[768,384]{1,0:T(8,128)(2,1)S(1)}, bf16[768,384]{1,0:T(8,128)(2,1)S(1)}, u32[]{:S(2)}, u32[]{:S(2)}) collective-permute-start(bf16[768,384]{1,0:T(8,128)(2,1)S(1)} %collective-permute-done.92.refs_0_), channel_id=1, source_target_pairs={{0,8},{8,16},{16,24},{24,28},{28,20},{20,12},{12,4},{4,0},{9,1},{1... | collective-permute-start | bytes 1769480 | tf_op jit(solution)/shard_map/ppermute | solution.py:1075
  591.4 28.1 %collective-permute-start.99 = (bf16[768,384]{1,0:T(8,128)(2,1)S(1)}, bf16[768,384]{1,0:T(8,128)(2,1)S(1)}, u32[]{:S(2)}, u32[]{:S(2)}) collective-permute-start(bf16[768,384]{1,0:T(8,128)(2,1)S(1)} %collective-permute-done.96.refs_1_), channel_id=1, source_target_pairs={{8,0},{16,8},{24,16},{28,24},{20,28},{12,20},{4,12},{0,4},{1,9},{9... | collective-permute-start | bytes 1769480 | tf_op jit(solution)/shard_map/ppermute | solution.py:1075
  596.9 18.5 %collective-permute-start.106 = (bf16[480,384]{1,0:T(8,128)(2,1)S(1)}, bf16[480,384]{1,0:T(8,128)(2,1)S(1)}, u32[]{:S(2)}, u32[]{:S(2)}) collective-permute-start(bf16[480,384]{1,0:T(8,128)(2,1)S(1)} %collective-permute-done.105.refs_11_), channel_id=1, source_target_pairs={{8,0},{16,8},{24,16},{28,24},{20,28},{12,20},{4,12},{0,4},{1,9},{9... | collective-permute-start | bytes 1105928 | tf_op jit(solution)/shard_map/ppermute | solution.py:1075
  598.9 20.5 %collective-permute-start.94 = (bf16[480,384]{1,0:T(8,128)(2,1)S(1)}, bf16[480,384]{1,0:T(8,128)(2,1)S(1)}, u32[]{:S(2)}, u32[]{:S(2)}) collective-permute-start(bf16[480,384]{1,0:T(8,128)(2,1)S(1)} %collective-permute-done.91.refs_4_), channel_id=1, source_target_pairs={{0,8},{8,16},{16,24},{24,28},{28,20},{20,12},{12,4},{4,0},{9,1},{1... | collective-permute-start | bytes 1105928 | tf_op jit(solution)/shard_map/ppermute | solution.py:1075
  619.5 22.8 %collective-permute-start.102 = (bf16[768,384]{1,0:T(8,128)(2,1)S(1)}, bf16[768,384]{1,0:T(8,128)(2,1)S(1)}, u32[]{:S(2)}, u32[]{:S(2)}) collective-permute-start(bf16[768,384]{1,0:T(8,128)(2,1)S(1)} %collective-permute-done.99.refs_1_), channel_id=1, source_target_pairs={{8,0},{16,8},{24,16},{28,24},{20,28},{12,20},{4,12},{0,4},{1,9},{9... | collective-permute-start | bytes 1769480 | tf_op jit(solution)/shard_map/ppermute | solution.py:1075
  621.4 20.0 %collective-permute-start.97 = (bf16[480,384]{1,0:T(8,128)(2,1)S(1)}, bf16[480,384]{1,0:T(8,128)(2,1)S(1)}, u32[]{:S(2)}, u32[]{:S(2)}) collective-permute-start(bf16[480,384]{1,0:T(8,128)(2,1)S(1)} %collective-permute-done.94.refs_5_), channel_id=1, source_target_pairs={{0,8},{8,16},{16,24},{24,28},{28,20},{20,12},{12,4},{4,0},{9,1},{1... | collective-permute-start | bytes 1105928 | tf_op jit(solution)/shard_map/ppermute | solution.py:1075
  621.9 27.0 %collective-permute-start.87 = (bf16[512,768]{1,0:T(8,128)(2,1)S(1)}, bf16[512,768]{1,0:T(8,128)(2,1)S(1)}, u32[]{:S(2)}, u32[]{:S(2)}) collective-permute-start(bf16[512,768]{1,0:T(8,128)(2,1)S(1)} %dynamic-slice_convert_fusion), channel_id=1, source_target_pairs={{0,2},{2,0},{1,3},{3,1},{4,6},{6,4},{5,7},{7,5},{8,10},{10,8},{9,1... | collective-permute-start | bytes 2359304 | tf_op jit(solution)/shard_map/ppermute | solution.py:51
  626.1 18.2 %collective-permute-start.108 = (bf16[480,384]{1,0:T(8,128)(2,1)S(1)}, bf16[480,384]{1,0:T(8,128)(2,1)S(1)}, u32[]{:S(2)}, u32[]{:S(2)}) collective-permute-start(bf16[480,384]{1,0:T(8,128)(2,1)S(1)} %collective-permute-done.107.refs_13_), channel_id=1, source_target_pairs={{8,0},{16,8},{24,16},{28,24},{20,28},{12,20},{4,12},{0,4},{1,9},{9... | collective-permute-start | bytes 1105928 | tf_op jit(solution)/shard_map/ppermute | solution.py:1075
  643.4 20.8 %collective-permute-start.100 = (bf16[480,384]{1,0:T(8,128)(2,1)S(1)}, bf16[480,384]{1,0:T(8,128)(2,1)S(1)}, u32[]{:S(2)}, u32[]{:S(2)}) collective-permute-start(bf16[480,384]{1,0:T(8,128)(2,1)S(1)} %collective-permute-done.97.refs_6_), channel_id=1, source_target_pairs={{0,8},{8,16},{16,24},{24,28},{28,20},{20,12},{12,4},{4,0},{9,1},{1... | collective-permute-start | bytes 1105928 | tf_op jit(solution)/shard_map/ppermute | solution.py:1075
  644.4 19.5 %collective-permute-start.109 = (bf16[480,384]{1,0:T(8,128)(2,1)S(1)}, bf16[480,384]{1,0:T(8,128)(2,1)S(1)}, u32[]{:S(2)}, u32[]{:S(2)}) collective-permute-start(bf16[480,384]{1,0:T(8,128)(2,1)S(1)} %collective-permute-done.108.refs_14_), channel_id=1, source_target_pairs={{8,0},{16,8},{24,16},{28,24},{20,28},{12,20},{4,12},{0,4},{1,9},{9... | collective-permute-start | bytes 1105928 | tf_op jit(solution)/shard_map/ppermute | solution.py:1075
  (140 other events, 1220.2 us)

commit v16 on v6

--- a/solution.py
+++ b/solution.py
@@ -877,13 +877,11 @@
     out_y = swap(out_y, "row")
     tokens_y = after(tokens_y, near[2], out_y)
     tokens_yc = swap(tokens_y, "col")
-    grad_cut = local_rows // 8 * 5
-    grad_y = swap(after(out_grad[:grad_cut], tokens_y), "row")
+    grad_y = swap(after(out_grad, tokens_y), "row")
     far = project_half(tokens_y, tokens_yc)
-
     shares = [out_y]
     for k in range(1, count):
-        part = out_y if k == 1 else after(out_y, far[2])
+        part = out_y if k < 3 else after(out_y, far[2])
         shares.append(lax.ppermute(part, "dp", [(m, m ^ k) for m in range(dp_size)]))
     where = after(where, grad_y, *shares)
 
@@ -902,12 +900,11 @@
         out_c,
     )
     down_c = swap(after(w_down, tokens_yc), "col")
-    rest_y = swap(after(out_grad[grad_cut:], attended_c), "row")
     attended_y = after(attended_y, before[0])
     out_y = join(member, *shares)
     out_yc = swap(out_y, "col")
     attended_yc = swap(attended_y, "col")
-    grad_own = join(row, out_grad, jnp.concatenate([grad_y, rest_y], axis=0))
+    grad_own = join(row, out_grad, grad_y)
     grad_other = swap(grad_own, "col")
     hidden, x_own, x_other, scale_ffn = hidden_after(
         where, before, [attended_y, attended_yc], out_y, out_yc, gains, gains_c

time: 667 us -> 663 us (level)
    ppermute x34 -> x33, starting transfers between devices: 20 us -> 21.1 us  [swap(): return lax.ppermute(values, axis, [(0, 1), (1, 0)])]
    ppermute x34 -> x33, waiting for transfers between devices: 43.6 us -> 42.9 us  [swap(): return lax.ppermute(values, axis, [(0, 1), (1, 0)])]
    unnamed x182 -> x188, local copies, waits for them, and re-layouts: 17.3 us -> 17.9 us
  transfers between devices with their start and end apart: 110 -> 109, of which waited for: 47 -> 48; matrix products, arithmetic and copies ran while one was open for 8% -> 7% of each run, Pallas kernels for 34% -> 35%
where the time goes in v16:
time: 663 us; the launch traced here: 653 us
  Pallas kernels  242 us (37%)
  waiting for transfers between devices  230 us (35%)
  starting transfers between devices  108 us (16%)
  other arithmetic  40.5 us (6%)
  local copies, waits for them, and re-layouts  23.9 us (4%)
    ppermute x70, waiting for transfers between devices, send(): return lax.ppermute(values, ('dp', 'col'), routes_of[which])  169 us
    pallas_call x9, Pallas kernels, expert_grads(): pl.pallas_call(functools.partial(expert_kernel, shared, aliased, first),...  79.4 us
    ppermute x70, starting transfers between devices, send(): return lax.ppermute(values, ('dp', 'col'), routes_of[which])  77.7 us
    ppermute x33, waiting for transfers between devices, swap(): return lax.ppermute(values, axis, [(0, 1), (1, 0)])  42.9 us
    pallas_call x4, Pallas kernels, mix(): pl.pallas_call(functools.partial(mix_kernel, back, group), grid_spec=pltp...  39.8 us
    pallas_call x16, Pallas kernels, unpack(): pl.pallas_call(functools.partial(unpack_kernel, aliased), grid_spec=pltpu...  39.8 us
    ppermute x33, starting transfers between devices, swap(): return lax.ppermute(values, axis, [(0, 1), (1, 0)])  21.1 us
    convert_element_type x13, other arithmetic, add_rounded(): return (left.astype(F32) + right.astype(F32)).astype(BF16)  20.3 us
  transfers between devices with their start and end apart: 109, of which 48 were waited for; matrix products, arithmetic and copies ran while one was open for 7% of the time, Pallas kernels for 35%

profile of v16, /device:TPU:0, one launch (start us, length us, event | category | flops | bytes accessed | tf_op | source)
XLA Modules:
  0.0 653.3 jit_solution(14423010678116785804)
XLA Ops:
  1.8 3.1 their_columns.1
  8.2 5.0 collective-permute-done.2.gains_c_ref.refs_7_
  13.3 2.9 collective-permute-start.4
  18.0 4.5 project.2
  22.4 10.0 %collective-permute-done.4.refs_0_ = bf16[192,768]{1,0:T(8,128)(2,1)S(1)} collective-permute-done((bf16[192,768]{1,0:T(8,128)(2,1)}, bf16[192,768]{1,0:T(8,128)(2,1)S(1)}, u32[]{:S(2)}, u32[]{:S(2)}) %collective-permute-start.4) | collective-permute-done | bytes 294944 | tf_op jit(solution)/shard_map/ppermute | solution.py:48
  40.7 4.5 project.3
  50.7 5.0 collective-permute-done.5.refs_1_
  57.5 6.2 attend.1.refs_4_.refs_5_
  69.5 9.0 %hidden_before.1 = (f32[1024,768]{1,0:T(8,128)}, f32[1024,768]{1,0:T(8,128)}) custom-call(s32[3]{0:T(128)} %copy-done.53, bf16[512,768]{1,0:T(8,128)(2,1)} %refs_0_.2, bf16[512,768]{1,0:T(8,128)(2,1)} %copy-done.75, bf16[512,768]{1,0:T(8,128)(2,1)} %collective-permute-done.own_ref.refs_2_, bf16[512,768]{1,0:T(8,128)(2,1)} %copy-done.76, ...), custom_call_target="tpu_custom_call" | custom-call | flops 2415919104 | bytes 12582912 | tf_op jit(solution)/shard_map/hidden_before/pallas_call | solution.py:398
  78.5 5.6 collective-permute-done.12.refs_2_
  87.5 9.4 %hidden_after.1 = (f32[1024,768]{1,0:T(8,128)}, bf16[1024,768]{1,0:T(8,128)(2,1)}, bf16[1024,768]{1,0:T(8,128)(2,1)}, f32[1024,1]{1,0:T(8,128)}) custom-call(s32[3]{0:T(128)} %copy-done.53, f32[1024,768]{1,0:T(8,128)} %get-tuple-element.253.refs_0_, f32[1024,768]{1,0:T(8,128)} %get-tuple-element.254.refs_1_, ...), custom_call_target="tpu_custom_call" | custom-call | tf_op jit(solution)/shard_map/hidden_after/pallas_call | solution.py:420
  100.3 9.0 %expert_grads.9 = (bf16[1,1536,384]{2,1,0:T(8,128)(2,1)S(1)}, bf16[1,1536,384]{2,1,0:T(8,128)(2,1)S(1)}, bf16[8,1024,512]{2,1,0:T(8,128)(2,1)}, bf16[8,1024,256]{2,1,0:T(8,128)(2,1)S(1)}) custom-call(s32[63]{0:T(128)S(1)} %fusion.18.order_ref.plan_ref, bf16[1024,768]{1,0:T(8,128)(2,1)S(1)} %copy-done.5, bf16[1024,768]{1,0:T(8,128)(2,1)S(1)} %copy-done.6, ...), custom_call_target="tpu_custom_call" | custom-call | tf_op jit(solution)/shard_map/expert_grads/pallas_call | solution.py:543
  110.9 8.8 %expert_grads.10 = (bf16[1,1536,384]{2,1,0:T(8,128)(2,1)S(1)}, bf16[1,1536,384]{2,1,0:T(8,128)(2,1)S(1)}, bf16[8,1024,512]{2,1,0:T(8,128)(2,1)}, bf16[8,1024,256]{2,1,0:T(8,128)(2,1)S(1)}) custom-call(s32[63]{0:T(128)S(1)} %fusion.18.order_ref.plan_ref, bf16[1024,768]{1,0:T(8,128)(2,1)S(1)} %copy-done.5, ...), custom_call_target="tpu_custom_call", output_to_operand_aliasing={{2}: (18, {}), {3}: (19, {})} | custom-call | tf_op jit(solution)/shard_map/expert_grads/pallas_call | solution.py:543
  120.2 8.8 %expert_grads.11 = (bf16[1,1536,384]{2,1,0:T(8,128)(2,1)S(1)}, bf16[1,1536,384]{2,1,0:T(8,128)(2,1)S(1)}, bf16[8,1024,512]{2,1,0:T(8,128)(2,1)}, bf16[8,1024,256]{2,1,0:T(8,128)(2,1)S(1)}) custom-call(s32[63]{0:T(128)S(1)} %fusion.18.order_ref.plan_ref, bf16[1024,768]{1,0:T(8,128)(2,1)S(1)} %copy-done.5, ...), custom_call_target="tpu_custom_call", output_to_operand_aliasing={{2}: (18, {}), {3}: (19, {})} | custom-call | tf_op jit(solution)/shard_map/expert_grads/pallas_call | solution.py:543
  131.9 9.2 %expert_grads.12 = (bf16[1,1536,384]{2,1,0:T(8,128)(2,1)S(1)}, bf16[1,1536,384]{2,1,0:T(8,128)(2,1)S(1)}, bf16[8,1024,512]{2,1,0:T(8,128)(2,1)}, bf16[8,1024,256]{2,1,0:T(8,128)(2,1)S(1)}) custom-call(s32[63]{0:T(128)S(1)} %fusion.18.order_ref.plan_ref, bf16[1024,768]{1,0:T(8,128)(2,1)S(1)} %copy-done.5, ...), custom_call_target="tpu_custom_call", output_to_operand_aliasing={{2}: (18, {}), {3}: (19, {})} | custom-call | tf_op jit(solution)/shard_map/expert_grads/pallas_call | solution.py:543
  145.8 8.8 %expert_grads.13 = (bf16[1,1536,384]{2,1,0:T(8,128)(2,1)S(1)}, bf16[1,1536,384]{2,1,0:T(8,128)(2,1)S(1)}, bf16[8,1024,512]{2,1,0:T(8,128)(2,1)}, bf16[8,1024,256]{2,1,0:T(8,128)(2,1)S(1)}) custom-call(s32[63]{0:T(128)S(1)} %fusion.18.order_ref.plan_ref, bf16[1024,768]{1,0:T(8,128)(2,1)S(1)} %copy-done.5, ...), custom_call_target="tpu_custom_call", output_to_operand_aliasing={{2}: (18, {}), {3}: (19, {})} | custom-call | tf_op jit(solution)/shard_map/expert_grads/pallas_call | solution.py:543
  156.8 8.8 %expert_grads.14 = (bf16[1,1536,384]{2,1,0:T(8,128)(2,1)S(1)}, bf16[1,1536,384]{2,1,0:T(8,128)(2,1)S(1)}, bf16[8,1024,512]{2,1,0:T(8,128)(2,1)}, bf16[8,1024,256]{2,1,0:T(8,128)(2,1)S(1)}) custom-call(s32[63]{0:T(128)S(1)} %fusion.18.order_ref.plan_ref, bf16[1024,768]{1,0:T(8,128)(2,1)S(1)} %copy-done.5, ...), custom_call_target="tpu_custom_call", output_to_operand_aliasing={{2}: (18, {}), {3}: (19, {})} | custom-call | tf_op jit(solution)/shard_map/expert_grads/pallas_call | solution.py:543
  171.2 9.0 %expert_grads.15 = (bf16[1,1536,384]{2,1,0:T(8,128)(2,1)S(1)}, bf16[1,1536,384]{2,1,0:T(8,128)(2,1)S(1)}, bf16[8,1024,512]{2,1,0:T(8,128)(2,1)}, bf16[8,1024,256]{2,1,0:T(8,128)(2,1)S(1)}) custom-call(s32[63]{0:T(128)S(1)} %fusion.18.order_ref.plan_ref, bf16[1024,768]{1,0:T(8,128)(2,1)S(1)} %copy-done.5, ...), custom_call_target="tpu_custom_call", output_to_operand_aliasing={{2}: (18, {}), {3}: (19, {})} | custom-call | tf_op jit(solution)/shard_map/expert_grads/pallas_call | solution.py:543
  182.9 8.8 %expert_grads.16 = (bf16[1,1536,384]{2,1,0:T(8,128)(2,1)S(1)}, bf16[1,1536,384]{2,1,0:T(8,128)(2,1)S(1)}, bf16[8,1024,512]{2,1,0:T(8,128)(2,1)}, bf16[8,1024,256]{2,1,0:T(8,128)(2,1)S(1)}) custom-call(s32[63]{0:T(128)S(1)} %fusion.18.order_ref.plan_ref, bf16[1024,768]{1,0:T(8,128)(2,1)S(1)} %copy-done.5, ...), custom_call_target="tpu_custom_call", output_to_operand_aliasing={{2}: (18, {}), {3}: (19, {})} | custom-call | tf_op jit(solution)/shard_map/expert_grads/pallas_call | solution.py:543
  193.0 4.5 add_convert_fusion.8
  199.5 7.9 %expert_grads.17 = (bf16[1,1536,384]{2,1,0:T(8,128)(2,1)S(1)}, bf16[1,1536,384]{2,1,0:T(8,128)(2,1)S(1)}, bf16[1,1024,512]{2,1,0:T(8,128)(2,1)S(1)}, bf16[1,1024,256]{2,1,0:T(8,128)(2,1)S(1)}) custom-call(s32[63]{0:T(128)S(1)} %fusion.18.order_ref.plan_ref, bf16[1024,768]{1,0:T(8,128)(2,1)S(1)} %copy-done.5, bf16[1024,768]{1,0:T(8,128)(2,1)S(1)} %copy-done.7, ...), custom_call_target="tpu_custom_call" | custom-call | tf_op jit(solution)/shard_map/expert_grads/pallas_call | solution.py:543
  209.5 2.7 add_convert_fusion.7
  212.2 12.4 %mix.4 = bf16[1024,768]{1,0:T(8,128)(2,1)S(1)} custom-call(s32[63]{0:T(128)S(1)} %fusion.18.order_ref.plan_ref, bf16[8,1024,512]{2,1,0:T(8,128)(2,1)} %get-tuple-element.294.refs_0_, bf16[1,1024,512]{2,1,0:T(8,128)(2,1)S(1)} %get-tuple-element.301.refs_1_, ...), custom_call_target="tpu_custom_call" | custom-call | tf_op jit(solution)/shard_map/mix/pallas_call | solution.py:614
  228.2 12.5 %mix.5 = f32[1024,768]{1,0:T(8,128)S(1)} custom-call(s32[63]{0:T(128)S(1)} %fusion.18.order_ref.plan_ref, bf16[8,1024,512]{2,1,0:T(8,128)(2,1)} %get-tuple-element.294.refs_0_, bf16[1,1024,512]{2,1,0:T(8,128)(2,1)S(1)} %get-tuple-element.301.refs_1_, bf16[16,768,256]{2,1,0:T(8,128)(2,1)} %refs_16_.1, bf16[16,768,256]{2,1,0:T(8,128)(2,1)} %refs_17_.1, ...), custom_call_target="tpu_custom_call" | custom-call | tf_op jit(solution)/shard_map/mix/pallas_call | solution.py:614
  240.7 10.8 %collective-permute-done.29 = bf16[1,1536,384]{2,1,0:T(8,128)(2,1)} collective-permute-done((bf16[1,1536,384]{2,1,0:T(8,128)(2,1)}, bf16[1,1536,384]{2,1,0:T(8,128)(2,1)}, u32[]{:S(2)}, u32[]{:S(2)}) %collective-permute-start.29) | collective-permute-done | bytes 1179680 | tf_op jit(solution)/shard_map/ppermute | solution.py:849
  258.8 7.6 %mix.6 = bf16[1024,768]{1,0:T(8,128)(2,1)S(1)} custom-call(s32[63]{0:T(128)S(1)} %fusion.18.order_ref.plan_ref, bf16[8,1024,256]{2,1,0:T(8,128)(2,1)} %copy-done, bf16[1,1024,256]{2,1,0:T(8,128)(2,1)S(1)} %get-tuple-element.312.refs_1_, ...), custom_call_target="tpu_custom_call" | custom-call | tf_op jit(solution)/shard_map/mix/pallas_call | solution.py:614
  268.3 7.3 %mix.7 = f32[1024,768]{1,0:T(8,128)S(1)} custom-call(s32[63]{0:T(128)S(1)} %fusion.18.order_ref.plan_ref, bf16[8,1024,256]{2,1,0:T(8,128)(2,1)} %copy-done, bf16[1,1024,256]{2,1,0:T(8,128)(2,1)S(1)} %get-tuple-element.312.refs_1_, bf16[16,256,768]{2,1,0:T(8,128)(2,1)} %refs_9_.19, bf16[16,256,768]{2,1,0:T(8,128)(2,1)} %refs_9_.19, ...), custom_call_target="tpu_custom_call" | custom-call | tf_op jit(solution)/shard_map/mix/pallas_call | solution.py:614
  278.3 10.5 %collective-permute-done.35 = bf16[1024,768]{1,0:T(8,128)(2,1)} collective-permute-done((bf16[1024,768]{1,0:T(8,128)(2,1)}, bf16[1024,768]{1,0:T(8,128)(2,1)}, u32[]{:S(2)}, u32[]{:S(2)}) %collective-permute-start.35) | collective-permute-done | bytes 1572896 | tf_op jit(solution)/shard_map/ppermute | solution.py:48
  288.8 3.9 multiply_reduce_fusion
  302.0 14.0 %collective-permute-done.39 = bf16[1,1536,384]{2,1,0:T(8,128)(2,1)} collective-permute-done((bf16[1,1536,384]{2,1,0:T(8,128)(2,1)S(1)}, bf16[1,1536,384]{2,1,0:T(8,128)(2,1)}, u32[]{:S(2)}, u32[]{:S(2)}) %collective-permute-start.39) | collective-permute-done | bytes 1179680 | tf_op jit(solution)/shard_map/ppermute | solution.py:849
  316.0 13.1 %attend_back.1.refs_4_ = bf16[1024,640]{1,0:T(8,128)(2,1)} custom-call(s32[3]{0:T(128)} %copy-done.53, bf16[512,640]{1,0:T(8,128)(2,1)} %get-tuple-element.245.own_ref, bf16[512,640]{1,0:T(8,128)(2,1)} %get-tuple-element.249.other_ref, bf16[1024,768]{1,0:T(8,128)(2,1)} %copy-done.58, bf16[1024,768]{1,0:T(8,128)(2,1)} %collective-permute-done.37.grad_c_ref.refs_7_, ...), custom_call_target="tpu_custom_call" | custom-call | tf_op jit(solution)/shard_map/attend_back/pallas_call | solution.py:166
  337.5 10.5 %collective-permute-done.42.refs_0_ = bf16[1,768,384]{2,1,0:T(8,128)(2,1)S(1)} collective-permute-done((bf16[1,768,384]{2,1,0:T(8,128)(2,1)S(1)}, bf16[1,768,384]{2,1,0:T(8,128)(2,1)S(1)}, u32[]{:S(2)}, u32[]{:S(2)}) %collective-permute-start.42) | collective-permute-done | bytes 589856 | tf_op jit(solution)/shard_map/ppermute | solution.py:849
  348.0 2.8 collective-permute-start.46
  350.8 13.3 %late_grads.1 = (bf16[2,768,896]{2,1,0:T(8,128)(2,1)}, bf16[2,768,896]{2,1,0:T(8,128)(2,1)}) custom-call(s32[3]{0:T(128)} %copy-done.53, bf16[512,768]{1,0:T(8,128)(2,1)} %get-tuple-element.335.refs_0_, bf16[512,768]{1,0:T(8,128)(2,1)} %get-tuple-element.336.refs_1_, bf16[512,768]{1,0:T(8,128)(2,1)} %get-tuple-element.337.refs_2_, ...), custom_call_target="tpu_custom_call" | custom-call | tf_op jit(solution)/shard_map/late_grads/pallas_call | solution.py:217
  369.0 4.6 collective-permute-done.47.refs_0_
  376.5 3.3 unpack.18
  379.8 5.4 collective-permute-done.45.refs_0_
  385.5 4.5 collective-permute-done.50.refs_0_
  397.7 4.8 collective-permute-done.48.refs_0_
  402.4 7.4 %collective-permute-done.52.refs_0_ = bf16[2,96,896]{2,1,0:T(8,128)(2,1)S(1)} collective-permute-done((bf16[2,96,896]{2,1,0:T(8,128)(2,1)S(1)}, bf16[2,96,896]{2,1,0:T(8,128)(2,1)S(1)}, u32[]{:S(2)}, u32[]{:S(2)}) %collective-permute-start.52) | collective-permute-done | bytes 344096 | tf_op jit(solution)/shard_map/ppermute | solution.py:849
  416.6 10.9 %collective-permute-done.74.refs_0_ = bf16[2,96,896]{2,1,0:T(8,128)(2,1)S(1)} collective-permute-done((bf16[2,96,896]{2,1,0:T(8,128)(2,1)S(1)}, bf16[2,96,896]{2,1,0:T(8,128)(2,1)S(1)}, u32[]{:S(2)}, u32[]{:S(2)}) %collective-permute-start.74) | collective-permute-done | bytes 344096 | tf_op jit(solution)/shard_map/ppermute | solution.py:849
  438.3 3.3 collective-permute-start.67
  441.5 14.0 %collective-permute-done.76.refs_0_ = bf16[2,96,896]{2,1,0:T(8,128)(2,1)S(1)} collective-permute-done((bf16[2,96,896]{2,1,0:T(8,128)(2,1)S(1)}, bf16[2,96,896]{2,1,0:T(8,128)(2,1)S(1)}, u32[]{:S(2)}, u32[]{:S(2)}) %collective-permute-start.76) | collective-permute-done | bytes 344096 | tf_op jit(solution)/shard_map/ppermute | solution.py:849
  467.7 5.8 collective-permute-done.66.refs_0_
  476.3 10.7 %collective-permute-done.78.refs_0_ = bf16[2,96,896]{2,1,0:T(8,128)(2,1)S(1)} collective-permute-done((bf16[2,96,896]{2,1,0:T(8,128)(2,1)S(1)}, bf16[2,96,896]{2,1,0:T(8,128)(2,1)S(1)}, u32[]{:S(2)}, u32[]{:S(2)}) %collective-permute-start.78) | collective-permute-done | bytes 344096 | tf_op jit(solution)/shard_map/ppermute | solution.py:849
  492.5 3.1 unpack.24
  495.6 6.6 %collective-permute-done.69.refs_0_ = bf16[2,96,896]{2,1,0:T(8,128)(2,1)S(1)} collective-permute-done((bf16[2,96,896]{2,1,0:T(8,128)(2,1)S(1)}, bf16[2,96,896]{2,1,0:T(8,128)(2,1)S(1)}, u32[]{:S(2)}, u32[]{:S(2)}) %collective-permute-start.69) | collective-permute-done | bytes 344096 | tf_op jit(solution)/shard_map/ppermute | solution.py:849
  516.9 3.1 unpack.25
  520.1 3.2 collective-permute-done.82.refs_1_
  525.5 5.3 collective-permute-done.102.refs_9_
  533.4 3.5 unpack.26
  536.8 2.9 collective-permute-done.86.refs_0_
  540.7 6.6 %collective-permute-done.85.refs_2_ = bf16[2,96,896]{2,1,0:T(8,128)(2,1)} collective-permute-done((bf16[2,96,896]{2,1,0:T(8,128)(2,1)S(1)}, bf16[2,96,896]{2,1,0:T(8,128)(2,1)}, u32[]{:S(2)}, u32[]{:S(2)}) %collective-permute-start.85) | collective-permute-done | bytes 344096 | tf_op jit(solution)/shard_map/ppermute | solution.py:849
  555.3 2.9 convert_add_fusion
  560.6 3.0 collective-permute-done.89.refs_0_
  564.8 5.3 collective-permute-done.88.refs_3_
  575.3 3.5 unpack.28
  578.8 3.9 collective-permute-done.92.refs_0_
  583.8 5.5 collective-permute-done.91.refs_4_
  601.6 2.7 collective-permute-done.95.refs_0_
  605.7 5.0 collective-permute-done.94.refs_5_
  614.8 9.9 %collective-permute-done.57 = f32[2,768]{1,0:T(2,128)S(1)} collective-permute-done((f32[2,768]{1,0:T(2,128)S(1)}, f32[2,768]{1,0:T(2,128)S(1)}, u32[]{:S(2)}, u32[]{:S(2)}) %collective-permute-start.57) | collective-permute-done | bytes 6176 | tf_op jit(solution)/shard_map/ppermute | solution.py:1165
  626.6 5.3 collective-permute-done.58
  646.5 6.4 unpack_late.1
  (454 shorter events, 217.8 us)
Async XLA Ops:
  0.7 34.4 %collective-permute-start.16 = (bf16[16,768,256]{2,1,0:T(8,128)(2,1)}, bf16[16,768,256]{2,1,0:T(8,128)(2,1)}, u32[]{:S(2)}, u32[]{:S(2)}) collective-permute-start(bf16[16,768,256]{2,1,0:T(8,128)(2,1)} %refs_16_.1), channel_id=1, source_target_pairs={{0,1},{1,0},{2,3},{3,2},{4,5},{5,4},{6,7},{7,6},{8,9},{9,8},{10,11... | collective-permute-start | bytes 18874376 | tf_op jit(solution)/shard_map/ppermute | solution.py:48
  5.4 27.1 %collective-permute-start = (bf16[512,768]{1,0:T(8,128)(2,1)S(1)}, bf16[512,768]{1,0:T(8,128)(2,1)}, u32[]{:S(2)}, u32[]{:S(2)}) collective-permute-start(bf16[512,768]{1,0:T(8,128)(2,1)S(1)} %copy-done.62), channel_id=1, source_target_pairs={{0,2},{2,0},{1,3},{3,1},{4,6},{6,4},{5,7},{7,5},{8,10},{10,8},{9,1... | collective-permute-start | bytes 2359304 | tf_op jit(solution)/shard_map/ppermute | solution.py:48
  13.3 19.1 %collective-permute-start.4 = (bf16[192,768]{1,0:T(8,128)(2,1)}, bf16[192,768]{1,0:T(8,128)(2,1)S(1)}, u32[]{:S(2)}, u32[]{:S(2)}) collective-permute-start(bf16[192,768]{1,0:T(8,128)(2,1)} %get-tuple-element.246), channel_id=1, source_target_pairs={{0,2},{2,0},{1,3},{3,1},{4,6},{6,4},{5,7},{7,5},{8,10},{10,8},{9,1... | collective-permute-start | bytes 884744 | tf_op jit(solution)/shard_map/ppermute | solution.py:48
  34.9 62.0 %collective-permute-start.18 = (bf16[16,256,768]{2,1,0:T(8,128)(2,1)}, bf16[16,256,768]{2,1,0:T(8,128)(2,1)}, u32[]{:S(2)}, u32[]{:S(2)}) collective-permute-start(bf16[16,256,768]{2,1,0:T(8,128)(2,1)} %refs_9_.19), channel_id=1, source_target_pairs={{0,1},{1,0},{2,3},{3,2},{4,5},{5,4},{6,7},{7,6},{8,9},{9,8},{10,11... | collective-permute-start | bytes 18874376 | tf_op jit(solution)/shard_map/ppermute | solution.py:48
  35.8 61.1 %collective-permute-start.17 = (bf16[16,768,256]{2,1,0:T(8,128)(2,1)}, bf16[16,768,256]{2,1,0:T(8,128)(2,1)}, u32[]{:S(2)}, u32[]{:S(2)}) collective-permute-start(bf16[16,768,256]{2,1,0:T(8,128)(2,1)} %refs_17_.1), channel_id=1, source_target_pairs={{0,1},{1,0},{2,3},{3,2},{4,5},{5,4},{6,7},{7,6},{8,9},{9,8},{10,11... | collective-permute-start | bytes 18874376 | tf_op jit(solution)/shard_map/ppermute | solution.py:48
  35.9 19.8 %collective-permute-start.5 = (bf16[512,768]{1,0:T(8,128)(2,1)S(1)}, bf16[512,768]{1,0:T(8,128)(2,1)S(1)}, u32[]{:S(2)}, u32[]{:S(2)}) collective-permute-start(bf16[512,768]{1,0:T(8,128)(2,1)S(1)} %copy-done.36), channel_id=1, source_target_pairs={{0,2},{2,0},{1,3},{3,1},{4,6},{6,4},{5,7},{7,5},{8,10},{10,8},{9,1... | collective-permute-start | bytes 2359304 | tf_op jit(solution)/shard_map/ppermute | solution.py:48
  50.6 17.8 %collective-permute-start.11 = (bf16[768,768]{1,0:T(8,128)(2,1)}, bf16[768,768]{1,0:T(8,128)(2,1)}, u32[]{:S(2)}, u32[]{:S(2)}) collective-permute-start(bf16[768,768]{1,0:T(8,128)(2,1)} %out_ref.1), channel_id=1, source_target_pairs={{0,1},{1,0},{2,3},{3,2},{4,5},{5,4},{6,7},{7,6},{8,9},{9,8},{10,11... | collective-permute-start | bytes 3538952 | tf_op jit(solution)/shard_map/ppermute | solution.py:48
  63.8 20.3 %collective-permute-start.12 = (bf16[1024,384]{1,0:T(8,128)(2,1)}, bf16[1024,384]{1,0:T(8,128)(2,1)}, u32[]{:S(2)}, u32[]{:S(2)}) collective-permute-start(bf16[1024,384]{1,0:T(8,128)(2,1)} %attend.1.refs_4_.refs_5_), channel_id=1, source_target_pairs={{0,2},{2,0},{1,3},{3,1},{4,6},{6,4},{5,7},{7,5},{8,10},{10,8},{9,1... | collective-permute-start | bytes 2359304 | tf_op jit(solution)/shard_map/ppermute | solution.py:48
  67.2 29.7 %collective-permute-start.15 = (bf16[1024,768]{1,0:T(8,128)(2,1)S(1)}, bf16[1024,768]{1,0:T(8,128)(2,1)S(1)}, u32[]{:S(2)}, u32[]{:S(2)}) collective-permute-start(bf16[1024,768]{1,0:T(8,128)(2,1)S(1)} %join.3.refs_2_), channel_id=1, source_target_pairs={{0,1},{1,0},{2,3},{3,2},{4,5},{5,4},{6,7},{7,6},{8,9},{9,8},{10,11... | collective-permute-start | bytes 4718600 | tf_op jit(solution)/shard_map/ppermute | solution.py:48
  109.3 19.7 %collective-permute-start.19 = (bf16[1,1536,384]{2,1,0:T(8,128)(2,1)S(1)}, bf16[1,1536,384]{2,1,0:T(8,128)(2,1)S(1)}, u32[]{:S(2)}, u32[]{:S(2)}) collective-permute-start(bf16[1,1536,384]{2,1,0:T(8,128)(2,1)S(1)} %get-tuple-element.261), channel_id=1, source_target_pairs={{0,8},{8,16},{16,24},{24,28},{28,20},{20,12},{12,4},{4,0},{9,1},{1... | collective-permute-start | bytes 3538952 | tf_op jit(solution)/shard_map/ppermute | solution.py:849
  119.7 23.3 %collective-permute-start.21 = (bf16[1,1536,384]{2,1,0:T(8,128)(2,1)S(1)}, bf16[1,1536,384]{2,1,0:T(8,128)(2,1)S(1)}, u32[]{:S(2)}, u32[]{:S(2)}) collective-permute-start(bf16[1,1536,384]{2,1,0:T(8,128)(2,1)S(1)} %get-tuple-element.271), channel_id=1, source_target_pairs={{8,0},{16,8},{24,16},{28,24},{20,28},{12,20},{4,12},{0,4},{1,9},{9... | collective-permute-start | bytes 3538952 | tf_op jit(solution)/shard_map/ppermute | solution.py:849
  129.4 25.3 %collective-permute-start.20 = (bf16[1,1536,384]{2,1,0:T(8,128)(2,1)S(1)}, bf16[1,1536,384]{2,1,0:T(8,128)(2,1)S(1)}, u32[]{:S(2)}, u32[]{:S(2)}) collective-permute-start(bf16[1,1536,384]{2,1,0:T(8,128)(2,1)S(1)} %add_convert_fusion.13), channel_id=1, source_target_pairs={{0,8},{8,16},{16,24},{24,28},{28,20},{20,12},{12,4},{4,0},{9,1},{1... | collective-permute-start | bytes 3538952 | tf_op jit(solution)/shard_map/ppermute | solution.py:849
  144.4 23.8 %collective-permute-start.23 = (bf16[1,1536,384]{2,1,0:T(8,128)(2,1)}, bf16[1,1536,384]{2,1,0:T(8,128)(2,1)S(1)}, u32[]{:S(2)}, u32[]{:S(2)}) collective-permute-start(bf16[1,1536,384]{2,1,0:T(8,128)(2,1)} %add_convert_fusion.12), channel_id=1, source_target_pairs={{8,0},{16,8},{24,16},{28,24},{20,28},{12,20},{4,12},{0,4},{1,9},{9... | collective-permute-start | bytes 3538952 | tf_op jit(solution)/shard_map/ppermute | solution.py:849
  155.0 25.2 %collective-permute-start.22 = (bf16[1,1536,384]{2,1,0:T(8,128)(2,1)S(1)}, bf16[1,1536,384]{2,1,0:T(8,128)(2,1)S(1)}, u32[]{:S(2)}, u32[]{:S(2)}) collective-permute-start(bf16[1,1536,384]{2,1,0:T(8,128)(2,1)S(1)} %add_convert_fusion.11), channel_id=1, source_target_pairs={{0,8},{8,16},{16,24},{24,28},{28,20},{20,12},{12,4},{4,0},{9,1},{1... | collective-permute-start | bytes 3538952 | tf_op jit(solution)/shard_map/ppermute | solution.py:849
  169.5 23.5 %collective-permute-start.25 = (bf16[1,1536,384]{2,1,0:T(8,128)(2,1)}, bf16[1,1536,384]{2,1,0:T(8,128)(2,1)}, u32[]{:S(2)}, u32[]{:S(2)}) collective-permute-start(bf16[1,1536,384]{2,1,0:T(8,128)(2,1)} %add_convert_fusion.10), channel_id=1, source_target_pairs={{8,0},{16,8},{24,16},{28,24},{20,28},{12,20},{4,12},{0,4},{1,9},{9... | collective-permute-start | bytes 3538952 | tf_op jit(solution)/shard_map/ppermute | solution.py:849
  180.6 28.9 %collective-permute-start.24 = (bf16[1,1536,384]{2,1,0:T(8,128)(2,1)S(1)}, bf16[1,1536,384]{2,1,0:T(8,128)(2,1)}, u32[]{:S(2)}, u32[]{:S(2)}) collective-permute-start(bf16[1,1536,384]{2,1,0:T(8,128)(2,1)S(1)} %add_convert_fusion.9), channel_id=1, source_target_pairs={{0,8},{8,16},{16,24},{24,28},{28,20},{20,12},{12,4},{4,0},{9,1},{1... | collective-permute-start | bytes 3538952 | tf_op jit(solution)/shard_map/ppermute | solution.py:849
  181.9 17.6 %collective-permute-start.26 = (bf16[1,768,512]{2,1,0:T(8,128)(2,1)S(1)}, bf16[1,768,512]{2,1,0:T(8,128)(2,1)S(1)}, u32[]{:S(2)}, u32[]{:S(2)}) collective-permute-start(bf16[1,768,512]{2,1,0:T(8,128)(2,1)S(1)} %bitcast.55), channel_id=1, source_target_pairs={{0,1},{1,0},{2,3},{3,2},{4,5},{5,4},{6,7},{7,6},{8,9},{9,8},{10,11... | collective-permute-start | bytes 2359304 | tf_op jit(solution)/shard_map/ppermute | solution.py:48
  182.4 17.1 %collective-permute-start.27 = (bf16[1,768,512]{2,1,0:T(8,128)(2,1)S(1)}, bf16[1,768,512]{2,1,0:T(8,128)(2,1)S(1)}, u32[]{:S(2)}, u32[]{:S(2)}) collective-permute-start(bf16[1,768,512]{2,1,0:T(8,128)(2,1)S(1)} %bitcast.60), channel_id=1, source_target_pairs={{0,1},{1,0},{2,3},{3,2},{4,5},{5,4},{6,7},{7,6},{8,9},{9,8},{10,11... | collective-permute-start | bytes 2359304 | tf_op jit(solution)/shard_map/ppermute | solution.py:48
  182.7 16.8 %collective-permute-start.28 = (bf16[1,512,768]{2,1,0:T(8,128)(2,1)S(1)}, bf16[1,512,768]{2,1,0:T(8,128)(2,1)S(1)}, u32[]{:S(2)}, u32[]{:S(2)}) collective-permute-start(bf16[1,512,768]{2,1,0:T(8,128)(2,1)S(1)} %bitcast.65), channel_id=1, source_target_pairs={{0,1},{1,0},{2,3},{3,2},{4,5},{5,4},{6,7},{7,6},{8,9},{9,8},{10,11... | collective-permute-start | bytes 2359304 | tf_op jit(solution)/shard_map/ppermute | solution.py:48
  197.5 28.3 %collective-permute-start.30 = (bf16[1,1536,384]{2,1,0:T(8,128)(2,1)}, bf16[1,1536,384]{2,1,0:T(8,128)(2,1)S(1)}, u32[]{:S(2)}, u32[]{:S(2)}) collective-permute-start(bf16[1,1536,384]{2,1,0:T(8,128)(2,1)} %add_convert_fusion.8), channel_id=1, source_target_pairs={{8,0},{16,8},{24,16},{28,24},{20,28},{12,20},{4,12},{0,4},{1,9},{9... | collective-permute-start | bytes 3538952 | tf_op jit(solution)/shard_map/ppermute | solution.py:849
  224.7 26.9 %collective-permute-start.34 = (bf16[1024,768]{1,0:T(8,128)(2,1)S(1)}, bf16[1024,768]{1,0:T(8,128)(2,1)S(1)}, u32[]{:S(2)}, u32[]{:S(2)}) collective-permute-start(bf16[1024,768]{1,0:T(8,128)(2,1)S(1)} %mix.4), channel_id=1, source_target_pairs={{0,1},{1,0},{2,3},{3,2},{4,5},{5,4},{6,7},{7,6},{8,9},{9,8},{10,11... | collective-permute-start | bytes 4718600 | tf_op jit(solution)/shard_map/ppermute | solution.py:48
  224.7 26.8 %collective-permute-start.29 = (bf16[1,1536,384]{2,1,0:T(8,128)(2,1)}, bf16[1,1536,384]{2,1,0:T(8,128)(2,1)}, u32[]{:S(2)}, u32[]{:S(2)}) collective-permute-start(bf16[1,1536,384]{2,1,0:T(8,128)(2,1)} %add_convert_fusion.7), channel_id=1, source_target_pairs={{0,8},{8,16},{16,24},{24,28},{28,20},{20,12},{12,4},{4,0},{9,1},{1... | collective-permute-start | bytes 3538952 | tf_op jit(solution)/shard_map/ppermute | solution.py:849
  227.2 39.2 %collective-permute-start.31 = (bf16[1,1536,384]{2,1,0:T(8,128)(2,1)}, bf16[1,1536,384]{2,1,0:T(8,128)(2,1)S(1)}, u32[]{:S(2)}, u32[]{:S(2)}) collective-permute-start(bf16[1,1536,384]{2,1,0:T(8,128)(2,1)} %add_convert_fusion.6), channel_id=1, source_target_pairs={{8,0},{16,8},{24,16},{28,24},{20,28},{12,20},{4,12},{0,4},{1,9},{9... | collective-permute-start | bytes 3538952 | tf_op jit(solution)/shard_map/ppermute | solution.py:849
  253.2 35.6 %collective-permute-start.35 = (bf16[1024,768]{1,0:T(8,128)(2,1)}, bf16[1024,768]{1,0:T(8,128)(2,1)}, u32[]{:S(2)}, u32[]{:S(2)}) collective-permute-start(bf16[1024,768]{1,0:T(8,128)(2,1)} %fusion), channel_id=1, source_target_pairs={{0,2},{2,0},{1,3},{3,1},{4,6},{6,4},{5,7},{7,5},{8,10},{10,8},{9,1... | collective-permute-start | bytes 4718600 | tf_op jit(solution)/shard_map/ppermute | solution.py:48
  256.9 21.4 %collective-permute-start.38 = (bf16[1,1536,384]{2,1,0:T(8,128)(2,1)}, bf16[1,1536,384]{2,1,0:T(8,128)(2,1)S(1)}, u32[]{:S(2)}, u32[]{:S(2)}) collective-permute-start(bf16[1,1536,384]{2,1,0:T(8,128)(2,1)} %add_convert_fusion.5), channel_id=1, source_target_pairs={{0,8},{8,16},{16,24},{24,28},{28,20},{20,12},{12,4},{4,0},{9,1},{1... | collective-permute-start | bytes 3538952 | tf_op jit(solution)/shard_map/ppermute | solution.py:849
  267.8 25.4 %collective-permute-start.40 = (bf16[1,1536,384]{2,1,0:T(8,128)(2,1)}, bf16[1,1536,384]{2,1,0:T(8,128)(2,1)S(1)}, u32[]{:S(2)}, u32[]{:S(2)}) collective-permute-start(bf16[1,1536,384]{2,1,0:T(8,128)(2,1)} %add_convert_fusion.4), channel_id=1, source_target_pairs={{8,0},{16,8},{24,16},{28,24},{20,28},{12,20},{4,12},{0,4},{1,9},{9... | collective-permute-start | bytes 3538952 | tf_op jit(solution)/shard_map/ppermute | solution.py:849
  293.2 22.8 %collective-permute-start.39 = (bf16[1,1536,384]{2,1,0:T(8,128)(2,1)S(1)}, bf16[1,1536,384]{2,1,0:T(8,128)(2,1)}, u32[]{:S(2)}, u32[]{:S(2)}) collective-permute-start(bf16[1,1536,384]{2,1,0:T(8,128)(2,1)S(1)} %add_convert_fusion.3), channel_id=1, source_target_pairs={{0,8},{8,16},{16,24},{24,28},{28,20},{20,12},{12,4},{4,0},{9,1},{1... | collective-permute-start | bytes 3538952 | tf_op jit(solution)/shard_map/ppermute | solution.py:849
  298.0 17.9 %collective-permute-start.37 = (bf16[1024,768]{1,0:T(8,128)(2,1)S(1)}, bf16[1024,768]{1,0:T(8,128)(2,1)}, u32[]{:S(2)}, u32[]{:S(2)}) collective-permute-start(bf16[1024,768]{1,0:T(8,128)(2,1)S(1)} %get-tuple-element.482.grad_ref.refs_6_), channel_id=1, source_target_pairs={{0,1},{1,0},{2,3},{3,2},{4,5},{5,4},{6,7},{7,6},{8,9},{9,8},{10,11... | collective-permute-start | bytes 4718600 | tf_op jit(solution)/shard_map/ppermute | solution.py:48
  299.6 29.5 %collective-permute-start.41 = (bf16[1,1536,384]{2,1,0:T(8,128)(2,1)}, bf16[1,1536,384]{2,1,0:T(8,128)(2,1)}, u32[]{:S(2)}, u32[]{:S(2)}) collective-permute-start(bf16[1,1536,384]{2,1,0:T(8,128)(2,1)} %add_convert_fusion.1), channel_id=1, source_target_pairs={{8,0},{16,8},{24,16},{28,24},{20,28},{12,20},{4,12},{0,4},{1,9},{9... | collective-permute-start | bytes 3538952 | tf_op jit(solution)/shard_map/ppermute | solution.py:849
  348.0 20.6 %collective-permute-start.43 = (bf16[1,768,384]{2,1,0:T(8,128)(2,1)S(1)}, bf16[1,768,384]{2,1,0:T(8,128)(2,1)}, u32[]{:S(2)}, u32[]{:S(2)}) collective-permute-start(bf16[1,768,384]{2,1,0:T(8,128)(2,1)S(1)} %collective-permute-done.42.refs_0_), channel_id=1, source_target_pairs={{0,8},{8,16},{16,24},{24,28},{28,20},{20,12},{12,4},{4,0},{9,1},{1... | collective-permute-start | bytes 1769480 | tf_op jit(solution)/shard_map/ppermute | solution.py:849
  348.0 26.4 %collective-permute-start.46 = (bf16[1,768,384]{2,1,0:T(8,128)(2,1)S(1)}, bf16[1,768,384]{2,1,0:T(8,128)(2,1)}, u32[]{:S(2)}, u32[]{:S(2)}) collective-permute-start(bf16[1,768,384]{2,1,0:T(8,128)(2,1)S(1)} %collective-permute-done.44.refs_1_), channel_id=1, source_target_pairs={{8,0},{16,8},{24,16},{28,24},{20,28},{12,20},{4,12},{0,4},{1,9},{9... | collective-permute-start | bytes 1769480 | tf_op jit(solution)/shard_map/ppermute | solution.py:849
  368.5 16.7 %collective-permute-start.45 = (bf16[1,768,384]{2,1,0:T(8,128)(2,1)}, bf16[1,768,384]{2,1,0:T(8,128)(2,1)S(1)}, u32[]{:S(2)}, u32[]{:S(2)}) collective-permute-start(bf16[1,768,384]{2,1,0:T(8,128)(2,1)} %collective-permute-done.43.refs_0_), channel_id=1, source_target_pairs={{0,8},{8,16},{16,24},{24,28},{28,20},{20,12},{12,4},{4,0},{9,1},{1... | collective-permute-start | bytes 1769480 | tf_op jit(solution)/shard_map/ppermute | solution.py:849
  385.2 17.2 %collective-permute-start.48 = (bf16[1,768,384]{2,1,0:T(8,128)(2,1)S(1)}, bf16[1,768,384]{2,1,0:T(8,128)(2,1)S(1)}, u32[]{:S(2)}, u32[]{:S(2)}) collective-permute-start(bf16[1,768,384]{2,1,0:T(8,128)(2,1)S(1)} %collective-permute-done.45.refs_0_), channel_id=1, source_target_pairs={{0,8},{8,16},{16,24},{24,28},{28,20},{20,12},{12,4},{4,0},{9,1},{1... | collective-permute-start | bytes 1769480 | tf_op jit(solution)/shard_map/ppermute | solution.py:849
  390.9 19.6 %collective-permute-start.51 = (bf16[1,768,384]{2,1,0:T(8,128)(2,1)S(1)}, bf16[1,768,384]{2,1,0:T(8,128)(2,1)S(1)}, u32[]{:S(2)}, u32[]{:S(2)}) collective-permute-start(bf16[1,768,384]{2,1,0:T(8,128)(2,1)S(1)} %collective-permute-done.49.refs_1_), channel_id=1, source_target_pairs={{8,0},{16,8},{24,16},{28,24},{20,28},{12,20},{4,12},{0,4},{1,9},{9... | collective-permute-start | bytes 1769480 | tf_op jit(solution)/shard_map/ppermute | solution.py:849
  392.9 16.9 %collective-permute-start.52 = (bf16[2,96,896]{2,1,0:T(8,128)(2,1)S(1)}, bf16[2,96,896]{2,1,0:T(8,128)(2,1)S(1)}, u32[]{:S(2)}, u32[]{:S(2)}) collective-permute-start(bf16[2,96,896]{2,1,0:T(8,128)(2,1)S(1)} %late_chunk.18), channel_id=1, source_target_pairs={{0,8},{8,16},{16,24},{24,28},{28,20},{20,12},{12,4},{4,0},{9,1},{1... | collective-permute-start | bytes 1032200 | tf_op jit(solution)/shard_map/ppermute | solution.py:849
  393.5 20.3 %collective-permute-start.73 = (bf16[2,96,896]{2,1,0:T(8,128)(2,1)S(1)}, bf16[2,96,896]{2,1,0:T(8,128)(2,1)S(1)}, u32[]{:S(2)}, u32[]{:S(2)}) collective-permute-start(bf16[2,96,896]{2,1,0:T(8,128)(2,1)S(1)} %late_chunk.24), channel_id=1, source_target_pairs={{8,0},{16,8},{24,16},{28,24},{20,28},{12,20},{4,12},{0,4},{1,9},{9... | collective-permute-start | bytes 1032200 | tf_op jit(solution)/shard_map/ppermute | solution.py:849
  402.4 29.6 %collective-permute-start.61 = (bf16[1,768,384]{2,1,0:T(8,128)(2,1)S(1)}, bf16[1,768,384]{2,1,0:T(8,128)(2,1)S(1)}, u32[]{:S(2)}, u32[]{:S(2)}) collective-permute-start(bf16[1,768,384]{2,1,0:T(8,128)(2,1)S(1)} %collective-permute-done.48.refs_0_), channel_id=1, source_target_pairs={{0,8},{8,16},{16,24},{24,28},{28,20},{20,12},{12,4},{4,0},{9,1},{1... | collective-permute-start | bytes 1769480 | tf_op jit(solution)/shard_map/ppermute | solution.py:849
  410.5 22.5 %collective-permute-start.62 = (bf16[1,768,384]{2,1,0:T(8,128)(2,1)S(1)}, bf16[1,768,384]{2,1,0:T(8,128)(2,1)S(1)}, u32[]{:S(2)}, u32[]{:S(2)}) collective-permute-start(bf16[1,768,384]{2,1,0:T(8,128)(2,1)S(1)} %collective-permute-done.51.refs_1_), channel_id=1, source_target_pairs={{8,0},{16,8},{24,16},{28,24},{20,28},{12,20},{4,12},{0,4},{1,9},{9... | collective-permute-start | bytes 1769480 | tf_op jit(solution)/shard_map/ppermute | solution.py:849
  432.1 25.8 %collective-permute-start.64 = (bf16[1,768,384]{2,1,0:T(8,128)(2,1)S(1)}, bf16[1,768,384]{2,1,0:T(8,128)(2,1)S(1)}, u32[]{:S(2)}, u32[]{:S(2)}) collective-permute-start(bf16[1,768,384]{2,1,0:T(8,128)(2,1)S(1)} %collective-permute-done.61.refs_0_), channel_id=1, source_target_pairs={{0,8},{8,16},{16,24},{24,28},{28,20},{20,12},{12,4},{4,0},{9,1},{1... | collective-permute-start | bytes 1769480 | tf_op jit(solution)/shard_map/ppermute | solution.py:849
  433.1 29.4 %collective-permute-start.65 = (bf16[1,768,384]{2,1,0:T(8,128)(2,1)S(1)}, bf16[1,768,384]{2,1,0:T(8,128)(2,1)S(1)}, u32[]{:S(2)}, u32[]{:S(2)}) collective-permute-start(bf16[1,768,384]{2,1,0:T(8,128)(2,1)S(1)} %collective-permute-done.62.refs_1_), channel_id=1, source_target_pairs={{8,0},{16,8},{24,16},{28,24},{20,28},{12,20},{4,12},{0,4},{1,9},{9... | collective-permute-start | bytes 1769480 | tf_op jit(solution)/shard_map/ppermute | solution.py:849
  436.2 19.3 %collective-permute-start.76 = (bf16[2,96,896]{2,1,0:T(8,128)(2,1)S(1)}, bf16[2,96,896]{2,1,0:T(8,128)(2,1)S(1)}, u32[]{:S(2)}, u32[]{:S(2)}) collective-permute-start(bf16[2,96,896]{2,1,0:T(8,128)(2,1)S(1)} %late_chunk.27), channel_id=1, source_target_pairs={{8,0},{16,8},{24,16},{28,24},{20,28},{12,20},{4,12},{0,4},{1,9},{9... | collective-permute-start | bytes 1032200 | tf_op jit(solution)/shard_map/ppermute | solution.py:849
  438.0 23.8 %collective-permute-start.63 = (bf16[2,96,896]{2,1,0:T(8,128)(2,1)S(1)}, bf16[2,96,896]{2,1,0:T(8,128)(2,1)S(1)}, u32[]{:S(2)}, u32[]{:S(2)}) collective-permute-start(bf16[2,96,896]{2,1,0:T(8,128)(2,1)S(1)} %late_chunk.20), channel_id=1, source_target_pairs={{0,8},{8,16},{16,24},{24,28},{28,20},{20,12},{12,4},{4,0},{9,1},{1... | collective-permute-start | bytes 1032200 | tf_op jit(solution)/shard_map/ppermute | solution.py:849
  438.3 26.3 %collective-permute-start.67 = (bf16[1,768,384]{2,1,0:T(8,128)(2,1)S(1)}, bf16[1,768,384]{2,1,0:T(8,128)(2,1)S(1)}, u32[]{:S(2)}, u32[]{:S(2)}) collective-permute-start(bf16[1,768,384]{2,1,0:T(8,128)(2,1)S(1)} %copy-done.79), channel_id=1, source_target_pairs={{0,1},{1,0},{2,3},{3,2},{4,5},{5,4},{6,7},{7,6},{8,9},{9,8},{10,11... | collective-permute-start | bytes 1769480 | tf_op jit(solution)/shard_map/ppermute | solution.py:48
  455.5 19.4 %collective-permute-start.68 = (bf16[1,768,384]{2,1,0:T(8,128)(2,1)S(1)}, bf16[1,768,384]{2,1,0:T(8,128)(2,1)}, u32[]{:S(2)}, u32[]{:S(2)}) collective-permute-start(bf16[1,768,384]{2,1,0:T(8,128)(2,1)S(1)} %copy-done.78), channel_id=1, source_target_pairs={{0,1},{1,0},{2,3},{3,2},{4,5},{5,4},{6,7},{7,6},{8,9},{9,8},{10,11... | collective-permute-start | bytes 1769480 | tf_op jit(solution)/shard_map/ppermute | solution.py:48
  462.8 27.3 %collective-permute-start.72 = (bf16[1,768,384]{2,1,0:T(8,128)(2,1)S(1)}, bf16[1,768,384]{2,1,0:T(8,128)(2,1)S(1)}, u32[]{:S(2)}, u32[]{:S(2)}) collective-permute-start(bf16[1,768,384]{2,1,0:T(8,128)(2,1)S(1)} %collective-permute-done.65.refs_1_), channel_id=1, source_target_pairs={{8,0},{16,8},{24,16},{28,24},{20,28},{12,20},{4,12},{0,4},{1,9},{9... | collective-permute-start | bytes 1769480 | tf_op jit(solution)/shard_map/ppermute | solution.py:849
  464.6 25.8 %collective-permute-start.71 = (bf16[1,768,384]{2,1,0:T(8,128)(2,1)S(1)}, bf16[1,768,384]{2,1,0:T(8,128)(2,1)S(1)}, u32[]{:S(2)}, u32[]{:S(2)}) collective-permute-start(bf16[1,768,384]{2,1,0:T(8,128)(2,1)S(1)} %collective-permute-done.64.refs_0_), channel_id=1, source_target_pairs={{0,8},{8,16},{16,24},{24,28},{28,20},{20,12},{12,4},{4,0},{9,1},{1... | collective-permute-start | bytes 1769480 | tf_op jit(solution)/shard_map/ppermute | solution.py:849
  467.0 28.7 %collective-permute-start.70 = (bf16[1,768,384]{2,1,0:T(8,128)(2,1)S(1)}, bf16[1,768,384]{2,1,0:T(8,128)(2,1)S(1)}, u32[]{:S(2)}, u32[]{:S(2)}) collective-permute-start(bf16[1,768,384]{2,1,0:T(8,128)(2,1)S(1)} %collective-permute-done.67.refs_0_), channel_id=1, source_target_pairs={{0,8},{8,16},{16,24},{24,28},{28,20},{20,12},{12,4},{4,0},{9,1},{1... | collective-permute-start | bytes 1769480 | tf_op jit(solution)/shard_map/ppermute | solution.py:849
  475.0 27.3 %collective-permute-start.69 = (bf16[2,96,896]{2,1,0:T(8,128)(2,1)S(1)}, bf16[2,96,896]{2,1,0:T(8,128)(2,1)S(1)}, u32[]{:S(2)}, u32[]{:S(2)}) collective-permute-start(bf16[2,96,896]{2,1,0:T(8,128)(2,1)S(1)} %late_chunk.22), channel_id=1, source_target_pairs={{0,8},{8,16},{16,24},{24,28},{28,20},{20,12},{12,4},{4,0},{9,1},{1... | collective-permute-start | bytes 1032200 | tf_op jit(solution)/shard_map/ppermute | solution.py:849
  486.9 18.4 %collective-permute-start.80 = (bf16[1,768,384]{2,1,0:T(8,128)(2,1)}, bf16[1,768,384]{2,1,0:T(8,128)(2,1)}, u32[]{:S(2)}, u32[]{:S(2)}) collective-permute-start(bf16[1,768,384]{2,1,0:T(8,128)(2,1)} %collective-permute-done.68.refs_1_), channel_id=1, source_target_pairs={{8,0},{16,8},{24,16},{28,24},{20,28},{12,20},{4,12},{0,4},{1,9},{9... | collective-permute-start | bytes 1769480 | tf_op jit(solution)/shard_map/ppermute | solution.py:849
  503.6 45.7 %collective-permute-start.32 = (bf16[1024,768]{1,0:T(8,128)(2,1)}, bf16[1024,768]{1,0:T(8,128)(2,1)}, u32[]{:S(2)}, u32[]{:S(2)}) collective-permute-start(bf16[1024,768]{1,0:T(8,128)(2,1)} %copy-done.19), channel_id=1, source_target_pairs={{0,1},{1,0},{2,3},{3,2},{4,5},{5,4},{6,7},{7,6},{8,9},{9,8},{10,11... | collective-permute-start | bytes 4718600 | tf_op jit(solution)/shard_map/ppermute | solution.py:48
  509.9 44.7 %collective-permute-start.53 = (bf16[1024,768]{1,0:T(8,128)(2,1)}, bf16[1024,768]{1,0:T(8,128)(2,1)}, u32[]{:S(2)}, u32[]{:S(2)}) collective-permute-start(bf16[1024,768]{1,0:T(8,128)(2,1)} %convolution_convert_fusion), channel_id=1, source_target_pairs={{0,1},{1,0},{2,3},{3,2},{4,5},{5,4},{6,7},{7,6},{8,9},{9,8},{10,11... | collective-permute-start | bytes 4718600 | tf_op jit(solution)/shard_map/ppermute | solution.py:48
  524.5 24.0 %collective-permute-start.87 = (bf16[1,768,384]{2,1,0:T(8,128)(2,1)S(1)}, bf16[1,768,384]{2,1,0:T(8,128)(2,1)S(1)}, u32[]{:S(2)}, u32[]{:S(2)}) collective-permute-start(bf16[1,768,384]{2,1,0:T(8,128)(2,1)S(1)} %collective-permute-done.84.refs_1_), channel_id=1, source_target_pairs={{8,0},{16,8},{24,16},{28,24},{20,28},{12,20},{4,12},{0,4},{1,9},{9... | collective-permute-start | bytes 1769480 | tf_op jit(solution)/shard_map/ppermute | solution.py:849
  548.5 21.7 %collective-permute-start.90 = (bf16[1,768,384]{2,1,0:T(8,128)(2,1)S(1)}, bf16[1,768,384]{2,1,0:T(8,128)(2,1)S(1)}, u32[]{:S(2)}, u32[]{:S(2)}) collective-permute-start(bf16[1,768,384]{2,1,0:T(8,128)(2,1)S(1)} %collective-permute-done.87.refs_1_), channel_id=1, source_target_pairs={{8,0},{16,8},{24,16},{28,24},{20,28},{12,20},{4,12},{0,4},{1,9},{9... | collective-permute-start | bytes 1769480 | tf_op jit(solution)/shard_map/ppermute | solution.py:849
  552.2 39.2 %collective-permute-start.33 = (bf16[512,768]{1,0:T(8,128)(2,1)}, bf16[512,768]{1,0:T(8,128)(2,1)}, u32[]{:S(2)}, u32[]{:S(2)}) collective-permute-start(bf16[512,768]{1,0:T(8,128)(2,1)} %dynamic-slice_convert_fusion.1), channel_id=1, source_target_pairs={{0,2},{2,0},{1,3},{3,1},{4,6},{6,4},{5,7},{7,5},{8,10},{10,8},{9,1... | collective-permute-start | bytes 2359304 | tf_op jit(solution)/shard_map/ppermute | solution.py:48
  553.3 16.8 %collective-permute-start.88 = (bf16[2,96,896]{2,1,0:T(8,128)(2,1)}, bf16[2,96,896]{2,1,0:T(8,128)(2,1)}, u32[]{:S(2)}, u32[]{:S(2)}) collective-permute-start(bf16[2,96,896]{2,1,0:T(8,128)(2,1)} %collective-permute-done.85.refs_2_), channel_id=1, source_target_pairs={{0,8},{8,16},{16,24},{24,28},{28,20},{20,12},{12,4},{4,0},{9,1},{1... | collective-permute-start | bytes 1032200 | tf_op jit(solution)/shard_map/ppermute | solution.py:849
  554.6 18.7 %collective-permute-start.104 = (bf16[2,96,896]{2,1,0:T(8,128)(2,1)S(1)}, bf16[2,96,896]{2,1,0:T(8,128)(2,1)S(1)}, u32[]{:S(2)}, u32[]{:S(2)}) collective-permute-start(bf16[2,96,896]{2,1,0:T(8,128)(2,1)S(1)} %collective-permute-done.103.refs_10_), channel_id=1, source_target_pairs={{8,0},{16,8},{24,16},{28,24},{20,28},{12,20},{4,12},{0,4},{1,9},{9... | collective-permute-start | bytes 1032200 | tf_op jit(solution)/shard_map/ppermute | solution.py:849
  563.6 19.1 %collective-permute-start.92 = (bf16[1,768,384]{2,1,0:T(8,128)(2,1)}, bf16[1,768,384]{2,1,0:T(8,128)(2,1)S(1)}, u32[]{:S(2)}, u32[]{:S(2)}) collective-permute-start(bf16[1,768,384]{2,1,0:T(8,128)(2,1)} %collective-permute-done.89.refs_0_), channel_id=1, source_target_pairs={{0,8},{8,16},{16,24},{24,28},{28,20},{20,12},{12,4},{4,0},{9,1},{1... | collective-permute-start | bytes 1769480 | tf_op jit(solution)/shard_map/ppermute | solution.py:849
  570.1 21.1 %collective-permute-start.93 = (bf16[1,768,384]{2,1,0:T(8,128)(2,1)S(1)}, bf16[1,768,384]{2,1,0:T(8,128)(2,1)S(1)}, u32[]{:S(2)}, u32[]{:S(2)}) collective-permute-start(bf16[1,768,384]{2,1,0:T(8,128)(2,1)S(1)} %collective-permute-done.90.refs_1_), channel_id=1, source_target_pairs={{8,0},{16,8},{24,16},{28,24},{20,28},{12,20},{4,12},{0,4},{1,9},{9... | collective-permute-start | bytes 1769480 | tf_op jit(solution)/shard_map/ppermute | solution.py:849
  572.3 23.5 %collective-permute-start.54 = (bf16[512,768]{1,0:T(8,128)(2,1)}, bf16[512,768]{1,0:T(8,128)(2,1)}, u32[]{:S(2)}, u32[]{:S(2)}) collective-permute-start(bf16[512,768]{1,0:T(8,128)(2,1)} %dynamic-slice_convert_fusion), channel_id=1, source_target_pairs={{0,2},{2,0},{1,3},{3,1},{4,6},{6,4},{5,7},{7,5},{8,10},{10,8},{9,1... | collective-permute-start | bytes 2359304 | tf_op jit(solution)/shard_map/ppermute | solution.py:48
  591.2 19.5 %collective-permute-start.96 = (bf16[1,768,384]{2,1,0:T(8,128)(2,1)S(1)}, bf16[1,768,384]{2,1,0:T(8,128)(2,1)S(1)}, u32[]{:S(2)}, u32[]{:S(2)}) collective-permute-start(bf16[1,768,384]{2,1,0:T(8,128)(2,1)S(1)} %collective-permute-done.93.refs_1_), channel_id=1, source_target_pairs={{8,0},{16,8},{24,16},{28,24},{20,28},{12,20},{4,12},{0,4},{1,9},{9... | collective-permute-start | bytes 1769480 | tf_op jit(solution)/shard_map/ppermute | solution.py:849
  593.8 16.8 %collective-permute-start.94 = (bf16[2,96,896]{2,1,0:T(8,128)(2,1)}, bf16[2,96,896]{2,1,0:T(8,128)(2,1)S(1)}, u32[]{:S(2)}, u32[]{:S(2)}) collective-permute-start(bf16[2,96,896]{2,1,0:T(8,128)(2,1)} %collective-permute-done.91.refs_4_), channel_id=1, source_target_pairs={{0,8},{8,16},{16,24},{24,28},{28,20},{20,12},{12,4},{4,0},{9,1},{1... | collective-permute-start | bytes 1032200 | tf_op jit(solution)/shard_map/ppermute | solution.py:849
  604.3 30.7 %collective-permute-start.98 = (bf16[1,768,384]{2,1,0:T(8,128)(2,1)S(1)}, bf16[1,768,384]{2,1,0:T(8,128)(2,1)S(1)}, u32[]{:S(2)}, u32[]{:S(2)}) collective-permute-start(bf16[1,768,384]{2,1,0:T(8,128)(2,1)S(1)} %collective-permute-done.95.refs_0_), channel_id=1, source_target_pairs={{0,8},{8,16},{16,24},{24,28},{28,20},{20,12},{12,4},{4,0},{9,1},{1... | collective-permute-start | bytes 1769480 | tf_op jit(solution)/shard_map/ppermute | solution.py:849
  610.7 24.4 %collective-permute-start.99 = (bf16[1,768,384]{2,1,0:T(8,128)(2,1)S(1)}, bf16[1,768,384]{2,1,0:T(8,128)(2,1)S(1)}, u32[]{:S(2)}, u32[]{:S(2)}) collective-permute-start(bf16[1,768,384]{2,1,0:T(8,128)(2,1)S(1)} %collective-permute-done.96.refs_1_), channel_id=1, source_target_pairs={{8,0},{16,8},{24,16},{28,24},{20,28},{12,20},{4,12},{0,4},{1,9},{9... | collective-permute-start | bytes 1769480 | tf_op jit(solution)/shard_map/ppermute | solution.py:849
  613.5 23.6 %collective-permute-start.97 = (bf16[2,96,896]{2,1,0:T(8,128)(2,1)S(1)}, bf16[2,96,896]{2,1,0:T(8,128)(2,1)S(1)}, u32[]{:S(2)}, u32[]{:S(2)}) collective-permute-start(bf16[2,96,896]{2,1,0:T(8,128)(2,1)S(1)} %collective-permute-done.94.refs_5_), channel_id=1, source_target_pairs={{0,8},{8,16},{16,24},{24,28},{28,20},{20,12},{12,4},{4,0},{9,1},{1... | collective-permute-start | bytes 1032200 | tf_op jit(solution)/shard_map/ppermute | solution.py:849
  (139 other events, 1376.1 us)

commit v17 on v16

--- a/solution.py
+++ b/solution.py
@@ -46,6 +46,12 @@
 
 def swap(values, axis):
     return lax.ppermute(values, axis, [(0, 1), (1, 0)])
+
+
+def swap_halves(values):
+    half = values.shape[0] // 2
+    parts = [swap(values[:half], "col"), swap(values[half:], "col")]
+    return jnp.concatenate(parts, axis=0)
 
 
 def halves(values, axis, mine):
@@ -993,7 +999,7 @@
     normed = {}
 
     def work_hidden(order):
-        normed_grad = mixed[True, 0] + swap(mixed[True, 1], "col").astype(F32)
+        normed_grad = mixed[True, 0] + swap_halves(mixed[True, 1]).astype(F32)
         came = swap(normed_grad.astype(BF16), "row")
         normed_grad = normed_grad + after(came, order).astype(F32)
         scaled = normed_grad * norm_gain_ffn
@@ -1004,7 +1010,7 @@
             grad_own.astype(F32) + scale_ffn * scaled - hidden * scale_ffn**3 * mean
         )
         normed["grad"] = normed["hidden"].astype(BF16)
-        normed["grad_c"] = swap(normed["grad"], "col")
+        normed["grad_c"] = swap_halves(normed["grad"])
         return normed["grad"]
 
     def work_attend(order):

time: 663 us -> 638 us (0.962)
  waiting for transfers between devices: 230 us -> 200 us
    ppermute x70, waiting for transfers between devices: 169 us -> 143 us  [send(): return lax.ppermute(values, ('dp', 'col'), routes_of[which])]
    ppermute x33 -> x35, waiting for transfers between devices: 42.9 us -> 38.1 us  [swap(): return lax.ppermute(values, axis, [(0, 1), (1, 0)])]
    ppermute x33 -> x35, starting transfers between devices: 21.1 us -> 19.5 us  [swap(): return lax.ppermute(values, axis, [(0, 1), (1, 0)])]
    unnamed x188 -> x173, local copies, waits for them, and re-layouts: 17.9 us -> 16.9 us
  transfers between devices with their start and end apart: 109 -> 111, of which waited for: 48 -> 46; matrix products, arithmetic and copies ran while one was open for 7% -> 9% of each run, Pallas kernels for 35% -> 36%
where the time goes in v17:
time: 638 us; the launch traced here: 629 us
  Pallas kernels  240 us (38%)
  waiting for transfers between devices  200 us (31%)
  starting transfers between devices  110 us (17%)
  other arithmetic  45.9 us (7%)
  local copies, waits for them, and re-layouts  24.1 us (4%)
    ppermute x70, waiting for transfers between devices, send(): return lax.ppermute(values, ('dp', 'col'), routes_of[which])  143 us
    ppermute x70, starting transfers between devices, send(): return lax.ppermute(values, ('dp', 'col'), routes_of[which])  81.3 us
    pallas_call x9, Pallas kernels, expert_grads(): pl.pallas_call(functools.partial(expert_kernel, shared, aliased, first),...  79.4 us
    pallas_call x4, Pallas kernels, mix(): pl.pallas_call(functools.partial(mix_kernel, back, group), grid_spec=pltp...  39.8 us
    pallas_call x16, Pallas kernels, unpack(): pl.pallas_call(functools.partial(unpack_kernel, aliased), grid_spec=pltpu...  38.2 us
    ppermute x35, waiting for transfers between devices, swap(): return lax.ppermute(values, axis, [(0, 1), (1, 0)])  38.1 us
    convert_element_type x13, other arithmetic, add_rounded(): return (left.astype(F32) + right.astype(F32)).astype(BF16)  26.3 us
    ppermute x35, starting transfers between devices, swap(): return lax.ppermute(values, axis, [(0, 1), (1, 0)])  19.5 us
  transfers between devices with their start and end apart: 111, of which 46 were waited for; matrix products, arithmetic and copies ran while one was open for 9% of the time, Pallas kernels for 36%

profile of v17, /device:TPU:0, one launch (start us, length us, event | category | flops | bytes accessed | tf_op | source)
XLA Modules:
  0.0 628.7 jit_solution(13867767668977714316)
XLA Ops:
  1.8 3.1 their_columns.1
  8.2 5.0 collective-permute-done.2.gains_c_ref.refs_7_
  13.3 2.9 collective-permute-start.4
  18.0 4.5 project.2
  22.5 9.9 %collective-permute-done.4.refs_0_ = bf16[192,768]{1,0:T(8,128)(2,1)S(1)} collective-permute-done((bf16[192,768]{1,0:T(8,128)(2,1)}, bf16[192,768]{1,0:T(8,128)(2,1)S(1)}, u32[]{:S(2)}, u32[]{:S(2)}) %collective-permute-start.4) | collective-permute-done | bytes 294944 | tf_op jit(solution)/shard_map/ppermute | solution.py:48
  40.7 4.5 project.3
  51.3 4.4 collective-permute-done.5.refs_1_
  58.2 6.2 attend.1.refs_4_.refs_5_
  70.0 9.0 %hidden_before.1 = (f32[1024,768]{1,0:T(8,128)}, f32[1024,768]{1,0:T(8,128)}) custom-call(s32[3]{0:T(128)} %copy-done.49, bf16[512,768]{1,0:T(8,128)(2,1)} %refs_0_.2, bf16[512,768]{1,0:T(8,128)(2,1)} %copy-done.68, bf16[512,768]{1,0:T(8,128)(2,1)} %collective-permute-done.own_ref.refs_2_, bf16[512,768]{1,0:T(8,128)(2,1)} %copy-done.69, ...), custom_call_target="tpu_custom_call" | custom-call | flops 2415919104 | bytes 12582912 | tf_op jit(solution)/shard_map/hidden_before/pallas_call | solution.py:404
  79.0 6.3 %collective-permute-done.12.refs_2_ = bf16[1024,384]{1,0:T(8,128)(2,1)} collective-permute-done((bf16[1024,384]{1,0:T(8,128)(2,1)}, bf16[1024,384]{1,0:T(8,128)(2,1)}, u32[]{:S(2)}, u32[]{:S(2)}) %collective-permute-start.12) | collective-permute-done | bytes 786464 | tf_op jit(solution)/shard_map/ppermute | solution.py:48
  88.7 9.4 %hidden_after.1 = (f32[1024,768]{1,0:T(8,128)}, bf16[1024,768]{1,0:T(8,128)(2,1)}, bf16[1024,768]{1,0:T(8,128)(2,1)}, f32[1024,1]{1,0:T(8,128)}) custom-call(s32[3]{0:T(128)} %copy-done.49, f32[1024,768]{1,0:T(8,128)} %get-tuple-element.253.refs_0_, f32[1024,768]{1,0:T(8,128)} %get-tuple-element.254.refs_1_, ...), custom_call_target="tpu_custom_call" | custom-call | tf_op jit(solution)/shard_map/hidden_after/pallas_call | solution.py:426
  101.6 9.1 %expert_grads.9 = (bf16[1,1536,384]{2,1,0:T(8,128)(2,1)S(1)}, bf16[1,1536,384]{2,1,0:T(8,128)(2,1)S(1)}, bf16[8,1024,512]{2,1,0:T(8,128)(2,1)}, bf16[8,1024,256]{2,1,0:T(8,128)(2,1)S(1)}) custom-call(s32[63]{0:T(128)S(1)} %fusion.18.order_ref.plan_ref, bf16[1024,768]{1,0:T(8,128)(2,1)S(1)} %copy-done.5, bf16[1024,768]{1,0:T(8,128)(2,1)S(1)} %copy-done.6, ...), custom_call_target="tpu_custom_call" | custom-call | tf_op jit(solution)/shard_map/expert_grads/pallas_call | solution.py:549
  112.2 8.9 %expert_grads.10 = (bf16[1,1536,384]{2,1,0:T(8,128)(2,1)S(1)}, bf16[1,1536,384]{2,1,0:T(8,128)(2,1)S(1)}, bf16[8,1024,512]{2,1,0:T(8,128)(2,1)}, bf16[8,1024,256]{2,1,0:T(8,128)(2,1)S(1)}) custom-call(s32[63]{0:T(128)S(1)} %fusion.18.order_ref.plan_ref, bf16[1024,768]{1,0:T(8,128)(2,1)S(1)} %copy-done.5, ...), custom_call_target="tpu_custom_call", output_to_operand_aliasing={{2}: (18, {}), {3}: (19, {})} | custom-call | tf_op jit(solution)/shard_map/expert_grads/pallas_call | solution.py:549
  121.5 8.9 %expert_grads.11 = (bf16[1,1536,384]{2,1,0:T(8,128)(2,1)S(1)}, bf16[1,1536,384]{2,1,0:T(8,128)(2,1)S(1)}, bf16[8,1024,512]{2,1,0:T(8,128)(2,1)}, bf16[8,1024,256]{2,1,0:T(8,128)(2,1)S(1)}) custom-call(s32[63]{0:T(128)S(1)} %fusion.18.order_ref.plan_ref, bf16[1024,768]{1,0:T(8,128)(2,1)S(1)} %copy-done.5, ...), custom_call_target="tpu_custom_call", output_to_operand_aliasing={{2}: (18, {}), {3}: (19, {})} | custom-call | tf_op jit(solution)/shard_map/expert_grads/pallas_call | solution.py:549
  133.2 9.3 %expert_grads.12 = (bf16[1,1536,384]{2,1,0:T(8,128)(2,1)S(1)}, bf16[1,1536,384]{2,1,0:T(8,128)(2,1)S(1)}, bf16[8,1024,512]{2,1,0:T(8,128)(2,1)}, bf16[8,1024,256]{2,1,0:T(8,128)(2,1)S(1)}) custom-call(s32[63]{0:T(128)S(1)} %fusion.18.order_ref.plan_ref, bf16[1024,768]{1,0:T(8,128)(2,1)S(1)} %copy-done.5, ...), custom_call_target="tpu_custom_call", output_to_operand_aliasing={{2}: (18, {}), {3}: (19, {})} | custom-call | tf_op jit(solution)/shard_map/expert_grads/pallas_call | solution.py:549
  147.1 8.9 %expert_grads.13 = (bf16[1,1536,384]{2,1,0:T(8,128)(2,1)S(1)}, bf16[1,1536,384]{2,1,0:T(8,128)(2,1)S(1)}, bf16[8,1024,512]{2,1,0:T(8,128)(2,1)}, bf16[8,1024,256]{2,1,0:T(8,128)(2,1)S(1)}) custom-call(s32[63]{0:T(128)S(1)} %fusion.18.order_ref.plan_ref, bf16[1024,768]{1,0:T(8,128)(2,1)S(1)} %copy-done.5, ...), custom_call_target="tpu_custom_call", output_to_operand_aliasing={{2}: (18, {}), {3}: (19, {})} | custom-call | tf_op jit(solution)/shard_map/expert_grads/pallas_call | solution.py:549
  158.2 8.9 %expert_grads.14 = (bf16[1,1536,384]{2,1,0:T(8,128)(2,1)S(1)}, bf16[1,1536,384]{2,1,0:T(8,128)(2,1)S(1)}, bf16[8,1024,512]{2,1,0:T(8,128)(2,1)}, bf16[8,1024,256]{2,1,0:T(8,128)(2,1)S(1)}) custom-call(s32[63]{0:T(128)S(1)} %fusion.18.order_ref.plan_ref, bf16[1024,768]{1,0:T(8,128)(2,1)S(1)} %copy-done.5, ...), custom_call_target="tpu_custom_call", output_to_operand_aliasing={{2}: (18, {}), {3}: (19, {})} | custom-call | tf_op jit(solution)/shard_map/expert_grads/pallas_call | solution.py:549
  172.5 9.0 %expert_grads.15 = (bf16[1,1536,384]{2,1,0:T(8,128)(2,1)S(1)}, bf16[1,1536,384]{2,1,0:T(8,128)(2,1)S(1)}, bf16[8,1024,512]{2,1,0:T(8,128)(2,1)}, bf16[8,1024,256]{2,1,0:T(8,128)(2,1)S(1)}) custom-call(s32[63]{0:T(128)S(1)} %fusion.18.order_ref.plan_ref, bf16[1024,768]{1,0:T(8,128)(2,1)S(1)} %copy-done.5, ...), custom_call_target="tpu_custom_call", output_to_operand_aliasing={{2}: (18, {}), {3}: (19, {})} | custom-call | tf_op jit(solution)/shard_map/expert_grads/pallas_call | solution.py:549
  184.7 8.9 %expert_grads.16 = (bf16[1,1536,384]{2,1,0:T(8,128)(2,1)S(1)}, bf16[1,1536,384]{2,1,0:T(8,128)(2,1)S(1)}, bf16[8,1024,512]{2,1,0:T(8,128)(2,1)}, bf16[8,1024,256]{2,1,0:T(8,128)(2,1)S(1)}) custom-call(s32[63]{0:T(128)S(1)} %fusion.18.order_ref.plan_ref, bf16[1024,768]{1,0:T(8,128)(2,1)S(1)} %copy-done.5, ...), custom_call_target="tpu_custom_call", output_to_operand_aliasing={{2}: (18, {}), {3}: (19, {})} | custom-call | tf_op jit(solution)/shard_map/expert_grads/pallas_call | solution.py:549
  195.6 3.6 add_convert_fusion.8
  200.9 7.7 %expert_grads.17 = (bf16[1,1536,384]{2,1,0:T(8,128)(2,1)S(1)}, bf16[1,1536,384]{2,1,0:T(8,128)(2,1)S(1)}, bf16[1,1024,512]{2,1,0:T(8,128)(2,1)S(1)}, bf16[1,1024,256]{2,1,0:T(8,128)(2,1)S(1)}) custom-call(s32[63]{0:T(128)S(1)} %fusion.18.order_ref.plan_ref, bf16[1024,768]{1,0:T(8,128)(2,1)S(1)} %copy-done.5, bf16[1024,768]{1,0:T(8,128)(2,1)S(1)} %copy-done.7, ...), custom_call_target="tpu_custom_call" | custom-call | tf_op jit(solution)/shard_map/expert_grads/pallas_call | solution.py:549
  211.7 12.8 %mix.4 = bf16[1024,768]{1,0:T(8,128)(2,1)S(1)} custom-call(s32[63]{0:T(128)S(1)} %fusion.18.order_ref.plan_ref, bf16[8,1024,512]{2,1,0:T(8,128)(2,1)} %get-tuple-element.294.refs_0_, bf16[1,1024,512]{2,1,0:T(8,128)(2,1)S(1)} %get-tuple-element.301.refs_1_, ...), custom_call_target="tpu_custom_call" | custom-call | tf_op jit(solution)/shard_map/mix/pallas_call | solution.py:620
  228.7 12.5 %mix.5 = f32[1024,768]{1,0:T(8,128)S(1)} custom-call(s32[63]{0:T(128)S(1)} %fusion.18.order_ref.plan_ref, bf16[8,1024,512]{2,1,0:T(8,128)(2,1)} %get-tuple-element.294.refs_0_, bf16[1,1024,512]{2,1,0:T(8,128)(2,1)S(1)} %get-tuple-element.301.refs_1_, bf16[16,768,256]{2,1,0:T(8,128)(2,1)} %refs_16_.1, bf16[16,768,256]{2,1,0:T(8,128)(2,1)} %refs_17_.1, ...), custom_call_target="tpu_custom_call" | custom-call | tf_op jit(solution)/shard_map/mix/pallas_call | solution.py:620
  244.6 7.2 %mix.6 = bf16[1024,768]{1,0:T(8,128)(2,1)S(1)} custom-call(s32[63]{0:T(128)S(1)} %fusion.18.order_ref.plan_ref, bf16[8,1024,256]{2,1,0:T(8,128)(2,1)} %copy-done, bf16[1,1024,256]{2,1,0:T(8,128)(2,1)S(1)} %get-tuple-element.312.refs_1_, ...), custom_call_target="tpu_custom_call" | custom-call | tf_op jit(solution)/shard_map/mix/pallas_call | solution.py:620
  251.8 3.2 add_convert_fusion.4
  257.0 7.3 %mix.7 = f32[1024,768]{1,0:T(8,128)S(1)} custom-call(s32[63]{0:T(128)S(1)} %fusion.18.order_ref.plan_ref, bf16[8,1024,256]{2,1,0:T(8,128)(2,1)} %copy-done, bf16[1,1024,256]{2,1,0:T(8,128)(2,1)S(1)} %get-tuple-element.312.refs_1_, bf16[16,256,768]{2,1,0:T(8,128)(2,1)} %refs_9_.19, bf16[16,256,768]{2,1,0:T(8,128)(2,1)} %refs_9_.19, ...), custom_call_target="tpu_custom_call" | custom-call | tf_op jit(solution)/shard_map/mix/pallas_call | solution.py:620
  264.3 3.7 add_convert_fusion.3
  268.5 5.1 collective-permute-done.42
  273.6 4.1 collective-permute-done.36
  280.3 3.5 add_convert_fusion.1
  291.9 13.3 %attend_back.1.refs_4_ = bf16[1024,640]{1,0:T(8,128)(2,1)} custom-call(s32[3]{0:T(128)} %copy-done.49, bf16[512,640]{1,0:T(8,128)(2,1)} %get-tuple-element.245.own_ref, bf16[512,640]{1,0:T(8,128)(2,1)} %get-tuple-element.249.other_ref, bf16[1024,768]{1,0:T(8,128)(2,1)} %copy-done.50, bf16[1024,768]{1,0:T(8,128)(2,1)} %constant_dynamic-update-slice_fusion.grad_c_ref.refs_7_, ...), custom_call_target="tpu_custom_call" | custom-call | tf_op jit(solution)/shard_map/attend_back/pallas_call | solution.py:172
  313.5 10.5 %collective-permute-done.44.refs_0_ = bf16[1,768,384]{2,1,0:T(8,128)(2,1)S(1)} collective-permute-done((bf16[1,768,384]{2,1,0:T(8,128)(2,1)S(1)}, bf16[1,768,384]{2,1,0:T(8,128)(2,1)S(1)}, u32[]{:S(2)}, u32[]{:S(2)}) %collective-permute-start.44) | collective-permute-done | bytes 589856 | tf_op jit(solution)/shard_map/ppermute | solution.py:855
  326.1 13.2 %late_grads.1 = (bf16[2,768,896]{2,1,0:T(8,128)(2,1)}, bf16[2,768,896]{2,1,0:T(8,128)(2,1)}) custom-call(s32[3]{0:T(128)} %copy-done.49, bf16[512,768]{1,0:T(8,128)(2,1)} %get-tuple-element.335.refs_0_, bf16[512,768]{1,0:T(8,128)(2,1)} %get-tuple-element.336.refs_1_, bf16[512,768]{1,0:T(8,128)(2,1)} %get-tuple-element.337.refs_2_, ...), custom_call_target="tpu_custom_call" | custom-call | tf_op jit(solution)/shard_map/late_grads/pallas_call | solution.py:223
  346.2 2.7 collective-permute-done.49.refs_0_
  351.7 3.1 unpack.18
  354.8 4.9 collective-permute-done.47.refs_0_
  361.3 4.1 collective-permute-done.52.refs_0_
  371.4 5.6 collective-permute-done.50.refs_0_
  378.6 5.8 collective-permute-done.54.refs_0_
  385.4 4.4 collective-permute-done.75.refs_0_
  392.6 11.3 %collective-permute-done.76.refs_0_ = bf16[2,96,896]{2,1,0:T(8,128)(2,1)S(1)} collective-permute-done((bf16[2,96,896]{2,1,0:T(8,128)(2,1)S(1)}, bf16[2,96,896]{2,1,0:T(8,128)(2,1)S(1)}, u32[]{:S(2)}, u32[]{:S(2)}) %collective-permute-start.76) | collective-permute-done | bytes 344096 | tf_op jit(solution)/shard_map/ppermute | solution.py:855
  416.0 15.9 %collective-permute-done.78.refs_0_ = bf16[2,96,896]{2,1,0:T(8,128)(2,1)S(1)} collective-permute-done((bf16[2,96,896]{2,1,0:T(8,128)(2,1)S(1)}, bf16[2,96,896]{2,1,0:T(8,128)(2,1)S(1)}, u32[]{:S(2)}, u32[]{:S(2)}) %collective-permute-start.78) | collective-permute-done | bytes 344096 | tf_op jit(solution)/shard_map/ppermute | solution.py:855
  444.0 2.8 collective-permute-done.68.refs_0_
  449.6 11.8 %collective-permute-done.80.refs_0_ = bf16[2,96,896]{2,1,0:T(8,128)(2,1)S(1)} collective-permute-done((bf16[2,96,896]{2,1,0:T(8,128)(2,1)S(1)}, bf16[2,96,896]{2,1,0:T(8,128)(2,1)S(1)}, u32[]{:S(2)}, u32[]{:S(2)}) %collective-permute-start.80) | collective-permute-done | bytes 344096 | tf_op jit(solution)/shard_map/ppermute | solution.py:855
  466.4 3.1 unpack.24
  469.5 6.9 %collective-permute-done.71.refs_0_ = bf16[2,96,896]{2,1,0:T(8,128)(2,1)S(1)} collective-permute-done((bf16[2,96,896]{2,1,0:T(8,128)(2,1)S(1)}, bf16[2,96,896]{2,1,0:T(8,128)(2,1)S(1)}, u32[]{:S(2)}, u32[]{:S(2)}) %collective-permute-start.71) | collective-permute-done | bytes 344096 | tf_op jit(solution)/shard_map/ppermute | solution.py:855
  491.0 3.1 unpack.25
  494.1 4.2 collective-permute-done.84.refs_1_
  500.6 6.3 %collective-permute-done.104.refs_9_ = bf16[2,96,896]{2,1,0:T(8,128)(2,1)} collective-permute-done((bf16[2,96,896]{2,1,0:T(8,128)(2,1)S(1)}, bf16[2,96,896]{2,1,0:T(8,128)(2,1)}, u32[]{:S(2)}, u32[]{:S(2)}) %collective-permute-start.104) | collective-permute-done | bytes 344096 | tf_op jit(solution)/shard_map/ppermute | solution.py:855
  510.2 3.5 unpack.26
  516.0 6.0 collective-permute-done.87.refs_2_
  530.5 2.8 convert_add_fusion
  535.7 2.6 collective-permute-done.91.refs_0_
  539.5 4.0 collective-permute-done.90.refs_3_
  543.5 2.9 collective-permute-start.95
  552.4 3.6 collective-permute-done.94.refs_0_
  556.0 2.9 collective-permute-start.107
  558.9 4.6 collective-permute-done.93.refs_4_
  576.8 2.9 collective-permute-done.97.refs_0_
  581.3 3.2 collective-permute-done.96.refs_5_
  590.5 9.6 %collective-permute-done.59 = f32[2,768]{1,0:T(2,128)S(1)} collective-permute-done((f32[2,768]{1,0:T(2,128)S(1)}, f32[2,768]{1,0:T(2,128)S(1)}, u32[]{:S(2)}, u32[]{:S(2)}) %collective-permute-start.59) | collective-permute-done | bytes 6176 | tf_op jit(solution)/shard_map/ppermute | solution.py:1171
  602.1 5.3 collective-permute-done.60
  614.6 2.6 fusion.3
  621.7 6.5 %unpack_late.1 = (f32[768,512]{1,0:T(8,128)}, f32[768,512]{1,0:T(8,128)}, f32[512,768]{1,0:T(8,128)}, f32[768,768]{1,0:T(8,128)}, f32[768,256]{1,0:T(8,128)}, /*index=5*/f32[768,256]{1,0:T(8,128)}, f32[768,768]{1,0:T(8,128)}) custom-call(s32[63]{0:T(128)S(1)} %fusion.18.order_ref.plan_ref, bf16[2,96,896]{2,1,0:T(8,128)(2,1)S(1)} %pad_maximum_fusion.1.refs_0_, ...), custom_call_target="tpu_custom_call" | custom-call | tf_op jit(solution)/shard_map/unpack_late/pallas_call | solution.py:766
  (446 shorter events, 221.9 us)
Async XLA Ops:
  0.7 34.4 %collective-permute-start.16 = (bf16[16,768,256]{2,1,0:T(8,128)(2,1)}, bf16[16,768,256]{2,1,0:T(8,128)(2,1)}, u32[]{:S(2)}, u32[]{:S(2)}) collective-permute-start(bf16[16,768,256]{2,1,0:T(8,128)(2,1)} %refs_16_.1), channel_id=1, source_target_pairs={{0,1},{1,0},{2,3},{3,2},{4,5},{5,4},{6,7},{7,6},{8,9},{9,8},{10,11... | collective-permute-start | bytes 18874376 | tf_op jit(solution)/shard_map/ppermute | solution.py:48
  5.4 27.1 %collective-permute-start = (bf16[512,768]{1,0:T(8,128)(2,1)S(1)}, bf16[512,768]{1,0:T(8,128)(2,1)}, u32[]{:S(2)}, u32[]{:S(2)}) collective-permute-start(bf16[512,768]{1,0:T(8,128)(2,1)S(1)} %copy-done.58), channel_id=1, source_target_pairs={{0,2},{2,0},{1,3},{3,1},{4,6},{6,4},{5,7},{7,5},{8,10},{10,8},{9,1... | collective-permute-start | bytes 2359304 | tf_op jit(solution)/shard_map/ppermute | solution.py:48
  13.3 19.1 %collective-permute-start.4 = (bf16[192,768]{1,0:T(8,128)(2,1)}, bf16[192,768]{1,0:T(8,128)(2,1)S(1)}, u32[]{:S(2)}, u32[]{:S(2)}) collective-permute-start(bf16[192,768]{1,0:T(8,128)(2,1)} %get-tuple-element.246), channel_id=1, source_target_pairs={{0,2},{2,0},{1,3},{3,1},{4,6},{6,4},{5,7},{7,5},{8,10},{10,8},{9,1... | collective-permute-start | bytes 884744 | tf_op jit(solution)/shard_map/ppermute | solution.py:48
  34.9 63.3 %collective-permute-start.18 = (bf16[16,256,768]{2,1,0:T(8,128)(2,1)}, bf16[16,256,768]{2,1,0:T(8,128)(2,1)}, u32[]{:S(2)}, u32[]{:S(2)}) collective-permute-start(bf16[16,256,768]{2,1,0:T(8,128)(2,1)} %refs_9_.19), channel_id=1, source_target_pairs={{0,1},{1,0},{2,3},{3,2},{4,5},{5,4},{6,7},{7,6},{8,9},{9,8},{10,11... | collective-permute-start | bytes 18874376 | tf_op jit(solution)/shard_map/ppermute | solution.py:48
  35.8 62.4 %collective-permute-start.17 = (bf16[16,768,256]{2,1,0:T(8,128)(2,1)}, bf16[16,768,256]{2,1,0:T(8,128)(2,1)}, u32[]{:S(2)}, u32[]{:S(2)}) collective-permute-start(bf16[16,768,256]{2,1,0:T(8,128)(2,1)} %refs_17_.1), channel_id=1, source_target_pairs={{0,1},{1,0},{2,3},{3,2},{4,5},{5,4},{6,7},{7,6},{8,9},{9,8},{10,11... | collective-permute-start | bytes 18874376 | tf_op jit(solution)/shard_map/ppermute | solution.py:48
  35.9 19.8 %collective-permute-start.5 = (bf16[512,768]{1,0:T(8,128)(2,1)S(1)}, bf16[512,768]{1,0:T(8,128)(2,1)S(1)}, u32[]{:S(2)}, u32[]{:S(2)}) collective-permute-start(bf16[512,768]{1,0:T(8,128)(2,1)S(1)} %copy-done.36), channel_id=1, source_target_pairs={{0,2},{2,0},{1,3},{3,1},{4,6},{6,4},{5,7},{7,5},{8,10},{10,8},{9,1... | collective-permute-start | bytes 2359304 | tf_op jit(solution)/shard_map/ppermute | solution.py:48
  51.3 17.6 %collective-permute-start.11 = (bf16[768,768]{1,0:T(8,128)(2,1)}, bf16[768,768]{1,0:T(8,128)(2,1)}, u32[]{:S(2)}, u32[]{:S(2)}) collective-permute-start(bf16[768,768]{1,0:T(8,128)(2,1)} %out_ref.1), channel_id=1, source_target_pairs={{0,1},{1,0},{2,3},{3,2},{4,5},{5,4},{6,7},{7,6},{8,9},{9,8},{10,11... | collective-permute-start | bytes 3538952 | tf_op jit(solution)/shard_map/ppermute | solution.py:48
  65.1 20.3 %collective-permute-start.12 = (bf16[1024,384]{1,0:T(8,128)(2,1)}, bf16[1024,384]{1,0:T(8,128)(2,1)}, u32[]{:S(2)}, u32[]{:S(2)}) collective-permute-start(bf16[1024,384]{1,0:T(8,128)(2,1)} %attend.1.refs_4_.refs_5_), channel_id=1, source_target_pairs={{0,2},{2,0},{1,3},{3,1},{4,6},{6,4},{5,7},{7,5},{8,10},{10,8},{9,1... | collective-permute-start | bytes 2359304 | tf_op jit(solution)/shard_map/ppermute | solution.py:48
  67.7 30.4 %collective-permute-start.15 = (bf16[1024,768]{1,0:T(8,128)(2,1)S(1)}, bf16[1024,768]{1,0:T(8,128)(2,1)S(1)}, u32[]{:S(2)}, u32[]{:S(2)}) collective-permute-start(bf16[1024,768]{1,0:T(8,128)(2,1)S(1)} %join.3.refs_2_), channel_id=1, source_target_pairs={{0,1},{1,0},{2,3},{3,2},{4,5},{5,4},{6,7},{7,6},{8,9},{9,8},{10,11... | collective-permute-start | bytes 4718600 | tf_op jit(solution)/shard_map/ppermute | solution.py:48
  69.0 16.6 %collective-permute-start.14 = (bf16[768,768]{1,0:T(8,128)(2,1)}, bf16[768,768]{1,0:T(8,128)(2,1)}, u32[]{:S(2)}, u32[]{:S(2)}) collective-permute-start(bf16[768,768]{1,0:T(8,128)(2,1)} %join.2.refs_4_), channel_id=1, source_target_pairs={{0,1},{1,0},{2,3},{3,2},{4,5},{5,4},{6,7},{7,6},{8,9},{9,8},{10,11... | collective-permute-start | bytes 3538952 | tf_op jit(solution)/shard_map/ppermute | solution.py:48
  110.6 19.8 %collective-permute-start.19 = (bf16[1,1536,384]{2,1,0:T(8,128)(2,1)S(1)}, bf16[1,1536,384]{2,1,0:T(8,128)(2,1)S(1)}, u32[]{:S(2)}, u32[]{:S(2)}) collective-permute-start(bf16[1,1536,384]{2,1,0:T(8,128)(2,1)S(1)} %get-tuple-element.261), channel_id=1, source_target_pairs={{0,8},{8,16},{16,24},{24,28},{28,20},{20,12},{12,4},{4,0},{9,1},{1... | collective-permute-start | bytes 3538952 | tf_op jit(solution)/shard_map/ppermute | solution.py:855
  121.1 23.2 %collective-permute-start.21 = (bf16[1,1536,384]{2,1,0:T(8,128)(2,1)S(1)}, bf16[1,1536,384]{2,1,0:T(8,128)(2,1)S(1)}, u32[]{:S(2)}, u32[]{:S(2)}) collective-permute-start(bf16[1,1536,384]{2,1,0:T(8,128)(2,1)S(1)} %get-tuple-element.271), channel_id=1, source_target_pairs={{8,0},{16,8},{24,16},{28,24},{20,28},{12,20},{4,12},{0,4},{1,9},{9... | collective-permute-start | bytes 3538952 | tf_op jit(solution)/shard_map/ppermute | solution.py:855
  130.7 25.2 %collective-permute-start.20 = (bf16[1,1536,384]{2,1,0:T(8,128)(2,1)S(1)}, bf16[1,1536,384]{2,1,0:T(8,128)(2,1)S(1)}, u32[]{:S(2)}, u32[]{:S(2)}) collective-permute-start(bf16[1,1536,384]{2,1,0:T(8,128)(2,1)S(1)} %add_convert_fusion.13), channel_id=1, source_target_pairs={{0,8},{8,16},{16,24},{24,28},{28,20},{20,12},{12,4},{4,0},{9,1},{1... | collective-permute-start | bytes 3538952 | tf_op jit(solution)/shard_map/ppermute | solution.py:855
  145.6 23.8 %collective-permute-start.23 = (bf16[1,1536,384]{2,1,0:T(8,128)(2,1)}, bf16[1,1536,384]{2,1,0:T(8,128)(2,1)S(1)}, u32[]{:S(2)}, u32[]{:S(2)}) collective-permute-start(bf16[1,1536,384]{2,1,0:T(8,128)(2,1)} %add_convert_fusion.12), channel_id=1, source_target_pairs={{8,0},{16,8},{24,16},{28,24},{20,28},{12,20},{4,12},{0,4},{1,9},{9... | collective-permute-start | bytes 3538952 | tf_op jit(solution)/shard_map/ppermute | solution.py:855
  156.3 25.3 %collective-permute-start.22 = (bf16[1,1536,384]{2,1,0:T(8,128)(2,1)S(1)}, bf16[1,1536,384]{2,1,0:T(8,128)(2,1)S(1)}, u32[]{:S(2)}, u32[]{:S(2)}) collective-permute-start(bf16[1,1536,384]{2,1,0:T(8,128)(2,1)S(1)} %add_convert_fusion.11), channel_id=1, source_target_pairs={{0,8},{8,16},{16,24},{24,28},{28,20},{20,12},{12,4},{4,0},{9,1},{1... | collective-permute-start | bytes 3538952 | tf_op jit(solution)/shard_map/ppermute | solution.py:855
  170.8 24.8 %collective-permute-start.25 = (bf16[1,1536,384]{2,1,0:T(8,128)(2,1)}, bf16[1,1536,384]{2,1,0:T(8,128)(2,1)}, u32[]{:S(2)}, u32[]{:S(2)}) collective-permute-start(bf16[1,1536,384]{2,1,0:T(8,128)(2,1)} %add_convert_fusion.10), channel_id=1, source_target_pairs={{8,0},{16,8},{24,16},{28,24},{20,28},{12,20},{4,12},{0,4},{1,9},{9... | collective-permute-start | bytes 3538952 | tf_op jit(solution)/shard_map/ppermute | solution.py:855
  183.0 25.7 %collective-permute-start.24 = (bf16[1,1536,384]{2,1,0:T(8,128)(2,1)}, bf16[1,1536,384]{2,1,0:T(8,128)(2,1)}, u32[]{:S(2)}, u32[]{:S(2)}) collective-permute-start(bf16[1,1536,384]{2,1,0:T(8,128)(2,1)} %add_convert_fusion.9), channel_id=1, source_target_pairs={{0,8},{8,16},{16,24},{24,28},{28,20},{20,12},{12,4},{4,0},{9,1},{1... | collective-permute-start | bytes 3538952 | tf_op jit(solution)/shard_map/ppermute | solution.py:855
  184.1 16.7 %collective-permute-start.26 = (bf16[1,768,512]{2,1,0:T(8,128)(2,1)S(1)}, bf16[1,768,512]{2,1,0:T(8,128)(2,1)S(1)}, u32[]{:S(2)}, u32[]{:S(2)}) collective-permute-start(bf16[1,768,512]{2,1,0:T(8,128)(2,1)S(1)} %bitcast.55), channel_id=1, source_target_pairs={{0,1},{1,0},{2,3},{3,2},{4,5},{5,4},{6,7},{7,6},{8,9},{9,8},{10,11... | collective-permute-start | bytes 2359304 | tf_op jit(solution)/shard_map/ppermute | solution.py:48
  184.1 16.7 %collective-permute-start.27 = (bf16[1,768,512]{2,1,0:T(8,128)(2,1)S(1)}, bf16[1,768,512]{2,1,0:T(8,128)(2,1)S(1)}, u32[]{:S(2)}, u32[]{:S(2)}) collective-permute-start(bf16[1,768,512]{2,1,0:T(8,128)(2,1)S(1)} %bitcast.60), channel_id=1, source_target_pairs={{0,1},{1,0},{2,3},{3,2},{4,5},{5,4},{6,7},{7,6},{8,9},{9,8},{10,11... | collective-permute-start | bytes 2359304 | tf_op jit(solution)/shard_map/ppermute | solution.py:48
  199.3 25.4 %collective-permute-start.30 = (bf16[1,1536,384]{2,1,0:T(8,128)(2,1)}, bf16[1,1536,384]{2,1,0:T(8,128)(2,1)S(1)}, u32[]{:S(2)}, u32[]{:S(2)}) collective-permute-start(bf16[1,1536,384]{2,1,0:T(8,128)(2,1)} %add_convert_fusion.8), channel_id=1, source_target_pairs={{8,0},{16,8},{24,16},{28,24},{20,28},{12,20},{4,12},{0,4},{1,9},{9... | collective-permute-start | bytes 3538952 | tf_op jit(solution)/shard_map/ppermute | solution.py:855
  211.2 31.6 %collective-permute-start.29 = (bf16[1,1536,384]{2,1,0:T(8,128)(2,1)S(1)}, bf16[1,1536,384]{2,1,0:T(8,128)(2,1)S(1)}, u32[]{:S(2)}, u32[]{:S(2)}) collective-permute-start(bf16[1,1536,384]{2,1,0:T(8,128)(2,1)S(1)} %add_convert_fusion.7), channel_id=1, source_target_pairs={{0,8},{8,16},{16,24},{24,28},{28,20},{20,12},{12,4},{4,0},{9,1},{1... | collective-permute-start | bytes 3538952 | tf_op jit(solution)/shard_map/ppermute | solution.py:855
  224.6 16.6 %collective-permute-start.34 = (bf16[512,768]{1,0:T(8,128)(2,1)S(1)}, bf16[512,768]{1,0:T(8,128)(2,1)S(1)}, u32[]{:S(2)}, u32[]{:S(2)}) collective-permute-start(bf16[512,768]{1,0:T(8,128)(2,1)S(1)} %get-tuple-element.490), channel_id=1, source_target_pairs={{0,1},{1,0},{2,3},{3,2},{4,5},{5,4},{6,7},{7,6},{8,9},{9,8},{10,11... | collective-permute-start | bytes 2359304 | tf_op jit(solution)/shard_map/ppermute | solution.py:48
  227.1 24.7 %collective-permute-start.31 = (bf16[1,1536,384]{2,1,0:T(8,128)(2,1)}, bf16[1,1536,384]{2,1,0:T(8,128)(2,1)}, u32[]{:S(2)}, u32[]{:S(2)}) collective-permute-start(bf16[1,1536,384]{2,1,0:T(8,128)(2,1)} %add_convert_fusion.6), channel_id=1, source_target_pairs={{8,0},{16,8},{24,16},{28,24},{20,28},{12,20},{4,12},{0,4},{1,9},{9... | collective-permute-start | bytes 3538952 | tf_op jit(solution)/shard_map/ppermute | solution.py:855
  241.6 36.1 %collective-permute-start.36 = (bf16[1024,768]{1,0:T(8,128)(2,1)S(1)}, bf16[1024,768]{1,0:T(8,128)(2,1)}, u32[]{:S(2)}, u32[]{:S(2)}) collective-permute-start(bf16[1024,768]{1,0:T(8,128)(2,1)S(1)} %fusion), channel_id=1, source_target_pairs={{0,2},{2,0},{1,3},{3,1},{4,6},{6,4},{5,7},{7,5},{8,10},{10,8},{9,1... | collective-permute-start | bytes 4718600 | tf_op jit(solution)/shard_map/ppermute | solution.py:48
  244.1 20.2 %collective-permute-start.40 = (bf16[1,1536,384]{2,1,0:T(8,128)(2,1)}, bf16[1,1536,384]{2,1,0:T(8,128)(2,1)}, u32[]{:S(2)}, u32[]{:S(2)}) collective-permute-start(bf16[1,1536,384]{2,1,0:T(8,128)(2,1)} %add_convert_fusion.5), channel_id=1, source_target_pairs={{0,8},{8,16},{16,24},{24,28},{28,20},{20,12},{12,4},{4,0},{9,1},{1... | collective-permute-start | bytes 3538952 | tf_op jit(solution)/shard_map/ppermute | solution.py:855
  255.0 18.5 %collective-permute-start.42 = (bf16[1,1536,384]{2,1,0:T(8,128)(2,1)}, bf16[1,1536,384]{2,1,0:T(8,128)(2,1)}, u32[]{:S(2)}, u32[]{:S(2)}) collective-permute-start(bf16[1,1536,384]{2,1,0:T(8,128)(2,1)} %add_convert_fusion.4), channel_id=1, source_target_pairs={{8,0},{16,8},{24,16},{28,24},{20,28},{12,20},{4,12},{0,4},{1,9},{9... | collective-permute-start | bytes 3538952 | tf_op jit(solution)/shard_map/ppermute | solution.py:855
  268.0 37.1 %collective-permute-start.41 = (bf16[1,1536,384]{2,1,0:T(8,128)(2,1)}, bf16[1,1536,384]{2,1,0:T(8,128)(2,1)}, u32[]{:S(2)}, u32[]{:S(2)}) collective-permute-start(bf16[1,1536,384]{2,1,0:T(8,128)(2,1)} %add_convert_fusion.3), channel_id=1, source_target_pairs={{0,8},{8,16},{16,24},{24,28},{28,20},{20,12},{12,4},{4,0},{9,1},{1... | collective-permute-start | bytes 3538952 | tf_op jit(solution)/shard_map/ppermute | solution.py:855
  283.8 21.4 %collective-permute-start.43 = (bf16[1,1536,384]{2,1,0:T(8,128)(2,1)}, bf16[1,1536,384]{2,1,0:T(8,128)(2,1)}, u32[]{:S(2)}, u32[]{:S(2)}) collective-permute-start(bf16[1,1536,384]{2,1,0:T(8,128)(2,1)} %add_convert_fusion.1), channel_id=1, source_target_pairs={{8,0},{16,8},{24,16},{28,24},{20,28},{12,20},{4,12},{0,4},{1,9},{9... | collective-permute-start | bytes 3538952 | tf_op jit(solution)/shard_map/ppermute | solution.py:855
  324.0 21.3 %collective-permute-start.45 = (bf16[1,768,384]{2,1,0:T(8,128)(2,1)S(1)}, bf16[1,768,384]{2,1,0:T(8,128)(2,1)}, u32[]{:S(2)}, u32[]{:S(2)}) collective-permute-start(bf16[1,768,384]{2,1,0:T(8,128)(2,1)S(1)} %collective-permute-done.44.refs_0_), channel_id=1, source_target_pairs={{0,8},{8,16},{16,24},{24,28},{28,20},{20,12},{12,4},{4,0},{9,1},{1... | collective-permute-start | bytes 1769480 | tf_op jit(solution)/shard_map/ppermute | solution.py:855
  325.6 24.0 %collective-permute-start.48 = (bf16[1,768,384]{2,1,0:T(8,128)(2,1)S(1)}, bf16[1,768,384]{2,1,0:T(8,128)(2,1)S(1)}, u32[]{:S(2)}, u32[]{:S(2)}) collective-permute-start(bf16[1,768,384]{2,1,0:T(8,128)(2,1)S(1)} %collective-permute-done.46.refs_1_), channel_id=1, source_target_pairs={{8,0},{16,8},{24,16},{28,24},{20,28},{12,20},{4,12},{0,4},{1,9},{9... | collective-permute-start | bytes 1769480 | tf_op jit(solution)/shard_map/ppermute | solution.py:855
  359.8 17.2 %collective-permute-start.50 = (bf16[1,768,384]{2,1,0:T(8,128)(2,1)S(1)}, bf16[1,768,384]{2,1,0:T(8,128)(2,1)S(1)}, u32[]{:S(2)}, u32[]{:S(2)}) collective-permute-start(bf16[1,768,384]{2,1,0:T(8,128)(2,1)S(1)} %collective-permute-done.47.refs_0_), channel_id=1, source_target_pairs={{0,8},{8,16},{16,24},{24,28},{28,20},{20,12},{12,4},{4,0},{9,1},{1... | collective-permute-start | bytes 1769480 | tf_op jit(solution)/shard_map/ppermute | solution.py:855
  366.1 18.9 %collective-permute-start.53 = (bf16[1,768,384]{2,1,0:T(8,128)(2,1)S(1)}, bf16[1,768,384]{2,1,0:T(8,128)(2,1)S(1)}, u32[]{:S(2)}, u32[]{:S(2)}) collective-permute-start(bf16[1,768,384]{2,1,0:T(8,128)(2,1)S(1)} %collective-permute-done.51.refs_1_), channel_id=1, source_target_pairs={{8,0},{16,8},{24,16},{28,24},{20,28},{12,20},{4,12},{0,4},{1,9},{9... | collective-permute-start | bytes 1769480 | tf_op jit(solution)/shard_map/ppermute | solution.py:855
  366.6 17.8 %collective-permute-start.54 = (bf16[2,96,896]{2,1,0:T(8,128)(2,1)S(1)}, bf16[2,96,896]{2,1,0:T(8,128)(2,1)S(1)}, u32[]{:S(2)}, u32[]{:S(2)}) collective-permute-start(bf16[2,96,896]{2,1,0:T(8,128)(2,1)S(1)} %late_chunk.18), channel_id=1, source_target_pairs={{0,8},{8,16},{16,24},{24,28},{28,20},{20,12},{12,4},{4,0},{9,1},{1... | collective-permute-start | bytes 1032200 | tf_op jit(solution)/shard_map/ppermute | solution.py:855
  368.8 21.0 %collective-permute-start.75 = (bf16[2,96,896]{2,1,0:T(8,128)(2,1)S(1)}, bf16[2,96,896]{2,1,0:T(8,128)(2,1)S(1)}, u32[]{:S(2)}, u32[]{:S(2)}) collective-permute-start(bf16[2,96,896]{2,1,0:T(8,128)(2,1)S(1)} %late_chunk.24), channel_id=1, source_target_pairs={{8,0},{16,8},{24,16},{28,24},{20,28},{12,20},{4,12},{0,4},{1,9},{9... | collective-permute-start | bytes 1032200 | tf_op jit(solution)/shard_map/ppermute | solution.py:855
  377.0 30.3 %collective-permute-start.63 = (bf16[1,768,384]{2,1,0:T(8,128)(2,1)S(1)}, bf16[1,768,384]{2,1,0:T(8,128)(2,1)S(1)}, u32[]{:S(2)}, u32[]{:S(2)}) collective-permute-start(bf16[1,768,384]{2,1,0:T(8,128)(2,1)S(1)} %collective-permute-done.50.refs_0_), channel_id=1, source_target_pairs={{0,8},{8,16},{16,24},{24,28},{28,20},{20,12},{12,4},{4,0},{9,1},{1... | collective-permute-start | bytes 1769480 | tf_op jit(solution)/shard_map/ppermute | solution.py:855
  385.1 24.4 %collective-permute-start.64 = (bf16[1,768,384]{2,1,0:T(8,128)(2,1)S(1)}, bf16[1,768,384]{2,1,0:T(8,128)(2,1)S(1)}, u32[]{:S(2)}, u32[]{:S(2)}) collective-permute-start(bf16[1,768,384]{2,1,0:T(8,128)(2,1)S(1)} %collective-permute-done.53.refs_1_), channel_id=1, source_target_pairs={{8,0},{16,8},{24,16},{28,24},{20,28},{12,20},{4,12},{0,4},{1,9},{9... | collective-permute-start | bytes 1769480 | tf_op jit(solution)/shard_map/ppermute | solution.py:855
  391.0 17.8 %collective-permute-start.62 = (bf16[2,96,896]{2,1,0:T(8,128)(2,1)S(1)}, bf16[2,96,896]{2,1,0:T(8,128)(2,1)S(1)}, u32[]{:S(2)}, u32[]{:S(2)}) collective-permute-start(bf16[2,96,896]{2,1,0:T(8,128)(2,1)S(1)} %late_chunk.19), channel_id=1, source_target_pairs={{0,8},{8,16},{16,24},{24,28},{28,20},{20,12},{12,4},{4,0},{9,1},{1... | collective-permute-start | bytes 1032200 | tf_op jit(solution)/shard_map/ppermute | solution.py:855
  407.3 25.5 %collective-permute-start.66 = (bf16[1,768,384]{2,1,0:T(8,128)(2,1)S(1)}, bf16[1,768,384]{2,1,0:T(8,128)(2,1)S(1)}, u32[]{:S(2)}, u32[]{:S(2)}) collective-permute-start(bf16[1,768,384]{2,1,0:T(8,128)(2,1)S(1)} %collective-permute-done.63.refs_0_), channel_id=1, source_target_pairs={{0,8},{8,16},{16,24},{24,28},{28,20},{20,12},{12,4},{4,0},{9,1},{1... | collective-permute-start | bytes 1769480 | tf_op jit(solution)/shard_map/ppermute | solution.py:855
  409.5 26.6 %collective-permute-start.67 = (bf16[1,768,384]{2,1,0:T(8,128)(2,1)S(1)}, bf16[1,768,384]{2,1,0:T(8,128)(2,1)S(1)}, u32[]{:S(2)}, u32[]{:S(2)}) collective-permute-start(bf16[1,768,384]{2,1,0:T(8,128)(2,1)S(1)} %collective-permute-done.64.refs_1_), channel_id=1, source_target_pairs={{8,0},{16,8},{24,16},{28,24},{20,28},{12,20},{4,12},{0,4},{1,9},{9... | collective-permute-start | bytes 1769480 | tf_op jit(solution)/shard_map/ppermute | solution.py:855
  412.6 19.3 %collective-permute-start.78 = (bf16[2,96,896]{2,1,0:T(8,128)(2,1)S(1)}, bf16[2,96,896]{2,1,0:T(8,128)(2,1)S(1)}, u32[]{:S(2)}, u32[]{:S(2)}) collective-permute-start(bf16[2,96,896]{2,1,0:T(8,128)(2,1)S(1)} %late_chunk.27), channel_id=1, source_target_pairs={{8,0},{16,8},{24,16},{28,24},{20,28},{12,20},{4,12},{0,4},{1,9},{9... | collective-permute-start | bytes 1032200 | tf_op jit(solution)/shard_map/ppermute | solution.py:855
  413.2 22.2 %collective-permute-start.65 = (bf16[2,96,896]{2,1,0:T(8,128)(2,1)S(1)}, bf16[2,96,896]{2,1,0:T(8,128)(2,1)S(1)}, u32[]{:S(2)}, u32[]{:S(2)}) collective-permute-start(bf16[2,96,896]{2,1,0:T(8,128)(2,1)S(1)} %late_chunk.20), channel_id=1, source_target_pairs={{0,8},{8,16},{16,24},{24,28},{28,20},{20,12},{12,4},{4,0},{9,1},{1... | collective-permute-start | bytes 1032200 | tf_op jit(solution)/shard_map/ppermute | solution.py:855
  414.7 23.5 %collective-permute-start.69 = (bf16[1,768,384]{2,1,0:T(8,128)(2,1)S(1)}, bf16[1,768,384]{2,1,0:T(8,128)(2,1)S(1)}, u32[]{:S(2)}, u32[]{:S(2)}) collective-permute-start(bf16[1,768,384]{2,1,0:T(8,128)(2,1)S(1)} %copy-done.72), channel_id=1, source_target_pairs={{0,1},{1,0},{2,3},{3,2},{4,5},{5,4},{6,7},{7,6},{8,9},{9,8},{10,11... | collective-permute-start | bytes 1769480 | tf_op jit(solution)/shard_map/ppermute | solution.py:48
  431.9 17.5 %collective-permute-start.70 = (bf16[1,768,384]{2,1,0:T(8,128)(2,1)S(1)}, bf16[1,768,384]{2,1,0:T(8,128)(2,1)}, u32[]{:S(2)}, u32[]{:S(2)}) collective-permute-start(bf16[1,768,384]{2,1,0:T(8,128)(2,1)S(1)} %copy-done.71), channel_id=1, source_target_pairs={{0,1},{1,0},{2,3},{3,2},{4,5},{5,4},{6,7},{7,6},{8,9},{9,8},{10,11... | collective-permute-start | bytes 1769480 | tf_op jit(solution)/shard_map/ppermute | solution.py:48
  437.8 24.8 %collective-permute-start.74 = (bf16[1,768,384]{2,1,0:T(8,128)(2,1)S(1)}, bf16[1,768,384]{2,1,0:T(8,128)(2,1)S(1)}, u32[]{:S(2)}, u32[]{:S(2)}) collective-permute-start(bf16[1,768,384]{2,1,0:T(8,128)(2,1)S(1)} %collective-permute-done.67.refs_1_), channel_id=1, source_target_pairs={{8,0},{16,8},{24,16},{28,24},{20,28},{12,20},{4,12},{0,4},{1,9},{9... | collective-permute-start | bytes 1769480 | tf_op jit(solution)/shard_map/ppermute | solution.py:855
  438.2 26.1 %collective-permute-start.73 = (bf16[1,768,384]{2,1,0:T(8,128)(2,1)S(1)}, bf16[1,768,384]{2,1,0:T(8,128)(2,1)S(1)}, u32[]{:S(2)}, u32[]{:S(2)}) collective-permute-start(bf16[1,768,384]{2,1,0:T(8,128)(2,1)S(1)} %collective-permute-done.66.refs_0_), channel_id=1, source_target_pairs={{0,8},{8,16},{16,24},{24,28},{28,20},{20,12},{12,4},{4,0},{9,1},{1... | collective-permute-start | bytes 1769480 | tf_op jit(solution)/shard_map/ppermute | solution.py:855
  441.9 27.6 %collective-permute-start.72 = (bf16[1,768,384]{2,1,0:T(8,128)(2,1)S(1)}, bf16[1,768,384]{2,1,0:T(8,128)(2,1)S(1)}, u32[]{:S(2)}, u32[]{:S(2)}) collective-permute-start(bf16[1,768,384]{2,1,0:T(8,128)(2,1)S(1)} %collective-permute-done.69.refs_0_), channel_id=1, source_target_pairs={{0,8},{8,16},{16,24},{24,28},{28,20},{20,12},{12,4},{4,0},{9,1},{1... | collective-permute-start | bytes 1769480 | tf_op jit(solution)/shard_map/ppermute | solution.py:855
  449.5 27.0 %collective-permute-start.71 = (bf16[2,96,896]{2,1,0:T(8,128)(2,1)S(1)}, bf16[2,96,896]{2,1,0:T(8,128)(2,1)S(1)}, u32[]{:S(2)}, u32[]{:S(2)}) collective-permute-start(bf16[2,96,896]{2,1,0:T(8,128)(2,1)S(1)} %late_chunk.22), channel_id=1, source_target_pairs={{0,8},{8,16},{16,24},{24,28},{28,20},{20,12},{12,4},{4,0},{9,1},{1... | collective-permute-start | bytes 1032200 | tf_op jit(solution)/shard_map/ppermute | solution.py:855
  461.4 19.0 %collective-permute-start.82 = (bf16[1,768,384]{2,1,0:T(8,128)(2,1)}, bf16[1,768,384]{2,1,0:T(8,128)(2,1)}, u32[]{:S(2)}, u32[]{:S(2)}) collective-permute-start(bf16[1,768,384]{2,1,0:T(8,128)(2,1)} %collective-permute-done.70.refs_1_), channel_id=1, source_target_pairs={{8,0},{16,8},{24,16},{28,24},{20,28},{12,20},{4,12},{0,4},{1,9},{9... | collective-permute-start | bytes 1769480 | tf_op jit(solution)/shard_map/ppermute | solution.py:855
  462.5 17.8 %collective-permute-start.81 = (bf16[2,96,896]{2,1,0:T(8,128)(2,1)S(1)}, bf16[2,96,896]{2,1,0:T(8,128)(2,1)}, u32[]{:S(2)}, u32[]{:S(2)}) collective-permute-start(bf16[2,96,896]{2,1,0:T(8,128)(2,1)S(1)} %late_chunk.30), channel_id=1, source_target_pairs={{8,0},{16,8},{24,16},{28,24},{20,28},{12,20},{4,12},{0,4},{1,9},{9... | collective-permute-start | bytes 1032200 | tf_op jit(solution)/shard_map/ppermute | solution.py:855
  477.9 46.2 %collective-permute-start.32 = (bf16[1024,768]{1,0:T(8,128)(2,1)}, bf16[1024,768]{1,0:T(8,128)(2,1)}, u32[]{:S(2)}, u32[]{:S(2)}) collective-permute-start(bf16[1024,768]{1,0:T(8,128)(2,1)} %copy-done.19), channel_id=1, source_target_pairs={{0,1},{1,0},{2,3},{3,2},{4,5},{5,4},{6,7},{7,6},{8,9},{9,8},{10,11... | collective-permute-start | bytes 4718600 | tf_op jit(solution)/shard_map/ppermute | solution.py:48
  485.6 43.9 %collective-permute-start.55 = (bf16[1024,768]{1,0:T(8,128)(2,1)}, bf16[1024,768]{1,0:T(8,128)(2,1)}, u32[]{:S(2)}, u32[]{:S(2)}) collective-permute-start(bf16[1024,768]{1,0:T(8,128)(2,1)} %convolution_convert_fusion), channel_id=1, source_target_pairs={{0,1},{1,0},{2,3},{3,2},{4,5},{5,4},{6,7},{7,6},{8,9},{9,8},{10,11... | collective-permute-start | bytes 4718600 | tf_op jit(solution)/shard_map/ppermute | solution.py:48
  488.8 18.1 %collective-permute-start.104 = (bf16[2,96,896]{2,1,0:T(8,128)(2,1)S(1)}, bf16[2,96,896]{2,1,0:T(8,128)(2,1)}, u32[]{:S(2)}, u32[]{:S(2)}) collective-permute-start(bf16[2,96,896]{2,1,0:T(8,128)(2,1)S(1)} %pad_maximum_fusion.2.refs_8_), channel_id=1, source_target_pairs={{8,0},{16,8},{24,16},{28,24},{20,28},{12,20},{4,12},{0,4},{1,9},{9... | collective-permute-start | bytes 1032200 | tf_op jit(solution)/shard_map/ppermute | solution.py:855
  499.9 23.3 %collective-permute-start.89 = (bf16[1,768,384]{2,1,0:T(8,128)(2,1)S(1)}, bf16[1,768,384]{2,1,0:T(8,128)(2,1)S(1)}, u32[]{:S(2)}, u32[]{:S(2)}) collective-permute-start(bf16[1,768,384]{2,1,0:T(8,128)(2,1)S(1)} %collective-permute-done.86.refs_1_), channel_id=1, source_target_pairs={{8,0},{16,8},{24,16},{28,24},{20,28},{12,20},{4,12},{0,4},{1,9},{9... | collective-permute-start | bytes 1769480 | tf_op jit(solution)/shard_map/ppermute | solution.py:855
  523.2 20.2 %collective-permute-start.92 = (bf16[1,768,384]{2,1,0:T(8,128)(2,1)S(1)}, bf16[1,768,384]{2,1,0:T(8,128)(2,1)S(1)}, u32[]{:S(2)}, u32[]{:S(2)}) collective-permute-start(bf16[1,768,384]{2,1,0:T(8,128)(2,1)S(1)} %collective-permute-done.89.refs_1_), channel_id=1, source_target_pairs={{8,0},{16,8},{24,16},{28,24},{20,28},{12,20},{4,12},{0,4},{1,9},{9... | collective-permute-start | bytes 1769480 | tf_op jit(solution)/shard_map/ppermute | solution.py:855
  527.1 39.1 %collective-permute-start.33 = (bf16[512,768]{1,0:T(8,128)(2,1)}, bf16[512,768]{1,0:T(8,128)(2,1)}, u32[]{:S(2)}, u32[]{:S(2)}) collective-permute-start(bf16[512,768]{1,0:T(8,128)(2,1)} %dynamic-slice_convert_fusion.1), channel_id=1, source_target_pairs={{0,2},{2,0},{1,3},{3,1},{4,6},{6,4},{5,7},{7,5},{8,10},{10,8},{9,1... | collective-permute-start | bytes 2359304 | tf_op jit(solution)/shard_map/ppermute | solution.py:48
  529.6 18.8 %collective-permute-start.106 = (bf16[2,96,896]{2,1,0:T(8,128)(2,1)S(1)}, bf16[2,96,896]{2,1,0:T(8,128)(2,1)S(1)}, u32[]{:S(2)}, u32[]{:S(2)}) collective-permute-start(bf16[2,96,896]{2,1,0:T(8,128)(2,1)S(1)} %collective-permute-done.105.refs_10_), channel_id=1, source_target_pairs={{8,0},{16,8},{24,16},{28,24},{20,28},{12,20},{4,12},{0,4},{1,9},{9... | collective-permute-start | bytes 1032200 | tf_op jit(solution)/shard_map/ppermute | solution.py:855
  538.3 17.7 %collective-permute-start.94 = (bf16[1,768,384]{2,1,0:T(8,128)(2,1)S(1)}, bf16[1,768,384]{2,1,0:T(8,128)(2,1)S(1)}, u32[]{:S(2)}, u32[]{:S(2)}) collective-permute-start(bf16[1,768,384]{2,1,0:T(8,128)(2,1)S(1)} %collective-permute-done.91.refs_0_), channel_id=1, source_target_pairs={{0,8},{8,16},{16,24},{24,28},{28,20},{20,12},{12,4},{4,0},{9,1},{1... | collective-permute-start | bytes 1769480 | tf_op jit(solution)/shard_map/ppermute | solution.py:855
  543.5 21.8 %collective-permute-start.95 = (bf16[1,768,384]{2,1,0:T(8,128)(2,1)S(1)}, bf16[1,768,384]{2,1,0:T(8,128)(2,1)S(1)}, u32[]{:S(2)}, u32[]{:S(2)}) collective-permute-start(bf16[1,768,384]{2,1,0:T(8,128)(2,1)S(1)} %collective-permute-done.92.refs_1_), channel_id=1, source_target_pairs={{8,0},{16,8},{24,16},{28,24},{20,28},{12,20},{4,12},{0,4},{1,9},{9... | collective-permute-start | bytes 1769480 | tf_op jit(solution)/shard_map/ppermute | solution.py:855
  547.3 22.4 %collective-permute-start.56 = (bf16[512,768]{1,0:T(8,128)(2,1)}, bf16[512,768]{1,0:T(8,128)(2,1)}, u32[]{:S(2)}, u32[]{:S(2)}) collective-permute-start(bf16[512,768]{1,0:T(8,128)(2,1)} %dynamic-slice_convert_fusion), channel_id=1, source_target_pairs={{0,2},{2,0},{1,3},{3,1},{4,6},{6,4},{5,7},{7,5},{8,10},{10,8},{9,1... | collective-permute-start | bytes 2359304 | tf_op jit(solution)/shard_map/ppermute | solution.py:48
  565.2 19.2 %collective-permute-start.98 = (bf16[1,768,384]{2,1,0:T(8,128)(2,1)S(1)}, bf16[1,768,384]{2,1,0:T(8,128)(2,1)S(1)}, u32[]{:S(2)}, u32[]{:S(2)}) collective-permute-start(bf16[1,768,384]{2,1,0:T(8,128)(2,1)S(1)} %collective-permute-done.95.refs_1_), channel_id=1, source_target_pairs={{8,0},{16,8},{24,16},{28,24},{20,28},{12,20},{4,12},{0,4},{1,9},{9... | collective-permute-start | bytes 1769480 | tf_op jit(solution)/shard_map/ppermute | solution.py:855
  571.6 17.3 %collective-permute-start.108 = (bf16[2,96,896]{2,1,0:T(8,128)(2,1)S(1)}, bf16[2,96,896]{2,1,0:T(8,128)(2,1)S(1)}, u32[]{:S(2)}, u32[]{:S(2)}) collective-permute-start(bf16[2,96,896]{2,1,0:T(8,128)(2,1)S(1)} %collective-permute-done.107.refs_12_), channel_id=1, source_target_pairs={{8,0},{16,8},{24,16},{28,24},{20,28},{12,20},{4,12},{0,4},{1,9},{9... | collective-permute-start | bytes 1032200 | tf_op jit(solution)/shard_map/ppermute | solution.py:855
  579.7 30.4 %collective-permute-start.100 = (bf16[1,768,384]{2,1,0:T(8,128)(2,1)S(1)}, bf16[1,768,384]{2,1,0:T(8,128)(2,1)S(1)}, u32[]{:S(2)}, u32[]{:S(2)}) collective-permute-start(bf16[1,768,384]{2,1,0:T(8,128)(2,1)S(1)} %collective-permute-done.97.refs_0_), channel_id=1, source_target_pairs={{0,8},{8,16},{16,24},{24,28},{28,20},{20,12},{12,4},{4,0},{9,1},{1... | collective-permute-start | bytes 1769480 | tf_op jit(solution)/shard_map/ppermute | solution.py:855
  584.4 25.7 %collective-permute-start.101 = (bf16[1,768,384]{2,1,0:T(8,128)(2,1)S(1)}, bf16[1,768,384]{2,1,0:T(8,128)(2,1)S(1)}, u32[]{:S(2)}, u32[]{:S(2)}) collective-permute-start(bf16[1,768,384]{2,1,0:T(8,128)(2,1)S(1)} %collective-permute-done.98.refs_1_), channel_id=1, source_target_pairs={{8,0},{16,8},{24,16},{28,24},{20,28},{12,20},{4,12},{0,4},{1,9},{9... | collective-permute-start | bytes 1769480 | tf_op jit(solution)/shard_map/ppermute | solution.py:855
  588.9 23.4 %collective-permute-start.99 = (bf16[2,96,896]{2,1,0:T(8,128)(2,1)S(1)}, bf16[2,96,896]{2,1,0:T(8,128)(2,1)S(1)}, u32[]{:S(2)}, u32[]{:S(2)}) collective-permute-start(bf16[2,96,896]{2,1,0:T(8,128)(2,1)S(1)} %collective-permute-done.96.refs_5_), channel_id=1, source_target_pairs={{0,8},{8,16},{16,24},{24,28},{28,20},{20,12},{12,4},{4,0},{9,1},{1... | collective-permute-start | bytes 1032200 | tf_op jit(solution)/shard_map/ppermute | solution.py:855
  (133 other events, 1260.5 us)
